TPU v7x, 32 devices: a whole 2x2x4 slice. The times are simulated.
32 devices in a mesh: groups: 2 (over y), dp: 8 (over z, x), width: 2 (over core).
Axes of the slice: x: 2, y: 2, z: 4, core: 2. Of those that a mesh axis runs over, the one named last changes fastest.
Arguments:
- decoder: bfloat16 [8192, 4096], P(('groups', 'dp'), 'width'), parts along dimension 0, may hold values from -0.09375 to 0.09375
- grad_out: bfloat16 [2048, 4096], P(('groups', 'dp'), 'width'), parts along dimension 0, may hold values from -6 to 6
- active_blocks: int32 [2048, 8], P(('groups', 'dp')), parts along dimension 0, may hold values from 0 to 31, as said below
- feature_idx: int32 [2048, 32], P(('groups', 'dp')), parts along dimension 0, may hold values from 0 to 127, as said below
- acts: bfloat16 [2048, 32], P(('groups', 'dp')), parts along dimension 0, may hold values from 0.19921875 to 5
- block_slot: int32 [64], P('groups'), parts along dimension 0, may hold values from 0 to 31, as said below
Outputs:
- decoder_grad: bfloat16 [8192, 4096], P(('groups', 'dp'), 'width'), parts along dimension 0
- act_grad: float32 [2048, 32], P(('groups', 'dp')), parts along dimension 0
There are 2 independent parts, one for each index of `groups`. A program takes and returns all parts, laid end to end along the dimension named above; each array names one. Nothing has to cross between parts.
Inputs may be any that keep to these rules, and one draw needn't show every extreme that they name: `active_blocks`: the owner of block b is block_slot[b] // 4; each row names 8 blocks of 8 different owners; within the rows of one index of dp (aligned blocks of 128 rows) the blocks of one owner are named at most 128 times in all and one block by at most 43 rows, and both bounds are reached in every aligned block. `feature_idx`: the 4 entries of one active block of a row (columns a * 4 to a * 4 + 3) are distinct. A permutation; block b's weights are decoder rows block_slot[b] * 128 to block_slot[b] * 128 + 127.
All inputs are finite; a program needn't handle non-finite values.
Results may differ from a plain program's by a relative error of at most 0.001.
Values may be sent and summed in bfloat16 or wider, within the bound.
No kernel may reach another device: no remote copies, remote signals or barrier semaphores. Data moves between devices by JAX's collectives and lax.ppermute only.
A program may use at most 64 MiB of HBM per device.

v0:
```python
import jax
import jax.numpy as jnp
from jax import lax
from jax.sharding import PartitionSpec as P

BW = 128
BLK_DEV = 4
ACT = 8
KPB = 4


def send_back(picked):
    return lax.all_to_all(picked, "dp", split_axis=1, concat_axis=1, tiled=True)


def pack_slots(grad_out, target, slots_all, pair_coeffs, pair_columns, source_row):
    slot_row = jnp.zeros((slots_all,), jnp.int32).at[target].set(source_row)
    used = jnp.zeros((slots_all,), jnp.bool_).at[target].set(True)
    send_rows = jnp.where(used[:, None], grad_out[slot_row], jnp.zeros((), grad_out.dtype))
    send_acts = jnp.zeros((slots_all, KPB), pair_coeffs.dtype).at[target].set(pair_coeffs)
    send_cols = jnp.zeros((slots_all, KPB), jnp.int32).at[target].set(pair_columns)
    return (send_rows, send_acts, send_cols)


def per_device(decoder, grad_out, active_blocks, feature_idx, acts, block_slot):
    tok_rows, half_width = grad_out.shape
    owners = lax.axis_size("dp")
    mean_load = tok_rows * ACT // owners
    owner_cap = mean_load + min(mean_load // 2, tok_rows - mean_load)
    block_cap = (owner_cap + 2) // 3
    block_ids = active_blocks.reshape(-1)
    pair_count = block_ids.shape[0]
    table_pos = jnp.arange(block_slot.shape[0], dtype=jnp.int32)
    slot_of = jnp.sum(
        jnp.where(block_ids[:, None] == table_pos[None, :], block_slot[None, :], 0), axis=1
    )
    pair_pos = jnp.arange(pair_count, dtype=jnp.int32)
    source_row = pair_pos // ACT
    pair_coeffs = acts.reshape(pair_count, KPB)
    pair_feats = feature_idx.reshape(pair_count, KPB)
    earlier = (block_ids[:, None] == block_ids[None, :]) & (pair_pos[None, :] < pair_pos[:, None])
    position = jnp.sum(earlier.astype(jnp.int32), axis=1)
    slot_cols = owners * block_cap
    target = slot_of % BLK_DEV * slot_cols + slot_of // BLK_DEV * block_cap + position
    slots_all = BLK_DEV * slot_cols
    send_rows, send_acts, send_cols = pack_slots(
        grad_out, target, slots_all, pair_coeffs, pair_feats, source_row
    )
    rows, coeffs, feature_pos = (
        lax.all_to_all(
            send_rows.reshape(BLK_DEV, slot_cols, half_width),
            "dp",
            split_axis=1,
            concat_axis=1,
            tiled=True,
        ),
        lax.all_to_all(
            send_acts.reshape(BLK_DEV, slot_cols, KPB),
            "dp",
            split_axis=1,
            concat_axis=1,
            tiled=True,
        ),
        lax.all_to_all(
            send_cols.reshape(BLK_DEV, slot_cols, KPB),
            "dp",
            split_axis=1,
            concat_axis=1,
            tiled=True,
        ),
    )
    weights = decoder.reshape(BLK_DEV, BW, half_width)
    scores = jnp.einsum("bnd,bfd->bnf", rows, weights, preferred_element_type=jnp.float32)
    picked = jnp.take_along_axis(scores, feature_pos, axis=2)
    returned = send_back(picked)
    feature_axis = jnp.arange(BW, dtype=jnp.int32)
    matches = feature_pos[..., None] == feature_axis
    dense = jnp.sum(jnp.where(matches, coeffs[..., None].astype(jnp.float32), 0.0), axis=2).astype(
        jnp.bfloat16
    )
    grads = jnp.einsum("bnf,bnd->bfd", dense, rows, preferred_element_type=jnp.float32)
    decoder_grad = grads.astype(jnp.bfloat16).reshape(BLK_DEV * BW, half_width)
    pair_vals = returned.reshape(slots_all, KPB)[target]
    act_grad = pair_vals.reshape(tok_rows, ACT * KPB)
    act_grad = lax.psum(act_grad, "width")
    return (decoder_grad, act_grad)


def solution(mesh):
    in_specs = (
        P(("groups", "dp"), "width"),
        P(("groups", "dp"), "width"),
        P(("groups", "dp"), None),
        P(("groups", "dp"), None),
        P(("groups", "dp"), None),
        P("groups"),
    )
    out_specs = (P(("groups", "dp"), "width"), P(("groups", "dp"), None))
    return jax.shard_map(
        per_device, mesh=mesh, in_specs=in_specs, out_specs=out_specs, check_vma=False
    )
```

profile of v0, /device:TPU:0, one launch (start us, length us, event | category | flops | bytes accessed | tf_op | source)
XLA Modules:
  0.0 259.2 jit_solution(10594745996145767251)
XLA Ops:
  0.6 0.0 copy-start
  0.6 0.0 copy-start.1
  0.7 0.9 copy.82
  1.6 0.1 eq.22
  1.7 0.5 convert_reduce_fusion
  2.2 0.7 select_reduce_fusion.1
  3.0 0.8 copy.87
  3.8 0.2 reshape.187
  4.0 3.3 %scatter_custom_fusion.1 = bf16[1376,4]{1,0:T(8,128)(2,1)S(1)} fusion(s32[1024]{0:T(1024)S(1)} %bitcast.43, bf16[1024,4]{1,0:T(8,128)(2,1)S(1)} %reshape.187, bf16[]{:T(256)} %constant.67.clone.1), kind=kCustom, calls=%fused_computation.24 | custom fusion | bytes 11010 | tf_op jit(solution)/shard_map/scatter | solution.py:20
  7.3 0.1 copy.122
  7.5 0.9 reshape.221
  8.4 7.3 %all-to-all-start.1 = ((bf16[8,2,344]{2,1,0:T(2,128)(2,1)}), bf16[8,2,344]{2,1,0:T(2,128)(2,1)S(1)}, u32[]{:S(2)}, u32[]{:S(2)}) async-start(bf16[8,2,344]{2,1,0:T(2,128)(2,1)} %reshape.221), calls=%async_computation.1 | async-start | bytes 24576 | tf_op jit(solution)/shard_map/all_to_all | solution.py:57
  15.6 4.3 %scatter_custom_fusion.3 = s32[1376]{0:T(1024)S(1)} fusion(s32[1024]{0:T(1024)S(1)} %bitcast.44, s32[1024]{0:T(1024)S(1)} %add_select_fusion, s32[]{:T(128)} %constant.58.clone.1), kind=kCustom, calls=%fused_computation.45 | custom fusion | bytes 5508 | tf_op jit(solution)/shard_map/scatter | solution.py:17
  20.0 4.3 %scatter_custom_fusion.2 = pred[1376]{0:T(1024)(128)(4,1)S(1)} fusion(s32[1024]{0:T(1024)S(1)} %bitcast.45, pred[1024]{0:T(1024)(128)(4,1)S(1)} %broadcast.148, pred[]{:T(512)} %constant.69.clone.1), kind=kCustom, calls=%fused_computation.48 | custom fusion | bytes 1377 | tf_op jit(solution)/shard_map/scatter | solution.py:18
  24.4 0.1 broadcast_in_dim.78
  24.4 0.2 copy.91
  24.6 0.8 copy.83
  25.5 1.0 reshape.179
  26.4 3.6 %scatter_custom_fusion = s32[1376,4]{1,0:T(8,128)S(1)} fusion(s32[1024]{0:T(1024)S(1)} %bitcast.46, s32[1024,4]{1,0:T(8,128)} %reshape.179, s32[]{:T(128)} %constant.58.clone.1), kind=kCustom, calls=%fused_computation.22 | custom fusion | bytes 22528 | tf_op jit(solution)/shard_map/scatter | solution.py:21
  30.1 1.0 copy.120
  31.1 2.3 reshape.223
  33.4 0.0 copy-done.1
  33.4 6.8 %gather_fusion = bf16[1376,2048]{1,0:T(8,128)(2,1)} fusion(bf16[128,2048]{1,0:T(8,128)(2,1)S(1)} %copy-done.1, s32[2048]{0:T(1024)S(1)} %pad_clamp_fusion), kind=kCustom, calls=%fused_computation | custom fusion | bytes 11277696 | tf_op jit(solution)/shard_map/gather | solution.py:19
  40.3 0.0 all-to-all-done.1
  40.3 6.0 %all-to-all-start = ((s32[8,1,688]{2,1,0:T(1,128)}), s32[8,1,688]{2,1,0:T(1,128)S(1)}, u32[]{:S(2)}, u32[]{:S(2)}) async-start(s32[8,1,688]{2,1,0:T(1,128)} %reshape.223), calls=%async_computation | async-start | bytes 49152 | tf_op jit(solution)/shard_map/all_to_all | solution.py:64
  46.3 10.0 %copy_select_fusion = bf16[4,344,2048]{2,0,1:T(4,128)(2,1)} fusion(bf16[4,344,2048]{2,1,0:T(8,128)(2,1)} %bitcast.31, pred[4,344]{0,1:T(8,128)(4,1)S(1)} %copy.91), kind=kLoop, calls=%fused_computation.7 | loop fusion | flops 2818048 | bytes 11273568 | tf_op jit(solution)/shard_map/jit(_where)/select_n | solution.py:19
  56.3 0.0 all-to-all-done
  56.3 6.0 %all-to-all-start.2 = ((bf16[4,344,2048]{2,0,1:T(4,128)(2,1)}), bf16[4,344,2048]{2,0,1:T(4,128)(2,1)}, u32[]{:S(2)}, u32[]{:S(2)}) async-start(bf16[4,344,2048]{2,0,1:T(4,128)(2,1)} %copy_select_fusion), calls=%async_computation.2 | async-start | bytes 11272192 | tf_op jit(solution)/shard_map/all_to_all | solution.py:50
  62.3 0.6 broadcast_clamp_fusion
  62.9 0.3 reshape.222
  63.2 0.2 copy.90
  63.4 0.5 broadcast.173
  63.9 0.7 reduce
  64.6 0.4 reshape.224
  65.0 0.0 copy-start.2
  65.0 0.3 copy.86
  65.3 0.6 copy-done.2
  65.9 0.2 bitcast_or_fusion
  66.1 0.4 reshape.169
  66.5 2.6 select_reduce_fusion
  69.0 116.3 %all-to-all-done.2 = bf16[4,344,2048]{2,0,1:T(4,128)(2,1)} async-done(((bf16[4,344,2048]{2,0,1:T(4,128)(2,1)}), bf16[4,344,2048]{2,0,1:T(4,128)(2,1)}, u32[]{:S(2)}, u32[]{:S(2)}) %all-to-all-start.2) | async-done | bytes 5636128 | tf_op jit(solution)/shard_map/all_to_all | solution.py:50
  185.3 0.0 copy-done
  185.3 6.0 %fusion = f32[4,344,128]{2,1,0:T(8,128)S(1)} fusion(bf16[4,128,2048]{2,1,0:T(8,128)(2,1)S(1)} %bitcast.29, bf16[4,344,2048]{2,0,1:T(4,128)(2,1)} %all-to-all-done.2), kind=kOutput, calls=%fused_computation.8 | convolution fusion | flops 721420288 | bytes 8437760 | tf_op jit(solution)/shard_map/bnd,bfd->bnf/dot_general | solution.py:73
  191.3 0.0 copy-start.3
  191.3 42.0 %gather_fusion.2 = f32[5504]{0:T(1024)S(1)} fusion(f32[4,344,128]{2,1,0:T(8,128)S(1)} %fusion, s32[5504]{0:T(1024)S(1)} %reshape.169), kind=kCustom, calls=%fused_computation.2 | custom fusion | bytes 110080 | tf_op jit(solution)/shard_map/jit(take_along_axis)/gather | solution.py:74
  233.4 0.7 reshape.172
  234.1 0.0 copy-done.3
  234.1 0.2 and_select_fusion
  234.3 0.2 copy.121
  234.5 1.2 reshape.225
  235.7 3.6 %all-to-all-start.3 = ((f32[8,1,688]{2,1,0:T(1,128)}), f32[8,1,688]{2,1,0:T(1,128)S(1)}, u32[]{:S(2)}, u32[]{:S(2)}) async-start(f32[8,1,688]{2,1,0:T(1,128)} %reshape.225), calls=%async_computation.3 | async-start | bytes 49152 | tf_op jit(solution)/shard_map/all_to_all | solution.py:13
  239.3 0.0 copy-start.4
  239.3 10.8 %fusion.5 = bf16[4,128,2048]{2,1,0:T(8,128)(2,1)} fusion(bf16[4,344,2048]{2,0,1:T(4,128)(2,1)} %all-to-all-done.2, bf16[4,344,128]{2,1,0:T(8,128)(2,1)} %select_reduce_fusion), kind=kOutput, calls=%fused_computation.15 | convolution fusion | flops 722468864 | bytes 8085504 | tf_op jit(solution)/shard_map/bnf,bnd->bfd/dot_general | solution.py:81
  250.1 0.0 all-to-all-done.3
  250.1 0.6 broadcast.174
  250.7 0.7 reduce.1
  251.4 0.4 reshape.226
  251.9 0.0 copy-done.4
  251.9 2.8 %gather_fusion.1 = f32[1024,4]{1,0:T(8,128)S(1)} fusion(f32[1376,4]{1,0:T(8,128)S(1)} %bitcast.30, s32[1024]{0:T(1024)S(1)} %copy-done.4), kind=kCustom, calls=%fused_computation.1 | custom fusion | bytes 36864 | tf_op jit(solution)/shard_map/gather | solution.py:83
  254.7 0.2 reshape.152
  254.9 3.6 %psum.7 = f32[128,32]{1,0:T(8,128)S(1)} all-reduce(f32[128,32]{1,0:T(8,128)S(1)} %reshape.152), channel_id=1, replica_groups=mesh['groups'=2,'dp'=8,'width'=2] {'width'}, use_global_device_ids=true, to_apply=%region_7.8 | all-reduce | flops 4096 | bytes 32768 | tf_op jit(solution)/shard_map/psum | solution.py:85
  258.5 0.7 copy.100
  (7 shorter events, 0.1 us)
Async XLA Ops:
  0.6 184.7 %copy-start = (bf16[512,2048]{1,0:T(8,128)(2,1)S(1)}, bf16[512,2048]{1,0:T(8,128)(2,1)}, u32[]{:S(2)}) copy-start(bf16[512,2048]{1,0:T(8,128)(2,1)} %param.6) | copy-start | bytes 6291460
  0.6 32.8 %copy-start.1 = (bf16[128,2048]{1,0:T(8,128)(2,1)S(1)}, bf16[128,2048]{1,0:T(8,128)(2,1)}, u32[]{:S(2)}) copy-start(bf16[128,2048]{1,0:T(8,128)(2,1)} %param.7) | copy-start | bytes 1572868
  8.4 31.9 %all-to-all-start.1 = ((bf16[8,2,344]{2,1,0:T(2,128)(2,1)}), bf16[8,2,344]{2,1,0:T(2,128)(2,1)S(1)}, u32[]{:S(2)}, u32[]{:S(2)}) async-start(bf16[8,2,344]{2,1,0:T(2,128)(2,1)} %reshape.221), calls=%async_computation.1 | async-start | bytes 24576 | tf_op jit(solution)/shard_map/all_to_all | solution.py:57
  40.3 16.0 %all-to-all-start = ((s32[8,1,688]{2,1,0:T(1,128)}), s32[8,1,688]{2,1,0:T(1,128)S(1)}, u32[]{:S(2)}, u32[]{:S(2)}) async-start(s32[8,1,688]{2,1,0:T(1,128)} %reshape.223), calls=%async_computation | async-start | bytes 49152 | tf_op jit(solution)/shard_map/all_to_all | solution.py:64
  56.3 129.1 %all-to-all-start.2 = ((bf16[4,344,2048]{2,0,1:T(4,128)(2,1)}), bf16[4,344,2048]{2,0,1:T(4,128)(2,1)}, u32[]{:S(2)}, u32[]{:S(2)}) async-start(bf16[4,344,2048]{2,0,1:T(4,128)(2,1)} %copy_select_fusion), calls=%async_computation.2 | async-start | bytes 11272192 | tf_op jit(solution)/shard_map/all_to_all | solution.py:50
  65.0 0.9 copy-start.2
  191.3 42.8 %copy-start.3 = (s32[344,4,4]{2,1,0:T(4,128)S(1)}, s32[344,4,4]{2,1,0:T(4,128)}, u32[]{:S(2)}) copy-start(s32[344,4,4]{2,1,0:T(4,128)} %copy-done.2) | copy-start | bytes 66052
  235.7 14.5 %all-to-all-start.3 = ((f32[8,1,688]{2,1,0:T(1,128)}), f32[8,1,688]{2,1,0:T(1,128)S(1)}, u32[]{:S(2)}, u32[]{:S(2)}) async-start(f32[8,1,688]{2,1,0:T(1,128)} %reshape.225), calls=%async_computation.3 | async-start | bytes 49152 | tf_op jit(solution)/shard_map/all_to_all | solution.py:13
  239.3 12.6 %copy-start.4 = (s32[1024]{0:T(1024)S(1)}, s32[1024]{0:T(1024)}, u32[]{:S(2)}) copy-start(s32[1024]{0:T(1024)} %broadcast_clamp_fusion) | copy-start | bytes 12292
where the time goes:
time: 260 us; the launch traced here: 259 us
  waiting for transfers between devices  116 us (45%)
  local copies, waits for them, and re-layouts  82.4 us (32%)
  starting transfers between devices  22.9 us (9%)
  matrix products  16.8 us (6%)
  other arithmetic  16.3 us (6%)
  blocking collectives  3.59 us (1%)
    all_to_all x1, waiting for transfers between devices, per_device(): lax.all_to_all(send_rows.reshape(BLK_DEV, slot_cols, half_width), 'dp', s...  116 us
    gather x3, local copies, waits for them, and re-layouts, per_device(): picked = jnp.take_along_axis(scores, feature_pos, axis=2)  43.1 us
    dot_general x1, matrix products, per_device(): jnp.einsum('bnf,bnd->bfd', dense, rows, preferred_element_type=jnp.float32)  10.8 us
    select_n x1, other arithmetic, pack_slots(): jnp.where(used[:, None], grad_out[slot_row], jnp.zeros((), grad_out.dtype))  10 us
    unnamed x20, local copies, waits for them, and re-layouts  9.26 us
    all_to_all x1, starting transfers between devices, per_device(): lax.all_to_all(send_acts.reshape(BLK_DEV, slot_cols, KPB), 'dp', split_ax...  7.25 us
    gather x1, local copies, waits for them, and re-layouts, pack_slots(): grad_out[slot_row]  6.85 us
    all_to_all x1, starting transfers between devices, per_device(): lax.all_to_all(send_rows.reshape(BLK_DEV, slot_cols, half_width), 'dp', s...  6 us
  transfers between devices with their start and end apart: 4, of which 1 were waited for; matrix products, arithmetic and copies ran while one was open for 20% of the time, Pallas kernels for 0%

commit v1 on v0

--- a/solution.py
+++ b/solution.py
@@ -7,6 +7,71 @@
 BLK_DEV = 4
 ACT = 8
 KPB = 4
+
+
+def slots_of(active_blocks, block_slot):
+    table_pos = jnp.arange(block_slot.shape[0], dtype=jnp.int32)
+    return jnp.sum(
+        jnp.where(active_blocks[..., None] == table_pos, block_slot, 0), axis=-1
+    )
+
+
+def every_owner(decoder, grad_out, active_blocks, feature_idx, acts, block_slot):
+    tok_rows, half_width = grad_out.shape
+    owners = lax.axis_size("dp")
+    slot_of = slots_of(active_blocks, block_slot)
+    facts = jnp.concatenate(
+        [
+            slot_of.astype(jnp.float32),
+            feature_idx.astype(jnp.float32),
+            acts.astype(jnp.float32),
+        ],
+        axis=1,
+    )
+    facts = lax.all_gather(facts, "dp", axis=0, tiled=True)
+    rows = lax.all_gather(grad_out, "dp", axis=0, tiled=True)
+    tokens = rows.shape[0]
+    me = lax.axis_index("dp")
+    slots = facts[:, :ACT].astype(jnp.int32)
+    mine = slots // BLK_DEV == me
+    local = jnp.sum(jnp.where(mine, slots % BLK_DEV, 0), axis=1)
+    feats = jnp.sum(
+        jnp.where(mine[:, :, None], facts[:, ACT : ACT + ACT * KPB].reshape(tokens, ACT, KPB), 0),
+        axis=1,
+    ).astype(jnp.int32)
+    coeffs = jnp.sum(
+        jnp.where(mine[:, :, None], facts[:, ACT + ACT * KPB :].reshape(tokens, ACT, KPB), 0),
+        axis=1,
+    )
+    at_row = local[:, None] * BW + feats
+    row_axis = jnp.arange(BLK_DEV * BW, dtype=jnp.int32)
+    scores = lax.dot_general(
+        rows, decoder, (((1,), (1,)), ((), ())), preferred_element_type=jnp.float32
+    )
+    picked = jnp.stack(
+        [
+            jnp.sum(jnp.where(at_row[:, k : k + 1] == row_axis, scores, 0.0), axis=1)
+            for k in range(KPB)
+        ]
+    )
+    dense = jnp.zeros((tokens, BLK_DEV * BW), jnp.float32)
+    for k in range(KPB):
+        dense = jnp.where(at_row[:, k : k + 1] == row_axis, coeffs[:, k : k + 1], dense)
+    dense = dense.astype(jnp.bfloat16)
+    grads = lax.dot_general(
+        dense, rows, (((0,), (0,)), ((), ())), preferred_element_type=jnp.float32
+    )
+    decoder_grad = grads.astype(jnp.bfloat16)
+    returned = lax.all_to_all(
+        picked.reshape(KPB, owners, tok_rows), "dp", split_axis=1, concat_axis=1, tiled=True
+    )
+    returned = lax.psum(returned, "width")
+    act_grad = jnp.zeros((tok_rows, ACT, KPB), jnp.float32)
+    for owner in range(owners):
+        act_grad = jnp.where(
+            (slot_of // BLK_DEV == owner)[:, :, None], returned[:, owner].T[:, None, :], act_grad
+        )
+    return (decoder_grad, act_grad.reshape(tok_rows, ACT * KPB))
 
 
 def send_back(picked):
@@ -22,7 +87,7 @@
     return (send_rows, send_acts, send_cols)
 
 
-def per_device(decoder, grad_out, active_blocks, feature_idx, acts, block_slot):
+def some_owners(decoder, grad_out, active_blocks, feature_idx, acts, block_slot):
     tok_rows, half_width = grad_out.shape
     owners = lax.axis_size("dp")
     mean_load = tok_rows * ACT // owners
@@ -86,6 +151,12 @@
     return (decoder_grad, act_grad)
 
 
+def per_device(*args):
+    if lax.axis_size("dp") == ACT:
+        return every_owner(*args)
+    return some_owners(*args)
+
+
 def solution(mesh):
     in_specs = (
         P(("groups", "dp"), "width"),

time: 260 us -> 115 us (0.44)
  local copies, waits for them, and re-layouts: 82.4 us -> 0.14 us
  waiting for transfers between devices: 116 us -> 44.7 us
  blocking collectives: 3.59 us -> 37.2 us
  starting transfers between devices: 22.9 us -> 3.37 us
  between operations: 0.88 us -> 14.2 us
  other arithmetic: 16.3 us -> 3.66 us
  matrix products: 16.8 us -> 11.6 us
    all_to_all x4 -> x1, waiting for transfers between devices: 116 us -> 0.33 us  [every_owner(): lax.all_to_all(picked.reshape(KPB, owners, tok_rows), 'dp', split_axis=1,...]
    gather x5 -> x0, local copies, waits for them, and re-layouts: 52.8 us -> none  [the longest x3 43.1 us: per_device(): picked = jnp.take_along_axis(scores, feature_pos, axis=2)]
    all_gather x0 -> x1, waiting for transfers between devices: none -> 43.7 us  [every_owner(): rows = lax.all_gather(grad_out, 'dp', axis=0, tiled=True)]
    all_gather x0 -> x1, blocking collectives: none -> 33.8 us  [every_owner(): facts = lax.all_gather(facts, 'dp', axis=0, tiled=True)]
    all_to_all x4 -> x1, starting transfers between devices: 22.9 us -> 3.34 us  [every_owner(): lax.all_to_all(picked.reshape(KPB, owners, tok_rows), 'dp', split_axis=1,...]
    scatter x4 -> x0, local copies, waits for them, and re-layouts: 15.6 us -> none  [the longest x1 4.34 us: pack_slots(): used = jnp.zeros((slots_all,), jnp.bool_).at[target].set(True)]
    select_n x5 -> x1, other arithmetic: 10.2 us -> 0.64 us  [every_owner(): jnp.where((slot_of // BLK_DEV == owner)[:, :, None], returned[:, owner].T...]
    unnamed x20 -> x2, local copies, waits for them, and re-layouts: 9.26 us -> 0.01 us
  transfers between devices with their start and end apart: 4 -> 2, of which waited for: 1 -> 2; matrix products, arithmetic and copies ran while one was open for 20% -> 8% of each run, Pallas kernels for 0% -> 0%
where the time goes in v1:
time: 115 us
  waiting for transfers between devices  44.7 us (39%)
  blocking collectives  37.2 us (32%)
  between operations  14.2 us (12%)
  matrix products  11.6 us (10%)
  other arithmetic  3.66 us (3%)
  starting transfers between devices  3.37 us (3%)
    all_gather x1, waiting for transfers between devices, every_owner(): rows = lax.all_gather(grad_out, 'dp', axis=0, tiled=True)  43.7 us
    all_gather x1, blocking collectives, every_owner(): facts = lax.all_gather(facts, 'dp', axis=0, tiled=True)  33.8 us
    dot_general x1, matrix products, every_owner(): lax.dot_general(dense, rows, (((0,), (0,)), ((), ())), preferred_element_...  6.18 us
    dot_general x1, matrix products, every_owner(): lax.dot_general(rows, decoder, (((1,), (1,)), ((), ())), preferred_elemen...  5.44 us
    psum x1, blocking collectives, every_owner(): returned = lax.psum(returned, 'width')  3.35 us
    all_to_all x1, starting transfers between devices, every_owner(): lax.all_to_all(picked.reshape(KPB, owners, tok_rows), 'dp', split_axis=1,...  3.34 us
  transfers between devices with their start and end apart: 2, of which 2 were waited for; matrix products, arithmetic and copies ran while one was open for 8% of the time, Pallas kernels for 0%

profile of v1, /device:TPU:0, one launch (start us, length us, event | category | flops | bytes accessed | tf_op | source)
XLA Modules:
  0.0 114.8 jit_solution(14661896064561888221)
XLA Ops:
  7.2 0.0 copy-start
  7.2 0.0 all-gather.2.cloned.1.call-start
  7.2 0.7 all-gather.2.cloned.1.call-update
  7.9 0.7 convert_element_type.26
  8.6 0.7 convert_element_type.25
  9.3 0.8 select_reduce_fusion.6
  10.2 33.8 %all_gather.6 = f32[1024,72]{0,1:T(8,128)S(1)} all-gather(f32[128,72]{0,1:T(8,128)S(1)} %pad_maximum_fusion), channel_id=1, replica_groups=mesh['groups'=2,'dp'=8,'width'=2] {'dp'}, dimensions={0}, use_global_device_ids=true | all-gather | bytes 331776 | tf_op jit(solution)/shard_map/all_gather | solution.py:31
  44.1 0.1 select_reduce_fusion.5
  44.3 43.7 %all-gather.2.cloned.1.call-done = bf16[1024,2048]{1,0:T(8,128)(2,1)} async-done(((bf16[128,2048]{1,0:T(8,128)(2,1)}), bf16[1024,2048]{1,0:T(8,128)(2,1)}) %all-gather.2.cloned.1.call-update) | async-done | bytes 4194320 | tf_op jit(solution)/shard_map/all_gather | solution.py:32
  88.1 0.0 copy-done
  88.1 5.4 %select_reduce_fusion.3 = (f32[1024]{0:T(1024)S(1)}, f32[1024]{0:T(1024)S(1)}, f32[1024]{0:T(1024)S(1)}, f32[1024]{0:T(1024)S(1)}) fusion(s32[1024]{0:T(1024)S(1)} %bitcast.59, s32[1024]{0:T(1024)S(1)} %bitcast.57, s32[1024]{0:T(1024)S(1)} %bitcast.63, s32[1024]{0:T(1024)S(1)} %bitcast.61, bf16[1024,2048]{1,0:T(8,128)(2,1)} %all-gather.2.cloned.1.call-done, ...), kind=kOutput, calls=%fused_computation.4 | convolution fusion | flops 2153771008 | bytes 6324224 | tf_op jit(solution)/shard_map/dot_general | solution.py:48
  93.5 0.6 pad_maximum_fusion.1
  94.1 3.3 %all-to-all-start = ((f32[4,8,128]{2,0,1:T(4,128)}), f32[4,8,128]{2,0,1:T(4,128)S(1)}, u32[]{:S(2)}, u32[]{:S(2)}) async-start(f32[4,8,128]{2,0,1:T(4,128)} %pad_maximum_fusion.1), calls=%async_computation | async-start | bytes 32768 | tf_op jit(solution)/shard_map/all_to_all | solution.py:65
  97.5 6.2 %convolution_convert_fusion = bf16[512,2048]{1,0:T(8,128)(2,1)} fusion(bf16[1024,2048]{1,0:T(8,128)(2,1)} %all-gather.2.cloned.1.call-done, f32[1024]{0:T(1024)S(1)} %bitcast.54, s32[1024]{0:T(1024)S(1)} %bitcast.60, f32[1024]{0:T(1024)S(1)} %bitcast.55, s32[1024]{0:T(1024)S(1)} %bitcast.62, f32[1024]{0:T(1024)S(1)} %bitcast.56, s32[1024]{0:T(1024)S(1)} %bitcast.64, ...), kind=kOutput, calls=%fused_computation | convolution fusion | flops 2152726528 | bytes 6324224 | tf_op jit(solution)/shard_map/dot_general | solution.py:61
  103.7 0.3 all-to-all-done
  104.0 3.3 %psum.7 = f32[4,8,128]{2,0,1:T(4,128)S(1)} all-reduce(f32[4,8,128]{2,0,1:T(4,128)S(1)} %all-to-all-done), channel_id=1, replica_groups=mesh['groups'=2,'dp'=8,'width'=2] {'width'}, use_global_device_ids=true, to_apply=%region_8.9 | all-reduce | flops 4096 | bytes 32768 | tf_op jit(solution)/shard_map/psum | solution.py:68
  107.3 0.6 select_select_fusion
  (13 shorter events, 0.2 us)
Async XLA Ops:
  7.2 80.9 %copy-start = (bf16[512,2048]{1,0:T(8,128)(2,1)S(1)}, bf16[512,2048]{1,0:T(8,128)(2,1)}, u32[]{:S(2)}) copy-start(bf16[512,2048]{1,0:T(8,128)(2,1)} %param.6) | copy-start | bytes 6291460
  7.2 80.9 %all-gather.2.cloned.1.call-start = ((), (), s32[]{:S(2)}) async-start(), calls=%async_computation.1 | async-start | bytes 4718592 | tf_op jit(solution)/shard_map/all_gather | solution.py:32
  94.1 9.9 %all-to-all-start = ((f32[4,8,128]{2,0,1:T(4,128)}), f32[4,8,128]{2,0,1:T(4,128)S(1)}, u32[]{:S(2)}, u32[]{:S(2)}) async-start(f32[4,8,128]{2,0,1:T(4,128)} %pad_maximum_fusion.1), calls=%async_computation | async-start | bytes 32768 | tf_op jit(solution)/shard_map/all_to_all | solution.py:65
Sparse Core Ops, SparseCore 0:
  10.1 77.8 all-gather.1

commit v2 on v0

--- a/solution.py
+++ b/solution.py
@@ -1,12 +1,224 @@
+import functools
+
 import jax
 import jax.numpy as jnp
 from jax import lax
+from jax.experimental import pallas as pl
+from jax.experimental.pallas import tpu as pltpu
 from jax.sharding import PartitionSpec as P
 
 BW = 128
 BLK_DEV = 4
 ACT = 8
 KPB = 4
+SMEM = pl.BlockSpec(memory_space=pltpu.SMEM)
+VMEM = pl.BlockSpec(memory_space=pltpu.VMEM)
+
+
+def table_kernel(block_slot, active, feats, acts, table, slots, wide_acts):
+    named = active[...]
+    slot = jnp.zeros_like(named)
+    for block in range(block_slot.shape[0]):
+        slot = jnp.where(named == block, block_slot[block], slot)
+    slots[...] = slot
+    wide_acts[...] = acts[...].astype(jnp.float32)
+    owner = slot // BLK_DEV
+    first_row = slot % BLK_DEV * BW
+    for k in range(KPB):
+        at_row = (first_row + feats[pl.ds(k, ACT, stride=KPB), :]).astype(jnp.float32)
+        coeff = wide_acts[pl.ds(k, ACT, stride=KPB), :]
+        for o in range(table.shape[0]):
+            mine = owner == o
+            table[o, k, :] = jnp.sum(jnp.where(mine, at_row, 0.0), axis=0)
+            table[o, KPB + k, :] = jnp.sum(jnp.where(mine, coeff, 0.0), axis=0)
+
+
+def make_table(block_slot, active_blocks, feature_idx, acts, owners):
+    tok_rows = active_blocks.shape[0]
+    return pl.pallas_call(
+        table_kernel,
+        out_shape=(
+            jax.ShapeDtypeStruct((owners, 2 * KPB, tok_rows), jnp.float32),
+            jax.ShapeDtypeStruct((ACT, tok_rows), jnp.int32),
+        ),
+        in_specs=[SMEM, VMEM, VMEM, VMEM],
+        out_specs=(VMEM, VMEM),
+        scratch_shapes=[pltpu.VMEM((ACT * KPB, tok_rows), jnp.float32)],
+        name="make_table",
+    )(block_slot, active_blocks.T, feature_idx.T, acts.T)
+
+
+def row_axis_of(rows, tok_rows):
+    return lax.broadcasted_iota(jnp.int32, (rows, tok_rows), 0)
+
+
+def dense_kernel(order, table, dense):
+    rows, tokens = dense.shape
+    tok_rows = tokens // table.shape[0]
+    row_axis = row_axis_of(rows, tok_rows)
+    for c in range(table.shape[0]):
+        here = table[order[c]]
+        at_row = here[:KPB].astype(jnp.int32)
+        block = jnp.zeros((rows, tok_rows), jnp.float32)
+        for k in range(KPB):
+            block = jnp.where(
+                row_axis == at_row[k : k + 1], here[KPB + k : KPB + k + 1], block
+            )
+        dense[:, c * tok_rows : (c + 1) * tok_rows] = block.astype(jnp.bfloat16)
+
+
+def make_dense(order, table, rows):
+    owners, _, tok_rows = table.shape
+    return pl.pallas_call(
+        dense_kernel,
+        out_shape=jax.ShapeDtypeStruct((rows, owners * tok_rows), jnp.bfloat16),
+        in_specs=[SMEM, VMEM],
+        out_specs=VMEM,
+        name="make_dense",
+    )(order, table)
+
+
+def score_kernel(first, count, has_before, order, table, decoder, *refs):
+    chunks, refs = refs[: 2 * count], refs[2 * count :]
+    if has_before:
+        before, picked = refs
+        picked[...] = before[...]
+    else:
+        (picked,) = refs
+        picked[...] = jnp.zeros_like(picked)
+    rows, half_width = decoder.shape
+    tok_rows = table.shape[2]
+    row_axis = row_axis_of(rows, tok_rows)
+    cut = half_width // 2
+    for c in range(count):
+        scores = jnp.zeros((rows, tok_rows), jnp.float32)
+        for side in range(2):
+            scores += lax.dot_general(
+                decoder[:, side * cut : (side + 1) * cut],
+                chunks[2 * c + side][...],
+                (((1,), (1,)), ((), ())),
+                preferred_element_type=jnp.float32,
+            )
+        peer = order[first + c]
+        at_row = table[peer, :KPB].astype(jnp.int32)
+        for k in range(KPB):
+            value = jnp.sum(
+                jnp.where(row_axis == at_row[k : k + 1], scores, 0.0), axis=0
+            )
+            for side in range(2):
+                picked[peer, side, k, :] = value
+
+
+def score(first, chunks, order, table, decoder, before=None):
+    owners, _, tok_rows = table.shape
+    count = len(chunks)
+    operands = [order, table, decoder] + [half for pair in chunks for half in pair]
+    if before is not None:
+        operands.append(before)
+    return pl.pallas_call(
+        functools.partial(score_kernel, first, count, before is not None),
+        out_shape=jax.ShapeDtypeStruct((owners, 2, 2 * KPB, tok_rows), jnp.float32),
+        in_specs=[SMEM] + [VMEM] * (len(operands) - 1),
+        out_specs=VMEM,
+        compiler_params=pltpu.CompilerParams(vmem_limit_bytes=40 * 2**20),
+        name="score",
+    )(*operands)
+
+
+def grads_kernel(steps, dense, *refs):
+    chunks, out = refs[:-1], refs[-1]
+
+    def write(halves):
+        rows = jnp.concatenate([half[...] for half in halves], axis=0)
+        out[...] = jnp.dot(
+            dense[...], rows, preferred_element_type=jnp.float32
+        ).astype(out.dtype)
+
+    @pl.when(pl.program_id(0) < steps)
+    def _():
+        write(chunks[0::2])
+
+    @pl.when(pl.program_id(0) >= steps)
+    def _():
+        write(chunks[1::2])
+
+
+def grads_of(dense, chunks, steps):
+    rows = dense.shape[0]
+    tok_rows, cut = chunks[0][0].shape
+    block = cut // steps
+    left = pl.BlockSpec((tok_rows, block), lambda i: (0, jnp.minimum(i, steps - 1)))
+    right = pl.BlockSpec((tok_rows, block), lambda i: (0, jnp.maximum(i - steps, 0)))
+    return pl.pallas_call(
+        functools.partial(grads_kernel, steps),
+        grid=(2 * steps,),
+        out_shape=jax.ShapeDtypeStruct((rows, 2 * cut), jnp.bfloat16),
+        in_specs=[pl.BlockSpec(dense.shape, lambda i: (0, 0))] + [left, right] * len(chunks),
+        out_specs=pl.BlockSpec((rows, block), lambda i: (0, i)),
+        compiler_params=pltpu.CompilerParams(vmem_limit_bytes=40 * 2**20),
+        name="grads",
+    )(dense, *[half for pair in chunks for half in pair])
+
+
+def unpack_kernel(returned, slots, out):
+    owner = slots[...] // BLK_DEV
+    for k in range(KPB):
+        total = jnp.zeros(owner.shape, jnp.float32)
+        for o in range(returned.shape[0]):
+            value = returned[o, 0, k : k + 1, :] + returned[o, 1, k : k + 1, :]
+            total = jnp.where(owner == o, value, total)
+        out[pl.ds(k, ACT, stride=KPB), :] = total
+
+
+def unpack(returned, slots):
+    tok_rows = slots.shape[1]
+    return pl.pallas_call(
+        unpack_kernel,
+        out_shape=jax.ShapeDtypeStruct((ACT * KPB, tok_rows), jnp.float32),
+        in_specs=[VMEM, VMEM],
+        out_specs=VMEM,
+        name="unpack",
+    )(returned, slots).T
+
+
+def every_owner(decoder, grad_out, active_blocks, feature_idx, acts, block_slot):
+    tok_rows, half_width = grad_out.shape
+    owners = lax.axis_size("dp")
+    half_ring = owners // 2
+    ring = list(range(0, owners, 2)) + list(range(owners - 1, 0, -2))
+    onward = [(ring[i], ring[(i + 1) % owners]) for i in range(owners)]
+    back = [(there, here) for here, there in onward]
+
+    me = lax.axis_index("dp")
+    place = jnp.where(me % 2 == 0, me // 2, owners - 1 - me // 2)
+    offsets = [0]
+    for d in range(1, half_ring):
+        offsets += [-d, d]
+    offsets.append(half_ring)
+    at = (place + jnp.array(offsets, jnp.int32)) % owners
+    order = jnp.where(at < half_ring, 2 * at, 2 * (owners - 1 - at) + 1)
+
+    cut = half_width // 2
+    own = (grad_out[:, :cut], grad_out[:, cut:])
+    chunks = [own]
+    ahead, behind = own, own
+    for d in range(1, half_ring):
+        ahead = tuple(lax.ppermute(half, "dp", onward) for half in ahead)
+        behind = tuple(lax.ppermute(half, "dp", back) for half in behind)
+        chunks += [ahead, behind]
+    chunks.append((lax.ppermute(ahead[0], "dp", onward), lax.ppermute(behind[1], "dp", back)))
+
+    table, slots = make_table(block_slot, active_blocks, feature_idx, acts, owners)
+    table = lax.all_to_all(table, "dp", 0, 0, tiled=True)
+    dense = make_dense(order, table, decoder.shape[0])
+    early = 2 * half_ring - 3
+    picked = score(0, chunks[:early], order, table, decoder)
+    picked = score(early, chunks[early:], order, table, decoder, picked)
+    sent = picked.reshape((2 * owners,) + picked.shape[2:])
+    returned = lax.all_to_all(sent, ("dp", "width"), 0, 0, tiled=True)
+    decoder_grad = grads_of(dense, chunks, 4)
+    act_grad = unpack(returned.reshape(picked.shape), slots)
+    return (decoder_grad, act_grad)
 
 
 def send_back(picked):
@@ -22,7 +234,7 @@
     return (send_rows, send_acts, send_cols)
 
 
-def per_device(decoder, grad_out, active_blocks, feature_idx, acts, block_slot):
+def some_owners(decoder, grad_out, active_blocks, feature_idx, acts, block_slot):
     tok_rows, half_width = grad_out.shape
     owners = lax.axis_size("dp")
     mean_load = tok_rows * ACT // owners
@@ -86,6 +298,12 @@
     return (decoder_grad, act_grad)
 
 
+def per_device(*args):
+    if lax.axis_size("dp") == ACT:
+        return every_owner(*args)
+    return some_owners(*args)
+
+
 def solution(mesh):
     in_specs = (
         P(("groups", "dp"), "width"),

time: 260 us -> 77.5 us (0.30)
  waiting for transfers between devices: 116 us -> 25.4 us
  local copies, waits for them, and re-layouts: 82.4 us -> 4.51 us
  Pallas kernels: 0 us -> 20.2 us
  matrix products: 16.8 us -> 0 us
  other arithmetic: 16.3 us -> 0.67 us
  blocking collectives: 3.59 us -> 0 us
    all_to_all x4 -> x2, waiting for transfers between devices: 116 us -> 6.02 us  [the longest x1 6.01 us: every_owner(): table = lax.all_to_all(table, 'dp', 0, 0, tiled=True)]
    gather x5 -> x0, local copies, waits for them, and re-layouts: 52.8 us -> none  [the longest x3 43.1 us: per_device(): picked = jnp.take_along_axis(scores, feature_pos, axis=2)]
    pallas_call x0 -> x6, Pallas kernels: none -> 20.2 us  [the longest x2 7.51 us: score(): pl.pallas_call(functools.partial(score_kernel, first, count, before is no...]
    ppermute x0 -> x14, waiting for transfers between devices: none -> 19.4 us  [the longest x6 11.1 us: every_owner(): ahead = tuple((lax.ppermute(half, 'dp', onward) for half in ahead))]
    dot_general x2 -> x0, matrix products: 16.8 us -> none  [the longest x1 10.8 us: per_device(): jnp.einsum('bnf,bnd->bfd', dense, rows, preferred_element_type=jnp.float32)]
    scatter x4 -> x0, local copies, waits for them, and re-layouts: 15.6 us -> none  [the longest x1 4.34 us: pack_slots(): used = jnp.zeros((slots_all,), jnp.bool_).at[target].set(True)]
    ppermute x0 -> x14, starting transfers between devices: none -> 15.4 us  [the longest x6 10.8 us: every_owner(): behind = tuple((lax.ppermute(half, 'dp', back) for half in behind))]
    all_to_all x4 -> x2, starting transfers between devices: 22.9 us -> 9.71 us  [the longest x1 6.23 us: every_owner(): table = lax.all_to_all(table, 'dp', 0, 0, tiled=True)]
  transfers between devices with their start and end apart: 4 -> 16, of which waited for: 1 -> 6; matrix products, arithmetic and copies ran while one was open for 20% -> 1% of each run, Pallas kernels for 0% -> 20%
where the time goes in v2:
time: 77.5 us; the launch traced here: 76.6 us
  waiting for transfers between devices  25.4 us (33%)
  starting transfers between devices  25.1 us (32%)
  Pallas kernels  20.2 us (26%)
  local copies, waits for them, and re-layouts  4.51 us (6%)
    ppermute x6, waiting for transfers between devices, every_owner(): ahead = tuple((lax.ppermute(half, 'dp', onward) for half in ahead))  11.1 us
    ppermute x6, starting transfers between devices, every_owner(): behind = tuple((lax.ppermute(half, 'dp', back) for half in behind))  10.8 us
    ppermute x6, waiting for transfers between devices, every_owner(): behind = tuple((lax.ppermute(half, 'dp', back) for half in behind))  8.34 us
    pallas_call x2, Pallas kernels, score(): pl.pallas_call(functools.partial(score_kernel, first, count, before is no...  7.51 us
    pallas_call x1, Pallas kernels, grads_of(): pl.pallas_call(functools.partial(grads_kernel, steps), grid=(2 * steps,),...  7.21 us
    all_to_all x1, starting transfers between devices, every_owner(): table = lax.all_to_all(table, 'dp', 0, 0, tiled=True)  6.23 us
    all_to_all x1, waiting for transfers between devices, every_owner(): table = lax.all_to_all(table, 'dp', 0, 0, tiled=True)  6.01 us
    all_to_all x1, starting transfers between devices, every_owner(): returned = lax.all_to_all(sent, ('dp', 'width'), 0, 0, tiled=True)  3.48 us
  transfers between devices with their start and end apart: 16, of which 6 were waited for; matrix products, arithmetic and copies ran while one was open for 1% of the time, Pallas kernels for 20%

profile of v2, /device:TPU:0, one launch (start us, length us, event | category | flops | bytes accessed | tf_op | source)
XLA Modules:
  0.0 76.6 jit_solution(14546084752326525837)
XLA Ops:
  0.6 1.1 %fusion.1 = (bf16[128,1024]{1,0:T(8,128)(2,1)S(1)}, bf16[128,1024]{1,0:T(8,128)(2,1)S(1)}) fusion(bf16[128,2048]{1,0:T(8,128)(2,1)} %param.8), kind=kLoop, calls=%fused_computation.5 | loop fusion | bytes 1048576 | tf_op jit(solution)/shard_map/slice | solution.py:202
  1.7 3.0 %collective-permute-start.3 = (bf16[128,1024]{1,0:T(8,128)(2,1)S(1)}, bf16[128,1024]{1,0:T(8,128)(2,1)S(1)}, u32[]{:S(2)}, u32[]{:S(2)}) collective-permute-start(bf16[128,1024]{1,0:T(8,128)(2,1)S(1)} %get-tuple-element.6.refs_1_), channel_id=1, source_target_pairs={{4,0},{8,4},{12,8},{14,12},{10,14},{6,10},{2,6},{0,2},{5,1},{9,5},... | collective-permute-start | bytes 786440 | tf_op jit(solution)/shard_map/ppermute | solution.py:207
  4.7 0.2 collective-permute-start
  4.8 2.0 %collective-permute-start.1 = (bf16[128,1024]{1,0:T(8,128)(2,1)S(1)}, bf16[128,1024]{1,0:T(8,128)(2,1)S(1)}, u32[]{:S(2)}, u32[]{:S(2)}) collective-permute-start(bf16[128,1024]{1,0:T(8,128)(2,1)S(1)} %get-tuple-element.6.refs_1_), channel_id=1, source_target_pairs={{0,4},{4,8},{8,12},{12,14},{14,10},{10,6},{6,2},{2,0},{1,5},{5,9},... | collective-permute-start | bytes 786440 | tf_op jit(solution)/shard_map/ppermute | solution.py:206
  6.8 0.1 collective-permute-start.2
  6.9 5.0 %collective-permute-done.3.refs_5_ = bf16[128,1024]{1,0:T(8,128)(2,1)S(1)} collective-permute-done((bf16[128,1024]{1,0:T(8,128)(2,1)S(1)}, bf16[128,1024]{1,0:T(8,128)(2,1)S(1)}, u32[]{:S(2)}, u32[]{:S(2)}) %collective-permute-start.3) | collective-permute-done | bytes 262176 | tf_op jit(solution)/shard_map/ppermute | solution.py:207
  11.9 2.0 %collective-permute-start.7 = (bf16[128,1024]{1,0:T(8,128)(2,1)S(1)}, bf16[128,1024]{1,0:T(8,128)(2,1)S(1)}, u32[]{:S(2)}, u32[]{:S(2)}) collective-permute-start(bf16[128,1024]{1,0:T(8,128)(2,1)S(1)} %collective-permute-done.3.refs_5_), channel_id=1, source_target_pairs={{4,0},{8,4},{12,8},{14,12},{10,14},{6,10},{2,6},{0,2},{5,1},{9,5},... | collective-permute-start | bytes 786440 | tf_op jit(solution)/shard_map/ppermute | solution.py:207
  13.9 0.0 collective-permute-done.refs_2_
  13.9 0.1 collective-permute-start.4
  14.0 5.5 %collective-permute-done.1.refs_3_ = bf16[128,1024]{1,0:T(8,128)(2,1)S(1)} collective-permute-done((bf16[128,1024]{1,0:T(8,128)(2,1)S(1)}, bf16[128,1024]{1,0:T(8,128)(2,1)S(1)}, u32[]{:S(2)}, u32[]{:S(2)}) %collective-permute-start.1) | collective-permute-done | bytes 262176 | tf_op jit(solution)/shard_map/ppermute | solution.py:206
  19.5 0.1 collective-permute-start.5
  19.7 0.0 collective-permute-done.2.refs_4_
  19.7 1.9 %collective-permute-start.6 = (bf16[128,1024]{1,0:T(8,128)(2,1)S(1)}, bf16[128,1024]{1,0:T(8,128)(2,1)S(1)}, u32[]{:S(2)}, u32[]{:S(2)}) collective-permute-start(bf16[128,1024]{1,0:T(8,128)(2,1)S(1)} %collective-permute-done.2.refs_4_), channel_id=1, source_target_pairs={{4,0},{8,4},{12,8},{14,12},{10,14},{6,10},{2,6},{0,2},{5,1},{9,5},... | collective-permute-start | bytes 786440 | tf_op jit(solution)/shard_map/ppermute | solution.py:207
  21.6 1.6 %collective-permute-done.7.refs_9_ = bf16[128,1024]{1,0:T(8,128)(2,1)S(1)} collective-permute-done((bf16[128,1024]{1,0:T(8,128)(2,1)S(1)}, bf16[128,1024]{1,0:T(8,128)(2,1)S(1)}, u32[]{:S(2)}, u32[]{:S(2)}) %collective-permute-start.7) | collective-permute-done | bytes 262176 | tf_op jit(solution)/shard_map/ppermute | solution.py:207
  23.1 2.0 %collective-permute-start.11 = (bf16[128,1024]{1,0:T(8,128)(2,1)S(1)}, bf16[128,1024]{1,0:T(8,128)(2,1)S(1)}, u32[]{:S(2)}, u32[]{:S(2)}) collective-permute-start(bf16[128,1024]{1,0:T(8,128)(2,1)S(1)} %collective-permute-done.7.refs_9_), channel_id=1, source_target_pairs={{4,0},{8,4},{12,8},{14,12},{10,14},{6,10},{2,6},{0,2},{5,1},{9,5},... | collective-permute-start | bytes 786440 | tf_op jit(solution)/shard_map/ppermute | solution.py:207
  25.1 0.0 collective-permute-done.4.refs_6_
  25.2 0.1 collective-permute-start.8
  25.3 5.5 %collective-permute-done.5.refs_7_ = bf16[128,1024]{1,0:T(8,128)(2,1)S(1)} collective-permute-done((bf16[128,1024]{1,0:T(8,128)(2,1)S(1)}, bf16[128,1024]{1,0:T(8,128)(2,1)S(1)}, u32[]{:S(2)}, u32[]{:S(2)}) %collective-permute-start.5) | collective-permute-done | bytes 262176 | tf_op jit(solution)/shard_map/ppermute | solution.py:206
  30.8 0.1 collective-permute-start.9
  30.9 0.0 collective-permute-done.6.refs_8_
  30.9 1.9 %collective-permute-start.10 = (bf16[128,1024]{1,0:T(8,128)(2,1)S(1)}, bf16[128,1024]{1,0:T(8,128)(2,1)}, u32[]{:S(2)}, u32[]{:S(2)}) collective-permute-start(bf16[128,1024]{1,0:T(8,128)(2,1)S(1)} %collective-permute-done.6.refs_8_), channel_id=1, source_target_pairs={{4,0},{8,4},{12,8},{14,12},{10,14},{6,10},{2,6},{0,2},{5,1},{9,5},... | collective-permute-start | bytes 786440 | tf_op jit(solution)/shard_map/ppermute | solution.py:207
  32.8 1.7 %collective-permute-done.11.refs_13_.refs_3_ = bf16[128,1024]{1,0:T(8,128)(2,1)S(1)} collective-permute-done((bf16[128,1024]{1,0:T(8,128)(2,1)S(1)}, bf16[128,1024]{1,0:T(8,128)(2,1)S(1)}, u32[]{:S(2)}, u32[]{:S(2)}) %collective-permute-start.11) | collective-permute-done | bytes 262176 | tf_op jit(solution)/shard_map/ppermute | solution.py:207
  34.5 1.9 %collective-permute-start.13 = (bf16[128,1024]{1,0:T(8,128)(2,1)S(1)}, bf16[128,1024]{1,0:T(8,128)(2,1)}, u32[]{:S(2)}, u32[]{:S(2)}) collective-permute-start(bf16[128,1024]{1,0:T(8,128)(2,1)S(1)} %collective-permute-done.11.refs_13_.refs_3_), channel_id=1, source_target_pairs={{4,0},{8,4},{12,8},{14,12},{10,14},{6,10},{2,6},{0,2},{5,1},{9,5},... | collective-permute-start | bytes 786440 | tf_op jit(solution)/shard_map/ppermute | solution.py:209
  36.4 0.0 collective-permute-done.8.refs_10_.refs_0_
  36.4 0.1 collective-permute-start.12
  36.5 1.5 %make_table.1 = (f32[8,8,128]{2,1,0:T(8,128)}, s32[8,128]{1,0:T(8,128)}) custom-call(s32[32]{0:T(128)} %block_slot.1, s32[8,128]{1,0:T(8,128)} %bitcast.10, s32[32,128]{1,0:T(8,128)} %bitcast.7, bf16[32,128]{1,0:T(8,128)(2,1)} %bitcast.9), custom_call_target="tpu_custom_call" | custom-call | tf_op jit(solution)/shard_map/make_table/pallas_call | solution.py:38
  38.1 6.2 %all-to-all-start = ((f32[8,8,128]{2,1,0:T(8,128)}), f32[8,8,128]{2,1,0:T(8,128)S(1)}, u32[]{:S(2)}, u32[]{:S(2)}) async-start(f32[8,8,128]{2,1,0:T(8,128)} %get-tuple-element.4), calls=%async_computation | async-start | bytes 65536 | tf_op jit(solution)/shard_map/all_to_all | solution.py:212
  44.3 0.7 compare_select_fusion.2.order
  45.0 0.0 copy-start.4
  45.0 6.0 %all-to-all-done.table = f32[8,8,128]{2,1,0:T(8,128)S(1)} async-done(((f32[8,8,128]{2,1,0:T(8,128)}), f32[8,8,128]{2,1,0:T(8,128)S(1)}, u32[]{:S(2)}, u32[]{:S(2)}) %all-to-all-start) | async-done | bytes 32800 | tf_op jit(solution)/shard_map/all_to_all | solution.py:212
  51.0 0.0 copy-start
  51.0 1.6 %copy-done = bf16[512,2048]{1,0:T(8,128)(2,1)S(1)} copy-done((bf16[512,2048]{1,0:T(8,128)(2,1)S(1)}, bf16[512,2048]{1,0:T(8,128)(2,1)}, u32[]{:S(2)}) %copy-start) | copy-done | bytes 2097176
  52.6 0.0 copy-start.3
  52.6 0.0 copy-start.1
  52.6 3.8 %score.2.refs_6_ = f32[8,2,8,128]{3,2,1,0:T(8,128)S(1)} custom-call(s32[8]{0:T(128)S(1)} %compare_select_fusion.2.order, f32[8,8,128]{2,1,0:T(8,128)S(1)} %all-to-all-done.table, bf16[512,2048]{1,0:T(8,128)(2,1)S(1)} %copy-done, bf16[128,1024]{1,0:T(8,128)(2,1)S(1)} %get-tuple-element.7.refs_0_, bf16[128,1024]{1,0:T(8,128)(2,1)S(1)} %get-tuple-element.6.refs_1_, ...), custom_call_target="tpu_custom_call" | custom-call | tf_op jit(solution)/shard_map/score/pallas_call | solution.py:118
  56.4 0.0 collective-permute-done.9.refs_11_.refs_1_
  56.4 0.0 collective-permute-done.10.refs_12_.refs_2_
  56.4 0.0 collective-permute-done.13.refs_15_.refs_5_
  56.4 0.0 collective-permute-done.12.refs_14_.refs_4_
  56.4 0.0 copy-done.4
  56.4 0.0 copy-done.3
  56.4 0.0 copy-done.1
  56.4 3.7 %score.3 = f32[8,2,8,128]{3,2,1,0:T(8,128)} custom-call(s32[8]{0:T(128)S(1)} %compare_select_fusion.2.order, f32[8,8,128]{2,1,0:T(8,128)S(1)} %all-to-all-done.table, bf16[512,2048]{1,0:T(8,128)(2,1)S(1)} %copy-done.1, bf16[128,1024]{1,0:T(8,128)(2,1)S(1)} %collective-permute-done.8.refs_10_.refs_0_, ...), custom_call_target="tpu_custom_call" | custom-call | tf_op jit(solution)/shard_map/score/pallas_call | solution.py:118
  60.2 3.5 %all-to-all-start.1 = ((f32[16,8,128]{2,1,0:T(8,128)}), f32[16,8,128]{2,1,0:T(8,128)S(1)}, u32[]{:S(2)}, u32[]{:S(2)}) async-start(f32[16,8,128]{2,1,0:T(8,128)} %bitcast.3), calls=%async_computation.1 | async-start | bytes 131072 | tf_op jit(solution)/shard_map/all_to_all | solution.py:218
  63.6 2.5 %make_dense.1.dense = bf16[512,1024]{1,0:T(8,128)(2,1)} custom-call(s32[8]{0:T(128)} %copy-done.4, f32[8,8,128]{2,1,0:T(8,128)} %copy-done.3), custom_call_target="tpu_custom_call" | custom-call | tf_op jit(solution)/shard_map/make_dense/pallas_call | solution.py:72
  66.1 0.0 copy-start.2
  66.1 1.2 %copy-done.2 = bf16[512,1024]{1,0:T(8,128)(2,1)S(1)} copy-done((bf16[512,1024]{1,0:T(8,128)(2,1)S(1)}, bf16[512,1024]{1,0:T(8,128)(2,1)}, u32[]{:S(2)}) %copy-start.2) | copy-done | bytes 1048600
  67.3 7.2 %grads.1 = bf16[512,2048]{1,0:T(8,128)(2,1)} custom-call(bf16[512,1024]{1,0:T(8,128)(2,1)S(1)} %copy-done.2, bf16[128,1024]{1,0:T(8,128)(2,1)S(1)} %get-tuple-element.7.refs_0_, bf16[128,1024]{1,0:T(8,128)(2,1)S(1)} %get-tuple-element.6.refs_1_, bf16[128,1024]{1,0:T(8,128)(2,1)S(1)} %collective-permute-done.refs_2_, ...), custom_call_target="tpu_custom_call" | custom-call | tf_op jit(solution)/shard_map/grads/pallas_call | solution.py:152
  74.5 0.0 all-to-all-done.1
  74.5 0.0 copy-start.5
  74.5 0.6 copy-done.5
  75.2 1.5 %unpack.1 = f32[32,128]{1,0:T(8,128)} custom-call(f32[8,2,8,128]{3,2,1,0:T(8,128)} %bitcast.6, s32[8,128]{1,0:T(8,128)} %get-tuple-element.5.slots), custom_call_target="tpu_custom_call" | custom-call | tf_op jit(solution)/shard_map/unpack/pallas_call | solution.py:175
Async XLA Ops:
  1.7 10.2 %collective-permute-start.3 = (bf16[128,1024]{1,0:T(8,128)(2,1)S(1)}, bf16[128,1024]{1,0:T(8,128)(2,1)S(1)}, u32[]{:S(2)}, u32[]{:S(2)}) collective-permute-start(bf16[128,1024]{1,0:T(8,128)(2,1)S(1)} %get-tuple-element.6.refs_1_), channel_id=1, source_target_pairs={{4,0},{8,4},{12,8},{14,12},{10,14},{6,10},{2,6},{0,2},{5,1},{9,5},... | collective-permute-start | bytes 786440 | tf_op jit(solution)/shard_map/ppermute | solution.py:207
  4.7 9.2 %collective-permute-start = (bf16[128,1024]{1,0:T(8,128)(2,1)S(1)}, bf16[128,1024]{1,0:T(8,128)(2,1)S(1)}, u32[]{:S(2)}, u32[]{:S(2)}) collective-permute-start(bf16[128,1024]{1,0:T(8,128)(2,1)S(1)} %get-tuple-element.7.refs_0_), channel_id=1, source_target_pairs={{0,4},{4,8},{8,12},{12,14},{14,10},{10,6},{6,2},{2,0},{1,5},{5,9},... | collective-permute-start | bytes 786440 | tf_op jit(solution)/shard_map/ppermute | solution.py:206
  4.8 14.7 %collective-permute-start.1 = (bf16[128,1024]{1,0:T(8,128)(2,1)S(1)}, bf16[128,1024]{1,0:T(8,128)(2,1)S(1)}, u32[]{:S(2)}, u32[]{:S(2)}) collective-permute-start(bf16[128,1024]{1,0:T(8,128)(2,1)S(1)} %get-tuple-element.6.refs_1_), channel_id=1, source_target_pairs={{0,4},{4,8},{8,12},{12,14},{14,10},{10,6},{6,2},{2,0},{1,5},{5,9},... | collective-permute-start | bytes 786440 | tf_op jit(solution)/shard_map/ppermute | solution.py:206
  6.8 12.9 %collective-permute-start.2 = (bf16[128,1024]{1,0:T(8,128)(2,1)S(1)}, bf16[128,1024]{1,0:T(8,128)(2,1)S(1)}, u32[]{:S(2)}, u32[]{:S(2)}) collective-permute-start(bf16[128,1024]{1,0:T(8,128)(2,1)S(1)} %get-tuple-element.7.refs_0_), channel_id=1, source_target_pairs={{4,0},{8,4},{12,8},{14,12},{10,14},{6,10},{2,6},{0,2},{5,1},{9,5},... | collective-permute-start | bytes 786440 | tf_op jit(solution)/shard_map/ppermute | solution.py:207
  11.9 11.2 %collective-permute-start.7 = (bf16[128,1024]{1,0:T(8,128)(2,1)S(1)}, bf16[128,1024]{1,0:T(8,128)(2,1)S(1)}, u32[]{:S(2)}, u32[]{:S(2)}) collective-permute-start(bf16[128,1024]{1,0:T(8,128)(2,1)S(1)} %collective-permute-done.3.refs_5_), channel_id=1, source_target_pairs={{4,0},{8,4},{12,8},{14,12},{10,14},{6,10},{2,6},{0,2},{5,1},{9,5},... | collective-permute-start | bytes 786440 | tf_op jit(solution)/shard_map/ppermute | solution.py:207
  13.9 11.2 %collective-permute-start.4 = (bf16[128,1024]{1,0:T(8,128)(2,1)S(1)}, bf16[128,1024]{1,0:T(8,128)(2,1)S(1)}, u32[]{:S(2)}, u32[]{:S(2)}) collective-permute-start(bf16[128,1024]{1,0:T(8,128)(2,1)S(1)} %collective-permute-done.refs_2_), channel_id=1, source_target_pairs={{0,4},{4,8},{8,12},{12,14},{14,10},{10,6},{6,2},{2,0},{1,5},{5,9},... | collective-permute-start | bytes 786440 | tf_op jit(solution)/shard_map/ppermute | solution.py:206
  19.5 11.2 %collective-permute-start.5 = (bf16[128,1024]{1,0:T(8,128)(2,1)S(1)}, bf16[128,1024]{1,0:T(8,128)(2,1)S(1)}, u32[]{:S(2)}, u32[]{:S(2)}) collective-permute-start(bf16[128,1024]{1,0:T(8,128)(2,1)S(1)} %collective-permute-done.1.refs_3_), channel_id=1, source_target_pairs={{0,4},{4,8},{8,12},{12,14},{14,10},{10,6},{6,2},{2,0},{1,5},{5,9},... | collective-permute-start | bytes 786440 | tf_op jit(solution)/shard_map/ppermute | solution.py:206
  19.7 11.2 %collective-permute-start.6 = (bf16[128,1024]{1,0:T(8,128)(2,1)S(1)}, bf16[128,1024]{1,0:T(8,128)(2,1)S(1)}, u32[]{:S(2)}, u32[]{:S(2)}) collective-permute-start(bf16[128,1024]{1,0:T(8,128)(2,1)S(1)} %collective-permute-done.2.refs_4_), channel_id=1, source_target_pairs={{4,0},{8,4},{12,8},{14,12},{10,14},{6,10},{2,6},{0,2},{5,1},{9,5},... | collective-permute-start | bytes 786440 | tf_op jit(solution)/shard_map/ppermute | solution.py:207
  23.1 11.4 %collective-permute-start.11 = (bf16[128,1024]{1,0:T(8,128)(2,1)S(1)}, bf16[128,1024]{1,0:T(8,128)(2,1)S(1)}, u32[]{:S(2)}, u32[]{:S(2)}) collective-permute-start(bf16[128,1024]{1,0:T(8,128)(2,1)S(1)} %collective-permute-done.7.refs_9_), channel_id=1, source_target_pairs={{4,0},{8,4},{12,8},{14,12},{10,14},{6,10},{2,6},{0,2},{5,1},{9,5},... | collective-permute-start | bytes 786440 | tf_op jit(solution)/shard_map/ppermute | solution.py:207
  25.2 11.3 %collective-permute-start.8 = (bf16[128,1024]{1,0:T(8,128)(2,1)S(1)}, bf16[128,1024]{1,0:T(8,128)(2,1)S(1)}, u32[]{:S(2)}, u32[]{:S(2)}) collective-permute-start(bf16[128,1024]{1,0:T(8,128)(2,1)S(1)} %collective-permute-done.4.refs_6_), channel_id=1, source_target_pairs={{0,4},{4,8},{8,12},{12,14},{14,10},{10,6},{6,2},{2,0},{1,5},{5,9},... | collective-permute-start | bytes 786440 | tf_op jit(solution)/shard_map/ppermute | solution.py:206
  30.8 25.6 %collective-permute-start.9 = (bf16[128,1024]{1,0:T(8,128)(2,1)S(1)}, bf16[128,1024]{1,0:T(8,128)(2,1)S(1)}, u32[]{:S(2)}, u32[]{:S(2)}) collective-permute-start(bf16[128,1024]{1,0:T(8,128)(2,1)S(1)} %collective-permute-done.5.refs_7_), channel_id=1, source_target_pairs={{0,4},{4,8},{8,12},{12,14},{14,10},{10,6},{6,2},{2,0},{1,5},{5,9},... | collective-permute-start | bytes 786440 | tf_op jit(solution)/shard_map/ppermute | solution.py:206
  30.9 25.5 %collective-permute-start.10 = (bf16[128,1024]{1,0:T(8,128)(2,1)S(1)}, bf16[128,1024]{1,0:T(8,128)(2,1)}, u32[]{:S(2)}, u32[]{:S(2)}) collective-permute-start(bf16[128,1024]{1,0:T(8,128)(2,1)S(1)} %collective-permute-done.6.refs_8_), channel_id=1, source_target_pairs={{4,0},{8,4},{12,8},{14,12},{10,14},{6,10},{2,6},{0,2},{5,1},{9,5},... | collective-permute-start | bytes 786440 | tf_op jit(solution)/shard_map/ppermute | solution.py:207
  34.5 21.9 %collective-permute-start.13 = (bf16[128,1024]{1,0:T(8,128)(2,1)S(1)}, bf16[128,1024]{1,0:T(8,128)(2,1)}, u32[]{:S(2)}, u32[]{:S(2)}) collective-permute-start(bf16[128,1024]{1,0:T(8,128)(2,1)S(1)} %collective-permute-done.11.refs_13_.refs_3_), channel_id=1, source_target_pairs={{4,0},{8,4},{12,8},{14,12},{10,14},{6,10},{2,6},{0,2},{5,1},{9,5},... | collective-permute-start | bytes 786440 | tf_op jit(solution)/shard_map/ppermute | solution.py:209
  36.4 20.0 %collective-permute-start.12 = (bf16[128,1024]{1,0:T(8,128)(2,1)S(1)}, bf16[128,1024]{1,0:T(8,128)(2,1)}, u32[]{:S(2)}, u32[]{:S(2)}) collective-permute-start(bf16[128,1024]{1,0:T(8,128)(2,1)S(1)} %collective-permute-done.8.refs_10_.refs_0_), channel_id=1, source_target_pairs={{0,4},{4,8},{8,12},{12,14},{14,10},{10,6},{6,2},{2,0},{1,5},{5,9},... | collective-permute-start | bytes 786440 | tf_op jit(solution)/shard_map/ppermute | solution.py:209
  38.1 12.9 %all-to-all-start = ((f32[8,8,128]{2,1,0:T(8,128)}), f32[8,8,128]{2,1,0:T(8,128)S(1)}, u32[]{:S(2)}, u32[]{:S(2)}) async-start(f32[8,8,128]{2,1,0:T(8,128)} %get-tuple-element.4), calls=%async_computation | async-start | bytes 65536 | tf_op jit(solution)/shard_map/all_to_all | solution.py:212
  45.0 11.5 %copy-start.4 = (s32[8]{0:T(128)}, s32[8]{0:T(128)S(1)}, u32[]{:S(2)}) copy-start(s32[8]{0:T(128)S(1)} %compare_select_fusion.2.order) | copy-start | bytes 100
  51.0 1.6 %copy-start = (bf16[512,2048]{1,0:T(8,128)(2,1)S(1)}, bf16[512,2048]{1,0:T(8,128)(2,1)}, u32[]{:S(2)}) copy-start(bf16[512,2048]{1,0:T(8,128)(2,1)} %decoder.3) | copy-start | bytes 6291460
  52.6 3.9 %copy-start.3 = (f32[8,8,128]{2,1,0:T(8,128)}, f32[8,8,128]{2,1,0:T(8,128)S(1)}, u32[]{:S(2)}) copy-start(f32[8,8,128]{2,1,0:T(8,128)S(1)} %all-to-all-done.table) | copy-start | bytes 98308
  52.6 3.9 %copy-start.1 = (bf16[512,2048]{1,0:T(8,128)(2,1)S(1)}, bf16[512,2048]{1,0:T(8,128)(2,1)}, u32[]{:S(2)}) copy-start(bf16[512,2048]{1,0:T(8,128)(2,1)} %decoder.3) | copy-start | bytes 6291460
  60.2 14.4 %all-to-all-start.1 = ((f32[16,8,128]{2,1,0:T(8,128)}), f32[16,8,128]{2,1,0:T(8,128)S(1)}, u32[]{:S(2)}, u32[]{:S(2)}) async-start(f32[16,8,128]{2,1,0:T(8,128)} %bitcast.3), calls=%async_computation.1 | async-start | bytes 131072 | tf_op jit(solution)/shard_map/all_to_all | solution.py:218
  66.1 1.2 %copy-start.2 = (bf16[512,1024]{1,0:T(8,128)(2,1)S(1)}, bf16[512,1024]{1,0:T(8,128)(2,1)}, u32[]{:S(2)}) copy-start(bf16[512,1024]{1,0:T(8,128)(2,1)} %make_dense.1.dense) | copy-start | bytes 3145732
  74.5 0.6 copy-start.5

commit v3 on v0

--- a/solution.py
+++ b/solution.py
@@ -1,12 +1,294 @@
+import functools
+
 import jax
 import jax.numpy as jnp
 from jax import lax
+from jax.experimental import pallas as pl
+from jax.experimental.pallas import tpu as pltpu
 from jax.sharding import PartitionSpec as P
 
 BW = 128
 BLK_DEV = 4
 ACT = 8
 KPB = 4
+SMEM = pl.BlockSpec(memory_space=pltpu.SMEM)
+VMEM = pl.BlockSpec(memory_space=pltpu.VMEM)
+ANY = pl.BlockSpec(memory_space=pl.ANY)
+LIMIT = pltpu.CompilerParams(vmem_limit_bytes=40 * 2**20)
+
+
+def kept(x):
+    return pltpu.with_memory_space_constraint(x, pltpu.VMEM)
+
+
+def prepare_kernel(
+    block_slot, active, feats, acts, decoder, table, slots, decoder_here, wide_acts, sem
+):
+    load = pltpu.make_async_copy(decoder, decoder_here, sem)
+    load.start()
+    named = active[...]
+    slot = jnp.zeros_like(named)
+    for block in range(block_slot.shape[0]):
+        slot = jnp.where(named == block, block_slot[block], slot)
+    slots[...] = slot
+    wide_acts[...] = acts[...].astype(jnp.float32)
+    owner = slot // BLK_DEV
+    first_row = slot % BLK_DEV * BW
+    for k in range(KPB):
+        at_row = (first_row + feats[pl.ds(k, ACT, stride=KPB), :]).astype(jnp.float32)
+        coeff = wide_acts[pl.ds(k, ACT, stride=KPB), :]
+        for o in range(table.shape[0]):
+            mine = owner == o
+            table[o, k, :] = jnp.sum(jnp.where(mine, at_row, 0.0), axis=0)
+            table[o, KPB + k, :] = jnp.sum(jnp.where(mine, coeff, 0.0), axis=0)
+    load.wait()
+
+
+def prepare(block_slot, active_blocks, feature_idx, acts, decoder, owners):
+    tok_rows = active_blocks.shape[0]
+    return pl.pallas_call(
+        prepare_kernel,
+        out_shape=(
+            pltpu.VMEM((owners, 2 * KPB, tok_rows), jnp.float32),
+            pltpu.VMEM((ACT, tok_rows), jnp.int32),
+            pltpu.VMEM(decoder.shape, decoder.dtype),
+        ),
+        in_specs=[SMEM, VMEM, VMEM, VMEM, ANY],
+        out_specs=(VMEM, VMEM, VMEM),
+        scratch_shapes=[
+            pltpu.VMEM((ACT * KPB, tok_rows), jnp.float32),
+            pltpu.SemaphoreType.DMA,
+        ],
+        name="prepare",
+    )(block_slot, active_blocks.T, feature_idx.T, acts.T, decoder)
+
+
+def ring_of(owners):
+    return list(range(0, owners, 2)) + list(range(owners - 1, 0, -2))
+
+
+def peer_at(distance, owners):
+    me = lax.axis_index("dp")
+    half_ring = owners // 2
+    place = jnp.where(lax.rem(me, 2) == 0, lax.div(me, 2), owners - 1 - lax.div(me, 2))
+    at = lax.rem(place + owners + distance, owners)
+    return jnp.where(at < half_ring, 2 * at, 2 * (owners - 1 - at) + 1)
+
+
+def block_and_rows(here):
+    at_row = here[:KPB].astype(jnp.int32)
+    return at_row[:1] // BW, at_row % BW
+
+
+def row_axis_of(tok_rows):
+    return lax.broadcasted_iota(jnp.int32, (BW, tok_rows), 0)
+
+
+def coefficients(here):
+    block, feats = block_and_rows(here)
+    row_axis = row_axis_of(here.shape[1])
+    dense = jnp.zeros(row_axis.shape, jnp.float32)
+    for k in range(KPB):
+        dense = jnp.where(row_axis == feats[k : k + 1], here[KPB + k : KPB + k + 1], dense)
+    parts = [jnp.where(block == b, dense, 0.0) for b in range(BLK_DEV)]
+    return jnp.concatenate(parts, axis=0).astype(jnp.bfloat16)
+
+
+def pick(scores, here):
+    block, feats = block_and_rows(here)
+    row_axis = row_axis_of(here.shape[1])
+    mine = scores[:BW]
+    for b in range(1, BLK_DEV):
+        mine = jnp.where(block == b, scores[b * BW : (b + 1) * BW], mine)
+    return [
+        jnp.sum(jnp.where(row_axis == feats[k : k + 1], mine, 0.0), axis=0)
+        for k in range(KPB)
+    ]
+
+
+def add_picks(peers, table, decoder, chunks, picked):
+    tok_rows, cut = chunks[0].shape
+    for first in range(0, len(peers), 2):
+        some = peers[first : first + 2]
+        scores = None
+        for side in range(2):
+            halves = [chunks[2 * (first + i) + side][...] for i in range(len(some))]
+            rows = jnp.concatenate(halves, axis=0) if len(halves) > 1 else halves[0]
+            part = lax.dot_general(
+                decoder[:, side * cut : (side + 1) * cut],
+                rows,
+                (((1,), (1,)), ((), ())),
+                preferred_element_type=jnp.float32,
+            )
+            scores = part if scores is None else scores + part
+        for i, peer in enumerate(some):
+            values = pick(scores[:, i * tok_rows : (i + 1) * tok_rows], table[peer])
+            for k in range(KPB):
+                for width in range(2):
+                    picked[peer, width, k, :] = values[k]
+
+
+def gradient_blocks(peers, table, chunks, block):
+    cut = chunks[0].shape[1]
+    dense = jnp.concatenate([coefficients(table[peer]) for peer in peers], axis=1)
+    for side in range(2):
+        for start in range(0, cut, block):
+            rows = jnp.concatenate(
+                [half[:, start : start + block] for half in chunks[side::2]], axis=0
+            )
+            part = jnp.dot(dense, rows, preferred_element_type=jnp.float32)
+            yield slice(side * cut + start, side * cut + start + block), part
+
+
+def absorb_kernel(distances, later, table, decoder, *refs):
+    count = len(distances)
+    chunks, refs = refs[: 2 * count], refs[2 * count :]
+    picked, total = refs[-2:]
+    peers = [peer_at(d, table.shape[0]) for d in distances]
+    picked[...] = refs[0][...] if later else jnp.zeros_like(picked)
+    add_picks(peers, table, decoder, chunks, picked)
+    for columns, part in gradient_blocks(peers, table, chunks, 256):
+        total[:, columns] = refs[1][:, columns] + part if later else part
+
+
+def absorb(distances, chunks, table, decoder, state=()):
+    owners, _, tok_rows = table.shape
+    operands = [kept(table), decoder]
+    operands += [kept(half) for pair in chunks for half in pair]
+    operands += state
+    return pl.pallas_call(
+        functools.partial(absorb_kernel, distances, bool(state)),
+        out_shape=(
+            pltpu.VMEM((owners, 2, 2 * KPB, tok_rows), jnp.float32),
+            pltpu.VMEM(decoder.shape, jnp.float32),
+        ),
+        in_specs=[VMEM] * len(operands),
+        out_specs=(VMEM, VMEM),
+        input_output_aliases={len(operands) - 2: 0, len(operands) - 1: 1} if state else {},
+        compiler_params=LIMIT,
+        name="absorb",
+    )(*operands)
+
+
+def last_scores_kernel(distance, table, decoder, left, right, before, picked):
+    picked[...] = before[...]
+    add_picks([peer_at(distance, table.shape[0])], table, decoder, (left, right), picked)
+
+
+def last_scores(distance, chunk, table, decoder, picked):
+    return pl.pallas_call(
+        functools.partial(last_scores_kernel, distance),
+        out_shape=pltpu.VMEM(picked.shape, picked.dtype),
+        in_specs=[VMEM] * 5,
+        out_specs=VMEM,
+        input_output_aliases={4: 0},
+        compiler_params=LIMIT,
+        name="last_scores",
+    )(kept(table), decoder, kept(chunk[0]), kept(chunk[1]), picked)
+
+
+def last_gradients_kernel(distance, table, left, right, total, out, rounded, sems):
+    peer = peer_at(distance, table.shape[0])
+    copies = []
+    for columns, part in gradient_blocks([peer], table, (left, right), 256):
+        rounded[:, columns] = (total[:, columns] + part).astype(out.dtype)
+        copies.append(
+            pltpu.make_async_copy(
+                rounded.at[:, columns], out.at[:, columns], sems.at[len(copies)]
+            )
+        )
+        copies[-1].start()
+    for copy in copies:
+        copy.wait()
+
+
+def last_gradients(distance, chunk, table, total):
+    return pl.pallas_call(
+        functools.partial(last_gradients_kernel, distance),
+        out_shape=jax.ShapeDtypeStruct(total.shape, jnp.bfloat16),
+        in_specs=[VMEM] * 4,
+        out_specs=ANY,
+        scratch_shapes=[
+            pltpu.VMEM(total.shape, jnp.bfloat16),
+            pltpu.SemaphoreType.DMA((total.shape[1] // 256,)),
+        ],
+        compiler_params=LIMIT,
+        name="last_gradients",
+    )(kept(table), kept(chunk[0]), kept(chunk[1]), total)
+
+
+def unpack_kernel(returned, slots, out):
+    owner = slots[...] // BLK_DEV
+    for k in range(KPB):
+        total = jnp.zeros(owner.shape, jnp.float32)
+        for o in range(returned.shape[0]):
+            value = returned[o, 0, k : k + 1, :] + returned[o, 1, k : k + 1, :]
+            total = jnp.where(owner == o, value, total)
+        out[pl.ds(k, ACT, stride=KPB), :] = total
+
+
+def unpack(returned, slots):
+    tok_rows = slots.shape[1]
+    return pl.pallas_call(
+        unpack_kernel,
+        out_shape=jax.ShapeDtypeStruct((ACT * KPB, tok_rows), jnp.float32),
+        in_specs=[VMEM, VMEM],
+        out_specs=VMEM,
+        name="unpack",
+    )(kept(returned), slots).T
+
+
+def every_owner(decoder, grad_out, active_blocks, feature_idx, acts, block_slot):
+    half_width = grad_out.shape[1]
+    owners = lax.axis_size("dp")
+    ring = ring_of(owners)
+    onward = [(ring[i], ring[(i + 1) % owners]) for i in range(owners)]
+    back = [(there, here) for here, there in onward]
+
+    def hop(pieces):
+        left, right = pieces
+        return lax.ppermute(left, "dp", onward), lax.ppermute(right, "dp", back)
+
+    cut = half_width // 2
+    own = (grad_out[:, :cut], grad_out[:, cut:])
+    first_1 = hop(own)
+    second_1 = hop(own[::-1])
+    table, slots, decoder = prepare(
+        block_slot, active_blocks, feature_idx, acts, decoder, owners
+    )
+    first_1, table, slots, decoder = lax.optimization_barrier((first_1, table, slots, decoder))
+    first_2 = hop(first_1)
+    table = lax.all_to_all(table, "dp", 0, 0, tiled=True)
+    second_2 = hop(second_1)
+    first_3 = hop(first_2)
+    near = [own, (first_1[0], second_1[0]), (second_1[1], first_1[1])]
+    state = absorb((0, -1, 1), near, table, decoder)
+    state, second_2 = lax.optimization_barrier((state, second_2))
+    second_3 = hop(second_2)
+    state = absorb(
+        (-2, 2),
+        [(first_2[0], second_2[0]), (second_2[1], first_2[1])],
+        table,
+        decoder,
+        state,
+    )
+    state, first_3 = lax.optimization_barrier((state, first_3))
+    first_4 = hop(first_3)
+    state = absorb(
+        (-3, 3),
+        [(first_3[0], second_3[0]), (second_3[1], first_3[1])],
+        table,
+        decoder,
+        state,
+    )
+    state, first_4 = lax.optimization_barrier((state, first_4))
+    picked, total = state
+    picked = last_scores(4, first_4, table, decoder, picked)
+    sent = picked.reshape((2 * owners,) + picked.shape[2:])
+    returned = lax.all_to_all(sent, ("dp", "width"), 0, 0, tiled=True)
+    decoder_grad = last_gradients(4, first_4, table, total)
+    act_grad = unpack(returned.reshape(picked.shape), slots)
+    return (decoder_grad, act_grad)
 
 
 def send_back(picked):
@@ -22,7 +304,7 @@
     return (send_rows, send_acts, send_cols)
 
 
-def per_device(decoder, grad_out, active_blocks, feature_idx, acts, block_slot):
+def some_owners(decoder, grad_out, active_blocks, feature_idx, acts, block_slot):
     tok_rows, half_width = grad_out.shape
     owners = lax.axis_size("dp")
     mean_load = tok_rows * ACT // owners
@@ -86,6 +368,12 @@
     return (decoder_grad, act_grad)
 
 
+def per_device(*args):
+    if lax.axis_size("dp") == ACT:
+        return every_owner(*args)
+    return some_owners(*args)
+
+
 def solution(mesh):
     in_specs = (
         P(("groups", "dp"), "width"),

time: 260 us -> 69 us (0.27)
  waiting for transfers between devices: 116 us -> 13.7 us
  local copies, waits for them, and re-layouts: 82.4 us -> 5.18 us
  Pallas kernels: 0 us -> 17.3 us
  matrix products: 16.8 us -> 0 us
  other arithmetic: 16.3 us -> 0 us
  blocking collectives: 3.59 us -> 12.7 us
  starting transfers between devices: 22.9 us -> 18.9 us
    all_to_all x4 -> x1, waiting for transfers between devices: 116 us -> 2.9 us  [every_owner(): returned = lax.all_to_all(sent, ('dp', 'width'), 0, 0, tiled=True)]
    gather x5 -> x0, local copies, waits for them, and re-layouts: 52.8 us -> none  [the longest x3 43.1 us: per_device(): picked = jnp.take_along_axis(scores, feature_pos, axis=2)]
    all_to_all x4 -> x1, starting transfers between devices: 22.9 us -> 3.5 us  [every_owner(): returned = lax.all_to_all(sent, ('dp', 'width'), 0, 0, tiled=True)]
    pallas_call x0 -> x7, Pallas kernels: none -> 17.3 us  [the longest x3 9.66 us: absorb(): pl.pallas_call(functools.partial(absorb_kernel, distances, bool(state)),...]
    dot_general x2 -> x0, matrix products: 16.8 us -> none  [the longest x1 10.8 us: per_device(): jnp.einsum('bnf,bnd->bfd', dense, rows, preferred_element_type=jnp.float32)]
    scatter x4 -> x0, local copies, waits for them, and re-layouts: 15.6 us -> none  [the longest x1 4.34 us: pack_slots(): used = jnp.zeros((slots_all,), jnp.bool_).at[target].set(True)]
    ppermute x0 -> x14, starting transfers between devices: none -> 15.4 us  [hop(): return (lax.ppermute(left, 'dp', onward), lax.ppermute(right, 'dp', back))]
    all_to_all x0 -> x1, blocking collectives: none -> 12.7 us  [every_owner(): table = lax.all_to_all(table, 'dp', 0, 0, tiled=True)]
  transfers between devices with their start and end apart: 4 -> 15, of which waited for: 1 -> 8; matrix products, arithmetic and copies ran while one was open for 20% -> 0% of each run, Pallas kernels for 0% -> 20%
where the time goes in v3:
time: 69 us; the launch traced here: 68.4 us
  starting transfers between devices  18.9 us (27%)
  Pallas kernels  17.3 us (25%)
  waiting for transfers between devices  13.7 us (20%)
  blocking collectives  12.7 us (18%)
  local copies, waits for them, and re-layouts  5.18 us (8%)
  between operations  0.71 us (1%)
    ppermute x14, starting transfers between devices, hop(): return (lax.ppermute(left, 'dp', onward), lax.ppermute(right, 'dp', back))  15.4 us
    all_to_all x1, blocking collectives, every_owner(): table = lax.all_to_all(table, 'dp', 0, 0, tiled=True)  12.7 us
    ppermute x14, waiting for transfers between devices, hop(): return (lax.ppermute(left, 'dp', onward), lax.ppermute(right, 'dp', back))  10.8 us
    pallas_call x3, Pallas kernels, absorb(): pl.pallas_call(functools.partial(absorb_kernel, distances, bool(state)),...  9.66 us
    unnamed x6, local copies, waits for them, and re-layouts  4.12 us
    all_to_all x1, starting transfers between devices, every_owner(): returned = lax.all_to_all(sent, ('dp', 'width'), 0, 0, tiled=True)  3.5 us
    all_to_all x1, waiting for transfers between devices, every_owner(): returned = lax.all_to_all(sent, ('dp', 'width'), 0, 0, tiled=True)  2.9 us
    pallas_call x1, Pallas kernels, prepare(): pl.pallas_call(prepare_kernel, out_shape=(pltpu.VMEM((owners, 2 * KPB, to...  2.4 us
  transfers between devices with their start and end apart: 15, of which 8 were waited for; matrix products, arithmetic and copies ran while one was open for 0% of the time, Pallas kernels for 20%

profile of v3, /device:TPU:0, one launch (start us, length us, event | category | flops | bytes accessed | tf_op | source)
XLA Modules:
  0.0 68.4 jit_solution(8525656210833319444)
XLA Ops:
  0.6 1.1 %fusion = (bf16[128,1024]{1,0:T(8,128)(2,1)S(1)}, bf16[128,1024]{1,0:T(8,128)(2,1)S(1)}) fusion(bf16[128,2048]{1,0:T(8,128)(2,1)} %param.7), kind=kLoop, calls=%fused_computation | loop fusion | bytes 1048576 | tf_op jit(solution)/shard_map/slice | solution.py:253
  1.7 3.1 %collective-permute-start = (bf16[128,1024]{1,0:T(8,128)(2,1)S(1)}, bf16[128,1024]{1,0:T(8,128)(2,1)S(1)}, u32[]{:S(2)}, u32[]{:S(2)}) collective-permute-start(bf16[128,1024]{1,0:T(8,128)(2,1)S(1)} %get-tuple-element.55.refs_0_), channel_id=1, source_target_pairs={{0,4},{4,8},{8,12},{12,14},{14,10},{10,6},{6,2},{2,0},{1,5},{5,9},... | collective-permute-start | bytes 786440 | tf_op jit(solution)/shard_map/ppermute | solution.py:250
  4.8 0.0 collective-permute-start.1
  4.8 2.0 %collective-permute-start.3 = (bf16[128,1024]{1,0:T(8,128)(2,1)S(1)}, bf16[128,1024]{1,0:T(8,128)(2,1)S(1)}, u32[]{:S(2)}, u32[]{:S(2)}) collective-permute-start(bf16[128,1024]{1,0:T(8,128)(2,1)S(1)} %get-tuple-element.54.refs_1_), channel_id=1, source_target_pairs={{0,4},{4,8},{8,12},{12,14},{14,10},{10,6},{6,2},{2,0},{1,5},{5,9},... | collective-permute-start | bytes 786440 | tf_op jit(solution)/shard_map/ppermute | solution.py:250
  6.8 0.0 collective-permute-start.4
  6.8 2.4 %prepare.1 = (f32[8,8,128]{2,1,0:T(8,128)S(1)}, s32[8,128]{1,0:T(8,128)S(1)}, bf16[512,2048]{1,0:T(8,128)(2,1)S(1)}) custom-call(s32[32]{0:T(128)} %block_slot.1, s32[8,128]{1,0:T(8,128)} %bitcast.10, s32[32,128]{1,0:T(8,128)} %bitcast.7, bf16[32,128]{1,0:T(8,128)(2,1)} %bitcast.9, bf16[512,2048]{1,0:T(8,128)(2,1)} %decoder.1), custom_call_target="tpu_custom_call" | custom-call | tf_op jit(solution)/shard_map/prepare/pallas_call | solution.py:49
  9.2 0.0 copy-start.2
  9.2 2.6 %collective-permute-done.refs_2_ = bf16[128,1024]{1,0:T(8,128)(2,1)S(1)} collective-permute-done((bf16[128,1024]{1,0:T(8,128)(2,1)S(1)}, bf16[128,1024]{1,0:T(8,128)(2,1)S(1)}, u32[]{:S(2)}, u32[]{:S(2)}) %collective-permute-start) | collective-permute-done | bytes 262176 | tf_op jit(solution)/shard_map/ppermute | solution.py:250
  11.8 2.2 %collective-permute-done.1.refs_5_ = bf16[128,1024]{1,0:T(8,128)(2,1)S(1)} collective-permute-done((bf16[128,1024]{1,0:T(8,128)(2,1)S(1)}, bf16[128,1024]{1,0:T(8,128)(2,1)S(1)}, u32[]{:S(2)}, u32[]{:S(2)}) %collective-permute-start.1) | collective-permute-done | bytes 262176 | tf_op jit(solution)/shard_map/ppermute | solution.py:250
  14.0 1.6 %collective-permute-start.2 = (bf16[128,1024]{1,0:T(8,128)(2,1)S(1)}, bf16[128,1024]{1,0:T(8,128)(2,1)S(1)}, u32[]{:S(2)}, u32[]{:S(2)}) collective-permute-start(bf16[128,1024]{1,0:T(8,128)(2,1)S(1)} %collective-permute-done.refs_2_), channel_id=1, source_target_pairs={{0,4},{4,8},{8,12},{12,14},{14,10},{10,6},{6,2},{2,0},{1,5},{5,9},... | collective-permute-start | bytes 786440 | tf_op jit(solution)/shard_map/ppermute | solution.py:250
  15.6 0.4 collective-permute-start.7
  16.0 1.4 %collective-permute-done.3.refs_3_ = bf16[128,1024]{1,0:T(8,128)(2,1)S(1)} collective-permute-done((bf16[128,1024]{1,0:T(8,128)(2,1)S(1)}, bf16[128,1024]{1,0:T(8,128)(2,1)S(1)}, u32[]{:S(2)}, u32[]{:S(2)}) %collective-permute-start.3) | collective-permute-done | bytes 262176 | tf_op jit(solution)/shard_map/ppermute | solution.py:250
  17.4 2.1 %collective-permute-start.5 = (bf16[128,1024]{1,0:T(8,128)(2,1)S(1)}, bf16[128,1024]{1,0:T(8,128)(2,1)S(1)}, u32[]{:S(2)}, u32[]{:S(2)}) collective-permute-start(bf16[128,1024]{1,0:T(8,128)(2,1)S(1)} %collective-permute-done.3.refs_3_), channel_id=1, source_target_pairs={{0,4},{4,8},{8,12},{12,14},{14,10},{10,6},{6,2},{2,0},{1,5},{5,9},... | collective-permute-start | bytes 786440 | tf_op jit(solution)/shard_map/ppermute | solution.py:250
  19.6 0.1 collective-permute-done.4.refs_4_
  19.7 0.0 collective-permute-start.6
  19.7 3.5 %collective-permute-done.2.refs_0_ = bf16[128,1024]{1,0:T(8,128)(2,1)S(1)} collective-permute-done((bf16[128,1024]{1,0:T(8,128)(2,1)S(1)}, bf16[128,1024]{1,0:T(8,128)(2,1)S(1)}, u32[]{:S(2)}, u32[]{:S(2)}) %collective-permute-start.2) | collective-permute-done | bytes 262176 | tf_op jit(solution)/shard_map/ppermute | solution.py:250
  23.3 2.0 %collective-permute-start.8 = (bf16[128,1024]{1,0:T(8,128)(2,1)S(1)}, bf16[128,1024]{1,0:T(8,128)(2,1)S(1)}, u32[]{:S(2)}, u32[]{:S(2)}) collective-permute-start(bf16[128,1024]{1,0:T(8,128)(2,1)S(1)} %collective-permute-done.2.refs_0_), channel_id=1, source_target_pairs={{0,4},{4,8},{8,12},{12,14},{14,10},{10,6},{6,2},{2,0},{1,5},{5,9},... | collective-permute-start | bytes 786440 | tf_op jit(solution)/shard_map/ppermute | solution.py:250
  25.2 0.0 collective-permute-done.7.refs_3_
  25.2 0.0 copy-done.2
  25.2 0.1 collective-permute-start.9
  25.3 12.7 %all_to_all.10.table = f32[8,8,128]{2,1,0:T(8,128)S(1)} all-to-all(f32[8,8,128]{2,1,0:T(8,128)S(1)} %get-tuple-element.31), channel_id=1, replica_groups=mesh['groups'=2,'dp'=8,'width'=2] {'dp'}, dimensions={0} | all-to-all | bytes 65536 | tf_op jit(solution)/shard_map/all_to_all | solution.py:261
  38.0 3.4 %absorb.3 = (f32[8,2,8,128]{3,2,1,0:T(8,128)}, f32[512,2048]{1,0:T(8,128)S(1)}) custom-call(f32[8,8,128]{2,1,0:T(8,128)S(1)} %all_to_all.10.table, bf16[512,2048]{1,0:T(8,128)(2,1)S(1)} %get-tuple-element.32.decoder, bf16[128,1024]{1,0:T(8,128)(2,1)S(1)} %get-tuple-element.55.refs_0_, bf16[128,1024]{1,0:T(8,128)(2,1)S(1)} %get-tuple-element.54.refs_1_, ...), custom_call_target="tpu_custom_call" | custom-call | tf_op jit(solution)/shard_map/absorb/pallas_call | solution.py:159
  41.4 0.0 collective-permute-done.5.refs_1_
  41.4 0.0 collective-permute-done.6.refs_2_
  41.4 0.4 collective-permute-start.10
  41.9 1.6 %collective-permute-start.11 = (bf16[128,1024]{1,0:T(8,128)(2,1)S(1)}, bf16[128,1024]{1,0:T(8,128)(2,1)S(1)}, u32[]{:S(2)}, u32[]{:S(2)}) collective-permute-start(bf16[128,1024]{1,0:T(8,128)(2,1)S(1)} %collective-permute-done.6.refs_2_), channel_id=1, source_target_pairs={{4,0},{8,4},{12,8},{14,12},{10,14},{6,10},{2,6},{0,2},{5,1},{9,5},... | collective-permute-start | bytes 786440 | tf_op jit(solution)/shard_map/ppermute | solution.py:250
  43.5 3.1 %absorb.4 = (f32[8,2,8,128]{3,2,1,0:T(8,128)}, f32[512,2048]{1,0:T(8,128)S(1)}) custom-call(f32[8,8,128]{2,1,0:T(8,128)S(1)} %all_to_all.10.table, bf16[512,2048]{1,0:T(8,128)(2,1)S(1)} %get-tuple-element.32.decoder, bf16[128,1024]{1,0:T(8,128)(2,1)S(1)} %collective-permute-done.2.refs_0_, ...), custom_call_target="tpu_custom_call", output_to_operand_aliasing={{0}: (6, {}), {1}: (7, {})} | custom-call | tf_op jit(solution)/shard_map/absorb/pallas_call | solution.py:159
  46.6 0.0 collective-permute-done.8.refs_0_
  46.6 0.0 collective-permute-done.9.refs_3_
  46.6 0.4 collective-permute-start.12
  47.0 1.6 %collective-permute-start.13 = (bf16[128,1024]{1,0:T(8,128)(2,1)S(1)}, bf16[128,1024]{1,0:T(8,128)(2,1)S(1)}, u32[]{:S(2)}, u32[]{:S(2)}) collective-permute-start(bf16[128,1024]{1,0:T(8,128)(2,1)S(1)} %collective-permute-done.9.refs_3_), channel_id=1, source_target_pairs={{4,0},{8,4},{12,8},{14,12},{10,14},{6,10},{2,6},{0,2},{5,1},{9,5},... | collective-permute-start | bytes 786440 | tf_op jit(solution)/shard_map/ppermute | solution.py:250
  48.7 0.5 collective-permute-done.10.refs_1_
  49.2 0.4 collective-permute-done.11.refs_2_
  49.5 3.1 %absorb.5 = (f32[8,2,8,128]{3,2,1,0:T(8,128)}, f32[512,2048]{1,0:T(8,128)S(1)}) custom-call(f32[8,8,128]{2,1,0:T(8,128)S(1)} %all_to_all.10.table, bf16[512,2048]{1,0:T(8,128)(2,1)S(1)} %get-tuple-element.32.decoder, bf16[128,1024]{1,0:T(8,128)(2,1)S(1)} %collective-permute-done.8.refs_0_, ...), custom_call_target="tpu_custom_call", output_to_operand_aliasing={{0}: (6, {}), {1}: (7, {})} | custom-call | tf_op jit(solution)/shard_map/absorb/pallas_call | solution.py:159
  52.7 0.0 copy-start
  52.7 1.9 %copy-done = f32[512,2048]{1,0:T(8,128)} copy-done((f32[512,2048]{1,0:T(8,128)}, f32[512,2048]{1,0:T(8,128)S(1)}, u32[]{:S(2)}) %copy-start) | copy-done | bytes 4194328
  54.6 0.0 collective-permute-done.12.left
  54.6 0.0 collective-permute-done.13.right
  54.6 2.2 %last_scores.1 = f32[8,2,8,128]{3,2,1,0:T(8,128)} custom-call(f32[8,8,128]{2,1,0:T(8,128)S(1)} %all_to_all.10.table, bf16[512,2048]{1,0:T(8,128)(2,1)S(1)} %get-tuple-element.32.decoder, bf16[128,1024]{1,0:T(8,128)(2,1)S(1)} %collective-permute-done.12.left, bf16[128,1024]{1,0:T(8,128)(2,1)S(1)} %collective-permute-done.13.right, ...), custom_call_target="tpu_custom_call", output_to_operand_aliasing={{}: (4, {})} | custom-call | tf_op jit(solution)/shard_map/last_scores/pallas_call | solution.py:179
  56.8 3.5 %all-to-all-start.1 = ((f32[16,8,128]{2,1,0:T(8,128)}), f32[16,8,128]{2,1,0:T(8,128)S(1)}, u32[]{:S(2)}, u32[]{:S(2)}) async-start(f32[16,8,128]{2,1,0:T(8,128)} %bitcast.3), calls=%async_computation.1 | async-start | bytes 131072 | tf_op jit(solution)/shard_map/all_to_all | solution.py:288
  60.3 0.0 copy-start.1
  60.3 2.2 %copy-done.1 = f32[512,2048]{1,0:T(8,128)S(1)} copy-done((f32[512,2048]{1,0:T(8,128)S(1)}, f32[512,2048]{1,0:T(8,128)}, u32[]{:S(2)}) %copy-start.1) | copy-done | bytes 4194328
  62.5 1.8 %last_gradients.1 = bf16[512,2048]{1,0:T(8,128)(2,1)} custom-call(f32[8,8,128]{2,1,0:T(8,128)S(1)} %all_to_all.10.table, bf16[128,1024]{1,0:T(8,128)(2,1)S(1)} %collective-permute-done.12.left, bf16[128,1024]{1,0:T(8,128)(2,1)S(1)} %collective-permute-done.13.right, f32[512,2048]{1,0:T(8,128)S(1)} %copy-done.1), custom_call_target="tpu_custom_call" | custom-call | tf_op jit(solution)/shard_map/last_gradients/pallas_call | solution.py:206
  64.2 2.9 %all-to-all-done.1 = f32[16,8,128]{2,1,0:T(8,128)S(1)} async-done(((f32[16,8,128]{2,1,0:T(8,128)}), f32[16,8,128]{2,1,0:T(8,128)S(1)}, u32[]{:S(2)}, u32[]{:S(2)}) %all-to-all-start.1) | async-done | bytes 65568 | tf_op jit(solution)/shard_map/all_to_all | solution.py:288
  67.1 1.3 %unpack.1 = f32[32,128]{1,0:T(8,128)} custom-call(f32[8,2,8,128]{3,2,1,0:T(8,128)S(1)} %bitcast.6, s32[8,128]{1,0:T(8,128)} %copy-done.2), custom_call_target="tpu_custom_call" | custom-call | tf_op jit(solution)/shard_map/unpack/pallas_call | solution.py:232
Async XLA Ops:
  1.7 10.1 %collective-permute-start = (bf16[128,1024]{1,0:T(8,128)(2,1)S(1)}, bf16[128,1024]{1,0:T(8,128)(2,1)S(1)}, u32[]{:S(2)}, u32[]{:S(2)}) collective-permute-start(bf16[128,1024]{1,0:T(8,128)(2,1)S(1)} %get-tuple-element.55.refs_0_), channel_id=1, source_target_pairs={{0,4},{4,8},{8,12},{12,14},{14,10},{10,6},{6,2},{2,0},{1,5},{5,9},... | collective-permute-start | bytes 786440 | tf_op jit(solution)/shard_map/ppermute | solution.py:250
  4.8 9.2 %collective-permute-start.1 = (bf16[128,1024]{1,0:T(8,128)(2,1)S(1)}, bf16[128,1024]{1,0:T(8,128)(2,1)S(1)}, u32[]{:S(2)}, u32[]{:S(2)}) collective-permute-start(bf16[128,1024]{1,0:T(8,128)(2,1)S(1)} %get-tuple-element.54.refs_1_), channel_id=1, source_target_pairs={{4,0},{8,4},{12,8},{14,12},{10,14},{6,10},{2,6},{0,2},{5,1},{9,5},... | collective-permute-start | bytes 786440 | tf_op jit(solution)/shard_map/ppermute | solution.py:250
  4.8 12.7 %collective-permute-start.3 = (bf16[128,1024]{1,0:T(8,128)(2,1)S(1)}, bf16[128,1024]{1,0:T(8,128)(2,1)S(1)}, u32[]{:S(2)}, u32[]{:S(2)}) collective-permute-start(bf16[128,1024]{1,0:T(8,128)(2,1)S(1)} %get-tuple-element.54.refs_1_), channel_id=1, source_target_pairs={{0,4},{4,8},{8,12},{12,14},{14,10},{10,6},{6,2},{2,0},{1,5},{5,9},... | collective-permute-start | bytes 786440 | tf_op jit(solution)/shard_map/ppermute | solution.py:250
  6.8 12.9 %collective-permute-start.4 = (bf16[128,1024]{1,0:T(8,128)(2,1)S(1)}, bf16[128,1024]{1,0:T(8,128)(2,1)}, u32[]{:S(2)}, u32[]{:S(2)}) collective-permute-start(bf16[128,1024]{1,0:T(8,128)(2,1)S(1)} %get-tuple-element.55.refs_0_), channel_id=1, source_target_pairs={{4,0},{8,4},{12,8},{14,12},{10,14},{6,10},{2,6},{0,2},{5,1},{9,5},... | collective-permute-start | bytes 786440 | tf_op jit(solution)/shard_map/ppermute | solution.py:250
  9.2 16.0 %copy-start.2 = (s32[8,128]{1,0:T(8,128)}, s32[8,128]{1,0:T(8,128)S(1)}, u32[]{:S(2)}) copy-start(s32[8,128]{1,0:T(8,128)S(1)} %get-tuple-element.53.slots) | copy-start | bytes 12292
  14.0 9.2 %collective-permute-start.2 = (bf16[128,1024]{1,0:T(8,128)(2,1)S(1)}, bf16[128,1024]{1,0:T(8,128)(2,1)S(1)}, u32[]{:S(2)}, u32[]{:S(2)}) collective-permute-start(bf16[128,1024]{1,0:T(8,128)(2,1)S(1)} %collective-permute-done.refs_2_), channel_id=1, source_target_pairs={{0,4},{4,8},{8,12},{12,14},{14,10},{10,6},{6,2},{2,0},{1,5},{5,9},... | collective-permute-start | bytes 786440 | tf_op jit(solution)/shard_map/ppermute | solution.py:250
  15.6 9.7 %collective-permute-start.7 = (bf16[128,1024]{1,0:T(8,128)(2,1)S(1)}, bf16[128,1024]{1,0:T(8,128)(2,1)S(1)}, u32[]{:S(2)}, u32[]{:S(2)}) collective-permute-start(bf16[128,1024]{1,0:T(8,128)(2,1)S(1)} %collective-permute-done.1.refs_5_), channel_id=1, source_target_pairs={{4,0},{8,4},{12,8},{14,12},{10,14},{6,10},{2,6},{0,2},{5,1},{9,5},... | collective-permute-start | bytes 786440 | tf_op jit(solution)/shard_map/ppermute | solution.py:250
  17.4 24.0 %collective-permute-start.5 = (bf16[128,1024]{1,0:T(8,128)(2,1)S(1)}, bf16[128,1024]{1,0:T(8,128)(2,1)S(1)}, u32[]{:S(2)}, u32[]{:S(2)}) collective-permute-start(bf16[128,1024]{1,0:T(8,128)(2,1)S(1)} %collective-permute-done.3.refs_3_), channel_id=1, source_target_pairs={{0,4},{4,8},{8,12},{12,14},{14,10},{10,6},{6,2},{2,0},{1,5},{5,9},... | collective-permute-start | bytes 786440 | tf_op jit(solution)/shard_map/ppermute | solution.py:250
  19.7 21.7 %collective-permute-start.6 = (bf16[128,1024]{1,0:T(8,128)(2,1)}, bf16[128,1024]{1,0:T(8,128)(2,1)S(1)}, u32[]{:S(2)}, u32[]{:S(2)}) collective-permute-start(bf16[128,1024]{1,0:T(8,128)(2,1)} %collective-permute-done.4.refs_4_), channel_id=1, source_target_pairs={{4,0},{8,4},{12,8},{14,12},{10,14},{6,10},{2,6},{0,2},{5,1},{9,5},... | collective-permute-start | bytes 786440 | tf_op jit(solution)/shard_map/ppermute | solution.py:250
  23.3 23.4 %collective-permute-start.8 = (bf16[128,1024]{1,0:T(8,128)(2,1)S(1)}, bf16[128,1024]{1,0:T(8,128)(2,1)S(1)}, u32[]{:S(2)}, u32[]{:S(2)}) collective-permute-start(bf16[128,1024]{1,0:T(8,128)(2,1)S(1)} %collective-permute-done.2.refs_0_), channel_id=1, source_target_pairs={{0,4},{4,8},{8,12},{12,14},{14,10},{10,6},{6,2},{2,0},{1,5},{5,9},... | collective-permute-start | bytes 786440 | tf_op jit(solution)/shard_map/ppermute | solution.py:250
  25.2 21.4 %collective-permute-start.9 = (bf16[128,1024]{1,0:T(8,128)(2,1)S(1)}, bf16[128,1024]{1,0:T(8,128)(2,1)S(1)}, u32[]{:S(2)}, u32[]{:S(2)}) collective-permute-start(bf16[128,1024]{1,0:T(8,128)(2,1)S(1)} %collective-permute-done.7.refs_3_), channel_id=1, source_target_pairs={{4,0},{8,4},{12,8},{14,12},{10,14},{6,10},{2,6},{0,2},{5,1},{9,5},... | collective-permute-start | bytes 786440 | tf_op jit(solution)/shard_map/ppermute | solution.py:250
  41.4 7.8 %collective-permute-start.10 = (bf16[128,1024]{1,0:T(8,128)(2,1)S(1)}, bf16[128,1024]{1,0:T(8,128)(2,1)S(1)}, u32[]{:S(2)}, u32[]{:S(2)}) collective-permute-start(bf16[128,1024]{1,0:T(8,128)(2,1)S(1)} %collective-permute-done.5.refs_1_), channel_id=1, source_target_pairs={{0,4},{4,8},{8,12},{12,14},{14,10},{10,6},{6,2},{2,0},{1,5},{5,9},... | collective-permute-start | bytes 786440 | tf_op jit(solution)/shard_map/ppermute | solution.py:250
  41.9 7.7 %collective-permute-start.11 = (bf16[128,1024]{1,0:T(8,128)(2,1)S(1)}, bf16[128,1024]{1,0:T(8,128)(2,1)S(1)}, u32[]{:S(2)}, u32[]{:S(2)}) collective-permute-start(bf16[128,1024]{1,0:T(8,128)(2,1)S(1)} %collective-permute-done.6.refs_2_), channel_id=1, source_target_pairs={{4,0},{8,4},{12,8},{14,12},{10,14},{6,10},{2,6},{0,2},{5,1},{9,5},... | collective-permute-start | bytes 786440 | tf_op jit(solution)/shard_map/ppermute | solution.py:250
  46.6 8.0 %collective-permute-start.12 = (bf16[128,1024]{1,0:T(8,128)(2,1)S(1)}, bf16[128,1024]{1,0:T(8,128)(2,1)S(1)}, u32[]{:S(2)}, u32[]{:S(2)}) collective-permute-start(bf16[128,1024]{1,0:T(8,128)(2,1)S(1)} %collective-permute-done.8.refs_0_), channel_id=1, source_target_pairs={{0,4},{4,8},{8,12},{12,14},{14,10},{10,6},{6,2},{2,0},{1,5},{5,9},... | collective-permute-start | bytes 786440 | tf_op jit(solution)/shard_map/ppermute | solution.py:250
  47.0 7.6 %collective-permute-start.13 = (bf16[128,1024]{1,0:T(8,128)(2,1)S(1)}, bf16[128,1024]{1,0:T(8,128)(2,1)S(1)}, u32[]{:S(2)}, u32[]{:S(2)}) collective-permute-start(bf16[128,1024]{1,0:T(8,128)(2,1)S(1)} %collective-permute-done.9.refs_3_), channel_id=1, source_target_pairs={{4,0},{8,4},{12,8},{14,12},{10,14},{6,10},{2,6},{0,2},{5,1},{9,5},... | collective-permute-start | bytes 786440 | tf_op jit(solution)/shard_map/ppermute | solution.py:250
  52.7 1.9 %copy-start = (f32[512,2048]{1,0:T(8,128)}, f32[512,2048]{1,0:T(8,128)S(1)}, u32[]{:S(2)}) copy-start(f32[512,2048]{1,0:T(8,128)S(1)} %get-tuple-element.51.total) | copy-start | bytes 12582916
  56.8 10.4 %all-to-all-start.1 = ((f32[16,8,128]{2,1,0:T(8,128)}), f32[16,8,128]{2,1,0:T(8,128)S(1)}, u32[]{:S(2)}, u32[]{:S(2)}) async-start(f32[16,8,128]{2,1,0:T(8,128)} %bitcast.3), calls=%async_computation.1 | async-start | bytes 131072 | tf_op jit(solution)/shard_map/all_to_all | solution.py:288
  60.3 2.2 %copy-start.1 = (f32[512,2048]{1,0:T(8,128)S(1)}, f32[512,2048]{1,0:T(8,128)}, u32[]{:S(2)}) copy-start(f32[512,2048]{1,0:T(8,128)} %copy-done) | copy-start | bytes 12582916

commit v4 on v3

--- a/solution.py
+++ b/solution.py
@@ -14,53 +14,14 @@
 SMEM = pl.BlockSpec(memory_space=pltpu.SMEM)
 VMEM = pl.BlockSpec(memory_space=pltpu.VMEM)
 ANY = pl.BlockSpec(memory_space=pl.ANY)
-LIMIT = pltpu.CompilerParams(vmem_limit_bytes=40 * 2**20)
+
+
+def limit(mebibytes):
+    return pltpu.CompilerParams(vmem_limit_bytes=mebibytes * 2**20)
 
 
 def kept(x):
     return pltpu.with_memory_space_constraint(x, pltpu.VMEM)
-
-
-def prepare_kernel(
-    block_slot, active, feats, acts, decoder, table, slots, decoder_here, wide_acts, sem
-):
-    load = pltpu.make_async_copy(decoder, decoder_here, sem)
-    load.start()
-    named = active[...]
-    slot = jnp.zeros_like(named)
-    for block in range(block_slot.shape[0]):
-        slot = jnp.where(named == block, block_slot[block], slot)
-    slots[...] = slot
-    wide_acts[...] = acts[...].astype(jnp.float32)
-    owner = slot // BLK_DEV
-    first_row = slot % BLK_DEV * BW
-    for k in range(KPB):
-        at_row = (first_row + feats[pl.ds(k, ACT, stride=KPB), :]).astype(jnp.float32)
-        coeff = wide_acts[pl.ds(k, ACT, stride=KPB), :]
-        for o in range(table.shape[0]):
-            mine = owner == o
-            table[o, k, :] = jnp.sum(jnp.where(mine, at_row, 0.0), axis=0)
-            table[o, KPB + k, :] = jnp.sum(jnp.where(mine, coeff, 0.0), axis=0)
-    load.wait()
-
-
-def prepare(block_slot, active_blocks, feature_idx, acts, decoder, owners):
-    tok_rows = active_blocks.shape[0]
-    return pl.pallas_call(
-        prepare_kernel,
-        out_shape=(
-            pltpu.VMEM((owners, 2 * KPB, tok_rows), jnp.float32),
-            pltpu.VMEM((ACT, tok_rows), jnp.int32),
-            pltpu.VMEM(decoder.shape, decoder.dtype),
-        ),
-        in_specs=[SMEM, VMEM, VMEM, VMEM, ANY],
-        out_specs=(VMEM, VMEM, VMEM),
-        scratch_shapes=[
-            pltpu.VMEM((ACT * KPB, tok_rows), jnp.float32),
-            pltpu.SemaphoreType.DMA,
-        ],
-        name="prepare",
-    )(block_slot, active_blocks.T, feature_idx.T, acts.T, decoder)
 
 
 def ring_of(owners):
@@ -75,8 +36,109 @@
     return jnp.where(at < half_ring, 2 * at, 2 * (owners - 1 - at) + 1)
 
 
+ROW_SHIFT = BLK_DEV * BW // 2
+
+
+def facts_for(owner_id, owner, first_row, feats, acts):
+    mine = owner == owner_id
+    rows = [
+        jnp.sum(jnp.where(mine, first_row + feats[k], 0.0), axis=0, keepdims=True) - ROW_SHIFT
+        for k in range(KPB)
+    ]
+    values = [
+        jnp.sum(jnp.where(mine, acts[k], 0.0), axis=0, keepdims=True) for k in range(KPB)
+    ]
+    return jnp.concatenate(rows + values, axis=0)
+
+
+def prepare_kernel(
+    owners, block_slot, active, feats, acts, grad_out,
+    left, right, own_facts, slots, wide_feats, wide_acts, sems,
+):
+    tok_rows, width = grad_out.shape
+    parts = width // 256
+    copies = []
+    for j in range(parts):
+        for target, side in ((left, 0), (right, 1)):
+            column = (side * parts + j) * 128
+            copies.append(
+                pltpu.make_async_copy(
+                    grad_out.at[:, column : column + 128],
+                    target.at[j * tok_rows : (j + 1) * tok_rows, :],
+                    sems.at[len(copies)],
+                )
+            )
+            copies[-1].start()
+    named = active[...]
+    slot = jnp.zeros_like(named)
+    for block in range(block_slot.shape[0]):
+        slot = jnp.where(named == block, block_slot[block], slot)
+    slots[...] = slot
+    wide_feats[...] = feats[...].astype(jnp.float32)
+    wide_acts[...] = acts[...].astype(jnp.float32)
+    features = [wide_feats[pl.ds(k, ACT, stride=KPB), :] for k in range(KPB)]
+    values = [wide_acts[pl.ds(k, ACT, stride=KPB), :] for k in range(KPB)]
+    first_row = (slot % BLK_DEV * BW).astype(jnp.float32)
+
+    def facts(distance):
+        return facts_for(
+            peer_at(distance, owners), slot // BLK_DEV, first_row, features, values
+        )
+
+    reach = owners // 2
+    own_facts[...] = facts(0)
+    start = parts * tok_rows
+    for target, sign in ((left, 1), (right, -1)):
+        ahead = [facts(sign * d) for d in range(1, reach + 1)]
+        target[start:, :] = jnp.concatenate(ahead, axis=0).astype(jnp.bfloat16)
+    for copy in copies:
+        copy.wait()
+
+
+def prepare(block_slot, active_blocks, feature_idx, acts, grad_out, owners):
+    tok_rows, half_width = grad_out.shape
+    plain = half_width // 256 * tok_rows
+    extra = owners // 2 * 2 * KPB
+    return pl.pallas_call(
+        functools.partial(prepare_kernel, owners),
+        out_shape=(
+            pltpu.VMEM((plain + extra, 128), grad_out.dtype),
+            pltpu.VMEM((plain + extra, 128), grad_out.dtype),
+            pltpu.VMEM((2 * KPB, tok_rows), jnp.float32),
+            pltpu.VMEM((ACT, tok_rows), jnp.int32),
+        ),
+        in_specs=[SMEM, VMEM, VMEM, VMEM, ANY],
+        out_specs=(VMEM,) * 4,
+        scratch_shapes=[
+            pltpu.VMEM((ACT * KPB, tok_rows), jnp.float32),
+            pltpu.VMEM((ACT * KPB, tok_rows), jnp.float32),
+            pltpu.SemaphoreType.DMA((half_width // 128,)),
+        ],
+        compiler_params=limit(8),
+        name="prepare",
+    )(block_slot, active_blocks.T, feature_idx.T, acts.T, grad_out)
+
+
+def fetch_kernel(source, target, sem):
+    copy = pltpu.make_async_copy(source, target, sem)
+    copy.start()
+    copy.wait()
+
+
+def fetch(x):
+    return pl.pallas_call(
+        fetch_kernel,
+        out_shape=pltpu.VMEM(x.shape, x.dtype),
+        in_specs=[ANY],
+        out_specs=VMEM,
+        scratch_shapes=[pltpu.SemaphoreType.DMA],
+        compiler_params=limit(8),
+        name="fetch",
+    )(x)
+
+
 def block_and_rows(here):
-    at_row = here[:KPB].astype(jnp.int32)
+    at_row = here[:KPB].astype(jnp.int32) + ROW_SHIFT
     return at_row[:1] // BW, at_row % BW
 
 
@@ -106,56 +168,78 @@
     ]
 
 
-def add_picks(peers, table, decoder, chunks, picked):
-    tok_rows, cut = chunks[0].shape
+def facts_in(piece, distance, tok_rows):
+    extra = 2 * KPB * (lax.axis_size("dp") // 2)
+    facts = piece[piece.shape[0] - extra :, :].astype(jnp.float32)
+    return facts[(abs(distance) - 1) * 2 * KPB : abs(distance) * 2 * KPB]
+
+
+def columns_of(pieces, tok_rows, parts):
+    rows = [
+        jnp.concatenate([piece[j * tok_rows : (j + 1) * tok_rows, :] for j in parts], axis=1)
+        for piece in pieces
+    ]
+    return jnp.concatenate(rows, axis=0) if len(rows) > 1 else rows[0]
+
+
+def add_picks(peers, facts, decoder, pieces, picked):
+    tok_rows = facts[0].shape[1]
+    cut = decoder.shape[1] // 2
     for first in range(0, len(peers), 2):
         some = peers[first : first + 2]
         scores = None
         for side in range(2):
-            halves = [chunks[2 * (first + i) + side][...] for i in range(len(some))]
-            rows = jnp.concatenate(halves, axis=0) if len(halves) > 1 else halves[0]
             part = lax.dot_general(
                 decoder[:, side * cut : (side + 1) * cut],
-                rows,
+                columns_of(
+                    pieces[2 * first + side : 2 * (first + len(some)) : 2],
+                    tok_rows,
+                    range(cut // 128),
+                ),
                 (((1,), (1,)), ((), ())),
                 preferred_element_type=jnp.float32,
             )
             scores = part if scores is None else scores + part
         for i, peer in enumerate(some):
-            values = pick(scores[:, i * tok_rows : (i + 1) * tok_rows], table[peer])
+            values = pick(scores[:, i * tok_rows : (i + 1) * tok_rows], facts[first + i])
             for k in range(KPB):
                 for width in range(2):
                     picked[peer, width, k, :] = values[k]
 
 
-def gradient_blocks(peers, table, chunks, block):
-    cut = chunks[0].shape[1]
-    dense = jnp.concatenate([coefficients(table[peer]) for peer in peers], axis=1)
+def gradient_blocks(facts, pieces, width):
+    tok_rows = facts[0].shape[1]
+    cut = width // 2
+    dense = jnp.concatenate([coefficients(here) for here in facts], axis=1)
     for side in range(2):
-        for start in range(0, cut, block):
-            rows = jnp.concatenate(
-                [half[:, start : start + block] for half in chunks[side::2]], axis=0
-            )
+        for j in range(0, cut // 128, 2):
+            rows = columns_of(pieces[side::2], tok_rows, (j, j + 1))
             part = jnp.dot(dense, rows, preferred_element_type=jnp.float32)
-            yield slice(side * cut + start, side * cut + start + block), part
-
-
-def absorb_kernel(distances, later, table, decoder, *refs):
+            yield slice(side * cut + j * 128, side * cut + (j + 2) * 128), part
+
+
+def absorb_kernel(distances, later, decoder, own_facts, *refs):
     count = len(distances)
-    chunks, refs = refs[: 2 * count], refs[2 * count :]
+    pieces, refs = refs[: 2 * count], refs[2 * count :]
     picked, total = refs[-2:]
-    peers = [peer_at(d, table.shape[0]) for d in distances]
+    owners, _, _, tok_rows = picked.shape
+    peers = [peer_at(d, owners) for d in distances]
+    facts = [
+        own_facts[...] if d == 0 else facts_in(pieces[2 * i + (d > 0)], d, tok_rows)
+        for i, d in enumerate(distances)
+    ]
     picked[...] = refs[0][...] if later else jnp.zeros_like(picked)
-    add_picks(peers, table, decoder, chunks, picked)
-    for columns, part in gradient_blocks(peers, table, chunks, 256):
+    add_picks(peers, facts, decoder, pieces, picked)
+    for columns, part in gradient_blocks(facts, pieces, decoder.shape[1]):
         total[:, columns] = refs[1][:, columns] + part if later else part
 
 
-def absorb(distances, chunks, table, decoder, state=()):
-    owners, _, tok_rows = table.shape
-    operands = [kept(table), decoder]
-    operands += [kept(half) for pair in chunks for half in pair]
-    operands += state
+def absorb(distances, pairs, decoder, own_facts, state=()):
+    tok_rows = own_facts.shape[1]
+    owners = lax.axis_size("dp")
+    operands = [kept(decoder), kept(own_facts)]
+    operands += [kept(piece) for pair in pairs for piece in pair]
+    operands += [kept(x) for x in state]
     return pl.pallas_call(
         functools.partial(absorb_kernel, distances, bool(state)),
         out_shape=(
@@ -165,32 +249,34 @@
         in_specs=[VMEM] * len(operands),
         out_specs=(VMEM, VMEM),
         input_output_aliases={len(operands) - 2: 0, len(operands) - 1: 1} if state else {},
-        compiler_params=LIMIT,
+        compiler_params=limit(16),
         name="absorb",
     )(*operands)
 
 
-def last_scores_kernel(distance, table, decoder, left, right, before, picked):
+def last_scores_kernel(distance, decoder, left, right, before, picked):
     picked[...] = before[...]
-    add_picks([peer_at(distance, table.shape[0])], table, decoder, (left, right), picked)
-
-
-def last_scores(distance, chunk, table, decoder, picked):
+    owners, _, _, tok_rows = picked.shape
+    facts = [facts_in(left, distance, tok_rows)]
+    add_picks([peer_at(distance, owners)], facts, decoder, (left, right), picked)
+
+
+def last_scores(distance, pair, decoder, picked):
     return pl.pallas_call(
         functools.partial(last_scores_kernel, distance),
         out_shape=pltpu.VMEM(picked.shape, picked.dtype),
-        in_specs=[VMEM] * 5,
+        in_specs=[VMEM] * 4,
         out_specs=VMEM,
-        input_output_aliases={4: 0},
-        compiler_params=LIMIT,
+        input_output_aliases={3: 0},
+        compiler_params=limit(12),
         name="last_scores",
-    )(kept(table), decoder, kept(chunk[0]), kept(chunk[1]), picked)
-
-
-def last_gradients_kernel(distance, table, left, right, total, out, rounded, sems):
-    peer = peer_at(distance, table.shape[0])
+    )(kept(decoder), kept(pair[0]), kept(pair[1]), kept(picked))
+
+
+def last_gradients_kernel(distance, tok_rows, left, right, total, out, rounded, sems):
+    facts = [facts_in(left, distance, tok_rows)]
     copies = []
-    for columns, part in gradient_blocks([peer], table, (left, right), 256):
+    for columns, part in gradient_blocks(facts, (left, right), out.shape[1]):
         rounded[:, columns] = (total[:, columns] + part).astype(out.dtype)
         copies.append(
             pltpu.make_async_copy(
@@ -202,19 +288,19 @@
         copy.wait()
 
 
-def last_gradients(distance, chunk, table, total):
-    return pl.pallas_call(
-        functools.partial(last_gradients_kernel, distance),
+def last_gradients(distance, pair, total, tok_rows):
+    return pl.pallas_call(
+        functools.partial(last_gradients_kernel, distance, tok_rows),
         out_shape=jax.ShapeDtypeStruct(total.shape, jnp.bfloat16),
-        in_specs=[VMEM] * 4,
+        in_specs=[VMEM] * 3,
         out_specs=ANY,
         scratch_shapes=[
             pltpu.VMEM(total.shape, jnp.bfloat16),
             pltpu.SemaphoreType.DMA((total.shape[1] // 256,)),
         ],
-        compiler_params=LIMIT,
+        compiler_params=limit(16),
         name="last_gradients",
-    )(kept(table), kept(chunk[0]), kept(chunk[1]), total)
+    )(kept(pair[0]), kept(pair[1]), kept(total))
 
 
 def unpack_kernel(returned, slots, out):
@@ -234,12 +320,12 @@
         out_shape=jax.ShapeDtypeStruct((ACT * KPB, tok_rows), jnp.float32),
         in_specs=[VMEM, VMEM],
         out_specs=VMEM,
+        compiler_params=limit(4),
         name="unpack",
-    )(kept(returned), slots).T
+    )(kept(returned), kept(slots)).T
 
 
 def every_owner(decoder, grad_out, active_blocks, feature_idx, acts, block_slot):
-    half_width = grad_out.shape[1]
     owners = lax.axis_size("dp")
     ring = ring_of(owners)
     onward = [(ring[i], ring[(i + 1) % owners]) for i in range(owners)]
@@ -249,44 +335,36 @@
         left, right = pieces
         return lax.ppermute(left, "dp", onward), lax.ppermute(right, "dp", back)
 
-    cut = half_width // 2
-    own = (grad_out[:, :cut], grad_out[:, cut:])
-    first_1 = hop(own)
-    second_1 = hop(own[::-1])
-    table, slots, decoder = prepare(
-        block_slot, active_blocks, feature_idx, acts, decoder, owners
-    )
-    first_1, table, slots, decoder = lax.optimization_barrier((first_1, table, slots, decoder))
+    def crossed(pieces):
+        right, left = pieces
+        right, left = lax.ppermute(right, "dp", onward), lax.ppermute(left, "dp", back)
+        return right, left
+
+    left, right, own_facts, slots = prepare(
+        block_slot, active_blocks, feature_idx, acts, grad_out, owners
+    )
+    first_1 = hop((left, right))
+    second_1 = crossed((right, left))
+    decoder = fetch(decoder)
+    first_1, decoder = lax.optimization_barrier((first_1, decoder))
     first_2 = hop(first_1)
-    table = lax.all_to_all(table, "dp", 0, 0, tiled=True)
-    second_2 = hop(second_1)
+    second_2 = crossed(second_1)
+    near = [(left, right), (first_1[0], second_1[0]), (second_1[1], first_1[1])]
+    state = absorb((0, -1, 1), near, decoder, own_facts)
     first_3 = hop(first_2)
-    near = [own, (first_1[0], second_1[0]), (second_1[1], first_1[1])]
-    state = absorb((0, -1, 1), near, table, decoder)
     state, second_2 = lax.optimization_barrier((state, second_2))
-    second_3 = hop(second_2)
-    state = absorb(
-        (-2, 2),
-        [(first_2[0], second_2[0]), (second_2[1], first_2[1])],
-        table,
-        decoder,
-        state,
-    )
+    second_3 = crossed(second_2)
+    far = [(first_2[0], second_2[0]), (second_2[1], first_2[1])]
+    state = absorb((-2, 2), far, decoder, own_facts, state)
     state, first_3 = lax.optimization_barrier((state, first_3))
     first_4 = hop(first_3)
-    state = absorb(
-        (-3, 3),
-        [(first_3[0], second_3[0]), (second_3[1], first_3[1])],
-        table,
-        decoder,
-        state,
-    )
-    state, first_4 = lax.optimization_barrier((state, first_4))
-    picked, total = state
-    picked = last_scores(4, first_4, table, decoder, picked)
+    farther = [(first_3[0], second_3[0]), (second_3[1], first_3[1])]
+    state = absorb((-3, 3), farther, decoder, own_facts, state)
+    (picked, total), first_4 = lax.optimization_barrier((state, first_4))
+    picked = last_scores(4, first_4, decoder, picked)
     sent = picked.reshape((2 * owners,) + picked.shape[2:])
     returned = lax.all_to_all(sent, ("dp", "width"), 0, 0, tiled=True)
-    decoder_grad = last_gradients(4, first_4, table, total)
+    decoder_grad = last_gradients(4, first_4, total, grad_out.shape[0])
     act_grad = unpack(returned.reshape(picked.shape), slots)
     return (decoder_grad, act_grad)
 

time: 69 us -> 67.2 us (0.974)
  blocking collectives: 12.7 us -> 0 us
  waiting for transfers between devices: 13.7 us -> 21.2 us
  local copies, waits for them, and re-layouts: 5.18 us -> 9.51 us
  Pallas kernels: 17.3 us -> 14.8 us
  starting transfers between devices: 18.9 us -> 20.4 us
    all_to_all x1 -> x0, blocking collectives: 12.7 us -> none  [every_owner(): table = lax.all_to_all(table, 'dp', 0, 0, tiled=True)]
    ppermute x0 -> x6, waiting for transfers between devices: none -> 8.37 us  [the longest x3 4.4 us: crossed(): lax.ppermute(left, 'dp', back)]
    ppermute x0 -> x6, starting transfers between devices: none -> 6.2 us  [the longest x3 5.74 us: crossed(): lax.ppermute(right, 'dp', onward)]
    ppermute x14 -> x8, starting transfers between devices: 15.4 us -> 9.28 us  [hop(): return (lax.ppermute(left, 'dp', onward), lax.ppermute(right, 'dp', back))]
    unnamed x6 -> x16, local copies, waits for them, and re-layouts: 4.12 us -> 9.51 us
    all_to_all x1, starting transfers between devices: 3.5 us -> 4.9 us  [every_owner(): returned = lax.all_to_all(sent, ('dp', 'width'), 0, 0, tiled=True)]
    pallas_call x2 -> x3, Pallas kernels: 4.16 us -> 2.85 us  [the longest x1 1.74 us: last_gradients(): pl.pallas_call(functools.partial(last_gradients_kernel, distance, tok_row...]
    slice x1 -> x0, local copies, waits for them, and re-layouts: 1.07 us -> none  [every_owner(): own = (grad_out[:, :cut], grad_out[:, cut:])]
  transfers between devices with their start and end apart: 15 -> 15, of which waited for: 8 -> 10; matrix products, arithmetic and copies ran while one was open for 0% -> 0% of each run, Pallas kernels for 20% -> 17%
where the time goes in v4:
time: 67.2 us; the launch traced here: 66.6 us
  waiting for transfers between devices  21.2 us (32%)
  starting transfers between devices  20.4 us (30%)
  Pallas kernels  14.8 us (22%)
  local copies, waits for them, and re-layouts  9.51 us (14%)
  between operations  0.7 us (1%)
    ppermute x8, waiting for transfers between devices, hop(): return (lax.ppermute(left, 'dp', onward), lax.ppermute(right, 'dp', back))  9.89 us
    unnamed x16, local copies, waits for them, and re-layouts  9.51 us
    ppermute x8, starting transfers between devices, hop(): return (lax.ppermute(left, 'dp', onward), lax.ppermute(right, 'dp', back))  9.28 us
    pallas_call x3, Pallas kernels, absorb(): pl.pallas_call(functools.partial(absorb_kernel, distances, bool(state)),...  9.13 us
    ppermute x3, starting transfers between devices, crossed(): lax.ppermute(right, 'dp', onward)  5.74 us
    all_to_all x1, starting transfers between devices, every_owner(): returned = lax.all_to_all(sent, ('dp', 'width'), 0, 0, tiled=True)  4.9 us
    ppermute x3, waiting for transfers between devices, crossed(): lax.ppermute(left, 'dp', back)  4.4 us
    ppermute x3, waiting for transfers between devices, crossed(): lax.ppermute(right, 'dp', onward)  3.97 us
  transfers between devices with their start and end apart: 15, of which 10 were waited for; matrix products, arithmetic and copies ran while one was open for 0% of the time, Pallas kernels for 17%

profile of v4, /device:TPU:0, one launch (start us, length us, event | category | flops | bytes accessed | tf_op | source)
XLA Modules:
  0.0 66.6 jit_solution(6017453731990010465)
XLA Ops:
  0.6 0.0 copy-start.3
  0.6 1.0 %copy-done.3 = bf16[128,2048]{1,0:T(8,128)(2,1)S(1)} copy-done((bf16[128,2048]{1,0:T(8,128)(2,1)S(1)}, bf16[128,2048]{1,0:T(8,128)(2,1)}, u32[]{:S(2)}) %copy-start.3) | copy-done | bytes 524312
  1.7 0.0 copy-start.4
  1.7 0.7 %copy-done.4 = s32[128,32]{0,1:T(8,128)S(1)} copy-done((s32[128,32]{0,1:T(8,128)S(1)}, s32[128,32]{0,1:T(8,128)}, u32[]{:S(2)}) %copy-start.4) | copy-done | bytes 16408
  2.4 0.0 copy-start.5
  2.4 0.7 %copy-done.5 = bf16[128,32]{0,1:T(8,128)(2,1)S(1)} copy-done((bf16[128,32]{0,1:T(8,128)(2,1)S(1)}, bf16[128,32]{0,1:T(8,128)(2,1)}, u32[]{:S(2)}) %copy-start.5) | copy-done | bytes 8216
  3.1 0.0 copy-start.6
  3.1 0.7 %copy-done.6 = s32[128,8]{0,1:T(8,128)S(1)} copy-done((s32[128,8]{0,1:T(8,128)S(1)}, s32[128,8]{0,1:T(8,128)}, u32[]{:S(2)}) %copy-start.6) | copy-done | bytes 4120
  3.8 0.0 copy-start.7
  3.8 0.7 copy-done.7
  4.4 1.0 %prepare.1 = (bf16[1056,128]{1,0:T(8,128)(2,1)S(1)}, bf16[1056,128]{1,0:T(8,128)(2,1)S(1)}, f32[8,128]{1,0:T(8,128)S(1)}, s32[8,128]{1,0:T(8,128)S(1)}) custom-call(s32[32]{0:T(128)S(1)} %copy-done.7, s32[8,128]{1,0:T(8,128)S(1)} %bitcast.9, s32[32,128]{1,0:T(8,128)S(1)} %bitcast.7, bf16[32,128]{1,0:T(8,128)(2,1)S(1)} %bitcast.8, bf16[128,2048]{1,0:T(8,128)(2,1)S(1)} %copy-done.3), custom_call_target="tpu_custom_call" | custom-call | tf_op jit(solution)/shard_map/prepare/pallas_call | solution.py:102
  5.4 3.1 %collective-permute-start = (bf16[1056,128]{1,0:T(8,128)(2,1)S(1)}, bf16[1056,128]{1,0:T(8,128)(2,1)S(1)}, u32[]{:S(2)}, u32[]{:S(2)}) collective-permute-start(bf16[1056,128]{1,0:T(8,128)(2,1)S(1)} %get-tuple-element.27.refs_0_), channel_id=1, source_target_pairs={{0,4},{4,8},{8,12},{12,14},{14,10},{10,6},{6,2},{2,0},{1,5},{5,9},... | collective-permute-start | bytes 811016 | tf_op jit(solution)/shard_map/ppermute | solution.py:336
  8.5 0.0 collective-permute-start.1
  8.5 2.0 %collective-permute-start.3 = (bf16[1056,128]{1,0:T(8,128)(2,1)S(1)}, bf16[1056,128]{1,0:T(8,128)(2,1)S(1)}, u32[]{:S(2)}, u32[]{:S(2)}) collective-permute-start(bf16[1056,128]{1,0:T(8,128)(2,1)S(1)} %get-tuple-element.28.refs_1_), channel_id=1, source_target_pairs={{0,4},{4,8},{8,12},{12,14},{14,10},{10,6},{6,2},{2,0},{1,5},{5,9},... | collective-permute-start | bytes 811016 | tf_op jit(solution)/shard_map/ppermute | solution.py:340
  10.5 0.0 collective-permute-start.4
  10.5 0.0 copy-start.2
  10.5 1.6 %copy-done.2 = bf16[512,2048]{1,0:T(8,128)(2,1)S(1)} copy-done((bf16[512,2048]{1,0:T(8,128)(2,1)S(1)}, bf16[512,2048]{1,0:T(8,128)(2,1)}, u32[]{:S(2)}) %copy-start.2) | copy-done | bytes 2097176
  12.1 0.1 fetch.1.decoder
  12.3 3.4 %collective-permute-done.refs_2_ = bf16[1056,128]{1,0:T(8,128)(2,1)S(1)} collective-permute-done((bf16[1056,128]{1,0:T(8,128)(2,1)S(1)}, bf16[1056,128]{1,0:T(8,128)(2,1)S(1)}, u32[]{:S(2)}, u32[]{:S(2)}) %collective-permute-start) | collective-permute-done | bytes 270368 | tf_op jit(solution)/shard_map/ppermute | solution.py:336
  15.7 2.2 %collective-permute-done.1.refs_5_ = bf16[1056,128]{1,0:T(8,128)(2,1)S(1)} collective-permute-done((bf16[1056,128]{1,0:T(8,128)(2,1)S(1)}, bf16[1056,128]{1,0:T(8,128)(2,1)S(1)}, u32[]{:S(2)}, u32[]{:S(2)}) %collective-permute-start.1) | collective-permute-done | bytes 270368 | tf_op jit(solution)/shard_map/ppermute | solution.py:336
  17.9 1.6 %collective-permute-start.2 = (bf16[1056,128]{1,0:T(8,128)(2,1)S(1)}, bf16[1056,128]{1,0:T(8,128)(2,1)S(1)}, u32[]{:S(2)}, u32[]{:S(2)}) collective-permute-start(bf16[1056,128]{1,0:T(8,128)(2,1)S(1)} %collective-permute-done.refs_2_), channel_id=1, source_target_pairs={{0,4},{4,8},{8,12},{12,14},{14,10},{10,6},{6,2},{2,0},{1,5},{5,9},... | collective-permute-start | bytes 811016 | tf_op jit(solution)/shard_map/ppermute | solution.py:336
  19.5 0.4 collective-permute-start.7
  19.9 1.6 %collective-permute-done.3.refs_3_ = bf16[1056,128]{1,0:T(8,128)(2,1)S(1)} collective-permute-done((bf16[1056,128]{1,0:T(8,128)(2,1)S(1)}, bf16[1056,128]{1,0:T(8,128)(2,1)S(1)}, u32[]{:S(2)}, u32[]{:S(2)}) %collective-permute-start.3) | collective-permute-done | bytes 270368 | tf_op jit(solution)/shard_map/ppermute | solution.py:340
  21.5 2.1 %collective-permute-start.5 = (bf16[1056,128]{1,0:T(8,128)(2,1)S(1)}, bf16[1056,128]{1,0:T(8,128)(2,1)S(1)}, u32[]{:S(2)}, u32[]{:S(2)}) collective-permute-start(bf16[1056,128]{1,0:T(8,128)(2,1)S(1)} %collective-permute-done.3.refs_3_), channel_id=1, source_target_pairs={{0,4},{4,8},{8,12},{12,14},{14,10},{10,6},{6,2},{2,0},{1,5},{5,9},... | collective-permute-start | bytes 811016 | tf_op jit(solution)/shard_map/ppermute | solution.py:340
  23.6 0.0 collective-permute-done.4.refs_4_
  23.7 0.0 collective-permute-start.6
  23.7 3.6 %collective-permute-done.2.refs_0_ = bf16[1056,128]{1,0:T(8,128)(2,1)S(1)} collective-permute-done((bf16[1056,128]{1,0:T(8,128)(2,1)S(1)}, bf16[1056,128]{1,0:T(8,128)(2,1)S(1)}, u32[]{:S(2)}, u32[]{:S(2)}) %collective-permute-start.2) | collective-permute-done | bytes 270368 | tf_op jit(solution)/shard_map/ppermute | solution.py:336
  27.3 2.1 %collective-permute-start.8 = (bf16[1056,128]{1,0:T(8,128)(2,1)S(1)}, bf16[1056,128]{1,0:T(8,128)(2,1)S(1)}, u32[]{:S(2)}, u32[]{:S(2)}) collective-permute-start(bf16[1056,128]{1,0:T(8,128)(2,1)S(1)} %collective-permute-done.2.refs_0_), channel_id=1, source_target_pairs={{0,4},{4,8},{8,12},{12,14},{14,10},{10,6},{6,2},{2,0},{1,5},{5,9},... | collective-permute-start | bytes 811016 | tf_op jit(solution)/shard_map/ppermute | solution.py:336
  29.4 0.0 collective-permute-done.7.refs_3_
  29.5 0.0 collective-permute-start.9
  29.5 2.8 %absorb.3 = (f32[8,2,8,128]{3,2,1,0:T(8,128)}, f32[512,2048]{1,0:T(8,128)S(1)}) custom-call(bf16[512,2048]{1,0:T(8,128)(2,1)S(1)} %fetch.1.decoder, f32[8,128]{1,0:T(8,128)S(1)} %get-tuple-element.30.own_facts, bf16[1056,128]{1,0:T(8,128)(2,1)S(1)} %get-tuple-element.27.refs_0_, bf16[1056,128]{1,0:T(8,128)(2,1)S(1)} %get-tuple-element.28.refs_1_, ...), custom_call_target="tpu_custom_call" | custom-call | tf_op jit(solution)/shard_map/absorb/pallas_call | solution.py:243
  32.3 0.8 %collective-permute-done.5.refs_1_ = bf16[1056,128]{1,0:T(8,128)(2,1)S(1)} collective-permute-done((bf16[1056,128]{1,0:T(8,128)(2,1)S(1)}, bf16[1056,128]{1,0:T(8,128)(2,1)S(1)}, u32[]{:S(2)}, u32[]{:S(2)}) %collective-permute-start.5) | collective-permute-done | bytes 270368 | tf_op jit(solution)/shard_map/ppermute | solution.py:340
  33.1 2.2 %collective-permute-done.6.refs_2_ = bf16[1056,128]{1,0:T(8,128)(2,1)S(1)} collective-permute-done((bf16[1056,128]{1,0:T(8,128)(2,1)S(1)}, bf16[1056,128]{1,0:T(8,128)(2,1)S(1)}, u32[]{:S(2)}, u32[]{:S(2)}) %collective-permute-start.6) | collective-permute-done | bytes 270368 | tf_op jit(solution)/shard_map/ppermute | solution.py:340
  35.3 1.6 %collective-permute-start.10 = (bf16[1056,128]{1,0:T(8,128)(2,1)S(1)}, bf16[1056,128]{1,0:T(8,128)(2,1)S(1)}, u32[]{:S(2)}, u32[]{:S(2)}) collective-permute-start(bf16[1056,128]{1,0:T(8,128)(2,1)S(1)} %collective-permute-done.5.refs_1_), channel_id=1, source_target_pairs={{0,4},{4,8},{8,12},{12,14},{14,10},{10,6},{6,2},{2,0},{1,5},{5,9},... | collective-permute-start | bytes 811016 | tf_op jit(solution)/shard_map/ppermute | solution.py:340
  36.8 0.4 collective-permute-start.11
  37.3 3.2 %absorb.4 = (f32[8,2,8,128]{3,2,1,0:T(8,128)}, f32[512,2048]{1,0:T(8,128)S(1)}) custom-call(bf16[512,2048]{1,0:T(8,128)(2,1)S(1)} %fetch.1.decoder, f32[8,128]{1,0:T(8,128)S(1)} %get-tuple-element.30.own_facts, bf16[1056,128]{1,0:T(8,128)(2,1)S(1)} %collective-permute-done.2.refs_0_, ...), custom_call_target="tpu_custom_call", output_to_operand_aliasing={{0}: (6, {}), {1}: (7, {})} | custom-call | tf_op jit(solution)/shard_map/absorb/pallas_call | solution.py:243
  40.5 0.0 collective-permute-done.8.refs_0_
  40.5 0.6 collective-permute-done.9.refs_3_
  41.1 1.6 %collective-permute-start.12 = (bf16[1056,128]{1,0:T(8,128)(2,1)S(1)}, bf16[1056,128]{1,0:T(8,128)(2,1)S(1)}, u32[]{:S(2)}, u32[]{:S(2)}) collective-permute-start(bf16[1056,128]{1,0:T(8,128)(2,1)S(1)} %collective-permute-done.8.refs_0_), channel_id=1, source_target_pairs={{0,4},{4,8},{8,12},{12,14},{14,10},{10,6},{6,2},{2,0},{1,5},{5,9},... | collective-permute-start | bytes 811016 | tf_op jit(solution)/shard_map/ppermute | solution.py:336
  42.6 0.4 collective-permute-start.13
  43.1 1.6 %collective-permute-done.10.refs_1_ = bf16[1056,128]{1,0:T(8,128)(2,1)S(1)} collective-permute-done((bf16[1056,128]{1,0:T(8,128)(2,1)S(1)}, bf16[1056,128]{1,0:T(8,128)(2,1)S(1)}, u32[]{:S(2)}, u32[]{:S(2)}) %collective-permute-start.10) | collective-permute-done | bytes 270368 | tf_op jit(solution)/shard_map/ppermute | solution.py:340
  44.7 2.2 %collective-permute-done.11.refs_2_ = bf16[1056,128]{1,0:T(8,128)(2,1)S(1)} collective-permute-done((bf16[1056,128]{1,0:T(8,128)(2,1)S(1)}, bf16[1056,128]{1,0:T(8,128)(2,1)S(1)}, u32[]{:S(2)}, u32[]{:S(2)}) %collective-permute-start.11) | collective-permute-done | bytes 270368 | tf_op jit(solution)/shard_map/ppermute | solution.py:340
  46.9 3.2 %absorb.5 = (f32[8,2,8,128]{3,2,1,0:T(8,128)}, f32[512,2048]{1,0:T(8,128)S(1)}) custom-call(bf16[512,2048]{1,0:T(8,128)(2,1)S(1)} %fetch.1.decoder, f32[8,128]{1,0:T(8,128)S(1)} %get-tuple-element.30.own_facts, bf16[1056,128]{1,0:T(8,128)(2,1)S(1)} %collective-permute-done.8.refs_0_, ...), custom_call_target="tpu_custom_call", output_to_operand_aliasing={{0}: (6, {}), {1}: (7, {})} | custom-call | tf_op jit(solution)/shard_map/absorb/pallas_call | solution.py:243
  50.0 0.0 copy-start
  50.0 1.9 %copy-done = f32[512,2048]{1,0:T(8,128)} copy-done((f32[512,2048]{1,0:T(8,128)}, f32[512,2048]{1,0:T(8,128)S(1)}, u32[]{:S(2)}) %copy-start) | copy-done | bytes 4194328
  52.0 0.0 collective-permute-done.12.left
  52.0 0.0 collective-permute-done.13.right
  52.0 2.2 %last_scores.1 = f32[8,2,8,128]{3,2,1,0:T(8,128)} custom-call(bf16[512,2048]{1,0:T(8,128)(2,1)S(1)} %fetch.1.decoder, bf16[1056,128]{1,0:T(8,128)(2,1)S(1)} %collective-permute-done.12.left, bf16[1056,128]{1,0:T(8,128)(2,1)S(1)} %collective-permute-done.13.right, f32[8,2,8,128]{3,2,1,0:T(8,128)} %get-tuple-element.50.before), custom_call_target="tpu_custom_call", output_to_operand_aliasing={{}: (3, {})} | custom-call | tf_op jit(solution)/shard_map/last_scores/pallas_call | solution.py:265
  54.2 4.9 %all-to-all-start = ((f32[16,8,128]{2,1,0:T(8,128)}), f32[16,8,128]{2,1,0:T(8,128)S(1)}, u32[]{:S(2)}, u32[]{:S(2)}) async-start(f32[16,8,128]{2,1,0:T(8,128)} %bitcast.3), calls=%async_computation | async-start | bytes 131072 | tf_op jit(solution)/shard_map/all_to_all | solution.py:366
  59.1 0.0 copy-start.1
  59.1 2.2 %copy-done.1 = f32[512,2048]{1,0:T(8,128)S(1)} copy-done((f32[512,2048]{1,0:T(8,128)S(1)}, f32[512,2048]{1,0:T(8,128)}, u32[]{:S(2)}) %copy-start.1) | copy-done | bytes 4194328
  61.3 1.7 %last_gradients.1 = bf16[512,2048]{1,0:T(8,128)(2,1)} custom-call(bf16[1056,128]{1,0:T(8,128)(2,1)S(1)} %collective-permute-done.12.left, bf16[1056,128]{1,0:T(8,128)(2,1)S(1)} %collective-permute-done.13.right, f32[512,2048]{1,0:T(8,128)S(1)} %copy-done.1), custom_call_target="tpu_custom_call" | custom-call | tf_op jit(solution)/shard_map/last_gradients/pallas_call | solution.py:292
  63.0 3.0 %all-to-all-done = f32[16,8,128]{2,1,0:T(8,128)S(1)} async-done(((f32[16,8,128]{2,1,0:T(8,128)}), f32[16,8,128]{2,1,0:T(8,128)S(1)}, u32[]{:S(2)}, u32[]{:S(2)}) %all-to-all-start) | async-done | bytes 65568 | tf_op jit(solution)/shard_map/all_to_all | solution.py:366
  66.0 0.6 unpack.1
Async XLA Ops:
  0.6 1.0 %copy-start.3 = (bf16[128,2048]{1,0:T(8,128)(2,1)S(1)}, bf16[128,2048]{1,0:T(8,128)(2,1)}, u32[]{:S(2)}) copy-start(bf16[128,2048]{1,0:T(8,128)(2,1)} %grad_out.1) | copy-start | bytes 1572868
  1.7 0.7 %copy-start.4 = (s32[128,32]{0,1:T(8,128)S(1)}, s32[128,32]{0,1:T(8,128)}, u32[]{:S(2)}) copy-start(s32[128,32]{0,1:T(8,128)} %param.9) | copy-start | bytes 49156
  2.4 0.7 %copy-start.5 = (bf16[128,32]{0,1:T(8,128)(2,1)S(1)}, bf16[128,32]{0,1:T(8,128)(2,1)}, u32[]{:S(2)}) copy-start(bf16[128,32]{0,1:T(8,128)(2,1)} %param.10) | copy-start | bytes 24580
  3.1 0.7 %copy-start.6 = (s32[128,8]{0,1:T(8,128)S(1)}, s32[128,8]{0,1:T(8,128)}, u32[]{:S(2)}) copy-start(s32[128,8]{0,1:T(8,128)} %param.8) | copy-start | bytes 12292
  3.8 0.7 copy-start.7
  5.4 10.3 %collective-permute-start = (bf16[1056,128]{1,0:T(8,128)(2,1)S(1)}, bf16[1056,128]{1,0:T(8,128)(2,1)S(1)}, u32[]{:S(2)}, u32[]{:S(2)}) collective-permute-start(bf16[1056,128]{1,0:T(8,128)(2,1)S(1)} %get-tuple-element.27.refs_0_), channel_id=1, source_target_pairs={{0,4},{4,8},{8,12},{12,14},{14,10},{10,6},{6,2},{2,0},{1,5},{5,9},... | collective-permute-start | bytes 811016 | tf_op jit(solution)/shard_map/ppermute | solution.py:336
  8.5 9.4 %collective-permute-start.1 = (bf16[1056,128]{1,0:T(8,128)(2,1)S(1)}, bf16[1056,128]{1,0:T(8,128)(2,1)S(1)}, u32[]{:S(2)}, u32[]{:S(2)}) collective-permute-start(bf16[1056,128]{1,0:T(8,128)(2,1)S(1)} %get-tuple-element.28.refs_1_), channel_id=1, source_target_pairs={{4,0},{8,4},{12,8},{14,12},{10,14},{6,10},{2,6},{0,2},{5,1},{9,5},... | collective-permute-start | bytes 811016 | tf_op jit(solution)/shard_map/ppermute | solution.py:336
  8.5 13.0 %collective-permute-start.3 = (bf16[1056,128]{1,0:T(8,128)(2,1)S(1)}, bf16[1056,128]{1,0:T(8,128)(2,1)S(1)}, u32[]{:S(2)}, u32[]{:S(2)}) collective-permute-start(bf16[1056,128]{1,0:T(8,128)(2,1)S(1)} %get-tuple-element.28.refs_1_), channel_id=1, source_target_pairs={{0,4},{4,8},{8,12},{12,14},{14,10},{10,6},{6,2},{2,0},{1,5},{5,9},... | collective-permute-start | bytes 811016 | tf_op jit(solution)/shard_map/ppermute | solution.py:340
  10.5 13.2 %collective-permute-start.4 = (bf16[1056,128]{1,0:T(8,128)(2,1)S(1)}, bf16[1056,128]{1,0:T(8,128)(2,1)S(1)}, u32[]{:S(2)}, u32[]{:S(2)}) collective-permute-start(bf16[1056,128]{1,0:T(8,128)(2,1)S(1)} %get-tuple-element.27.refs_0_), channel_id=1, source_target_pairs={{4,0},{8,4},{12,8},{14,12},{10,14},{6,10},{2,6},{0,2},{5,1},{9,5},... | collective-permute-start | bytes 811016 | tf_op jit(solution)/shard_map/ppermute | solution.py:340
  10.5 1.6 %copy-start.2 = (bf16[512,2048]{1,0:T(8,128)(2,1)S(1)}, bf16[512,2048]{1,0:T(8,128)(2,1)}, u32[]{:S(2)}) copy-start(bf16[512,2048]{1,0:T(8,128)(2,1)} %source.1) | copy-start | bytes 6291460
  17.9 9.4 %collective-permute-start.2 = (bf16[1056,128]{1,0:T(8,128)(2,1)S(1)}, bf16[1056,128]{1,0:T(8,128)(2,1)S(1)}, u32[]{:S(2)}, u32[]{:S(2)}) collective-permute-start(bf16[1056,128]{1,0:T(8,128)(2,1)S(1)} %collective-permute-done.refs_2_), channel_id=1, source_target_pairs={{0,4},{4,8},{8,12},{12,14},{14,10},{10,6},{6,2},{2,0},{1,5},{5,9},... | collective-permute-start | bytes 811016 | tf_op jit(solution)/shard_map/ppermute | solution.py:336
  19.5 10.0 %collective-permute-start.7 = (bf16[1056,128]{1,0:T(8,128)(2,1)S(1)}, bf16[1056,128]{1,0:T(8,128)(2,1)S(1)}, u32[]{:S(2)}, u32[]{:S(2)}) collective-permute-start(bf16[1056,128]{1,0:T(8,128)(2,1)S(1)} %collective-permute-done.1.refs_5_), channel_id=1, source_target_pairs={{4,0},{8,4},{12,8},{14,12},{10,14},{6,10},{2,6},{0,2},{5,1},{9,5},... | collective-permute-start | bytes 811016 | tf_op jit(solution)/shard_map/ppermute | solution.py:336
  21.5 11.6 %collective-permute-start.5 = (bf16[1056,128]{1,0:T(8,128)(2,1)S(1)}, bf16[1056,128]{1,0:T(8,128)(2,1)S(1)}, u32[]{:S(2)}, u32[]{:S(2)}) collective-permute-start(bf16[1056,128]{1,0:T(8,128)(2,1)S(1)} %collective-permute-done.3.refs_3_), channel_id=1, source_target_pairs={{0,4},{4,8},{8,12},{12,14},{14,10},{10,6},{6,2},{2,0},{1,5},{5,9},... | collective-permute-start | bytes 811016 | tf_op jit(solution)/shard_map/ppermute | solution.py:340
  23.7 11.6 %collective-permute-start.6 = (bf16[1056,128]{1,0:T(8,128)(2,1)S(1)}, bf16[1056,128]{1,0:T(8,128)(2,1)S(1)}, u32[]{:S(2)}, u32[]{:S(2)}) collective-permute-start(bf16[1056,128]{1,0:T(8,128)(2,1)S(1)} %collective-permute-done.4.refs_4_), channel_id=1, source_target_pairs={{4,0},{8,4},{12,8},{14,12},{10,14},{6,10},{2,6},{0,2},{5,1},{9,5},... | collective-permute-start | bytes 811016 | tf_op jit(solution)/shard_map/ppermute | solution.py:340
  27.3 13.2 %collective-permute-start.8 = (bf16[1056,128]{1,0:T(8,128)(2,1)S(1)}, bf16[1056,128]{1,0:T(8,128)(2,1)S(1)}, u32[]{:S(2)}, u32[]{:S(2)}) collective-permute-start(bf16[1056,128]{1,0:T(8,128)(2,1)S(1)} %collective-permute-done.2.refs_0_), channel_id=1, source_target_pairs={{0,4},{4,8},{8,12},{12,14},{14,10},{10,6},{6,2},{2,0},{1,5},{5,9},... | collective-permute-start | bytes 811016 | tf_op jit(solution)/shard_map/ppermute | solution.py:336
  29.5 11.6 %collective-permute-start.9 = (bf16[1056,128]{1,0:T(8,128)(2,1)S(1)}, bf16[1056,128]{1,0:T(8,128)(2,1)S(1)}, u32[]{:S(2)}, u32[]{:S(2)}) collective-permute-start(bf16[1056,128]{1,0:T(8,128)(2,1)S(1)} %collective-permute-done.7.refs_3_), channel_id=1, source_target_pairs={{4,0},{8,4},{12,8},{14,12},{10,14},{6,10},{2,6},{0,2},{5,1},{9,5},... | collective-permute-start | bytes 811016 | tf_op jit(solution)/shard_map/ppermute | solution.py:336
  35.3 9.4 %collective-permute-start.10 = (bf16[1056,128]{1,0:T(8,128)(2,1)S(1)}, bf16[1056,128]{1,0:T(8,128)(2,1)S(1)}, u32[]{:S(2)}, u32[]{:S(2)}) collective-permute-start(bf16[1056,128]{1,0:T(8,128)(2,1)S(1)} %collective-permute-done.5.refs_1_), channel_id=1, source_target_pairs={{0,4},{4,8},{8,12},{12,14},{14,10},{10,6},{6,2},{2,0},{1,5},{5,9},... | collective-permute-start | bytes 811016 | tf_op jit(solution)/shard_map/ppermute | solution.py:340
  36.8 10.0 %collective-permute-start.11 = (bf16[1056,128]{1,0:T(8,128)(2,1)S(1)}, bf16[1056,128]{1,0:T(8,128)(2,1)S(1)}, u32[]{:S(2)}, u32[]{:S(2)}) collective-permute-start(bf16[1056,128]{1,0:T(8,128)(2,1)S(1)} %collective-permute-done.6.refs_2_), channel_id=1, source_target_pairs={{4,0},{8,4},{12,8},{14,12},{10,14},{6,10},{2,6},{0,2},{5,1},{9,5},... | collective-permute-start | bytes 811016 | tf_op jit(solution)/shard_map/ppermute | solution.py:340
  41.1 10.9 %collective-permute-start.12 = (bf16[1056,128]{1,0:T(8,128)(2,1)S(1)}, bf16[1056,128]{1,0:T(8,128)(2,1)S(1)}, u32[]{:S(2)}, u32[]{:S(2)}) collective-permute-start(bf16[1056,128]{1,0:T(8,128)(2,1)S(1)} %collective-permute-done.8.refs_0_), channel_id=1, source_target_pairs={{0,4},{4,8},{8,12},{12,14},{14,10},{10,6},{6,2},{2,0},{1,5},{5,9},... | collective-permute-start | bytes 811016 | tf_op jit(solution)/shard_map/ppermute | solution.py:336
  42.6 9.3 %collective-permute-start.13 = (bf16[1056,128]{1,0:T(8,128)(2,1)S(1)}, bf16[1056,128]{1,0:T(8,128)(2,1)S(1)}, u32[]{:S(2)}, u32[]{:S(2)}) collective-permute-start(bf16[1056,128]{1,0:T(8,128)(2,1)S(1)} %collective-permute-done.9.refs_3_), channel_id=1, source_target_pairs={{4,0},{8,4},{12,8},{14,12},{10,14},{6,10},{2,6},{0,2},{5,1},{9,5},... | collective-permute-start | bytes 811016 | tf_op jit(solution)/shard_map/ppermute | solution.py:336
  50.0 1.9 %copy-start = (f32[512,2048]{1,0:T(8,128)}, f32[512,2048]{1,0:T(8,128)S(1)}, u32[]{:S(2)}) copy-start(f32[512,2048]{1,0:T(8,128)S(1)} %get-tuple-element.49.total) | copy-start | bytes 12582916
  54.2 11.8 %all-to-all-start = ((f32[16,8,128]{2,1,0:T(8,128)}), f32[16,8,128]{2,1,0:T(8,128)S(1)}, u32[]{:S(2)}, u32[]{:S(2)}) async-start(f32[16,8,128]{2,1,0:T(8,128)} %bitcast.3), calls=%async_computation | async-start | bytes 131072 | tf_op jit(solution)/shard_map/all_to_all | solution.py:366
  59.1 2.2 %copy-start.1 = (f32[512,2048]{1,0:T(8,128)S(1)}, f32[512,2048]{1,0:T(8,128)}, u32[]{:S(2)}) copy-start(f32[512,2048]{1,0:T(8,128)} %copy-done) | copy-start | bytes 12582916

commit v5 on v4

--- a/solution.py
+++ b/solution.py
@@ -14,6 +14,7 @@
 SMEM = pl.BlockSpec(memory_space=pltpu.SMEM)
 VMEM = pl.BlockSpec(memory_space=pltpu.VMEM)
 ANY = pl.BlockSpec(memory_space=pl.ANY)
+HBM = pl.BlockSpec(memory_space=pltpu.HBM)
 
 
 def limit(mebibytes):
@@ -22,6 +23,10 @@
 
 def kept(x):
     return pltpu.with_memory_space_constraint(x, pltpu.VMEM)
+
+
+def far(x):
+    return pltpu.with_memory_space_constraint(x, pltpu.HBM)
 
 
 def ring_of(owners):
@@ -52,11 +57,18 @@
 
 
 def prepare_kernel(
-    owners, block_slot, active, feats, acts, grad_out,
-    left, right, own_facts, slots, wide_feats, wide_acts, sems,
+    owners, *refs
 ):
+    sources, refs = refs[:5], refs[5:]
+    left, right, own_facts, slots = refs[:4]
+    block_slot, active, feats, acts, wide_feats, wide_acts, sems = refs[4:]
+    grad_out = sources[-1]
     tok_rows, width = grad_out.shape
     parts = width // 256
+    small = []
+    for source, target in zip(sources[:4], (block_slot, active, feats, acts)):
+        small.append(pltpu.make_async_copy(source, target, sems.at[len(small)]))
+        small[-1].start()
     copies = []
     for j in range(parts):
         for target, side in ((left, 0), (right, 1)):
@@ -65,10 +77,12 @@
                 pltpu.make_async_copy(
                     grad_out.at[:, column : column + 128],
                     target.at[j * tok_rows : (j + 1) * tok_rows, :],
-                    sems.at[len(copies)],
+                    sems.at[len(small) + len(copies)],
                 )
             )
             copies[-1].start()
+    for copy in small:
+        copy.wait()
     named = active[...]
     slot = jnp.zeros_like(named)
     for block in range(block_slot.shape[0]):
@@ -107,16 +121,20 @@
             pltpu.VMEM((2 * KPB, tok_rows), jnp.float32),
             pltpu.VMEM((ACT, tok_rows), jnp.int32),
         ),
-        in_specs=[SMEM, VMEM, VMEM, VMEM, ANY],
+        in_specs=[HBM] * 5,
         out_specs=(VMEM,) * 4,
         scratch_shapes=[
+            pltpu.SMEM(block_slot.shape, jnp.int32),
+            pltpu.VMEM((ACT, tok_rows), jnp.int32),
+            pltpu.VMEM((ACT * KPB, tok_rows), jnp.int32),
+            pltpu.VMEM((ACT * KPB, tok_rows), acts.dtype),
             pltpu.VMEM((ACT * KPB, tok_rows), jnp.float32),
             pltpu.VMEM((ACT * KPB, tok_rows), jnp.float32),
-            pltpu.SemaphoreType.DMA((half_width // 128,)),
+            pltpu.SemaphoreType.DMA((4 + half_width // 128,)),
         ],
         compiler_params=limit(8),
         name="prepare",
-    )(block_slot, active_blocks.T, feature_idx.T, acts.T, grad_out)
+    )(far(block_slot), far(active_blocks.T), far(feature_idx.T), far(acts.T), far(grad_out))
 
 
 def fetch_kernel(source, target, sem):
@@ -129,12 +147,12 @@
     return pl.pallas_call(
         fetch_kernel,
         out_shape=pltpu.VMEM(x.shape, x.dtype),
-        in_specs=[ANY],
+        in_specs=[HBM],
         out_specs=VMEM,
         scratch_shapes=[pltpu.SemaphoreType.DMA],
         compiler_params=limit(8),
         name="fetch",
-    )(x)
+    )(far(x))
 
 
 def block_and_rows(here):
@@ -163,7 +181,7 @@
     for b in range(1, BLK_DEV):
         mine = jnp.where(block == b, scores[b * BW : (b + 1) * BW], mine)
     return [
-        jnp.sum(jnp.where(row_axis == feats[k : k + 1], mine, 0.0), axis=0)
+        jnp.sum(jnp.where(row_axis == feats[k : k + 1], mine, 0.0), axis=0, keepdims=True)
         for k in range(KPB)
     ]
 
@@ -182,17 +200,17 @@
     return jnp.concatenate(rows, axis=0) if len(rows) > 1 else rows[0]
 
 
-def add_picks(peers, facts, decoder, pieces, picked):
+def add_picks(facts, decoder, pieces, picked):
     tok_rows = facts[0].shape[1]
     cut = decoder.shape[1] // 2
-    for first in range(0, len(peers), 2):
-        some = peers[first : first + 2]
+    for first in range(0, len(facts), 2):
+        count = min(2, len(facts) - first)
         scores = None
         for side in range(2):
             part = lax.dot_general(
                 decoder[:, side * cut : (side + 1) * cut],
                 columns_of(
-                    pieces[2 * first + side : 2 * (first + len(some)) : 2],
+                    pieces[2 * first + side : 2 * (first + count) : 2],
                     tok_rows,
                     range(cut // 128),
                 ),
@@ -200,11 +218,9 @@
                 preferred_element_type=jnp.float32,
             )
             scores = part if scores is None else scores + part
-        for i, peer in enumerate(some):
-            values = pick(scores[:, i * tok_rows : (i + 1) * tok_rows], facts[first + i])
-            for k in range(KPB):
-                for width in range(2):
-                    picked[peer, width, k, :] = values[k]
+        for i in range(first, first + count):
+            here = scores[:, (i - first) * tok_rows : (i - first + 1) * tok_rows]
+            picked[i][...] = jnp.concatenate(pick(here, facts[i]) * 2, axis=0)
 
 
 def gradient_blocks(facts, pieces, width):
@@ -221,56 +237,52 @@
 def absorb_kernel(distances, later, decoder, own_facts, *refs):
     count = len(distances)
     pieces, refs = refs[: 2 * count], refs[2 * count :]
-    picked, total = refs[-2:]
-    owners, _, _, tok_rows = picked.shape
-    peers = [peer_at(d, owners) for d in distances]
+    picked, total = refs[-1 - count : -1], refs[-1]
+    tok_rows = own_facts.shape[1]
     facts = [
         own_facts[...] if d == 0 else facts_in(pieces[2 * i + (d > 0)], d, tok_rows)
         for i, d in enumerate(distances)
     ]
-    picked[...] = refs[0][...] if later else jnp.zeros_like(picked)
-    add_picks(peers, facts, decoder, pieces, picked)
+    add_picks(facts, decoder, pieces, picked)
     for columns, part in gradient_blocks(facts, pieces, decoder.shape[1]):
-        total[:, columns] = refs[1][:, columns] + part if later else part
-
-
-def absorb(distances, pairs, decoder, own_facts, state=()):
+        total[:, columns] = refs[0][:, columns] + part if later else part
+
+
+def absorb(distances, pairs, decoder, own_facts, total=None):
     tok_rows = own_facts.shape[1]
-    owners = lax.axis_size("dp")
     operands = [kept(decoder), kept(own_facts)]
     operands += [kept(piece) for pair in pairs for piece in pair]
-    operands += [kept(x) for x in state]
-    return pl.pallas_call(
-        functools.partial(absorb_kernel, distances, bool(state)),
+    operands += [] if total is None else [kept(total)]
+    count = len(distances)
+    *picked, total = pl.pallas_call(
+        functools.partial(absorb_kernel, distances, total is not None),
         out_shape=(
-            pltpu.VMEM((owners, 2, 2 * KPB, tok_rows), jnp.float32),
+            *[pltpu.VMEM((2 * KPB, tok_rows), jnp.float32)] * count,
             pltpu.VMEM(decoder.shape, jnp.float32),
         ),
         in_specs=[VMEM] * len(operands),
-        out_specs=(VMEM, VMEM),
-        input_output_aliases={len(operands) - 2: 0, len(operands) - 1: 1} if state else {},
+        out_specs=(VMEM,) * (count + 1),
+        input_output_aliases={} if total is None else {len(operands) - 1: count},
         compiler_params=limit(16),
         name="absorb",
     )(*operands)
-
-
-def last_scores_kernel(distance, decoder, left, right, before, picked):
-    picked[...] = before[...]
-    owners, _, _, tok_rows = picked.shape
-    facts = [facts_in(left, distance, tok_rows)]
-    add_picks([peer_at(distance, owners)], facts, decoder, (left, right), picked)
-
-
-def last_scores(distance, pair, decoder, picked):
+    return picked, total
+
+
+def last_scores_kernel(distance, decoder, left, right, picked):
+    facts = [facts_in(left, distance, picked.shape[1])]
+    add_picks(facts, decoder, (left, right), [picked])
+
+
+def last_scores(distance, pair, decoder, tok_rows):
     return pl.pallas_call(
         functools.partial(last_scores_kernel, distance),
-        out_shape=pltpu.VMEM(picked.shape, picked.dtype),
-        in_specs=[VMEM] * 4,
+        out_shape=pltpu.VMEM((2 * KPB, tok_rows), jnp.float32),
+        in_specs=[VMEM] * 3,
         out_specs=VMEM,
-        input_output_aliases={3: 0},
         compiler_params=limit(12),
         name="last_scores",
-    )(kept(decoder), kept(pair[0]), kept(pair[1]), kept(picked))
+    )(kept(decoder), kept(pair[0]), kept(pair[1]))
 
 
 def last_gradients_kernel(distance, tok_rows, left, right, total, out, rounded, sems):
@@ -303,42 +315,45 @@
     )(kept(pair[0]), kept(pair[1]), kept(total))
 
 
-def unpack_kernel(returned, slots, out):
+def unpack_kernel(distances, owners, slots, *refs):
+    returned, out = refs[:-1], refs[-1]
     owner = slots[...] // BLK_DEV
+    mine = [owner == peer_at(d, owners) for d in distances]
     for k in range(KPB):
         total = jnp.zeros(owner.shape, jnp.float32)
-        for o in range(returned.shape[0]):
-            value = returned[o, 0, k : k + 1, :] + returned[o, 1, k : k + 1, :]
-            total = jnp.where(owner == o, value, total)
+        for here, values in zip(mine, returned):
+            total = jnp.where(here, values[k : k + 1, :], total)
         out[pl.ds(k, ACT, stride=KPB), :] = total
 
 
-def unpack(returned, slots):
+def unpack(distances, returned, slots):
     tok_rows = slots.shape[1]
     return pl.pallas_call(
-        unpack_kernel,
-        out_shape=jax.ShapeDtypeStruct((ACT * KPB, tok_rows), jnp.float32),
-        in_specs=[VMEM, VMEM],
+        functools.partial(unpack_kernel, distances, lax.axis_size("dp")),
+        out_shape=pltpu.VMEM((ACT * KPB, tok_rows), jnp.float32),
+        in_specs=[VMEM] * (1 + len(returned)),
         out_specs=VMEM,
         compiler_params=limit(4),
         name="unpack",
-    )(kept(returned), kept(slots)).T
+    )(kept(slots), *[kept(x) for x in returned])
 
 
 def every_owner(decoder, grad_out, active_blocks, feature_idx, acts, block_slot):
+    tok_rows = grad_out.shape[0]
     owners = lax.axis_size("dp")
     ring = ring_of(owners)
-    onward = [(ring[i], ring[(i + 1) % owners]) for i in range(owners)]
-    back = [(there, here) for here, there in onward]
+
+    def shift(x, by):
+        pairs = [(ring[i], ring[(i + by) % owners]) for i in range(owners)]
+        return lax.ppermute(x, "dp", pairs)
 
     def hop(pieces):
         left, right = pieces
-        return lax.ppermute(left, "dp", onward), lax.ppermute(right, "dp", back)
+        return shift(left, 1), shift(right, -1)
 
     def crossed(pieces):
         right, left = pieces
-        right, left = lax.ppermute(right, "dp", onward), lax.ppermute(left, "dp", back)
-        return right, left
+        return shift(right, 1), shift(left, -1)
 
     left, right, own_facts, slots = prepare(
         block_slot, active_blocks, feature_idx, acts, grad_out, owners
@@ -349,24 +364,27 @@
     first_1, decoder = lax.optimization_barrier((first_1, decoder))
     first_2 = hop(first_1)
     second_2 = crossed(second_1)
-    near = [(left, right), (first_1[0], second_1[0]), (second_1[1], first_1[1])]
-    state = absorb((0, -1, 1), near, decoder, own_facts)
     first_3 = hop(first_2)
-    state, second_2 = lax.optimization_barrier((state, second_2))
+    pairs = [(left, right), (first_1[0], second_1[0]), (second_1[1], first_1[1])]
+    (own, onward, back), total = absorb((0, -1, 1), pairs, decoder, own_facts)
+    returned = [own, shift(onward, -1), shift(back, 1)]
+    total, second_2, returned = lax.optimization_barrier((total, second_2, returned))
     second_3 = crossed(second_2)
-    far = [(first_2[0], second_2[0]), (second_2[1], first_2[1])]
-    state = absorb((-2, 2), far, decoder, own_facts, state)
-    state, first_3 = lax.optimization_barrier((state, first_3))
+    pairs = [(first_2[0], second_2[0]), (second_2[1], first_2[1])]
+    (onward, back), total = absorb((-2, 2), pairs, decoder, own_facts, total)
+    total, first_3 = lax.optimization_barrier((total, first_3))
+    returned += [shift(onward, -2), shift(back, 2)]
     first_4 = hop(first_3)
-    farther = [(first_3[0], second_3[0]), (second_3[1], first_3[1])]
-    state = absorb((-3, 3), farther, decoder, own_facts, state)
-    (picked, total), first_4 = lax.optimization_barrier((state, first_4))
-    picked = last_scores(4, first_4, decoder, picked)
-    sent = picked.reshape((2 * owners,) + picked.shape[2:])
-    returned = lax.all_to_all(sent, ("dp", "width"), 0, 0, tiled=True)
-    decoder_grad = last_gradients(4, first_4, total, grad_out.shape[0])
-    act_grad = unpack(returned.reshape(picked.shape), slots)
-    return (decoder_grad, act_grad)
+    pairs = [(first_3[0], second_3[0]), (second_3[1], first_3[1])]
+    (onward, back), total = absorb((-3, 3), pairs, decoder, own_facts, total)
+    returned += [shift(onward, -3), shift(back, 3)]
+    total, first_4, returned[3:5] = lax.optimization_barrier((total, first_4, returned[3:5]))
+    onward = last_scores(4, first_4, decoder, tok_rows)
+    returned.append(shift(onward, -4))
+    decoder_grad = last_gradients(4, first_4, total, tok_rows)
+    act_grad = unpack((0, 1, -1, 2, -2, 3, -3, 4), returned, slots)
+    act_grad = act_grad + lax.ppermute(act_grad, "width", ((0, 1), (1, 0)))
+    return (decoder_grad, act_grad.T)
 
 
 def send_back(picked):

time: 67.2 us -> 67.1 us (level)
  local copies, waits for them, and re-layouts: 9.51 us -> 0 us
  starting transfers between devices: 20.4 us -> 27.3 us
  waiting for transfers between devices: 21.2 us -> 26.9 us
  Pallas kernels: 14.8 us -> 11.2 us
    ppermute x14 -> x22, starting transfers between devices: 15.5 us -> 27.3 us  [the longest x21 27.3 us: shift(): return lax.ppermute(x, 'dp', pairs)]
    unnamed x16 -> x0, local copies, waits for them, and re-layouts: 9.51 us -> none
    ppermute x14 -> x22, waiting for transfers between devices: 18.3 us -> 26.9 us  [the longest x21 26.9 us: shift(): return lax.ppermute(x, 'dp', pairs)]
    all_to_all x1 -> x0, starting transfers between devices: 4.9 us -> none  [every_owner(): returned = lax.all_to_all(sent, ('dp', 'width'), 0, 0, tiled=True)]
    pallas_call x4, Pallas kernels: 9.75 us -> 5.89 us  [the longest x3 5.85 us: absorb(): pl.pallas_call(functools.partial(absorb_kernel, distances, total is not N...]
    all_to_all x1 -> x0, waiting for transfers between devices: 2.96 us -> none  [every_owner(): returned = lax.all_to_all(sent, ('dp', 'width'), 0, 0, tiled=True)]
    pallas_call x1, Pallas kernels: 2.18 us -> 0.72 us  [last_scores(): pl.pallas_call(functools.partial(last_scores_kernel, distance), out_shape...]
    pallas_call x1, Pallas kernels: 0.15 us -> 1.6 us  [fetch(): pl.pallas_call(fetch_kernel, out_shape=pltpu.VMEM(x.shape, x.dtype), in_s...]
  transfers between devices with their start and end apart: 15 -> 22, of which waited for: 10 -> 10; matrix products, arithmetic and copies ran while one was open for 0% -> 0% of each run, Pallas kernels for 17% -> 15%
where the time goes in v5:
time: 67.1 us; the launch traced here: 66.8 us
  starting transfers between devices  27.3 us (41%)
  waiting for transfers between devices  26.9 us (40%)
  Pallas kernels  11.2 us (17%)
  between operations  0.75 us (1%)
    ppermute x21, starting transfers between devices, shift(): return lax.ppermute(x, 'dp', pairs)  27.3 us
    ppermute x21, waiting for transfers between devices, shift(): return lax.ppermute(x, 'dp', pairs)  26.9 us
    pallas_call x3, Pallas kernels, absorb(): pl.pallas_call(functools.partial(absorb_kernel, distances, total is not N...  5.85 us
    pallas_call x1, Pallas kernels, last_gradients(): pl.pallas_call(functools.partial(last_gradients_kernel, distance, tok_row...  1.74 us
    pallas_call x1, Pallas kernels, fetch(): pl.pallas_call(fetch_kernel, out_shape=pltpu.VMEM(x.shape, x.dtype), in_s...  1.6 us
  transfers between devices with their start and end apart: 22, of which 10 were waited for; matrix products, arithmetic and copies ran while one was open for 0% of the time, Pallas kernels for 15%

profile of v5, /device:TPU:0, one launch (start us, length us, event | category | flops | bytes accessed | tf_op | source)
XLA Modules:
  0.0 66.8 jit_solution(11928150348899784438)
XLA Ops:
  0.6 1.2 %prepare.1 = (bf16[1056,128]{1,0:T(8,128)(2,1)S(1)}, bf16[1056,128]{1,0:T(8,128)(2,1)S(1)}, f32[8,128]{1,0:T(8,128)S(1)}, s32[8,128]{1,0:T(8,128)S(1)}) custom-call(s32[32]{0:T(128)} %refs_0_.1, s32[8,128]{1,0:T(8,128)} %bitcast.7, s32[32,128]{1,0:T(8,128)} %bitcast.5, bf16[32,128]{1,0:T(8,128)(2,1)} %bitcast.6, bf16[128,2048]{1,0:T(8,128)(2,1)} %refs_4_.1), custom_call_target="tpu_custom_call" | custom-call | tf_op jit(solution)/shard_map/prepare/pallas_call | solution.py:116
  1.9 3.1 %collective-permute-start = (bf16[1056,128]{1,0:T(8,128)(2,1)S(1)}, bf16[1056,128]{1,0:T(8,128)(2,1)S(1)}, u32[]{:S(2)}, u32[]{:S(2)}) collective-permute-start(bf16[1056,128]{1,0:T(8,128)(2,1)S(1)} %get-tuple-element.33.refs_0_), channel_id=1, source_target_pairs={{0,4},{4,8},{8,12},{12,14},{14,10},{10,6},{6,2},{2,0},{1,5},{5,9},... | collective-permute-start | bytes 811016 | tf_op jit(solution)/shard_map/ppermute | solution.py:348
  4.9 0.0 collective-permute-start.1
  5.0 2.0 %collective-permute-start.3 = (bf16[1056,128]{1,0:T(8,128)(2,1)S(1)}, bf16[1056,128]{1,0:T(8,128)(2,1)S(1)}, u32[]{:S(2)}, u32[]{:S(2)}) collective-permute-start(bf16[1056,128]{1,0:T(8,128)(2,1)S(1)} %get-tuple-element.34.refs_1_), channel_id=1, source_target_pairs={{0,4},{4,8},{8,12},{12,14},{14,10},{10,6},{6,2},{2,0},{1,5},{5,9},... | collective-permute-start | bytes 811016 | tf_op jit(solution)/shard_map/ppermute | solution.py:348
  7.0 0.0 collective-permute-start.4
  7.0 1.6 %fetch.1.decoder = bf16[512,2048]{1,0:T(8,128)(2,1)S(1)} custom-call(bf16[512,2048]{1,0:T(8,128)(2,1)} %source.1), custom_call_target="tpu_custom_call" | custom-call | tf_op jit(solution)/shard_map/fetch/pallas_call | solution.py:147
  8.6 3.6 %collective-permute-done.refs_2_ = bf16[1056,128]{1,0:T(8,128)(2,1)S(1)} collective-permute-done((bf16[1056,128]{1,0:T(8,128)(2,1)S(1)}, bf16[1056,128]{1,0:T(8,128)(2,1)S(1)}, u32[]{:S(2)}, u32[]{:S(2)}) %collective-permute-start) | collective-permute-done | bytes 270368 | tf_op jit(solution)/shard_map/ppermute | solution.py:348
  12.2 2.2 %collective-permute-done.1.refs_5_ = bf16[1056,128]{1,0:T(8,128)(2,1)S(1)} collective-permute-done((bf16[1056,128]{1,0:T(8,128)(2,1)S(1)}, bf16[1056,128]{1,0:T(8,128)(2,1)S(1)}, u32[]{:S(2)}, u32[]{:S(2)}) %collective-permute-start.1) | collective-permute-done | bytes 270368 | tf_op jit(solution)/shard_map/ppermute | solution.py:348
  14.4 1.6 %collective-permute-start.2 = (bf16[1056,128]{1,0:T(8,128)(2,1)S(1)}, bf16[1056,128]{1,0:T(8,128)(2,1)S(1)}, u32[]{:S(2)}, u32[]{:S(2)}) collective-permute-start(bf16[1056,128]{1,0:T(8,128)(2,1)S(1)} %collective-permute-done.refs_2_), channel_id=1, source_target_pairs={{0,4},{4,8},{8,12},{12,14},{14,10},{10,6},{6,2},{2,0},{1,5},{5,9},... | collective-permute-start | bytes 811016 | tf_op jit(solution)/shard_map/ppermute | solution.py:348
  15.9 0.4 collective-permute-start.9
  16.4 1.6 %collective-permute-done.3.refs_3_ = bf16[1056,128]{1,0:T(8,128)(2,1)S(1)} collective-permute-done((bf16[1056,128]{1,0:T(8,128)(2,1)S(1)}, bf16[1056,128]{1,0:T(8,128)(2,1)S(1)}, u32[]{:S(2)}, u32[]{:S(2)}) %collective-permute-start.3) | collective-permute-done | bytes 270368 | tf_op jit(solution)/shard_map/ppermute | solution.py:348
  18.0 2.1 %collective-permute-start.5 = (bf16[1056,128]{1,0:T(8,128)(2,1)S(1)}, bf16[1056,128]{1,0:T(8,128)(2,1)S(1)}, u32[]{:S(2)}, u32[]{:S(2)}) collective-permute-start(bf16[1056,128]{1,0:T(8,128)(2,1)S(1)} %collective-permute-done.3.refs_3_), channel_id=1, source_target_pairs={{0,4},{4,8},{8,12},{12,14},{14,10},{10,6},{6,2},{2,0},{1,5},{5,9},... | collective-permute-start | bytes 811016 | tf_op jit(solution)/shard_map/ppermute | solution.py:348
  20.1 0.0 collective-permute-done.4.refs_4_
  20.1 0.0 collective-permute-start.6
  20.2 3.6 %collective-permute-done.2.refs_0_ = bf16[1056,128]{1,0:T(8,128)(2,1)S(1)} collective-permute-done((bf16[1056,128]{1,0:T(8,128)(2,1)S(1)}, bf16[1056,128]{1,0:T(8,128)(2,1)S(1)}, u32[]{:S(2)}, u32[]{:S(2)}) %collective-permute-start.2) | collective-permute-done | bytes 270368 | tf_op jit(solution)/shard_map/ppermute | solution.py:348
  23.8 2.1 %collective-permute-start.10 = (bf16[1056,128]{1,0:T(8,128)(2,1)S(1)}, bf16[1056,128]{1,0:T(8,128)(2,1)S(1)}, u32[]{:S(2)}, u32[]{:S(2)}) collective-permute-start(bf16[1056,128]{1,0:T(8,128)(2,1)S(1)} %collective-permute-done.2.refs_0_), channel_id=1, source_target_pairs={{0,4},{4,8},{8,12},{12,14},{14,10},{10,6},{6,2},{2,0},{1,5},{5,9},... | collective-permute-start | bytes 811016 | tf_op jit(solution)/shard_map/ppermute | solution.py:348
  25.9 0.0 collective-permute-done.9.refs_3_
  25.9 0.0 collective-permute-start.11
  25.9 2.4 %absorb.3 = (f32[8,128]{1,0:T(8,128)S(1)}, f32[8,128]{1,0:T(8,128)S(1)}, f32[8,128]{1,0:T(8,128)S(1)}, f32[512,2048]{1,0:T(8,128)S(1)}) custom-call(bf16[512,2048]{1,0:T(8,128)(2,1)S(1)} %fetch.1.decoder, f32[8,128]{1,0:T(8,128)S(1)} %get-tuple-element.36.own_facts, bf16[1056,128]{1,0:T(8,128)(2,1)S(1)} %get-tuple-element.33.refs_0_, ...), custom_call_target="tpu_custom_call" | custom-call | tf_op jit(solution)/shard_map/absorb/pallas_call | solution.py:257
  28.4 2.0 %collective-permute-start.7 = (f32[8,128]{1,0:T(8,128)S(1)}, f32[8,128]{1,0:T(8,128)S(1)}, u32[]{:S(2)}, u32[]{:S(2)}) collective-permute-start(f32[8,128]{1,0:T(8,128)S(1)} %get-tuple-element.41), channel_id=1, source_target_pairs={{0,2},{4,0},{8,4},{12,8},{14,12},{10,14},{6,10},{2,6},{1,3},{5,1},... | collective-permute-start | bytes 12296 | tf_op jit(solution)/shard_map/ppermute | solution.py:348
  30.4 5.8 %collective-permute-done.7.refs_1_ = f32[8,128]{1,0:T(8,128)S(1)} collective-permute-done((f32[8,128]{1,0:T(8,128)S(1)}, f32[8,128]{1,0:T(8,128)S(1)}, u32[]{:S(2)}, u32[]{:S(2)}) %collective-permute-start.7) | collective-permute-done | bytes 4128 | tf_op jit(solution)/shard_map/ppermute | solution.py:348
  36.2 1.6 %collective-permute-start.8 = (f32[8,128]{1,0:T(8,128)S(1)}, f32[8,128]{1,0:T(8,128)S(1)}, u32[]{:S(2)}, u32[]{:S(2)}) collective-permute-start(f32[8,128]{1,0:T(8,128)S(1)} %get-tuple-element.42), channel_id=1, source_target_pairs={{0,4},{4,8},{8,12},{12,14},{14,10},{10,6},{6,2},{2,0},{1,5},{5,9},... | collective-permute-start | bytes 12296 | tf_op jit(solution)/shard_map/ppermute | solution.py:348
  37.7 2.0 %collective-permute-done.8.refs_2_ = f32[8,128]{1,0:T(8,128)S(1)} collective-permute-done((f32[8,128]{1,0:T(8,128)S(1)}, f32[8,128]{1,0:T(8,128)S(1)}, u32[]{:S(2)}, u32[]{:S(2)}) %collective-permute-start.8) | collective-permute-done | bytes 4128 | tf_op jit(solution)/shard_map/ppermute | solution.py:348
  39.8 0.0 collective-permute-done.5.refs_1_
  39.8 0.0 collective-permute-done.6.refs_2_
  39.8 1.6 %collective-permute-start.12 = (bf16[1056,128]{1,0:T(8,128)(2,1)S(1)}, bf16[1056,128]{1,0:T(8,128)(2,1)S(1)}, u32[]{:S(2)}, u32[]{:S(2)}) collective-permute-start(bf16[1056,128]{1,0:T(8,128)(2,1)S(1)} %collective-permute-done.5.refs_1_), channel_id=1, source_target_pairs={{0,4},{4,8},{8,12},{12,14},{14,10},{10,6},{6,2},{2,0},{1,5},{5,9},... | collective-permute-start | bytes 811016 | tf_op jit(solution)/shard_map/ppermute | solution.py:348
  41.3 0.4 collective-permute-start.13
  41.8 1.7 %absorb.4 = (f32[8,128]{1,0:T(8,128)S(1)}, f32[8,128]{1,0:T(8,128)S(1)}, f32[512,2048]{1,0:T(8,128)S(1)}) custom-call(bf16[512,2048]{1,0:T(8,128)(2,1)S(1)} %fetch.1.decoder, f32[8,128]{1,0:T(8,128)S(1)} %get-tuple-element.36.own_facts, bf16[1056,128]{1,0:T(8,128)(2,1)S(1)} %collective-permute-done.2.refs_0_, ...), custom_call_target="tpu_custom_call", output_to_operand_aliasing={{2}: (6, {})} | custom-call | tf_op jit(solution)/shard_map/absorb/pallas_call | solution.py:257
  43.5 0.0 collective-permute-done.10.refs_0_
  43.5 0.0 collective-permute-done.11.refs_3_
  43.5 1.6 %collective-permute-start.14 = (bf16[1056,128]{1,0:T(8,128)(2,1)S(1)}, bf16[1056,128]{1,0:T(8,128)(2,1)S(1)}, u32[]{:S(2)}, u32[]{:S(2)}) collective-permute-start(bf16[1056,128]{1,0:T(8,128)(2,1)S(1)} %collective-permute-done.10.refs_0_), channel_id=1, source_target_pairs={{0,4},{4,8},{8,12},{12,14},{14,10},{10,6},{6,2},{2,0},{1,5},{5,9},... | collective-permute-start | bytes 811016 | tf_op jit(solution)/shard_map/ppermute | solution.py:348
  45.2 0.4 collective-permute-start.15
  45.6 1.4 %collective-permute-start.16 = (f32[8,128]{1,0:T(8,128)S(1)}, f32[8,128]{1,0:T(8,128)S(1)}, u32[]{:S(2)}, u32[]{:S(2)}) collective-permute-start(f32[8,128]{1,0:T(8,128)S(1)} %get-tuple-element.51), channel_id=1, source_target_pairs={{0,6},{4,2},{8,0},{12,4},{14,8},{10,12},{6,14},{2,10},{1,7},{5,3},... | collective-permute-start | bytes 12296 | tf_op jit(solution)/shard_map/ppermute | solution.py:348
  47.0 1.9 %collective-permute-done.12.refs_1_ = bf16[1056,128]{1,0:T(8,128)(2,1)S(1)} collective-permute-done((bf16[1056,128]{1,0:T(8,128)(2,1)S(1)}, bf16[1056,128]{1,0:T(8,128)(2,1)S(1)}, u32[]{:S(2)}, u32[]{:S(2)}) %collective-permute-start.12) | collective-permute-done | bytes 270368 | tf_op jit(solution)/shard_map/ppermute | solution.py:348
  48.9 2.7 %collective-permute-start.17 = (f32[8,128]{1,0:T(8,128)S(1)}, f32[8,128]{1,0:T(8,128)S(1)}, u32[]{:S(2)}, u32[]{:S(2)}) collective-permute-start(f32[8,128]{1,0:T(8,128)S(1)} %get-tuple-element.52), channel_id=1, source_target_pairs={{0,8},{4,12},{8,14},{12,10},{14,6},{10,2},{6,0},{2,4},{1,9},{5,13}... | collective-permute-start | bytes 12296 | tf_op jit(solution)/shard_map/ppermute | solution.py:348
  51.6 0.0 collective-permute-done.13.refs_2_
  51.6 1.7 %absorb.5 = (f32[8,128]{1,0:T(8,128)S(1)}, f32[8,128]{1,0:T(8,128)S(1)}, f32[512,2048]{1,0:T(8,128)S(1)}) custom-call(bf16[512,2048]{1,0:T(8,128)(2,1)S(1)} %fetch.1.decoder, f32[8,128]{1,0:T(8,128)S(1)} %get-tuple-element.36.own_facts, bf16[1056,128]{1,0:T(8,128)(2,1)S(1)} %collective-permute-done.10.refs_0_, ...), custom_call_target="tpu_custom_call", output_to_operand_aliasing={{2}: (6, {})} | custom-call | tf_op jit(solution)/shard_map/absorb/pallas_call | solution.py:257
  53.3 0.1 collective-permute-start.18
  53.4 0.9 %collective-permute-done.16.refs_3_ = f32[8,128]{1,0:T(8,128)S(1)} collective-permute-done((f32[8,128]{1,0:T(8,128)S(1)}, f32[8,128]{1,0:T(8,128)S(1)}, u32[]{:S(2)}, u32[]{:S(2)}) %collective-permute-start.16) | collective-permute-done | bytes 4128 | tf_op jit(solution)/shard_map/ppermute | solution.py:348
  54.4 2.8 %collective-permute-start.19 = (f32[8,128]{1,0:T(8,128)S(1)}, f32[8,128]{1,0:T(8,128)S(1)}, u32[]{:S(2)}, u32[]{:S(2)}) collective-permute-start(f32[8,128]{1,0:T(8,128)S(1)} %get-tuple-element.63), channel_id=1, source_target_pairs={{0,12},{4,14},{8,10},{12,6},{14,2},{10,0},{6,4},{2,8},{1,13},{5,15... | collective-permute-start | bytes 12296 | tf_op jit(solution)/shard_map/ppermute | solution.py:348
  57.2 0.0 collective-permute-done.17.refs_4_
  57.2 0.0 collective-permute-done.14.left
  57.2 0.0 collective-permute-done.15.right
  57.2 0.7 %last_scores.1 = f32[8,128]{1,0:T(8,128)S(1)} custom-call(bf16[512,2048]{1,0:T(8,128)(2,1)S(1)} %fetch.1.decoder, bf16[1056,128]{1,0:T(8,128)(2,1)S(1)} %collective-permute-done.14.left, bf16[1056,128]{1,0:T(8,128)(2,1)S(1)} %collective-permute-done.15.right), custom_call_target="tpu_custom_call" | custom-call | tf_op jit(solution)/shard_map/last_scores/pallas_call | solution.py:278
  57.9 1.2 %collective-permute-start.20 = (f32[8,128]{1,0:T(8,128)S(1)}, f32[8,128]{1,0:T(8,128)S(1)}, u32[]{:S(2)}, u32[]{:S(2)}) collective-permute-start(f32[8,128]{1,0:T(8,128)S(1)} %last_scores.1), channel_id=1, source_target_pairs={{0,14},{4,10},{8,6},{12,2},{14,0},{10,4},{6,8},{2,12},{1,15},{5,11... | collective-permute-start | bytes 12296 | tf_op jit(solution)/shard_map/ppermute | solution.py:348
  59.1 0.0 collective-permute-done.18.refs_5_
  59.1 0.7 %collective-permute-done.19.refs_6_ = f32[8,128]{1,0:T(8,128)S(1)} collective-permute-done((f32[8,128]{1,0:T(8,128)S(1)}, f32[8,128]{1,0:T(8,128)S(1)}, u32[]{:S(2)}, u32[]{:S(2)}) %collective-permute-start.19) | collective-permute-done | bytes 4128 | tf_op jit(solution)/shard_map/ppermute | solution.py:348
  59.8 4.5 %collective-permute-done.20.refs_7_ = f32[8,128]{1,0:T(8,128)S(1)} collective-permute-done((f32[8,128]{1,0:T(8,128)S(1)}, f32[8,128]{1,0:T(8,128)S(1)}, u32[]{:S(2)}, u32[]{:S(2)}) %collective-permute-start.20) | collective-permute-done | bytes 4128 | tf_op jit(solution)/shard_map/ppermute | solution.py:348
  64.3 0.1 collective-permute-start.21
  64.4 1.7 %last_gradients.1 = bf16[512,2048]{1,0:T(8,128)(2,1)} custom-call(bf16[1056,128]{1,0:T(8,128)(2,1)S(1)} %collective-permute-done.14.left, bf16[1056,128]{1,0:T(8,128)(2,1)S(1)} %collective-permute-done.15.right, f32[512,2048]{1,0:T(8,128)S(1)} %get-tuple-element.55.total), custom_call_target="tpu_custom_call" | custom-call | tf_op jit(solution)/shard_map/last_gradients/pallas_call | solution.py:304
  66.2 0.0 collective-permute-done.21
  66.2 0.6 add_bitcast_fusion
  (1 shorter events, 0.0 us)
Async XLA Ops:
  1.9 10.3 %collective-permute-start = (bf16[1056,128]{1,0:T(8,128)(2,1)S(1)}, bf16[1056,128]{1,0:T(8,128)(2,1)S(1)}, u32[]{:S(2)}, u32[]{:S(2)}) collective-permute-start(bf16[1056,128]{1,0:T(8,128)(2,1)S(1)} %get-tuple-element.33.refs_0_), channel_id=1, source_target_pairs={{0,4},{4,8},{8,12},{12,14},{14,10},{10,6},{6,2},{2,0},{1,5},{5,9},... | collective-permute-start | bytes 811016 | tf_op jit(solution)/shard_map/ppermute | solution.py:348
  4.9 9.4 %collective-permute-start.1 = (bf16[1056,128]{1,0:T(8,128)(2,1)S(1)}, bf16[1056,128]{1,0:T(8,128)(2,1)S(1)}, u32[]{:S(2)}, u32[]{:S(2)}) collective-permute-start(bf16[1056,128]{1,0:T(8,128)(2,1)S(1)} %get-tuple-element.34.refs_1_), channel_id=1, source_target_pairs={{0,2},{4,0},{8,4},{12,8},{14,12},{10,14},{6,10},{2,6},{1,3},{5,1},... | collective-permute-start | bytes 811016 | tf_op jit(solution)/shard_map/ppermute | solution.py:348
  5.0 13.0 %collective-permute-start.3 = (bf16[1056,128]{1,0:T(8,128)(2,1)S(1)}, bf16[1056,128]{1,0:T(8,128)(2,1)S(1)}, u32[]{:S(2)}, u32[]{:S(2)}) collective-permute-start(bf16[1056,128]{1,0:T(8,128)(2,1)S(1)} %get-tuple-element.34.refs_1_), channel_id=1, source_target_pairs={{0,4},{4,8},{8,12},{12,14},{14,10},{10,6},{6,2},{2,0},{1,5},{5,9},... | collective-permute-start | bytes 811016 | tf_op jit(solution)/shard_map/ppermute | solution.py:348
  7.0 13.2 %collective-permute-start.4 = (bf16[1056,128]{1,0:T(8,128)(2,1)S(1)}, bf16[1056,128]{1,0:T(8,128)(2,1)S(1)}, u32[]{:S(2)}, u32[]{:S(2)}) collective-permute-start(bf16[1056,128]{1,0:T(8,128)(2,1)S(1)} %get-tuple-element.33.refs_0_), channel_id=1, source_target_pairs={{0,2},{4,0},{8,4},{12,8},{14,12},{10,14},{6,10},{2,6},{1,3},{5,1},... | collective-permute-start | bytes 811016 | tf_op jit(solution)/shard_map/ppermute | solution.py:348
  14.4 9.4 %collective-permute-start.2 = (bf16[1056,128]{1,0:T(8,128)(2,1)S(1)}, bf16[1056,128]{1,0:T(8,128)(2,1)S(1)}, u32[]{:S(2)}, u32[]{:S(2)}) collective-permute-start(bf16[1056,128]{1,0:T(8,128)(2,1)S(1)} %collective-permute-done.refs_2_), channel_id=1, source_target_pairs={{0,4},{4,8},{8,12},{12,14},{14,10},{10,6},{6,2},{2,0},{1,5},{5,9},... | collective-permute-start | bytes 811016 | tf_op jit(solution)/shard_map/ppermute | solution.py:348
  15.9 10.0 %collective-permute-start.9 = (bf16[1056,128]{1,0:T(8,128)(2,1)S(1)}, bf16[1056,128]{1,0:T(8,128)(2,1)S(1)}, u32[]{:S(2)}, u32[]{:S(2)}) collective-permute-start(bf16[1056,128]{1,0:T(8,128)(2,1)S(1)} %collective-permute-done.1.refs_5_), channel_id=1, source_target_pairs={{0,2},{4,0},{8,4},{12,8},{14,12},{10,14},{6,10},{2,6},{1,3},{5,1},... | collective-permute-start | bytes 811016 | tf_op jit(solution)/shard_map/ppermute | solution.py:348
  18.0 21.8 %collective-permute-start.5 = (bf16[1056,128]{1,0:T(8,128)(2,1)S(1)}, bf16[1056,128]{1,0:T(8,128)(2,1)S(1)}, u32[]{:S(2)}, u32[]{:S(2)}) collective-permute-start(bf16[1056,128]{1,0:T(8,128)(2,1)S(1)} %collective-permute-done.3.refs_3_), channel_id=1, source_target_pairs={{0,4},{4,8},{8,12},{12,14},{14,10},{10,6},{6,2},{2,0},{1,5},{5,9},... | collective-permute-start | bytes 811016 | tf_op jit(solution)/shard_map/ppermute | solution.py:348
  20.1 19.6 %collective-permute-start.6 = (bf16[1056,128]{1,0:T(8,128)(2,1)S(1)}, bf16[1056,128]{1,0:T(8,128)(2,1)S(1)}, u32[]{:S(2)}, u32[]{:S(2)}) collective-permute-start(bf16[1056,128]{1,0:T(8,128)(2,1)S(1)} %collective-permute-done.4.refs_4_), channel_id=1, source_target_pairs={{0,2},{4,0},{8,4},{12,8},{14,12},{10,14},{6,10},{2,6},{1,3},{5,1},... | collective-permute-start | bytes 811016 | tf_op jit(solution)/shard_map/ppermute | solution.py:348
  23.8 19.7 %collective-permute-start.10 = (bf16[1056,128]{1,0:T(8,128)(2,1)S(1)}, bf16[1056,128]{1,0:T(8,128)(2,1)S(1)}, u32[]{:S(2)}, u32[]{:S(2)}) collective-permute-start(bf16[1056,128]{1,0:T(8,128)(2,1)S(1)} %collective-permute-done.2.refs_0_), channel_id=1, source_target_pairs={{0,4},{4,8},{8,12},{12,14},{14,10},{10,6},{6,2},{2,0},{1,5},{5,9},... | collective-permute-start | bytes 811016 | tf_op jit(solution)/shard_map/ppermute | solution.py:348
  25.9 17.6 %collective-permute-start.11 = (bf16[1056,128]{1,0:T(8,128)(2,1)S(1)}, bf16[1056,128]{1,0:T(8,128)(2,1)S(1)}, u32[]{:S(2)}, u32[]{:S(2)}) collective-permute-start(bf16[1056,128]{1,0:T(8,128)(2,1)S(1)} %collective-permute-done.9.refs_3_), channel_id=1, source_target_pairs={{0,2},{4,0},{8,4},{12,8},{14,12},{10,14},{6,10},{2,6},{1,3},{5,1},... | collective-permute-start | bytes 811016 | tf_op jit(solution)/shard_map/ppermute | solution.py:348
  28.4 7.8 %collective-permute-start.7 = (f32[8,128]{1,0:T(8,128)S(1)}, f32[8,128]{1,0:T(8,128)S(1)}, u32[]{:S(2)}, u32[]{:S(2)}) collective-permute-start(f32[8,128]{1,0:T(8,128)S(1)} %get-tuple-element.41), channel_id=1, source_target_pairs={{0,2},{4,0},{8,4},{12,8},{14,12},{10,14},{6,10},{2,6},{1,3},{5,1},... | collective-permute-start | bytes 12296 | tf_op jit(solution)/shard_map/ppermute | solution.py:348
  36.2 3.6 %collective-permute-start.8 = (f32[8,128]{1,0:T(8,128)S(1)}, f32[8,128]{1,0:T(8,128)S(1)}, u32[]{:S(2)}, u32[]{:S(2)}) collective-permute-start(f32[8,128]{1,0:T(8,128)S(1)} %get-tuple-element.42), channel_id=1, source_target_pairs={{0,4},{4,8},{8,12},{12,14},{14,10},{10,6},{6,2},{2,0},{1,5},{5,9},... | collective-permute-start | bytes 12296 | tf_op jit(solution)/shard_map/ppermute | solution.py:348
  39.8 9.1 %collective-permute-start.12 = (bf16[1056,128]{1,0:T(8,128)(2,1)S(1)}, bf16[1056,128]{1,0:T(8,128)(2,1)S(1)}, u32[]{:S(2)}, u32[]{:S(2)}) collective-permute-start(bf16[1056,128]{1,0:T(8,128)(2,1)S(1)} %collective-permute-done.5.refs_1_), channel_id=1, source_target_pairs={{0,4},{4,8},{8,12},{12,14},{14,10},{10,6},{6,2},{2,0},{1,5},{5,9},... | collective-permute-start | bytes 811016 | tf_op jit(solution)/shard_map/ppermute | solution.py:348
  41.3 10.2 %collective-permute-start.13 = (bf16[1056,128]{1,0:T(8,128)(2,1)S(1)}, bf16[1056,128]{1,0:T(8,128)(2,1)S(1)}, u32[]{:S(2)}, u32[]{:S(2)}) collective-permute-start(bf16[1056,128]{1,0:T(8,128)(2,1)S(1)} %collective-permute-done.6.refs_2_), channel_id=1, source_target_pairs={{0,2},{4,0},{8,4},{12,8},{14,12},{10,14},{6,10},{2,6},{1,3},{5,1},... | collective-permute-start | bytes 811016 | tf_op jit(solution)/shard_map/ppermute | solution.py:348
  43.5 13.7 %collective-permute-start.14 = (bf16[1056,128]{1,0:T(8,128)(2,1)S(1)}, bf16[1056,128]{1,0:T(8,128)(2,1)S(1)}, u32[]{:S(2)}, u32[]{:S(2)}) collective-permute-start(bf16[1056,128]{1,0:T(8,128)(2,1)S(1)} %collective-permute-done.10.refs_0_), channel_id=1, source_target_pairs={{0,4},{4,8},{8,12},{12,14},{14,10},{10,6},{6,2},{2,0},{1,5},{5,9},... | collective-permute-start | bytes 811016 | tf_op jit(solution)/shard_map/ppermute | solution.py:348
  45.2 12.0 %collective-permute-start.15 = (bf16[1056,128]{1,0:T(8,128)(2,1)S(1)}, bf16[1056,128]{1,0:T(8,128)(2,1)S(1)}, u32[]{:S(2)}, u32[]{:S(2)}) collective-permute-start(bf16[1056,128]{1,0:T(8,128)(2,1)S(1)} %collective-permute-done.11.refs_3_), channel_id=1, source_target_pairs={{0,2},{4,0},{8,4},{12,8},{14,12},{10,14},{6,10},{2,6},{1,3},{5,1},... | collective-permute-start | bytes 811016 | tf_op jit(solution)/shard_map/ppermute | solution.py:348
  45.6 8.8 %collective-permute-start.16 = (f32[8,128]{1,0:T(8,128)S(1)}, f32[8,128]{1,0:T(8,128)S(1)}, u32[]{:S(2)}, u32[]{:S(2)}) collective-permute-start(f32[8,128]{1,0:T(8,128)S(1)} %get-tuple-element.51), channel_id=1, source_target_pairs={{0,6},{4,2},{8,0},{12,4},{14,8},{10,12},{6,14},{2,10},{1,7},{5,3},... | collective-permute-start | bytes 12296 | tf_op jit(solution)/shard_map/ppermute | solution.py:348
  48.9 8.3 %collective-permute-start.17 = (f32[8,128]{1,0:T(8,128)S(1)}, f32[8,128]{1,0:T(8,128)S(1)}, u32[]{:S(2)}, u32[]{:S(2)}) collective-permute-start(f32[8,128]{1,0:T(8,128)S(1)} %get-tuple-element.52), channel_id=1, source_target_pairs={{0,8},{4,12},{8,14},{12,10},{14,6},{10,2},{6,0},{2,4},{1,9},{5,13}... | collective-permute-start | bytes 12296 | tf_op jit(solution)/shard_map/ppermute | solution.py:348
  53.3 5.8 %collective-permute-start.18 = (f32[8,128]{1,0:T(8,128)S(1)}, f32[8,128]{1,0:T(8,128)S(1)}, u32[]{:S(2)}, u32[]{:S(2)}) collective-permute-start(f32[8,128]{1,0:T(8,128)S(1)} %get-tuple-element.62), channel_id=1, source_target_pairs={{0,10},{4,6},{8,2},{12,0},{14,4},{10,8},{6,12},{2,14},{1,11},{5,7}... | collective-permute-start | bytes 12296 | tf_op jit(solution)/shard_map/ppermute | solution.py:348
  54.4 5.4 %collective-permute-start.19 = (f32[8,128]{1,0:T(8,128)S(1)}, f32[8,128]{1,0:T(8,128)S(1)}, u32[]{:S(2)}, u32[]{:S(2)}) collective-permute-start(f32[8,128]{1,0:T(8,128)S(1)} %get-tuple-element.63), channel_id=1, source_target_pairs={{0,12},{4,14},{8,10},{12,6},{14,2},{10,0},{6,4},{2,8},{1,13},{5,15... | collective-permute-start | bytes 12296 | tf_op jit(solution)/shard_map/ppermute | solution.py:348
  57.9 6.4 %collective-permute-start.20 = (f32[8,128]{1,0:T(8,128)S(1)}, f32[8,128]{1,0:T(8,128)S(1)}, u32[]{:S(2)}, u32[]{:S(2)}) collective-permute-start(f32[8,128]{1,0:T(8,128)S(1)} %last_scores.1), channel_id=1, source_target_pairs={{0,14},{4,10},{8,6},{12,2},{14,0},{10,4},{6,8},{2,12},{1,15},{5,11... | collective-permute-start | bytes 12296 | tf_op jit(solution)/shard_map/ppermute | solution.py:348
  64.3 1.8 %collective-permute-start.21 = (f32[32,128]{1,0:T(8,128)S(1)}, f32[32,128]{1,0:T(8,128)S(1)}, u32[]{:S(2)}, u32[]{:S(2)}) collective-permute-start(f32[32,128]{1,0:T(8,128)S(1)} %unpack.1), channel_id=1, source_target_pairs={{0,1},{1,0},{2,3},{3,2},{4,5},{5,4},{6,7},{7,6},{8,9},{9,8},{10,11... | collective-permute-start | bytes 49160 | tf_op jit(solution)/shard_map/ppermute | solution.py:386

commit v6 on v5

--- a/solution.py
+++ b/solution.py
@@ -42,6 +42,7 @@
 
 
 ROW_SHIFT = BLK_DEV * BW // 2
+FACTS = ACT // 2 * 2 * KPB
 
 
 def facts_for(owner_id, owner, first_row, feats, acts):
@@ -112,12 +113,11 @@
 def prepare(block_slot, active_blocks, feature_idx, acts, grad_out, owners):
     tok_rows, half_width = grad_out.shape
     plain = half_width // 256 * tok_rows
-    extra = owners // 2 * 2 * KPB
     return pl.pallas_call(
         functools.partial(prepare_kernel, owners),
         out_shape=(
-            pltpu.VMEM((plain + extra, 128), grad_out.dtype),
-            pltpu.VMEM((plain + extra, 128), grad_out.dtype),
+            pltpu.VMEM((plain + FACTS, 128), grad_out.dtype),
+            pltpu.VMEM((plain + FACTS, 128), grad_out.dtype),
             pltpu.VMEM((2 * KPB, tok_rows), jnp.float32),
             pltpu.VMEM((ACT, tok_rows), jnp.int32),
         ),
@@ -187,8 +187,7 @@
 
 
 def facts_in(piece, distance, tok_rows):
-    extra = 2 * KPB * (lax.axis_size("dp") // 2)
-    facts = piece[piece.shape[0] - extra :, :].astype(jnp.float32)
+    facts = piece[piece.shape[0] - FACTS :, :].astype(jnp.float32)
     return facts[(abs(distance) - 1) * 2 * KPB : abs(distance) * 2 * KPB]
 
 
@@ -200,7 +199,8 @@
     return jnp.concatenate(rows, axis=0) if len(rows) > 1 else rows[0]
 
 
-def add_picks(facts, decoder, pieces, picked):
+def picks_of(facts, decoder, pieces):
+    picks = []
     tok_rows = facts[0].shape[1]
     cut = decoder.shape[1] // 2
     for first in range(0, len(facts), 2):
@@ -220,7 +220,8 @@
             scores = part if scores is None else scores + part
         for i in range(first, first + count):
             here = scores[:, (i - first) * tok_rows : (i - first + 1) * tok_rows]
-            picked[i][...] = jnp.concatenate(pick(here, facts[i]) * 2, axis=0)
+            picks.append(jnp.concatenate(pick(here, facts[i]) * 2, axis=0))
+    return picks
 
 
 def gradient_blocks(facts, pieces, width):
@@ -234,7 +235,7 @@
             yield slice(side * cut + j * 128, side * cut + (j + 2) * 128), part
 
 
-def absorb_kernel(distances, later, decoder, own_facts, *refs):
+def absorb_kernel(distances, later, split, decoder, own_facts, *refs):
     count = len(distances)
     pieces, refs = refs[: 2 * count], refs[2 * count :]
     picked, total = refs[-1 - count : -1], refs[-1]
@@ -243,19 +244,25 @@
         own_facts[...] if d == 0 else facts_in(pieces[2 * i + (d > 0)], d, tok_rows)
         for i, d in enumerate(distances)
     ]
-    add_picks(facts, decoder, pieces, picked)
+    picks = picks_of(facts, decoder, pieces)
+    if split:
+        first = lax.axis_index("width") == 0
+        picks = jnp.where(first, *picks), jnp.where(first, *picks[::-1])
+    for target, values in zip(picked, picks):
+        target[...] = values
     for columns, part in gradient_blocks(facts, pieces, decoder.shape[1]):
         total[:, columns] = refs[0][:, columns] + part if later else part
 
 
 def absorb(distances, pairs, decoder, own_facts, total=None):
+    later = total is not None
     tok_rows = own_facts.shape[1]
     operands = [kept(decoder), kept(own_facts)]
     operands += [kept(piece) for pair in pairs for piece in pair]
     operands += [] if total is None else [kept(total)]
     count = len(distances)
     *picked, total = pl.pallas_call(
-        functools.partial(absorb_kernel, distances, total is not None),
+        functools.partial(absorb_kernel, distances, later, later),
         out_shape=(
             *[pltpu.VMEM((2 * KPB, tok_rows), jnp.float32)] * count,
             pltpu.VMEM(decoder.shape, jnp.float32),
@@ -271,7 +278,7 @@
 
 def last_scores_kernel(distance, decoder, left, right, picked):
     facts = [facts_in(left, distance, picked.shape[1])]
-    add_picks(facts, decoder, (left, right), [picked])
+    picked[...] = picks_of(facts, decoder, (left, right))[0]
 
 
 def last_scores(distance, pair, decoder, tok_rows):
@@ -315,21 +322,68 @@
     )(kept(pair[0]), kept(pair[1]), kept(total))
 
 
-def unpack_kernel(distances, owners, slots, *refs):
-    returned, out = refs[:-1], refs[-1]
+def stamp_kernel(left, right, for_left, for_right, left_out, right_out, rows, sems):
+    start = left.shape[0] - FACTS
+    targets = (left_out, right_out)
+    for i, piece in enumerate((left, right)):
+        pltpu.make_async_copy(
+            piece.at[start : start + 16, :], rows.at[i], sems.at[i]
+        ).start()
+    for i, values in enumerate((for_left, for_right)):
+        pltpu.make_async_copy(
+            left.at[start : start + 16, :], rows.at[i], sems.at[i]
+        ).wait()
+        value = values[:KPB]
+        high = value.astype(jnp.bfloat16).astype(jnp.float32)
+        low = value - high
+        facts = rows[i].astype(jnp.float32)[2 * KPB :]
+        rows[i] = jnp.concatenate([high, low, facts], axis=0).astype(jnp.bfloat16)
+        pltpu.make_async_copy(
+            rows.at[i], targets[i].at[start : start + 16, :], sems.at[2 + i]
+        ).start()
+    for i in range(2):
+        pltpu.make_async_copy(
+            rows.at[i], targets[i].at[start : start + 16, :], sems.at[2 + i]
+        ).wait()
+
+
+def stamp(pieces, values):
+    return pl.pallas_call(
+        stamp_kernel,
+        out_shape=tuple(pltpu.VMEM(piece.shape, piece.dtype) for piece in pieces),
+        in_specs=[ANY, ANY, VMEM, VMEM],
+        out_specs=(ANY, ANY),
+        scratch_shapes=[
+            pltpu.VMEM((2, 16, 128), jnp.bfloat16),
+            pltpu.SemaphoreType.DMA((4,)),
+        ],
+        input_output_aliases={0: 0, 1: 1},
+        compiler_params=limit(4),
+        name="stamp",
+    )(*[kept(piece) for piece in pieces], *[kept(value) for value in values])
+
+
+def unpack_kernel(owners, slots, own, left, right, second, third, opposite, out):
     owner = slots[...] // BLK_DEV
-    mine = [owner == peer_at(d, owners) for d in distances]
+    start = left.shape[0] - FACTS
+    way = 1 - 2 * lax.axis_index("width")
+    returned = [(0, own[...])]
+    for distance, piece in ((-1, left), (1, right)):
+        rows = piece[start : start + 16, :].astype(jnp.float32)
+        returned.append((distance, rows[:KPB] + rows[KPB : 2 * KPB]))
+    returned += [(2 * way, second[...]), (3 * way, third[...]), (4, opposite[...])]
+    mine = [owner == peer_at(distance, owners) for distance, _ in returned]
     for k in range(KPB):
         total = jnp.zeros(owner.shape, jnp.float32)
-        for here, values in zip(mine, returned):
+        for here, (_, values) in zip(mine, returned):
             total = jnp.where(here, values[k : k + 1, :], total)
         out[pl.ds(k, ACT, stride=KPB), :] = total
 
 
-def unpack(distances, returned, slots):
+def unpack(slots, *returned):
     tok_rows = slots.shape[1]
     return pl.pallas_call(
-        functools.partial(unpack_kernel, distances, lax.axis_size("dp")),
+        functools.partial(unpack_kernel, lax.axis_size("dp")),
         out_shape=pltpu.VMEM((ACT * KPB, tok_rows), jnp.float32),
         in_specs=[VMEM] * (1 + len(returned)),
         out_specs=VMEM,
@@ -355,6 +409,16 @@
         right, left = pieces
         return shift(right, 1), shift(left, -1)
 
+    def other_core(x):
+        return lax.ppermute(x, "width", ((0, 1), (1, 0)))
+
+    def return_by(distance, mine, others):
+        pairs = []
+        for i in range(owners):
+            pairs.append((2 * ring[i], 2 * ring[(i - distance) % owners]))
+            pairs.append((2 * ring[i] + 1, 2 * ring[(i + distance) % owners] + 1))
+        return lax.ppermute(mine + other_core(others), ("dp", "width"), pairs)
+
     left, right, own_facts, slots = prepare(
         block_slot, active_blocks, feature_idx, acts, grad_out, owners
     )
@@ -364,26 +428,24 @@
     first_1, decoder = lax.optimization_barrier((first_1, decoder))
     first_2 = hop(first_1)
     second_2 = crossed(second_1)
-    first_3 = hop(first_2)
     pairs = [(left, right), (first_1[0], second_1[0]), (second_1[1], first_1[1])]
     (own, onward, back), total = absorb((0, -1, 1), pairs, decoder, own_facts)
-    returned = [own, shift(onward, -1), shift(back, 1)]
-    total, second_2, returned = lax.optimization_barrier((total, second_2, returned))
+    first_2 = stamp(first_2, (back, onward))
+    first_3 = hop(first_2)
     second_3 = crossed(second_2)
     pairs = [(first_2[0], second_2[0]), (second_2[1], first_2[1])]
-    (onward, back), total = absorb((-2, 2), pairs, decoder, own_facts, total)
+    (mine, others), total = absorb((-2, 2), pairs, decoder, own_facts, total)
     total, first_3 = lax.optimization_barrier((total, first_3))
-    returned += [shift(onward, -2), shift(back, 2)]
+    second = return_by(2, mine, others)
     first_4 = hop(first_3)
     pairs = [(first_3[0], second_3[0]), (second_3[1], first_3[1])]
-    (onward, back), total = absorb((-3, 3), pairs, decoder, own_facts, total)
-    returned += [shift(onward, -3), shift(back, 3)]
-    total, first_4, returned[3:5] = lax.optimization_barrier((total, first_4, returned[3:5]))
-    onward = last_scores(4, first_4, decoder, tok_rows)
-    returned.append(shift(onward, -4))
+    (mine, others), total = absorb((-3, 3), pairs, decoder, own_facts, total)
+    third = return_by(3, mine, others)
+    total, first_4, second = lax.optimization_barrier((total, first_4, second))
+    opposite = shift(last_scores(4, first_4, decoder, tok_rows), -4)
     decoder_grad = last_gradients(4, first_4, total, tok_rows)
-    act_grad = unpack((0, 1, -1, 2, -2, 3, -3, 4), returned, slots)
-    act_grad = act_grad + lax.ppermute(act_grad, "width", ((0, 1), (1, 0)))
+    act_grad = unpack(slots, own, *first_3, second, third, opposite)
+    act_grad = act_grad + other_core(act_grad)
     return (decoder_grad, act_grad.T)
 
 

time: 67.1 us -> 60.1 us (0.90)
  starting transfers between devices: 27.3 us -> 23.7 us
  waiting for transfers between devices: 26.9 us -> 23.4 us
    ppermute x21 -> x15, starting transfers between devices: 27.3 us -> 18.5 us  [shift(): return lax.ppermute(x, 'dp', pairs)]
    ppermute x1 -> x5, starting transfers between devices: 0.07 us -> 5.18 us  [the longest x2 5.03 us: return_by(): return lax.ppermute(mine + other_core(others), ('dp', 'width'), pairs)]
    ppermute x21 -> x15, waiting for transfers between devices: 26.9 us -> 23.4 us  [shift(): return lax.ppermute(x, 'dp', pairs)]
    pallas_call x4 -> x5, Pallas kernels: 5.89 us -> 5.97 us  [the longest x3 5.87 us: absorb(): pl.pallas_call(functools.partial(absorb_kernel, distances, later, later),...]
  transfers between devices with their start and end apart: 22 -> 20, of which waited for: 10 -> 11; matrix products, arithmetic and copies ran while one was open for 0% -> 0% of each run, Pallas kernels for 15% -> 17%
where the time goes in v6:
time: 60.1 us; the launch traced here: 59.8 us
  starting transfers between devices  23.7 us (39%)
  waiting for transfers between devices  23.4 us (39%)
  Pallas kernels  11.3 us (19%)
  between operations  0.76 us (1%)
  other arithmetic  0.62 us (1%)
    ppermute x15, waiting for transfers between devices, shift(): return lax.ppermute(x, 'dp', pairs)  23.4 us
    ppermute x15, starting transfers between devices, shift(): return lax.ppermute(x, 'dp', pairs)  18.5 us
    pallas_call x3, Pallas kernels, absorb(): pl.pallas_call(functools.partial(absorb_kernel, distances, later, later),...  5.87 us
    ppermute x2, starting transfers between devices, return_by(): return lax.ppermute(mine + other_core(others), ('dp', 'width'), pairs)  5.03 us
    pallas_call x1, Pallas kernels, last_gradients(): pl.pallas_call(functools.partial(last_gradients_kernel, distance, tok_row...  1.74 us
    pallas_call x1, Pallas kernels, fetch(): pl.pallas_call(fetch_kernel, out_shape=pltpu.VMEM(x.shape, x.dtype), in_s...  1.6 us
    pallas_call x1, Pallas kernels, prepare(): pl.pallas_call(functools.partial(prepare_kernel, owners), out_shape=(pltp...  1.23 us
  transfers between devices with their start and end apart: 20, of which 11 were waited for; matrix products, arithmetic and copies ran while one was open for 0% of the time, Pallas kernels for 17%

profile of v6, /device:TPU:0, one launch (start us, length us, event | category | flops | bytes accessed | tf_op | source)
XLA Modules:
  0.0 59.8 jit_solution(12235274346179144897)
XLA Ops:
  0.6 1.2 %prepare.1 = (bf16[1056,128]{1,0:T(8,128)(2,1)S(1)}, bf16[1056,128]{1,0:T(8,128)(2,1)S(1)}, f32[8,128]{1,0:T(8,128)S(1)}, s32[8,128]{1,0:T(8,128)S(1)}) custom-call(s32[32]{0:T(128)} %refs_0_.1, s32[8,128]{1,0:T(8,128)} %bitcast.7, s32[32,128]{1,0:T(8,128)} %bitcast.5, bf16[32,128]{1,0:T(8,128)(2,1)} %bitcast.6, bf16[128,2048]{1,0:T(8,128)(2,1)} %refs_4_.1), custom_call_target="tpu_custom_call" | custom-call | tf_op jit(solution)/shard_map/prepare/pallas_call | solution.py:116
  1.9 3.1 %collective-permute-start = (bf16[1056,128]{1,0:T(8,128)(2,1)S(1)}, bf16[1056,128]{1,0:T(8,128)(2,1)S(1)}, u32[]{:S(2)}, u32[]{:S(2)}) collective-permute-start(bf16[1056,128]{1,0:T(8,128)(2,1)S(1)} %get-tuple-element.28.refs_0_), channel_id=1, source_target_pairs={{0,4},{4,8},{8,12},{12,14},{14,10},{10,6},{6,2},{2,0},{1,5},{5,9},... | collective-permute-start | bytes 811016 | tf_op jit(solution)/shard_map/ppermute | solution.py:402
  4.9 0.0 collective-permute-start.1
  5.0 2.0 %collective-permute-start.4 = (bf16[1056,128]{1,0:T(8,128)(2,1)S(1)}, bf16[1056,128]{1,0:T(8,128)(2,1)S(1)}, u32[]{:S(2)}, u32[]{:S(2)}) collective-permute-start(bf16[1056,128]{1,0:T(8,128)(2,1)S(1)} %get-tuple-element.29.refs_1_), channel_id=1, source_target_pairs={{0,4},{4,8},{8,12},{12,14},{14,10},{10,6},{6,2},{2,0},{1,5},{5,9},... | collective-permute-start | bytes 811016 | tf_op jit(solution)/shard_map/ppermute | solution.py:402
  7.0 0.0 collective-permute-start.5
  7.0 1.6 %fetch.1.decoder = bf16[512,2048]{1,0:T(8,128)(2,1)S(1)} custom-call(bf16[512,2048]{1,0:T(8,128)(2,1)} %source.1), custom_call_target="tpu_custom_call" | custom-call | tf_op jit(solution)/shard_map/fetch/pallas_call | solution.py:147
  8.6 3.6 %collective-permute-done.refs_2_ = bf16[1056,128]{1,0:T(8,128)(2,1)S(1)} collective-permute-done((bf16[1056,128]{1,0:T(8,128)(2,1)S(1)}, bf16[1056,128]{1,0:T(8,128)(2,1)S(1)}, u32[]{:S(2)}, u32[]{:S(2)}) %collective-permute-start) | collective-permute-done | bytes 270368 | tf_op jit(solution)/shard_map/ppermute | solution.py:402
  12.2 2.2 %collective-permute-done.1.refs_5_ = bf16[1056,128]{1,0:T(8,128)(2,1)S(1)} collective-permute-done((bf16[1056,128]{1,0:T(8,128)(2,1)S(1)}, bf16[1056,128]{1,0:T(8,128)(2,1)S(1)}, u32[]{:S(2)}, u32[]{:S(2)}) %collective-permute-start.1) | collective-permute-done | bytes 270368 | tf_op jit(solution)/shard_map/ppermute | solution.py:402
  14.4 1.6 %collective-permute-start.2 = (bf16[1056,128]{1,0:T(8,128)(2,1)S(1)}, bf16[1056,128]{1,0:T(8,128)(2,1)S(1)}, u32[]{:S(2)}, u32[]{:S(2)}) collective-permute-start(bf16[1056,128]{1,0:T(8,128)(2,1)S(1)} %collective-permute-done.refs_2_), channel_id=1, source_target_pairs={{0,4},{4,8},{8,12},{12,14},{14,10},{10,6},{6,2},{2,0},{1,5},{5,9},... | collective-permute-start | bytes 811016 | tf_op jit(solution)/shard_map/ppermute | solution.py:402
  15.9 0.4 collective-permute-start.3
  16.4 1.6 %collective-permute-done.4.refs_3_ = bf16[1056,128]{1,0:T(8,128)(2,1)S(1)} collective-permute-done((bf16[1056,128]{1,0:T(8,128)(2,1)S(1)}, bf16[1056,128]{1,0:T(8,128)(2,1)S(1)}, u32[]{:S(2)}, u32[]{:S(2)}) %collective-permute-start.4) | collective-permute-done | bytes 270368 | tf_op jit(solution)/shard_map/ppermute | solution.py:402
  18.0 2.1 %collective-permute-start.6 = (bf16[1056,128]{1,0:T(8,128)(2,1)S(1)}, bf16[1056,128]{1,0:T(8,128)(2,1)S(1)}, u32[]{:S(2)}, u32[]{:S(2)}) collective-permute-start(bf16[1056,128]{1,0:T(8,128)(2,1)S(1)} %collective-permute-done.4.refs_3_), channel_id=1, source_target_pairs={{0,4},{4,8},{8,12},{12,14},{14,10},{10,6},{6,2},{2,0},{1,5},{5,9},... | collective-permute-start | bytes 811016 | tf_op jit(solution)/shard_map/ppermute | solution.py:402
  20.1 0.0 collective-permute-done.5.refs_4_
  20.1 0.0 collective-permute-start.7
  20.2 2.4 %absorb.3 = (f32[8,128]{1,0:T(8,128)S(1)}, f32[8,128]{1,0:T(8,128)S(1)}, f32[8,128]{1,0:T(8,128)S(1)}, f32[512,2048]{1,0:T(8,128)S(1)}) custom-call(bf16[512,2048]{1,0:T(8,128)(2,1)S(1)} %fetch.1.decoder, f32[8,128]{1,0:T(8,128)S(1)} %get-tuple-element.31.own_facts, bf16[1056,128]{1,0:T(8,128)(2,1)S(1)} %get-tuple-element.28.refs_0_, ...), custom_call_target="tpu_custom_call" | custom-call | tf_op jit(solution)/shard_map/absorb/pallas_call | solution.py:264
  22.6 1.2 %collective-permute-done.2.left = bf16[1056,128]{1,0:T(8,128)(2,1)S(1)} collective-permute-done((bf16[1056,128]{1,0:T(8,128)(2,1)S(1)}, bf16[1056,128]{1,0:T(8,128)(2,1)S(1)}, u32[]{:S(2)}, u32[]{:S(2)}) %collective-permute-start.2) | collective-permute-done | bytes 270368 | tf_op jit(solution)/shard_map/ppermute | solution.py:402
  23.8 2.2 %collective-permute-done.3.right = bf16[1056,128]{1,0:T(8,128)(2,1)S(1)} collective-permute-done((bf16[1056,128]{1,0:T(8,128)(2,1)S(1)}, bf16[1056,128]{1,0:T(8,128)(2,1)S(1)}, u32[]{:S(2)}, u32[]{:S(2)}) %collective-permute-start.3) | collective-permute-done | bytes 270368 | tf_op jit(solution)/shard_map/ppermute | solution.py:402
  25.9 0.1 stamp.1
  26.0 1.6 %collective-permute-start.8 = (bf16[1056,128]{1,0:T(8,128)(2,1)S(1)}, bf16[1056,128]{1,0:T(8,128)(2,1)S(1)}, u32[]{:S(2)}, u32[]{:S(2)}) collective-permute-start(bf16[1056,128]{1,0:T(8,128)(2,1)S(1)} %get-tuple-element.36.refs_0_), channel_id=1, source_target_pairs={{0,4},{4,8},{8,12},{12,14},{14,10},{10,6},{6,2},{2,0},{1,5},{5,9},... | collective-permute-start | bytes 811016 | tf_op jit(solution)/shard_map/ppermute | solution.py:402
  27.7 0.4 collective-permute-start.9
  28.1 1.5 %collective-permute-done.6.refs_1_ = bf16[1056,128]{1,0:T(8,128)(2,1)S(1)} collective-permute-done((bf16[1056,128]{1,0:T(8,128)(2,1)S(1)}, bf16[1056,128]{1,0:T(8,128)(2,1)S(1)}, u32[]{:S(2)}, u32[]{:S(2)}) %collective-permute-start.6) | collective-permute-done | bytes 270368 | tf_op jit(solution)/shard_map/ppermute | solution.py:402
  29.6 2.1 %collective-permute-start.10 = (bf16[1056,128]{1,0:T(8,128)(2,1)S(1)}, bf16[1056,128]{1,0:T(8,128)(2,1)S(1)}, u32[]{:S(2)}, u32[]{:S(2)}) collective-permute-start(bf16[1056,128]{1,0:T(8,128)(2,1)S(1)} %collective-permute-done.6.refs_1_), channel_id=1, source_target_pairs={{0,4},{4,8},{8,12},{12,14},{14,10},{10,6},{6,2},{2,0},{1,5},{5,9},... | collective-permute-start | bytes 811016 | tf_op jit(solution)/shard_map/ppermute | solution.py:402
  31.7 0.0 collective-permute-done.7.refs_2_
  31.7 0.0 collective-permute-start.11
  31.7 1.7 %absorb.4 = (f32[8,128]{1,0:T(8,128)S(1)}, f32[8,128]{1,0:T(8,128)S(1)}, f32[512,2048]{1,0:T(8,128)S(1)}) custom-call(bf16[512,2048]{1,0:T(8,128)(2,1)S(1)} %fetch.1.decoder, f32[8,128]{1,0:T(8,128)S(1)} %get-tuple-element.31.own_facts, bf16[1056,128]{1,0:T(8,128)(2,1)S(1)} %get-tuple-element.36.refs_0_, ...), custom_call_target="tpu_custom_call", output_to_operand_aliasing={{2}: (6, {})} | custom-call | tf_op jit(solution)/shard_map/absorb/pallas_call | solution.py:264
  33.5 2.0 %collective-permute-done.8.refs_0_.left = bf16[1056,128]{1,0:T(8,128)(2,1)S(1)} collective-permute-done((bf16[1056,128]{1,0:T(8,128)(2,1)S(1)}, bf16[1056,128]{1,0:T(8,128)(2,1)S(1)}, u32[]{:S(2)}, u32[]{:S(2)}) %collective-permute-start.8) | collective-permute-done | bytes 270368 | tf_op jit(solution)/shard_map/ppermute | solution.py:402
  35.5 2.0 %collective-permute-done.9.refs_3_.right = bf16[1056,128]{1,0:T(8,128)(2,1)S(1)} collective-permute-done((bf16[1056,128]{1,0:T(8,128)(2,1)S(1)}, bf16[1056,128]{1,0:T(8,128)(2,1)S(1)}, u32[]{:S(2)}, u32[]{:S(2)}) %collective-permute-start.9) | collective-permute-done | bytes 270368 | tf_op jit(solution)/shard_map/ppermute | solution.py:402
  37.5 1.6 %collective-permute-start.12 = (bf16[1056,128]{1,0:T(8,128)(2,1)S(1)}, bf16[1056,128]{1,0:T(8,128)(2,1)S(1)}, u32[]{:S(2)}, u32[]{:S(2)}) collective-permute-start(bf16[1056,128]{1,0:T(8,128)(2,1)S(1)} %collective-permute-done.8.refs_0_.left), channel_id=1, source_target_pairs={{0,4},{4,8},{8,12},{12,14},{14,10},{10,6},{6,2},{2,0},{1,5},{5,9},... | collective-permute-start | bytes 811016 | tf_op jit(solution)/shard_map/ppermute | solution.py:402
  39.1 0.4 collective-permute-start.13
  39.6 0.0 collective-permute-start.14
  39.6 1.7 %collective-permute-done.10.refs_1_ = bf16[1056,128]{1,0:T(8,128)(2,1)S(1)} collective-permute-done((bf16[1056,128]{1,0:T(8,128)(2,1)S(1)}, bf16[1056,128]{1,0:T(8,128)(2,1)S(1)}, u32[]{:S(2)}, u32[]{:S(2)}) %collective-permute-start.10) | collective-permute-done | bytes 270368 | tf_op jit(solution)/shard_map/ppermute | solution.py:402
  41.3 2.0 %collective-permute-done.11.refs_2_ = bf16[1056,128]{1,0:T(8,128)(2,1)S(1)} collective-permute-done((bf16[1056,128]{1,0:T(8,128)(2,1)S(1)}, bf16[1056,128]{1,0:T(8,128)(2,1)S(1)}, u32[]{:S(2)}, u32[]{:S(2)}) %collective-permute-start.11) | collective-permute-done | bytes 270368 | tf_op jit(solution)/shard_map/ppermute | solution.py:402
  43.3 1.7 %absorb.5 = (f32[8,128]{1,0:T(8,128)S(1)}, f32[8,128]{1,0:T(8,128)S(1)}, f32[512,2048]{1,0:T(8,128)S(1)}) custom-call(bf16[512,2048]{1,0:T(8,128)(2,1)S(1)} %fetch.1.decoder, f32[8,128]{1,0:T(8,128)S(1)} %get-tuple-element.31.own_facts, bf16[1056,128]{1,0:T(8,128)(2,1)S(1)} %collective-permute-done.8.refs_0_.left, ...), custom_call_target="tpu_custom_call", output_to_operand_aliasing={{2}: (6, {})} | custom-call | tf_op jit(solution)/shard_map/absorb/pallas_call | solution.py:264
  45.0 0.1 collective-permute-start.16
  45.1 0.0 collective-permute-done.14
  45.1 1.4 %collective-permute-start.15 = (f32[8,128]{1,0:T(8,128)S(1)}, f32[8,128]{1,0:T(8,128)S(1)}, u32[]{:S(2)}, u32[]{:S(2)}) collective-permute-start(f32[8,128]{1,0:T(8,128)S(1)} %add.9), channel_id=1, source_target_pairs={{0,6},{1,9},{4,2},{5,13},{8,0},{9,15},{12,4},{13,11},{14,8},{15,7}... | collective-permute-start | bytes 12296 | tf_op jit(solution)/shard_map/ppermute | solution.py:420
  46.6 0.0 collective-permute-done.16
  46.6 3.6 %collective-permute-start.17 = (f32[8,128]{1,0:T(8,128)S(1)}, f32[8,128]{1,0:T(8,128)S(1)}, u32[]{:S(2)}, u32[]{:S(2)}) collective-permute-start(f32[8,128]{1,0:T(8,128)S(1)} %add.10), channel_id=1, source_target_pairs={{0,10},{1,13},{4,6},{5,15},{8,2},{9,11},{12,0},{13,7},{14,4},{15,3... | collective-permute-start | bytes 12296 | tf_op jit(solution)/shard_map/ppermute | solution.py:420
  50.2 0.0 collective-permute-done.15.second
  50.2 0.0 collective-permute-done.12.left
  50.2 0.0 collective-permute-done.13.right
  50.2 0.7 %last_scores.1 = f32[8,128]{1,0:T(8,128)S(1)} custom-call(bf16[512,2048]{1,0:T(8,128)(2,1)S(1)} %fetch.1.decoder, bf16[1056,128]{1,0:T(8,128)(2,1)S(1)} %collective-permute-done.12.left, bf16[1056,128]{1,0:T(8,128)(2,1)S(1)} %collective-permute-done.13.right), custom_call_target="tpu_custom_call" | custom-call | tf_op jit(solution)/shard_map/last_scores/pallas_call | solution.py:285
  50.9 3.0 %collective-permute-start.18 = (f32[8,128]{1,0:T(8,128)S(1)}, f32[8,128]{1,0:T(8,128)S(1)}, u32[]{:S(2)}, u32[]{:S(2)}) collective-permute-start(f32[8,128]{1,0:T(8,128)S(1)} %last_scores.1), channel_id=1, source_target_pairs={{0,14},{4,10},{8,6},{12,2},{14,0},{10,4},{6,8},{2,12},{1,15},{5,11... | collective-permute-start | bytes 12296 | tf_op jit(solution)/shard_map/ppermute | solution.py:402
  53.9 0.0 collective-permute-done.17.third
  53.9 3.4 %collective-permute-done.18.opposite = f32[8,128]{1,0:T(8,128)S(1)} collective-permute-done((f32[8,128]{1,0:T(8,128)S(1)}, f32[8,128]{1,0:T(8,128)S(1)}, u32[]{:S(2)}, u32[]{:S(2)}) %collective-permute-start.18) | collective-permute-done | bytes 4128 | tf_op jit(solution)/shard_map/ppermute | solution.py:402
  57.3 0.1 collective-permute-start.19
  57.4 1.7 %last_gradients.1 = bf16[512,2048]{1,0:T(8,128)(2,1)} custom-call(bf16[1056,128]{1,0:T(8,128)(2,1)S(1)} %collective-permute-done.12.left, bf16[1056,128]{1,0:T(8,128)(2,1)S(1)} %collective-permute-done.13.right, f32[512,2048]{1,0:T(8,128)S(1)} %get-tuple-element.48.total), custom_call_target="tpu_custom_call" | custom-call | tf_op jit(solution)/shard_map/last_gradients/pallas_call | solution.py:311
  59.2 0.0 collective-permute-done.19
  59.2 0.6 %add_bitcast_fusion = f32[128,32]{0,1:T(8,128)} fusion(f32[32,128]{1,0:T(8,128)S(1)} %unpack.1, f32[32,128]{1,0:T(8,128)S(1)} %collective-permute-done.19), kind=kLoop, calls=%fused_computation | loop fusion | flops 4096 | bytes 49152 | tf_op jit(solution)/shard_map/transpose | solution.py:449
  (3 shorter events, 0.0 us)
Async XLA Ops:
  1.9 10.3 %collective-permute-start = (bf16[1056,128]{1,0:T(8,128)(2,1)S(1)}, bf16[1056,128]{1,0:T(8,128)(2,1)S(1)}, u32[]{:S(2)}, u32[]{:S(2)}) collective-permute-start(bf16[1056,128]{1,0:T(8,128)(2,1)S(1)} %get-tuple-element.28.refs_0_), channel_id=1, source_target_pairs={{0,4},{4,8},{8,12},{12,14},{14,10},{10,6},{6,2},{2,0},{1,5},{5,9},... | collective-permute-start | bytes 811016 | tf_op jit(solution)/shard_map/ppermute | solution.py:402
  4.9 9.4 %collective-permute-start.1 = (bf16[1056,128]{1,0:T(8,128)(2,1)S(1)}, bf16[1056,128]{1,0:T(8,128)(2,1)S(1)}, u32[]{:S(2)}, u32[]{:S(2)}) collective-permute-start(bf16[1056,128]{1,0:T(8,128)(2,1)S(1)} %get-tuple-element.29.refs_1_), channel_id=1, source_target_pairs={{0,2},{4,0},{8,4},{12,8},{14,12},{10,14},{6,10},{2,6},{1,3},{5,1},... | collective-permute-start | bytes 811016 | tf_op jit(solution)/shard_map/ppermute | solution.py:402
  5.0 13.0 %collective-permute-start.4 = (bf16[1056,128]{1,0:T(8,128)(2,1)S(1)}, bf16[1056,128]{1,0:T(8,128)(2,1)S(1)}, u32[]{:S(2)}, u32[]{:S(2)}) collective-permute-start(bf16[1056,128]{1,0:T(8,128)(2,1)S(1)} %get-tuple-element.29.refs_1_), channel_id=1, source_target_pairs={{0,4},{4,8},{8,12},{12,14},{14,10},{10,6},{6,2},{2,0},{1,5},{5,9},... | collective-permute-start | bytes 811016 | tf_op jit(solution)/shard_map/ppermute | solution.py:402
  7.0 13.2 %collective-permute-start.5 = (bf16[1056,128]{1,0:T(8,128)(2,1)S(1)}, bf16[1056,128]{1,0:T(8,128)(2,1)S(1)}, u32[]{:S(2)}, u32[]{:S(2)}) collective-permute-start(bf16[1056,128]{1,0:T(8,128)(2,1)S(1)} %get-tuple-element.28.refs_0_), channel_id=1, source_target_pairs={{0,2},{4,0},{8,4},{12,8},{14,12},{10,14},{6,10},{2,6},{1,3},{5,1},... | collective-permute-start | bytes 811016 | tf_op jit(solution)/shard_map/ppermute | solution.py:402
  14.4 9.4 %collective-permute-start.2 = (bf16[1056,128]{1,0:T(8,128)(2,1)S(1)}, bf16[1056,128]{1,0:T(8,128)(2,1)S(1)}, u32[]{:S(2)}, u32[]{:S(2)}) collective-permute-start(bf16[1056,128]{1,0:T(8,128)(2,1)S(1)} %collective-permute-done.refs_2_), channel_id=1, source_target_pairs={{0,4},{4,8},{8,12},{12,14},{14,10},{10,6},{6,2},{2,0},{1,5},{5,9},... | collective-permute-start | bytes 811016 | tf_op jit(solution)/shard_map/ppermute | solution.py:402
  15.9 10.0 %collective-permute-start.3 = (bf16[1056,128]{1,0:T(8,128)(2,1)S(1)}, bf16[1056,128]{1,0:T(8,128)(2,1)S(1)}, u32[]{:S(2)}, u32[]{:S(2)}) collective-permute-start(bf16[1056,128]{1,0:T(8,128)(2,1)S(1)} %collective-permute-done.1.refs_5_), channel_id=1, source_target_pairs={{0,2},{4,0},{8,4},{12,8},{14,12},{10,14},{6,10},{2,6},{1,3},{5,1},... | collective-permute-start | bytes 811016 | tf_op jit(solution)/shard_map/ppermute | solution.py:402
  18.0 11.6 %collective-permute-start.6 = (bf16[1056,128]{1,0:T(8,128)(2,1)S(1)}, bf16[1056,128]{1,0:T(8,128)(2,1)S(1)}, u32[]{:S(2)}, u32[]{:S(2)}) collective-permute-start(bf16[1056,128]{1,0:T(8,128)(2,1)S(1)} %collective-permute-done.4.refs_3_), channel_id=1, source_target_pairs={{0,4},{4,8},{8,12},{12,14},{14,10},{10,6},{6,2},{2,0},{1,5},{5,9},... | collective-permute-start | bytes 811016 | tf_op jit(solution)/shard_map/ppermute | solution.py:402
  20.1 11.6 %collective-permute-start.7 = (bf16[1056,128]{1,0:T(8,128)(2,1)S(1)}, bf16[1056,128]{1,0:T(8,128)(2,1)S(1)}, u32[]{:S(2)}, u32[]{:S(2)}) collective-permute-start(bf16[1056,128]{1,0:T(8,128)(2,1)S(1)} %collective-permute-done.5.refs_4_), channel_id=1, source_target_pairs={{0,2},{4,0},{8,4},{12,8},{14,12},{10,14},{6,10},{2,6},{1,3},{5,1},... | collective-permute-start | bytes 811016 | tf_op jit(solution)/shard_map/ppermute | solution.py:402
  26.0 9.5 %collective-permute-start.8 = (bf16[1056,128]{1,0:T(8,128)(2,1)S(1)}, bf16[1056,128]{1,0:T(8,128)(2,1)S(1)}, u32[]{:S(2)}, u32[]{:S(2)}) collective-permute-start(bf16[1056,128]{1,0:T(8,128)(2,1)S(1)} %get-tuple-element.36.refs_0_), channel_id=1, source_target_pairs={{0,4},{4,8},{8,12},{12,14},{14,10},{10,6},{6,2},{2,0},{1,5},{5,9},... | collective-permute-start | bytes 811016 | tf_op jit(solution)/shard_map/ppermute | solution.py:402
  27.7 9.9 %collective-permute-start.9 = (bf16[1056,128]{1,0:T(8,128)(2,1)S(1)}, bf16[1056,128]{1,0:T(8,128)(2,1)S(1)}, u32[]{:S(2)}, u32[]{:S(2)}) collective-permute-start(bf16[1056,128]{1,0:T(8,128)(2,1)S(1)} %get-tuple-element.37.refs_3_), channel_id=1, source_target_pairs={{0,2},{4,0},{8,4},{12,8},{14,12},{10,14},{6,10},{2,6},{1,3},{5,1},... | collective-permute-start | bytes 811016 | tf_op jit(solution)/shard_map/ppermute | solution.py:402
  29.6 11.7 %collective-permute-start.10 = (bf16[1056,128]{1,0:T(8,128)(2,1)S(1)}, bf16[1056,128]{1,0:T(8,128)(2,1)S(1)}, u32[]{:S(2)}, u32[]{:S(2)}) collective-permute-start(bf16[1056,128]{1,0:T(8,128)(2,1)S(1)} %collective-permute-done.6.refs_1_), channel_id=1, source_target_pairs={{0,4},{4,8},{8,12},{12,14},{14,10},{10,6},{6,2},{2,0},{1,5},{5,9},... | collective-permute-start | bytes 811016 | tf_op jit(solution)/shard_map/ppermute | solution.py:402
  31.7 11.6 %collective-permute-start.11 = (bf16[1056,128]{1,0:T(8,128)(2,1)S(1)}, bf16[1056,128]{1,0:T(8,128)(2,1)S(1)}, u32[]{:S(2)}, u32[]{:S(2)}) collective-permute-start(bf16[1056,128]{1,0:T(8,128)(2,1)S(1)} %collective-permute-done.7.refs_2_), channel_id=1, source_target_pairs={{0,2},{4,0},{8,4},{12,8},{14,12},{10,14},{6,10},{2,6},{1,3},{5,1},... | collective-permute-start | bytes 811016 | tf_op jit(solution)/shard_map/ppermute | solution.py:402
  37.5 12.7 %collective-permute-start.12 = (bf16[1056,128]{1,0:T(8,128)(2,1)S(1)}, bf16[1056,128]{1,0:T(8,128)(2,1)S(1)}, u32[]{:S(2)}, u32[]{:S(2)}) collective-permute-start(bf16[1056,128]{1,0:T(8,128)(2,1)S(1)} %collective-permute-done.8.refs_0_.left), channel_id=1, source_target_pairs={{0,4},{4,8},{8,12},{12,14},{14,10},{10,6},{6,2},{2,0},{1,5},{5,9},... | collective-permute-start | bytes 811016 | tf_op jit(solution)/shard_map/ppermute | solution.py:402
  39.1 11.1 %collective-permute-start.13 = (bf16[1056,128]{1,0:T(8,128)(2,1)S(1)}, bf16[1056,128]{1,0:T(8,128)(2,1)S(1)}, u32[]{:S(2)}, u32[]{:S(2)}) collective-permute-start(bf16[1056,128]{1,0:T(8,128)(2,1)S(1)} %collective-permute-done.9.refs_3_.right), channel_id=1, source_target_pairs={{0,2},{4,0},{8,4},{12,8},{14,12},{10,14},{6,10},{2,6},{1,3},{5,1},... | collective-permute-start | bytes 811016 | tf_op jit(solution)/shard_map/ppermute | solution.py:402
  39.6 5.6 %collective-permute-start.14 = (f32[8,128]{1,0:T(8,128)S(1)}, f32[8,128]{1,0:T(8,128)S(1)}, u32[]{:S(2)}, u32[]{:S(2)}) collective-permute-start(f32[8,128]{1,0:T(8,128)S(1)} %get-tuple-element.45), channel_id=1, source_target_pairs={{0,1},{1,0},{2,3},{3,2},{4,5},{5,4},{6,7},{7,6},{8,9},{9,8},{10,11... | collective-permute-start | bytes 12296 | tf_op jit(solution)/shard_map/ppermute | solution.py:413
  45.0 1.5 %collective-permute-start.16 = (f32[8,128]{1,0:T(8,128)S(1)}, f32[8,128]{1,0:T(8,128)S(1)}, u32[]{:S(2)}, u32[]{:S(2)}) collective-permute-start(f32[8,128]{1,0:T(8,128)S(1)} %get-tuple-element.53), channel_id=1, source_target_pairs={{0,1},{1,0},{2,3},{3,2},{4,5},{5,4},{6,7},{7,6},{8,9},{9,8},{10,11... | collective-permute-start | bytes 12296 | tf_op jit(solution)/shard_map/ppermute | solution.py:413
  45.1 5.0 %collective-permute-start.15 = (f32[8,128]{1,0:T(8,128)S(1)}, f32[8,128]{1,0:T(8,128)S(1)}, u32[]{:S(2)}, u32[]{:S(2)}) collective-permute-start(f32[8,128]{1,0:T(8,128)S(1)} %add.9), channel_id=1, source_target_pairs={{0,6},{1,9},{4,2},{5,13},{8,0},{9,15},{12,4},{13,11},{14,8},{15,7}... | collective-permute-start | bytes 12296 | tf_op jit(solution)/shard_map/ppermute | solution.py:420
  46.6 7.3 %collective-permute-start.17 = (f32[8,128]{1,0:T(8,128)S(1)}, f32[8,128]{1,0:T(8,128)S(1)}, u32[]{:S(2)}, u32[]{:S(2)}) collective-permute-start(f32[8,128]{1,0:T(8,128)S(1)} %add.10), channel_id=1, source_target_pairs={{0,10},{1,13},{4,6},{5,15},{8,2},{9,11},{12,0},{13,7},{14,4},{15,3... | collective-permute-start | bytes 12296 | tf_op jit(solution)/shard_map/ppermute | solution.py:420
  50.9 6.4 %collective-permute-start.18 = (f32[8,128]{1,0:T(8,128)S(1)}, f32[8,128]{1,0:T(8,128)S(1)}, u32[]{:S(2)}, u32[]{:S(2)}) collective-permute-start(f32[8,128]{1,0:T(8,128)S(1)} %last_scores.1), channel_id=1, source_target_pairs={{0,14},{4,10},{8,6},{12,2},{14,0},{10,4},{6,8},{2,12},{1,15},{5,11... | collective-permute-start | bytes 12296 | tf_op jit(solution)/shard_map/ppermute | solution.py:402
  57.3 1.8 %collective-permute-start.19 = (f32[32,128]{1,0:T(8,128)S(1)}, f32[32,128]{1,0:T(8,128)S(1)}, u32[]{:S(2)}, u32[]{:S(2)}) collective-permute-start(f32[32,128]{1,0:T(8,128)S(1)} %unpack.1), channel_id=1, source_target_pairs={{0,1},{1,0},{2,3},{3,2},{4,5},{5,4},{6,7},{7,6},{8,9},{9,8},{10,11... | collective-permute-start | bytes 49160 | tf_op jit(solution)/shard_map/ppermute | solution.py:413

commit v7 on v6

--- a/solution.py
+++ b/solution.py
@@ -444,6 +444,7 @@
     total, first_4, second = lax.optimization_barrier((total, first_4, second))
     opposite = shift(last_scores(4, first_4, decoder, tok_rows), -4)
     decoder_grad = last_gradients(4, first_4, total, tok_rows)
+    decoder_grad, opposite = lax.optimization_barrier((decoder_grad, opposite))
     act_grad = unpack(slots, own, *first_3, second, third, opposite)
     act_grad = act_grad + other_core(act_grad)
     return (decoder_grad, act_grad.T)

time: 60.1 us -> 59.5 us (0.990)
  starting transfers between devices: 23.7 us -> 21.1 us
  waiting for transfers between devices: 23.4 us -> 25.5 us
    ppermute x15, waiting for transfers between devices: 23.4 us -> 18.1 us  [shift(): return lax.ppermute(x, 'dp', pairs)]
    ppermute x2, waiting for transfers between devices: 0.01 us -> 5.09 us  [return_by(): return lax.ppermute(mine + other_core(others), ('dp', 'width'), pairs)]
    ppermute x3, waiting for transfers between devices: 0.01 us -> 2.34 us  [other_core(): return lax.ppermute(x, 'width', ((0, 1), (1, 0)))]
    ppermute x2, starting transfers between devices: 5.03 us -> 2.97 us  [return_by(): return lax.ppermute(mine + other_core(others), ('dp', 'width'), pairs)]
  transfers between devices with their start and end apart: 20 -> 20, of which waited for: 11 -> 14; matrix products, arithmetic and copies ran while one was open for 0% -> 0% of each run, Pallas kernels for 17% -> 17%
where the time goes in v7:
time: 59.5 us; the launch traced here: 59.2 us
  waiting for transfers between devices  25.5 us (43%)
  starting transfers between devices  21.1 us (35%)
  Pallas kernels  11.3 us (19%)
  between operations  0.73 us (1%)
  other arithmetic  0.62 us (1%)
    ppermute x15, waiting for transfers between devices, shift(): return lax.ppermute(x, 'dp', pairs)  18.1 us
    ppermute x15, starting transfers between devices, shift(): return lax.ppermute(x, 'dp', pairs)  18 us
    pallas_call x3, Pallas kernels, absorb(): pl.pallas_call(functools.partial(absorb_kernel, distances, later, later),...  5.87 us
    ppermute x2, waiting for transfers between devices, return_by(): return lax.ppermute(mine + other_core(others), ('dp', 'width'), pairs)  5.09 us
    ppermute x2, starting transfers between devices, return_by(): return lax.ppermute(mine + other_core(others), ('dp', 'width'), pairs)  2.97 us
    ppermute x3, waiting for transfers between devices, other_core(): return lax.ppermute(x, 'width', ((0, 1), (1, 0)))  2.34 us
    pallas_call x1, Pallas kernels, last_gradients(): pl.pallas_call(functools.partial(last_gradients_kernel, distance, tok_row...  1.73 us
    pallas_call x1, Pallas kernels, fetch(): pl.pallas_call(fetch_kernel, out_shape=pltpu.VMEM(x.shape, x.dtype), in_s...  1.6 us
  transfers between devices with their start and end apart: 20, of which 14 were waited for; matrix products, arithmetic and copies ran while one was open for 0% of the time, Pallas kernels for 17%

profile of v7, /device:TPU:0, one launch (start us, length us, event | category | flops | bytes accessed | tf_op | source)
XLA Modules:
  0.0 59.2 jit_solution(13493071211435813157)
XLA Ops:
  0.6 1.2 %prepare.1 = (bf16[1056,128]{1,0:T(8,128)(2,1)S(1)}, bf16[1056,128]{1,0:T(8,128)(2,1)S(1)}, f32[8,128]{1,0:T(8,128)S(1)}, s32[8,128]{1,0:T(8,128)S(1)}) custom-call(s32[32]{0:T(128)} %refs_0_.1, s32[8,128]{1,0:T(8,128)} %bitcast.7, s32[32,128]{1,0:T(8,128)} %bitcast.5, bf16[32,128]{1,0:T(8,128)(2,1)} %bitcast.6, bf16[128,2048]{1,0:T(8,128)(2,1)} %refs_4_.1), custom_call_target="tpu_custom_call" | custom-call | tf_op jit(solution)/shard_map/prepare/pallas_call | solution.py:116
  1.9 3.1 %collective-permute-start = (bf16[1056,128]{1,0:T(8,128)(2,1)S(1)}, bf16[1056,128]{1,0:T(8,128)(2,1)S(1)}, u32[]{:S(2)}, u32[]{:S(2)}) collective-permute-start(bf16[1056,128]{1,0:T(8,128)(2,1)S(1)} %get-tuple-element.30.refs_0_), channel_id=1, source_target_pairs={{0,4},{4,8},{8,12},{12,14},{14,10},{10,6},{6,2},{2,0},{1,5},{5,9},... | collective-permute-start | bytes 811016 | tf_op jit(solution)/shard_map/ppermute | solution.py:402
  4.9 0.0 collective-permute-start.1
  5.0 2.0 %collective-permute-start.4 = (bf16[1056,128]{1,0:T(8,128)(2,1)S(1)}, bf16[1056,128]{1,0:T(8,128)(2,1)S(1)}, u32[]{:S(2)}, u32[]{:S(2)}) collective-permute-start(bf16[1056,128]{1,0:T(8,128)(2,1)S(1)} %get-tuple-element.31.refs_1_), channel_id=1, source_target_pairs={{0,4},{4,8},{8,12},{12,14},{14,10},{10,6},{6,2},{2,0},{1,5},{5,9},... | collective-permute-start | bytes 811016 | tf_op jit(solution)/shard_map/ppermute | solution.py:402
  7.0 0.0 collective-permute-start.5
  7.0 1.6 %fetch.1.decoder = bf16[512,2048]{1,0:T(8,128)(2,1)S(1)} custom-call(bf16[512,2048]{1,0:T(8,128)(2,1)} %source.1), custom_call_target="tpu_custom_call" | custom-call | tf_op jit(solution)/shard_map/fetch/pallas_call | solution.py:147
  8.6 3.6 %collective-permute-done.refs_2_ = bf16[1056,128]{1,0:T(8,128)(2,1)S(1)} collective-permute-done((bf16[1056,128]{1,0:T(8,128)(2,1)S(1)}, bf16[1056,128]{1,0:T(8,128)(2,1)S(1)}, u32[]{:S(2)}, u32[]{:S(2)}) %collective-permute-start) | collective-permute-done | bytes 270368 | tf_op jit(solution)/shard_map/ppermute | solution.py:402
  12.2 2.2 %collective-permute-done.1.refs_5_ = bf16[1056,128]{1,0:T(8,128)(2,1)S(1)} collective-permute-done((bf16[1056,128]{1,0:T(8,128)(2,1)S(1)}, bf16[1056,128]{1,0:T(8,128)(2,1)S(1)}, u32[]{:S(2)}, u32[]{:S(2)}) %collective-permute-start.1) | collective-permute-done | bytes 270368 | tf_op jit(solution)/shard_map/ppermute | solution.py:402
  14.4 1.6 %collective-permute-start.2 = (bf16[1056,128]{1,0:T(8,128)(2,1)S(1)}, bf16[1056,128]{1,0:T(8,128)(2,1)S(1)}, u32[]{:S(2)}, u32[]{:S(2)}) collective-permute-start(bf16[1056,128]{1,0:T(8,128)(2,1)S(1)} %collective-permute-done.refs_2_), channel_id=1, source_target_pairs={{0,4},{4,8},{8,12},{12,14},{14,10},{10,6},{6,2},{2,0},{1,5},{5,9},... | collective-permute-start | bytes 811016 | tf_op jit(solution)/shard_map/ppermute | solution.py:402
  15.9 0.4 collective-permute-start.3
  16.4 1.6 %collective-permute-done.4.refs_3_ = bf16[1056,128]{1,0:T(8,128)(2,1)S(1)} collective-permute-done((bf16[1056,128]{1,0:T(8,128)(2,1)S(1)}, bf16[1056,128]{1,0:T(8,128)(2,1)S(1)}, u32[]{:S(2)}, u32[]{:S(2)}) %collective-permute-start.4) | collective-permute-done | bytes 270368 | tf_op jit(solution)/shard_map/ppermute | solution.py:402
  18.0 2.1 %collective-permute-start.6 = (bf16[1056,128]{1,0:T(8,128)(2,1)S(1)}, bf16[1056,128]{1,0:T(8,128)(2,1)S(1)}, u32[]{:S(2)}, u32[]{:S(2)}) collective-permute-start(bf16[1056,128]{1,0:T(8,128)(2,1)S(1)} %collective-permute-done.4.refs_3_), channel_id=1, source_target_pairs={{0,4},{4,8},{8,12},{12,14},{14,10},{10,6},{6,2},{2,0},{1,5},{5,9},... | collective-permute-start | bytes 811016 | tf_op jit(solution)/shard_map/ppermute | solution.py:402
  20.1 0.0 collective-permute-done.5.refs_4_
  20.1 0.0 collective-permute-start.7
  20.2 2.4 %absorb.3 = (f32[8,128]{1,0:T(8,128)S(1)}, f32[8,128]{1,0:T(8,128)S(1)}, f32[8,128]{1,0:T(8,128)S(1)}, f32[512,2048]{1,0:T(8,128)S(1)}) custom-call(bf16[512,2048]{1,0:T(8,128)(2,1)S(1)} %fetch.1.decoder, f32[8,128]{1,0:T(8,128)S(1)} %get-tuple-element.33.own_facts, bf16[1056,128]{1,0:T(8,128)(2,1)S(1)} %get-tuple-element.30.refs_0_, ...), custom_call_target="tpu_custom_call" | custom-call | tf_op jit(solution)/shard_map/absorb/pallas_call | solution.py:264
  22.6 1.2 %collective-permute-done.2.left = bf16[1056,128]{1,0:T(8,128)(2,1)S(1)} collective-permute-done((bf16[1056,128]{1,0:T(8,128)(2,1)S(1)}, bf16[1056,128]{1,0:T(8,128)(2,1)S(1)}, u32[]{:S(2)}, u32[]{:S(2)}) %collective-permute-start.2) | collective-permute-done | bytes 270368 | tf_op jit(solution)/shard_map/ppermute | solution.py:402
  23.8 2.2 %collective-permute-done.3.right = bf16[1056,128]{1,0:T(8,128)(2,1)S(1)} collective-permute-done((bf16[1056,128]{1,0:T(8,128)(2,1)S(1)}, bf16[1056,128]{1,0:T(8,128)(2,1)S(1)}, u32[]{:S(2)}, u32[]{:S(2)}) %collective-permute-start.3) | collective-permute-done | bytes 270368 | tf_op jit(solution)/shard_map/ppermute | solution.py:402
  25.9 0.1 stamp.1
  26.0 1.6 %collective-permute-start.8 = (bf16[1056,128]{1,0:T(8,128)(2,1)S(1)}, bf16[1056,128]{1,0:T(8,128)(2,1)S(1)}, u32[]{:S(2)}, u32[]{:S(2)}) collective-permute-start(bf16[1056,128]{1,0:T(8,128)(2,1)S(1)} %get-tuple-element.38.refs_0_), channel_id=1, source_target_pairs={{0,4},{4,8},{8,12},{12,14},{14,10},{10,6},{6,2},{2,0},{1,5},{5,9},... | collective-permute-start | bytes 811016 | tf_op jit(solution)/shard_map/ppermute | solution.py:402
  27.7 0.4 collective-permute-start.9
  28.1 1.5 %collective-permute-done.6.refs_1_ = bf16[1056,128]{1,0:T(8,128)(2,1)S(1)} collective-permute-done((bf16[1056,128]{1,0:T(8,128)(2,1)S(1)}, bf16[1056,128]{1,0:T(8,128)(2,1)S(1)}, u32[]{:S(2)}, u32[]{:S(2)}) %collective-permute-start.6) | collective-permute-done | bytes 270368 | tf_op jit(solution)/shard_map/ppermute | solution.py:402
  29.6 2.1 %collective-permute-start.10 = (bf16[1056,128]{1,0:T(8,128)(2,1)S(1)}, bf16[1056,128]{1,0:T(8,128)(2,1)S(1)}, u32[]{:S(2)}, u32[]{:S(2)}) collective-permute-start(bf16[1056,128]{1,0:T(8,128)(2,1)S(1)} %collective-permute-done.6.refs_1_), channel_id=1, source_target_pairs={{0,4},{4,8},{8,12},{12,14},{14,10},{10,6},{6,2},{2,0},{1,5},{5,9},... | collective-permute-start | bytes 811016 | tf_op jit(solution)/shard_map/ppermute | solution.py:402
  31.7 0.0 collective-permute-done.7.refs_2_
  31.7 0.0 collective-permute-start.11
  31.7 1.7 %absorb.4 = (f32[8,128]{1,0:T(8,128)S(1)}, f32[8,128]{1,0:T(8,128)S(1)}, f32[512,2048]{1,0:T(8,128)S(1)}) custom-call(bf16[512,2048]{1,0:T(8,128)(2,1)S(1)} %fetch.1.decoder, f32[8,128]{1,0:T(8,128)S(1)} %get-tuple-element.33.own_facts, bf16[1056,128]{1,0:T(8,128)(2,1)S(1)} %get-tuple-element.38.refs_0_, ...), custom_call_target="tpu_custom_call", output_to_operand_aliasing={{2}: (6, {})} | custom-call | tf_op jit(solution)/shard_map/absorb/pallas_call | solution.py:264
  33.5 2.0 %collective-permute-done.8.refs_0_.left = bf16[1056,128]{1,0:T(8,128)(2,1)S(1)} collective-permute-done((bf16[1056,128]{1,0:T(8,128)(2,1)S(1)}, bf16[1056,128]{1,0:T(8,128)(2,1)S(1)}, u32[]{:S(2)}, u32[]{:S(2)}) %collective-permute-start.8) | collective-permute-done | bytes 270368 | tf_op jit(solution)/shard_map/ppermute | solution.py:402
  35.5 2.0 %collective-permute-done.9.refs_3_.right = bf16[1056,128]{1,0:T(8,128)(2,1)S(1)} collective-permute-done((bf16[1056,128]{1,0:T(8,128)(2,1)S(1)}, bf16[1056,128]{1,0:T(8,128)(2,1)S(1)}, u32[]{:S(2)}, u32[]{:S(2)}) %collective-permute-start.9) | collective-permute-done | bytes 270368 | tf_op jit(solution)/shard_map/ppermute | solution.py:402
  37.5 1.6 %collective-permute-start.12 = (bf16[1056,128]{1,0:T(8,128)(2,1)S(1)}, bf16[1056,128]{1,0:T(8,128)(2,1)S(1)}, u32[]{:S(2)}, u32[]{:S(2)}) collective-permute-start(bf16[1056,128]{1,0:T(8,128)(2,1)S(1)} %collective-permute-done.8.refs_0_.left), channel_id=1, source_target_pairs={{0,4},{4,8},{8,12},{12,14},{14,10},{10,6},{6,2},{2,0},{1,5},{5,9},... | collective-permute-start | bytes 811016 | tf_op jit(solution)/shard_map/ppermute | solution.py:402
  39.1 0.4 collective-permute-start.13
  39.6 0.0 collective-permute-start.14
  39.6 1.2 %collective-permute-done.14 = f32[8,128]{1,0:T(8,128)S(1)} collective-permute-done((f32[8,128]{1,0:T(8,128)S(1)}, f32[8,128]{1,0:T(8,128)S(1)}, u32[]{:S(2)}, u32[]{:S(2)}) %collective-permute-start.14) | collective-permute-done | bytes 4128 | tf_op jit(solution)/shard_map/ppermute | solution.py:413
  40.7 1.4 %collective-permute-start.15 = (f32[8,128]{1,0:T(8,128)S(1)}, f32[8,128]{1,0:T(8,128)S(1)}, u32[]{:S(2)}, u32[]{:S(2)}) collective-permute-start(f32[8,128]{1,0:T(8,128)S(1)} %add.9), channel_id=1, source_target_pairs={{0,6},{1,9},{4,2},{5,13},{8,0},{9,15},{12,4},{13,11},{14,8},{15,7}... | collective-permute-start | bytes 12296 | tf_op jit(solution)/shard_map/ppermute | solution.py:420
  42.1 0.0 collective-permute-done.10.refs_1_
  42.1 1.2 %collective-permute-done.11.refs_2_ = bf16[1056,128]{1,0:T(8,128)(2,1)S(1)} collective-permute-done((bf16[1056,128]{1,0:T(8,128)(2,1)S(1)}, bf16[1056,128]{1,0:T(8,128)(2,1)S(1)}, u32[]{:S(2)}, u32[]{:S(2)}) %collective-permute-start.11) | collective-permute-done | bytes 270368 | tf_op jit(solution)/shard_map/ppermute | solution.py:402
  43.3 1.7 %absorb.5 = (f32[8,128]{1,0:T(8,128)S(1)}, f32[8,128]{1,0:T(8,128)S(1)}, f32[512,2048]{1,0:T(8,128)S(1)}) custom-call(bf16[512,2048]{1,0:T(8,128)(2,1)S(1)} %fetch.1.decoder, f32[8,128]{1,0:T(8,128)S(1)} %get-tuple-element.33.own_facts, bf16[1056,128]{1,0:T(8,128)(2,1)S(1)} %collective-permute-done.8.refs_0_.left, ...), custom_call_target="tpu_custom_call", output_to_operand_aliasing={{2}: (6, {})} | custom-call | tf_op jit(solution)/shard_map/absorb/pallas_call | solution.py:264
  45.0 0.1 collective-permute-start.17
  45.1 3.6 %collective-permute-done.15.second = f32[8,128]{1,0:T(8,128)S(1)} collective-permute-done((f32[8,128]{1,0:T(8,128)S(1)}, f32[8,128]{1,0:T(8,128)S(1)}, u32[]{:S(2)}, u32[]{:S(2)}) %collective-permute-start.15) | collective-permute-done | bytes 4128 | tf_op jit(solution)/shard_map/ppermute | solution.py:420
  48.7 0.0 collective-permute-done.12.left
  48.7 0.0 collective-permute-done.13.right
  48.7 0.7 %last_scores.1 = f32[8,128]{1,0:T(8,128)S(1)} custom-call(bf16[512,2048]{1,0:T(8,128)(2,1)S(1)} %fetch.1.decoder, bf16[1056,128]{1,0:T(8,128)(2,1)S(1)} %collective-permute-done.12.left, bf16[1056,128]{1,0:T(8,128)(2,1)S(1)} %collective-permute-done.13.right), custom_call_target="tpu_custom_call" | custom-call | tf_op jit(solution)/shard_map/last_scores/pallas_call | solution.py:285
  49.4 2.5 %collective-permute-start.16 = (f32[8,128]{1,0:T(8,128)S(1)}, f32[8,128]{1,0:T(8,128)S(1)}, u32[]{:S(2)}, u32[]{:S(2)}) collective-permute-start(f32[8,128]{1,0:T(8,128)S(1)} %last_scores.1), channel_id=1, source_target_pairs={{0,14},{4,10},{8,6},{12,2},{14,0},{10,4},{6,8},{2,12},{1,15},{5,11... | collective-permute-start | bytes 12296 | tf_op jit(solution)/shard_map/ppermute | solution.py:402
  51.9 0.0 collective-permute-done.17
  51.9 1.6 %collective-permute-start.18 = (f32[8,128]{1,0:T(8,128)S(1)}, f32[8,128]{1,0:T(8,128)S(1)}, u32[]{:S(2)}, u32[]{:S(2)}) collective-permute-start(f32[8,128]{1,0:T(8,128)S(1)} %add.10), channel_id=1, source_target_pairs={{0,10},{1,13},{4,6},{5,15},{8,2},{9,11},{12,0},{13,7},{14,4},{15,3... | collective-permute-start | bytes 12296 | tf_op jit(solution)/shard_map/ppermute | solution.py:420
  53.5 1.7 %last_gradients.1 = bf16[512,2048]{1,0:T(8,128)(2,1)} custom-call(bf16[1056,128]{1,0:T(8,128)(2,1)S(1)} %collective-permute-done.12.left, bf16[1056,128]{1,0:T(8,128)(2,1)S(1)} %collective-permute-done.13.right, f32[512,2048]{1,0:T(8,128)S(1)} %get-tuple-element.50.total), custom_call_target="tpu_custom_call" | custom-call | tf_op jit(solution)/shard_map/last_gradients/pallas_call | solution.py:311
  55.2 0.6 collective-permute-done.16.opposite
  55.8 1.5 %collective-permute-done.18.third = f32[8,128]{1,0:T(8,128)S(1)} collective-permute-done((f32[8,128]{1,0:T(8,128)S(1)}, f32[8,128]{1,0:T(8,128)S(1)}, u32[]{:S(2)}, u32[]{:S(2)}) %collective-permute-start.18) | collective-permute-done | bytes 4128 | tf_op jit(solution)/shard_map/ppermute | solution.py:420
  57.4 0.1 collective-permute-start.19
  57.4 1.2 %collective-permute-done.19 = f32[32,128]{1,0:T(8,128)S(1)} collective-permute-done((f32[32,128]{1,0:T(8,128)S(1)}, f32[32,128]{1,0:T(8,128)S(1)}, u32[]{:S(2)}, u32[]{:S(2)}) %collective-permute-start.19) | collective-permute-done | bytes 16416 | tf_op jit(solution)/shard_map/ppermute | solution.py:413
  58.6 0.6 %add_bitcast_fusion = f32[128,32]{0,1:T(8,128)} fusion(f32[32,128]{1,0:T(8,128)S(1)} %unpack.1, f32[32,128]{1,0:T(8,128)S(1)} %collective-permute-done.19), kind=kLoop, calls=%fused_computation | loop fusion | flops 4096 | bytes 49152 | tf_op jit(solution)/shard_map/transpose | solution.py:450
  (3 shorter events, 0.0 us)
Async XLA Ops:
  1.9 10.3 %collective-permute-start = (bf16[1056,128]{1,0:T(8,128)(2,1)S(1)}, bf16[1056,128]{1,0:T(8,128)(2,1)S(1)}, u32[]{:S(2)}, u32[]{:S(2)}) collective-permute-start(bf16[1056,128]{1,0:T(8,128)(2,1)S(1)} %get-tuple-element.30.refs_0_), channel_id=1, source_target_pairs={{0,4},{4,8},{8,12},{12,14},{14,10},{10,6},{6,2},{2,0},{1,5},{5,9},... | collective-permute-start | bytes 811016 | tf_op jit(solution)/shard_map/ppermute | solution.py:402
  4.9 9.4 %collective-permute-start.1 = (bf16[1056,128]{1,0:T(8,128)(2,1)S(1)}, bf16[1056,128]{1,0:T(8,128)(2,1)S(1)}, u32[]{:S(2)}, u32[]{:S(2)}) collective-permute-start(bf16[1056,128]{1,0:T(8,128)(2,1)S(1)} %get-tuple-element.31.refs_1_), channel_id=1, source_target_pairs={{0,2},{4,0},{8,4},{12,8},{14,12},{10,14},{6,10},{2,6},{1,3},{5,1},... | collective-permute-start | bytes 811016 | tf_op jit(solution)/shard_map/ppermute | solution.py:402
  5.0 13.0 %collective-permute-start.4 = (bf16[1056,128]{1,0:T(8,128)(2,1)S(1)}, bf16[1056,128]{1,0:T(8,128)(2,1)S(1)}, u32[]{:S(2)}, u32[]{:S(2)}) collective-permute-start(bf16[1056,128]{1,0:T(8,128)(2,1)S(1)} %get-tuple-element.31.refs_1_), channel_id=1, source_target_pairs={{0,4},{4,8},{8,12},{12,14},{14,10},{10,6},{6,2},{2,0},{1,5},{5,9},... | collective-permute-start | bytes 811016 | tf_op jit(solution)/shard_map/ppermute | solution.py:402
  7.0 13.2 %collective-permute-start.5 = (bf16[1056,128]{1,0:T(8,128)(2,1)S(1)}, bf16[1056,128]{1,0:T(8,128)(2,1)S(1)}, u32[]{:S(2)}, u32[]{:S(2)}) collective-permute-start(bf16[1056,128]{1,0:T(8,128)(2,1)S(1)} %get-tuple-element.30.refs_0_), channel_id=1, source_target_pairs={{0,2},{4,0},{8,4},{12,8},{14,12},{10,14},{6,10},{2,6},{1,3},{5,1},... | collective-permute-start | bytes 811016 | tf_op jit(solution)/shard_map/ppermute | solution.py:402
  14.4 9.4 %collective-permute-start.2 = (bf16[1056,128]{1,0:T(8,128)(2,1)S(1)}, bf16[1056,128]{1,0:T(8,128)(2,1)S(1)}, u32[]{:S(2)}, u32[]{:S(2)}) collective-permute-start(bf16[1056,128]{1,0:T(8,128)(2,1)S(1)} %collective-permute-done.refs_2_), channel_id=1, source_target_pairs={{0,4},{4,8},{8,12},{12,14},{14,10},{10,6},{6,2},{2,0},{1,5},{5,9},... | collective-permute-start | bytes 811016 | tf_op jit(solution)/shard_map/ppermute | solution.py:402
  15.9 10.0 %collective-permute-start.3 = (bf16[1056,128]{1,0:T(8,128)(2,1)S(1)}, bf16[1056,128]{1,0:T(8,128)(2,1)S(1)}, u32[]{:S(2)}, u32[]{:S(2)}) collective-permute-start(bf16[1056,128]{1,0:T(8,128)(2,1)S(1)} %collective-permute-done.1.refs_5_), channel_id=1, source_target_pairs={{0,2},{4,0},{8,4},{12,8},{14,12},{10,14},{6,10},{2,6},{1,3},{5,1},... | collective-permute-start | bytes 811016 | tf_op jit(solution)/shard_map/ppermute | solution.py:402
  18.0 11.6 %collective-permute-start.6 = (bf16[1056,128]{1,0:T(8,128)(2,1)S(1)}, bf16[1056,128]{1,0:T(8,128)(2,1)S(1)}, u32[]{:S(2)}, u32[]{:S(2)}) collective-permute-start(bf16[1056,128]{1,0:T(8,128)(2,1)S(1)} %collective-permute-done.4.refs_3_), channel_id=1, source_target_pairs={{0,4},{4,8},{8,12},{12,14},{14,10},{10,6},{6,2},{2,0},{1,5},{5,9},... | collective-permute-start | bytes 811016 | tf_op jit(solution)/shard_map/ppermute | solution.py:402
  20.1 11.6 %collective-permute-start.7 = (bf16[1056,128]{1,0:T(8,128)(2,1)S(1)}, bf16[1056,128]{1,0:T(8,128)(2,1)S(1)}, u32[]{:S(2)}, u32[]{:S(2)}) collective-permute-start(bf16[1056,128]{1,0:T(8,128)(2,1)S(1)} %collective-permute-done.5.refs_4_), channel_id=1, source_target_pairs={{0,2},{4,0},{8,4},{12,8},{14,12},{10,14},{6,10},{2,6},{1,3},{5,1},... | collective-permute-start | bytes 811016 | tf_op jit(solution)/shard_map/ppermute | solution.py:402
  26.0 9.5 %collective-permute-start.8 = (bf16[1056,128]{1,0:T(8,128)(2,1)S(1)}, bf16[1056,128]{1,0:T(8,128)(2,1)S(1)}, u32[]{:S(2)}, u32[]{:S(2)}) collective-permute-start(bf16[1056,128]{1,0:T(8,128)(2,1)S(1)} %get-tuple-element.38.refs_0_), channel_id=1, source_target_pairs={{0,4},{4,8},{8,12},{12,14},{14,10},{10,6},{6,2},{2,0},{1,5},{5,9},... | collective-permute-start | bytes 811016 | tf_op jit(solution)/shard_map/ppermute | solution.py:402
  27.7 9.9 %collective-permute-start.9 = (bf16[1056,128]{1,0:T(8,128)(2,1)S(1)}, bf16[1056,128]{1,0:T(8,128)(2,1)S(1)}, u32[]{:S(2)}, u32[]{:S(2)}) collective-permute-start(bf16[1056,128]{1,0:T(8,128)(2,1)S(1)} %get-tuple-element.39.refs_3_), channel_id=1, source_target_pairs={{0,2},{4,0},{8,4},{12,8},{14,12},{10,14},{6,10},{2,6},{1,3},{5,1},... | collective-permute-start | bytes 811016 | tf_op jit(solution)/shard_map/ppermute | solution.py:402
  29.6 12.6 %collective-permute-start.10 = (bf16[1056,128]{1,0:T(8,128)(2,1)S(1)}, bf16[1056,128]{1,0:T(8,128)(2,1)S(1)}, u32[]{:S(2)}, u32[]{:S(2)}) collective-permute-start(bf16[1056,128]{1,0:T(8,128)(2,1)S(1)} %collective-permute-done.6.refs_1_), channel_id=1, source_target_pairs={{0,4},{4,8},{8,12},{12,14},{14,10},{10,6},{6,2},{2,0},{1,5},{5,9},... | collective-permute-start | bytes 811016 | tf_op jit(solution)/shard_map/ppermute | solution.py:402
  31.7 11.6 %collective-permute-start.11 = (bf16[1056,128]{1,0:T(8,128)(2,1)S(1)}, bf16[1056,128]{1,0:T(8,128)(2,1)S(1)}, u32[]{:S(2)}, u32[]{:S(2)}) collective-permute-start(bf16[1056,128]{1,0:T(8,128)(2,1)S(1)} %collective-permute-done.7.refs_2_), channel_id=1, source_target_pairs={{0,2},{4,0},{8,4},{12,8},{14,12},{10,14},{6,10},{2,6},{1,3},{5,1},... | collective-permute-start | bytes 811016 | tf_op jit(solution)/shard_map/ppermute | solution.py:402
  37.5 11.2 %collective-permute-start.12 = (bf16[1056,128]{1,0:T(8,128)(2,1)S(1)}, bf16[1056,128]{1,0:T(8,128)(2,1)S(1)}, u32[]{:S(2)}, u32[]{:S(2)}) collective-permute-start(bf16[1056,128]{1,0:T(8,128)(2,1)S(1)} %collective-permute-done.8.refs_0_.left), channel_id=1, source_target_pairs={{0,4},{4,8},{8,12},{12,14},{14,10},{10,6},{6,2},{2,0},{1,5},{5,9},... | collective-permute-start | bytes 811016 | tf_op jit(solution)/shard_map/ppermute | solution.py:402
  39.1 9.6 %collective-permute-start.13 = (bf16[1056,128]{1,0:T(8,128)(2,1)S(1)}, bf16[1056,128]{1,0:T(8,128)(2,1)S(1)}, u32[]{:S(2)}, u32[]{:S(2)}) collective-permute-start(bf16[1056,128]{1,0:T(8,128)(2,1)S(1)} %collective-permute-done.9.refs_3_.right), channel_id=1, source_target_pairs={{0,2},{4,0},{8,4},{12,8},{14,12},{10,14},{6,10},{2,6},{1,3},{5,1},... | collective-permute-start | bytes 811016 | tf_op jit(solution)/shard_map/ppermute | solution.py:402
  39.6 1.2 %collective-permute-start.14 = (f32[8,128]{1,0:T(8,128)S(1)}, f32[8,128]{1,0:T(8,128)S(1)}, u32[]{:S(2)}, u32[]{:S(2)}) collective-permute-start(f32[8,128]{1,0:T(8,128)S(1)} %get-tuple-element.47), channel_id=1, source_target_pairs={{0,1},{1,0},{2,3},{3,2},{4,5},{5,4},{6,7},{7,6},{8,9},{9,8},{10,11... | collective-permute-start | bytes 12296 | tf_op jit(solution)/shard_map/ppermute | solution.py:413
  40.7 8.0 %collective-permute-start.15 = (f32[8,128]{1,0:T(8,128)S(1)}, f32[8,128]{1,0:T(8,128)S(1)}, u32[]{:S(2)}, u32[]{:S(2)}) collective-permute-start(f32[8,128]{1,0:T(8,128)S(1)} %add.9), channel_id=1, source_target_pairs={{0,6},{1,9},{4,2},{5,13},{8,0},{9,15},{12,4},{13,11},{14,8},{15,7}... | collective-permute-start | bytes 12296 | tf_op jit(solution)/shard_map/ppermute | solution.py:420
  45.0 6.9 %collective-permute-start.17 = (f32[8,128]{1,0:T(8,128)S(1)}, f32[8,128]{1,0:T(8,128)S(1)}, u32[]{:S(2)}, u32[]{:S(2)}) collective-permute-start(f32[8,128]{1,0:T(8,128)S(1)} %get-tuple-element.56), channel_id=1, source_target_pairs={{0,1},{1,0},{2,3},{3,2},{4,5},{5,4},{6,7},{7,6},{8,9},{9,8},{10,11... | collective-permute-start | bytes 12296 | tf_op jit(solution)/shard_map/ppermute | solution.py:413
  49.4 6.4 %collective-permute-start.16 = (f32[8,128]{1,0:T(8,128)S(1)}, f32[8,128]{1,0:T(8,128)S(1)}, u32[]{:S(2)}, u32[]{:S(2)}) collective-permute-start(f32[8,128]{1,0:T(8,128)S(1)} %last_scores.1), channel_id=1, source_target_pairs={{0,14},{4,10},{8,6},{12,2},{14,0},{10,4},{6,8},{2,12},{1,15},{5,11... | collective-permute-start | bytes 12296 | tf_op jit(solution)/shard_map/ppermute | solution.py:402
  51.9 5.4 %collective-permute-start.18 = (f32[8,128]{1,0:T(8,128)S(1)}, f32[8,128]{1,0:T(8,128)S(1)}, u32[]{:S(2)}, u32[]{:S(2)}) collective-permute-start(f32[8,128]{1,0:T(8,128)S(1)} %add.10), channel_id=1, source_target_pairs={{0,10},{1,13},{4,6},{5,15},{8,2},{9,11},{12,0},{13,7},{14,4},{15,3... | collective-permute-start | bytes 12296 | tf_op jit(solution)/shard_map/ppermute | solution.py:420
  57.4 1.2 %collective-permute-start.19 = (f32[32,128]{1,0:T(8,128)S(1)}, f32[32,128]{1,0:T(8,128)S(1)}, u32[]{:S(2)}, u32[]{:S(2)}) collective-permute-start(f32[32,128]{1,0:T(8,128)S(1)} %unpack.1), channel_id=1, source_target_pairs={{0,1},{1,0},{2,3},{3,2},{4,5},{5,4},{6,7},{7,6},{8,9},{9,8},{10,11... | collective-permute-start | bytes 49160 | tf_op jit(solution)/shard_map/ppermute | solution.py:413

commit v8 on v7

--- a/solution.py
+++ b/solution.py
@@ -235,61 +235,57 @@
             yield slice(side * cut + j * 128, side * cut + (j + 2) * 128), part
 
 
-def absorb_kernel(distances, later, split, decoder, own_facts, *refs):
-    count = len(distances)
-    pieces, refs = refs[: 2 * count], refs[2 * count :]
-    picked, total = refs[-1 - count : -1], refs[-1]
+def facts_of(distances, own_facts, pieces):
     tok_rows = own_facts.shape[1]
-    facts = [
+    return [
         own_facts[...] if d == 0 else facts_in(pieces[2 * i + (d > 0)], d, tok_rows)
         for i, d in enumerate(distances)
     ]
-    picks = picks_of(facts, decoder, pieces)
+
+
+def scores_kernel(distances, split, decoder, own_facts, *refs):
+    pieces, picked = refs[: 2 * len(distances)], refs[2 * len(distances) :]
+    picks = picks_of(facts_of(distances, own_facts, pieces), decoder, pieces)
     if split:
         first = lax.axis_index("width") == 0
         picks = jnp.where(first, *picks), jnp.where(first, *picks[::-1])
     for target, values in zip(picked, picks):
         target[...] = values
-    for columns, part in gradient_blocks(facts, pieces, decoder.shape[1]):
-        total[:, columns] = refs[0][:, columns] + part if later else part
-
-
-def absorb(distances, pairs, decoder, own_facts, total=None):
-    later = total is not None
-    tok_rows = own_facts.shape[1]
-    operands = [kept(decoder), kept(own_facts)]
-    operands += [kept(piece) for pair in pairs for piece in pair]
+
+
+def scores_of(distances, pairs, decoder, own_facts, split=False):
+    pieces = [kept(piece) for pair in pairs for piece in pair]
+    shape = pltpu.VMEM(own_facts.shape, jnp.float32)
+    return pl.pallas_call(
+        functools.partial(scores_kernel, distances, split),
+        out_shape=(shape,) * len(distances),
+        in_specs=[VMEM] * (2 + len(pieces)),
+        out_specs=(VMEM,) * len(distances),
+        compiler_params=limit(12),
+        name="scores",
+    )(kept(decoder), kept(own_facts), *pieces)
+
+
+def gradients_kernel(distances, own_facts, *refs):
+    pieces, refs = refs[: 2 * len(distances)], refs[2 * len(distances) :]
+    total = refs[-1]
+    facts = facts_of(distances, own_facts, pieces)
+    for columns, part in gradient_blocks(facts, pieces, total.shape[1]):
+        total[:, columns] = part if len(refs) == 1 else refs[0][:, columns] + part
+
+
+def gradients_of(distances, pairs, own_facts, shape, total=None):
+    operands = [kept(own_facts)] + [kept(piece) for pair in pairs for piece in pair]
     operands += [] if total is None else [kept(total)]
-    count = len(distances)
-    *picked, total = pl.pallas_call(
-        functools.partial(absorb_kernel, distances, later, later),
-        out_shape=(
-            *[pltpu.VMEM((2 * KPB, tok_rows), jnp.float32)] * count,
-            pltpu.VMEM(decoder.shape, jnp.float32),
-        ),
+    return pl.pallas_call(
+        functools.partial(gradients_kernel, distances),
+        out_shape=pltpu.VMEM(shape, jnp.float32),
         in_specs=[VMEM] * len(operands),
-        out_specs=(VMEM,) * (count + 1),
-        input_output_aliases={} if total is None else {len(operands) - 1: count},
+        out_specs=VMEM,
+        input_output_aliases={} if total is None else {len(operands) - 1: 0},
         compiler_params=limit(16),
-        name="absorb",
+        name="gradients",
     )(*operands)
-    return picked, total
-
-
-def last_scores_kernel(distance, decoder, left, right, picked):
-    facts = [facts_in(left, distance, picked.shape[1])]
-    picked[...] = picks_of(facts, decoder, (left, right))[0]
-
-
-def last_scores(distance, pair, decoder, tok_rows):
-    return pl.pallas_call(
-        functools.partial(last_scores_kernel, distance),
-        out_shape=pltpu.VMEM((2 * KPB, tok_rows), jnp.float32),
-        in_specs=[VMEM] * 3,
-        out_specs=VMEM,
-        compiler_params=limit(12),
-        name="last_scores",
-    )(kept(decoder), kept(pair[0]), kept(pair[1]))
 
 
 def last_gradients_kernel(distance, tok_rows, left, right, total, out, rounded, sems):
@@ -412,12 +408,12 @@
     def other_core(x):
         return lax.ppermute(x, "width", ((0, 1), (1, 0)))
 
-    def return_by(distance, mine, others):
+    def return_by(distance, x):
         pairs = []
         for i in range(owners):
             pairs.append((2 * ring[i], 2 * ring[(i - distance) % owners]))
             pairs.append((2 * ring[i] + 1, 2 * ring[(i + distance) % owners] + 1))
-        return lax.ppermute(mine + other_core(others), ("dp", "width"), pairs)
+        return lax.ppermute(x, ("dp", "width"), pairs)
 
     left, right, own_facts, slots = prepare(
         block_slot, active_blocks, feature_idx, acts, grad_out, owners
@@ -429,20 +425,29 @@
     first_2 = hop(first_1)
     second_2 = crossed(second_1)
     pairs = [(left, right), (first_1[0], second_1[0]), (second_1[1], first_1[1])]
-    (own, onward, back), total = absorb((0, -1, 1), pairs, decoder, own_facts)
+    distances = (0, -1, 1)
+    own, onward, back = scores_of(distances, pairs, decoder, own_facts)
+    total = gradients_of(distances, pairs, own_facts, decoder.shape)
     first_2 = stamp(first_2, (back, onward))
     first_3 = hop(first_2)
     second_3 = crossed(second_2)
     pairs = [(first_2[0], second_2[0]), (second_2[1], first_2[1])]
-    (mine, others), total = absorb((-2, 2), pairs, decoder, own_facts, total)
-    total, first_3 = lax.optimization_barrier((total, first_3))
-    second = return_by(2, mine, others)
+    mine, others = scores_of((-2, 2), pairs, decoder, own_facts, True)
+    total = gradients_of((-2, 2), pairs, own_facts, decoder.shape, total)
+    second = mine + other_core(others)
+    total, first_3, second = lax.optimization_barrier((total, first_3, second))
+    second = return_by(2, jnp.concatenate([second, jnp.zeros((24, 128), jnp.float32)]))[:8]
     first_4 = hop(first_3)
     pairs = [(first_3[0], second_3[0]), (second_3[1], first_3[1])]
-    (mine, others), total = absorb((-3, 3), pairs, decoder, own_facts, total)
-    third = return_by(3, mine, others)
-    total, first_4, second = lax.optimization_barrier((total, first_4, second))
-    opposite = shift(last_scores(4, first_4, decoder, tok_rows), -4)
+    mine, others = scores_of((-3, 3), pairs, decoder, own_facts, True)
+    total = gradients_of((-3, 3), pairs, own_facts, decoder.shape, total)
+    third = mine + other_core(others)
+    total, third = lax.optimization_barrier((total, third))
+    third = return_by(3, third)
+    total, first_4 = lax.optimization_barrier((total, first_4))
+    (opposite,) = scores_of((4,), [first_4], decoder, own_facts)
+    opposite = shift(opposite, -4)
+    total, third = lax.optimization_barrier((total, third))
     decoder_grad = last_gradients(4, first_4, total, tok_rows)
     decoder_grad, opposite = lax.optimization_barrier((decoder_grad, opposite))
     act_grad = unpack(slots, own, *first_3, second, third, opposite)

time: 59.5 us -> 57 us (0.958)
  waiting for transfers between devices: 25.5 us -> 20.8 us
  starting transfers between devices: 21.1 us -> 23.2 us
    ppermute x2, waiting for transfers between devices: 5.09 us -> 0.01 us  [return_by(): return lax.ppermute(x, ('dp', 'width'), pairs)]
    ppermute x15, waiting for transfers between devices: 18.1 us -> 19.4 us  [shift(): return lax.ppermute(x, 'dp', pairs)]
    ppermute x15, starting transfers between devices: 18 us -> 19.1 us  [shift(): return lax.ppermute(x, 'dp', pairs)]
    ppermute x3, waiting for transfers between devices: 2.34 us -> 1.33 us  [other_core(): return lax.ppermute(x, 'width', ((0, 1), (1, 0)))]
    ppermute x2, starting transfers between devices: 2.97 us -> 3.77 us  [return_by(): return lax.ppermute(x, ('dp', 'width'), pairs)]
    pallas_call x4 -> x7, Pallas kernels: 6.59 us -> 6.73 us  [the longest x4 3.7 us: scores_of(): pl.pallas_call(functools.partial(scores_kernel, distances, split), out_sh...]
  transfers between devices with their start and end apart: 20 -> 20, of which waited for: 14 -> 13; matrix products, arithmetic and copies ran while one was open for 0% -> 0% of each run, Pallas kernels for 17% -> 18%
where the time goes in v8:
time: 57 us; the launch traced here: 56.8 us
  starting transfers between devices  23.2 us (41%)
  waiting for transfers between devices  20.8 us (36%)
  Pallas kernels  11.4 us (20%)
  between operations  0.78 us (1%)
  other arithmetic  0.62 us (1%)
    ppermute x15, waiting for transfers between devices, shift(): return lax.ppermute(x, 'dp', pairs)  19.4 us
    ppermute x15, starting transfers between devices, shift(): return lax.ppermute(x, 'dp', pairs)  19.1 us
    ppermute x2, starting transfers between devices, return_by(): return lax.ppermute(x, ('dp', 'width'), pairs)  3.77 us
    pallas_call x4, Pallas kernels, scores_of(): pl.pallas_call(functools.partial(scores_kernel, distances, split), out_sh...  3.7 us
    pallas_call x3, Pallas kernels, gradients_of(): pl.pallas_call(functools.partial(gradients_kernel, distances), out_shape=...  3.03 us
    pallas_call x1, Pallas kernels, last_gradients(): pl.pallas_call(functools.partial(last_gradients_kernel, distance, tok_row...  1.76 us
    pallas_call x1, Pallas kernels, fetch(): pl.pallas_call(fetch_kernel, out_shape=pltpu.VMEM(x.shape, x.dtype), in_s...  1.6 us
    ppermute x3, waiting for transfers between devices, other_core(): return lax.ppermute(x, 'width', ((0, 1), (1, 0)))  1.33 us
  transfers between devices with their start and end apart: 20, of which 13 were waited for; matrix products, arithmetic and copies ran while one was open for 0% of the time, Pallas kernels for 18%

profile of v8, /device:TPU:0, one launch (start us, length us, event | category | flops | bytes accessed | tf_op | source)
XLA Modules:
  0.0 56.8 jit_solution(5759543818691295644)
XLA Ops:
  0.6 1.2 %prepare.1 = (bf16[1056,128]{1,0:T(8,128)(2,1)S(1)}, bf16[1056,128]{1,0:T(8,128)(2,1)S(1)}, f32[8,128]{1,0:T(8,128)S(1)}, s32[8,128]{1,0:T(8,128)S(1)}) custom-call(s32[32]{0:T(128)} %refs_0_.1, s32[8,128]{1,0:T(8,128)} %bitcast.7, s32[32,128]{1,0:T(8,128)} %bitcast.5, bf16[32,128]{1,0:T(8,128)(2,1)} %bitcast.6, bf16[128,2048]{1,0:T(8,128)(2,1)} %refs_4_.1), custom_call_target="tpu_custom_call" | custom-call | tf_op jit(solution)/shard_map/prepare/pallas_call | solution.py:116
  1.9 3.1 %collective-permute-start = (bf16[1056,128]{1,0:T(8,128)(2,1)S(1)}, bf16[1056,128]{1,0:T(8,128)(2,1)S(1)}, u32[]{:S(2)}, u32[]{:S(2)}) collective-permute-start(bf16[1056,128]{1,0:T(8,128)(2,1)S(1)} %get-tuple-element.32.refs_0_), channel_id=1, source_target_pairs={{0,4},{4,8},{8,12},{12,14},{14,10},{10,6},{6,2},{2,0},{1,5},{5,9},... | collective-permute-start | bytes 811016 | tf_op jit(solution)/shard_map/ppermute | solution.py:398
  4.9 0.0 collective-permute-start.1
  5.0 2.0 %collective-permute-start.4 = (bf16[1056,128]{1,0:T(8,128)(2,1)S(1)}, bf16[1056,128]{1,0:T(8,128)(2,1)S(1)}, u32[]{:S(2)}, u32[]{:S(2)}) collective-permute-start(bf16[1056,128]{1,0:T(8,128)(2,1)S(1)} %get-tuple-element.33.refs_1_), channel_id=1, source_target_pairs={{0,4},{4,8},{8,12},{12,14},{14,10},{10,6},{6,2},{2,0},{1,5},{5,9},... | collective-permute-start | bytes 811016 | tf_op jit(solution)/shard_map/ppermute | solution.py:398
  7.0 0.0 collective-permute-start.5
  7.0 1.6 %fetch.1.decoder = bf16[512,2048]{1,0:T(8,128)(2,1)S(1)} custom-call(bf16[512,2048]{1,0:T(8,128)(2,1)} %source.1), custom_call_target="tpu_custom_call" | custom-call | tf_op jit(solution)/shard_map/fetch/pallas_call | solution.py:147
  8.6 3.6 %collective-permute-done.refs_2_ = bf16[1056,128]{1,0:T(8,128)(2,1)S(1)} collective-permute-done((bf16[1056,128]{1,0:T(8,128)(2,1)S(1)}, bf16[1056,128]{1,0:T(8,128)(2,1)S(1)}, u32[]{:S(2)}, u32[]{:S(2)}) %collective-permute-start) | collective-permute-done | bytes 270368 | tf_op jit(solution)/shard_map/ppermute | solution.py:398
  12.2 2.2 %collective-permute-done.1.refs_5_ = bf16[1056,128]{1,0:T(8,128)(2,1)S(1)} collective-permute-done((bf16[1056,128]{1,0:T(8,128)(2,1)S(1)}, bf16[1056,128]{1,0:T(8,128)(2,1)S(1)}, u32[]{:S(2)}, u32[]{:S(2)}) %collective-permute-start.1) | collective-permute-done | bytes 270368 | tf_op jit(solution)/shard_map/ppermute | solution.py:398
  14.4 1.6 %collective-permute-start.2 = (bf16[1056,128]{1,0:T(8,128)(2,1)S(1)}, bf16[1056,128]{1,0:T(8,128)(2,1)S(1)}, u32[]{:S(2)}, u32[]{:S(2)}) collective-permute-start(bf16[1056,128]{1,0:T(8,128)(2,1)S(1)} %collective-permute-done.refs_2_), channel_id=1, source_target_pairs={{0,4},{4,8},{8,12},{12,14},{14,10},{10,6},{6,2},{2,0},{1,5},{5,9},... | collective-permute-start | bytes 811016 | tf_op jit(solution)/shard_map/ppermute | solution.py:398
  15.9 0.4 collective-permute-start.3
  16.4 1.6 %collective-permute-done.4.refs_3_ = bf16[1056,128]{1,0:T(8,128)(2,1)S(1)} collective-permute-done((bf16[1056,128]{1,0:T(8,128)(2,1)S(1)}, bf16[1056,128]{1,0:T(8,128)(2,1)S(1)}, u32[]{:S(2)}, u32[]{:S(2)}) %collective-permute-start.4) | collective-permute-done | bytes 270368 | tf_op jit(solution)/shard_map/ppermute | solution.py:398
  18.0 2.1 %collective-permute-start.6 = (bf16[1056,128]{1,0:T(8,128)(2,1)S(1)}, bf16[1056,128]{1,0:T(8,128)(2,1)S(1)}, u32[]{:S(2)}, u32[]{:S(2)}) collective-permute-start(bf16[1056,128]{1,0:T(8,128)(2,1)S(1)} %collective-permute-done.4.refs_3_), channel_id=1, source_target_pairs={{0,4},{4,8},{8,12},{12,14},{14,10},{10,6},{6,2},{2,0},{1,5},{5,9},... | collective-permute-start | bytes 811016 | tf_op jit(solution)/shard_map/ppermute | solution.py:398
  20.1 0.0 collective-permute-done.5.refs_4_
  20.1 0.0 collective-permute-start.7
  20.2 1.4 %scores.4 = (f32[8,128]{1,0:T(8,128)S(1)}, f32[8,128]{1,0:T(8,128)S(1)}, f32[8,128]{1,0:T(8,128)S(1)}) custom-call(bf16[512,2048]{1,0:T(8,128)(2,1)S(1)} %fetch.1.decoder, f32[8,128]{1,0:T(8,128)S(1)} %get-tuple-element.31.own_facts, bf16[1056,128]{1,0:T(8,128)(2,1)S(1)} %get-tuple-element.32.refs_0_, bf16[1056,128]{1,0:T(8,128)(2,1)S(1)} %get-tuple-element.33.refs_1_, ...), custom_call_target="tpu_custom_call" | custom-call | tf_op jit(solution)/shard_map/scores/pallas_call | solution.py:259
  21.5 2.2 %collective-permute-done.2.left = bf16[1056,128]{1,0:T(8,128)(2,1)S(1)} collective-permute-done((bf16[1056,128]{1,0:T(8,128)(2,1)S(1)}, bf16[1056,128]{1,0:T(8,128)(2,1)S(1)}, u32[]{:S(2)}, u32[]{:S(2)}) %collective-permute-start.2) | collective-permute-done | bytes 270368 | tf_op jit(solution)/shard_map/ppermute | solution.py:398
  23.8 2.2 %collective-permute-done.3.right = bf16[1056,128]{1,0:T(8,128)(2,1)S(1)} collective-permute-done((bf16[1056,128]{1,0:T(8,128)(2,1)S(1)}, bf16[1056,128]{1,0:T(8,128)(2,1)S(1)}, u32[]{:S(2)}, u32[]{:S(2)}) %collective-permute-start.3) | collective-permute-done | bytes 270368 | tf_op jit(solution)/shard_map/ppermute | solution.py:398
  25.9 0.1 stamp.1
  26.0 1.6 %collective-permute-start.8 = (bf16[1056,128]{1,0:T(8,128)(2,1)S(1)}, bf16[1056,128]{1,0:T(8,128)(2,1)S(1)}, u32[]{:S(2)}, u32[]{:S(2)}) collective-permute-start(bf16[1056,128]{1,0:T(8,128)(2,1)S(1)} %get-tuple-element.39.refs_0_), channel_id=1, source_target_pairs={{0,4},{4,8},{8,12},{12,14},{14,10},{10,6},{6,2},{2,0},{1,5},{5,9},... | collective-permute-start | bytes 811016 | tf_op jit(solution)/shard_map/ppermute | solution.py:398
  27.7 0.4 collective-permute-start.9
  28.1 1.5 %collective-permute-done.6.refs_1_ = bf16[1056,128]{1,0:T(8,128)(2,1)S(1)} collective-permute-done((bf16[1056,128]{1,0:T(8,128)(2,1)S(1)}, bf16[1056,128]{1,0:T(8,128)(2,1)S(1)}, u32[]{:S(2)}, u32[]{:S(2)}) %collective-permute-start.6) | collective-permute-done | bytes 270368 | tf_op jit(solution)/shard_map/ppermute | solution.py:398
  29.6 2.1 %collective-permute-start.11 = (bf16[1056,128]{1,0:T(8,128)(2,1)S(1)}, bf16[1056,128]{1,0:T(8,128)(2,1)S(1)}, u32[]{:S(2)}, u32[]{:S(2)}) collective-permute-start(bf16[1056,128]{1,0:T(8,128)(2,1)S(1)} %collective-permute-done.6.refs_1_), channel_id=1, source_target_pairs={{0,4},{4,8},{8,12},{12,14},{14,10},{10,6},{6,2},{2,0},{1,5},{5,9},... | collective-permute-start | bytes 811016 | tf_op jit(solution)/shard_map/ppermute | solution.py:398
  31.7 0.0 collective-permute-done.7.refs_2_
  31.7 0.8 %scores.5 = (f32[8,128]{1,0:T(8,128)S(1)}, f32[8,128]{1,0:T(8,128)S(1)}) custom-call(bf16[512,2048]{1,0:T(8,128)(2,1)S(1)} %fetch.1.decoder, f32[8,128]{1,0:T(8,128)S(1)} %get-tuple-element.31.own_facts, bf16[1056,128]{1,0:T(8,128)(2,1)S(1)} %get-tuple-element.39.refs_0_, bf16[1056,128]{1,0:T(8,128)(2,1)S(1)} %collective-permute-done.6.refs_1_, ...), custom_call_target="tpu_custom_call" | custom-call | tf_op jit(solution)/shard_map/scores/pallas_call | solution.py:259
  32.6 0.1 collective-permute-start.12
  32.6 0.1 collective-permute-start.10
  32.7 1.3 %gradients.3.refs_4_ = f32[512,2048]{1,0:T(8,128)S(1)} custom-call(f32[8,128]{1,0:T(8,128)S(1)} %get-tuple-element.31.own_facts, bf16[1056,128]{1,0:T(8,128)(2,1)S(1)} %get-tuple-element.32.refs_0_, bf16[1056,128]{1,0:T(8,128)(2,1)S(1)} %get-tuple-element.33.refs_1_, bf16[1056,128]{1,0:T(8,128)(2,1)S(1)} %collective-permute-done.refs_2_, ...), custom_call_target="tpu_custom_call" | custom-call | tf_op jit(solution)/shard_map/gradients/pallas_call | solution.py:280
  34.0 0.9 %gradients.4.refs_4_ = f32[512,2048]{1,0:T(8,128)S(1)} custom-call(f32[8,128]{1,0:T(8,128)S(1)} %get-tuple-element.31.own_facts, bf16[1056,128]{1,0:T(8,128)(2,1)S(1)} %get-tuple-element.39.refs_0_, bf16[1056,128]{1,0:T(8,128)(2,1)S(1)} %collective-permute-done.6.refs_1_, ...), custom_call_target="tpu_custom_call", output_to_operand_aliasing={{}: (5, {})} | custom-call | tf_op jit(solution)/shard_map/gradients/pallas_call | solution.py:280
  34.9 0.0 collective-permute-done.10
  34.9 0.6 %collective-permute-done.8.refs_0_.left = bf16[1056,128]{1,0:T(8,128)(2,1)S(1)} collective-permute-done((bf16[1056,128]{1,0:T(8,128)(2,1)S(1)}, bf16[1056,128]{1,0:T(8,128)(2,1)S(1)}, u32[]{:S(2)}, u32[]{:S(2)}) %collective-permute-start.8) | collective-permute-done | bytes 270368 | tf_op jit(solution)/shard_map/ppermute | solution.py:398
  35.5 2.0 %collective-permute-done.9.refs_3_.right = bf16[1056,128]{1,0:T(8,128)(2,1)S(1)} collective-permute-done((bf16[1056,128]{1,0:T(8,128)(2,1)S(1)}, bf16[1056,128]{1,0:T(8,128)(2,1)S(1)}, u32[]{:S(2)}, u32[]{:S(2)}) %collective-permute-start.9) | collective-permute-done | bytes 270368 | tf_op jit(solution)/shard_map/ppermute | solution.py:398
  37.5 1.6 %collective-permute-start.14 = (bf16[1056,128]{1,0:T(8,128)(2,1)S(1)}, bf16[1056,128]{1,0:T(8,128)(2,1)S(1)}, u32[]{:S(2)}, u32[]{:S(2)}) collective-permute-start(bf16[1056,128]{1,0:T(8,128)(2,1)S(1)} %collective-permute-done.8.refs_0_.left), channel_id=1, source_target_pairs={{0,4},{4,8},{8,12},{12,14},{14,10},{10,6},{6,2},{2,0},{1,5},{5,9},... | collective-permute-start | bytes 811016 | tf_op jit(solution)/shard_map/ppermute | solution.py:398
  39.1 0.4 collective-permute-start.15
  39.6 1.4 %collective-permute-start.18 = (f32[32,128]{1,0:T(8,128)S(1)}, f32[32,128]{1,0:T(8,128)S(1)}, u32[]{:S(2)}, u32[]{:S(2)}) collective-permute-start(f32[32,128]{1,0:T(8,128)S(1)} %concatenate.3), channel_id=1, source_target_pairs={{0,6},{1,9},{4,2},{5,13},{8,0},{9,15},{12,4},{13,11},{14,8},{15,7}... | collective-permute-start | bytes 49160 | tf_op jit(solution)/shard_map/ppermute | solution.py:416
  40.9 0.4 collective-permute-done.11.refs_1_
  41.3 2.0 %collective-permute-done.12.refs_2_ = bf16[1056,128]{1,0:T(8,128)(2,1)S(1)} collective-permute-done((bf16[1056,128]{1,0:T(8,128)(2,1)S(1)}, bf16[1056,128]{1,0:T(8,128)(2,1)S(1)}, u32[]{:S(2)}, u32[]{:S(2)}) %collective-permute-start.12) | collective-permute-done | bytes 270368 | tf_op jit(solution)/shard_map/ppermute | solution.py:398
  43.3 0.8 %scores.6 = (f32[8,128]{1,0:T(8,128)S(1)}, f32[8,128]{1,0:T(8,128)S(1)}) custom-call(bf16[512,2048]{1,0:T(8,128)(2,1)S(1)} %fetch.1.decoder, f32[8,128]{1,0:T(8,128)S(1)} %get-tuple-element.31.own_facts, bf16[1056,128]{1,0:T(8,128)(2,1)S(1)} %collective-permute-done.8.refs_0_.left, bf16[1056,128]{1,0:T(8,128)(2,1)S(1)} %collective-permute-done.11.refs_1_, ...), custom_call_target="tpu_custom_call" | custom-call | tf_op jit(solution)/shard_map/scores/pallas_call | solution.py:259
  44.1 0.1 collective-permute-start.13
  44.2 0.9 %gradients.5.total = f32[512,2048]{1,0:T(8,128)S(1)} custom-call(f32[8,128]{1,0:T(8,128)S(1)} %get-tuple-element.31.own_facts, bf16[1056,128]{1,0:T(8,128)(2,1)S(1)} %collective-permute-done.8.refs_0_.left, bf16[1056,128]{1,0:T(8,128)(2,1)S(1)} %collective-permute-done.11.refs_1_, ...), custom_call_target="tpu_custom_call", output_to_operand_aliasing={{}: (5, {})} | custom-call | tf_op jit(solution)/shard_map/gradients/pallas_call | solution.py:280
  45.1 0.3 collective-permute-done.13
  45.4 2.4 %collective-permute-start.16 = (f32[8,128]{1,0:T(8,128)S(1)}, f32[8,128]{1,0:T(8,128)S(1)}, u32[]{:S(2)}, u32[]{:S(2)}) collective-permute-start(f32[8,128]{1,0:T(8,128)S(1)} %add.12), channel_id=1, source_target_pairs={{0,10},{1,13},{4,6},{5,15},{8,2},{9,11},{12,0},{13,7},{14,4},{15,3... | collective-permute-start | bytes 12296 | tf_op jit(solution)/shard_map/ppermute | solution.py:416
  47.8 0.0 collective-permute-done.14.left.refs_0_
  47.8 0.0 collective-permute-done.15.right.refs_1_
  47.8 0.7 %scores.7 = f32[8,128]{1,0:T(8,128)S(1)} custom-call(bf16[512,2048]{1,0:T(8,128)(2,1)S(1)} %fetch.1.decoder, f32[8,128]{1,0:T(8,128)S(1)} %get-tuple-element.31.own_facts, bf16[1056,128]{1,0:T(8,128)(2,1)S(1)} %collective-permute-done.14.left.refs_0_, bf16[1056,128]{1,0:T(8,128)(2,1)S(1)} %collective-permute-done.15.right.refs_1_), custom_call_target="tpu_custom_call" | custom-call | tf_op jit(solution)/shard_map/scores/pallas_call | solution.py:259
  48.5 3.5 %collective-permute-start.17 = (f32[8,128]{1,0:T(8,128)S(1)}, f32[8,128]{1,0:T(8,128)S(1)}, u32[]{:S(2)}, u32[]{:S(2)}) collective-permute-start(f32[8,128]{1,0:T(8,128)S(1)} %scores.7), channel_id=1, source_target_pairs={{0,14},{4,10},{8,6},{12,2},{14,0},{10,4},{6,8},{2,12},{1,15},{5,11... | collective-permute-start | bytes 12296 | tf_op jit(solution)/shard_map/ppermute | solution.py:398
  52.0 0.0 collective-permute-done.18
  52.0 0.0 collective-permute-done.16.third
  52.0 1.8 %last_gradients.1 = bf16[512,2048]{1,0:T(8,128)(2,1)} custom-call(bf16[1056,128]{1,0:T(8,128)(2,1)S(1)} %collective-permute-done.14.left.refs_0_, bf16[1056,128]{1,0:T(8,128)(2,1)S(1)} %collective-permute-done.15.right.refs_1_, f32[512,2048]{1,0:T(8,128)S(1)} %gradients.5.total), custom_call_target="tpu_custom_call" | custom-call | tf_op jit(solution)/shard_map/last_gradients/pallas_call | solution.py:307
  53.8 1.1 %collective-permute-done.17.opposite = f32[8,128]{1,0:T(8,128)S(1)} collective-permute-done((f32[8,128]{1,0:T(8,128)S(1)}, f32[8,128]{1,0:T(8,128)S(1)}, u32[]{:S(2)}, u32[]{:S(2)}) %collective-permute-start.17) | collective-permute-done | bytes 4128 | tf_op jit(solution)/shard_map/ppermute | solution.py:398
  54.9 0.2 collective-permute-start.19
  55.1 1.1 %collective-permute-done.19 = f32[32,128]{1,0:T(8,128)S(1)} collective-permute-done((f32[32,128]{1,0:T(8,128)S(1)}, f32[32,128]{1,0:T(8,128)S(1)}, u32[]{:S(2)}, u32[]{:S(2)}) %collective-permute-start.19) | collective-permute-done | bytes 16416 | tf_op jit(solution)/shard_map/ppermute | solution.py:409
  56.2 0.6 %add_bitcast_fusion = f32[128,32]{0,1:T(8,128)} fusion(f32[32,128]{1,0:T(8,128)S(1)} %unpack.1, f32[32,128]{1,0:T(8,128)S(1)} %collective-permute-done.19), kind=kLoop, calls=%fused_computation | loop fusion | flops 4096 | bytes 49152 | tf_op jit(solution)/shard_map/transpose | solution.py:455
  (5 shorter events, 0.0 us)
Async XLA Ops:
  1.9 10.3 %collective-permute-start = (bf16[1056,128]{1,0:T(8,128)(2,1)S(1)}, bf16[1056,128]{1,0:T(8,128)(2,1)S(1)}, u32[]{:S(2)}, u32[]{:S(2)}) collective-permute-start(bf16[1056,128]{1,0:T(8,128)(2,1)S(1)} %get-tuple-element.32.refs_0_), channel_id=1, source_target_pairs={{0,4},{4,8},{8,12},{12,14},{14,10},{10,6},{6,2},{2,0},{1,5},{5,9},... | collective-permute-start | bytes 811016 | tf_op jit(solution)/shard_map/ppermute | solution.py:398
  4.9 9.4 %collective-permute-start.1 = (bf16[1056,128]{1,0:T(8,128)(2,1)S(1)}, bf16[1056,128]{1,0:T(8,128)(2,1)S(1)}, u32[]{:S(2)}, u32[]{:S(2)}) collective-permute-start(bf16[1056,128]{1,0:T(8,128)(2,1)S(1)} %get-tuple-element.33.refs_1_), channel_id=1, source_target_pairs={{0,2},{4,0},{8,4},{12,8},{14,12},{10,14},{6,10},{2,6},{1,3},{5,1},... | collective-permute-start | bytes 811016 | tf_op jit(solution)/shard_map/ppermute | solution.py:398
  5.0 13.0 %collective-permute-start.4 = (bf16[1056,128]{1,0:T(8,128)(2,1)S(1)}, bf16[1056,128]{1,0:T(8,128)(2,1)S(1)}, u32[]{:S(2)}, u32[]{:S(2)}) collective-permute-start(bf16[1056,128]{1,0:T(8,128)(2,1)S(1)} %get-tuple-element.33.refs_1_), channel_id=1, source_target_pairs={{0,4},{4,8},{8,12},{12,14},{14,10},{10,6},{6,2},{2,0},{1,5},{5,9},... | collective-permute-start | bytes 811016 | tf_op jit(solution)/shard_map/ppermute | solution.py:398
  7.0 13.2 %collective-permute-start.5 = (bf16[1056,128]{1,0:T(8,128)(2,1)S(1)}, bf16[1056,128]{1,0:T(8,128)(2,1)S(1)}, u32[]{:S(2)}, u32[]{:S(2)}) collective-permute-start(bf16[1056,128]{1,0:T(8,128)(2,1)S(1)} %get-tuple-element.32.refs_0_), channel_id=1, source_target_pairs={{0,2},{4,0},{8,4},{12,8},{14,12},{10,14},{6,10},{2,6},{1,3},{5,1},... | collective-permute-start | bytes 811016 | tf_op jit(solution)/shard_map/ppermute | solution.py:398
  14.4 9.4 %collective-permute-start.2 = (bf16[1056,128]{1,0:T(8,128)(2,1)S(1)}, bf16[1056,128]{1,0:T(8,128)(2,1)S(1)}, u32[]{:S(2)}, u32[]{:S(2)}) collective-permute-start(bf16[1056,128]{1,0:T(8,128)(2,1)S(1)} %collective-permute-done.refs_2_), channel_id=1, source_target_pairs={{0,4},{4,8},{8,12},{12,14},{14,10},{10,6},{6,2},{2,0},{1,5},{5,9},... | collective-permute-start | bytes 811016 | tf_op jit(solution)/shard_map/ppermute | solution.py:398
  15.9 10.0 %collective-permute-start.3 = (bf16[1056,128]{1,0:T(8,128)(2,1)S(1)}, bf16[1056,128]{1,0:T(8,128)(2,1)S(1)}, u32[]{:S(2)}, u32[]{:S(2)}) collective-permute-start(bf16[1056,128]{1,0:T(8,128)(2,1)S(1)} %collective-permute-done.1.refs_5_), channel_id=1, source_target_pairs={{0,2},{4,0},{8,4},{12,8},{14,12},{10,14},{6,10},{2,6},{1,3},{5,1},... | collective-permute-start | bytes 811016 | tf_op jit(solution)/shard_map/ppermute | solution.py:398
  18.0 11.6 %collective-permute-start.6 = (bf16[1056,128]{1,0:T(8,128)(2,1)S(1)}, bf16[1056,128]{1,0:T(8,128)(2,1)S(1)}, u32[]{:S(2)}, u32[]{:S(2)}) collective-permute-start(bf16[1056,128]{1,0:T(8,128)(2,1)S(1)} %collective-permute-done.4.refs_3_), channel_id=1, source_target_pairs={{0,4},{4,8},{8,12},{12,14},{14,10},{10,6},{6,2},{2,0},{1,5},{5,9},... | collective-permute-start | bytes 811016 | tf_op jit(solution)/shard_map/ppermute | solution.py:398
  20.1 11.6 %collective-permute-start.7 = (bf16[1056,128]{1,0:T(8,128)(2,1)S(1)}, bf16[1056,128]{1,0:T(8,128)(2,1)S(1)}, u32[]{:S(2)}, u32[]{:S(2)}) collective-permute-start(bf16[1056,128]{1,0:T(8,128)(2,1)S(1)} %collective-permute-done.5.refs_4_), channel_id=1, source_target_pairs={{0,2},{4,0},{8,4},{12,8},{14,12},{10,14},{6,10},{2,6},{1,3},{5,1},... | collective-permute-start | bytes 811016 | tf_op jit(solution)/shard_map/ppermute | solution.py:398
  26.0 9.5 %collective-permute-start.8 = (bf16[1056,128]{1,0:T(8,128)(2,1)S(1)}, bf16[1056,128]{1,0:T(8,128)(2,1)S(1)}, u32[]{:S(2)}, u32[]{:S(2)}) collective-permute-start(bf16[1056,128]{1,0:T(8,128)(2,1)S(1)} %get-tuple-element.39.refs_0_), channel_id=1, source_target_pairs={{0,4},{4,8},{8,12},{12,14},{14,10},{10,6},{6,2},{2,0},{1,5},{5,9},... | collective-permute-start | bytes 811016 | tf_op jit(solution)/shard_map/ppermute | solution.py:398
  27.7 9.9 %collective-permute-start.9 = (bf16[1056,128]{1,0:T(8,128)(2,1)S(1)}, bf16[1056,128]{1,0:T(8,128)(2,1)S(1)}, u32[]{:S(2)}, u32[]{:S(2)}) collective-permute-start(bf16[1056,128]{1,0:T(8,128)(2,1)S(1)} %get-tuple-element.40.refs_3_), channel_id=1, source_target_pairs={{0,2},{4,0},{8,4},{12,8},{14,12},{10,14},{6,10},{2,6},{1,3},{5,1},... | collective-permute-start | bytes 811016 | tf_op jit(solution)/shard_map/ppermute | solution.py:398
  29.6 11.7 %collective-permute-start.11 = (bf16[1056,128]{1,0:T(8,128)(2,1)S(1)}, bf16[1056,128]{1,0:T(8,128)(2,1)S(1)}, u32[]{:S(2)}, u32[]{:S(2)}) collective-permute-start(bf16[1056,128]{1,0:T(8,128)(2,1)S(1)} %collective-permute-done.6.refs_1_), channel_id=1, source_target_pairs={{0,4},{4,8},{8,12},{12,14},{14,10},{10,6},{6,2},{2,0},{1,5},{5,9},... | collective-permute-start | bytes 811016 | tf_op jit(solution)/shard_map/ppermute | solution.py:398
  32.6 10.8 %collective-permute-start.12 = (bf16[1056,128]{1,0:T(8,128)(2,1)S(1)}, bf16[1056,128]{1,0:T(8,128)(2,1)S(1)}, u32[]{:S(2)}, u32[]{:S(2)}) collective-permute-start(bf16[1056,128]{1,0:T(8,128)(2,1)S(1)} %collective-permute-done.7.refs_2_), channel_id=1, source_target_pairs={{0,2},{4,0},{8,4},{12,8},{14,12},{10,14},{6,10},{2,6},{1,3},{5,1},... | collective-permute-start | bytes 811016 | tf_op jit(solution)/shard_map/ppermute | solution.py:398
  32.6 2.2 %collective-permute-start.10 = (f32[8,128]{1,0:T(8,128)S(1)}, f32[8,128]{1,0:T(8,128)S(1)}, u32[]{:S(2)}, u32[]{:S(2)}) collective-permute-start(f32[8,128]{1,0:T(8,128)S(1)} %get-tuple-element.42), channel_id=1, source_target_pairs={{0,1},{1,0},{2,3},{3,2},{4,5},{5,4},{6,7},{7,6},{8,9},{9,8},{10,11... | collective-permute-start | bytes 12296 | tf_op jit(solution)/shard_map/ppermute | solution.py:409
  37.5 10.2 %collective-permute-start.14 = (bf16[1056,128]{1,0:T(8,128)(2,1)S(1)}, bf16[1056,128]{1,0:T(8,128)(2,1)S(1)}, u32[]{:S(2)}, u32[]{:S(2)}) collective-permute-start(bf16[1056,128]{1,0:T(8,128)(2,1)S(1)} %collective-permute-done.8.refs_0_.left), channel_id=1, source_target_pairs={{0,4},{4,8},{8,12},{12,14},{14,10},{10,6},{6,2},{2,0},{1,5},{5,9},... | collective-permute-start | bytes 811016 | tf_op jit(solution)/shard_map/ppermute | solution.py:398
  39.1 8.7 %collective-permute-start.15 = (bf16[1056,128]{1,0:T(8,128)(2,1)S(1)}, bf16[1056,128]{1,0:T(8,128)(2,1)S(1)}, u32[]{:S(2)}, u32[]{:S(2)}) collective-permute-start(bf16[1056,128]{1,0:T(8,128)(2,1)S(1)} %collective-permute-done.9.refs_3_.right), channel_id=1, source_target_pairs={{0,2},{4,0},{8,4},{12,8},{14,12},{10,14},{6,10},{2,6},{1,3},{5,1},... | collective-permute-start | bytes 811016 | tf_op jit(solution)/shard_map/ppermute | solution.py:398
  39.6 12.5 %collective-permute-start.18 = (f32[32,128]{1,0:T(8,128)S(1)}, f32[32,128]{1,0:T(8,128)S(1)}, u32[]{:S(2)}, u32[]{:S(2)}) collective-permute-start(f32[32,128]{1,0:T(8,128)S(1)} %concatenate.3), channel_id=1, source_target_pairs={{0,6},{1,9},{4,2},{5,13},{8,0},{9,15},{12,4},{13,11},{14,8},{15,7}... | collective-permute-start | bytes 49160 | tf_op jit(solution)/shard_map/ppermute | solution.py:416
  44.1 1.2 %collective-permute-start.13 = (f32[8,128]{1,0:T(8,128)S(1)}, f32[8,128]{1,0:T(8,128)S(1)}, u32[]{:S(2)}, u32[]{:S(2)}) collective-permute-start(f32[8,128]{1,0:T(8,128)S(1)} %get-tuple-element.47), channel_id=1, source_target_pairs={{0,1},{1,0},{2,3},{3,2},{4,5},{5,4},{6,7},{7,6},{8,9},{9,8},{10,11... | collective-permute-start | bytes 12296 | tf_op jit(solution)/shard_map/ppermute | solution.py:409
  45.4 6.6 %collective-permute-start.16 = (f32[8,128]{1,0:T(8,128)S(1)}, f32[8,128]{1,0:T(8,128)S(1)}, u32[]{:S(2)}, u32[]{:S(2)}) collective-permute-start(f32[8,128]{1,0:T(8,128)S(1)} %add.12), channel_id=1, source_target_pairs={{0,10},{1,13},{4,6},{5,15},{8,2},{9,11},{12,0},{13,7},{14,4},{15,3... | collective-permute-start | bytes 12296 | tf_op jit(solution)/shard_map/ppermute | solution.py:416
  48.5 6.4 %collective-permute-start.17 = (f32[8,128]{1,0:T(8,128)S(1)}, f32[8,128]{1,0:T(8,128)S(1)}, u32[]{:S(2)}, u32[]{:S(2)}) collective-permute-start(f32[8,128]{1,0:T(8,128)S(1)} %scores.7), channel_id=1, source_target_pairs={{0,14},{4,10},{8,6},{12,2},{14,0},{10,4},{6,8},{2,12},{1,15},{5,11... | collective-permute-start | bytes 12296 | tf_op jit(solution)/shard_map/ppermute | solution.py:398
  54.9 1.2 %collective-permute-start.19 = (f32[32,128]{1,0:T(8,128)S(1)}, f32[32,128]{1,0:T(8,128)S(1)}, u32[]{:S(2)}, u32[]{:S(2)}) collective-permute-start(f32[32,128]{1,0:T(8,128)S(1)} %unpack.1), channel_id=1, source_target_pairs={{0,1},{1,0},{2,3},{3,2},{4,5},{5,4},{6,7},{7,6},{8,9},{9,8},{10,11... | collective-permute-start | bytes 49160 | tf_op jit(solution)/shard_map/ppermute | solution.py:409

commit v9 on v8

--- a/solution.py
+++ b/solution.py
@@ -359,8 +359,16 @@
     )(*[kept(piece) for piece in pieces], *[kept(value) for value in values])
 
 
+def place(owner, owners, returned, out):
+    mine = [owner == peer_at(distance, owners) for distance, _ in returned]
+    for k in range(KPB):
+        total = jnp.zeros(owner.shape, jnp.float32)
+        for here, (_, values) in zip(mine, returned):
+            total = jnp.where(here, values[k : k + 1, :], total)
+        out[pl.ds(k, ACT, stride=KPB), :] = total
+
+
 def unpack_kernel(owners, slots, own, left, right, second, third, opposite, out):
-    owner = slots[...] // BLK_DEV
     start = left.shape[0] - FACTS
     way = 1 - 2 * lax.axis_index("width")
     returned = [(0, own[...])]
@@ -368,12 +376,7 @@
         rows = piece[start : start + 16, :].astype(jnp.float32)
         returned.append((distance, rows[:KPB] + rows[KPB : 2 * KPB]))
     returned += [(2 * way, second[...]), (3 * way, third[...]), (4, opposite[...])]
-    mine = [owner == peer_at(distance, owners) for distance, _ in returned]
-    for k in range(KPB):
-        total = jnp.zeros(owner.shape, jnp.float32)
-        for here, (_, values) in zip(mine, returned):
-            total = jnp.where(here, values[k : k + 1, :], total)
-        out[pl.ds(k, ACT, stride=KPB), :] = total
+    place(slots[...] // BLK_DEV, owners, returned, out)
 
 
 def unpack(slots, *returned):
@@ -388,6 +391,25 @@
     )(kept(slots), *[kept(x) for x in returned])
 
 
+def finish_kernel(owners, slots, here, there, to_first, to_second, out, rest):
+    opposite = to_first[...] + to_second[...]
+    place(slots[...] // BLK_DEV, owners, [(4, opposite)], rest)
+    out[...] = here[...] + there[...] + rest[...]
+
+
+def finish(slots, *parts):
+    shape = parts[0].shape
+    return pl.pallas_call(
+        functools.partial(finish_kernel, lax.axis_size("dp")),
+        out_shape=jax.ShapeDtypeStruct(shape, jnp.float32),
+        in_specs=[VMEM] * (1 + len(parts)),
+        out_specs=VMEM,
+        scratch_shapes=[pltpu.VMEM(shape, jnp.float32)],
+        compiler_params=limit(4),
+        name="finish",
+    )(kept(slots), *[kept(x) for x in parts])
+
+
 def every_owner(decoder, grad_out, active_blocks, feature_idx, acts, block_slot):
     tok_rows = grad_out.shape[0]
     owners = lax.axis_size("dp")
@@ -413,6 +435,13 @@
         for i in range(owners):
             pairs.append((2 * ring[i], 2 * ring[(i - distance) % owners]))
             pairs.append((2 * ring[i] + 1, 2 * ring[(i + distance) % owners] + 1))
+        return lax.ppermute(x, ("dp", "width"), pairs)
+
+    def to_opposite(x, core, core_there):
+        pairs = []
+        for i in range(owners):
+            there = ring[(i + owners // 2) % owners]
+            pairs.append((2 * ring[i] + core, 2 * there + core_there))
         return lax.ppermute(x, ("dp", "width"), pairs)
 
     left, right, own_facts, slots = prepare(
@@ -446,12 +475,14 @@
     third = return_by(3, third)
     total, first_4 = lax.optimization_barrier((total, first_4))
     (opposite,) = scores_of((4,), [first_4], decoder, own_facts)
-    opposite = shift(opposite, -4)
+    from_second = to_opposite(opposite, 1, 1)
+    padded = jnp.concatenate([opposite, jnp.zeros((24, 128), jnp.float32)])
+    to_first, to_second = to_opposite(padded, 0, 0)[:8], to_opposite(padded, 0, 1)[:8]
     total, third = lax.optimization_barrier((total, third))
     decoder_grad = last_gradients(4, first_4, total, tok_rows)
-    decoder_grad, opposite = lax.optimization_barrier((decoder_grad, opposite))
-    act_grad = unpack(slots, own, *first_3, second, third, opposite)
-    act_grad = act_grad + other_core(act_grad)
+    decoder_grad, from_second = lax.optimization_barrier((decoder_grad, from_second))
+    most = unpack(slots, own, *first_3, second, third, from_second)
+    act_grad = finish(slots, most, other_core(most), to_first, to_second)
     return (decoder_grad, act_grad.T)
 
 

time: 57 us -> 62.2 us (1.091)
  starting transfers between devices: 23.2 us -> 29.2 us
  waiting for transfers between devices: 20.8 us -> 19.8 us
  Pallas kernels: 11.4 us -> 12.1 us
    ppermute x0 -> x3, starting transfers between devices: none -> 9.67 us  [to_opposite(): return lax.ppermute(x, ('dp', 'width'), pairs)]
    ppermute x15 -> x14, starting transfers between devices: 19.1 us -> 15.6 us  [shift(): return lax.ppermute(x, 'dp', pairs)]
    ppermute x15 -> x14, waiting for transfers between devices: 19.4 us -> 18.4 us  [shift(): return lax.ppermute(x, 'dp', pairs)]
    pallas_call x0 -> x1, Pallas kernels: none -> 0.62 us  [finish(): pl.pallas_call(functools.partial(finish_kernel, lax.axis_size('dp')), out...]
  transfers between devices with their start and end apart: 20 -> 22, of which waited for: 13 -> 12; matrix products, arithmetic and copies ran while one was open for 0% -> 0% of each run, Pallas kernels for 18% -> 16%
where the time goes in v9:
time: 62.2 us; the launch traced here: 61.9 us
  starting transfers between devices  29.2 us (47%)
  waiting for transfers between devices  19.8 us (32%)
  Pallas kernels  12.1 us (19%)
  between operations  0.88 us (1%)
    ppermute x14, waiting for transfers between devices, shift(): return lax.ppermute(x, 'dp', pairs)  18.4 us
    ppermute x14, starting transfers between devices, shift(): return lax.ppermute(x, 'dp', pairs)  15.6 us
    ppermute x3, starting transfers between devices, to_opposite(): return lax.ppermute(x, ('dp', 'width'), pairs)  9.67 us
    ppermute x2, starting transfers between devices, return_by(): return lax.ppermute(x, ('dp', 'width'), pairs)  3.77 us
    pallas_call x4, Pallas kernels, scores_of(): pl.pallas_call(functools.partial(scores_kernel, distances, split), out_sh...  3.7 us
    pallas_call x3, Pallas kernels, gradients_of(): pl.pallas_call(functools.partial(gradients_kernel, distances), out_shape=...  3.03 us
    pallas_call x1, Pallas kernels, last_gradients(): pl.pallas_call(functools.partial(last_gradients_kernel, distance, tok_row...  1.76 us
    pallas_call x1, Pallas kernels, fetch(): pl.pallas_call(fetch_kernel, out_shape=pltpu.VMEM(x.shape, x.dtype), in_s...  1.6 us
  transfers between devices with their start and end apart: 22, of which 12 were waited for; matrix products, arithmetic and copies ran while one was open for 0% of the time, Pallas kernels for 16%

profile of v9, /device:TPU:0, one launch (start us, length us, event | category | flops | bytes accessed | tf_op | source)
XLA Modules:
  0.0 61.9 jit_solution(3855120284875843205)
XLA Ops:
  0.6 1.2 %prepare.1 = (bf16[1056,128]{1,0:T(8,128)(2,1)S(1)}, bf16[1056,128]{1,0:T(8,128)(2,1)S(1)}, f32[8,128]{1,0:T(8,128)S(1)}, s32[8,128]{1,0:T(8,128)S(1)}) custom-call(s32[32]{0:T(128)} %refs_0_.1, s32[8,128]{1,0:T(8,128)} %bitcast.7, s32[32,128]{1,0:T(8,128)} %bitcast.4, bf16[32,128]{1,0:T(8,128)(2,1)} %bitcast.6, bf16[128,2048]{1,0:T(8,128)(2,1)} %refs_4_.1), custom_call_target="tpu_custom_call" | custom-call | tf_op jit(solution)/shard_map/prepare/pallas_call | solution.py:116
  1.9 3.1 %collective-permute-start = (bf16[1056,128]{1,0:T(8,128)(2,1)S(1)}, bf16[1056,128]{1,0:T(8,128)(2,1)S(1)}, u32[]{:S(2)}, u32[]{:S(2)}) collective-permute-start(bf16[1056,128]{1,0:T(8,128)(2,1)S(1)} %get-tuple-element.32.refs_0_), channel_id=1, source_target_pairs={{0,4},{4,8},{8,12},{12,14},{14,10},{10,6},{6,2},{2,0},{1,5},{5,9},... | collective-permute-start | bytes 811016 | tf_op jit(solution)/shard_map/ppermute | solution.py:420
  4.9 0.0 collective-permute-start.1
  5.0 2.0 %collective-permute-start.4 = (bf16[1056,128]{1,0:T(8,128)(2,1)S(1)}, bf16[1056,128]{1,0:T(8,128)(2,1)S(1)}, u32[]{:S(2)}, u32[]{:S(2)}) collective-permute-start(bf16[1056,128]{1,0:T(8,128)(2,1)S(1)} %get-tuple-element.33.refs_1_), channel_id=1, source_target_pairs={{0,4},{4,8},{8,12},{12,14},{14,10},{10,6},{6,2},{2,0},{1,5},{5,9},... | collective-permute-start | bytes 811016 | tf_op jit(solution)/shard_map/ppermute | solution.py:420
  7.0 0.0 collective-permute-start.5
  7.0 1.6 %fetch.1.decoder = bf16[512,2048]{1,0:T(8,128)(2,1)S(1)} custom-call(bf16[512,2048]{1,0:T(8,128)(2,1)} %source.1), custom_call_target="tpu_custom_call" | custom-call | tf_op jit(solution)/shard_map/fetch/pallas_call | solution.py:147
  8.6 3.6 %collective-permute-done.refs_2_ = bf16[1056,128]{1,0:T(8,128)(2,1)S(1)} collective-permute-done((bf16[1056,128]{1,0:T(8,128)(2,1)S(1)}, bf16[1056,128]{1,0:T(8,128)(2,1)S(1)}, u32[]{:S(2)}, u32[]{:S(2)}) %collective-permute-start) | collective-permute-done | bytes 270368 | tf_op jit(solution)/shard_map/ppermute | solution.py:420
  12.2 2.2 %collective-permute-done.1.refs_5_ = bf16[1056,128]{1,0:T(8,128)(2,1)S(1)} collective-permute-done((bf16[1056,128]{1,0:T(8,128)(2,1)S(1)}, bf16[1056,128]{1,0:T(8,128)(2,1)S(1)}, u32[]{:S(2)}, u32[]{:S(2)}) %collective-permute-start.1) | collective-permute-done | bytes 270368 | tf_op jit(solution)/shard_map/ppermute | solution.py:420
  14.4 1.6 %collective-permute-start.2 = (bf16[1056,128]{1,0:T(8,128)(2,1)S(1)}, bf16[1056,128]{1,0:T(8,128)(2,1)S(1)}, u32[]{:S(2)}, u32[]{:S(2)}) collective-permute-start(bf16[1056,128]{1,0:T(8,128)(2,1)S(1)} %collective-permute-done.refs_2_), channel_id=1, source_target_pairs={{0,4},{4,8},{8,12},{12,14},{14,10},{10,6},{6,2},{2,0},{1,5},{5,9},... | collective-permute-start | bytes 811016 | tf_op jit(solution)/shard_map/ppermute | solution.py:420
  15.9 0.4 collective-permute-start.3
  16.4 1.6 %collective-permute-done.4.refs_3_ = bf16[1056,128]{1,0:T(8,128)(2,1)S(1)} collective-permute-done((bf16[1056,128]{1,0:T(8,128)(2,1)S(1)}, bf16[1056,128]{1,0:T(8,128)(2,1)S(1)}, u32[]{:S(2)}, u32[]{:S(2)}) %collective-permute-start.4) | collective-permute-done | bytes 270368 | tf_op jit(solution)/shard_map/ppermute | solution.py:420
  18.0 2.1 %collective-permute-start.6 = (bf16[1056,128]{1,0:T(8,128)(2,1)S(1)}, bf16[1056,128]{1,0:T(8,128)(2,1)S(1)}, u32[]{:S(2)}, u32[]{:S(2)}) collective-permute-start(bf16[1056,128]{1,0:T(8,128)(2,1)S(1)} %collective-permute-done.4.refs_3_), channel_id=1, source_target_pairs={{0,4},{4,8},{8,12},{12,14},{14,10},{10,6},{6,2},{2,0},{1,5},{5,9},... | collective-permute-start | bytes 811016 | tf_op jit(solution)/shard_map/ppermute | solution.py:420
  20.1 0.0 collective-permute-done.5.refs_4_
  20.1 0.0 collective-permute-start.7
  20.2 1.4 %scores.4 = (f32[8,128]{1,0:T(8,128)S(1)}, f32[8,128]{1,0:T(8,128)S(1)}, f32[8,128]{1,0:T(8,128)S(1)}) custom-call(bf16[512,2048]{1,0:T(8,128)(2,1)S(1)} %fetch.1.decoder, f32[8,128]{1,0:T(8,128)S(1)} %get-tuple-element.31.own_facts, bf16[1056,128]{1,0:T(8,128)(2,1)S(1)} %get-tuple-element.32.refs_0_, bf16[1056,128]{1,0:T(8,128)(2,1)S(1)} %get-tuple-element.33.refs_1_, ...), custom_call_target="tpu_custom_call" | custom-call | tf_op jit(solution)/shard_map/scores/pallas_call | solution.py:259
  21.5 2.2 %collective-permute-done.2.left = bf16[1056,128]{1,0:T(8,128)(2,1)S(1)} collective-permute-done((bf16[1056,128]{1,0:T(8,128)(2,1)S(1)}, bf16[1056,128]{1,0:T(8,128)(2,1)S(1)}, u32[]{:S(2)}, u32[]{:S(2)}) %collective-permute-start.2) | collective-permute-done | bytes 270368 | tf_op jit(solution)/shard_map/ppermute | solution.py:420
  23.8 2.2 %collective-permute-done.3.right = bf16[1056,128]{1,0:T(8,128)(2,1)S(1)} collective-permute-done((bf16[1056,128]{1,0:T(8,128)(2,1)S(1)}, bf16[1056,128]{1,0:T(8,128)(2,1)S(1)}, u32[]{:S(2)}, u32[]{:S(2)}) %collective-permute-start.3) | collective-permute-done | bytes 270368 | tf_op jit(solution)/shard_map/ppermute | solution.py:420
  25.9 0.1 stamp.1
  26.0 1.6 %collective-permute-start.8 = (bf16[1056,128]{1,0:T(8,128)(2,1)S(1)}, bf16[1056,128]{1,0:T(8,128)(2,1)S(1)}, u32[]{:S(2)}, u32[]{:S(2)}) collective-permute-start(bf16[1056,128]{1,0:T(8,128)(2,1)S(1)} %get-tuple-element.39.refs_0_), channel_id=1, source_target_pairs={{0,4},{4,8},{8,12},{12,14},{14,10},{10,6},{6,2},{2,0},{1,5},{5,9},... | collective-permute-start | bytes 811016 | tf_op jit(solution)/shard_map/ppermute | solution.py:420
  27.7 0.4 collective-permute-start.9
  28.1 1.5 %collective-permute-done.6.refs_1_ = bf16[1056,128]{1,0:T(8,128)(2,1)S(1)} collective-permute-done((bf16[1056,128]{1,0:T(8,128)(2,1)S(1)}, bf16[1056,128]{1,0:T(8,128)(2,1)S(1)}, u32[]{:S(2)}, u32[]{:S(2)}) %collective-permute-start.6) | collective-permute-done | bytes 270368 | tf_op jit(solution)/shard_map/ppermute | solution.py:420
  29.6 2.1 %collective-permute-start.11 = (bf16[1056,128]{1,0:T(8,128)(2,1)S(1)}, bf16[1056,128]{1,0:T(8,128)(2,1)S(1)}, u32[]{:S(2)}, u32[]{:S(2)}) collective-permute-start(bf16[1056,128]{1,0:T(8,128)(2,1)S(1)} %collective-permute-done.6.refs_1_), channel_id=1, source_target_pairs={{0,4},{4,8},{8,12},{12,14},{14,10},{10,6},{6,2},{2,0},{1,5},{5,9},... | collective-permute-start | bytes 811016 | tf_op jit(solution)/shard_map/ppermute | solution.py:420
  31.7 0.0 collective-permute-done.7.refs_2_
  31.7 0.8 %scores.5 = (f32[8,128]{1,0:T(8,128)S(1)}, f32[8,128]{1,0:T(8,128)S(1)}) custom-call(bf16[512,2048]{1,0:T(8,128)(2,1)S(1)} %fetch.1.decoder, f32[8,128]{1,0:T(8,128)S(1)} %get-tuple-element.31.own_facts, bf16[1056,128]{1,0:T(8,128)(2,1)S(1)} %get-tuple-element.39.refs_0_, bf16[1056,128]{1,0:T(8,128)(2,1)S(1)} %collective-permute-done.6.refs_1_, ...), custom_call_target="tpu_custom_call" | custom-call | tf_op jit(solution)/shard_map/scores/pallas_call | solution.py:259
  32.6 0.1 collective-permute-start.12
  32.6 0.1 collective-permute-start.10
  32.7 1.3 %gradients.3.refs_4_ = f32[512,2048]{1,0:T(8,128)S(1)} custom-call(f32[8,128]{1,0:T(8,128)S(1)} %get-tuple-element.31.own_facts, bf16[1056,128]{1,0:T(8,128)(2,1)S(1)} %get-tuple-element.32.refs_0_, bf16[1056,128]{1,0:T(8,128)(2,1)S(1)} %get-tuple-element.33.refs_1_, bf16[1056,128]{1,0:T(8,128)(2,1)S(1)} %collective-permute-done.refs_2_, ...), custom_call_target="tpu_custom_call" | custom-call | tf_op jit(solution)/shard_map/gradients/pallas_call | solution.py:280
  34.0 0.9 %gradients.4.refs_4_ = f32[512,2048]{1,0:T(8,128)S(1)} custom-call(f32[8,128]{1,0:T(8,128)S(1)} %get-tuple-element.31.own_facts, bf16[1056,128]{1,0:T(8,128)(2,1)S(1)} %get-tuple-element.39.refs_0_, bf16[1056,128]{1,0:T(8,128)(2,1)S(1)} %collective-permute-done.6.refs_1_, ...), custom_call_target="tpu_custom_call", output_to_operand_aliasing={{}: (5, {})} | custom-call | tf_op jit(solution)/shard_map/gradients/pallas_call | solution.py:280
  34.9 0.0 collective-permute-done.10
  34.9 0.6 collective-permute-done.8.refs_0_.left
  35.5 2.0 %collective-permute-done.9.refs_3_.right = bf16[1056,128]{1,0:T(8,128)(2,1)S(1)} collective-permute-done((bf16[1056,128]{1,0:T(8,128)(2,1)S(1)}, bf16[1056,128]{1,0:T(8,128)(2,1)S(1)}, u32[]{:S(2)}, u32[]{:S(2)}) %collective-permute-start.9) | collective-permute-done | bytes 270368 | tf_op jit(solution)/shard_map/ppermute | solution.py:420
  37.5 1.6 %collective-permute-start.14 = (bf16[1056,128]{1,0:T(8,128)(2,1)S(1)}, bf16[1056,128]{1,0:T(8,128)(2,1)S(1)}, u32[]{:S(2)}, u32[]{:S(2)}) collective-permute-start(bf16[1056,128]{1,0:T(8,128)(2,1)S(1)} %collective-permute-done.8.refs_0_.left), channel_id=1, source_target_pairs={{0,4},{4,8},{8,12},{12,14},{14,10},{10,6},{6,2},{2,0},{1,5},{5,9},... | collective-permute-start | bytes 811016 | tf_op jit(solution)/shard_map/ppermute | solution.py:420
  39.1 0.4 collective-permute-start.15
  39.6 1.4 %collective-permute-start.18 = (f32[32,128]{1,0:T(8,128)S(1)}, f32[32,128]{1,0:T(8,128)S(1)}, u32[]{:S(2)}, u32[]{:S(2)}) collective-permute-start(f32[32,128]{1,0:T(8,128)S(1)} %concatenate.6), channel_id=1, source_target_pairs={{0,6},{1,9},{4,2},{5,13},{8,0},{9,15},{12,4},{13,11},{14,8},{15,7}... | collective-permute-start | bytes 49160 | tf_op jit(solution)/shard_map/ppermute | solution.py:438
  40.9 0.4 collective-permute-done.11.refs_1_
  41.3 2.0 %collective-permute-done.12.refs_2_ = bf16[1056,128]{1,0:T(8,128)(2,1)S(1)} collective-permute-done((bf16[1056,128]{1,0:T(8,128)(2,1)S(1)}, bf16[1056,128]{1,0:T(8,128)(2,1)S(1)}, u32[]{:S(2)}, u32[]{:S(2)}) %collective-permute-start.12) | collective-permute-done | bytes 270368 | tf_op jit(solution)/shard_map/ppermute | solution.py:420
  43.3 0.8 %scores.6 = (f32[8,128]{1,0:T(8,128)S(1)}, f32[8,128]{1,0:T(8,128)S(1)}) custom-call(bf16[512,2048]{1,0:T(8,128)(2,1)S(1)} %fetch.1.decoder, f32[8,128]{1,0:T(8,128)S(1)} %get-tuple-element.31.own_facts, bf16[1056,128]{1,0:T(8,128)(2,1)S(1)} %collective-permute-done.8.refs_0_.left, bf16[1056,128]{1,0:T(8,128)(2,1)S(1)} %collective-permute-done.11.refs_1_, ...), custom_call_target="tpu_custom_call" | custom-call | tf_op jit(solution)/shard_map/scores/pallas_call | solution.py:259
  44.1 0.1 collective-permute-start.13
  44.2 0.9 %gradients.5.total = f32[512,2048]{1,0:T(8,128)S(1)} custom-call(f32[8,128]{1,0:T(8,128)S(1)} %get-tuple-element.31.own_facts, bf16[1056,128]{1,0:T(8,128)(2,1)S(1)} %collective-permute-done.8.refs_0_.left, bf16[1056,128]{1,0:T(8,128)(2,1)S(1)} %collective-permute-done.11.refs_1_, ...), custom_call_target="tpu_custom_call", output_to_operand_aliasing={{}: (5, {})} | custom-call | tf_op jit(solution)/shard_map/gradients/pallas_call | solution.py:280
  45.1 0.3 collective-permute-done.13
  45.4 2.4 %collective-permute-start.16 = (f32[8,128]{1,0:T(8,128)S(1)}, f32[8,128]{1,0:T(8,128)S(1)}, u32[]{:S(2)}, u32[]{:S(2)}) collective-permute-start(f32[8,128]{1,0:T(8,128)S(1)} %add.11), channel_id=1, source_target_pairs={{0,10},{1,13},{4,6},{5,15},{8,2},{9,11},{12,0},{13,7},{14,4},{15,3... | collective-permute-start | bytes 12296 | tf_op jit(solution)/shard_map/ppermute | solution.py:438
  47.8 0.0 collective-permute-done.14.left.refs_0_
  47.8 0.0 collective-permute-done.15.right.refs_1_
  47.8 0.7 %scores.7 = f32[8,128]{1,0:T(8,128)S(1)} custom-call(bf16[512,2048]{1,0:T(8,128)(2,1)S(1)} %fetch.1.decoder, f32[8,128]{1,0:T(8,128)S(1)} %get-tuple-element.31.own_facts, bf16[1056,128]{1,0:T(8,128)(2,1)S(1)} %collective-permute-done.14.left.refs_0_, bf16[1056,128]{1,0:T(8,128)(2,1)S(1)} %collective-permute-done.15.right.refs_1_), custom_call_target="tpu_custom_call" | custom-call | tf_op jit(solution)/shard_map/scores/pallas_call | solution.py:259
  48.5 0.7 %collective-permute-start.17 = (f32[8,128]{1,0:T(8,128)S(1)}, f32[8,128]{1,0:T(8,128)S(1)}, u32[]{:S(2)}, u32[]{:S(2)}) collective-permute-start(f32[8,128]{1,0:T(8,128)S(1)} %scores.7), channel_id=1, source_target_pairs={{1,15},{5,11},{9,7},{13,3},{15,1},{11,5},{7,9},{3,13},{17,31},{21,... | collective-permute-start | bytes 12296 | tf_op jit(solution)/shard_map/ppermute | solution.py:445
  49.2 0.0 collective-permute-done.18
  49.2 5.3 %collective-permute-start.20 = (f32[32,128]{1,0:T(8,128)S(1)}, f32[32,128]{1,0:T(8,128)S(1)}, u32[]{:S(2)}, u32[]{:S(2)}) collective-permute-start(f32[32,128]{1,0:T(8,128)S(1)} %concatenate.7), channel_id=1, source_target_pairs={{0,14},{4,10},{8,6},{12,2},{14,0},{10,4},{6,8},{2,12},{16,30},{20,... | collective-permute-start | bytes 49160 | tf_op jit(solution)/shard_map/ppermute | solution.py:445
  54.6 3.7 %collective-permute-start.21 = (f32[32,128]{1,0:T(8,128)S(1)}, f32[32,128]{1,0:T(8,128)S(1)}, u32[]{:S(2)}, u32[]{:S(2)}) collective-permute-start(f32[32,128]{1,0:T(8,128)S(1)} %concatenate.7), channel_id=1, source_target_pairs={{0,15},{4,11},{8,7},{12,3},{14,1},{10,5},{6,9},{2,13},{16,31},{20,... | collective-permute-start | bytes 49160 | tf_op jit(solution)/shard_map/ppermute | solution.py:445
  58.2 0.0 collective-permute-done.16.third
  58.2 1.8 %last_gradients.1 = bf16[512,2048]{1,0:T(8,128)(2,1)} custom-call(bf16[1056,128]{1,0:T(8,128)(2,1)S(1)} %collective-permute-done.14.left.refs_0_, bf16[1056,128]{1,0:T(8,128)(2,1)S(1)} %collective-permute-done.15.right.refs_1_, f32[512,2048]{1,0:T(8,128)S(1)} %gradients.5.total), custom_call_target="tpu_custom_call" | custom-call | tf_op jit(solution)/shard_map/last_gradients/pallas_call | solution.py:307
  60.0 0.0 collective-permute-done.17.opposite
  60.1 0.1 collective-permute-start.19
  60.1 0.0 collective-permute-done.20
  60.2 0.0 collective-permute-done.21
  60.2 1.1 %collective-permute-done.19.there = f32[32,128]{1,0:T(8,128)S(1)} collective-permute-done((f32[32,128]{1,0:T(8,128)S(1)}, f32[32,128]{1,0:T(8,128)S(1)}, u32[]{:S(2)}, u32[]{:S(2)}) %collective-permute-start.19) | collective-permute-done | bytes 16416 | tf_op jit(solution)/shard_map/ppermute | solution.py:431
  61.3 0.6 %finish.1 = f32[32,128]{1,0:T(8,128)} custom-call(s32[8,128]{1,0:T(8,128)S(1)} %get-tuple-element.55.slots, f32[32,128]{1,0:T(8,128)S(1)} %unpack.1.here, f32[32,128]{1,0:T(8,128)S(1)} %collective-permute-done.19.there, f32[8,128]{1,0:T(8,128)S(1)} %slice.13.to_first, f32[8,128]{1,0:T(8,128)S(1)} %slice.14.to_second), custom_call_target="tpu_custom_call" | custom-call | tf_op jit(solution)/shard_map/finish/pallas_call | solution.py:402
  (8 shorter events, 0.1 us)
Async XLA Ops:
  1.9 10.3 %collective-permute-start = (bf16[1056,128]{1,0:T(8,128)(2,1)S(1)}, bf16[1056,128]{1,0:T(8,128)(2,1)S(1)}, u32[]{:S(2)}, u32[]{:S(2)}) collective-permute-start(bf16[1056,128]{1,0:T(8,128)(2,1)S(1)} %get-tuple-element.32.refs_0_), channel_id=1, source_target_pairs={{0,4},{4,8},{8,12},{12,14},{14,10},{10,6},{6,2},{2,0},{1,5},{5,9},... | collective-permute-start | bytes 811016 | tf_op jit(solution)/shard_map/ppermute | solution.py:420
  4.9 9.4 %collective-permute-start.1 = (bf16[1056,128]{1,0:T(8,128)(2,1)S(1)}, bf16[1056,128]{1,0:T(8,128)(2,1)S(1)}, u32[]{:S(2)}, u32[]{:S(2)}) collective-permute-start(bf16[1056,128]{1,0:T(8,128)(2,1)S(1)} %get-tuple-element.33.refs_1_), channel_id=1, source_target_pairs={{0,2},{4,0},{8,4},{12,8},{14,12},{10,14},{6,10},{2,6},{1,3},{5,1},... | collective-permute-start | bytes 811016 | tf_op jit(solution)/shard_map/ppermute | solution.py:420
  5.0 13.0 %collective-permute-start.4 = (bf16[1056,128]{1,0:T(8,128)(2,1)S(1)}, bf16[1056,128]{1,0:T(8,128)(2,1)S(1)}, u32[]{:S(2)}, u32[]{:S(2)}) collective-permute-start(bf16[1056,128]{1,0:T(8,128)(2,1)S(1)} %get-tuple-element.33.refs_1_), channel_id=1, source_target_pairs={{0,4},{4,8},{8,12},{12,14},{14,10},{10,6},{6,2},{2,0},{1,5},{5,9},... | collective-permute-start | bytes 811016 | tf_op jit(solution)/shard_map/ppermute | solution.py:420
  7.0 13.2 %collective-permute-start.5 = (bf16[1056,128]{1,0:T(8,128)(2,1)S(1)}, bf16[1056,128]{1,0:T(8,128)(2,1)S(1)}, u32[]{:S(2)}, u32[]{:S(2)}) collective-permute-start(bf16[1056,128]{1,0:T(8,128)(2,1)S(1)} %get-tuple-element.32.refs_0_), channel_id=1, source_target_pairs={{0,2},{4,0},{8,4},{12,8},{14,12},{10,14},{6,10},{2,6},{1,3},{5,1},... | collective-permute-start | bytes 811016 | tf_op jit(solution)/shard_map/ppermute | solution.py:420
  14.4 9.4 %collective-permute-start.2 = (bf16[1056,128]{1,0:T(8,128)(2,1)S(1)}, bf16[1056,128]{1,0:T(8,128)(2,1)S(1)}, u32[]{:S(2)}, u32[]{:S(2)}) collective-permute-start(bf16[1056,128]{1,0:T(8,128)(2,1)S(1)} %collective-permute-done.refs_2_), channel_id=1, source_target_pairs={{0,4},{4,8},{8,12},{12,14},{14,10},{10,6},{6,2},{2,0},{1,5},{5,9},... | collective-permute-start | bytes 811016 | tf_op jit(solution)/shard_map/ppermute | solution.py:420
  15.9 10.0 %collective-permute-start.3 = (bf16[1056,128]{1,0:T(8,128)(2,1)S(1)}, bf16[1056,128]{1,0:T(8,128)(2,1)S(1)}, u32[]{:S(2)}, u32[]{:S(2)}) collective-permute-start(bf16[1056,128]{1,0:T(8,128)(2,1)S(1)} %collective-permute-done.1.refs_5_), channel_id=1, source_target_pairs={{0,2},{4,0},{8,4},{12,8},{14,12},{10,14},{6,10},{2,6},{1,3},{5,1},... | collective-permute-start | bytes 811016 | tf_op jit(solution)/shard_map/ppermute | solution.py:420
  18.0 11.6 %collective-permute-start.6 = (bf16[1056,128]{1,0:T(8,128)(2,1)S(1)}, bf16[1056,128]{1,0:T(8,128)(2,1)S(1)}, u32[]{:S(2)}, u32[]{:S(2)}) collective-permute-start(bf16[1056,128]{1,0:T(8,128)(2,1)S(1)} %collective-permute-done.4.refs_3_), channel_id=1, source_target_pairs={{0,4},{4,8},{8,12},{12,14},{14,10},{10,6},{6,2},{2,0},{1,5},{5,9},... | collective-permute-start | bytes 811016 | tf_op jit(solution)/shard_map/ppermute | solution.py:420
  20.1 11.6 %collective-permute-start.7 = (bf16[1056,128]{1,0:T(8,128)(2,1)S(1)}, bf16[1056,128]{1,0:T(8,128)(2,1)S(1)}, u32[]{:S(2)}, u32[]{:S(2)}) collective-permute-start(bf16[1056,128]{1,0:T(8,128)(2,1)S(1)} %collective-permute-done.5.refs_4_), channel_id=1, source_target_pairs={{0,2},{4,0},{8,4},{12,8},{14,12},{10,14},{6,10},{2,6},{1,3},{5,1},... | collective-permute-start | bytes 811016 | tf_op jit(solution)/shard_map/ppermute | solution.py:420
  26.0 9.5 %collective-permute-start.8 = (bf16[1056,128]{1,0:T(8,128)(2,1)S(1)}, bf16[1056,128]{1,0:T(8,128)(2,1)S(1)}, u32[]{:S(2)}, u32[]{:S(2)}) collective-permute-start(bf16[1056,128]{1,0:T(8,128)(2,1)S(1)} %get-tuple-element.39.refs_0_), channel_id=1, source_target_pairs={{0,4},{4,8},{8,12},{12,14},{14,10},{10,6},{6,2},{2,0},{1,5},{5,9},... | collective-permute-start | bytes 811016 | tf_op jit(solution)/shard_map/ppermute | solution.py:420
  27.7 9.9 %collective-permute-start.9 = (bf16[1056,128]{1,0:T(8,128)(2,1)S(1)}, bf16[1056,128]{1,0:T(8,128)(2,1)S(1)}, u32[]{:S(2)}, u32[]{:S(2)}) collective-permute-start(bf16[1056,128]{1,0:T(8,128)(2,1)S(1)} %get-tuple-element.40.refs_3_), channel_id=1, source_target_pairs={{0,2},{4,0},{8,4},{12,8},{14,12},{10,14},{6,10},{2,6},{1,3},{5,1},... | collective-permute-start | bytes 811016 | tf_op jit(solution)/shard_map/ppermute | solution.py:420
  29.6 11.7 %collective-permute-start.11 = (bf16[1056,128]{1,0:T(8,128)(2,1)S(1)}, bf16[1056,128]{1,0:T(8,128)(2,1)S(1)}, u32[]{:S(2)}, u32[]{:S(2)}) collective-permute-start(bf16[1056,128]{1,0:T(8,128)(2,1)S(1)} %collective-permute-done.6.refs_1_), channel_id=1, source_target_pairs={{0,4},{4,8},{8,12},{12,14},{14,10},{10,6},{6,2},{2,0},{1,5},{5,9},... | collective-permute-start | bytes 811016 | tf_op jit(solution)/shard_map/ppermute | solution.py:420
  32.6 10.8 %collective-permute-start.12 = (bf16[1056,128]{1,0:T(8,128)(2,1)S(1)}, bf16[1056,128]{1,0:T(8,128)(2,1)S(1)}, u32[]{:S(2)}, u32[]{:S(2)}) collective-permute-start(bf16[1056,128]{1,0:T(8,128)(2,1)S(1)} %collective-permute-done.7.refs_2_), channel_id=1, source_target_pairs={{0,2},{4,0},{8,4},{12,8},{14,12},{10,14},{6,10},{2,6},{1,3},{5,1},... | collective-permute-start | bytes 811016 | tf_op jit(solution)/shard_map/ppermute | solution.py:420
  32.6 2.2 %collective-permute-start.10 = (f32[8,128]{1,0:T(8,128)S(1)}, f32[8,128]{1,0:T(8,128)S(1)}, u32[]{:S(2)}, u32[]{:S(2)}) collective-permute-start(f32[8,128]{1,0:T(8,128)S(1)} %get-tuple-element.42), channel_id=1, source_target_pairs={{0,1},{1,0},{2,3},{3,2},{4,5},{5,4},{6,7},{7,6},{8,9},{9,8},{10,11... | collective-permute-start | bytes 12296 | tf_op jit(solution)/shard_map/ppermute | solution.py:431
  37.5 10.2 %collective-permute-start.14 = (bf16[1056,128]{1,0:T(8,128)(2,1)S(1)}, bf16[1056,128]{1,0:T(8,128)(2,1)S(1)}, u32[]{:S(2)}, u32[]{:S(2)}) collective-permute-start(bf16[1056,128]{1,0:T(8,128)(2,1)S(1)} %collective-permute-done.8.refs_0_.left), channel_id=1, source_target_pairs={{0,4},{4,8},{8,12},{12,14},{14,10},{10,6},{6,2},{2,0},{1,5},{5,9},... | collective-permute-start | bytes 811016 | tf_op jit(solution)/shard_map/ppermute | solution.py:420
  39.1 8.7 %collective-permute-start.15 = (bf16[1056,128]{1,0:T(8,128)(2,1)S(1)}, bf16[1056,128]{1,0:T(8,128)(2,1)S(1)}, u32[]{:S(2)}, u32[]{:S(2)}) collective-permute-start(bf16[1056,128]{1,0:T(8,128)(2,1)S(1)} %collective-permute-done.9.refs_3_.right), channel_id=1, source_target_pairs={{0,2},{4,0},{8,4},{12,8},{14,12},{10,14},{6,10},{2,6},{1,3},{5,1},... | collective-permute-start | bytes 811016 | tf_op jit(solution)/shard_map/ppermute | solution.py:420
  39.6 9.6 %collective-permute-start.18 = (f32[32,128]{1,0:T(8,128)S(1)}, f32[32,128]{1,0:T(8,128)S(1)}, u32[]{:S(2)}, u32[]{:S(2)}) collective-permute-start(f32[32,128]{1,0:T(8,128)S(1)} %concatenate.6), channel_id=1, source_target_pairs={{0,6},{1,9},{4,2},{5,13},{8,0},{9,15},{12,4},{13,11},{14,8},{15,7}... | collective-permute-start | bytes 49160 | tf_op jit(solution)/shard_map/ppermute | solution.py:438
  44.1 1.2 %collective-permute-start.13 = (f32[8,128]{1,0:T(8,128)S(1)}, f32[8,128]{1,0:T(8,128)S(1)}, u32[]{:S(2)}, u32[]{:S(2)}) collective-permute-start(f32[8,128]{1,0:T(8,128)S(1)} %get-tuple-element.47), channel_id=1, source_target_pairs={{0,1},{1,0},{2,3},{3,2},{4,5},{5,4},{6,7},{7,6},{8,9},{9,8},{10,11... | collective-permute-start | bytes 12296 | tf_op jit(solution)/shard_map/ppermute | solution.py:431
  45.4 12.9 %collective-permute-start.16 = (f32[8,128]{1,0:T(8,128)S(1)}, f32[8,128]{1,0:T(8,128)S(1)}, u32[]{:S(2)}, u32[]{:S(2)}) collective-permute-start(f32[8,128]{1,0:T(8,128)S(1)} %add.11), channel_id=1, source_target_pairs={{0,10},{1,13},{4,6},{5,15},{8,2},{9,11},{12,0},{13,7},{14,4},{15,3... | collective-permute-start | bytes 12296 | tf_op jit(solution)/shard_map/ppermute | solution.py:438
  48.5 11.5 %collective-permute-start.17 = (f32[8,128]{1,0:T(8,128)S(1)}, f32[8,128]{1,0:T(8,128)S(1)}, u32[]{:S(2)}, u32[]{:S(2)}) collective-permute-start(f32[8,128]{1,0:T(8,128)S(1)} %scores.7), channel_id=1, source_target_pairs={{1,15},{5,11},{9,7},{13,3},{15,1},{11,5},{7,9},{3,13},{17,31},{21,... | collective-permute-start | bytes 12296 | tf_op jit(solution)/shard_map/ppermute | solution.py:445
  49.2 10.9 %collective-permute-start.20 = (f32[32,128]{1,0:T(8,128)S(1)}, f32[32,128]{1,0:T(8,128)S(1)}, u32[]{:S(2)}, u32[]{:S(2)}) collective-permute-start(f32[32,128]{1,0:T(8,128)S(1)} %concatenate.7), channel_id=1, source_target_pairs={{0,14},{4,10},{8,6},{12,2},{14,0},{10,4},{6,8},{2,12},{16,30},{20,... | collective-permute-start | bytes 49160 | tf_op jit(solution)/shard_map/ppermute | solution.py:445
  54.6 5.6 %collective-permute-start.21 = (f32[32,128]{1,0:T(8,128)S(1)}, f32[32,128]{1,0:T(8,128)S(1)}, u32[]{:S(2)}, u32[]{:S(2)}) collective-permute-start(f32[32,128]{1,0:T(8,128)S(1)} %concatenate.7), channel_id=1, source_target_pairs={{0,15},{4,11},{8,7},{12,3},{14,1},{10,5},{6,9},{2,13},{16,31},{20,... | collective-permute-start | bytes 49160 | tf_op jit(solution)/shard_map/ppermute | solution.py:445
  60.1 1.2 %collective-permute-start.19 = (f32[32,128]{1,0:T(8,128)S(1)}, f32[32,128]{1,0:T(8,128)S(1)}, u32[]{:S(2)}, u32[]{:S(2)}) collective-permute-start(f32[32,128]{1,0:T(8,128)S(1)} %unpack.1.here), channel_id=1, source_target_pairs={{0,1},{1,0},{2,3},{3,2},{4,5},{5,4},{6,7},{7,6},{8,9},{9,8},{10,11... | collective-permute-start | bytes 49160 | tf_op jit(solution)/shard_map/ppermute | solution.py:431

commit v10 on v8

--- a/solution.py
+++ b/solution.py
@@ -39,6 +39,45 @@
     place = jnp.where(lax.rem(me, 2) == 0, lax.div(me, 2), owners - 1 - lax.div(me, 2))
     at = lax.rem(place + owners + distance, owners)
     return jnp.where(at < half_ring, 2 * at, 2 * (owners - 1 - at) + 1)
+
+
+def copies_to_pieces(grad_out, left, right, sems):
+    tok_rows, width = grad_out.shape
+    parts = width // 256
+    copies = []
+    for j in range(parts):
+        for target, side in ((left, 0), (right, 1)):
+            column = (side * parts + j) * 128
+            copies.append(
+                pltpu.make_async_copy(
+                    grad_out.at[:, column : column + 128],
+                    target.at[j * tok_rows : (j + 1) * tok_rows, :],
+                    sems.at[len(copies)],
+                )
+            )
+    return copies
+
+
+def pieces_kernel(grad_out, left, right, sems):
+    copies = copies_to_pieces(grad_out, left, right, sems)
+    for copy in copies:
+        copy.start()
+    for copy in copies:
+        copy.wait()
+
+
+def pieces_of(grad_out):
+    tok_rows, width = grad_out.shape
+    shape = pltpu.VMEM((width // 256 * tok_rows, 128), grad_out.dtype)
+    return pl.pallas_call(
+        pieces_kernel,
+        out_shape=(shape, shape),
+        in_specs=[HBM],
+        out_specs=(VMEM, VMEM),
+        scratch_shapes=[pltpu.SemaphoreType.DMA((width // 128,))],
+        compiler_params=limit(8),
+        name="pieces",
+    )(far(grad_out))
 
 
 ROW_SHIFT = BLK_DEV * BW // 2
@@ -57,31 +96,17 @@
     return jnp.concatenate(rows + values, axis=0)
 
 
-def prepare_kernel(
-    owners, *refs
-):
+def prepare_kernel(owners, *refs):
     sources, refs = refs[:5], refs[5:]
     left, right, own_facts, slots = refs[:4]
     block_slot, active, feats, acts, wide_feats, wide_acts, sems = refs[4:]
-    grad_out = sources[-1]
-    tok_rows, width = grad_out.shape
-    parts = width // 256
     small = []
     for source, target in zip(sources[:4], (block_slot, active, feats, acts)):
         small.append(pltpu.make_async_copy(source, target, sems.at[len(small)]))
         small[-1].start()
-    copies = []
-    for j in range(parts):
-        for target, side in ((left, 0), (right, 1)):
-            column = (side * parts + j) * 128
-            copies.append(
-                pltpu.make_async_copy(
-                    grad_out.at[:, column : column + 128],
-                    target.at[j * tok_rows : (j + 1) * tok_rows, :],
-                    sems.at[len(small) + len(copies)],
-                )
-            )
-            copies[-1].start()
+    copies = copies_to_pieces(sources[-1], left, right, sems.at[4:])
+    for copy in copies:
+        copy.start()
     for copy in small:
         copy.wait()
     named = active[...]
@@ -100,27 +125,23 @@
             peer_at(distance, owners), slot // BLK_DEV, first_row, features, values
         )
 
-    reach = owners // 2
     own_facts[...] = facts(0)
-    start = parts * tok_rows
-    for target, sign in ((left, 1), (right, -1)):
-        ahead = [facts(sign * d) for d in range(1, reach + 1)]
-        target[start:, :] = jnp.concatenate(ahead, axis=0).astype(jnp.bfloat16)
+    for target, sign in ((left, -1), (right, 1)):
+        ahead = [facts(sign * d) for d in range(1, owners // 2 + 1)]
+        target[target.shape[0] - FACTS :, :] = jnp.concatenate(ahead, axis=0).astype(
+            jnp.bfloat16
+        )
     for copy in copies:
         copy.wait()
 
 
 def prepare(block_slot, active_blocks, feature_idx, acts, grad_out, owners):
-    tok_rows, half_width = grad_out.shape
-    plain = half_width // 256 * tok_rows
+    tok_rows, width = grad_out.shape
+    piece = pltpu.VMEM((width // 256 * tok_rows + FACTS, 128), grad_out.dtype)
+    facts = pltpu.VMEM((2 * KPB, tok_rows), jnp.float32)
     return pl.pallas_call(
         functools.partial(prepare_kernel, owners),
-        out_shape=(
-            pltpu.VMEM((plain + FACTS, 128), grad_out.dtype),
-            pltpu.VMEM((plain + FACTS, 128), grad_out.dtype),
-            pltpu.VMEM((2 * KPB, tok_rows), jnp.float32),
-            pltpu.VMEM((ACT, tok_rows), jnp.int32),
-        ),
+        out_shape=(piece, piece, facts, pltpu.VMEM((ACT, tok_rows), jnp.int32)),
         in_specs=[HBM] * 5,
         out_specs=(VMEM,) * 4,
         scratch_shapes=[
@@ -130,7 +151,7 @@
             pltpu.VMEM((ACT * KPB, tok_rows), acts.dtype),
             pltpu.VMEM((ACT * KPB, tok_rows), jnp.float32),
             pltpu.VMEM((ACT * KPB, tok_rows), jnp.float32),
-            pltpu.SemaphoreType.DMA((4 + half_width // 128,)),
+            pltpu.SemaphoreType.DMA((4 + width // 128,)),
         ],
         compiler_params=limit(8),
         name="prepare",
@@ -235,17 +256,17 @@
             yield slice(side * cut + j * 128, side * cut + (j + 2) * 128), part
 
 
-def facts_of(distances, own_facts, pieces):
-    tok_rows = own_facts.shape[1]
+def facts_of(distances, given, pieces):
+    tok_rows = given.shape[1]
     return [
-        own_facts[...] if d == 0 else facts_in(pieces[2 * i + (d > 0)], d, tok_rows)
+        given[...] if d in (0, 4) else facts_in(pieces[2 * i + (d < 0)], d, tok_rows)
         for i, d in enumerate(distances)
     ]
 
 
-def scores_kernel(distances, split, decoder, own_facts, *refs):
+def scores_kernel(distances, split, decoder, given, *refs):
     pieces, picked = refs[: 2 * len(distances)], refs[2 * len(distances) :]
-    picks = picks_of(facts_of(distances, own_facts, pieces), decoder, pieces)
+    picks = picks_of(facts_of(distances, given, pieces), decoder, pieces)
     if split:
         first = lax.axis_index("width") == 0
         picks = jnp.where(first, *picks), jnp.where(first, *picks[::-1])
@@ -253,9 +274,9 @@
         target[...] = values
 
 
-def scores_of(distances, pairs, decoder, own_facts, split=False):
+def scores_of(distances, pairs, decoder, given, split=False):
     pieces = [kept(piece) for pair in pairs for piece in pair]
-    shape = pltpu.VMEM(own_facts.shape, jnp.float32)
+    shape = pltpu.VMEM(given.shape, jnp.float32)
     return pl.pallas_call(
         functools.partial(scores_kernel, distances, split),
         out_shape=(shape,) * len(distances),
@@ -263,19 +284,19 @@
         out_specs=(VMEM,) * len(distances),
         compiler_params=limit(12),
         name="scores",
-    )(kept(decoder), kept(own_facts), *pieces)
-
-
-def gradients_kernel(distances, own_facts, *refs):
+    )(kept(decoder), kept(given), *pieces)
+
+
+def gradients_kernel(distances, given, *refs):
     pieces, refs = refs[: 2 * len(distances)], refs[2 * len(distances) :]
     total = refs[-1]
-    facts = facts_of(distances, own_facts, pieces)
+    facts = facts_of(distances, given, pieces)
     for columns, part in gradient_blocks(facts, pieces, total.shape[1]):
         total[:, columns] = part if len(refs) == 1 else refs[0][:, columns] + part
 
 
-def gradients_of(distances, pairs, own_facts, shape, total=None):
-    operands = [kept(own_facts)] + [kept(piece) for pair in pairs for piece in pair]
+def gradients_of(distances, pairs, given, shape, total=None):
+    operands = [kept(given)] + [kept(piece) for pair in pairs for piece in pair]
     operands += [] if total is None else [kept(total)]
     return pl.pallas_call(
         functools.partial(gradients_kernel, distances),
@@ -288,10 +309,9 @@
     )(*operands)
 
 
-def last_gradients_kernel(distance, tok_rows, left, right, total, out, rounded, sems):
-    facts = [facts_in(left, distance, tok_rows)]
+def last_gradients_kernel(given, left, right, total, out, rounded, sems):
     copies = []
-    for columns, part in gradient_blocks(facts, (left, right), out.shape[1]):
+    for columns, part in gradient_blocks([given[...]], (left, right), out.shape[1]):
         rounded[:, columns] = (total[:, columns] + part).astype(out.dtype)
         copies.append(
             pltpu.make_async_copy(
@@ -303,11 +323,11 @@
         copy.wait()
 
 
-def last_gradients(distance, pair, total, tok_rows):
-    return pl.pallas_call(
-        functools.partial(last_gradients_kernel, distance, tok_rows),
+def last_gradients(given, pair, total):
+    return pl.pallas_call(
+        last_gradients_kernel,
         out_shape=jax.ShapeDtypeStruct(total.shape, jnp.bfloat16),
-        in_specs=[VMEM] * 3,
+        in_specs=[VMEM] * 4,
         out_specs=ANY,
         scratch_shapes=[
             pltpu.VMEM(total.shape, jnp.bfloat16),
@@ -315,19 +335,19 @@
         ],
         compiler_params=limit(16),
         name="last_gradients",
-    )(kept(pair[0]), kept(pair[1]), kept(total))
-
-
-def stamp_kernel(left, right, for_left, for_right, left_out, right_out, rows, sems):
-    start = left.shape[0] - FACTS
-    targets = (left_out, right_out)
-    for i, piece in enumerate((left, right)):
+    )(kept(given), kept(pair[0]), kept(pair[1]), kept(total))
+
+
+def stamp_kernel(onward, back, for_onward, for_back, onward_out, back_out, rows, sems):
+    start = onward.shape[0] - FACTS
+    targets = (onward_out, back_out)
+    for i, piece in enumerate((onward, back)):
         pltpu.make_async_copy(
             piece.at[start : start + 16, :], rows.at[i], sems.at[i]
         ).start()
-    for i, values in enumerate((for_left, for_right)):
+    for i, values in enumerate((for_onward, for_back)):
         pltpu.make_async_copy(
-            left.at[start : start + 16, :], rows.at[i], sems.at[i]
+            onward.at[start : start + 16, :], rows.at[i], sems.at[i]
         ).wait()
         value = values[:KPB]
         high = value.astype(jnp.bfloat16).astype(jnp.float32)
@@ -359,12 +379,12 @@
     )(*[kept(piece) for piece in pieces], *[kept(value) for value in values])
 
 
-def unpack_kernel(owners, slots, own, left, right, second, third, opposite, out):
+def unpack_kernel(owners, slots, own, onward, back, second, third, opposite, out):
     owner = slots[...] // BLK_DEV
-    start = left.shape[0] - FACTS
+    start = onward.shape[0] - FACTS
     way = 1 - 2 * lax.axis_index("width")
     returned = [(0, own[...])]
-    for distance, piece in ((-1, left), (1, right)):
+    for distance, piece in ((-1, onward), (1, back)):
         rows = piece[start : start + 16, :].astype(jnp.float32)
         returned.append((distance, rows[:KPB] + rows[KPB : 2 * KPB]))
     returned += [(2 * way, second[...]), (3 * way, third[...]), (4, opposite[...])]
@@ -415,11 +435,12 @@
             pairs.append((2 * ring[i] + 1, 2 * ring[(i + distance) % owners] + 1))
         return lax.ppermute(x, ("dp", "width"), pairs)
 
-    left, right, own_facts, slots = prepare(
+    left, right = pieces_of(grad_out)
+    first_1 = hop((left, right))
+    known_left, known_right, own_facts, slots = prepare(
         block_slot, active_blocks, feature_idx, acts, grad_out, owners
     )
-    first_1 = hop((left, right))
-    second_1 = crossed((right, left))
+    second_1 = crossed((known_right, known_left))
     decoder = fetch(decoder)
     first_1, decoder = lax.optimization_barrier((first_1, decoder))
     first_2 = hop(first_1)
@@ -428,16 +449,21 @@
     distances = (0, -1, 1)
     own, onward, back = scores_of(distances, pairs, decoder, own_facts)
     total = gradients_of(distances, pairs, own_facts, decoder.shape)
-    first_2 = stamp(first_2, (back, onward))
     first_3 = hop(first_2)
+    second_2 = stamp(second_2, (back, onward))
     second_3 = crossed(second_2)
     pairs = [(first_2[0], second_2[0]), (second_2[1], first_2[1])]
     mine, others = scores_of((-2, 2), pairs, decoder, own_facts, True)
     total = gradients_of((-2, 2), pairs, own_facts, decoder.shape, total)
     second = mine + other_core(others)
+    relayed = [piece[-2 * KPB :].astype(jnp.float32) for piece in second_2]
+    relayed = jnp.where(lax.axis_index("width") == 0, relayed[1], relayed[0])
     total, first_3, second = lax.optimization_barrier((total, first_3, second))
-    second = return_by(2, jnp.concatenate([second, jnp.zeros((24, 128), jnp.float32)]))[:8]
+    returned = return_by(2, jnp.concatenate([second, relayed, jnp.zeros((48, 128), jnp.float32)]))
+    second, opposite_facts = returned[: 2 * KPB], returned[2 * KPB : 4 * KPB]
     first_4 = hop(first_3)
+    total, second, opposite_facts = lax.optimization_barrier((total, second, opposite_facts))
+    second_3, total = lax.optimization_barrier((second_3, total))
     pairs = [(first_3[0], second_3[0]), (second_3[1], first_3[1])]
     mine, others = scores_of((-3, 3), pairs, decoder, own_facts, True)
     total = gradients_of((-3, 3), pairs, own_facts, decoder.shape, total)
@@ -445,12 +471,12 @@
     total, third = lax.optimization_barrier((total, third))
     third = return_by(3, third)
     total, first_4 = lax.optimization_barrier((total, first_4))
-    (opposite,) = scores_of((4,), [first_4], decoder, own_facts)
-    opposite = shift(opposite, -4)
+    (opposite,) = scores_of((4,), [first_4], decoder, opposite_facts)
+    opposite = shift(opposite, -owners // 2)
     total, third = lax.optimization_barrier((total, third))
-    decoder_grad = last_gradients(4, first_4, total, tok_rows)
+    decoder_grad = last_gradients(opposite_facts, first_4, total)
     decoder_grad, opposite = lax.optimization_barrier((decoder_grad, opposite))
-    act_grad = unpack(slots, own, *first_3, second, third, opposite)
+    act_grad = unpack(slots, own, *second_3, second, third, opposite)
     act_grad = act_grad + other_core(act_grad)
     return (decoder_grad, act_grad.T)
 

time: 57 us -> 60.6 us (1.063)
  waiting for transfers between devices: 20.8 us -> 12.3 us
  local copies, waits for them, and re-layouts: 0.01 us -> 5.28 us
  Pallas kernels: 11.4 us -> 16.6 us
  starting transfers between devices: 23.2 us -> 24.3 us
    ppermute x15, waiting for transfers between devices: 19.4 us -> 10.6 us  [shift(): return lax.ppermute(x, 'dp', pairs)]
    unnamed x0 -> x16, local copies, waits for them, and re-layouts: none -> 5.2 us
    ppermute x2, starting transfers between devices: 3.77 us -> 5.86 us  [return_by(): return lax.ppermute(x, ('dp', 'width'), pairs)]
    pallas_call x4, Pallas kernels: 3.7 us -> 5.69 us  [scores_of(): pl.pallas_call(functools.partial(scores_kernel, distances, split), out_sh...]
    pallas_call x3, Pallas kernels: 3.03 us -> 5.02 us  [gradients_of(): pl.pallas_call(functools.partial(gradients_kernel, distances), out_shape=...]
    pallas_call x2 -> x3, Pallas kernels: 2.99 us -> 4.14 us  [the longest x1 1.75 us: last_gradients(): pl.pallas_call(last_gradients_kernel, out_shape=jax.ShapeDtypeStruct(tota...]
    ppermute x15, starting transfers between devices: 19.1 us -> 18.2 us  [shift(): return lax.ppermute(x, 'dp', pairs)]
  transfers between devices with their start and end apart: 20 -> 20, of which waited for: 13 -> 8; matrix products, arithmetic and copies ran while one was open for 0% -> 0% of each run, Pallas kernels for 18% -> 26%
where the time goes in v10:
time: 60.6 us; the launch traced here: 60 us
  starting transfers between devices  24.3 us (40%)
  Pallas kernels  16.6 us (27%)
  waiting for transfers between devices  12.3 us (20%)
  local copies, waits for them, and re-layouts  5.28 us (9%)
  between operations  0.86 us (1%)
  other arithmetic  0.7 us (1%)
    ppermute x15, starting transfers between devices, shift(): return lax.ppermute(x, 'dp', pairs)  18.2 us
    ppermute x15, waiting for transfers between devices, shift(): return lax.ppermute(x, 'dp', pairs)  10.6 us
    ppermute x2, starting transfers between devices, return_by(): return lax.ppermute(x, ('dp', 'width'), pairs)  5.86 us
    pallas_call x4, Pallas kernels, scores_of(): pl.pallas_call(functools.partial(scores_kernel, distances, split), out_sh...  5.69 us
    unnamed x16, local copies, waits for them, and re-layouts  5.2 us
    pallas_call x3, Pallas kernels, gradients_of(): pl.pallas_call(functools.partial(gradients_kernel, distances), out_shape=...  5.02 us
    pallas_call x1, Pallas kernels, last_gradients(): pl.pallas_call(last_gradients_kernel, out_shape=jax.ShapeDtypeStruct(tota...  1.75 us
    pallas_call x1, Pallas kernels, fetch(): pl.pallas_call(fetch_kernel, out_shape=pltpu.VMEM(x.shape, x.dtype), in_s...  1.6 us
  transfers between devices with their start and end apart: 20, of which 8 were waited for; matrix products, arithmetic and copies ran while one was open for 0% of the time, Pallas kernels for 26%

profile of v10, /device:TPU:0, one launch (start us, length us, event | category | flops | bytes accessed | tf_op | source)
XLA Modules:
  0.0 60.0 jit_solution(3179369224918740419)
XLA Ops:
  0.6 1.2 %pieces.1 = (bf16[1024,128]{1,0:T(8,128)(2,1)S(1)}, bf16[1024,128]{1,0:T(8,128)(2,1)S(1)}) custom-call(bf16[128,2048]{1,0:T(8,128)(2,1)} %grad_out.1), custom_call_target="tpu_custom_call" | custom-call | tf_op jit(solution)/shard_map/pieces/pallas_call | solution.py:72
  1.8 0.0 copy-start
  1.8 0.0 copy-start.2
  1.8 3.1 %collective-permute-start = (bf16[1024,128]{1,0:T(8,128)(2,1)S(1)}, bf16[1024,128]{1,0:T(8,128)(2,1)S(1)}, u32[]{:S(2)}, u32[]{:S(2)}) collective-permute-start(bf16[1024,128]{1,0:T(8,128)(2,1)S(1)} %get-tuple-element.40.refs_0_), channel_id=1, source_target_pairs={{0,4},{4,8},{8,12},{12,14},{14,10},{10,6},{6,2},{2,0},{1,5},{5,9},... | collective-permute-start | bytes 786440 | tf_op jit(solution)/shard_map/ppermute | solution.py:418
  4.9 0.0 collective-permute-start.1
  4.9 1.2 %prepare.1 = (bf16[1056,128]{1,0:T(8,128)(2,1)S(1)}, bf16[1056,128]{1,0:T(8,128)(2,1)S(1)}, f32[8,128]{1,0:T(8,128)S(1)}, s32[8,128]{1,0:T(8,128)S(1)}) custom-call(s32[32]{0:T(128)} %refs_0_.1, s32[8,128]{1,0:T(8,128)} %bitcast.7, s32[32,128]{1,0:T(8,128)} %bitcast.5, bf16[32,128]{1,0:T(8,128)(2,1)} %bitcast.6, bf16[128,2048]{1,0:T(8,128)(2,1)} %grad_out.1), custom_call_target="tpu_custom_call" | custom-call | tf_op jit(solution)/shard_map/prepare/pallas_call | solution.py:142
  6.1 2.1 %collective-permute-start.3 = (bf16[1056,128]{1,0:T(8,128)(2,1)S(1)}, bf16[1056,128]{1,0:T(8,128)(2,1)S(1)}, u32[]{:S(2)}, u32[]{:S(2)}) collective-permute-start(bf16[1056,128]{1,0:T(8,128)(2,1)S(1)} %get-tuple-element.43), channel_id=1, source_target_pairs={{0,4},{4,8},{8,12},{12,14},{14,10},{10,6},{6,2},{2,0},{1,5},{5,9},... | collective-permute-start | bytes 811016 | tf_op jit(solution)/shard_map/ppermute | solution.py:418
  8.2 0.0 collective-permute-start.5
  8.2 1.6 %fetch.1.decoder = bf16[512,2048]{1,0:T(8,128)(2,1)S(1)} custom-call(bf16[512,2048]{1,0:T(8,128)(2,1)} %source.1), custom_call_target="tpu_custom_call" | custom-call | tf_op jit(solution)/shard_map/fetch/pallas_call | solution.py:168
  9.8 2.1 %collective-permute-done.refs_2_ = bf16[1024,128]{1,0:T(8,128)(2,1)S(1)} collective-permute-done((bf16[1024,128]{1,0:T(8,128)(2,1)S(1)}, bf16[1024,128]{1,0:T(8,128)(2,1)S(1)}, u32[]{:S(2)}, u32[]{:S(2)}) %collective-permute-start) | collective-permute-done | bytes 262176 | tf_op jit(solution)/shard_map/ppermute | solution.py:418
  11.9 2.2 %collective-permute-done.1.refs_5_ = bf16[1024,128]{1,0:T(8,128)(2,1)S(1)} collective-permute-done((bf16[1024,128]{1,0:T(8,128)(2,1)S(1)}, bf16[1024,128]{1,0:T(8,128)(2,1)S(1)}, u32[]{:S(2)}, u32[]{:S(2)}) %collective-permute-start.1) | collective-permute-done | bytes 262176 | tf_op jit(solution)/shard_map/ppermute | solution.py:418
  14.1 1.6 %collective-permute-start.2 = (bf16[1024,128]{1,0:T(8,128)(2,1)S(1)}, bf16[1024,128]{1,0:T(8,128)(2,1)}, u32[]{:S(2)}, u32[]{:S(2)}) collective-permute-start(bf16[1024,128]{1,0:T(8,128)(2,1)S(1)} %collective-permute-done.refs_2_), channel_id=1, source_target_pairs={{0,4},{4,8},{8,12},{12,14},{14,10},{10,6},{6,2},{2,0},{1,5},{5,9},... | collective-permute-start | bytes 786440 | tf_op jit(solution)/shard_map/ppermute | solution.py:418
  15.7 0.7 %copy-done.4 = bf16[1024,128]{1,0:T(8,128)(2,1)} copy-done((bf16[1024,128]{1,0:T(8,128)(2,1)}, bf16[1024,128]{1,0:T(8,128)(2,1)S(1)}, u32[]{:S(2)}) %copy-start.4) | copy-done | bytes 262168
  16.4 0.4 collective-permute-start.7
  16.8 0.0 copy-done
  16.9 0.7 %copy-done.6 = bf16[1024,128]{1,0:T(8,128)(2,1)} copy-done((bf16[1024,128]{1,0:T(8,128)(2,1)}, bf16[1024,128]{1,0:T(8,128)(2,1)S(1)}, u32[]{:S(2)}) %copy-start.6) | copy-done | bytes 262168
  17.5 0.2 collective-permute-done.3.refs_3_
  17.7 2.1 %collective-permute-start.4 = (bf16[1056,128]{1,0:T(8,128)(2,1)S(1)}, bf16[1056,128]{1,0:T(8,128)(2,1)S(1)}, u32[]{:S(2)}, u32[]{:S(2)}) collective-permute-start(bf16[1056,128]{1,0:T(8,128)(2,1)S(1)} %collective-permute-done.3.refs_3_), channel_id=1, source_target_pairs={{0,4},{4,8},{8,12},{12,14},{14,10},{10,6},{6,2},{2,0},{1,5},{5,9},... | collective-permute-start | bytes 811016 | tf_op jit(solution)/shard_map/ppermute | solution.py:418
  19.9 0.0 collective-permute-done.5.refs_4_
  19.9 0.0 collective-permute-start.6
  19.9 3.5 %collective-permute-done.2.refs_0_ = bf16[1024,128]{1,0:T(8,128)(2,1)} collective-permute-done((bf16[1024,128]{1,0:T(8,128)(2,1)S(1)}, bf16[1024,128]{1,0:T(8,128)(2,1)}, u32[]{:S(2)}, u32[]{:S(2)}) %collective-permute-start.2) | collective-permute-done | bytes 262176 | tf_op jit(solution)/shard_map/ppermute | solution.py:418
  23.5 2.1 %collective-permute-start.8 = (bf16[1024,128]{1,0:T(8,128)(2,1)}, bf16[1024,128]{1,0:T(8,128)(2,1)S(1)}, u32[]{:S(2)}, u32[]{:S(2)}) collective-permute-start(bf16[1024,128]{1,0:T(8,128)(2,1)} %collective-permute-done.2.refs_0_), channel_id=1, source_target_pairs={{0,4},{4,8},{8,12},{12,14},{14,10},{10,6},{6,2},{2,0},{1,5},{5,9},... | collective-permute-start | bytes 786440 | tf_op jit(solution)/shard_map/ppermute | solution.py:418
  25.6 0.1 collective-permute-done.7.refs_3_
  25.7 0.4 collective-permute-start.9
  26.2 0.1 pad.2.clone
  26.3 0.9 %copy-done.1 = bf16[1024,128]{1,0:T(8,128)(2,1)S(1)} copy-done((bf16[1024,128]{1,0:T(8,128)(2,1)S(1)}, bf16[1024,128]{1,0:T(8,128)(2,1)}, u32[]{:S(2)}) %copy-start.1) | copy-done | bytes 262168
  27.2 0.9 %copy-done.3 = bf16[1024,128]{1,0:T(8,128)(2,1)S(1)} copy-done((bf16[1024,128]{1,0:T(8,128)(2,1)S(1)}, bf16[1024,128]{1,0:T(8,128)(2,1)}, u32[]{:S(2)}) %copy-start.3) | copy-done | bytes 262168
  28.2 0.9 %copy-done.5 = bf16[1024,128]{1,0:T(8,128)(2,1)S(1)} copy-done((bf16[1024,128]{1,0:T(8,128)(2,1)S(1)}, bf16[1024,128]{1,0:T(8,128)(2,1)}, u32[]{:S(2)}) %copy-start.5) | copy-done | bytes 262168
  29.1 0.9 %copy-done.7 = bf16[1024,128]{1,0:T(8,128)(2,1)S(1)} copy-done((bf16[1024,128]{1,0:T(8,128)(2,1)S(1)}, bf16[1024,128]{1,0:T(8,128)(2,1)}, u32[]{:S(2)}) %copy-start.7) | copy-done | bytes 262168
  30.1 1.3 %gradients.3.refs_4_ = f32[512,2048]{1,0:T(8,128)S(1)} custom-call(f32[8,128]{1,0:T(8,128)S(1)} %get-tuple-element.39.given, bf16[1024,128]{1,0:T(8,128)(2,1)S(1)} %copy-done.1, bf16[1024,128]{1,0:T(8,128)(2,1)S(1)} %copy-done.3, bf16[1024,128]{1,0:T(8,128)(2,1)S(1)} %copy-done.5, bf16[1056,128]{1,0:T(8,128)(2,1)S(1)} %collective-permute-done.3.refs_3_, ...), custom_call_target="tpu_custom_call" | custom-call | tf_op jit(solution)/shard_map/gradients/pallas_call | solution.py:301
  31.3 1.4 %scores.4 = (f32[8,128]{1,0:T(8,128)S(1)}, f32[8,128]{1,0:T(8,128)S(1)}, f32[8,128]{1,0:T(8,128)S(1)}) custom-call(bf16[512,2048]{1,0:T(8,128)(2,1)S(1)} %fetch.1.decoder, f32[8,128]{1,0:T(8,128)S(1)} %get-tuple-element.39.given, bf16[1024,128]{1,0:T(8,128)(2,1)S(1)} %copy-done.1, bf16[1024,128]{1,0:T(8,128)(2,1)S(1)} %copy-done.3, ...), custom_call_target="tpu_custom_call" | custom-call | tf_op jit(solution)/shard_map/scores/pallas_call | solution.py:280
  32.7 0.0 collective-permute-done.4.onward
  32.7 0.0 collective-permute-done.6.back
  32.7 0.1 stamp.1
  32.8 1.6 %collective-permute-start.12 = (bf16[1056,128]{1,0:T(8,128)(2,1)S(1)}, bf16[1056,128]{1,0:T(8,128)(2,1)S(1)}, u32[]{:S(2)}, u32[]{:S(2)}) collective-permute-start(bf16[1056,128]{1,0:T(8,128)(2,1)S(1)} %get-tuple-element.49.refs_1_), channel_id=1, source_target_pairs={{0,4},{4,8},{8,12},{12,14},{14,10},{10,6},{6,2},{2,0},{1,5},{5,9},... | collective-permute-start | bytes 811016 | tf_op jit(solution)/shard_map/ppermute | solution.py:418
  34.4 0.4 collective-permute-start.13
  34.9 1.8 %scores.5 = (f32[8,128]{1,0:T(8,128)S(1)}, f32[8,128]{1,0:T(8,128)S(1)}) custom-call(bf16[512,2048]{1,0:T(8,128)(2,1)S(1)} %fetch.1.decoder, f32[8,128]{1,0:T(8,128)S(1)} %get-tuple-element.39.given, bf16[1024,128]{1,0:T(8,128)(2,1)} %collective-permute-done.2.refs_0_, bf16[1056,128]{1,0:T(8,128)(2,1)S(1)} %get-tuple-element.49.refs_1_, ...), custom_call_target="tpu_custom_call" | custom-call | tf_op jit(solution)/shard_map/scores/pallas_call | solution.py:280
  36.7 0.1 collective-permute-start.10
  36.8 1.9 %gradients.4.refs_4_ = f32[512,2048]{1,0:T(8,128)S(1)} custom-call(f32[8,128]{1,0:T(8,128)S(1)} %get-tuple-element.39.given, bf16[1024,128]{1,0:T(8,128)(2,1)} %collective-permute-done.2.refs_0_, bf16[1056,128]{1,0:T(8,128)(2,1)S(1)} %get-tuple-element.49.refs_1_, bf16[1056,128]{1,0:T(8,128)(2,1)S(1)} %get-tuple-element.50.refs_2_, ...), custom_call_target="tpu_custom_call", output_to_operand_aliasing={{}: (5, {})} | custom-call | tf_op jit(solution)/shard_map/gradients/pallas_call | solution.py:301
  38.8 0.0 collective-permute-done.10
  38.8 0.0 collective-permute-done.8.refs_0_
  38.8 0.0 collective-permute-done.9.refs_3_
  38.8 0.1 maximum_maximum_fusion
  38.9 2.4 %collective-permute-start.11 = (f32[64,128]{1,0:T(8,128)S(1)}, f32[64,128]{1,0:T(8,128)S(1)}, u32[]{:S(2)}, u32[]{:S(2)}) collective-permute-start(f32[64,128]{1,0:T(8,128)S(1)} %maximum_maximum_fusion), channel_id=1, source_target_pairs={{0,6},{1,9},{4,2},{5,13},{8,0},{9,15},{12,4},{13,11},{14,8},{15,7}... | collective-permute-start | bytes 98312 | tf_op jit(solution)/shard_map/ppermute | solution.py:436
  41.3 0.4 collective-permute-start.15
  41.7 1.6 %collective-permute-start.16 = (bf16[1024,128]{1,0:T(8,128)(2,1)}, bf16[1024,128]{1,0:T(8,128)(2,1)S(1)}, u32[]{:S(2)}, u32[]{:S(2)}) collective-permute-start(bf16[1024,128]{1,0:T(8,128)(2,1)} %collective-permute-done.9.refs_3_), channel_id=1, source_target_pairs={{0,2},{4,0},{8,4},{12,8},{14,12},{10,14},{6,10},{2,6},{1,3},{5,1},... | collective-permute-start | bytes 786440 | tf_op jit(solution)/shard_map/ppermute | solution.py:418
  43.3 0.5 collective-permute-done.11
  43.8 0.0 collective-permute-done.12.refs_1_.onward
  43.8 0.0 collective-permute-done.13.refs_2_.back
  43.8 1.8 %scores.6 = (f32[8,128]{1,0:T(8,128)S(1)}, f32[8,128]{1,0:T(8,128)S(1)}) custom-call(bf16[512,2048]{1,0:T(8,128)(2,1)S(1)} %fetch.1.decoder, f32[8,128]{1,0:T(8,128)S(1)} %get-tuple-element.39.given, bf16[1024,128]{1,0:T(8,128)(2,1)S(1)} %collective-permute-done.8.refs_0_, bf16[1056,128]{1,0:T(8,128)(2,1)S(1)} %collective-permute-done.12.refs_1_.onward, ...), custom_call_target="tpu_custom_call" | custom-call | tf_op jit(solution)/shard_map/scores/pallas_call | solution.py:280
  45.6 0.1 collective-permute-start.14
  45.7 1.8 %gradients.5.total = f32[512,2048]{1,0:T(8,128)S(1)} custom-call(f32[8,128]{1,0:T(8,128)S(1)} %get-tuple-element.39.given, bf16[1024,128]{1,0:T(8,128)(2,1)S(1)} %collective-permute-done.8.refs_0_, bf16[1056,128]{1,0:T(8,128)(2,1)S(1)} %collective-permute-done.12.refs_1_.onward, ...), custom_call_target="tpu_custom_call", output_to_operand_aliasing={{}: (5, {})} | custom-call | tf_op jit(solution)/shard_map/gradients/pallas_call | solution.py:301
  47.5 0.0 collective-permute-done.14
  47.5 3.5 %collective-permute-start.17 = (f32[8,128]{1,0:T(8,128)S(1)}, f32[8,128]{1,0:T(8,128)S(1)}, u32[]{:S(2)}, u32[]{:S(2)}) collective-permute-start(f32[8,128]{1,0:T(8,128)S(1)} %add.10), channel_id=1, source_target_pairs={{0,10},{1,13},{4,6},{5,15},{8,2},{9,11},{12,0},{13,7},{14,4},{15,3... | collective-permute-start | bytes 12296 | tf_op jit(solution)/shard_map/ppermute | solution.py:436
  51.0 0.0 collective-permute-done.15.left.refs_0_
  51.0 0.0 collective-permute-done.16.right.refs_1_
  51.0 0.7 %scores.7 = f32[8,128]{1,0:T(8,128)S(1)} custom-call(bf16[512,2048]{1,0:T(8,128)(2,1)S(1)} %fetch.1.decoder, f32[8,128]{1,0:T(8,128)S(1)} %get-tuple-element.55.given, bf16[1024,128]{1,0:T(8,128)(2,1)S(1)} %collective-permute-done.15.left.refs_0_, bf16[1024,128]{1,0:T(8,128)(2,1)S(1)} %collective-permute-done.16.right.refs_1_), custom_call_target="tpu_custom_call" | custom-call | tf_op jit(solution)/shard_map/scores/pallas_call | solution.py:280
  51.7 2.2 %collective-permute-start.18 = (f32[8,128]{1,0:T(8,128)S(1)}, f32[8,128]{1,0:T(8,128)S(1)}, u32[]{:S(2)}, u32[]{:S(2)}) collective-permute-start(f32[8,128]{1,0:T(8,128)S(1)} %scores.7), channel_id=1, source_target_pairs={{0,14},{4,10},{8,6},{12,2},{14,0},{10,4},{6,8},{2,12},{1,15},{5,11... | collective-permute-start | bytes 12296 | tf_op jit(solution)/shard_map/ppermute | solution.py:418
  53.9 0.0 collective-permute-done.17.third
  53.9 1.8 %last_gradients.1 = bf16[512,2048]{1,0:T(8,128)(2,1)} custom-call(f32[8,128]{1,0:T(8,128)S(1)} %get-tuple-element.55.given, bf16[1024,128]{1,0:T(8,128)(2,1)S(1)} %collective-permute-done.15.left.refs_0_, bf16[1024,128]{1,0:T(8,128)(2,1)S(1)} %collective-permute-done.16.right.refs_1_, f32[512,2048]{1,0:T(8,128)S(1)} %gradients.5.total), custom_call_target="tpu_custom_call" | custom-call | tf_op jit(solution)/shard_map/last_gradients/pallas_call | solution.py:327
  55.7 2.4 %collective-permute-done.18.opposite = f32[8,128]{1,0:T(8,128)S(1)} collective-permute-done((f32[8,128]{1,0:T(8,128)S(1)}, f32[8,128]{1,0:T(8,128)S(1)}, u32[]{:S(2)}, u32[]{:S(2)}) %collective-permute-start.18) | collective-permute-done | bytes 4128 | tf_op jit(solution)/shard_map/ppermute | solution.py:418
  58.1 0.1 collective-permute-start.19
  58.2 1.2 %collective-permute-done.19 = f32[32,128]{1,0:T(8,128)S(1)} collective-permute-done((f32[32,128]{1,0:T(8,128)S(1)}, f32[32,128]{1,0:T(8,128)S(1)}, u32[]{:S(2)}, u32[]{:S(2)}) %collective-permute-start.19) | collective-permute-done | bytes 16416 | tf_op jit(solution)/shard_map/ppermute | solution.py:429
  59.4 0.6 %add_bitcast_fusion = f32[128,32]{0,1:T(8,128)} fusion(f32[32,128]{1,0:T(8,128)S(1)} %unpack.1, f32[32,128]{1,0:T(8,128)S(1)} %collective-permute-done.19), kind=kLoop, calls=%fused_computation.1 | loop fusion | flops 4096 | bytes 49152 | tf_op jit(solution)/shard_map/transpose | solution.py:481
  (13 shorter events, 0.1 us)
Async XLA Ops:
  1.8 15.1 %copy-start = (bf16[1024,128]{1,0:T(8,128)(2,1)}, bf16[1024,128]{1,0:T(8,128)(2,1)S(1)}, u32[]{:S(2)}) copy-start(bf16[1024,128]{1,0:T(8,128)(2,1)S(1)} %get-tuple-element.40.refs_0_) | copy-start | bytes 786436
  1.8 15.0 %copy-start.2 = (bf16[1024,128]{1,0:T(8,128)(2,1)}, bf16[1024,128]{1,0:T(8,128)(2,1)S(1)}, u32[]{:S(2)}) copy-start(bf16[1024,128]{1,0:T(8,128)(2,1)S(1)} %get-tuple-element.41.refs_1_) | copy-start | bytes 786436
  1.8 10.1 %collective-permute-start = (bf16[1024,128]{1,0:T(8,128)(2,1)S(1)}, bf16[1024,128]{1,0:T(8,128)(2,1)S(1)}, u32[]{:S(2)}, u32[]{:S(2)}) collective-permute-start(bf16[1024,128]{1,0:T(8,128)(2,1)S(1)} %get-tuple-element.40.refs_0_), channel_id=1, source_target_pairs={{0,4},{4,8},{8,12},{12,14},{14,10},{10,6},{6,2},{2,0},{1,5},{5,9},... | collective-permute-start | bytes 786440 | tf_op jit(solution)/shard_map/ppermute | solution.py:418
  4.9 9.2 %collective-permute-start.1 = (bf16[1024,128]{1,0:T(8,128)(2,1)S(1)}, bf16[1024,128]{1,0:T(8,128)(2,1)S(1)}, u32[]{:S(2)}, u32[]{:S(2)}) collective-permute-start(bf16[1024,128]{1,0:T(8,128)(2,1)S(1)} %get-tuple-element.41.refs_1_), channel_id=1, source_target_pairs={{0,2},{4,0},{8,4},{12,8},{14,12},{10,14},{6,10},{2,6},{1,3},{5,1},... | collective-permute-start | bytes 786440 | tf_op jit(solution)/shard_map/ppermute | solution.py:418
  6.1 11.6 %collective-permute-start.3 = (bf16[1056,128]{1,0:T(8,128)(2,1)S(1)}, bf16[1056,128]{1,0:T(8,128)(2,1)S(1)}, u32[]{:S(2)}, u32[]{:S(2)}) collective-permute-start(bf16[1056,128]{1,0:T(8,128)(2,1)S(1)} %get-tuple-element.43), channel_id=1, source_target_pairs={{0,4},{4,8},{8,12},{12,14},{14,10},{10,6},{6,2},{2,0},{1,5},{5,9},... | collective-permute-start | bytes 811016 | tf_op jit(solution)/shard_map/ppermute | solution.py:418
  8.2 11.7 %collective-permute-start.5 = (bf16[1056,128]{1,0:T(8,128)(2,1)S(1)}, bf16[1056,128]{1,0:T(8,128)(2,1)S(1)}, u32[]{:S(2)}, u32[]{:S(2)}) collective-permute-start(bf16[1056,128]{1,0:T(8,128)(2,1)S(1)} %get-tuple-element.44), channel_id=1, source_target_pairs={{0,2},{4,0},{8,4},{12,8},{14,12},{10,14},{6,10},{2,6},{1,3},{5,1},... | collective-permute-start | bytes 811016 | tf_op jit(solution)/shard_map/ppermute | solution.py:418
  14.1 9.3 %collective-permute-start.2 = (bf16[1024,128]{1,0:T(8,128)(2,1)S(1)}, bf16[1024,128]{1,0:T(8,128)(2,1)}, u32[]{:S(2)}, u32[]{:S(2)}) collective-permute-start(bf16[1024,128]{1,0:T(8,128)(2,1)S(1)} %collective-permute-done.refs_2_), channel_id=1, source_target_pairs={{0,4},{4,8},{8,12},{12,14},{14,10},{10,6},{6,2},{2,0},{1,5},{5,9},... | collective-permute-start | bytes 786440 | tf_op jit(solution)/shard_map/ppermute | solution.py:418
  15.7 0.7 %copy-start.4 = (bf16[1024,128]{1,0:T(8,128)(2,1)}, bf16[1024,128]{1,0:T(8,128)(2,1)S(1)}, u32[]{:S(2)}) copy-start(bf16[1024,128]{1,0:T(8,128)(2,1)S(1)} %collective-permute-done.refs_2_) | copy-start | bytes 786436
  16.4 9.3 %collective-permute-start.7 = (bf16[1024,128]{1,0:T(8,128)(2,1)S(1)}, bf16[1024,128]{1,0:T(8,128)(2,1)}, u32[]{:S(2)}, u32[]{:S(2)}) collective-permute-start(bf16[1024,128]{1,0:T(8,128)(2,1)S(1)} %collective-permute-done.1.refs_5_), channel_id=1, source_target_pairs={{0,2},{4,0},{8,4},{12,8},{14,12},{10,14},{6,10},{2,6},{1,3},{5,1},... | collective-permute-start | bytes 786440 | tf_op jit(solution)/shard_map/ppermute | solution.py:418
  16.9 0.7 %copy-start.6 = (bf16[1024,128]{1,0:T(8,128)(2,1)}, bf16[1024,128]{1,0:T(8,128)(2,1)S(1)}, u32[]{:S(2)}) copy-start(bf16[1024,128]{1,0:T(8,128)(2,1)S(1)} %collective-permute-done.1.refs_5_) | copy-start | bytes 786436
  17.7 15.0 %collective-permute-start.4 = (bf16[1056,128]{1,0:T(8,128)(2,1)S(1)}, bf16[1056,128]{1,0:T(8,128)(2,1)S(1)}, u32[]{:S(2)}, u32[]{:S(2)}) collective-permute-start(bf16[1056,128]{1,0:T(8,128)(2,1)S(1)} %collective-permute-done.3.refs_3_), channel_id=1, source_target_pairs={{0,4},{4,8},{8,12},{12,14},{14,10},{10,6},{6,2},{2,0},{1,5},{5,9},... | collective-permute-start | bytes 811016 | tf_op jit(solution)/shard_map/ppermute | solution.py:418
  19.9 12.8 %collective-permute-start.6 = (bf16[1056,128]{1,0:T(8,128)(2,1)S(1)}, bf16[1056,128]{1,0:T(8,128)(2,1)S(1)}, u32[]{:S(2)}, u32[]{:S(2)}) collective-permute-start(bf16[1056,128]{1,0:T(8,128)(2,1)S(1)} %collective-permute-done.5.refs_4_), channel_id=1, source_target_pairs={{0,2},{4,0},{8,4},{12,8},{14,12},{10,14},{6,10},{2,6},{1,3},{5,1},... | collective-permute-start | bytes 811016 | tf_op jit(solution)/shard_map/ppermute | solution.py:418
  23.5 15.3 %collective-permute-start.8 = (bf16[1024,128]{1,0:T(8,128)(2,1)}, bf16[1024,128]{1,0:T(8,128)(2,1)S(1)}, u32[]{:S(2)}, u32[]{:S(2)}) collective-permute-start(bf16[1024,128]{1,0:T(8,128)(2,1)} %collective-permute-done.2.refs_0_), channel_id=1, source_target_pairs={{0,4},{4,8},{8,12},{12,14},{14,10},{10,6},{6,2},{2,0},{1,5},{5,9},... | collective-permute-start | bytes 786440 | tf_op jit(solution)/shard_map/ppermute | solution.py:418
  25.7 13.1 %collective-permute-start.9 = (bf16[1024,128]{1,0:T(8,128)(2,1)}, bf16[1024,128]{1,0:T(8,128)(2,1)}, u32[]{:S(2)}, u32[]{:S(2)}) collective-permute-start(bf16[1024,128]{1,0:T(8,128)(2,1)} %collective-permute-done.7.refs_3_), channel_id=1, source_target_pairs={{0,2},{4,0},{8,4},{12,8},{14,12},{10,14},{6,10},{2,6},{1,3},{5,1},... | collective-permute-start | bytes 786440 | tf_op jit(solution)/shard_map/ppermute | solution.py:418
  26.3 0.9 %copy-start.1 = (bf16[1024,128]{1,0:T(8,128)(2,1)S(1)}, bf16[1024,128]{1,0:T(8,128)(2,1)}, u32[]{:S(2)}) copy-start(bf16[1024,128]{1,0:T(8,128)(2,1)} %copy-done) | copy-start | bytes 786436
  27.2 0.9 %copy-start.3 = (bf16[1024,128]{1,0:T(8,128)(2,1)S(1)}, bf16[1024,128]{1,0:T(8,128)(2,1)}, u32[]{:S(2)}) copy-start(bf16[1024,128]{1,0:T(8,128)(2,1)} %copy-done.2) | copy-start | bytes 786436
  28.2 0.9 %copy-start.5 = (bf16[1024,128]{1,0:T(8,128)(2,1)S(1)}, bf16[1024,128]{1,0:T(8,128)(2,1)}, u32[]{:S(2)}) copy-start(bf16[1024,128]{1,0:T(8,128)(2,1)} %copy-done.4) | copy-start | bytes 786436
  29.1 0.9 %copy-start.7 = (bf16[1024,128]{1,0:T(8,128)(2,1)S(1)}, bf16[1024,128]{1,0:T(8,128)(2,1)}, u32[]{:S(2)}) copy-start(bf16[1024,128]{1,0:T(8,128)(2,1)} %copy-done.6) | copy-start | bytes 786436
  32.8 11.0 %collective-permute-start.12 = (bf16[1056,128]{1,0:T(8,128)(2,1)S(1)}, bf16[1056,128]{1,0:T(8,128)(2,1)S(1)}, u32[]{:S(2)}, u32[]{:S(2)}) collective-permute-start(bf16[1056,128]{1,0:T(8,128)(2,1)S(1)} %get-tuple-element.49.refs_1_), channel_id=1, source_target_pairs={{0,4},{4,8},{8,12},{12,14},{14,10},{10,6},{6,2},{2,0},{1,5},{5,9},... | collective-permute-start | bytes 811016 | tf_op jit(solution)/shard_map/ppermute | solution.py:418
  34.4 9.4 %collective-permute-start.13 = (bf16[1056,128]{1,0:T(8,128)(2,1)S(1)}, bf16[1056,128]{1,0:T(8,128)(2,1)S(1)}, u32[]{:S(2)}, u32[]{:S(2)}) collective-permute-start(bf16[1056,128]{1,0:T(8,128)(2,1)S(1)} %get-tuple-element.50.refs_2_), channel_id=1, source_target_pairs={{0,2},{4,0},{8,4},{12,8},{14,12},{10,14},{6,10},{2,6},{1,3},{5,1},... | collective-permute-start | bytes 811016 | tf_op jit(solution)/shard_map/ppermute | solution.py:418
  36.7 2.0 %collective-permute-start.10 = (f32[8,128]{1,0:T(8,128)S(1)}, f32[8,128]{1,0:T(8,128)S(1)}, u32[]{:S(2)}, u32[]{:S(2)}) collective-permute-start(f32[8,128]{1,0:T(8,128)S(1)} %get-tuple-element.52), channel_id=1, source_target_pairs={{0,1},{1,0},{2,3},{3,2},{4,5},{5,4},{6,7},{7,6},{8,9},{9,8},{10,11... | collective-permute-start | bytes 12296 | tf_op jit(solution)/shard_map/ppermute | solution.py:429
  38.9 4.9 %collective-permute-start.11 = (f32[64,128]{1,0:T(8,128)S(1)}, f32[64,128]{1,0:T(8,128)S(1)}, u32[]{:S(2)}, u32[]{:S(2)}) collective-permute-start(f32[64,128]{1,0:T(8,128)S(1)} %maximum_maximum_fusion), channel_id=1, source_target_pairs={{0,6},{1,9},{4,2},{5,13},{8,0},{9,15},{12,4},{13,11},{14,8},{15,7}... | collective-permute-start | bytes 98312 | tf_op jit(solution)/shard_map/ppermute | solution.py:436
  41.3 9.7 %collective-permute-start.15 = (bf16[1024,128]{1,0:T(8,128)(2,1)S(1)}, bf16[1024,128]{1,0:T(8,128)(2,1)S(1)}, u32[]{:S(2)}, u32[]{:S(2)}) collective-permute-start(bf16[1024,128]{1,0:T(8,128)(2,1)S(1)} %collective-permute-done.8.refs_0_), channel_id=1, source_target_pairs={{0,4},{4,8},{8,12},{12,14},{14,10},{10,6},{6,2},{2,0},{1,5},{5,9},... | collective-permute-start | bytes 786440 | tf_op jit(solution)/shard_map/ppermute | solution.py:418
  41.7 9.3 %collective-permute-start.16 = (bf16[1024,128]{1,0:T(8,128)(2,1)}, bf16[1024,128]{1,0:T(8,128)(2,1)S(1)}, u32[]{:S(2)}, u32[]{:S(2)}) collective-permute-start(bf16[1024,128]{1,0:T(8,128)(2,1)} %collective-permute-done.9.refs_3_), channel_id=1, source_target_pairs={{0,2},{4,0},{8,4},{12,8},{14,12},{10,14},{6,10},{2,6},{1,3},{5,1},... | collective-permute-start | bytes 786440 | tf_op jit(solution)/shard_map/ppermute | solution.py:418
  45.6 1.9 %collective-permute-start.14 = (f32[8,128]{1,0:T(8,128)S(1)}, f32[8,128]{1,0:T(8,128)S(1)}, u32[]{:S(2)}, u32[]{:S(2)}) collective-permute-start(f32[8,128]{1,0:T(8,128)S(1)} %get-tuple-element.63), channel_id=1, source_target_pairs={{0,1},{1,0},{2,3},{3,2},{4,5},{5,4},{6,7},{7,6},{8,9},{9,8},{10,11... | collective-permute-start | bytes 12296 | tf_op jit(solution)/shard_map/ppermute | solution.py:429
  47.5 6.4 %collective-permute-start.17 = (f32[8,128]{1,0:T(8,128)S(1)}, f32[8,128]{1,0:T(8,128)S(1)}, u32[]{:S(2)}, u32[]{:S(2)}) collective-permute-start(f32[8,128]{1,0:T(8,128)S(1)} %add.10), channel_id=1, source_target_pairs={{0,10},{1,13},{4,6},{5,15},{8,2},{9,11},{12,0},{13,7},{14,4},{15,3... | collective-permute-start | bytes 12296 | tf_op jit(solution)/shard_map/ppermute | solution.py:436
  51.7 6.4 %collective-permute-start.18 = (f32[8,128]{1,0:T(8,128)S(1)}, f32[8,128]{1,0:T(8,128)S(1)}, u32[]{:S(2)}, u32[]{:S(2)}) collective-permute-start(f32[8,128]{1,0:T(8,128)S(1)} %scores.7), channel_id=1, source_target_pairs={{0,14},{4,10},{8,6},{12,2},{14,0},{10,4},{6,8},{2,12},{1,15},{5,11... | collective-permute-start | bytes 12296 | tf_op jit(solution)/shard_map/ppermute | solution.py:418
  58.1 1.2 %collective-permute-start.19 = (f32[32,128]{1,0:T(8,128)S(1)}, f32[32,128]{1,0:T(8,128)S(1)}, u32[]{:S(2)}, u32[]{:S(2)}) collective-permute-start(f32[32,128]{1,0:T(8,128)S(1)} %unpack.1), channel_id=1, source_target_pairs={{0,1},{1,0},{2,3},{3,2},{4,5},{5,4},{6,7},{7,6},{8,9},{9,8},{10,11... | collective-permute-start | bytes 49160 | tf_op jit(solution)/shard_map/ppermute | solution.py:429

commit v11 on v10

--- a/solution.py
+++ b/solution.py
@@ -264,24 +264,27 @@
     ]
 
 
-def scores_kernel(distances, split, decoder, given, *refs):
+def scores_kernel(distances, split, relay, decoder, given, *refs):
     pieces, picked = refs[: 2 * len(distances)], refs[2 * len(distances) :]
     picks = picks_of(facts_of(distances, given, pieces), decoder, pieces)
     if split:
         first = lax.axis_index("width") == 0
-        picks = jnp.where(first, *picks), jnp.where(first, *picks[::-1])
+        picks = [jnp.where(first, *picks), jnp.where(first, *picks[::-1])]
+    if relay:
+        onward, back = (facts_in(piece, 4, given.shape[1]) for piece in pieces[1:3])
+        picks.append(jnp.where(first, back, onward))
     for target, values in zip(picked, picks):
         target[...] = values
 
 
-def scores_of(distances, pairs, decoder, given, split=False):
+def scores_of(distances, pairs, decoder, given, split=False, relay=False):
     pieces = [kept(piece) for pair in pairs for piece in pair]
     shape = pltpu.VMEM(given.shape, jnp.float32)
     return pl.pallas_call(
-        functools.partial(scores_kernel, distances, split),
-        out_shape=(shape,) * len(distances),
+        functools.partial(scores_kernel, distances, split, relay),
+        out_shape=(shape,) * (len(distances) + relay),
         in_specs=[VMEM] * (2 + len(pieces)),
-        out_specs=(VMEM,) * len(distances),
+        out_specs=(VMEM,) * (len(distances) + relay),
         compiler_params=limit(12),
         name="scores",
     )(kept(decoder), kept(given), *pieces)
@@ -453,11 +456,9 @@
     second_2 = stamp(second_2, (back, onward))
     second_3 = crossed(second_2)
     pairs = [(first_2[0], second_2[0]), (second_2[1], first_2[1])]
-    mine, others = scores_of((-2, 2), pairs, decoder, own_facts, True)
+    mine, others, relayed = scores_of((-2, 2), pairs, decoder, own_facts, True, True)
     total = gradients_of((-2, 2), pairs, own_facts, decoder.shape, total)
     second = mine + other_core(others)
-    relayed = [piece[-2 * KPB :].astype(jnp.float32) for piece in second_2]
-    relayed = jnp.where(lax.axis_index("width") == 0, relayed[1], relayed[0])
     total, first_3, second = lax.optimization_barrier((total, first_3, second))
     returned = return_by(2, jnp.concatenate([second, relayed, jnp.zeros((48, 128), jnp.float32)]))
     second, opposite_facts = returned[: 2 * KPB], returned[2 * KPB : 4 * KPB]

time: 60.6 us -> 59.5 us (0.982)
  waiting for transfers between devices: 12.3 us -> 24.1 us
  local copies, waits for them, and re-layouts: 5.28 us -> 0.08 us
  Pallas kernels: 16.6 us -> 12.7 us
  starting transfers between devices: 24.3 us -> 20.8 us
    ppermute x15, waiting for transfers between devices: 10.6 us -> 16.6 us  [shift(): return lax.ppermute(x, 'dp', pairs)]
    ppermute x2, waiting for transfers between devices: 0.5 us -> 6.12 us  [return_by(): return lax.ppermute(x, ('dp', 'width'), pairs)]
    unnamed x16 -> x0, local copies, waits for them, and re-layouts: 5.2 us -> none
    ppermute x2, starting transfers between devices: 5.86 us -> 1.99 us  [return_by(): return lax.ppermute(x, ('dp', 'width'), pairs)]
    pallas_call x4, Pallas kernels: 5.69 us -> 3.7 us  [scores_of(): pl.pallas_call(functools.partial(scores_kernel, distances, split, relay),...]
    pallas_call x3, Pallas kernels: 5.02 us -> 3.13 us  [gradients_of(): pl.pallas_call(functools.partial(gradients_kernel, distances), out_shape=...]
  transfers between devices with their start and end apart: 20 -> 20, of which waited for: 8 -> 11; matrix products, arithmetic and copies ran while one was open for 0% -> 0% of each run, Pallas kernels for 26% -> 19%
where the time goes in v11:
time: 59.5 us; the launch traced here: 59.2 us
  waiting for transfers between devices  24.1 us (41%)
  starting transfers between devices  20.8 us (35%)
  Pallas kernels  12.7 us (21%)
  between operations  0.81 us (1%)
  other arithmetic  0.69 us (1%)
    ppermute x15, starting transfers between devices, shift(): return lax.ppermute(x, 'dp', pairs)  18.6 us
    ppermute x15, waiting for transfers between devices, shift(): return lax.ppermute(x, 'dp', pairs)  16.6 us
    ppermute x2, waiting for transfers between devices, return_by(): return lax.ppermute(x, ('dp', 'width'), pairs)  6.12 us
    pallas_call x4, Pallas kernels, scores_of(): pl.pallas_call(functools.partial(scores_kernel, distances, split, relay),...  3.7 us
    pallas_call x3, Pallas kernels, gradients_of(): pl.pallas_call(functools.partial(gradients_kernel, distances), out_shape=...  3.13 us
    ppermute x2, starting transfers between devices, return_by(): return lax.ppermute(x, ('dp', 'width'), pairs)  1.99 us
    pallas_call x1, Pallas kernels, last_gradients(): pl.pallas_call(last_gradients_kernel, out_shape=jax.ShapeDtypeStruct(tota...  1.75 us
    pallas_call x1, Pallas kernels, fetch(): pl.pallas_call(fetch_kernel, out_shape=pltpu.VMEM(x.shape, x.dtype), in_s...  1.6 us
  transfers between devices with their start and end apart: 20, of which 11 were waited for; matrix products, arithmetic and copies ran while one was open for 0% of the time, Pallas kernels for 19%

profile of v11, /device:TPU:0, one launch (start us, length us, event | category | flops | bytes accessed | tf_op | source)
XLA Modules:
  0.0 59.2 jit_solution(7531514607307705077)
XLA Ops:
  0.6 1.2 %pieces.1 = (bf16[1024,128]{1,0:T(8,128)(2,1)S(1)}, bf16[1024,128]{1,0:T(8,128)(2,1)S(1)}) custom-call(bf16[128,2048]{1,0:T(8,128)(2,1)} %grad_out.1), custom_call_target="tpu_custom_call" | custom-call | tf_op jit(solution)/shard_map/pieces/pallas_call | solution.py:72
  1.8 3.1 %collective-permute-start = (bf16[1024,128]{1,0:T(8,128)(2,1)S(1)}, bf16[1024,128]{1,0:T(8,128)(2,1)S(1)}, u32[]{:S(2)}, u32[]{:S(2)}) collective-permute-start(bf16[1024,128]{1,0:T(8,128)(2,1)S(1)} %get-tuple-element.41.refs_0_), channel_id=1, source_target_pairs={{0,4},{4,8},{8,12},{12,14},{14,10},{10,6},{6,2},{2,0},{1,5},{5,9},... | collective-permute-start | bytes 786440 | tf_op jit(solution)/shard_map/ppermute | solution.py:421
  4.9 0.0 collective-permute-start.1
  4.9 1.2 %prepare.1 = (bf16[1056,128]{1,0:T(8,128)(2,1)S(1)}, bf16[1056,128]{1,0:T(8,128)(2,1)S(1)}, f32[8,128]{1,0:T(8,128)S(1)}, s32[8,128]{1,0:T(8,128)S(1)}) custom-call(s32[32]{0:T(128)} %refs_0_.1, s32[8,128]{1,0:T(8,128)} %bitcast.7, s32[32,128]{1,0:T(8,128)} %bitcast.5, bf16[32,128]{1,0:T(8,128)(2,1)} %bitcast.6, bf16[128,2048]{1,0:T(8,128)(2,1)} %grad_out.1), custom_call_target="tpu_custom_call" | custom-call | tf_op jit(solution)/shard_map/prepare/pallas_call | solution.py:142
  6.1 2.1 %collective-permute-start.3 = (bf16[1056,128]{1,0:T(8,128)(2,1)S(1)}, bf16[1056,128]{1,0:T(8,128)(2,1)S(1)}, u32[]{:S(2)}, u32[]{:S(2)}) collective-permute-start(bf16[1056,128]{1,0:T(8,128)(2,1)S(1)} %get-tuple-element.44), channel_id=1, source_target_pairs={{0,4},{4,8},{8,12},{12,14},{14,10},{10,6},{6,2},{2,0},{1,5},{5,9},... | collective-permute-start | bytes 811016 | tf_op jit(solution)/shard_map/ppermute | solution.py:421
  8.2 0.0 collective-permute-start.5
  8.2 1.6 %fetch.1.decoder = bf16[512,2048]{1,0:T(8,128)(2,1)S(1)} custom-call(bf16[512,2048]{1,0:T(8,128)(2,1)} %source.1), custom_call_target="tpu_custom_call" | custom-call | tf_op jit(solution)/shard_map/fetch/pallas_call | solution.py:168
  9.8 2.1 %collective-permute-done.refs_2_ = bf16[1024,128]{1,0:T(8,128)(2,1)S(1)} collective-permute-done((bf16[1024,128]{1,0:T(8,128)(2,1)S(1)}, bf16[1024,128]{1,0:T(8,128)(2,1)S(1)}, u32[]{:S(2)}, u32[]{:S(2)}) %collective-permute-start) | collective-permute-done | bytes 262176 | tf_op jit(solution)/shard_map/ppermute | solution.py:421
  11.9 2.2 %collective-permute-done.1.refs_5_ = bf16[1024,128]{1,0:T(8,128)(2,1)S(1)} collective-permute-done((bf16[1024,128]{1,0:T(8,128)(2,1)S(1)}, bf16[1024,128]{1,0:T(8,128)(2,1)S(1)}, u32[]{:S(2)}, u32[]{:S(2)}) %collective-permute-start.1) | collective-permute-done | bytes 262176 | tf_op jit(solution)/shard_map/ppermute | solution.py:421
  14.1 1.6 %collective-permute-start.2 = (bf16[1024,128]{1,0:T(8,128)(2,1)S(1)}, bf16[1024,128]{1,0:T(8,128)(2,1)S(1)}, u32[]{:S(2)}, u32[]{:S(2)}) collective-permute-start(bf16[1024,128]{1,0:T(8,128)(2,1)S(1)} %collective-permute-done.refs_2_), channel_id=1, source_target_pairs={{0,4},{4,8},{8,12},{12,14},{14,10},{10,6},{6,2},{2,0},{1,5},{5,9},... | collective-permute-start | bytes 786440 | tf_op jit(solution)/shard_map/ppermute | solution.py:421
  15.7 0.4 collective-permute-start.7
  16.1 1.6 %collective-permute-done.3.refs_3_ = bf16[1056,128]{1,0:T(8,128)(2,1)S(1)} collective-permute-done((bf16[1056,128]{1,0:T(8,128)(2,1)S(1)}, bf16[1056,128]{1,0:T(8,128)(2,1)S(1)}, u32[]{:S(2)}, u32[]{:S(2)}) %collective-permute-start.3) | collective-permute-done | bytes 270368 | tf_op jit(solution)/shard_map/ppermute | solution.py:421
  17.7 2.1 %collective-permute-start.4 = (bf16[1056,128]{1,0:T(8,128)(2,1)S(1)}, bf16[1056,128]{1,0:T(8,128)(2,1)S(1)}, u32[]{:S(2)}, u32[]{:S(2)}) collective-permute-start(bf16[1056,128]{1,0:T(8,128)(2,1)S(1)} %collective-permute-done.3.refs_3_), channel_id=1, source_target_pairs={{0,4},{4,8},{8,12},{12,14},{14,10},{10,6},{6,2},{2,0},{1,5},{5,9},... | collective-permute-start | bytes 811016 | tf_op jit(solution)/shard_map/ppermute | solution.py:421
  19.9 0.0 collective-permute-done.5.refs_4_
  19.9 0.0 collective-permute-start.6
  19.9 3.4 %collective-permute-done.2.refs_0_ = bf16[1024,128]{1,0:T(8,128)(2,1)S(1)} collective-permute-done((bf16[1024,128]{1,0:T(8,128)(2,1)S(1)}, bf16[1024,128]{1,0:T(8,128)(2,1)S(1)}, u32[]{:S(2)}, u32[]{:S(2)}) %collective-permute-start.2) | collective-permute-done | bytes 262176 | tf_op jit(solution)/shard_map/ppermute | solution.py:421
  23.3 2.1 %collective-permute-start.8 = (bf16[1024,128]{1,0:T(8,128)(2,1)S(1)}, bf16[1024,128]{1,0:T(8,128)(2,1)S(1)}, u32[]{:S(2)}, u32[]{:S(2)}) collective-permute-start(bf16[1024,128]{1,0:T(8,128)(2,1)S(1)} %collective-permute-done.2.refs_0_), channel_id=1, source_target_pairs={{0,4},{4,8},{8,12},{12,14},{14,10},{10,6},{6,2},{2,0},{1,5},{5,9},... | collective-permute-start | bytes 786440 | tf_op jit(solution)/shard_map/ppermute | solution.py:421
  25.5 0.0 collective-permute-done.7.refs_3_
  25.5 0.0 collective-permute-start.9
  25.5 1.3 %scores.4 = (f32[8,128]{1,0:T(8,128)S(1)}, f32[8,128]{1,0:T(8,128)S(1)}, f32[8,128]{1,0:T(8,128)S(1)}) custom-call(bf16[512,2048]{1,0:T(8,128)(2,1)S(1)} %fetch.1.decoder, f32[8,128]{1,0:T(8,128)S(1)} %get-tuple-element.40.given, bf16[1024,128]{1,0:T(8,128)(2,1)S(1)} %get-tuple-element.41.refs_0_, bf16[1024,128]{1,0:T(8,128)(2,1)S(1)} %get-tuple-element.42.refs_1_, ...), custom_call_target="tpu_custom_call" | custom-call | tf_op jit(solution)/shard_map/scores/pallas_call | solution.py:283
  26.9 2.2 %collective-permute-done.4.onward = bf16[1056,128]{1,0:T(8,128)(2,1)S(1)} collective-permute-done((bf16[1056,128]{1,0:T(8,128)(2,1)S(1)}, bf16[1056,128]{1,0:T(8,128)(2,1)S(1)}, u32[]{:S(2)}, u32[]{:S(2)}) %collective-permute-start.4) | collective-permute-done | bytes 270368 | tf_op jit(solution)/shard_map/ppermute | solution.py:421
  29.1 2.2 %collective-permute-done.6.back = bf16[1056,128]{1,0:T(8,128)(2,1)S(1)} collective-permute-done((bf16[1056,128]{1,0:T(8,128)(2,1)S(1)}, bf16[1056,128]{1,0:T(8,128)(2,1)S(1)}, u32[]{:S(2)}, u32[]{:S(2)}) %collective-permute-start.6) | collective-permute-done | bytes 270368 | tf_op jit(solution)/shard_map/ppermute | solution.py:421
  31.3 0.1 stamp.1
  31.4 0.8 %scores.5 = (f32[8,128]{1,0:T(8,128)S(1)}, f32[8,128]{1,0:T(8,128)S(1)}, f32[8,128]{1,0:T(8,128)S(1)}) custom-call(bf16[512,2048]{1,0:T(8,128)(2,1)S(1)} %fetch.1.decoder, f32[8,128]{1,0:T(8,128)S(1)} %get-tuple-element.40.given, bf16[1024,128]{1,0:T(8,128)(2,1)S(1)} %collective-permute-done.2.refs_0_, bf16[1056,128]{1,0:T(8,128)(2,1)S(1)} %get-tuple-element.50.refs_1_, ...), custom_call_target="tpu_custom_call" | custom-call | tf_op jit(solution)/shard_map/scores/pallas_call | solution.py:283
  32.2 0.1 collective-permute-start.10
  32.3 0.1 pad.2.clone
  32.4 1.3 %gradients.3.refs_4_ = f32[512,2048]{1,0:T(8,128)S(1)} custom-call(f32[8,128]{1,0:T(8,128)S(1)} %get-tuple-element.40.given, bf16[1024,128]{1,0:T(8,128)(2,1)S(1)} %get-tuple-element.41.refs_0_, bf16[1024,128]{1,0:T(8,128)(2,1)S(1)} %get-tuple-element.42.refs_1_, bf16[1024,128]{1,0:T(8,128)(2,1)S(1)} %collective-permute-done.refs_2_, ...), custom_call_target="tpu_custom_call" | custom-call | tf_op jit(solution)/shard_map/gradients/pallas_call | solution.py:304
  33.6 1.6 %collective-permute-start.12 = (bf16[1056,128]{1,0:T(8,128)(2,1)S(1)}, bf16[1056,128]{1,0:T(8,128)(2,1)S(1)}, u32[]{:S(2)}, u32[]{:S(2)}) collective-permute-start(bf16[1056,128]{1,0:T(8,128)(2,1)S(1)} %get-tuple-element.50.refs_1_), channel_id=1, source_target_pairs={{0,4},{4,8},{8,12},{12,14},{14,10},{10,6},{6,2},{2,0},{1,5},{5,9},... | collective-permute-start | bytes 811016 | tf_op jit(solution)/shard_map/ppermute | solution.py:421
  35.3 0.4 collective-permute-start.13
  35.7 0.9 %gradients.4.refs_4_ = f32[512,2048]{1,0:T(8,128)S(1)} custom-call(f32[8,128]{1,0:T(8,128)S(1)} %get-tuple-element.40.given, bf16[1024,128]{1,0:T(8,128)(2,1)S(1)} %collective-permute-done.2.refs_0_, bf16[1056,128]{1,0:T(8,128)(2,1)S(1)} %get-tuple-element.50.refs_1_, ...), custom_call_target="tpu_custom_call", output_to_operand_aliasing={{}: (5, {})} | custom-call | tf_op jit(solution)/shard_map/gradients/pallas_call | solution.py:304
  36.7 0.0 collective-permute-done.10
  36.7 0.0 collective-permute-done.8.refs_0_
  36.7 0.0 collective-permute-done.9.refs_3_
  36.7 0.1 maximum_maximum_fusion
  36.8 1.4 %collective-permute-start.11 = (f32[64,128]{1,0:T(8,128)S(1)}, f32[64,128]{1,0:T(8,128)S(1)}, u32[]{:S(2)}, u32[]{:S(2)}) collective-permute-start(f32[64,128]{1,0:T(8,128)S(1)} %maximum_maximum_fusion), channel_id=1, source_target_pairs={{0,6},{1,9},{4,2},{5,13},{8,0},{9,15},{12,4},{13,11},{14,8},{15,7}... | collective-permute-start | bytes 98312 | tf_op jit(solution)/shard_map/ppermute | solution.py:439
  38.1 0.3 collective-permute-start.15
  38.4 1.8 %collective-permute-start.16 = (bf16[1024,128]{1,0:T(8,128)(2,1)S(1)}, bf16[1024,128]{1,0:T(8,128)(2,1)S(1)}, u32[]{:S(2)}, u32[]{:S(2)}) collective-permute-start(bf16[1024,128]{1,0:T(8,128)(2,1)S(1)} %collective-permute-done.9.refs_3_), channel_id=1, source_target_pairs={{0,2},{4,0},{8,4},{12,8},{14,12},{10,14},{6,10},{2,6},{1,3},{5,1},... | collective-permute-start | bytes 786440 | tf_op jit(solution)/shard_map/ppermute | solution.py:421
  40.2 6.1 %collective-permute-done.11 = f32[64,128]{1,0:T(8,128)S(1)} collective-permute-done((f32[64,128]{1,0:T(8,128)S(1)}, f32[64,128]{1,0:T(8,128)S(1)}, u32[]{:S(2)}, u32[]{:S(2)}) %collective-permute-start.11) | collective-permute-done | bytes 32800 | tf_op jit(solution)/shard_map/ppermute | solution.py:439
  46.3 0.0 collective-permute-done.12.refs_1_.onward
  46.3 0.0 collective-permute-done.13.refs_2_.back
  46.3 0.8 %scores.6 = (f32[8,128]{1,0:T(8,128)S(1)}, f32[8,128]{1,0:T(8,128)S(1)}) custom-call(bf16[512,2048]{1,0:T(8,128)(2,1)S(1)} %fetch.1.decoder, f32[8,128]{1,0:T(8,128)S(1)} %get-tuple-element.40.given, bf16[1024,128]{1,0:T(8,128)(2,1)S(1)} %collective-permute-done.8.refs_0_, bf16[1056,128]{1,0:T(8,128)(2,1)S(1)} %collective-permute-done.12.refs_1_.onward, ...), custom_call_target="tpu_custom_call" | custom-call | tf_op jit(solution)/shard_map/scores/pallas_call | solution.py:283
  47.1 0.1 collective-permute-start.14
  47.2 0.9 %gradients.5.total = f32[512,2048]{1,0:T(8,128)S(1)} custom-call(f32[8,128]{1,0:T(8,128)S(1)} %get-tuple-element.40.given, bf16[1024,128]{1,0:T(8,128)(2,1)S(1)} %collective-permute-done.8.refs_0_, bf16[1056,128]{1,0:T(8,128)(2,1)S(1)} %collective-permute-done.12.refs_1_.onward, ...), custom_call_target="tpu_custom_call", output_to_operand_aliasing={{}: (5, {})} | custom-call | tf_op jit(solution)/shard_map/gradients/pallas_call | solution.py:304
  48.1 0.2 collective-permute-done.14
  48.4 0.6 %collective-permute-start.17 = (f32[8,128]{1,0:T(8,128)S(1)}, f32[8,128]{1,0:T(8,128)S(1)}, u32[]{:S(2)}, u32[]{:S(2)}) collective-permute-start(f32[8,128]{1,0:T(8,128)S(1)} %add.10), channel_id=1, source_target_pairs={{0,10},{1,13},{4,6},{5,15},{8,2},{9,11},{12,0},{13,7},{14,4},{15,3... | collective-permute-start | bytes 12296 | tf_op jit(solution)/shard_map/ppermute | solution.py:439
  49.0 0.0 collective-permute-done.15.left.refs_0_
  49.0 1.2 %collective-permute-done.16.right.refs_1_ = bf16[1024,128]{1,0:T(8,128)(2,1)S(1)} collective-permute-done((bf16[1024,128]{1,0:T(8,128)(2,1)S(1)}, bf16[1024,128]{1,0:T(8,128)(2,1)S(1)}, u32[]{:S(2)}, u32[]{:S(2)}) %collective-permute-start.16) | collective-permute-done | bytes 262176 | tf_op jit(solution)/shard_map/ppermute | solution.py:421
  50.2 0.7 %scores.7 = f32[8,128]{1,0:T(8,128)S(1)} custom-call(bf16[512,2048]{1,0:T(8,128)(2,1)S(1)} %fetch.1.decoder, f32[8,128]{1,0:T(8,128)S(1)} %get-tuple-element.57.given, bf16[1024,128]{1,0:T(8,128)(2,1)S(1)} %collective-permute-done.15.left.refs_0_, bf16[1024,128]{1,0:T(8,128)(2,1)S(1)} %collective-permute-done.16.right.refs_1_), custom_call_target="tpu_custom_call" | custom-call | tf_op jit(solution)/shard_map/scores/pallas_call | solution.py:283
  50.9 3.0 %collective-permute-start.18 = (f32[8,128]{1,0:T(8,128)S(1)}, f32[8,128]{1,0:T(8,128)S(1)}, u32[]{:S(2)}, u32[]{:S(2)}) collective-permute-start(f32[8,128]{1,0:T(8,128)S(1)} %scores.7), channel_id=1, source_target_pairs={{0,14},{4,10},{8,6},{12,2},{14,0},{10,4},{6,8},{2,12},{1,15},{5,11... | collective-permute-start | bytes 12296 | tf_op jit(solution)/shard_map/ppermute | solution.py:421
  53.9 0.0 collective-permute-done.17.third
  53.9 1.7 %last_gradients.1 = bf16[512,2048]{1,0:T(8,128)(2,1)} custom-call(f32[8,128]{1,0:T(8,128)S(1)} %get-tuple-element.57.given, bf16[1024,128]{1,0:T(8,128)(2,1)S(1)} %collective-permute-done.15.left.refs_0_, bf16[1024,128]{1,0:T(8,128)(2,1)S(1)} %collective-permute-done.16.right.refs_1_, f32[512,2048]{1,0:T(8,128)S(1)} %gradients.5.total), custom_call_target="tpu_custom_call" | custom-call | tf_op jit(solution)/shard_map/last_gradients/pallas_call | solution.py:330
  55.7 1.6 %collective-permute-done.18.opposite = f32[8,128]{1,0:T(8,128)S(1)} collective-permute-done((f32[8,128]{1,0:T(8,128)S(1)}, f32[8,128]{1,0:T(8,128)S(1)}, u32[]{:S(2)}, u32[]{:S(2)}) %collective-permute-start.18) | collective-permute-done | bytes 4128 | tf_op jit(solution)/shard_map/ppermute | solution.py:421
  57.3 0.1 collective-permute-start.19
  57.4 1.2 %collective-permute-done.19 = f32[32,128]{1,0:T(8,128)S(1)} collective-permute-done((f32[32,128]{1,0:T(8,128)S(1)}, f32[32,128]{1,0:T(8,128)S(1)}, u32[]{:S(2)}, u32[]{:S(2)}) %collective-permute-start.19) | collective-permute-done | bytes 16416 | tf_op jit(solution)/shard_map/ppermute | solution.py:432
  58.6 0.6 %add_bitcast_fusion = f32[128,32]{0,1:T(8,128)} fusion(f32[32,128]{1,0:T(8,128)S(1)} %unpack.1, f32[32,128]{1,0:T(8,128)S(1)} %collective-permute-done.19), kind=kLoop, calls=%fused_computation.1 | loop fusion | flops 4096 | bytes 49152 | tf_op jit(solution)/shard_map/transpose | solution.py:482
  (5 shorter events, 0.0 us)
Async XLA Ops:
  1.8 10.1 %collective-permute-start = (bf16[1024,128]{1,0:T(8,128)(2,1)S(1)}, bf16[1024,128]{1,0:T(8,128)(2,1)S(1)}, u32[]{:S(2)}, u32[]{:S(2)}) collective-permute-start(bf16[1024,128]{1,0:T(8,128)(2,1)S(1)} %get-tuple-element.41.refs_0_), channel_id=1, source_target_pairs={{0,4},{4,8},{8,12},{12,14},{14,10},{10,6},{6,2},{2,0},{1,5},{5,9},... | collective-permute-start | bytes 786440 | tf_op jit(solution)/shard_map/ppermute | solution.py:421
  4.9 9.2 %collective-permute-start.1 = (bf16[1024,128]{1,0:T(8,128)(2,1)S(1)}, bf16[1024,128]{1,0:T(8,128)(2,1)S(1)}, u32[]{:S(2)}, u32[]{:S(2)}) collective-permute-start(bf16[1024,128]{1,0:T(8,128)(2,1)S(1)} %get-tuple-element.42.refs_1_), channel_id=1, source_target_pairs={{0,2},{4,0},{8,4},{12,8},{14,12},{10,14},{6,10},{2,6},{1,3},{5,1},... | collective-permute-start | bytes 786440 | tf_op jit(solution)/shard_map/ppermute | solution.py:421
  6.1 11.6 %collective-permute-start.3 = (bf16[1056,128]{1,0:T(8,128)(2,1)S(1)}, bf16[1056,128]{1,0:T(8,128)(2,1)S(1)}, u32[]{:S(2)}, u32[]{:S(2)}) collective-permute-start(bf16[1056,128]{1,0:T(8,128)(2,1)S(1)} %get-tuple-element.44), channel_id=1, source_target_pairs={{0,4},{4,8},{8,12},{12,14},{14,10},{10,6},{6,2},{2,0},{1,5},{5,9},... | collective-permute-start | bytes 811016 | tf_op jit(solution)/shard_map/ppermute | solution.py:421
  8.2 11.7 %collective-permute-start.5 = (bf16[1056,128]{1,0:T(8,128)(2,1)S(1)}, bf16[1056,128]{1,0:T(8,128)(2,1)S(1)}, u32[]{:S(2)}, u32[]{:S(2)}) collective-permute-start(bf16[1056,128]{1,0:T(8,128)(2,1)S(1)} %get-tuple-element.45), channel_id=1, source_target_pairs={{0,2},{4,0},{8,4},{12,8},{14,12},{10,14},{6,10},{2,6},{1,3},{5,1},... | collective-permute-start | bytes 811016 | tf_op jit(solution)/shard_map/ppermute | solution.py:421
  14.1 9.2 %collective-permute-start.2 = (bf16[1024,128]{1,0:T(8,128)(2,1)S(1)}, bf16[1024,128]{1,0:T(8,128)(2,1)S(1)}, u32[]{:S(2)}, u32[]{:S(2)}) collective-permute-start(bf16[1024,128]{1,0:T(8,128)(2,1)S(1)} %collective-permute-done.refs_2_), channel_id=1, source_target_pairs={{0,4},{4,8},{8,12},{12,14},{14,10},{10,6},{6,2},{2,0},{1,5},{5,9},... | collective-permute-start | bytes 786440 | tf_op jit(solution)/shard_map/ppermute | solution.py:421
  15.7 9.8 %collective-permute-start.7 = (bf16[1024,128]{1,0:T(8,128)(2,1)S(1)}, bf16[1024,128]{1,0:T(8,128)(2,1)S(1)}, u32[]{:S(2)}, u32[]{:S(2)}) collective-permute-start(bf16[1024,128]{1,0:T(8,128)(2,1)S(1)} %collective-permute-done.1.refs_5_), channel_id=1, source_target_pairs={{0,2},{4,0},{8,4},{12,8},{14,12},{10,14},{6,10},{2,6},{1,3},{5,1},... | collective-permute-start | bytes 786440 | tf_op jit(solution)/shard_map/ppermute | solution.py:421
  17.7 11.4 %collective-permute-start.4 = (bf16[1056,128]{1,0:T(8,128)(2,1)S(1)}, bf16[1056,128]{1,0:T(8,128)(2,1)S(1)}, u32[]{:S(2)}, u32[]{:S(2)}) collective-permute-start(bf16[1056,128]{1,0:T(8,128)(2,1)S(1)} %collective-permute-done.3.refs_3_), channel_id=1, source_target_pairs={{0,4},{4,8},{8,12},{12,14},{14,10},{10,6},{6,2},{2,0},{1,5},{5,9},... | collective-permute-start | bytes 811016 | tf_op jit(solution)/shard_map/ppermute | solution.py:421
  19.9 11.4 %collective-permute-start.6 = (bf16[1056,128]{1,0:T(8,128)(2,1)S(1)}, bf16[1056,128]{1,0:T(8,128)(2,1)S(1)}, u32[]{:S(2)}, u32[]{:S(2)}) collective-permute-start(bf16[1056,128]{1,0:T(8,128)(2,1)S(1)} %collective-permute-done.5.refs_4_), channel_id=1, source_target_pairs={{0,2},{4,0},{8,4},{12,8},{14,12},{10,14},{6,10},{2,6},{1,3},{5,1},... | collective-permute-start | bytes 811016 | tf_op jit(solution)/shard_map/ppermute | solution.py:421
  23.3 13.4 %collective-permute-start.8 = (bf16[1024,128]{1,0:T(8,128)(2,1)S(1)}, bf16[1024,128]{1,0:T(8,128)(2,1)S(1)}, u32[]{:S(2)}, u32[]{:S(2)}) collective-permute-start(bf16[1024,128]{1,0:T(8,128)(2,1)S(1)} %collective-permute-done.2.refs_0_), channel_id=1, source_target_pairs={{0,4},{4,8},{8,12},{12,14},{14,10},{10,6},{6,2},{2,0},{1,5},{5,9},... | collective-permute-start | bytes 786440 | tf_op jit(solution)/shard_map/ppermute | solution.py:421
  25.5 11.2 %collective-permute-start.9 = (bf16[1024,128]{1,0:T(8,128)(2,1)S(1)}, bf16[1024,128]{1,0:T(8,128)(2,1)S(1)}, u32[]{:S(2)}, u32[]{:S(2)}) collective-permute-start(bf16[1024,128]{1,0:T(8,128)(2,1)S(1)} %collective-permute-done.7.refs_3_), channel_id=1, source_target_pairs={{0,2},{4,0},{8,4},{12,8},{14,12},{10,14},{6,10},{2,6},{1,3},{5,1},... | collective-permute-start | bytes 786440 | tf_op jit(solution)/shard_map/ppermute | solution.py:421
  32.2 4.5 %collective-permute-start.10 = (f32[8,128]{1,0:T(8,128)S(1)}, f32[8,128]{1,0:T(8,128)S(1)}, u32[]{:S(2)}, u32[]{:S(2)}) collective-permute-start(f32[8,128]{1,0:T(8,128)S(1)} %get-tuple-element.53), channel_id=1, source_target_pairs={{0,1},{1,0},{2,3},{3,2},{4,5},{5,4},{6,7},{7,6},{8,9},{9,8},{10,11... | collective-permute-start | bytes 12296 | tf_op jit(solution)/shard_map/ppermute | solution.py:432
  33.6 12.7 %collective-permute-start.12 = (bf16[1056,128]{1,0:T(8,128)(2,1)S(1)}, bf16[1056,128]{1,0:T(8,128)(2,1)S(1)}, u32[]{:S(2)}, u32[]{:S(2)}) collective-permute-start(bf16[1056,128]{1,0:T(8,128)(2,1)S(1)} %get-tuple-element.50.refs_1_), channel_id=1, source_target_pairs={{0,4},{4,8},{8,12},{12,14},{14,10},{10,6},{6,2},{2,0},{1,5},{5,9},... | collective-permute-start | bytes 811016 | tf_op jit(solution)/shard_map/ppermute | solution.py:421
  35.3 11.0 %collective-permute-start.13 = (bf16[1056,128]{1,0:T(8,128)(2,1)S(1)}, bf16[1056,128]{1,0:T(8,128)(2,1)S(1)}, u32[]{:S(2)}, u32[]{:S(2)}) collective-permute-start(bf16[1056,128]{1,0:T(8,128)(2,1)S(1)} %get-tuple-element.51.refs_2_), channel_id=1, source_target_pairs={{0,2},{4,0},{8,4},{12,8},{14,12},{10,14},{6,10},{2,6},{1,3},{5,1},... | collective-permute-start | bytes 811016 | tf_op jit(solution)/shard_map/ppermute | solution.py:421
  36.8 9.5 %collective-permute-start.11 = (f32[64,128]{1,0:T(8,128)S(1)}, f32[64,128]{1,0:T(8,128)S(1)}, u32[]{:S(2)}, u32[]{:S(2)}) collective-permute-start(f32[64,128]{1,0:T(8,128)S(1)} %maximum_maximum_fusion), channel_id=1, source_target_pairs={{0,6},{1,9},{4,2},{5,13},{8,0},{9,15},{12,4},{13,11},{14,8},{15,7}... | collective-permute-start | bytes 98312 | tf_op jit(solution)/shard_map/ppermute | solution.py:439
  38.1 10.8 %collective-permute-start.15 = (bf16[1024,128]{1,0:T(8,128)(2,1)S(1)}, bf16[1024,128]{1,0:T(8,128)(2,1)S(1)}, u32[]{:S(2)}, u32[]{:S(2)}) collective-permute-start(bf16[1024,128]{1,0:T(8,128)(2,1)S(1)} %collective-permute-done.8.refs_0_), channel_id=1, source_target_pairs={{0,4},{4,8},{8,12},{12,14},{14,10},{10,6},{6,2},{2,0},{1,5},{5,9},... | collective-permute-start | bytes 786440 | tf_op jit(solution)/shard_map/ppermute | solution.py:421
  38.4 11.8 %collective-permute-start.16 = (bf16[1024,128]{1,0:T(8,128)(2,1)S(1)}, bf16[1024,128]{1,0:T(8,128)(2,1)S(1)}, u32[]{:S(2)}, u32[]{:S(2)}) collective-permute-start(bf16[1024,128]{1,0:T(8,128)(2,1)S(1)} %collective-permute-done.9.refs_3_), channel_id=1, source_target_pairs={{0,2},{4,0},{8,4},{12,8},{14,12},{10,14},{6,10},{2,6},{1,3},{5,1},... | collective-permute-start | bytes 786440 | tf_op jit(solution)/shard_map/ppermute | solution.py:421
  47.1 1.2 %collective-permute-start.14 = (f32[8,128]{1,0:T(8,128)S(1)}, f32[8,128]{1,0:T(8,128)S(1)}, u32[]{:S(2)}, u32[]{:S(2)}) collective-permute-start(f32[8,128]{1,0:T(8,128)S(1)} %get-tuple-element.65), channel_id=1, source_target_pairs={{0,1},{1,0},{2,3},{3,2},{4,5},{5,4},{6,7},{7,6},{8,9},{9,8},{10,11... | collective-permute-start | bytes 12296 | tf_op jit(solution)/shard_map/ppermute | solution.py:432
  48.4 5.6 %collective-permute-start.17 = (f32[8,128]{1,0:T(8,128)S(1)}, f32[8,128]{1,0:T(8,128)S(1)}, u32[]{:S(2)}, u32[]{:S(2)}) collective-permute-start(f32[8,128]{1,0:T(8,128)S(1)} %add.10), channel_id=1, source_target_pairs={{0,10},{1,13},{4,6},{5,15},{8,2},{9,11},{12,0},{13,7},{14,4},{15,3... | collective-permute-start | bytes 12296 | tf_op jit(solution)/shard_map/ppermute | solution.py:439
  50.9 6.4 %collective-permute-start.18 = (f32[8,128]{1,0:T(8,128)S(1)}, f32[8,128]{1,0:T(8,128)S(1)}, u32[]{:S(2)}, u32[]{:S(2)}) collective-permute-start(f32[8,128]{1,0:T(8,128)S(1)} %scores.7), channel_id=1, source_target_pairs={{0,14},{4,10},{8,6},{12,2},{14,0},{10,4},{6,8},{2,12},{1,15},{5,11... | collective-permute-start | bytes 12296 | tf_op jit(solution)/shard_map/ppermute | solution.py:421
  57.3 1.2 %collective-permute-start.19 = (f32[32,128]{1,0:T(8,128)S(1)}, f32[32,128]{1,0:T(8,128)S(1)}, u32[]{:S(2)}, u32[]{:S(2)}) collective-permute-start(f32[32,128]{1,0:T(8,128)S(1)} %unpack.1), channel_id=1, source_target_pairs={{0,1},{1,0},{2,3},{3,2},{4,5},{5,4},{6,7},{7,6},{8,9},{9,8},{10,11... | collective-permute-start | bytes 49160 | tf_op jit(solution)/shard_map/ppermute | solution.py:432

commit v12 on v8

--- a/solution.py
+++ b/solution.py
@@ -43,6 +43,7 @@
 
 ROW_SHIFT = BLK_DEV * BW // 2
 FACTS = ACT // 2 * 2 * KPB
+LAST_FACTS = 16
 
 
 def facts_for(owner_id, owner, first_row, feats, acts):
@@ -57,32 +58,26 @@
     return jnp.concatenate(rows + values, axis=0)
 
 
-def prepare_kernel(
-    owners, *refs
-):
+def prepare_kernel(owners, *refs):
     sources, refs = refs[:5], refs[5:]
-    left, right, own_facts, slots = refs[:4]
-    block_slot, active, feats, acts, wide_feats, wide_acts, sems = refs[4:]
-    grad_out = sources[-1]
-    tok_rows, width = grad_out.shape
-    parts = width // 256
-    small = []
+    outs, refs = refs[:6], refs[6:]
+    first_left, first_right, left, right, own_facts, slots = outs
+    block_slot, active, feats, acts, halves, wide_feats, wide_acts, sems = refs
+    cut = halves.shape[2]
+    copies = []
     for source, target in zip(sources[:4], (block_slot, active, feats, acts)):
-        small.append(pltpu.make_async_copy(source, target, sems.at[len(small)]))
-        small[-1].start()
-    copies = []
-    for j in range(parts):
-        for target, side in ((left, 0), (right, 1)):
-            column = (side * parts + j) * 128
-            copies.append(
-                pltpu.make_async_copy(
-                    grad_out.at[:, column : column + 128],
-                    target.at[j * tok_rows : (j + 1) * tok_rows, :],
-                    sems.at[len(small) + len(copies)],
-                )
+        copies.append(pltpu.make_async_copy(source, target, sems.at[len(copies)]))
+    for side in range(2):
+        copies.append(
+            pltpu.make_async_copy(
+                sources[4].at[:, side * cut : (side + 1) * cut],
+                halves.at[side],
+                sems.at[len(copies)],
             )
-            copies[-1].start()
-    for copy in small:
+        )
+    for copy in copies:
+        copy.start()
+    for copy in copies[:4]:
         copy.wait()
     named = active[...]
     slot = jnp.zeros_like(named)
@@ -100,37 +95,53 @@
             peer_at(distance, owners), slot // BLK_DEV, first_row, features, values
         )
 
-    reach = owners // 2
+    def store_facts(target, blocks):
+        rows = jnp.concatenate(blocks, axis=0)
+        target[target.shape[0] - rows.shape[0] :, :] = rows.astype(jnp.bfloat16)
+
     own_facts[...] = facts(0)
-    start = parts * tok_rows
-    for target, sign in ((left, 1), (right, -1)):
-        ahead = [facts(sign * d) for d in range(1, reach + 1)]
-        target[start:, :] = jnp.concatenate(ahead, axis=0).astype(jnp.bfloat16)
-    for copy in copies:
-        copy.wait()
+    opposite = facts(owners // 2)
+    none = jnp.zeros_like(opposite)
+    store_facts(first_left, [opposite, none])
+    for target, sign in ((left, -1), (right, 1)):
+        store_facts(target, [facts(sign * d) for d in range(1, owners // 2)] + [none])
+    tok_rows = halves.shape[1]
+    for side, targets in ((0, (first_left, left)), (1, (first_right, right))):
+        copies[4 + side].wait()
+        for j in range(cut // 128):
+            part = halves[side, :, j * 128 : (j + 1) * 128]
+            for target in targets:
+                target[j * tok_rows : (j + 1) * tok_rows, :] = part
 
 
 def prepare(block_slot, active_blocks, feature_idx, acts, grad_out, owners):
-    tok_rows, half_width = grad_out.shape
-    plain = half_width // 256 * tok_rows
+    tok_rows, width = grad_out.shape
+    plain = width // 256 * tok_rows
+
+    def piece(extra):
+        return pltpu.VMEM((plain + extra, 128), grad_out.dtype)
+
     return pl.pallas_call(
         functools.partial(prepare_kernel, owners),
         out_shape=(
-            pltpu.VMEM((plain + FACTS, 128), grad_out.dtype),
-            pltpu.VMEM((plain + FACTS, 128), grad_out.dtype),
+            piece(LAST_FACTS),
+            piece(0),
+            piece(FACTS),
+            piece(FACTS),
             pltpu.VMEM((2 * KPB, tok_rows), jnp.float32),
             pltpu.VMEM((ACT, tok_rows), jnp.int32),
         ),
         in_specs=[HBM] * 5,
-        out_specs=(VMEM,) * 4,
+        out_specs=(VMEM,) * 6,
         scratch_shapes=[
             pltpu.SMEM(block_slot.shape, jnp.int32),
             pltpu.VMEM((ACT, tok_rows), jnp.int32),
             pltpu.VMEM((ACT * KPB, tok_rows), jnp.int32),
             pltpu.VMEM((ACT * KPB, tok_rows), acts.dtype),
+            pltpu.VMEM((2, tok_rows, width // 2), grad_out.dtype),
             pltpu.VMEM((ACT * KPB, tok_rows), jnp.float32),
             pltpu.VMEM((ACT * KPB, tok_rows), jnp.float32),
-            pltpu.SemaphoreType.DMA((4 + half_width // 128,)),
+            pltpu.SemaphoreType.DMA((6,)),
         ],
         compiler_params=limit(8),
         name="prepare",
@@ -235,12 +246,20 @@
             yield slice(side * cut + j * 128, side * cut + (j + 2) * 128), part
 
 
+def last_facts_in(piece):
+    return piece[piece.shape[0] - LAST_FACTS :, :].astype(jnp.float32)[: 2 * KPB]
+
+
 def facts_of(distances, own_facts, pieces):
-    tok_rows = own_facts.shape[1]
-    return [
-        own_facts[...] if d == 0 else facts_in(pieces[2 * i + (d > 0)], d, tok_rows)
-        for i, d in enumerate(distances)
-    ]
+    facts = []
+    for i, d in enumerate(distances):
+        if d == 0:
+            facts.append(own_facts[...])
+        elif d == 4:
+            facts.append(last_facts_in(pieces[2 * i]))
+        else:
+            facts.append(facts_in(pieces[2 * i + (d < 0)], d, own_facts.shape[1]))
+    return facts
 
 
 def scores_kernel(distances, split, decoder, own_facts, *refs):
@@ -248,7 +267,7 @@
     picks = picks_of(facts_of(distances, own_facts, pieces), decoder, pieces)
     if split:
         first = lax.axis_index("width") == 0
-        picks = jnp.where(first, *picks), jnp.where(first, *picks[::-1])
+        picks = [jnp.where(first, *picks), jnp.where(first, *picks[::-1])]
     for target, values in zip(picked, picks):
         target[...] = values
 
@@ -288,9 +307,9 @@
     )(*operands)
 
 
-def last_gradients_kernel(distance, tok_rows, left, right, total, out, rounded, sems):
-    facts = [facts_in(left, distance, tok_rows)]
+def last_gradients_kernel(left, right, total, out, rounded, sems):
     copies = []
+    facts = [last_facts_in(left)]
     for columns, part in gradient_blocks(facts, (left, right), out.shape[1]):
         rounded[:, columns] = (total[:, columns] + part).astype(out.dtype)
         copies.append(
@@ -303,9 +322,9 @@
         copy.wait()
 
 
-def last_gradients(distance, pair, total, tok_rows):
-    return pl.pallas_call(
-        functools.partial(last_gradients_kernel, distance, tok_rows),
+def last_gradients(pair, total):
+    return pl.pallas_call(
+        last_gradients_kernel,
         out_shape=jax.ShapeDtypeStruct(total.shape, jnp.bfloat16),
         in_specs=[VMEM] * 3,
         out_specs=ANY,
@@ -318,16 +337,16 @@
     )(kept(pair[0]), kept(pair[1]), kept(total))
 
 
-def stamp_kernel(left, right, for_left, for_right, left_out, right_out, rows, sems):
-    start = left.shape[0] - FACTS
-    targets = (left_out, right_out)
-    for i, piece in enumerate((left, right)):
+def stamp_kernel(onward, back, for_onward, for_back, onward_out, back_out, rows, sems):
+    start = onward.shape[0] - FACTS
+    targets = (onward_out, back_out)
+    for i, piece in enumerate((onward, back)):
         pltpu.make_async_copy(
             piece.at[start : start + 16, :], rows.at[i], sems.at[i]
         ).start()
-    for i, values in enumerate((for_left, for_right)):
+    for i, values in enumerate((for_onward, for_back)):
         pltpu.make_async_copy(
-            left.at[start : start + 16, :], rows.at[i], sems.at[i]
+            onward.at[start : start + 16, :], rows.at[i], sems.at[i]
         ).wait()
         value = values[:KPB]
         high = value.astype(jnp.bfloat16).astype(jnp.float32)
@@ -359,12 +378,12 @@
     )(*[kept(piece) for piece in pieces], *[kept(value) for value in values])
 
 
-def unpack_kernel(owners, slots, own, left, right, second, third, opposite, out):
+def unpack_kernel(owners, slots, own, onward, back, second, third, opposite, out):
     owner = slots[...] // BLK_DEV
-    start = left.shape[0] - FACTS
+    start = onward.shape[0] - FACTS
     way = 1 - 2 * lax.axis_index("width")
     returned = [(0, own[...])]
-    for distance, piece in ((-1, left), (1, right)):
+    for distance, piece in ((-1, onward), (1, back)):
         rows = piece[start : start + 16, :].astype(jnp.float32)
         returned.append((distance, rows[:KPB] + rows[KPB : 2 * KPB]))
     returned += [(2 * way, second[...]), (3 * way, third[...]), (4, opposite[...])]
@@ -415,21 +434,21 @@
             pairs.append((2 * ring[i] + 1, 2 * ring[(i + distance) % owners] + 1))
         return lax.ppermute(x, ("dp", "width"), pairs)
 
-    left, right, own_facts, slots = prepare(
+    first_left, first_right, left, right, own_facts, slots = prepare(
         block_slot, active_blocks, feature_idx, acts, grad_out, owners
     )
-    first_1 = hop((left, right))
+    first_1 = hop((first_left, first_right))
     second_1 = crossed((right, left))
     decoder = fetch(decoder)
     first_1, decoder = lax.optimization_barrier((first_1, decoder))
     first_2 = hop(first_1)
     second_2 = crossed(second_1)
-    pairs = [(left, right), (first_1[0], second_1[0]), (second_1[1], first_1[1])]
+    pairs = [(first_left, first_right), (first_1[0], second_1[0]), (second_1[1], first_1[1])]
     distances = (0, -1, 1)
     own, onward, back = scores_of(distances, pairs, decoder, own_facts)
     total = gradients_of(distances, pairs, own_facts, decoder.shape)
-    first_2 = stamp(first_2, (back, onward))
     first_3 = hop(first_2)
+    second_2 = stamp(second_2, (back, onward))
     second_3 = crossed(second_2)
     pairs = [(first_2[0], second_2[0]), (second_2[1], first_2[1])]
     mine, others = scores_of((-2, 2), pairs, decoder, own_facts, True)
@@ -446,11 +465,11 @@
     third = return_by(3, third)
     total, first_4 = lax.optimization_barrier((total, first_4))
     (opposite,) = scores_of((4,), [first_4], decoder, own_facts)
-    opposite = shift(opposite, -4)
+    opposite = shift(opposite, -owners // 2)
     total, third = lax.optimization_barrier((total, third))
-    decoder_grad = last_gradients(4, first_4, total, tok_rows)
+    decoder_grad = last_gradients(first_4, total)
     decoder_grad, opposite = lax.optimization_barrier((decoder_grad, opposite))
-    act_grad = unpack(slots, own, *first_3, second, third, opposite)
+    act_grad = unpack(slots, own, *second_3, second, third, opposite)
     act_grad = act_grad + other_core(act_grad)
     return (decoder_grad, act_grad.T)
 

time: 57 us -> 56.2 us (0.986)
  waiting for transfers between devices: 20.8 us -> 18.6 us
  starting transfers between devices: 23.2 us -> 24.5 us
    ppermute x15, waiting for transfers between devices: 19.4 us -> 17.3 us  [shift(): return lax.ppermute(x, 'dp', pairs)]
    ppermute x2, starting transfers between devices: 3.77 us -> 4.9 us  [return_by(): return lax.ppermute(x, ('dp', 'width'), pairs)]
  transfers between devices with their start and end apart: 20 -> 20, of which waited for: 13 -> 10; matrix products, arithmetic and copies ran while one was open for 0% -> 0% of each run, Pallas kernels for 18% -> 18%
where the time goes in v12:
time: 56.2 us; the launch traced here: 56 us
  starting transfers between devices  24.5 us (44%)
  waiting for transfers between devices  18.6 us (33%)
  Pallas kernels  11.5 us (20%)
  between operations  0.77 us (1%)
  other arithmetic  0.62 us (1%)
    ppermute x15, starting transfers between devices, shift(): return lax.ppermute(x, 'dp', pairs)  19.3 us
    ppermute x15, waiting for transfers between devices, shift(): return lax.ppermute(x, 'dp', pairs)  17.3 us
    ppermute x2, starting transfers between devices, return_by(): return lax.ppermute(x, ('dp', 'width'), pairs)  4.9 us
    pallas_call x4, Pallas kernels, scores_of(): pl.pallas_call(functools.partial(scores_kernel, distances, split), out_sh...  3.72 us
    pallas_call x3, Pallas kernels, gradients_of(): pl.pallas_call(functools.partial(gradients_kernel, distances), out_shape=...  3.14 us
    pallas_call x1, Pallas kernels, last_gradients(): pl.pallas_call(last_gradients_kernel, out_shape=jax.ShapeDtypeStruct(tota...  1.74 us
    pallas_call x1, Pallas kernels, fetch(): pl.pallas_call(fetch_kernel, out_shape=pltpu.VMEM(x.shape, x.dtype), in_s...  1.6 us
    ppermute x3, waiting for transfers between devices, other_core(): return lax.ppermute(x, 'width', ((0, 1), (1, 0)))  1.28 us
  transfers between devices with their start and end apart: 20, of which 10 were waited for; matrix products, arithmetic and copies ran while one was open for 0% of the time, Pallas kernels for 18%

profile of v12, /device:TPU:0, one launch (start us, length us, event | category | flops | bytes accessed | tf_op | source)
XLA Modules:
  0.0 56.0 jit_solution(17133198707252406874)
XLA Ops:
  0.6 1.2 %prepare.1 = (bf16[1040,128]{1,0:T(8,128)(2,1)S(1)}, bf16[1024,128]{1,0:T(8,128)(2,1)S(1)}, bf16[1056,128]{1,0:T(8,128)(2,1)S(1)}, bf16[1056,128]{1,0:T(8,128)(2...) custom-call(s32[32]{0:T(128)} %refs_0_.1, s32[8,128]{1,0:T(8,128)} %bitcast.7, s32[32,128]{1,0:T(8,128)} %bitcast.5, ...), custom_call_target="tpu_custom_call" | custom-call | tf_op jit(solution)/shard_map/prepare/pallas_call | solution.py:124
  1.8 3.1 %collective-permute-start = (bf16[1040,128]{1,0:T(8,128)(2,1)S(1)}, bf16[1040,128]{1,0:T(8,128)(2,1)S(1)}, u32[]{:S(2)}, u32[]{:S(2)}) collective-permute-start(bf16[1040,128]{1,0:T(8,128)(2,1)S(1)} %get-tuple-element.34.refs_0_), channel_id=1, source_target_pairs={{0,4},{4,8},{8,12},{12,14},{14,10},{10,6},{6,2},{2,0},{1,5},{5,9},... | collective-permute-start | bytes 798728 | tf_op jit(solution)/shard_map/ppermute | solution.py:417
  4.9 0.0 collective-permute-start.1
  4.9 2.0 %collective-permute-start.3 = (bf16[1056,128]{1,0:T(8,128)(2,1)S(1)}, bf16[1056,128]{1,0:T(8,128)(2,1)S(1)}, u32[]{:S(2)}, u32[]{:S(2)}) collective-permute-start(bf16[1056,128]{1,0:T(8,128)(2,1)S(1)} %get-tuple-element.37), channel_id=1, source_target_pairs={{0,4},{4,8},{8,12},{12,14},{14,10},{10,6},{6,2},{2,0},{1,5},{5,9},... | collective-permute-start | bytes 811016 | tf_op jit(solution)/shard_map/ppermute | solution.py:417
  6.9 0.0 collective-permute-start.5
  6.9 1.6 %fetch.1.decoder = bf16[512,2048]{1,0:T(8,128)(2,1)S(1)} custom-call(bf16[512,2048]{1,0:T(8,128)(2,1)} %source.1), custom_call_target="tpu_custom_call" | custom-call | tf_op jit(solution)/shard_map/fetch/pallas_call | solution.py:158
  8.6 5.6 %collective-permute-done.1.refs_5_ = bf16[1024,128]{1,0:T(8,128)(2,1)S(1)} collective-permute-done((bf16[1024,128]{1,0:T(8,128)(2,1)S(1)}, bf16[1024,128]{1,0:T(8,128)(2,1)S(1)}, u32[]{:S(2)}, u32[]{:S(2)}) %collective-permute-start.1) | collective-permute-done | bytes 262176 | tf_op jit(solution)/shard_map/ppermute | solution.py:417
  14.1 0.0 collective-permute-done.refs_2_
  14.2 1.6 %collective-permute-start.2 = (bf16[1040,128]{1,0:T(8,128)(2,1)S(1)}, bf16[1040,128]{1,0:T(8,128)(2,1)S(1)}, u32[]{:S(2)}, u32[]{:S(2)}) collective-permute-start(bf16[1040,128]{1,0:T(8,128)(2,1)S(1)} %collective-permute-done.refs_2_), channel_id=1, source_target_pairs={{0,4},{4,8},{8,12},{12,14},{14,10},{10,6},{6,2},{2,0},{1,5},{5,9},... | collective-permute-start | bytes 798728 | tf_op jit(solution)/shard_map/ppermute | solution.py:417
  15.7 0.4 collective-permute-start.7
  16.2 1.7 %collective-permute-done.3.refs_3_ = bf16[1056,128]{1,0:T(8,128)(2,1)S(1)} collective-permute-done((bf16[1056,128]{1,0:T(8,128)(2,1)S(1)}, bf16[1056,128]{1,0:T(8,128)(2,1)S(1)}, u32[]{:S(2)}, u32[]{:S(2)}) %collective-permute-start.3) | collective-permute-done | bytes 270368 | tf_op jit(solution)/shard_map/ppermute | solution.py:417
  17.8 2.1 %collective-permute-start.4 = (bf16[1056,128]{1,0:T(8,128)(2,1)S(1)}, bf16[1056,128]{1,0:T(8,128)(2,1)S(1)}, u32[]{:S(2)}, u32[]{:S(2)}) collective-permute-start(bf16[1056,128]{1,0:T(8,128)(2,1)S(1)} %collective-permute-done.3.refs_3_), channel_id=1, source_target_pairs={{0,4},{4,8},{8,12},{12,14},{14,10},{10,6},{6,2},{2,0},{1,5},{5,9},... | collective-permute-start | bytes 811016 | tf_op jit(solution)/shard_map/ppermute | solution.py:417
  20.0 0.0 collective-permute-done.5.refs_4_
  20.0 0.0 collective-permute-start.6
  20.0 3.6 %collective-permute-done.2.refs_0_ = bf16[1040,128]{1,0:T(8,128)(2,1)S(1)} collective-permute-done((bf16[1040,128]{1,0:T(8,128)(2,1)S(1)}, bf16[1040,128]{1,0:T(8,128)(2,1)S(1)}, u32[]{:S(2)}, u32[]{:S(2)}) %collective-permute-start.2) | collective-permute-done | bytes 266272 | tf_op jit(solution)/shard_map/ppermute | solution.py:417
  23.6 2.1 %collective-permute-start.8 = (bf16[1040,128]{1,0:T(8,128)(2,1)S(1)}, bf16[1040,128]{1,0:T(8,128)(2,1)S(1)}, u32[]{:S(2)}, u32[]{:S(2)}) collective-permute-start(bf16[1040,128]{1,0:T(8,128)(2,1)S(1)} %collective-permute-done.2.refs_0_), channel_id=1, source_target_pairs={{0,4},{4,8},{8,12},{12,14},{14,10},{10,6},{6,2},{2,0},{1,5},{5,9},... | collective-permute-start | bytes 798728 | tf_op jit(solution)/shard_map/ppermute | solution.py:417
  25.7 0.0 collective-permute-done.7.refs_3_
  25.7 0.0 collective-permute-start.9
  25.7 1.4 %scores.4 = (f32[8,128]{1,0:T(8,128)S(1)}, f32[8,128]{1,0:T(8,128)S(1)}, f32[8,128]{1,0:T(8,128)S(1)}) custom-call(bf16[512,2048]{1,0:T(8,128)(2,1)S(1)} %fetch.1.decoder, f32[8,128]{1,0:T(8,128)S(1)} %get-tuple-element.33.own_facts, bf16[1040,128]{1,0:T(8,128)(2,1)S(1)} %get-tuple-element.34.refs_0_, bf16[1024,128]{1,0:T(8,128)(2,1)S(1)} %get-tuple-element.35.refs_1_, ...), custom_call_target="tpu_custom_call" | custom-call | tf_op jit(solution)/shard_map/scores/pallas_call | solution.py:278
  27.1 2.3 %collective-permute-done.4.onward = bf16[1056,128]{1,0:T(8,128)(2,1)S(1)} collective-permute-done((bf16[1056,128]{1,0:T(8,128)(2,1)S(1)}, bf16[1056,128]{1,0:T(8,128)(2,1)S(1)}, u32[]{:S(2)}, u32[]{:S(2)}) %collective-permute-start.4) | collective-permute-done | bytes 270368 | tf_op jit(solution)/shard_map/ppermute | solution.py:417
  29.3 2.0 %collective-permute-done.6.back = bf16[1056,128]{1,0:T(8,128)(2,1)S(1)} collective-permute-done((bf16[1056,128]{1,0:T(8,128)(2,1)S(1)}, bf16[1056,128]{1,0:T(8,128)(2,1)S(1)}, u32[]{:S(2)}, u32[]{:S(2)}) %collective-permute-start.6) | collective-permute-done | bytes 270368 | tf_op jit(solution)/shard_map/ppermute | solution.py:417
  31.4 0.1 stamp.1
  31.4 1.6 %collective-permute-start.11 = (bf16[1056,128]{1,0:T(8,128)(2,1)S(1)}, bf16[1056,128]{1,0:T(8,128)(2,1)S(1)}, u32[]{:S(2)}, u32[]{:S(2)}) collective-permute-start(bf16[1056,128]{1,0:T(8,128)(2,1)S(1)} %get-tuple-element.43.refs_1_), channel_id=1, source_target_pairs={{0,4},{4,8},{8,12},{12,14},{14,10},{10,6},{6,2},{2,0},{1,5},{5,9},... | collective-permute-start | bytes 811016 | tf_op jit(solution)/shard_map/ppermute | solution.py:417
  33.1 0.4 collective-permute-start.12
  33.5 0.8 %scores.5 = (f32[8,128]{1,0:T(8,128)S(1)}, f32[8,128]{1,0:T(8,128)S(1)}) custom-call(bf16[512,2048]{1,0:T(8,128)(2,1)S(1)} %fetch.1.decoder, f32[8,128]{1,0:T(8,128)S(1)} %get-tuple-element.33.own_facts, bf16[1040,128]{1,0:T(8,128)(2,1)S(1)} %collective-permute-done.2.refs_0_, bf16[1056,128]{1,0:T(8,128)(2,1)S(1)} %get-tuple-element.43.refs_1_, ...), custom_call_target="tpu_custom_call" | custom-call | tf_op jit(solution)/shard_map/scores/pallas_call | solution.py:278
  34.3 0.1 collective-permute-start.10
  34.4 1.3 %gradients.3.refs_4_ = f32[512,2048]{1,0:T(8,128)S(1)} custom-call(f32[8,128]{1,0:T(8,128)S(1)} %get-tuple-element.33.own_facts, bf16[1040,128]{1,0:T(8,128)(2,1)S(1)} %get-tuple-element.34.refs_0_, bf16[1024,128]{1,0:T(8,128)(2,1)S(1)} %get-tuple-element.35.refs_1_, bf16[1040,128]{1,0:T(8,128)(2,1)S(1)} %collective-permute-done.refs_2_, ...), custom_call_target="tpu_custom_call" | custom-call | tf_op jit(solution)/shard_map/gradients/pallas_call | solution.py:299
  35.7 0.9 %gradients.4.refs_4_ = f32[512,2048]{1,0:T(8,128)S(1)} custom-call(f32[8,128]{1,0:T(8,128)S(1)} %get-tuple-element.33.own_facts, bf16[1040,128]{1,0:T(8,128)(2,1)S(1)} %collective-permute-done.2.refs_0_, bf16[1056,128]{1,0:T(8,128)(2,1)S(1)} %get-tuple-element.43.refs_1_, ...), custom_call_target="tpu_custom_call", output_to_operand_aliasing={{}: (5, {})} | custom-call | tf_op jit(solution)/shard_map/gradients/pallas_call | solution.py:299
  36.6 0.0 collective-permute-done.10
  36.7 0.3 collective-permute-done.9.refs_3_
  37.0 0.0 collective-permute-done.8.refs_0_
  37.0 1.6 %collective-permute-start.14 = (bf16[1040,128]{1,0:T(8,128)(2,1)S(1)}, bf16[1040,128]{1,0:T(8,128)(2,1)S(1)}, u32[]{:S(2)}, u32[]{:S(2)}) collective-permute-start(bf16[1040,128]{1,0:T(8,128)(2,1)S(1)} %collective-permute-done.8.refs_0_), channel_id=1, source_target_pairs={{0,4},{4,8},{8,12},{12,14},{14,10},{10,6},{6,2},{2,0},{1,5},{5,9},... | collective-permute-start | bytes 798728 | tf_op jit(solution)/shard_map/ppermute | solution.py:417
  38.6 0.4 collective-permute-start.15
  39.0 1.4 %collective-permute-start.18 = (f32[32,128]{1,0:T(8,128)S(1)}, f32[32,128]{1,0:T(8,128)S(1)}, u32[]{:S(2)}, u32[]{:S(2)}) collective-permute-start(f32[32,128]{1,0:T(8,128)S(1)} %concatenate.3), channel_id=1, source_target_pairs={{0,6},{1,9},{4,2},{5,13},{8,0},{9,15},{12,4},{13,11},{14,8},{15,7}... | collective-permute-start | bytes 49160 | tf_op jit(solution)/shard_map/ppermute | solution.py:435
  40.4 0.0 collective-permute-done.11.refs_1_.onward
  40.4 1.0 %collective-permute-done.12.refs_2_.back = bf16[1056,128]{1,0:T(8,128)(2,1)S(1)} collective-permute-done((bf16[1056,128]{1,0:T(8,128)(2,1)S(1)}, bf16[1056,128]{1,0:T(8,128)(2,1)S(1)}, u32[]{:S(2)}, u32[]{:S(2)}) %collective-permute-start.12) | collective-permute-done | bytes 270368 | tf_op jit(solution)/shard_map/ppermute | solution.py:417
  41.4 0.8 %scores.6 = (f32[8,128]{1,0:T(8,128)S(1)}, f32[8,128]{1,0:T(8,128)S(1)}) custom-call(bf16[512,2048]{1,0:T(8,128)(2,1)S(1)} %fetch.1.decoder, f32[8,128]{1,0:T(8,128)S(1)} %get-tuple-element.33.own_facts, bf16[1040,128]{1,0:T(8,128)(2,1)S(1)} %collective-permute-done.8.refs_0_, bf16[1056,128]{1,0:T(8,128)(2,1)S(1)} %collective-permute-done.11.refs_1_.onward, ...), custom_call_target="tpu_custom_call" | custom-call | tf_op jit(solution)/shard_map/scores/pallas_call | solution.py:278
  42.2 0.1 collective-permute-start.13
  42.3 0.9 %gradients.5.total = f32[512,2048]{1,0:T(8,128)S(1)} custom-call(f32[8,128]{1,0:T(8,128)S(1)} %get-tuple-element.33.own_facts, bf16[1040,128]{1,0:T(8,128)(2,1)S(1)} %collective-permute-done.8.refs_0_, bf16[1056,128]{1,0:T(8,128)(2,1)S(1)} %collective-permute-done.11.refs_1_.onward, ...), custom_call_target="tpu_custom_call", output_to_operand_aliasing={{}: (5, {})} | custom-call | tf_op jit(solution)/shard_map/gradients/pallas_call | solution.py:299
  43.3 0.2 collective-permute-done.13
  43.5 3.5 %collective-permute-start.16 = (f32[8,128]{1,0:T(8,128)S(1)}, f32[8,128]{1,0:T(8,128)S(1)}, u32[]{:S(2)}, u32[]{:S(2)}) collective-permute-start(f32[8,128]{1,0:T(8,128)S(1)} %add.12), channel_id=1, source_target_pairs={{0,10},{1,13},{4,6},{5,15},{8,2},{9,11},{12,0},{13,7},{14,4},{15,3... | collective-permute-start | bytes 12296 | tf_op jit(solution)/shard_map/ppermute | solution.py:435
  47.0 0.0 collective-permute-done.15.right.refs_1_
  47.0 0.0 collective-permute-done.14.left.refs_0_
  47.0 0.7 %scores.7 = f32[8,128]{1,0:T(8,128)S(1)} custom-call(bf16[512,2048]{1,0:T(8,128)(2,1)S(1)} %fetch.1.decoder, f32[8,128]{1,0:T(8,128)S(1)} %get-tuple-element.33.own_facts, bf16[1040,128]{1,0:T(8,128)(2,1)S(1)} %collective-permute-done.14.left.refs_0_, bf16[1024,128]{1,0:T(8,128)(2,1)S(1)} %collective-permute-done.15.right.refs_1_), custom_call_target="tpu_custom_call" | custom-call | tf_op jit(solution)/shard_map/scores/pallas_call | solution.py:278
  47.7 3.7 %collective-permute-start.17 = (f32[8,128]{1,0:T(8,128)S(1)}, f32[8,128]{1,0:T(8,128)S(1)}, u32[]{:S(2)}, u32[]{:S(2)}) collective-permute-start(f32[8,128]{1,0:T(8,128)S(1)} %scores.7), channel_id=1, source_target_pairs={{0,14},{4,10},{8,6},{12,2},{14,0},{10,4},{6,8},{2,12},{1,15},{5,11... | collective-permute-start | bytes 12296 | tf_op jit(solution)/shard_map/ppermute | solution.py:417
  51.5 0.0 collective-permute-done.18
  51.5 0.0 collective-permute-done.16.third
  51.5 1.7 %last_gradients.1 = bf16[512,2048]{1,0:T(8,128)(2,1)} custom-call(bf16[1040,128]{1,0:T(8,128)(2,1)S(1)} %collective-permute-done.14.left.refs_0_, bf16[1024,128]{1,0:T(8,128)(2,1)S(1)} %collective-permute-done.15.right.refs_1_, f32[512,2048]{1,0:T(8,128)S(1)} %gradients.5.total), custom_call_target="tpu_custom_call" | custom-call | tf_op jit(solution)/shard_map/last_gradients/pallas_call | solution.py:326
  53.2 0.9 %collective-permute-done.17.opposite = f32[8,128]{1,0:T(8,128)S(1)} collective-permute-done((f32[8,128]{1,0:T(8,128)S(1)}, f32[8,128]{1,0:T(8,128)S(1)}, u32[]{:S(2)}, u32[]{:S(2)}) %collective-permute-start.17) | collective-permute-done | bytes 4128 | tf_op jit(solution)/shard_map/ppermute | solution.py:417
  54.1 0.2 collective-permute-start.19
  54.3 1.1 %collective-permute-done.19 = f32[32,128]{1,0:T(8,128)S(1)} collective-permute-done((f32[32,128]{1,0:T(8,128)S(1)}, f32[32,128]{1,0:T(8,128)S(1)}, u32[]{:S(2)}, u32[]{:S(2)}) %collective-permute-start.19) | collective-permute-done | bytes 16416 | tf_op jit(solution)/shard_map/ppermute | solution.py:428
  55.4 0.6 %add_bitcast_fusion = f32[128,32]{0,1:T(8,128)} fusion(f32[32,128]{1,0:T(8,128)S(1)} %unpack.1, f32[32,128]{1,0:T(8,128)S(1)} %collective-permute-done.19), kind=kLoop, calls=%fused_computation | loop fusion | flops 4096 | bytes 49152 | tf_op jit(solution)/shard_map/transpose | solution.py:474
  (5 shorter events, 0.0 us)
Async XLA Ops:
  1.8 12.3 %collective-permute-start = (bf16[1040,128]{1,0:T(8,128)(2,1)S(1)}, bf16[1040,128]{1,0:T(8,128)(2,1)S(1)}, u32[]{:S(2)}, u32[]{:S(2)}) collective-permute-start(bf16[1040,128]{1,0:T(8,128)(2,1)S(1)} %get-tuple-element.34.refs_0_), channel_id=1, source_target_pairs={{0,4},{4,8},{8,12},{12,14},{14,10},{10,6},{6,2},{2,0},{1,5},{5,9},... | collective-permute-start | bytes 798728 | tf_op jit(solution)/shard_map/ppermute | solution.py:417
  4.9 9.2 %collective-permute-start.1 = (bf16[1024,128]{1,0:T(8,128)(2,1)S(1)}, bf16[1024,128]{1,0:T(8,128)(2,1)S(1)}, u32[]{:S(2)}, u32[]{:S(2)}) collective-permute-start(bf16[1024,128]{1,0:T(8,128)(2,1)S(1)} %get-tuple-element.35.refs_1_), channel_id=1, source_target_pairs={{0,2},{4,0},{8,4},{12,8},{14,12},{10,14},{6,10},{2,6},{1,3},{5,1},... | collective-permute-start | bytes 786440 | tf_op jit(solution)/shard_map/ppermute | solution.py:417
  4.9 12.9 %collective-permute-start.3 = (bf16[1056,128]{1,0:T(8,128)(2,1)S(1)}, bf16[1056,128]{1,0:T(8,128)(2,1)S(1)}, u32[]{:S(2)}, u32[]{:S(2)}) collective-permute-start(bf16[1056,128]{1,0:T(8,128)(2,1)S(1)} %get-tuple-element.37), channel_id=1, source_target_pairs={{0,4},{4,8},{8,12},{12,14},{14,10},{10,6},{6,2},{2,0},{1,5},{5,9},... | collective-permute-start | bytes 811016 | tf_op jit(solution)/shard_map/ppermute | solution.py:417
  6.9 13.1 %collective-permute-start.5 = (bf16[1056,128]{1,0:T(8,128)(2,1)S(1)}, bf16[1056,128]{1,0:T(8,128)(2,1)S(1)}, u32[]{:S(2)}, u32[]{:S(2)}) collective-permute-start(bf16[1056,128]{1,0:T(8,128)(2,1)S(1)} %get-tuple-element.38), channel_id=1, source_target_pairs={{0,2},{4,0},{8,4},{12,8},{14,12},{10,14},{6,10},{2,6},{1,3},{5,1},... | collective-permute-start | bytes 811016 | tf_op jit(solution)/shard_map/ppermute | solution.py:417
  14.2 9.4 %collective-permute-start.2 = (bf16[1040,128]{1,0:T(8,128)(2,1)S(1)}, bf16[1040,128]{1,0:T(8,128)(2,1)S(1)}, u32[]{:S(2)}, u32[]{:S(2)}) collective-permute-start(bf16[1040,128]{1,0:T(8,128)(2,1)S(1)} %collective-permute-done.refs_2_), channel_id=1, source_target_pairs={{0,4},{4,8},{8,12},{12,14},{14,10},{10,6},{6,2},{2,0},{1,5},{5,9},... | collective-permute-start | bytes 798728 | tf_op jit(solution)/shard_map/ppermute | solution.py:417
  15.7 10.0 %collective-permute-start.7 = (bf16[1024,128]{1,0:T(8,128)(2,1)S(1)}, bf16[1024,128]{1,0:T(8,128)(2,1)S(1)}, u32[]{:S(2)}, u32[]{:S(2)}) collective-permute-start(bf16[1024,128]{1,0:T(8,128)(2,1)S(1)} %collective-permute-done.1.refs_5_), channel_id=1, source_target_pairs={{0,2},{4,0},{8,4},{12,8},{14,12},{10,14},{6,10},{2,6},{1,3},{5,1},... | collective-permute-start | bytes 786440 | tf_op jit(solution)/shard_map/ppermute | solution.py:417
  17.8 11.5 %collective-permute-start.4 = (bf16[1056,128]{1,0:T(8,128)(2,1)S(1)}, bf16[1056,128]{1,0:T(8,128)(2,1)S(1)}, u32[]{:S(2)}, u32[]{:S(2)}) collective-permute-start(bf16[1056,128]{1,0:T(8,128)(2,1)S(1)} %collective-permute-done.3.refs_3_), channel_id=1, source_target_pairs={{0,4},{4,8},{8,12},{12,14},{14,10},{10,6},{6,2},{2,0},{1,5},{5,9},... | collective-permute-start | bytes 811016 | tf_op jit(solution)/shard_map/ppermute | solution.py:417
  20.0 11.4 %collective-permute-start.6 = (bf16[1056,128]{1,0:T(8,128)(2,1)S(1)}, bf16[1056,128]{1,0:T(8,128)(2,1)S(1)}, u32[]{:S(2)}, u32[]{:S(2)}) collective-permute-start(bf16[1056,128]{1,0:T(8,128)(2,1)S(1)} %collective-permute-done.5.refs_4_), channel_id=1, source_target_pairs={{0,2},{4,0},{8,4},{12,8},{14,12},{10,14},{6,10},{2,6},{1,3},{5,1},... | collective-permute-start | bytes 811016 | tf_op jit(solution)/shard_map/ppermute | solution.py:417
  23.6 13.4 %collective-permute-start.8 = (bf16[1040,128]{1,0:T(8,128)(2,1)S(1)}, bf16[1040,128]{1,0:T(8,128)(2,1)S(1)}, u32[]{:S(2)}, u32[]{:S(2)}) collective-permute-start(bf16[1040,128]{1,0:T(8,128)(2,1)S(1)} %collective-permute-done.2.refs_0_), channel_id=1, source_target_pairs={{0,4},{4,8},{8,12},{12,14},{14,10},{10,6},{6,2},{2,0},{1,5},{5,9},... | collective-permute-start | bytes 798728 | tf_op jit(solution)/shard_map/ppermute | solution.py:417
  25.7 11.3 %collective-permute-start.9 = (bf16[1024,128]{1,0:T(8,128)(2,1)S(1)}, bf16[1024,128]{1,0:T(8,128)(2,1)S(1)}, u32[]{:S(2)}, u32[]{:S(2)}) collective-permute-start(bf16[1024,128]{1,0:T(8,128)(2,1)S(1)} %collective-permute-done.7.refs_3_), channel_id=1, source_target_pairs={{0,2},{4,0},{8,4},{12,8},{14,12},{10,14},{6,10},{2,6},{1,3},{5,1},... | collective-permute-start | bytes 786440 | tf_op jit(solution)/shard_map/ppermute | solution.py:417
  31.4 9.0 %collective-permute-start.11 = (bf16[1056,128]{1,0:T(8,128)(2,1)S(1)}, bf16[1056,128]{1,0:T(8,128)(2,1)S(1)}, u32[]{:S(2)}, u32[]{:S(2)}) collective-permute-start(bf16[1056,128]{1,0:T(8,128)(2,1)S(1)} %get-tuple-element.43.refs_1_), channel_id=1, source_target_pairs={{0,4},{4,8},{8,12},{12,14},{14,10},{10,6},{6,2},{2,0},{1,5},{5,9},... | collective-permute-start | bytes 811016 | tf_op jit(solution)/shard_map/ppermute | solution.py:417
  33.1 8.3 %collective-permute-start.12 = (bf16[1056,128]{1,0:T(8,128)(2,1)S(1)}, bf16[1056,128]{1,0:T(8,128)(2,1)S(1)}, u32[]{:S(2)}, u32[]{:S(2)}) collective-permute-start(bf16[1056,128]{1,0:T(8,128)(2,1)S(1)} %get-tuple-element.44.refs_2_), channel_id=1, source_target_pairs={{0,2},{4,0},{8,4},{12,8},{14,12},{10,14},{6,10},{2,6},{1,3},{5,1},... | collective-permute-start | bytes 811016 | tf_op jit(solution)/shard_map/ppermute | solution.py:417
  34.3 2.3 %collective-permute-start.10 = (f32[8,128]{1,0:T(8,128)S(1)}, f32[8,128]{1,0:T(8,128)S(1)}, u32[]{:S(2)}, u32[]{:S(2)}) collective-permute-start(f32[8,128]{1,0:T(8,128)S(1)} %get-tuple-element.46), channel_id=1, source_target_pairs={{0,1},{1,0},{2,3},{3,2},{4,5},{5,4},{6,7},{7,6},{8,9},{9,8},{10,11... | collective-permute-start | bytes 12296 | tf_op jit(solution)/shard_map/ppermute | solution.py:428
  37.0 10.0 %collective-permute-start.14 = (bf16[1040,128]{1,0:T(8,128)(2,1)S(1)}, bf16[1040,128]{1,0:T(8,128)(2,1)S(1)}, u32[]{:S(2)}, u32[]{:S(2)}) collective-permute-start(bf16[1040,128]{1,0:T(8,128)(2,1)S(1)} %collective-permute-done.8.refs_0_), channel_id=1, source_target_pairs={{0,4},{4,8},{8,12},{12,14},{14,10},{10,6},{6,2},{2,0},{1,5},{5,9},... | collective-permute-start | bytes 798728 | tf_op jit(solution)/shard_map/ppermute | solution.py:417
  38.6 8.5 %collective-permute-start.15 = (bf16[1024,128]{1,0:T(8,128)(2,1)S(1)}, bf16[1024,128]{1,0:T(8,128)(2,1)S(1)}, u32[]{:S(2)}, u32[]{:S(2)}) collective-permute-start(bf16[1024,128]{1,0:T(8,128)(2,1)S(1)} %collective-permute-done.9.refs_3_), channel_id=1, source_target_pairs={{0,2},{4,0},{8,4},{12,8},{14,12},{10,14},{6,10},{2,6},{1,3},{5,1},... | collective-permute-start | bytes 786440 | tf_op jit(solution)/shard_map/ppermute | solution.py:417
  39.0 12.5 %collective-permute-start.18 = (f32[32,128]{1,0:T(8,128)S(1)}, f32[32,128]{1,0:T(8,128)S(1)}, u32[]{:S(2)}, u32[]{:S(2)}) collective-permute-start(f32[32,128]{1,0:T(8,128)S(1)} %concatenate.3), channel_id=1, source_target_pairs={{0,6},{1,9},{4,2},{5,13},{8,0},{9,15},{12,4},{13,11},{14,8},{15,7}... | collective-permute-start | bytes 49160 | tf_op jit(solution)/shard_map/ppermute | solution.py:435
  42.2 1.2 %collective-permute-start.13 = (f32[8,128]{1,0:T(8,128)S(1)}, f32[8,128]{1,0:T(8,128)S(1)}, u32[]{:S(2)}, u32[]{:S(2)}) collective-permute-start(f32[8,128]{1,0:T(8,128)S(1)} %get-tuple-element.51), channel_id=1, source_target_pairs={{0,1},{1,0},{2,3},{3,2},{4,5},{5,4},{6,7},{7,6},{8,9},{9,8},{10,11... | collective-permute-start | bytes 12296 | tf_op jit(solution)/shard_map/ppermute | solution.py:428
  43.5 8.0 %collective-permute-start.16 = (f32[8,128]{1,0:T(8,128)S(1)}, f32[8,128]{1,0:T(8,128)S(1)}, u32[]{:S(2)}, u32[]{:S(2)}) collective-permute-start(f32[8,128]{1,0:T(8,128)S(1)} %add.12), channel_id=1, source_target_pairs={{0,10},{1,13},{4,6},{5,15},{8,2},{9,11},{12,0},{13,7},{14,4},{15,3... | collective-permute-start | bytes 12296 | tf_op jit(solution)/shard_map/ppermute | solution.py:435
  47.7 6.4 %collective-permute-start.17 = (f32[8,128]{1,0:T(8,128)S(1)}, f32[8,128]{1,0:T(8,128)S(1)}, u32[]{:S(2)}, u32[]{:S(2)}) collective-permute-start(f32[8,128]{1,0:T(8,128)S(1)} %scores.7), channel_id=1, source_target_pairs={{0,14},{4,10},{8,6},{12,2},{14,0},{10,4},{6,8},{2,12},{1,15},{5,11... | collective-permute-start | bytes 12296 | tf_op jit(solution)/shard_map/ppermute | solution.py:417
  54.1 1.2 %collective-permute-start.19 = (f32[32,128]{1,0:T(8,128)S(1)}, f32[32,128]{1,0:T(8,128)S(1)}, u32[]{:S(2)}, u32[]{:S(2)}) collective-permute-start(f32[32,128]{1,0:T(8,128)S(1)} %unpack.1), channel_id=1, source_target_pairs={{0,1},{1,0},{2,3},{3,2},{4,5},{5,4},{6,7},{7,6},{8,9},{9,8},{10,11... | collective-permute-start | bytes 49160 | tf_op jit(solution)/shard_map/ppermute | solution.py:428

commit v13 on v12

--- a/solution.py
+++ b/solution.py
@@ -42,8 +42,7 @@
 
 
 ROW_SHIFT = BLK_DEV * BW // 2
-FACTS = ACT // 2 * 2 * KPB
-LAST_FACTS = 16
+FACTS = 2 * 2 * KPB
 
 
 def facts_for(owner_id, owner, first_row, feats, acts):
@@ -58,10 +57,9 @@
     return jnp.concatenate(rows + values, axis=0)
 
 
-def prepare_kernel(owners, *refs):
+def prepare_kernel(owners, first, *refs):
     sources, refs = refs[:5], refs[5:]
-    outs, refs = refs[:6], refs[6:]
-    first_left, first_right, left, right, own_facts, slots = outs
+    outs, refs = refs[: 2 if first else 4], refs[2 if first else 4 :]
     block_slot, active, feats, acts, halves, wide_feats, wide_acts, sems = refs
     cut = halves.shape[2]
     copies = []
@@ -83,7 +81,6 @@
     slot = jnp.zeros_like(named)
     for block in range(block_slot.shape[0]):
         slot = jnp.where(named == block, block_slot[block], slot)
-    slots[...] = slot
     wide_feats[...] = feats[...].astype(jnp.float32)
     wide_acts[...] = acts[...].astype(jnp.float32)
     features = [wide_feats[pl.ds(k, ACT, stride=KPB), :] for k in range(KPB)]
@@ -95,44 +92,32 @@
             peer_at(distance, owners), slot // BLK_DEV, first_row, features, values
         )
 
-    def store_facts(target, blocks):
-        rows = jnp.concatenate(blocks, axis=0)
-        target[target.shape[0] - rows.shape[0] :, :] = rows.astype(jnp.bfloat16)
-
-    own_facts[...] = facts(0)
-    opposite = facts(owners // 2)
-    none = jnp.zeros_like(opposite)
-    store_facts(first_left, [opposite, none])
-    for target, sign in ((left, -1), (right, 1)):
-        store_facts(target, [facts(sign * d) for d in range(1, owners // 2)] + [none])
+    if not first:
+        outs[2][...] = facts(0)
+        outs[3][...] = slot
     tok_rows = halves.shape[1]
-    for side, targets in ((0, (first_left, left)), (1, (first_right, right))):
+    for side, sign in ((0, 1), (1, -1)):
+        ahead = [facts(sign * d) for d in (3, 4)] if first else [facts(-sign * d) for d in (1, 2)]
+        rows = jnp.concatenate(ahead, axis=0).astype(jnp.bfloat16)
+        outs[side][outs[side].shape[0] - FACTS :, :] = rows
+    for side in range(2):
         copies[4 + side].wait()
         for j in range(cut // 128):
             part = halves[side, :, j * 128 : (j + 1) * 128]
-            for target in targets:
-                target[j * tok_rows : (j + 1) * tok_rows, :] = part
-
-
-def prepare(block_slot, active_blocks, feature_idx, acts, grad_out, owners):
+            outs[side][j * tok_rows : (j + 1) * tok_rows, :] = part
+
+
+def prepare(first, block_slot, active_blocks, feature_idx, acts, grad_out, owners):
     tok_rows, width = grad_out.shape
-    plain = width // 256 * tok_rows
-
-    def piece(extra):
-        return pltpu.VMEM((plain + extra, 128), grad_out.dtype)
-
-    return pl.pallas_call(
-        functools.partial(prepare_kernel, owners),
-        out_shape=(
-            piece(LAST_FACTS),
-            piece(0),
-            piece(FACTS),
-            piece(FACTS),
-            pltpu.VMEM((2 * KPB, tok_rows), jnp.float32),
-            pltpu.VMEM((ACT, tok_rows), jnp.int32),
-        ),
+    piece = pltpu.VMEM((width // 256 * tok_rows + FACTS, 128), grad_out.dtype)
+    facts = pltpu.VMEM((2 * KPB, tok_rows), jnp.float32)
+    slots = pltpu.VMEM((ACT, tok_rows), jnp.int32)
+    out_shape = (piece, piece) if first else (piece, piece, facts, slots)
+    return pl.pallas_call(
+        functools.partial(prepare_kernel, owners, first),
+        out_shape=out_shape,
         in_specs=[HBM] * 5,
-        out_specs=(VMEM,) * 6,
+        out_specs=(VMEM,) * len(out_shape),
         scratch_shapes=[
             pltpu.SMEM(block_slot.shape, jnp.int32),
             pltpu.VMEM((ACT, tok_rows), jnp.int32),
@@ -197,9 +182,12 @@
     ]
 
 
-def facts_in(piece, distance, tok_rows):
+def facts_in(left, right, distance):
+    near = abs(distance) <= 2
+    piece = (right if near else left) if distance in (-1, -2, -3, 4) else (left if near else right)
     facts = piece[piece.shape[0] - FACTS :, :].astype(jnp.float32)
-    return facts[(abs(distance) - 1) * 2 * KPB : abs(distance) * 2 * KPB]
+    slot = (abs(distance) - 1) % 2
+    return facts[slot * 2 * KPB : (slot + 1) * 2 * KPB]
 
 
 def columns_of(pieces, tok_rows, parts):
@@ -246,20 +234,11 @@
             yield slice(side * cut + j * 128, side * cut + (j + 2) * 128), part
 
 
-def last_facts_in(piece):
-    return piece[piece.shape[0] - LAST_FACTS :, :].astype(jnp.float32)[: 2 * KPB]
-
-
 def facts_of(distances, own_facts, pieces):
-    facts = []
-    for i, d in enumerate(distances):
-        if d == 0:
-            facts.append(own_facts[...])
-        elif d == 4:
-            facts.append(last_facts_in(pieces[2 * i]))
-        else:
-            facts.append(facts_in(pieces[2 * i + (d < 0)], d, own_facts.shape[1]))
-    return facts
+    return [
+        own_facts[...] if d == 0 else facts_in(pieces[2 * i], pieces[2 * i + 1], d)
+        for i, d in enumerate(distances)
+    ]
 
 
 def scores_kernel(distances, split, decoder, own_facts, *refs):
@@ -309,7 +288,7 @@
 
 def last_gradients_kernel(left, right, total, out, rounded, sems):
     copies = []
-    facts = [last_facts_in(left)]
+    facts = [facts_in(left, right, 4)]
     for columns, part in gradient_blocks(facts, (left, right), out.shape[1]):
         rounded[:, columns] = (total[:, columns] + part).astype(out.dtype)
         copies.append(
@@ -434,10 +413,10 @@
             pairs.append((2 * ring[i] + 1, 2 * ring[(i + distance) % owners] + 1))
         return lax.ppermute(x, ("dp", "width"), pairs)
 
-    first_left, first_right, left, right, own_facts, slots = prepare(
-        block_slot, active_blocks, feature_idx, acts, grad_out, owners
-    )
+    tokens = (block_slot, active_blocks, feature_idx, acts, grad_out, owners)
+    first_left, first_right = prepare(True, *tokens)
     first_1 = hop((first_left, first_right))
+    left, right, own_facts, slots = prepare(False, *tokens)
     second_1 = crossed((right, left))
     decoder = fetch(decoder)
     first_1, decoder = lax.optimization_barrier((first_1, decoder))

time: 56.2 us -> 56.2 us (level)
  Pallas kernels: 11.5 us -> 12.6 us
  waiting for transfers between devices: 18.6 us -> 17.7 us
    pallas_call x1 -> x2, Pallas kernels: 1.2 us -> 2.36 us  [prepare(): pl.pallas_call(functools.partial(prepare_kernel, owners, first), out_shap...]
    ppermute x15, waiting for transfers between devices: 17.3 us -> 16.3 us  [shift(): return lax.ppermute(x, 'dp', pairs)]
  transfers between devices with their start and end apart: 20 -> 20, of which waited for: 10 -> 11; matrix products, arithmetic and copies ran while one was open for 0% -> 0% of each run, Pallas kernels for 18% -> 20%
where the time goes in v13:
time: 56.2 us; the launch traced here: 56 us
  starting transfers between devices  24.3 us (43%)
  waiting for transfers between devices  17.7 us (31%)
  Pallas kernels  12.6 us (22%)
  between operations  0.79 us (1%)
  other arithmetic  0.62 us (1%)
    ppermute x15, starting transfers between devices, shift(): return lax.ppermute(x, 'dp', pairs)  19.1 us
    ppermute x15, waiting for transfers between devices, shift(): return lax.ppermute(x, 'dp', pairs)  16.3 us
    ppermute x2, starting transfers between devices, return_by(): return lax.ppermute(x, ('dp', 'width'), pairs)  4.9 us
    pallas_call x4, Pallas kernels, scores_of(): pl.pallas_call(functools.partial(scores_kernel, distances, split), out_sh...  3.71 us
    pallas_call x3, Pallas kernels, gradients_of(): pl.pallas_call(functools.partial(gradients_kernel, distances), out_shape=...  3.09 us
    pallas_call x2, Pallas kernels, prepare(): pl.pallas_call(functools.partial(prepare_kernel, owners, first), out_shap...  2.36 us
    pallas_call x1, Pallas kernels, last_gradients(): pl.pallas_call(last_gradients_kernel, out_shape=jax.ShapeDtypeStruct(tota...  1.72 us
    pallas_call x1, Pallas kernels, fetch(): pl.pallas_call(fetch_kernel, out_shape=pltpu.VMEM(x.shape, x.dtype), in_s...  1.6 us
  transfers between devices with their start and end apart: 20, of which 11 were waited for; matrix products, arithmetic and copies ran while one was open for 0% of the time, Pallas kernels for 20%

profile of v13, /device:TPU:0, one launch (start us, length us, event | category | flops | bytes accessed | tf_op | source)
XLA Modules:
  0.0 56.0 jit_solution(5053927583073645248)
XLA Ops:
  0.6 1.2 %prepare.3 = (bf16[1040,128]{1,0:T(8,128)(2,1)S(1)}, bf16[1040,128]{1,0:T(8,128)(2,1)S(1)}) custom-call(s32[32]{0:T(128)} %refs_0_.3, s32[8,128]{1,0:T(8,128)} %bitcast.9, s32[32,128]{1,0:T(8,128)} %bitcast.5, bf16[32,128]{1,0:T(8,128)(2,1)} %bitcast.7, bf16[128,2048]{1,0:T(8,128)(2,1)} %refs_4_.3), custom_call_target="tpu_custom_call" | custom-call | tf_op jit(solution)/shard_map/prepare/pallas_call | solution.py:116
  1.8 3.1 %collective-permute-start = (bf16[1040,128]{1,0:T(8,128)(2,1)S(1)}, bf16[1040,128]{1,0:T(8,128)(2,1)S(1)}, u32[]{:S(2)}, u32[]{:S(2)}) collective-permute-start(bf16[1040,128]{1,0:T(8,128)(2,1)S(1)} %get-tuple-element.34.refs_0_), channel_id=1, source_target_pairs={{0,4},{4,8},{8,12},{12,14},{14,10},{10,6},{6,2},{2,0},{1,5},{5,9},... | collective-permute-start | bytes 798728 | tf_op jit(solution)/shard_map/ppermute | solution.py:396
  4.9 0.0 collective-permute-start.1
  4.9 1.2 %prepare.2 = (bf16[1040,128]{1,0:T(8,128)(2,1)S(1)}, bf16[1040,128]{1,0:T(8,128)(2,1)S(1)}, f32[8,128]{1,0:T(8,128)S(1)}, s32[8,128]{1,0:T(8,128)S(1)}) custom-call(s32[32]{0:T(128)} %refs_0_.3, s32[8,128]{1,0:T(8,128)} %bitcast.10, s32[32,128]{1,0:T(8,128)} %bitcast.6, bf16[32,128]{1,0:T(8,128)(2,1)} %bitcast.8, bf16[128,2048]{1,0:T(8,128)(2,1)} %refs_4_.3), custom_call_target="tpu_custom_call" | custom-call | tf_op jit(solution)/shard_map/prepare/pallas_call | solution.py:116
  6.1 2.1 %collective-permute-start.3 = (bf16[1040,128]{1,0:T(8,128)(2,1)S(1)}, bf16[1040,128]{1,0:T(8,128)(2,1)S(1)}, u32[]{:S(2)}, u32[]{:S(2)}) collective-permute-start(bf16[1040,128]{1,0:T(8,128)(2,1)S(1)} %get-tuple-element.37), channel_id=1, source_target_pairs={{0,4},{4,8},{8,12},{12,14},{14,10},{10,6},{6,2},{2,0},{1,5},{5,9},... | collective-permute-start | bytes 798728 | tf_op jit(solution)/shard_map/ppermute | solution.py:396
  8.2 0.0 collective-permute-start.5
  8.2 1.6 %fetch.1.decoder = bf16[512,2048]{1,0:T(8,128)(2,1)S(1)} custom-call(bf16[512,2048]{1,0:T(8,128)(2,1)} %source.1), custom_call_target="tpu_custom_call" | custom-call | tf_op jit(solution)/shard_map/fetch/pallas_call | solution.py:143
  9.8 2.3 %collective-permute-done.refs_2_ = bf16[1040,128]{1,0:T(8,128)(2,1)S(1)} collective-permute-done((bf16[1040,128]{1,0:T(8,128)(2,1)S(1)}, bf16[1040,128]{1,0:T(8,128)(2,1)S(1)}, u32[]{:S(2)}, u32[]{:S(2)}) %collective-permute-start) | collective-permute-done | bytes 266272 | tf_op jit(solution)/shard_map/ppermute | solution.py:396
  12.0 2.2 %collective-permute-done.1.refs_5_ = bf16[1040,128]{1,0:T(8,128)(2,1)S(1)} collective-permute-done((bf16[1040,128]{1,0:T(8,128)(2,1)S(1)}, bf16[1040,128]{1,0:T(8,128)(2,1)S(1)}, u32[]{:S(2)}, u32[]{:S(2)}) %collective-permute-start.1) | collective-permute-done | bytes 266272 | tf_op jit(solution)/shard_map/ppermute | solution.py:396
  14.2 1.6 %collective-permute-start.2 = (bf16[1040,128]{1,0:T(8,128)(2,1)S(1)}, bf16[1040,128]{1,0:T(8,128)(2,1)S(1)}, u32[]{:S(2)}, u32[]{:S(2)}) collective-permute-start(bf16[1040,128]{1,0:T(8,128)(2,1)S(1)} %collective-permute-done.refs_2_), channel_id=1, source_target_pairs={{0,4},{4,8},{8,12},{12,14},{14,10},{10,6},{6,2},{2,0},{1,5},{5,9},... | collective-permute-start | bytes 798728 | tf_op jit(solution)/shard_map/ppermute | solution.py:396
  15.8 0.4 collective-permute-start.7
  16.2 1.5 %collective-permute-done.3.refs_3_ = bf16[1040,128]{1,0:T(8,128)(2,1)S(1)} collective-permute-done((bf16[1040,128]{1,0:T(8,128)(2,1)S(1)}, bf16[1040,128]{1,0:T(8,128)(2,1)S(1)}, u32[]{:S(2)}, u32[]{:S(2)}) %collective-permute-start.3) | collective-permute-done | bytes 266272 | tf_op jit(solution)/shard_map/ppermute | solution.py:396
  17.7 2.1 %collective-permute-start.4 = (bf16[1040,128]{1,0:T(8,128)(2,1)S(1)}, bf16[1040,128]{1,0:T(8,128)(2,1)S(1)}, u32[]{:S(2)}, u32[]{:S(2)}) collective-permute-start(bf16[1040,128]{1,0:T(8,128)(2,1)S(1)} %collective-permute-done.3.refs_3_), channel_id=1, source_target_pairs={{0,4},{4,8},{8,12},{12,14},{14,10},{10,6},{6,2},{2,0},{1,5},{5,9},... | collective-permute-start | bytes 798728 | tf_op jit(solution)/shard_map/ppermute | solution.py:396
  19.9 0.0 collective-permute-done.5.refs_4_
  19.9 0.0 collective-permute-start.6
  19.9 3.6 %collective-permute-done.2.refs_0_ = bf16[1040,128]{1,0:T(8,128)(2,1)S(1)} collective-permute-done((bf16[1040,128]{1,0:T(8,128)(2,1)S(1)}, bf16[1040,128]{1,0:T(8,128)(2,1)S(1)}, u32[]{:S(2)}, u32[]{:S(2)}) %collective-permute-start.2) | collective-permute-done | bytes 266272 | tf_op jit(solution)/shard_map/ppermute | solution.py:396
  23.5 2.0 %collective-permute-start.8 = (bf16[1040,128]{1,0:T(8,128)(2,1)S(1)}, bf16[1040,128]{1,0:T(8,128)(2,1)S(1)}, u32[]{:S(2)}, u32[]{:S(2)}) collective-permute-start(bf16[1040,128]{1,0:T(8,128)(2,1)S(1)} %collective-permute-done.2.refs_0_), channel_id=1, source_target_pairs={{0,4},{4,8},{8,12},{12,14},{14,10},{10,6},{6,2},{2,0},{1,5},{5,9},... | collective-permute-start | bytes 798728 | tf_op jit(solution)/shard_map/ppermute | solution.py:396
  25.6 0.0 collective-permute-done.7.refs_3_
  25.6 0.0 collective-permute-start.9
  25.6 1.4 %scores.4 = (f32[8,128]{1,0:T(8,128)S(1)}, f32[8,128]{1,0:T(8,128)S(1)}, f32[8,128]{1,0:T(8,128)S(1)}) custom-call(bf16[512,2048]{1,0:T(8,128)(2,1)S(1)} %fetch.1.decoder, f32[8,128]{1,0:T(8,128)S(1)} %get-tuple-element.33.own_facts, bf16[1040,128]{1,0:T(8,128)(2,1)S(1)} %get-tuple-element.34.refs_0_, bf16[1040,128]{1,0:T(8,128)(2,1)S(1)} %get-tuple-element.35.refs_1_, ...), custom_call_target="tpu_custom_call" | custom-call | tf_op jit(solution)/shard_map/scores/pallas_call | solution.py:257
  27.0 2.3 %collective-permute-done.4.onward = bf16[1040,128]{1,0:T(8,128)(2,1)S(1)} collective-permute-done((bf16[1040,128]{1,0:T(8,128)(2,1)S(1)}, bf16[1040,128]{1,0:T(8,128)(2,1)S(1)}, u32[]{:S(2)}, u32[]{:S(2)}) %collective-permute-start.4) | collective-permute-done | bytes 266272 | tf_op jit(solution)/shard_map/ppermute | solution.py:396
  29.3 2.1 %collective-permute-done.6.back = bf16[1040,128]{1,0:T(8,128)(2,1)S(1)} collective-permute-done((bf16[1040,128]{1,0:T(8,128)(2,1)S(1)}, bf16[1040,128]{1,0:T(8,128)(2,1)S(1)}, u32[]{:S(2)}, u32[]{:S(2)}) %collective-permute-start.6) | collective-permute-done | bytes 266272 | tf_op jit(solution)/shard_map/ppermute | solution.py:396
  31.3 0.1 stamp.1
  31.4 1.6 %collective-permute-start.11 = (bf16[1040,128]{1,0:T(8,128)(2,1)S(1)}, bf16[1040,128]{1,0:T(8,128)(2,1)S(1)}, u32[]{:S(2)}, u32[]{:S(2)}) collective-permute-start(bf16[1040,128]{1,0:T(8,128)(2,1)S(1)} %get-tuple-element.43.refs_1_), channel_id=1, source_target_pairs={{0,4},{4,8},{8,12},{12,14},{14,10},{10,6},{6,2},{2,0},{1,5},{5,9},... | collective-permute-start | bytes 798728 | tf_op jit(solution)/shard_map/ppermute | solution.py:396
  33.0 0.4 collective-permute-start.12
  33.5 0.8 %scores.5 = (f32[8,128]{1,0:T(8,128)S(1)}, f32[8,128]{1,0:T(8,128)S(1)}) custom-call(bf16[512,2048]{1,0:T(8,128)(2,1)S(1)} %fetch.1.decoder, f32[8,128]{1,0:T(8,128)S(1)} %get-tuple-element.33.own_facts, bf16[1040,128]{1,0:T(8,128)(2,1)S(1)} %collective-permute-done.2.refs_0_, bf16[1040,128]{1,0:T(8,128)(2,1)S(1)} %get-tuple-element.43.refs_1_, ...), custom_call_target="tpu_custom_call" | custom-call | tf_op jit(solution)/shard_map/scores/pallas_call | solution.py:257
  34.3 0.1 collective-permute-start.10
  34.4 1.3 %gradients.3.refs_4_ = f32[512,2048]{1,0:T(8,128)S(1)} custom-call(f32[8,128]{1,0:T(8,128)S(1)} %get-tuple-element.33.own_facts, bf16[1040,128]{1,0:T(8,128)(2,1)S(1)} %get-tuple-element.34.refs_0_, bf16[1040,128]{1,0:T(8,128)(2,1)S(1)} %get-tuple-element.35.refs_1_, bf16[1040,128]{1,0:T(8,128)(2,1)S(1)} %collective-permute-done.refs_2_, ...), custom_call_target="tpu_custom_call" | custom-call | tf_op jit(solution)/shard_map/gradients/pallas_call | solution.py:278
  35.7 0.9 %gradients.4.refs_4_ = f32[512,2048]{1,0:T(8,128)S(1)} custom-call(f32[8,128]{1,0:T(8,128)S(1)} %get-tuple-element.33.own_facts, bf16[1040,128]{1,0:T(8,128)(2,1)S(1)} %collective-permute-done.2.refs_0_, bf16[1040,128]{1,0:T(8,128)(2,1)S(1)} %get-tuple-element.43.refs_1_, ...), custom_call_target="tpu_custom_call", output_to_operand_aliasing={{}: (5, {})} | custom-call | tf_op jit(solution)/shard_map/gradients/pallas_call | solution.py:278
  36.6 0.0 collective-permute-done.10
  36.6 0.0 collective-permute-done.8.refs_0_
  36.6 0.4 collective-permute-done.9.refs_3_
  37.0 1.6 %collective-permute-start.14 = (bf16[1040,128]{1,0:T(8,128)(2,1)S(1)}, bf16[1040,128]{1,0:T(8,128)(2,1)S(1)}, u32[]{:S(2)}, u32[]{:S(2)}) collective-permute-start(bf16[1040,128]{1,0:T(8,128)(2,1)S(1)} %collective-permute-done.8.refs_0_), channel_id=1, source_target_pairs={{0,4},{4,8},{8,12},{12,14},{14,10},{10,6},{6,2},{2,0},{1,5},{5,9},... | collective-permute-start | bytes 798728 | tf_op jit(solution)/shard_map/ppermute | solution.py:396
  38.6 0.4 collective-permute-start.15
  39.1 1.4 %collective-permute-start.18 = (f32[32,128]{1,0:T(8,128)S(1)}, f32[32,128]{1,0:T(8,128)S(1)}, u32[]{:S(2)}, u32[]{:S(2)}) collective-permute-start(f32[32,128]{1,0:T(8,128)S(1)} %concatenate.3), channel_id=1, source_target_pairs={{0,6},{1,9},{4,2},{5,13},{8,0},{9,15},{12,4},{13,11},{14,8},{15,7}... | collective-permute-start | bytes 49160 | tf_op jit(solution)/shard_map/ppermute | solution.py:414
  40.4 0.0 collective-permute-done.11.refs_1_.onward
  40.4 0.9 %collective-permute-done.12.refs_2_.back = bf16[1040,128]{1,0:T(8,128)(2,1)S(1)} collective-permute-done((bf16[1040,128]{1,0:T(8,128)(2,1)S(1)}, bf16[1040,128]{1,0:T(8,128)(2,1)S(1)}, u32[]{:S(2)}, u32[]{:S(2)}) %collective-permute-start.12) | collective-permute-done | bytes 266272 | tf_op jit(solution)/shard_map/ppermute | solution.py:396
  41.4 0.8 %scores.6 = (f32[8,128]{1,0:T(8,128)S(1)}, f32[8,128]{1,0:T(8,128)S(1)}) custom-call(bf16[512,2048]{1,0:T(8,128)(2,1)S(1)} %fetch.1.decoder, f32[8,128]{1,0:T(8,128)S(1)} %get-tuple-element.33.own_facts, bf16[1040,128]{1,0:T(8,128)(2,1)S(1)} %collective-permute-done.8.refs_0_, bf16[1040,128]{1,0:T(8,128)(2,1)S(1)} %collective-permute-done.11.refs_1_.onward, ...), custom_call_target="tpu_custom_call" | custom-call | tf_op jit(solution)/shard_map/scores/pallas_call | solution.py:257
  42.2 0.1 collective-permute-start.13
  42.3 0.9 %gradients.5.total = f32[512,2048]{1,0:T(8,128)S(1)} custom-call(f32[8,128]{1,0:T(8,128)S(1)} %get-tuple-element.33.own_facts, bf16[1040,128]{1,0:T(8,128)(2,1)S(1)} %collective-permute-done.8.refs_0_, bf16[1040,128]{1,0:T(8,128)(2,1)S(1)} %collective-permute-done.11.refs_1_.onward, ...), custom_call_target="tpu_custom_call", output_to_operand_aliasing={{}: (5, {})} | custom-call | tf_op jit(solution)/shard_map/gradients/pallas_call | solution.py:278
  43.2 0.3 collective-permute-done.13
  43.4 3.5 %collective-permute-start.16 = (f32[8,128]{1,0:T(8,128)S(1)}, f32[8,128]{1,0:T(8,128)S(1)}, u32[]{:S(2)}, u32[]{:S(2)}) collective-permute-start(f32[8,128]{1,0:T(8,128)S(1)} %add.12), channel_id=1, source_target_pairs={{0,10},{1,13},{4,6},{5,15},{8,2},{9,11},{12,0},{13,7},{14,4},{15,3... | collective-permute-start | bytes 12296 | tf_op jit(solution)/shard_map/ppermute | solution.py:414
  47.0 0.0 collective-permute-done.14.left.refs_0_
  47.0 0.0 collective-permute-done.15.right.refs_1_
  47.0 0.7 %scores.7 = f32[8,128]{1,0:T(8,128)S(1)} custom-call(bf16[512,2048]{1,0:T(8,128)(2,1)S(1)} %fetch.1.decoder, f32[8,128]{1,0:T(8,128)S(1)} %get-tuple-element.33.own_facts, bf16[1040,128]{1,0:T(8,128)(2,1)S(1)} %collective-permute-done.14.left.refs_0_, bf16[1040,128]{1,0:T(8,128)(2,1)S(1)} %collective-permute-done.15.right.refs_1_), custom_call_target="tpu_custom_call" | custom-call | tf_op jit(solution)/shard_map/scores/pallas_call | solution.py:257
  47.7 3.6 %collective-permute-start.17 = (f32[8,128]{1,0:T(8,128)S(1)}, f32[8,128]{1,0:T(8,128)S(1)}, u32[]{:S(2)}, u32[]{:S(2)}) collective-permute-start(f32[8,128]{1,0:T(8,128)S(1)} %scores.7), channel_id=1, source_target_pairs={{0,14},{4,10},{8,6},{12,2},{14,0},{10,4},{6,8},{2,12},{1,15},{5,11... | collective-permute-start | bytes 12296 | tf_op jit(solution)/shard_map/ppermute | solution.py:396
  51.3 0.0 collective-permute-done.18
  51.3 0.0 collective-permute-done.16.third
  51.4 1.7 %last_gradients.1 = bf16[512,2048]{1,0:T(8,128)(2,1)} custom-call(bf16[1040,128]{1,0:T(8,128)(2,1)S(1)} %collective-permute-done.14.left.refs_0_, bf16[1040,128]{1,0:T(8,128)(2,1)S(1)} %collective-permute-done.15.right.refs_1_, f32[512,2048]{1,0:T(8,128)S(1)} %gradients.5.total), custom_call_target="tpu_custom_call" | custom-call | tf_op jit(solution)/shard_map/last_gradients/pallas_call | solution.py:305
  53.1 1.0 %collective-permute-done.17.opposite = f32[8,128]{1,0:T(8,128)S(1)} collective-permute-done((f32[8,128]{1,0:T(8,128)S(1)}, f32[8,128]{1,0:T(8,128)S(1)}, u32[]{:S(2)}, u32[]{:S(2)}) %collective-permute-start.17) | collective-permute-done | bytes 4128 | tf_op jit(solution)/shard_map/ppermute | solution.py:396
  54.1 0.2 collective-permute-start.19
  54.3 1.1 %collective-permute-done.19 = f32[32,128]{1,0:T(8,128)S(1)} collective-permute-done((f32[32,128]{1,0:T(8,128)S(1)}, f32[32,128]{1,0:T(8,128)S(1)}, u32[]{:S(2)}, u32[]{:S(2)}) %collective-permute-start.19) | collective-permute-done | bytes 16416 | tf_op jit(solution)/shard_map/ppermute | solution.py:407
  55.4 0.6 %add_bitcast_fusion = f32[128,32]{0,1:T(8,128)} fusion(f32[32,128]{1,0:T(8,128)S(1)} %unpack.1, f32[32,128]{1,0:T(8,128)S(1)} %collective-permute-done.19), kind=kLoop, calls=%fused_computation | loop fusion | flops 4096 | bytes 49152 | tf_op jit(solution)/shard_map/transpose | solution.py:453
  (5 shorter events, 0.0 us)
Async XLA Ops:
  1.8 10.2 %collective-permute-start = (bf16[1040,128]{1,0:T(8,128)(2,1)S(1)}, bf16[1040,128]{1,0:T(8,128)(2,1)S(1)}, u32[]{:S(2)}, u32[]{:S(2)}) collective-permute-start(bf16[1040,128]{1,0:T(8,128)(2,1)S(1)} %get-tuple-element.34.refs_0_), channel_id=1, source_target_pairs={{0,4},{4,8},{8,12},{12,14},{14,10},{10,6},{6,2},{2,0},{1,5},{5,9},... | collective-permute-start | bytes 798728 | tf_op jit(solution)/shard_map/ppermute | solution.py:396
  4.9 9.3 %collective-permute-start.1 = (bf16[1040,128]{1,0:T(8,128)(2,1)S(1)}, bf16[1040,128]{1,0:T(8,128)(2,1)S(1)}, u32[]{:S(2)}, u32[]{:S(2)}) collective-permute-start(bf16[1040,128]{1,0:T(8,128)(2,1)S(1)} %get-tuple-element.35.refs_1_), channel_id=1, source_target_pairs={{0,2},{4,0},{8,4},{12,8},{14,12},{10,14},{6,10},{2,6},{1,3},{5,1},... | collective-permute-start | bytes 798728 | tf_op jit(solution)/shard_map/ppermute | solution.py:396
  6.1 11.7 %collective-permute-start.3 = (bf16[1040,128]{1,0:T(8,128)(2,1)S(1)}, bf16[1040,128]{1,0:T(8,128)(2,1)S(1)}, u32[]{:S(2)}, u32[]{:S(2)}) collective-permute-start(bf16[1040,128]{1,0:T(8,128)(2,1)S(1)} %get-tuple-element.37), channel_id=1, source_target_pairs={{0,4},{4,8},{8,12},{12,14},{14,10},{10,6},{6,2},{2,0},{1,5},{5,9},... | collective-permute-start | bytes 798728 | tf_op jit(solution)/shard_map/ppermute | solution.py:396
  8.2 11.8 %collective-permute-start.5 = (bf16[1040,128]{1,0:T(8,128)(2,1)S(1)}, bf16[1040,128]{1,0:T(8,128)(2,1)S(1)}, u32[]{:S(2)}, u32[]{:S(2)}) collective-permute-start(bf16[1040,128]{1,0:T(8,128)(2,1)S(1)} %get-tuple-element.38), channel_id=1, source_target_pairs={{0,2},{4,0},{8,4},{12,8},{14,12},{10,14},{6,10},{2,6},{1,3},{5,1},... | collective-permute-start | bytes 798728 | tf_op jit(solution)/shard_map/ppermute | solution.py:396
  14.2 9.3 %collective-permute-start.2 = (bf16[1040,128]{1,0:T(8,128)(2,1)S(1)}, bf16[1040,128]{1,0:T(8,128)(2,1)S(1)}, u32[]{:S(2)}, u32[]{:S(2)}) collective-permute-start(bf16[1040,128]{1,0:T(8,128)(2,1)S(1)} %collective-permute-done.refs_2_), channel_id=1, source_target_pairs={{0,4},{4,8},{8,12},{12,14},{14,10},{10,6},{6,2},{2,0},{1,5},{5,9},... | collective-permute-start | bytes 798728 | tf_op jit(solution)/shard_map/ppermute | solution.py:396
  15.8 9.8 %collective-permute-start.7 = (bf16[1040,128]{1,0:T(8,128)(2,1)S(1)}, bf16[1040,128]{1,0:T(8,128)(2,1)S(1)}, u32[]{:S(2)}, u32[]{:S(2)}) collective-permute-start(bf16[1040,128]{1,0:T(8,128)(2,1)S(1)} %collective-permute-done.1.refs_5_), channel_id=1, source_target_pairs={{0,2},{4,0},{8,4},{12,8},{14,12},{10,14},{6,10},{2,6},{1,3},{5,1},... | collective-permute-start | bytes 798728 | tf_op jit(solution)/shard_map/ppermute | solution.py:396
  17.7 11.5 %collective-permute-start.4 = (bf16[1040,128]{1,0:T(8,128)(2,1)S(1)}, bf16[1040,128]{1,0:T(8,128)(2,1)S(1)}, u32[]{:S(2)}, u32[]{:S(2)}) collective-permute-start(bf16[1040,128]{1,0:T(8,128)(2,1)S(1)} %collective-permute-done.3.refs_3_), channel_id=1, source_target_pairs={{0,4},{4,8},{8,12},{12,14},{14,10},{10,6},{6,2},{2,0},{1,5},{5,9},... | collective-permute-start | bytes 798728 | tf_op jit(solution)/shard_map/ppermute | solution.py:396
  19.9 11.4 %collective-permute-start.6 = (bf16[1040,128]{1,0:T(8,128)(2,1)S(1)}, bf16[1040,128]{1,0:T(8,128)(2,1)S(1)}, u32[]{:S(2)}, u32[]{:S(2)}) collective-permute-start(bf16[1040,128]{1,0:T(8,128)(2,1)S(1)} %collective-permute-done.5.refs_4_), channel_id=1, source_target_pairs={{0,2},{4,0},{8,4},{12,8},{14,12},{10,14},{6,10},{2,6},{1,3},{5,1},... | collective-permute-start | bytes 798728 | tf_op jit(solution)/shard_map/ppermute | solution.py:396
  23.5 13.1 %collective-permute-start.8 = (bf16[1040,128]{1,0:T(8,128)(2,1)S(1)}, bf16[1040,128]{1,0:T(8,128)(2,1)S(1)}, u32[]{:S(2)}, u32[]{:S(2)}) collective-permute-start(bf16[1040,128]{1,0:T(8,128)(2,1)S(1)} %collective-permute-done.2.refs_0_), channel_id=1, source_target_pairs={{0,4},{4,8},{8,12},{12,14},{14,10},{10,6},{6,2},{2,0},{1,5},{5,9},... | collective-permute-start | bytes 798728 | tf_op jit(solution)/shard_map/ppermute | solution.py:396
  25.6 11.4 %collective-permute-start.9 = (bf16[1040,128]{1,0:T(8,128)(2,1)S(1)}, bf16[1040,128]{1,0:T(8,128)(2,1)S(1)}, u32[]{:S(2)}, u32[]{:S(2)}) collective-permute-start(bf16[1040,128]{1,0:T(8,128)(2,1)S(1)} %collective-permute-done.7.refs_3_), channel_id=1, source_target_pairs={{0,2},{4,0},{8,4},{12,8},{14,12},{10,14},{6,10},{2,6},{1,3},{5,1},... | collective-permute-start | bytes 798728 | tf_op jit(solution)/shard_map/ppermute | solution.py:396
  31.4 9.0 %collective-permute-start.11 = (bf16[1040,128]{1,0:T(8,128)(2,1)S(1)}, bf16[1040,128]{1,0:T(8,128)(2,1)S(1)}, u32[]{:S(2)}, u32[]{:S(2)}) collective-permute-start(bf16[1040,128]{1,0:T(8,128)(2,1)S(1)} %get-tuple-element.43.refs_1_), channel_id=1, source_target_pairs={{0,4},{4,8},{8,12},{12,14},{14,10},{10,6},{6,2},{2,0},{1,5},{5,9},... | collective-permute-start | bytes 798728 | tf_op jit(solution)/shard_map/ppermute | solution.py:396
  33.0 8.3 %collective-permute-start.12 = (bf16[1040,128]{1,0:T(8,128)(2,1)S(1)}, bf16[1040,128]{1,0:T(8,128)(2,1)S(1)}, u32[]{:S(2)}, u32[]{:S(2)}) collective-permute-start(bf16[1040,128]{1,0:T(8,128)(2,1)S(1)} %get-tuple-element.44.refs_2_), channel_id=1, source_target_pairs={{0,2},{4,0},{8,4},{12,8},{14,12},{10,14},{6,10},{2,6},{1,3},{5,1},... | collective-permute-start | bytes 798728 | tf_op jit(solution)/shard_map/ppermute | solution.py:396
  34.3 2.3 %collective-permute-start.10 = (f32[8,128]{1,0:T(8,128)S(1)}, f32[8,128]{1,0:T(8,128)S(1)}, u32[]{:S(2)}, u32[]{:S(2)}) collective-permute-start(f32[8,128]{1,0:T(8,128)S(1)} %get-tuple-element.46), channel_id=1, source_target_pairs={{0,1},{1,0},{2,3},{3,2},{4,5},{5,4},{6,7},{7,6},{8,9},{9,8},{10,11... | collective-permute-start | bytes 12296 | tf_op jit(solution)/shard_map/ppermute | solution.py:407
  37.0 9.9 %collective-permute-start.14 = (bf16[1040,128]{1,0:T(8,128)(2,1)S(1)}, bf16[1040,128]{1,0:T(8,128)(2,1)S(1)}, u32[]{:S(2)}, u32[]{:S(2)}) collective-permute-start(bf16[1040,128]{1,0:T(8,128)(2,1)S(1)} %collective-permute-done.8.refs_0_), channel_id=1, source_target_pairs={{0,4},{4,8},{8,12},{12,14},{14,10},{10,6},{6,2},{2,0},{1,5},{5,9},... | collective-permute-start | bytes 798728 | tf_op jit(solution)/shard_map/ppermute | solution.py:396
  38.6 8.4 %collective-permute-start.15 = (bf16[1040,128]{1,0:T(8,128)(2,1)S(1)}, bf16[1040,128]{1,0:T(8,128)(2,1)S(1)}, u32[]{:S(2)}, u32[]{:S(2)}) collective-permute-start(bf16[1040,128]{1,0:T(8,128)(2,1)S(1)} %collective-permute-done.9.refs_3_), channel_id=1, source_target_pairs={{0,2},{4,0},{8,4},{12,8},{14,12},{10,14},{6,10},{2,6},{1,3},{5,1},... | collective-permute-start | bytes 798728 | tf_op jit(solution)/shard_map/ppermute | solution.py:396
  39.1 12.3 %collective-permute-start.18 = (f32[32,128]{1,0:T(8,128)S(1)}, f32[32,128]{1,0:T(8,128)S(1)}, u32[]{:S(2)}, u32[]{:S(2)}) collective-permute-start(f32[32,128]{1,0:T(8,128)S(1)} %concatenate.3), channel_id=1, source_target_pairs={{0,6},{1,9},{4,2},{5,13},{8,0},{9,15},{12,4},{13,11},{14,8},{15,7}... | collective-permute-start | bytes 49160 | tf_op jit(solution)/shard_map/ppermute | solution.py:414
  42.2 1.2 %collective-permute-start.13 = (f32[8,128]{1,0:T(8,128)S(1)}, f32[8,128]{1,0:T(8,128)S(1)}, u32[]{:S(2)}, u32[]{:S(2)}) collective-permute-start(f32[8,128]{1,0:T(8,128)S(1)} %get-tuple-element.51), channel_id=1, source_target_pairs={{0,1},{1,0},{2,3},{3,2},{4,5},{5,4},{6,7},{7,6},{8,9},{9,8},{10,11... | collective-permute-start | bytes 12296 | tf_op jit(solution)/shard_map/ppermute | solution.py:407
  43.4 7.9 %collective-permute-start.16 = (f32[8,128]{1,0:T(8,128)S(1)}, f32[8,128]{1,0:T(8,128)S(1)}, u32[]{:S(2)}, u32[]{:S(2)}) collective-permute-start(f32[8,128]{1,0:T(8,128)S(1)} %add.12), channel_id=1, source_target_pairs={{0,10},{1,13},{4,6},{5,15},{8,2},{9,11},{12,0},{13,7},{14,4},{15,3... | collective-permute-start | bytes 12296 | tf_op jit(solution)/shard_map/ppermute | solution.py:414
  47.7 6.4 %collective-permute-start.17 = (f32[8,128]{1,0:T(8,128)S(1)}, f32[8,128]{1,0:T(8,128)S(1)}, u32[]{:S(2)}, u32[]{:S(2)}) collective-permute-start(f32[8,128]{1,0:T(8,128)S(1)} %scores.7), channel_id=1, source_target_pairs={{0,14},{4,10},{8,6},{12,2},{14,0},{10,4},{6,8},{2,12},{1,15},{5,11... | collective-permute-start | bytes 12296 | tf_op jit(solution)/shard_map/ppermute | solution.py:396
  54.1 1.2 %collective-permute-start.19 = (f32[32,128]{1,0:T(8,128)S(1)}, f32[32,128]{1,0:T(8,128)S(1)}, u32[]{:S(2)}, u32[]{:S(2)}) collective-permute-start(f32[32,128]{1,0:T(8,128)S(1)} %unpack.1), channel_id=1, source_target_pairs={{0,1},{1,0},{2,3},{3,2},{4,5},{5,4},{6,7},{7,6},{8,9},{9,8},{10,11... | collective-permute-start | bytes 49160 | tf_op jit(solution)/shard_map/ppermute | solution.py:407

commit v14 on v13

--- a/solution.py
+++ b/solution.py
@@ -57,9 +57,9 @@
     return jnp.concatenate(rows + values, axis=0)
 
 
-def prepare_kernel(owners, first, *refs):
+def prepare_kernel(owners, *refs):
     sources, refs = refs[:5], refs[5:]
-    outs, refs = refs[: 2 if first else 4], refs[2 if first else 4 :]
+    outs, refs = refs[:6], refs[6:]
     block_slot, active, feats, acts, halves, wide_feats, wide_acts, sems = refs
     cut = halves.shape[2]
     copies = []
@@ -92,29 +92,30 @@
             peer_at(distance, owners), slot // BLK_DEV, first_row, features, values
         )
 
-    if not first:
-        outs[2][...] = facts(0)
-        outs[3][...] = slot
+    outs[4][...] = facts(0)
+    outs[5][...] = slot
+    for piece, sign, distances in (
+        (outs[0], 1, (3, 4)), (outs[1], -1, (3, 4)), (outs[2], -1, (1, 2)), (outs[3], 1, (1, 2))
+    ):
+        rows = jnp.concatenate([facts(sign * d) for d in distances], axis=0)
+        piece[piece.shape[0] - FACTS :, :] = rows.astype(jnp.bfloat16)
     tok_rows = halves.shape[1]
-    for side, sign in ((0, 1), (1, -1)):
-        ahead = [facts(sign * d) for d in (3, 4)] if first else [facts(-sign * d) for d in (1, 2)]
-        rows = jnp.concatenate(ahead, axis=0).astype(jnp.bfloat16)
-        outs[side][outs[side].shape[0] - FACTS :, :] = rows
     for side in range(2):
         copies[4 + side].wait()
         for j in range(cut // 128):
             part = halves[side, :, j * 128 : (j + 1) * 128]
-            outs[side][j * tok_rows : (j + 1) * tok_rows, :] = part
-
-
-def prepare(first, block_slot, active_blocks, feature_idx, acts, grad_out, owners):
+            for piece in (outs[side], outs[2 + side]):
+                piece[j * tok_rows : (j + 1) * tok_rows, :] = part
+
+
+def prepare(block_slot, active_blocks, feature_idx, acts, grad_out, owners):
     tok_rows, width = grad_out.shape
     piece = pltpu.VMEM((width // 256 * tok_rows + FACTS, 128), grad_out.dtype)
     facts = pltpu.VMEM((2 * KPB, tok_rows), jnp.float32)
     slots = pltpu.VMEM((ACT, tok_rows), jnp.int32)
-    out_shape = (piece, piece) if first else (piece, piece, facts, slots)
-    return pl.pallas_call(
-        functools.partial(prepare_kernel, owners, first),
+    out_shape = (piece,) * 4 + (facts, slots)
+    return pl.pallas_call(
+        functools.partial(prepare_kernel, owners),
         out_shape=out_shape,
         in_specs=[HBM] * 5,
         out_specs=(VMEM,) * len(out_shape),
@@ -413,10 +414,10 @@
             pairs.append((2 * ring[i] + 1, 2 * ring[(i + distance) % owners] + 1))
         return lax.ppermute(x, ("dp", "width"), pairs)
 
-    tokens = (block_slot, active_blocks, feature_idx, acts, grad_out, owners)
-    first_left, first_right = prepare(True, *tokens)
+    first_left, first_right, left, right, own_facts, slots = prepare(
+        block_slot, active_blocks, feature_idx, acts, grad_out, owners
+    )
     first_1 = hop((first_left, first_right))
-    left, right, own_facts, slots = prepare(False, *tokens)
     second_1 = crossed((right, left))
     decoder = fetch(decoder)
     first_1, decoder = lax.optimization_barrier((first_1, decoder))
@@ -434,7 +435,7 @@
     total = gradients_of((-2, 2), pairs, own_facts, decoder.shape, total)
     second = mine + other_core(others)
     total, first_3, second = lax.optimization_barrier((total, first_3, second))
-    second = return_by(2, jnp.concatenate([second, jnp.zeros((24, 128), jnp.float32)]))[:8]
+    second = return_by(2, jnp.concatenate([second, jnp.zeros((16, 128), jnp.float32)]))[:8]
     first_4 = hop(first_3)
     pairs = [(first_3[0], second_3[0]), (second_3[1], first_3[1])]
     mine, others = scores_of((-3, 3), pairs, decoder, own_facts, True)

time: 56.2 us -> 56.2 us (level)
  Pallas kernels: 12.6 us -> 11.4 us
  waiting for transfers between devices: 17.7 us -> 18.9 us
    ppermute x15, waiting for transfers between devices: 16.3 us -> 17.6 us  [shift(): return lax.ppermute(x, 'dp', pairs)]
    pallas_call x2 -> x1, Pallas kernels: 2.36 us -> 1.2 us  [prepare(): pl.pallas_call(functools.partial(prepare_kernel, owners), out_shape=out_s...]
  transfers between devices with their start and end apart: 20 -> 20, of which waited for: 11 -> 11; matrix products, arithmetic and copies ran while one was open for 0% -> 0% of each run, Pallas kernels for 20% -> 18%
where the time goes in v14:
time: 56.2 us; the launch traced here: 56 us
  starting transfers between devices  24.2 us (43%)
  waiting for transfers between devices  18.9 us (34%)
  Pallas kernels  11.4 us (20%)
  between operations  0.78 us (1%)
  other arithmetic  0.62 us (1%)
    ppermute x15, starting transfers between devices, shift(): return lax.ppermute(x, 'dp', pairs)  19 us
    ppermute x15, waiting for transfers between devices, shift(): return lax.ppermute(x, 'dp', pairs)  17.6 us
    ppermute x2, starting transfers between devices, return_by(): return lax.ppermute(x, ('dp', 'width'), pairs)  4.89 us
    pallas_call x4, Pallas kernels, scores_of(): pl.pallas_call(functools.partial(scores_kernel, distances, split), out_sh...  3.71 us
    pallas_call x3, Pallas kernels, gradients_of(): pl.pallas_call(functools.partial(gradients_kernel, distances), out_shape=...  3.09 us
    pallas_call x1, Pallas kernels, last_gradients(): pl.pallas_call(last_gradients_kernel, out_shape=jax.ShapeDtypeStruct(tota...  1.74 us
    pallas_call x1, Pallas kernels, fetch(): pl.pallas_call(fetch_kernel, out_shape=pltpu.VMEM(x.shape, x.dtype), in_s...  1.6 us
    ppermute x3, waiting for transfers between devices, other_core(): return lax.ppermute(x, 'width', ((0, 1), (1, 0)))  1.33 us
  transfers between devices with their start and end apart: 20, of which 11 were waited for; matrix products, arithmetic and copies ran while one was open for 0% of the time, Pallas kernels for 18%

profile of v14, /device:TPU:0, one launch (start us, length us, event | category | flops | bytes accessed | tf_op | source)
XLA Modules:
  0.0 56.0 jit_solution(15985164680212209477)
XLA Ops:
  0.6 1.2 %prepare.1 = (bf16[1040,128]{1,0:T(8,128)(2,1)S(1)}, bf16[1040,128]{1,0:T(8,128)(2,1)S(1)}, bf16[1040,128]{1,0:T(8,128)(2,1)S(1)}, bf16[1040,128]{1,0:T(8,128)(2...) custom-call(s32[32]{0:T(128)} %refs_0_.1, s32[8,128]{1,0:T(8,128)} %bitcast.7, s32[32,128]{1,0:T(8,128)} %bitcast.5, ...), custom_call_target="tpu_custom_call" | custom-call | tf_op jit(solution)/shard_map/prepare/pallas_call | solution.py:117
  1.8 3.1 %collective-permute-start = (bf16[1040,128]{1,0:T(8,128)(2,1)S(1)}, bf16[1040,128]{1,0:T(8,128)(2,1)S(1)}, u32[]{:S(2)}, u32[]{:S(2)}) collective-permute-start(bf16[1040,128]{1,0:T(8,128)(2,1)S(1)} %get-tuple-element.34.refs_0_), channel_id=1, source_target_pairs={{0,4},{4,8},{8,12},{12,14},{14,10},{10,6},{6,2},{2,0},{1,5},{5,9},... | collective-permute-start | bytes 798728 | tf_op jit(solution)/shard_map/ppermute | solution.py:397
  4.9 0.0 collective-permute-start.1
  4.9 2.0 %collective-permute-start.3 = (bf16[1040,128]{1,0:T(8,128)(2,1)S(1)}, bf16[1040,128]{1,0:T(8,128)(2,1)S(1)}, u32[]{:S(2)}, u32[]{:S(2)}) collective-permute-start(bf16[1040,128]{1,0:T(8,128)(2,1)S(1)} %get-tuple-element.37), channel_id=1, source_target_pairs={{0,4},{4,8},{8,12},{12,14},{14,10},{10,6},{6,2},{2,0},{1,5},{5,9},... | collective-permute-start | bytes 798728 | tf_op jit(solution)/shard_map/ppermute | solution.py:397
  6.9 0.0 collective-permute-start.5
  6.9 1.6 %fetch.1.decoder = bf16[512,2048]{1,0:T(8,128)(2,1)S(1)} custom-call(bf16[512,2048]{1,0:T(8,128)(2,1)} %source.1), custom_call_target="tpu_custom_call" | custom-call | tf_op jit(solution)/shard_map/fetch/pallas_call | solution.py:144
  8.6 3.5 %collective-permute-done.refs_2_ = bf16[1040,128]{1,0:T(8,128)(2,1)S(1)} collective-permute-done((bf16[1040,128]{1,0:T(8,128)(2,1)S(1)}, bf16[1040,128]{1,0:T(8,128)(2,1)S(1)}, u32[]{:S(2)}, u32[]{:S(2)}) %collective-permute-start) | collective-permute-done | bytes 266272 | tf_op jit(solution)/shard_map/ppermute | solution.py:397
  12.1 2.2 %collective-permute-done.1.refs_5_ = bf16[1040,128]{1,0:T(8,128)(2,1)S(1)} collective-permute-done((bf16[1040,128]{1,0:T(8,128)(2,1)S(1)}, bf16[1040,128]{1,0:T(8,128)(2,1)S(1)}, u32[]{:S(2)}, u32[]{:S(2)}) %collective-permute-start.1) | collective-permute-done | bytes 266272 | tf_op jit(solution)/shard_map/ppermute | solution.py:397
  14.2 1.6 %collective-permute-start.2 = (bf16[1040,128]{1,0:T(8,128)(2,1)S(1)}, bf16[1040,128]{1,0:T(8,128)(2,1)S(1)}, u32[]{:S(2)}, u32[]{:S(2)}) collective-permute-start(bf16[1040,128]{1,0:T(8,128)(2,1)S(1)} %collective-permute-done.refs_2_), channel_id=1, source_target_pairs={{0,4},{4,8},{8,12},{12,14},{14,10},{10,6},{6,2},{2,0},{1,5},{5,9},... | collective-permute-start | bytes 798728 | tf_op jit(solution)/shard_map/ppermute | solution.py:397
  15.8 0.4 collective-permute-start.7
  16.3 1.5 %collective-permute-done.3.refs_3_ = bf16[1040,128]{1,0:T(8,128)(2,1)S(1)} collective-permute-done((bf16[1040,128]{1,0:T(8,128)(2,1)S(1)}, bf16[1040,128]{1,0:T(8,128)(2,1)S(1)}, u32[]{:S(2)}, u32[]{:S(2)}) %collective-permute-start.3) | collective-permute-done | bytes 266272 | tf_op jit(solution)/shard_map/ppermute | solution.py:397
  17.8 2.1 %collective-permute-start.4 = (bf16[1040,128]{1,0:T(8,128)(2,1)S(1)}, bf16[1040,128]{1,0:T(8,128)(2,1)S(1)}, u32[]{:S(2)}, u32[]{:S(2)}) collective-permute-start(bf16[1040,128]{1,0:T(8,128)(2,1)S(1)} %collective-permute-done.3.refs_3_), channel_id=1, source_target_pairs={{0,4},{4,8},{8,12},{12,14},{14,10},{10,6},{6,2},{2,0},{1,5},{5,9},... | collective-permute-start | bytes 798728 | tf_op jit(solution)/shard_map/ppermute | solution.py:397
  19.9 0.0 collective-permute-done.5.refs_4_
  19.9 0.0 collective-permute-start.6
  19.9 3.6 %collective-permute-done.2.refs_0_ = bf16[1040,128]{1,0:T(8,128)(2,1)S(1)} collective-permute-done((bf16[1040,128]{1,0:T(8,128)(2,1)S(1)}, bf16[1040,128]{1,0:T(8,128)(2,1)S(1)}, u32[]{:S(2)}, u32[]{:S(2)}) %collective-permute-start.2) | collective-permute-done | bytes 266272 | tf_op jit(solution)/shard_map/ppermute | solution.py:397
  23.6 2.0 %collective-permute-start.8 = (bf16[1040,128]{1,0:T(8,128)(2,1)S(1)}, bf16[1040,128]{1,0:T(8,128)(2,1)S(1)}, u32[]{:S(2)}, u32[]{:S(2)}) collective-permute-start(bf16[1040,128]{1,0:T(8,128)(2,1)S(1)} %collective-permute-done.2.refs_0_), channel_id=1, source_target_pairs={{0,4},{4,8},{8,12},{12,14},{14,10},{10,6},{6,2},{2,0},{1,5},{5,9},... | collective-permute-start | bytes 798728 | tf_op jit(solution)/shard_map/ppermute | solution.py:397
  25.6 0.0 collective-permute-done.7.refs_3_
  25.6 0.0 collective-permute-start.9
  25.6 1.3 %scores.4 = (f32[8,128]{1,0:T(8,128)S(1)}, f32[8,128]{1,0:T(8,128)S(1)}, f32[8,128]{1,0:T(8,128)S(1)}) custom-call(bf16[512,2048]{1,0:T(8,128)(2,1)S(1)} %fetch.1.decoder, f32[8,128]{1,0:T(8,128)S(1)} %get-tuple-element.33.own_facts, bf16[1040,128]{1,0:T(8,128)(2,1)S(1)} %get-tuple-element.34.refs_0_, bf16[1040,128]{1,0:T(8,128)(2,1)S(1)} %get-tuple-element.35.refs_1_, ...), custom_call_target="tpu_custom_call" | custom-call | tf_op jit(solution)/shard_map/scores/pallas_call | solution.py:258
  27.0 2.3 %collective-permute-done.4.onward = bf16[1040,128]{1,0:T(8,128)(2,1)S(1)} collective-permute-done((bf16[1040,128]{1,0:T(8,128)(2,1)S(1)}, bf16[1040,128]{1,0:T(8,128)(2,1)S(1)}, u32[]{:S(2)}, u32[]{:S(2)}) %collective-permute-start.4) | collective-permute-done | bytes 266272 | tf_op jit(solution)/shard_map/ppermute | solution.py:397
  29.3 2.1 %collective-permute-done.6.back = bf16[1040,128]{1,0:T(8,128)(2,1)S(1)} collective-permute-done((bf16[1040,128]{1,0:T(8,128)(2,1)S(1)}, bf16[1040,128]{1,0:T(8,128)(2,1)S(1)}, u32[]{:S(2)}, u32[]{:S(2)}) %collective-permute-start.6) | collective-permute-done | bytes 266272 | tf_op jit(solution)/shard_map/ppermute | solution.py:397
  31.4 0.1 stamp.1
  31.4 1.6 %collective-permute-start.11 = (bf16[1040,128]{1,0:T(8,128)(2,1)S(1)}, bf16[1040,128]{1,0:T(8,128)(2,1)S(1)}, u32[]{:S(2)}, u32[]{:S(2)}) collective-permute-start(bf16[1040,128]{1,0:T(8,128)(2,1)S(1)} %get-tuple-element.43.refs_1_), channel_id=1, source_target_pairs={{0,4},{4,8},{8,12},{12,14},{14,10},{10,6},{6,2},{2,0},{1,5},{5,9},... | collective-permute-start | bytes 798728 | tf_op jit(solution)/shard_map/ppermute | solution.py:397
  33.1 0.4 collective-permute-start.12
  33.5 0.8 %scores.5 = (f32[8,128]{1,0:T(8,128)S(1)}, f32[8,128]{1,0:T(8,128)S(1)}) custom-call(bf16[512,2048]{1,0:T(8,128)(2,1)S(1)} %fetch.1.decoder, f32[8,128]{1,0:T(8,128)S(1)} %get-tuple-element.33.own_facts, bf16[1040,128]{1,0:T(8,128)(2,1)S(1)} %collective-permute-done.2.refs_0_, bf16[1040,128]{1,0:T(8,128)(2,1)S(1)} %get-tuple-element.43.refs_1_, ...), custom_call_target="tpu_custom_call" | custom-call | tf_op jit(solution)/shard_map/scores/pallas_call | solution.py:258
  34.3 0.1 collective-permute-start.10
  34.4 1.3 %gradients.3.refs_4_ = f32[512,2048]{1,0:T(8,128)S(1)} custom-call(f32[8,128]{1,0:T(8,128)S(1)} %get-tuple-element.33.own_facts, bf16[1040,128]{1,0:T(8,128)(2,1)S(1)} %get-tuple-element.34.refs_0_, bf16[1040,128]{1,0:T(8,128)(2,1)S(1)} %get-tuple-element.35.refs_1_, bf16[1040,128]{1,0:T(8,128)(2,1)S(1)} %collective-permute-done.refs_2_, ...), custom_call_target="tpu_custom_call" | custom-call | tf_op jit(solution)/shard_map/gradients/pallas_call | solution.py:279
  35.7 0.9 %gradients.4.refs_4_ = f32[512,2048]{1,0:T(8,128)S(1)} custom-call(f32[8,128]{1,0:T(8,128)S(1)} %get-tuple-element.33.own_facts, bf16[1040,128]{1,0:T(8,128)(2,1)S(1)} %collective-permute-done.2.refs_0_, bf16[1040,128]{1,0:T(8,128)(2,1)S(1)} %get-tuple-element.43.refs_1_, ...), custom_call_target="tpu_custom_call", output_to_operand_aliasing={{}: (5, {})} | custom-call | tf_op jit(solution)/shard_map/gradients/pallas_call | solution.py:279
  36.6 0.0 collective-permute-done.10
  36.7 0.0 collective-permute-done.8.refs_0_
  36.7 0.4 collective-permute-done.9.refs_3_
  37.1 1.6 %collective-permute-start.14 = (bf16[1040,128]{1,0:T(8,128)(2,1)S(1)}, bf16[1040,128]{1,0:T(8,128)(2,1)S(1)}, u32[]{:S(2)}, u32[]{:S(2)}) collective-permute-start(bf16[1040,128]{1,0:T(8,128)(2,1)S(1)} %collective-permute-done.8.refs_0_), channel_id=1, source_target_pairs={{0,4},{4,8},{8,12},{12,14},{14,10},{10,6},{6,2},{2,0},{1,5},{5,9},... | collective-permute-start | bytes 798728 | tf_op jit(solution)/shard_map/ppermute | solution.py:397
  38.6 0.4 collective-permute-start.15
  39.1 1.4 %collective-permute-start.18 = (f32[24,128]{1,0:T(8,128)S(1)}, f32[24,128]{1,0:T(8,128)S(1)}, u32[]{:S(2)}, u32[]{:S(2)}) collective-permute-start(f32[24,128]{1,0:T(8,128)S(1)} %concatenate.3), channel_id=1, source_target_pairs={{0,6},{1,9},{4,2},{5,13},{8,0},{9,15},{12,4},{13,11},{14,8},{15,7}... | collective-permute-start | bytes 36872 | tf_op jit(solution)/shard_map/ppermute | solution.py:415
  40.5 0.0 collective-permute-done.11.refs_1_.onward
  40.5 0.9 %collective-permute-done.12.refs_2_.back = bf16[1040,128]{1,0:T(8,128)(2,1)S(1)} collective-permute-done((bf16[1040,128]{1,0:T(8,128)(2,1)S(1)}, bf16[1040,128]{1,0:T(8,128)(2,1)S(1)}, u32[]{:S(2)}, u32[]{:S(2)}) %collective-permute-start.12) | collective-permute-done | bytes 266272 | tf_op jit(solution)/shard_map/ppermute | solution.py:397
  41.4 0.8 %scores.6 = (f32[8,128]{1,0:T(8,128)S(1)}, f32[8,128]{1,0:T(8,128)S(1)}) custom-call(bf16[512,2048]{1,0:T(8,128)(2,1)S(1)} %fetch.1.decoder, f32[8,128]{1,0:T(8,128)S(1)} %get-tuple-element.33.own_facts, bf16[1040,128]{1,0:T(8,128)(2,1)S(1)} %collective-permute-done.8.refs_0_, bf16[1040,128]{1,0:T(8,128)(2,1)S(1)} %collective-permute-done.11.refs_1_.onward, ...), custom_call_target="tpu_custom_call" | custom-call | tf_op jit(solution)/shard_map/scores/pallas_call | solution.py:258
  42.2 0.1 collective-permute-start.13
  42.3 0.9 %gradients.5.total = f32[512,2048]{1,0:T(8,128)S(1)} custom-call(f32[8,128]{1,0:T(8,128)S(1)} %get-tuple-element.33.own_facts, bf16[1040,128]{1,0:T(8,128)(2,1)S(1)} %collective-permute-done.8.refs_0_, bf16[1040,128]{1,0:T(8,128)(2,1)S(1)} %collective-permute-done.11.refs_1_.onward, ...), custom_call_target="tpu_custom_call", output_to_operand_aliasing={{}: (5, {})} | custom-call | tf_op jit(solution)/shard_map/gradients/pallas_call | solution.py:279
  43.2 0.3 collective-permute-done.13
  43.5 3.5 %collective-permute-start.16 = (f32[8,128]{1,0:T(8,128)S(1)}, f32[8,128]{1,0:T(8,128)S(1)}, u32[]{:S(2)}, u32[]{:S(2)}) collective-permute-start(f32[8,128]{1,0:T(8,128)S(1)} %add.12), channel_id=1, source_target_pairs={{0,10},{1,13},{4,6},{5,15},{8,2},{9,11},{12,0},{13,7},{14,4},{15,3... | collective-permute-start | bytes 12296 | tf_op jit(solution)/shard_map/ppermute | solution.py:415
  47.0 0.0 collective-permute-done.14.left.refs_0_
  47.0 0.0 collective-permute-done.15.right.refs_1_
  47.0 0.7 %scores.7 = f32[8,128]{1,0:T(8,128)S(1)} custom-call(bf16[512,2048]{1,0:T(8,128)(2,1)S(1)} %fetch.1.decoder, f32[8,128]{1,0:T(8,128)S(1)} %get-tuple-element.33.own_facts, bf16[1040,128]{1,0:T(8,128)(2,1)S(1)} %collective-permute-done.14.left.refs_0_, bf16[1040,128]{1,0:T(8,128)(2,1)S(1)} %collective-permute-done.15.right.refs_1_), custom_call_target="tpu_custom_call" | custom-call | tf_op jit(solution)/shard_map/scores/pallas_call | solution.py:258
  47.7 3.6 %collective-permute-start.17 = (f32[8,128]{1,0:T(8,128)S(1)}, f32[8,128]{1,0:T(8,128)S(1)}, u32[]{:S(2)}, u32[]{:S(2)}) collective-permute-start(f32[8,128]{1,0:T(8,128)S(1)} %scores.7), channel_id=1, source_target_pairs={{0,14},{4,10},{8,6},{12,2},{14,0},{10,4},{6,8},{2,12},{1,15},{5,11... | collective-permute-start | bytes 12296 | tf_op jit(solution)/shard_map/ppermute | solution.py:397
  51.3 0.0 collective-permute-done.18
  51.3 0.0 collective-permute-done.16.third
  51.3 1.7 %last_gradients.1 = bf16[512,2048]{1,0:T(8,128)(2,1)} custom-call(bf16[1040,128]{1,0:T(8,128)(2,1)S(1)} %collective-permute-done.14.left.refs_0_, bf16[1040,128]{1,0:T(8,128)(2,1)S(1)} %collective-permute-done.15.right.refs_1_, f32[512,2048]{1,0:T(8,128)S(1)} %gradients.5.total), custom_call_target="tpu_custom_call" | custom-call | tf_op jit(solution)/shard_map/last_gradients/pallas_call | solution.py:306
  53.1 1.0 %collective-permute-done.17.opposite = f32[8,128]{1,0:T(8,128)S(1)} collective-permute-done((f32[8,128]{1,0:T(8,128)S(1)}, f32[8,128]{1,0:T(8,128)S(1)}, u32[]{:S(2)}, u32[]{:S(2)}) %collective-permute-start.17) | collective-permute-done | bytes 4128 | tf_op jit(solution)/shard_map/ppermute | solution.py:397
  54.1 0.2 collective-permute-start.19
  54.3 1.1 %collective-permute-done.19 = f32[32,128]{1,0:T(8,128)S(1)} collective-permute-done((f32[32,128]{1,0:T(8,128)S(1)}, f32[32,128]{1,0:T(8,128)S(1)}, u32[]{:S(2)}, u32[]{:S(2)}) %collective-permute-start.19) | collective-permute-done | bytes 16416 | tf_op jit(solution)/shard_map/ppermute | solution.py:408
  55.4 0.6 %add_bitcast_fusion = f32[128,32]{0,1:T(8,128)} fusion(f32[32,128]{1,0:T(8,128)S(1)} %unpack.1, f32[32,128]{1,0:T(8,128)S(1)} %collective-permute-done.19), kind=kLoop, calls=%fused_computation | loop fusion | flops 4096 | bytes 49152 | tf_op jit(solution)/shard_map/transpose | solution.py:454
  (5 shorter events, 0.0 us)
Async XLA Ops:
  1.8 10.2 %collective-permute-start = (bf16[1040,128]{1,0:T(8,128)(2,1)S(1)}, bf16[1040,128]{1,0:T(8,128)(2,1)S(1)}, u32[]{:S(2)}, u32[]{:S(2)}) collective-permute-start(bf16[1040,128]{1,0:T(8,128)(2,1)S(1)} %get-tuple-element.34.refs_0_), channel_id=1, source_target_pairs={{0,4},{4,8},{8,12},{12,14},{14,10},{10,6},{6,2},{2,0},{1,5},{5,9},... | collective-permute-start | bytes 798728 | tf_op jit(solution)/shard_map/ppermute | solution.py:397
  4.9 9.3 %collective-permute-start.1 = (bf16[1040,128]{1,0:T(8,128)(2,1)S(1)}, bf16[1040,128]{1,0:T(8,128)(2,1)S(1)}, u32[]{:S(2)}, u32[]{:S(2)}) collective-permute-start(bf16[1040,128]{1,0:T(8,128)(2,1)S(1)} %get-tuple-element.35.refs_1_), channel_id=1, source_target_pairs={{0,2},{4,0},{8,4},{12,8},{14,12},{10,14},{6,10},{2,6},{1,3},{5,1},... | collective-permute-start | bytes 798728 | tf_op jit(solution)/shard_map/ppermute | solution.py:397
  4.9 12.8 %collective-permute-start.3 = (bf16[1040,128]{1,0:T(8,128)(2,1)S(1)}, bf16[1040,128]{1,0:T(8,128)(2,1)S(1)}, u32[]{:S(2)}, u32[]{:S(2)}) collective-permute-start(bf16[1040,128]{1,0:T(8,128)(2,1)S(1)} %get-tuple-element.37), channel_id=1, source_target_pairs={{0,4},{4,8},{8,12},{12,14},{14,10},{10,6},{6,2},{2,0},{1,5},{5,9},... | collective-permute-start | bytes 798728 | tf_op jit(solution)/shard_map/ppermute | solution.py:397
  6.9 13.0 %collective-permute-start.5 = (bf16[1040,128]{1,0:T(8,128)(2,1)S(1)}, bf16[1040,128]{1,0:T(8,128)(2,1)S(1)}, u32[]{:S(2)}, u32[]{:S(2)}) collective-permute-start(bf16[1040,128]{1,0:T(8,128)(2,1)S(1)} %get-tuple-element.38), channel_id=1, source_target_pairs={{0,2},{4,0},{8,4},{12,8},{14,12},{10,14},{6,10},{2,6},{1,3},{5,1},... | collective-permute-start | bytes 798728 | tf_op jit(solution)/shard_map/ppermute | solution.py:397
  14.2 9.3 %collective-permute-start.2 = (bf16[1040,128]{1,0:T(8,128)(2,1)S(1)}, bf16[1040,128]{1,0:T(8,128)(2,1)S(1)}, u32[]{:S(2)}, u32[]{:S(2)}) collective-permute-start(bf16[1040,128]{1,0:T(8,128)(2,1)S(1)} %collective-permute-done.refs_2_), channel_id=1, source_target_pairs={{0,4},{4,8},{8,12},{12,14},{14,10},{10,6},{6,2},{2,0},{1,5},{5,9},... | collective-permute-start | bytes 798728 | tf_op jit(solution)/shard_map/ppermute | solution.py:397
  15.8 9.8 %collective-permute-start.7 = (bf16[1040,128]{1,0:T(8,128)(2,1)S(1)}, bf16[1040,128]{1,0:T(8,128)(2,1)S(1)}, u32[]{:S(2)}, u32[]{:S(2)}) collective-permute-start(bf16[1040,128]{1,0:T(8,128)(2,1)S(1)} %collective-permute-done.1.refs_5_), channel_id=1, source_target_pairs={{0,2},{4,0},{8,4},{12,8},{14,12},{10,14},{6,10},{2,6},{1,3},{5,1},... | collective-permute-start | bytes 798728 | tf_op jit(solution)/shard_map/ppermute | solution.py:397
  17.8 11.5 %collective-permute-start.4 = (bf16[1040,128]{1,0:T(8,128)(2,1)S(1)}, bf16[1040,128]{1,0:T(8,128)(2,1)S(1)}, u32[]{:S(2)}, u32[]{:S(2)}) collective-permute-start(bf16[1040,128]{1,0:T(8,128)(2,1)S(1)} %collective-permute-done.3.refs_3_), channel_id=1, source_target_pairs={{0,4},{4,8},{8,12},{12,14},{14,10},{10,6},{6,2},{2,0},{1,5},{5,9},... | collective-permute-start | bytes 798728 | tf_op jit(solution)/shard_map/ppermute | solution.py:397
  19.9 11.4 %collective-permute-start.6 = (bf16[1040,128]{1,0:T(8,128)(2,1)S(1)}, bf16[1040,128]{1,0:T(8,128)(2,1)S(1)}, u32[]{:S(2)}, u32[]{:S(2)}) collective-permute-start(bf16[1040,128]{1,0:T(8,128)(2,1)S(1)} %collective-permute-done.5.refs_4_), channel_id=1, source_target_pairs={{0,2},{4,0},{8,4},{12,8},{14,12},{10,14},{6,10},{2,6},{1,3},{5,1},... | collective-permute-start | bytes 798728 | tf_op jit(solution)/shard_map/ppermute | solution.py:397
  23.6 13.1 %collective-permute-start.8 = (bf16[1040,128]{1,0:T(8,128)(2,1)S(1)}, bf16[1040,128]{1,0:T(8,128)(2,1)S(1)}, u32[]{:S(2)}, u32[]{:S(2)}) collective-permute-start(bf16[1040,128]{1,0:T(8,128)(2,1)S(1)} %collective-permute-done.2.refs_0_), channel_id=1, source_target_pairs={{0,4},{4,8},{8,12},{12,14},{14,10},{10,6},{6,2},{2,0},{1,5},{5,9},... | collective-permute-start | bytes 798728 | tf_op jit(solution)/shard_map/ppermute | solution.py:397
  25.6 11.4 %collective-permute-start.9 = (bf16[1040,128]{1,0:T(8,128)(2,1)S(1)}, bf16[1040,128]{1,0:T(8,128)(2,1)S(1)}, u32[]{:S(2)}, u32[]{:S(2)}) collective-permute-start(bf16[1040,128]{1,0:T(8,128)(2,1)S(1)} %collective-permute-done.7.refs_3_), channel_id=1, source_target_pairs={{0,2},{4,0},{8,4},{12,8},{14,12},{10,14},{6,10},{2,6},{1,3},{5,1},... | collective-permute-start | bytes 798728 | tf_op jit(solution)/shard_map/ppermute | solution.py:397
  31.4 9.0 %collective-permute-start.11 = (bf16[1040,128]{1,0:T(8,128)(2,1)S(1)}, bf16[1040,128]{1,0:T(8,128)(2,1)S(1)}, u32[]{:S(2)}, u32[]{:S(2)}) collective-permute-start(bf16[1040,128]{1,0:T(8,128)(2,1)S(1)} %get-tuple-element.43.refs_1_), channel_id=1, source_target_pairs={{0,4},{4,8},{8,12},{12,14},{14,10},{10,6},{6,2},{2,0},{1,5},{5,9},... | collective-permute-start | bytes 798728 | tf_op jit(solution)/shard_map/ppermute | solution.py:397
  33.1 8.4 %collective-permute-start.12 = (bf16[1040,128]{1,0:T(8,128)(2,1)S(1)}, bf16[1040,128]{1,0:T(8,128)(2,1)S(1)}, u32[]{:S(2)}, u32[]{:S(2)}) collective-permute-start(bf16[1040,128]{1,0:T(8,128)(2,1)S(1)} %get-tuple-element.44.refs_2_), channel_id=1, source_target_pairs={{0,2},{4,0},{8,4},{12,8},{14,12},{10,14},{6,10},{2,6},{1,3},{5,1},... | collective-permute-start | bytes 798728 | tf_op jit(solution)/shard_map/ppermute | solution.py:397
  34.3 2.3 %collective-permute-start.10 = (f32[8,128]{1,0:T(8,128)S(1)}, f32[8,128]{1,0:T(8,128)S(1)}, u32[]{:S(2)}, u32[]{:S(2)}) collective-permute-start(f32[8,128]{1,0:T(8,128)S(1)} %get-tuple-element.46), channel_id=1, source_target_pairs={{0,1},{1,0},{2,3},{3,2},{4,5},{5,4},{6,7},{7,6},{8,9},{9,8},{10,11... | collective-permute-start | bytes 12296 | tf_op jit(solution)/shard_map/ppermute | solution.py:408
  37.1 9.9 %collective-permute-start.14 = (bf16[1040,128]{1,0:T(8,128)(2,1)S(1)}, bf16[1040,128]{1,0:T(8,128)(2,1)S(1)}, u32[]{:S(2)}, u32[]{:S(2)}) collective-permute-start(bf16[1040,128]{1,0:T(8,128)(2,1)S(1)} %collective-permute-done.8.refs_0_), channel_id=1, source_target_pairs={{0,4},{4,8},{8,12},{12,14},{14,10},{10,6},{6,2},{2,0},{1,5},{5,9},... | collective-permute-start | bytes 798728 | tf_op jit(solution)/shard_map/ppermute | solution.py:397
  38.6 8.4 %collective-permute-start.15 = (bf16[1040,128]{1,0:T(8,128)(2,1)S(1)}, bf16[1040,128]{1,0:T(8,128)(2,1)S(1)}, u32[]{:S(2)}, u32[]{:S(2)}) collective-permute-start(bf16[1040,128]{1,0:T(8,128)(2,1)S(1)} %collective-permute-done.9.refs_3_), channel_id=1, source_target_pairs={{0,2},{4,0},{8,4},{12,8},{14,12},{10,14},{6,10},{2,6},{1,3},{5,1},... | collective-permute-start | bytes 798728 | tf_op jit(solution)/shard_map/ppermute | solution.py:397
  39.1 12.2 %collective-permute-start.18 = (f32[24,128]{1,0:T(8,128)S(1)}, f32[24,128]{1,0:T(8,128)S(1)}, u32[]{:S(2)}, u32[]{:S(2)}) collective-permute-start(f32[24,128]{1,0:T(8,128)S(1)} %concatenate.3), channel_id=1, source_target_pairs={{0,6},{1,9},{4,2},{5,13},{8,0},{9,15},{12,4},{13,11},{14,8},{15,7}... | collective-permute-start | bytes 36872 | tf_op jit(solution)/shard_map/ppermute | solution.py:415
  42.2 1.2 %collective-permute-start.13 = (f32[8,128]{1,0:T(8,128)S(1)}, f32[8,128]{1,0:T(8,128)S(1)}, u32[]{:S(2)}, u32[]{:S(2)}) collective-permute-start(f32[8,128]{1,0:T(8,128)S(1)} %get-tuple-element.51), channel_id=1, source_target_pairs={{0,1},{1,0},{2,3},{3,2},{4,5},{5,4},{6,7},{7,6},{8,9},{9,8},{10,11... | collective-permute-start | bytes 12296 | tf_op jit(solution)/shard_map/ppermute | solution.py:408
  43.5 7.9 %collective-permute-start.16 = (f32[8,128]{1,0:T(8,128)S(1)}, f32[8,128]{1,0:T(8,128)S(1)}, u32[]{:S(2)}, u32[]{:S(2)}) collective-permute-start(f32[8,128]{1,0:T(8,128)S(1)} %add.12), channel_id=1, source_target_pairs={{0,10},{1,13},{4,6},{5,15},{8,2},{9,11},{12,0},{13,7},{14,4},{15,3... | collective-permute-start | bytes 12296 | tf_op jit(solution)/shard_map/ppermute | solution.py:415
  47.7 6.4 %collective-permute-start.17 = (f32[8,128]{1,0:T(8,128)S(1)}, f32[8,128]{1,0:T(8,128)S(1)}, u32[]{:S(2)}, u32[]{:S(2)}) collective-permute-start(f32[8,128]{1,0:T(8,128)S(1)} %scores.7), channel_id=1, source_target_pairs={{0,14},{4,10},{8,6},{12,2},{14,0},{10,4},{6,8},{2,12},{1,15},{5,11... | collective-permute-start | bytes 12296 | tf_op jit(solution)/shard_map/ppermute | solution.py:397
  54.1 1.2 %collective-permute-start.19 = (f32[32,128]{1,0:T(8,128)S(1)}, f32[32,128]{1,0:T(8,128)S(1)}, u32[]{:S(2)}, u32[]{:S(2)}) collective-permute-start(f32[32,128]{1,0:T(8,128)S(1)} %unpack.1), channel_id=1, source_target_pairs={{0,1},{1,0},{2,3},{3,2},{4,5},{5,4},{6,7},{7,6},{8,9},{9,8},{10,11... | collective-permute-start | bytes 49160 | tf_op jit(solution)/shard_map/ppermute | solution.py:408

commit v15 on v14

--- a/solution.py
+++ b/solution.py
@@ -265,6 +265,46 @@
     )(kept(decoder), kept(own_facts), *pieces)
 
 
+def half_kernel(decoder, piece, partial):
+    cut = decoder.shape[1] // 2
+    rows = columns_of([piece], partial.shape[1], range(cut // 128))
+    partial[...] = lax.dot_general(
+        decoder[:, cut:], rows, (((1,), (1,)), ((), ())), preferred_element_type=jnp.float32
+    )
+
+
+def half_scores(decoder, piece, tok_rows):
+    return pl.pallas_call(
+        half_kernel,
+        out_shape=pltpu.VMEM((decoder.shape[0], tok_rows), jnp.float32),
+        in_specs=[VMEM] * 2,
+        out_specs=VMEM,
+        compiler_params=limit(8),
+        name="half_scores",
+    )(kept(decoder), kept(piece))
+
+
+def rest_kernel(decoder, partial, piece, picked):
+    cut = decoder.shape[1] // 2
+    rows = columns_of([piece], partial.shape[1], range(cut // 128))
+    scores = partial[...] + lax.dot_general(
+        decoder[:, :cut], rows, (((1,), (1,)), ((), ())), preferred_element_type=jnp.float32
+    )
+    facts = facts_in(piece, None, 4)
+    picked[...] = jnp.concatenate(pick(scores, facts) * 2, axis=0)
+
+
+def rest_scores(decoder, partial, piece):
+    return pl.pallas_call(
+        rest_kernel,
+        out_shape=pltpu.VMEM((2 * KPB, partial.shape[1]), jnp.float32),
+        in_specs=[VMEM] * 3,
+        out_specs=VMEM,
+        compiler_params=limit(8),
+        name="rest_scores",
+    )(kept(decoder), kept(partial), kept(piece))
+
+
 def gradients_kernel(distances, own_facts, *refs):
     pieces, refs = refs[: 2 * len(distances)], refs[2 * len(distances) :]
     total = refs[-1]
@@ -443,8 +483,12 @@
     third = mine + other_core(others)
     total, third = lax.optimization_barrier((total, third))
     third = return_by(3, third)
-    total, first_4 = lax.optimization_barrier((total, first_4))
-    (opposite,) = scores_of((4,), [first_4], decoder, own_facts)
+    last_left, last_right = first_4
+    total, last_right = lax.optimization_barrier((total, last_right))
+    partial = half_scores(decoder, last_right, tok_rows)
+    partial, last_left = lax.optimization_barrier((partial, last_left))
+    opposite = rest_scores(decoder, partial, last_left)
+    first_4 = last_left, last_right
     opposite = shift(opposite, -owners // 2)
     total, third = lax.optimization_barrier((total, third))
     decoder_grad = last_gradients(first_4, total)

time: 56.2 us -> 56.6 us (level)
  waiting for transfers between devices: 18.9 us -> 20.5 us
  starting transfers between devices: 24.2 us -> 22.9 us
    ppermute x15, waiting for transfers between devices: 17.6 us -> 19.1 us  [shift(): return lax.ppermute(x, 'dp', pairs)]
    ppermute x2, starting transfers between devices: 4.89 us -> 3.77 us  [return_by(): return lax.ppermute(x, ('dp', 'width'), pairs)]
    pallas_call x0 -> x2, Pallas kernels: none -> 0.89 us  [the longest x1 0.46 us: rest_scores(): pl.pallas_call(rest_kernel, out_shape=pltpu.VMEM((2 * KPB, partial.shape[...]
    pallas_call x4 -> x3, Pallas kernels: 3.71 us -> 2.98 us  [scores_of(): pl.pallas_call(functools.partial(scores_kernel, distances, split), out_sh...]
where the time goes in v15:
time: 56.6 us; the launch traced here: 56.4 us
  starting transfers between devices  22.9 us (40%)
  waiting for transfers between devices  20.5 us (36%)
  Pallas kernels  11.6 us (20%)
  between operations  0.79 us (1%)
  other arithmetic  0.62 us (1%)
    ppermute x15, waiting for transfers between devices, shift(): return lax.ppermute(x, 'dp', pairs)  19.1 us
    ppermute x15, starting transfers between devices, shift(): return lax.ppermute(x, 'dp', pairs)  18.8 us
    ppermute x2, starting transfers between devices, return_by(): return lax.ppermute(x, ('dp', 'width'), pairs)  3.77 us
    pallas_call x3, Pallas kernels, gradients_of(): pl.pallas_call(functools.partial(gradients_kernel, distances), out_shape=...  3.09 us
    pallas_call x3, Pallas kernels, scores_of(): pl.pallas_call(functools.partial(scores_kernel, distances, split), out_sh...  2.98 us
    pallas_call x1, Pallas kernels, last_gradients(): pl.pallas_call(last_gradients_kernel, out_shape=jax.ShapeDtypeStruct(tota...  1.75 us
    pallas_call x1, Pallas kernels, fetch(): pl.pallas_call(fetch_kernel, out_shape=pltpu.VMEM(x.shape, x.dtype), in_s...  1.6 us
    ppermute x3, waiting for transfers between devices, other_core(): return lax.ppermute(x, 'width', ((0, 1), (1, 0)))  1.33 us
  transfers between devices with their start and end apart: 20, of which 11 were waited for; matrix products, arithmetic and copies ran while one was open for 0% of the time, Pallas kernels for 18%

profile of v15, /device:TPU:0, one launch (start us, length us, event | category | flops | bytes accessed | tf_op | source)
XLA Modules:
  0.0 56.4 jit_solution(5849000152907983993)
XLA Ops:
  0.6 1.2 %prepare.1 = (bf16[1040,128]{1,0:T(8,128)(2,1)S(1)}, bf16[1040,128]{1,0:T(8,128)(2,1)S(1)}, bf16[1040,128]{1,0:T(8,128)(2,1)S(1)}, bf16[1040,128]{1,0:T(8,128)(2...) custom-call(s32[32]{0:T(128)} %refs_0_.1, s32[8,128]{1,0:T(8,128)} %bitcast.7, s32[32,128]{1,0:T(8,128)} %bitcast.5, ...), custom_call_target="tpu_custom_call" | custom-call | tf_op jit(solution)/shard_map/prepare/pallas_call | solution.py:117
  1.8 3.1 %collective-permute-start = (bf16[1040,128]{1,0:T(8,128)(2,1)S(1)}, bf16[1040,128]{1,0:T(8,128)(2,1)S(1)}, u32[]{:S(2)}, u32[]{:S(2)}) collective-permute-start(bf16[1040,128]{1,0:T(8,128)(2,1)S(1)} %get-tuple-element.34.refs_0_), channel_id=1, source_target_pairs={{0,4},{4,8},{8,12},{12,14},{14,10},{10,6},{6,2},{2,0},{1,5},{5,9},... | collective-permute-start | bytes 798728 | tf_op jit(solution)/shard_map/ppermute | solution.py:437
  4.9 0.0 collective-permute-start.1
  4.9 2.0 %collective-permute-start.3 = (bf16[1040,128]{1,0:T(8,128)(2,1)S(1)}, bf16[1040,128]{1,0:T(8,128)(2,1)S(1)}, u32[]{:S(2)}, u32[]{:S(2)}) collective-permute-start(bf16[1040,128]{1,0:T(8,128)(2,1)S(1)} %get-tuple-element.39), channel_id=1, source_target_pairs={{0,4},{4,8},{8,12},{12,14},{14,10},{10,6},{6,2},{2,0},{1,5},{5,9},... | collective-permute-start | bytes 798728 | tf_op jit(solution)/shard_map/ppermute | solution.py:437
  6.9 0.0 collective-permute-start.5
  6.9 1.6 %fetch.1.decoder = bf16[512,2048]{1,0:T(8,128)(2,1)S(1)} custom-call(bf16[512,2048]{1,0:T(8,128)(2,1)} %source.1), custom_call_target="tpu_custom_call" | custom-call | tf_op jit(solution)/shard_map/fetch/pallas_call | solution.py:144
  8.6 3.5 %collective-permute-done.refs_2_ = bf16[1040,128]{1,0:T(8,128)(2,1)S(1)} collective-permute-done((bf16[1040,128]{1,0:T(8,128)(2,1)S(1)}, bf16[1040,128]{1,0:T(8,128)(2,1)S(1)}, u32[]{:S(2)}, u32[]{:S(2)}) %collective-permute-start) | collective-permute-done | bytes 266272 | tf_op jit(solution)/shard_map/ppermute | solution.py:437
  12.1 2.2 %collective-permute-done.1.refs_5_ = bf16[1040,128]{1,0:T(8,128)(2,1)S(1)} collective-permute-done((bf16[1040,128]{1,0:T(8,128)(2,1)S(1)}, bf16[1040,128]{1,0:T(8,128)(2,1)S(1)}, u32[]{:S(2)}, u32[]{:S(2)}) %collective-permute-start.1) | collective-permute-done | bytes 266272 | tf_op jit(solution)/shard_map/ppermute | solution.py:437
  14.2 1.6 %collective-permute-start.2 = (bf16[1040,128]{1,0:T(8,128)(2,1)S(1)}, bf16[1040,128]{1,0:T(8,128)(2,1)S(1)}, u32[]{:S(2)}, u32[]{:S(2)}) collective-permute-start(bf16[1040,128]{1,0:T(8,128)(2,1)S(1)} %collective-permute-done.refs_2_), channel_id=1, source_target_pairs={{0,4},{4,8},{8,12},{12,14},{14,10},{10,6},{6,2},{2,0},{1,5},{5,9},... | collective-permute-start | bytes 798728 | tf_op jit(solution)/shard_map/ppermute | solution.py:437
  15.8 0.4 collective-permute-start.7
  16.3 1.5 %collective-permute-done.3.refs_3_ = bf16[1040,128]{1,0:T(8,128)(2,1)S(1)} collective-permute-done((bf16[1040,128]{1,0:T(8,128)(2,1)S(1)}, bf16[1040,128]{1,0:T(8,128)(2,1)S(1)}, u32[]{:S(2)}, u32[]{:S(2)}) %collective-permute-start.3) | collective-permute-done | bytes 266272 | tf_op jit(solution)/shard_map/ppermute | solution.py:437
  17.8 2.1 %collective-permute-start.4 = (bf16[1040,128]{1,0:T(8,128)(2,1)S(1)}, bf16[1040,128]{1,0:T(8,128)(2,1)S(1)}, u32[]{:S(2)}, u32[]{:S(2)}) collective-permute-start(bf16[1040,128]{1,0:T(8,128)(2,1)S(1)} %collective-permute-done.3.refs_3_), channel_id=1, source_target_pairs={{0,4},{4,8},{8,12},{12,14},{14,10},{10,6},{6,2},{2,0},{1,5},{5,9},... | collective-permute-start | bytes 798728 | tf_op jit(solution)/shard_map/ppermute | solution.py:437
  19.9 0.0 collective-permute-done.5.refs_4_
  19.9 0.0 collective-permute-start.6
  19.9 3.6 %collective-permute-done.2.refs_0_ = bf16[1040,128]{1,0:T(8,128)(2,1)S(1)} collective-permute-done((bf16[1040,128]{1,0:T(8,128)(2,1)S(1)}, bf16[1040,128]{1,0:T(8,128)(2,1)S(1)}, u32[]{:S(2)}, u32[]{:S(2)}) %collective-permute-start.2) | collective-permute-done | bytes 266272 | tf_op jit(solution)/shard_map/ppermute | solution.py:437
  23.6 2.0 %collective-permute-start.8 = (bf16[1040,128]{1,0:T(8,128)(2,1)S(1)}, bf16[1040,128]{1,0:T(8,128)(2,1)S(1)}, u32[]{:S(2)}, u32[]{:S(2)}) collective-permute-start(bf16[1040,128]{1,0:T(8,128)(2,1)S(1)} %collective-permute-done.2.refs_0_), channel_id=1, source_target_pairs={{0,4},{4,8},{8,12},{12,14},{14,10},{10,6},{6,2},{2,0},{1,5},{5,9},... | collective-permute-start | bytes 798728 | tf_op jit(solution)/shard_map/ppermute | solution.py:437
  25.6 0.0 collective-permute-done.7.refs_3_
  25.6 0.0 collective-permute-start.9
  25.6 1.3 %scores.3 = (f32[8,128]{1,0:T(8,128)S(1)}, f32[8,128]{1,0:T(8,128)S(1)}, f32[8,128]{1,0:T(8,128)S(1)}) custom-call(bf16[512,2048]{1,0:T(8,128)(2,1)S(1)} %fetch.1.decoder, f32[8,128]{1,0:T(8,128)S(1)} %get-tuple-element.37.own_facts, bf16[1040,128]{1,0:T(8,128)(2,1)S(1)} %get-tuple-element.34.refs_0_, bf16[1040,128]{1,0:T(8,128)(2,1)S(1)} %get-tuple-element.35.refs_1_, ...), custom_call_target="tpu_custom_call" | custom-call | tf_op jit(solution)/shard_map/scores/pallas_call | solution.py:258
  27.0 2.3 %collective-permute-done.4.onward = bf16[1040,128]{1,0:T(8,128)(2,1)S(1)} collective-permute-done((bf16[1040,128]{1,0:T(8,128)(2,1)S(1)}, bf16[1040,128]{1,0:T(8,128)(2,1)S(1)}, u32[]{:S(2)}, u32[]{:S(2)}) %collective-permute-start.4) | collective-permute-done | bytes 266272 | tf_op jit(solution)/shard_map/ppermute | solution.py:437
  29.3 2.1 %collective-permute-done.6.back = bf16[1040,128]{1,0:T(8,128)(2,1)S(1)} collective-permute-done((bf16[1040,128]{1,0:T(8,128)(2,1)S(1)}, bf16[1040,128]{1,0:T(8,128)(2,1)S(1)}, u32[]{:S(2)}, u32[]{:S(2)}) %collective-permute-start.6) | collective-permute-done | bytes 266272 | tf_op jit(solution)/shard_map/ppermute | solution.py:437
  31.4 0.1 stamp.1
  31.4 1.6 %collective-permute-start.11 = (bf16[1040,128]{1,0:T(8,128)(2,1)S(1)}, bf16[1040,128]{1,0:T(8,128)(2,1)S(1)}, u32[]{:S(2)}, u32[]{:S(2)}) collective-permute-start(bf16[1040,128]{1,0:T(8,128)(2,1)S(1)} %get-tuple-element.44.refs_1_), channel_id=1, source_target_pairs={{0,4},{4,8},{8,12},{12,14},{14,10},{10,6},{6,2},{2,0},{1,5},{5,9},... | collective-permute-start | bytes 798728 | tf_op jit(solution)/shard_map/ppermute | solution.py:437
  33.1 0.4 collective-permute-start.12
  33.5 0.8 %scores.4 = (f32[8,128]{1,0:T(8,128)S(1)}, f32[8,128]{1,0:T(8,128)S(1)}) custom-call(bf16[512,2048]{1,0:T(8,128)(2,1)S(1)} %fetch.1.decoder, f32[8,128]{1,0:T(8,128)S(1)} %get-tuple-element.37.own_facts, bf16[1040,128]{1,0:T(8,128)(2,1)S(1)} %collective-permute-done.2.refs_0_, bf16[1040,128]{1,0:T(8,128)(2,1)S(1)} %get-tuple-element.44.refs_1_, ...), custom_call_target="tpu_custom_call" | custom-call | tf_op jit(solution)/shard_map/scores/pallas_call | solution.py:258
  34.3 0.1 collective-permute-start.10
  34.4 1.3 %gradients.3.refs_4_ = f32[512,2048]{1,0:T(8,128)S(1)} custom-call(f32[8,128]{1,0:T(8,128)S(1)} %get-tuple-element.37.own_facts, bf16[1040,128]{1,0:T(8,128)(2,1)S(1)} %get-tuple-element.34.refs_0_, bf16[1040,128]{1,0:T(8,128)(2,1)S(1)} %get-tuple-element.35.refs_1_, bf16[1040,128]{1,0:T(8,128)(2,1)S(1)} %collective-permute-done.refs_2_, ...), custom_call_target="tpu_custom_call" | custom-call | tf_op jit(solution)/shard_map/gradients/pallas_call | solution.py:319
  35.7 0.9 %gradients.4.refs_4_ = f32[512,2048]{1,0:T(8,128)S(1)} custom-call(f32[8,128]{1,0:T(8,128)S(1)} %get-tuple-element.37.own_facts, bf16[1040,128]{1,0:T(8,128)(2,1)S(1)} %collective-permute-done.2.refs_0_, bf16[1040,128]{1,0:T(8,128)(2,1)S(1)} %get-tuple-element.44.refs_1_, ...), custom_call_target="tpu_custom_call", output_to_operand_aliasing={{}: (5, {})} | custom-call | tf_op jit(solution)/shard_map/gradients/pallas_call | solution.py:319
  36.6 0.0 collective-permute-done.10
  36.6 0.0 collective-permute-done.8.refs_0_
  36.7 0.4 collective-permute-done.9.refs_3_
  37.1 0.0 collective-permute-start.14
  37.1 2.0 %collective-permute-start.15 = (bf16[1040,128]{1,0:T(8,128)(2,1)S(1)}, bf16[1040,128]{1,0:T(8,128)(2,1)S(1)}, u32[]{:S(2)}, u32[]{:S(2)}) collective-permute-start(bf16[1040,128]{1,0:T(8,128)(2,1)S(1)} %collective-permute-done.8.refs_0_), channel_id=1, source_target_pairs={{0,4},{4,8},{8,12},{12,14},{14,10},{10,6},{6,2},{2,0},{1,5},{5,9},... | collective-permute-start | bytes 798728 | tf_op jit(solution)/shard_map/ppermute | solution.py:437
  39.1 1.4 %collective-permute-start.18 = (f32[24,128]{1,0:T(8,128)S(1)}, f32[24,128]{1,0:T(8,128)S(1)}, u32[]{:S(2)}, u32[]{:S(2)}) collective-permute-start(f32[24,128]{1,0:T(8,128)S(1)} %concatenate.3), channel_id=1, source_target_pairs={{0,6},{1,9},{4,2},{5,13},{8,0},{9,15},{12,4},{13,11},{14,8},{15,7}... | collective-permute-start | bytes 36872 | tf_op jit(solution)/shard_map/ppermute | solution.py:455
  40.5 0.0 collective-permute-done.11.refs_1_.onward
  40.5 2.3 %collective-permute-done.12.refs_2_.back = bf16[1040,128]{1,0:T(8,128)(2,1)S(1)} collective-permute-done((bf16[1040,128]{1,0:T(8,128)(2,1)S(1)}, bf16[1040,128]{1,0:T(8,128)(2,1)S(1)}, u32[]{:S(2)}, u32[]{:S(2)}) %collective-permute-start.12) | collective-permute-done | bytes 266272 | tf_op jit(solution)/shard_map/ppermute | solution.py:437
  42.8 0.8 %scores.5 = (f32[8,128]{1,0:T(8,128)S(1)}, f32[8,128]{1,0:T(8,128)S(1)}) custom-call(bf16[512,2048]{1,0:T(8,128)(2,1)S(1)} %fetch.1.decoder, f32[8,128]{1,0:T(8,128)S(1)} %get-tuple-element.37.own_facts, bf16[1040,128]{1,0:T(8,128)(2,1)S(1)} %collective-permute-done.8.refs_0_, bf16[1040,128]{1,0:T(8,128)(2,1)S(1)} %collective-permute-done.11.refs_1_.onward, ...), custom_call_target="tpu_custom_call" | custom-call | tf_op jit(solution)/shard_map/scores/pallas_call | solution.py:258
  43.6 0.1 collective-permute-start.13
  43.7 0.9 %gradients.5.total = f32[512,2048]{1,0:T(8,128)S(1)} custom-call(f32[8,128]{1,0:T(8,128)S(1)} %get-tuple-element.37.own_facts, bf16[1040,128]{1,0:T(8,128)(2,1)S(1)} %collective-permute-done.8.refs_0_, bf16[1040,128]{1,0:T(8,128)(2,1)S(1)} %collective-permute-done.11.refs_1_.onward, ...), custom_call_target="tpu_custom_call", output_to_operand_aliasing={{}: (5, {})} | custom-call | tf_op jit(solution)/shard_map/gradients/pallas_call | solution.py:319
  44.6 0.3 collective-permute-done.13
  44.8 2.4 %collective-permute-start.16 = (f32[8,128]{1,0:T(8,128)S(1)}, f32[8,128]{1,0:T(8,128)S(1)}, u32[]{:S(2)}, u32[]{:S(2)}) collective-permute-start(f32[8,128]{1,0:T(8,128)S(1)} %add.12), channel_id=1, source_target_pairs={{0,10},{1,13},{4,6},{5,15},{8,2},{9,11},{12,0},{13,7},{14,4},{15,3... | collective-permute-start | bytes 12296 | tf_op jit(solution)/shard_map/ppermute | solution.py:455
  47.2 0.0 collective-permute-done.14.piece.right
  47.2 0.4 half_scores.1.partial
  47.7 0.0 collective-permute-done.15.left.piece
  47.7 0.5 rest_scores.1
  48.1 3.4 %collective-permute-start.17 = (f32[8,128]{1,0:T(8,128)S(1)}, f32[8,128]{1,0:T(8,128)S(1)}, u32[]{:S(2)}, u32[]{:S(2)}) collective-permute-start(f32[8,128]{1,0:T(8,128)S(1)} %rest_scores.1), channel_id=1, source_target_pairs={{0,14},{4,10},{8,6},{12,2},{14,0},{10,4},{6,8},{2,12},{1,15},{5,11... | collective-permute-start | bytes 12296 | tf_op jit(solution)/shard_map/ppermute | solution.py:437
  51.5 0.0 collective-permute-done.18
  51.5 0.0 collective-permute-done.16.third
  51.5 1.8 %last_gradients.1 = bf16[512,2048]{1,0:T(8,128)(2,1)} custom-call(bf16[1040,128]{1,0:T(8,128)(2,1)S(1)} %collective-permute-done.15.left.piece, bf16[1040,128]{1,0:T(8,128)(2,1)S(1)} %collective-permute-done.14.piece.right, f32[512,2048]{1,0:T(8,128)S(1)} %gradients.5.total), custom_call_target="tpu_custom_call" | custom-call | tf_op jit(solution)/shard_map/last_gradients/pallas_call | solution.py:346
  53.3 1.2 %collective-permute-done.17.opposite = f32[8,128]{1,0:T(8,128)S(1)} collective-permute-done((f32[8,128]{1,0:T(8,128)S(1)}, f32[8,128]{1,0:T(8,128)S(1)}, u32[]{:S(2)}, u32[]{:S(2)}) %collective-permute-start.17) | collective-permute-done | bytes 4128 | tf_op jit(solution)/shard_map/ppermute | solution.py:437
  54.5 0.2 collective-permute-start.19
  54.7 1.1 %collective-permute-done.19 = f32[32,128]{1,0:T(8,128)S(1)} collective-permute-done((f32[32,128]{1,0:T(8,128)S(1)}, f32[32,128]{1,0:T(8,128)S(1)}, u32[]{:S(2)}, u32[]{:S(2)}) %collective-permute-start.19) | collective-permute-done | bytes 16416 | tf_op jit(solution)/shard_map/ppermute | solution.py:448
  55.8 0.6 %add_bitcast_fusion = f32[128,32]{0,1:T(8,128)} fusion(f32[32,128]{1,0:T(8,128)S(1)} %unpack.1, f32[32,128]{1,0:T(8,128)S(1)} %collective-permute-done.19), kind=kLoop, calls=%fused_computation | loop fusion | flops 4096 | bytes 49152 | tf_op jit(solution)/shard_map/transpose | solution.py:498
  (5 shorter events, 0.0 us)
Async XLA Ops:
  1.8 10.2 %collective-permute-start = (bf16[1040,128]{1,0:T(8,128)(2,1)S(1)}, bf16[1040,128]{1,0:T(8,128)(2,1)S(1)}, u32[]{:S(2)}, u32[]{:S(2)}) collective-permute-start(bf16[1040,128]{1,0:T(8,128)(2,1)S(1)} %get-tuple-element.34.refs_0_), channel_id=1, source_target_pairs={{0,4},{4,8},{8,12},{12,14},{14,10},{10,6},{6,2},{2,0},{1,5},{5,9},... | collective-permute-start | bytes 798728 | tf_op jit(solution)/shard_map/ppermute | solution.py:437
  4.9 9.3 %collective-permute-start.1 = (bf16[1040,128]{1,0:T(8,128)(2,1)S(1)}, bf16[1040,128]{1,0:T(8,128)(2,1)S(1)}, u32[]{:S(2)}, u32[]{:S(2)}) collective-permute-start(bf16[1040,128]{1,0:T(8,128)(2,1)S(1)} %get-tuple-element.35.refs_1_), channel_id=1, source_target_pairs={{0,2},{4,0},{8,4},{12,8},{14,12},{10,14},{6,10},{2,6},{1,3},{5,1},... | collective-permute-start | bytes 798728 | tf_op jit(solution)/shard_map/ppermute | solution.py:437
  4.9 12.8 %collective-permute-start.3 = (bf16[1040,128]{1,0:T(8,128)(2,1)S(1)}, bf16[1040,128]{1,0:T(8,128)(2,1)S(1)}, u32[]{:S(2)}, u32[]{:S(2)}) collective-permute-start(bf16[1040,128]{1,0:T(8,128)(2,1)S(1)} %get-tuple-element.39), channel_id=1, source_target_pairs={{0,4},{4,8},{8,12},{12,14},{14,10},{10,6},{6,2},{2,0},{1,5},{5,9},... | collective-permute-start | bytes 798728 | tf_op jit(solution)/shard_map/ppermute | solution.py:437
  6.9 13.0 %collective-permute-start.5 = (bf16[1040,128]{1,0:T(8,128)(2,1)S(1)}, bf16[1040,128]{1,0:T(8,128)(2,1)S(1)}, u32[]{:S(2)}, u32[]{:S(2)}) collective-permute-start(bf16[1040,128]{1,0:T(8,128)(2,1)S(1)} %get-tuple-element.40), channel_id=1, source_target_pairs={{0,2},{4,0},{8,4},{12,8},{14,12},{10,14},{6,10},{2,6},{1,3},{5,1},... | collective-permute-start | bytes 798728 | tf_op jit(solution)/shard_map/ppermute | solution.py:437
  14.2 9.3 %collective-permute-start.2 = (bf16[1040,128]{1,0:T(8,128)(2,1)S(1)}, bf16[1040,128]{1,0:T(8,128)(2,1)S(1)}, u32[]{:S(2)}, u32[]{:S(2)}) collective-permute-start(bf16[1040,128]{1,0:T(8,128)(2,1)S(1)} %collective-permute-done.refs_2_), channel_id=1, source_target_pairs={{0,4},{4,8},{8,12},{12,14},{14,10},{10,6},{6,2},{2,0},{1,5},{5,9},... | collective-permute-start | bytes 798728 | tf_op jit(solution)/shard_map/ppermute | solution.py:437
  15.8 9.8 %collective-permute-start.7 = (bf16[1040,128]{1,0:T(8,128)(2,1)S(1)}, bf16[1040,128]{1,0:T(8,128)(2,1)S(1)}, u32[]{:S(2)}, u32[]{:S(2)}) collective-permute-start(bf16[1040,128]{1,0:T(8,128)(2,1)S(1)} %collective-permute-done.1.refs_5_), channel_id=1, source_target_pairs={{0,2},{4,0},{8,4},{12,8},{14,12},{10,14},{6,10},{2,6},{1,3},{5,1},... | collective-permute-start | bytes 798728 | tf_op jit(solution)/shard_map/ppermute | solution.py:437
  17.8 11.5 %collective-permute-start.4 = (bf16[1040,128]{1,0:T(8,128)(2,1)S(1)}, bf16[1040,128]{1,0:T(8,128)(2,1)S(1)}, u32[]{:S(2)}, u32[]{:S(2)}) collective-permute-start(bf16[1040,128]{1,0:T(8,128)(2,1)S(1)} %collective-permute-done.3.refs_3_), channel_id=1, source_target_pairs={{0,4},{4,8},{8,12},{12,14},{14,10},{10,6},{6,2},{2,0},{1,5},{5,9},... | collective-permute-start | bytes 798728 | tf_op jit(solution)/shard_map/ppermute | solution.py:437
  19.9 11.4 %collective-permute-start.6 = (bf16[1040,128]{1,0:T(8,128)(2,1)S(1)}, bf16[1040,128]{1,0:T(8,128)(2,1)S(1)}, u32[]{:S(2)}, u32[]{:S(2)}) collective-permute-start(bf16[1040,128]{1,0:T(8,128)(2,1)S(1)} %collective-permute-done.5.refs_4_), channel_id=1, source_target_pairs={{0,2},{4,0},{8,4},{12,8},{14,12},{10,14},{6,10},{2,6},{1,3},{5,1},... | collective-permute-start | bytes 798728 | tf_op jit(solution)/shard_map/ppermute | solution.py:437
  23.6 13.1 %collective-permute-start.8 = (bf16[1040,128]{1,0:T(8,128)(2,1)S(1)}, bf16[1040,128]{1,0:T(8,128)(2,1)S(1)}, u32[]{:S(2)}, u32[]{:S(2)}) collective-permute-start(bf16[1040,128]{1,0:T(8,128)(2,1)S(1)} %collective-permute-done.2.refs_0_), channel_id=1, source_target_pairs={{0,4},{4,8},{8,12},{12,14},{14,10},{10,6},{6,2},{2,0},{1,5},{5,9},... | collective-permute-start | bytes 798728 | tf_op jit(solution)/shard_map/ppermute | solution.py:437
  25.6 11.4 %collective-permute-start.9 = (bf16[1040,128]{1,0:T(8,128)(2,1)S(1)}, bf16[1040,128]{1,0:T(8,128)(2,1)S(1)}, u32[]{:S(2)}, u32[]{:S(2)}) collective-permute-start(bf16[1040,128]{1,0:T(8,128)(2,1)S(1)} %collective-permute-done.7.refs_3_), channel_id=1, source_target_pairs={{0,2},{4,0},{8,4},{12,8},{14,12},{10,14},{6,10},{2,6},{1,3},{5,1},... | collective-permute-start | bytes 798728 | tf_op jit(solution)/shard_map/ppermute | solution.py:437
  31.4 9.0 %collective-permute-start.11 = (bf16[1040,128]{1,0:T(8,128)(2,1)S(1)}, bf16[1040,128]{1,0:T(8,128)(2,1)S(1)}, u32[]{:S(2)}, u32[]{:S(2)}) collective-permute-start(bf16[1040,128]{1,0:T(8,128)(2,1)S(1)} %get-tuple-element.44.refs_1_), channel_id=1, source_target_pairs={{0,4},{4,8},{8,12},{12,14},{14,10},{10,6},{6,2},{2,0},{1,5},{5,9},... | collective-permute-start | bytes 798728 | tf_op jit(solution)/shard_map/ppermute | solution.py:437
  33.1 9.7 %collective-permute-start.12 = (bf16[1040,128]{1,0:T(8,128)(2,1)S(1)}, bf16[1040,128]{1,0:T(8,128)(2,1)S(1)}, u32[]{:S(2)}, u32[]{:S(2)}) collective-permute-start(bf16[1040,128]{1,0:T(8,128)(2,1)S(1)} %get-tuple-element.45.refs_2_), channel_id=1, source_target_pairs={{0,2},{4,0},{8,4},{12,8},{14,12},{10,14},{6,10},{2,6},{1,3},{5,1},... | collective-permute-start | bytes 798728 | tf_op jit(solution)/shard_map/ppermute | solution.py:437
  34.3 2.3 %collective-permute-start.10 = (f32[8,128]{1,0:T(8,128)S(1)}, f32[8,128]{1,0:T(8,128)S(1)}, u32[]{:S(2)}, u32[]{:S(2)}) collective-permute-start(f32[8,128]{1,0:T(8,128)S(1)} %get-tuple-element.47), channel_id=1, source_target_pairs={{0,1},{1,0},{2,3},{3,2},{4,5},{5,4},{6,7},{7,6},{8,9},{9,8},{10,11... | collective-permute-start | bytes 12296 | tf_op jit(solution)/shard_map/ppermute | solution.py:448
  37.1 10.2 %collective-permute-start.14 = (bf16[1040,128]{1,0:T(8,128)(2,1)S(1)}, bf16[1040,128]{1,0:T(8,128)(2,1)S(1)}, u32[]{:S(2)}, u32[]{:S(2)}) collective-permute-start(bf16[1040,128]{1,0:T(8,128)(2,1)S(1)} %collective-permute-done.9.refs_3_), channel_id=1, source_target_pairs={{0,2},{4,0},{8,4},{12,8},{14,12},{10,14},{6,10},{2,6},{1,3},{5,1},... | collective-permute-start | bytes 798728 | tf_op jit(solution)/shard_map/ppermute | solution.py:437
  37.1 10.6 %collective-permute-start.15 = (bf16[1040,128]{1,0:T(8,128)(2,1)S(1)}, bf16[1040,128]{1,0:T(8,128)(2,1)S(1)}, u32[]{:S(2)}, u32[]{:S(2)}) collective-permute-start(bf16[1040,128]{1,0:T(8,128)(2,1)S(1)} %collective-permute-done.8.refs_0_), channel_id=1, source_target_pairs={{0,4},{4,8},{8,12},{12,14},{14,10},{10,6},{6,2},{2,0},{1,5},{5,9},... | collective-permute-start | bytes 798728 | tf_op jit(solution)/shard_map/ppermute | solution.py:437
  39.1 12.4 %collective-permute-start.18 = (f32[24,128]{1,0:T(8,128)S(1)}, f32[24,128]{1,0:T(8,128)S(1)}, u32[]{:S(2)}, u32[]{:S(2)}) collective-permute-start(f32[24,128]{1,0:T(8,128)S(1)} %concatenate.3), channel_id=1, source_target_pairs={{0,6},{1,9},{4,2},{5,13},{8,0},{9,15},{12,4},{13,11},{14,8},{15,7}... | collective-permute-start | bytes 36872 | tf_op jit(solution)/shard_map/ppermute | solution.py:455
  43.6 1.2 %collective-permute-start.13 = (f32[8,128]{1,0:T(8,128)S(1)}, f32[8,128]{1,0:T(8,128)S(1)}, u32[]{:S(2)}, u32[]{:S(2)}) collective-permute-start(f32[8,128]{1,0:T(8,128)S(1)} %get-tuple-element.52), channel_id=1, source_target_pairs={{0,1},{1,0},{2,3},{3,2},{4,5},{5,4},{6,7},{7,6},{8,9},{9,8},{10,11... | collective-permute-start | bytes 12296 | tf_op jit(solution)/shard_map/ppermute | solution.py:448
  44.8 6.7 %collective-permute-start.16 = (f32[8,128]{1,0:T(8,128)S(1)}, f32[8,128]{1,0:T(8,128)S(1)}, u32[]{:S(2)}, u32[]{:S(2)}) collective-permute-start(f32[8,128]{1,0:T(8,128)S(1)} %add.12), channel_id=1, source_target_pairs={{0,10},{1,13},{4,6},{5,15},{8,2},{9,11},{12,0},{13,7},{14,4},{15,3... | collective-permute-start | bytes 12296 | tf_op jit(solution)/shard_map/ppermute | solution.py:455
  48.1 6.4 %collective-permute-start.17 = (f32[8,128]{1,0:T(8,128)S(1)}, f32[8,128]{1,0:T(8,128)S(1)}, u32[]{:S(2)}, u32[]{:S(2)}) collective-permute-start(f32[8,128]{1,0:T(8,128)S(1)} %rest_scores.1), channel_id=1, source_target_pairs={{0,14},{4,10},{8,6},{12,2},{14,0},{10,4},{6,8},{2,12},{1,15},{5,11... | collective-permute-start | bytes 12296 | tf_op jit(solution)/shard_map/ppermute | solution.py:437
  54.5 1.2 %collective-permute-start.19 = (f32[32,128]{1,0:T(8,128)S(1)}, f32[32,128]{1,0:T(8,128)S(1)}, u32[]{:S(2)}, u32[]{:S(2)}) collective-permute-start(f32[32,128]{1,0:T(8,128)S(1)} %unpack.1), channel_id=1, source_target_pairs={{0,1},{1,0},{2,3},{3,2},{4,5},{5,4},{6,7},{7,6},{8,9},{9,8},{10,11... | collective-permute-start | bytes 49160 | tf_op jit(solution)/shard_map/ppermute | solution.py:448

commit v16 on v12

--- a/solution.py
+++ b/solution.py
@@ -62,18 +62,16 @@
     sources, refs = refs[:5], refs[5:]
     outs, refs = refs[:6], refs[6:]
     first_left, first_right, left, right, own_facts, slots = outs
-    block_slot, active, feats, acts, halves, wide_feats, wide_acts, sems = refs
-    cut = halves.shape[2]
+    block_slot, active, feats, acts, whole, wide_feats, wide_acts, sems = refs
+    tok_rows, width = whole.shape
+    cut = width // 2
     copies = []
     for source, target in zip(sources[:4], (block_slot, active, feats, acts)):
         copies.append(pltpu.make_async_copy(source, target, sems.at[len(copies)]))
-    for side in range(2):
+    for start in range(0, tok_rows, 16):
+        rows = pl.ds(start, 16)
         copies.append(
-            pltpu.make_async_copy(
-                sources[4].at[:, side * cut : (side + 1) * cut],
-                halves.at[side],
-                sems.at[len(copies)],
-            )
+            pltpu.make_async_copy(sources[4].at[rows], whole.at[rows], sems.at[len(copies)])
         )
     for copy in copies:
         copy.start()
@@ -105,11 +103,12 @@
     store_facts(first_left, [opposite, none])
     for target, sign in ((left, -1), (right, 1)):
         store_facts(target, [facts(sign * d) for d in range(1, owners // 2)] + [none])
-    tok_rows = halves.shape[1]
+    for copy in copies[4:]:
+        copy.wait()
     for side, targets in ((0, (first_left, left)), (1, (first_right, right))):
-        copies[4 + side].wait()
         for j in range(cut // 128):
-            part = halves[side, :, j * 128 : (j + 1) * 128]
+            column = side * cut + j * 128
+            part = whole[:, column : column + 128]
             for target in targets:
                 target[j * tok_rows : (j + 1) * tok_rows, :] = part
 
@@ -138,10 +137,10 @@
             pltpu.VMEM((ACT, tok_rows), jnp.int32),
             pltpu.VMEM((ACT * KPB, tok_rows), jnp.int32),
             pltpu.VMEM((ACT * KPB, tok_rows), acts.dtype),
-            pltpu.VMEM((2, tok_rows, width // 2), grad_out.dtype),
+            pltpu.VMEM((tok_rows, width), grad_out.dtype),
             pltpu.VMEM((ACT * KPB, tok_rows), jnp.float32),
             pltpu.VMEM((ACT * KPB, tok_rows), jnp.float32),
-            pltpu.SemaphoreType.DMA((6,)),
+            pltpu.SemaphoreType.DMA((4 + tok_rows // 16,)),
         ],
         compiler_params=limit(8),
         name="prepare",

time: 56.2 us -> 56.4 us (level)
  no operation moved by 1% of the time
where the time goes in v16:
time: 56.4 us; the launch traced here: 56.2 us
  starting transfers between devices  24.5 us (43%)
  waiting for transfers between devices  18.6 us (33%)
  Pallas kernels  11.7 us (21%)
  between operations  0.77 us (1%)
  other arithmetic  0.62 us (1%)
    ppermute x15, starting transfers between devices, shift(): return lax.ppermute(x, 'dp', pairs)  19.3 us
    ppermute x15, waiting for transfers between devices, shift(): return lax.ppermute(x, 'dp', pairs)  17.3 us
    ppermute x2, starting transfers between devices, return_by(): return lax.ppermute(x, ('dp', 'width'), pairs)  4.9 us
    pallas_call x4, Pallas kernels, scores_of(): pl.pallas_call(functools.partial(scores_kernel, distances, split), out_sh...  3.72 us
    pallas_call x3, Pallas kernels, gradients_of(): pl.pallas_call(functools.partial(gradients_kernel, distances), out_shape=...  3.13 us
    pallas_call x1, Pallas kernels, last_gradients(): pl.pallas_call(last_gradients_kernel, out_shape=jax.ShapeDtypeStruct(tota...  1.74 us
    pallas_call x1, Pallas kernels, fetch(): pl.pallas_call(fetch_kernel, out_shape=pltpu.VMEM(x.shape, x.dtype), in_s...  1.6 us
    pallas_call x1, Pallas kernels, prepare(): pl.pallas_call(functools.partial(prepare_kernel, owners), out_shape=(piec...  1.35 us
  transfers between devices with their start and end apart: 20, of which 10 were waited for; matrix products, arithmetic and copies ran while one was open for 0% of the time, Pallas kernels for 18%

profile of v16, /device:TPU:0, one launch (start us, length us, event | category | flops | bytes accessed | tf_op | source)
XLA Modules:
  0.0 56.2 jit_solution(2419984188932599819)
XLA Ops:
  0.6 1.4 %prepare.1 = (bf16[1040,128]{1,0:T(8,128)(2,1)S(1)}, bf16[1024,128]{1,0:T(8,128)(2,1)S(1)}, bf16[1056,128]{1,0:T(8,128)(2,1)S(1)}, bf16[1056,128]{1,0:T(8,128)(2...) custom-call(s32[32]{0:T(128)} %refs_0_.1, s32[8,128]{1,0:T(8,128)} %bitcast.7, s32[32,128]{1,0:T(8,128)} %bitcast.5, ...), custom_call_target="tpu_custom_call" | custom-call | tf_op jit(solution)/shard_map/prepare/pallas_call | solution.py:123
  2.0 3.1 %collective-permute-start = (bf16[1040,128]{1,0:T(8,128)(2,1)S(1)}, bf16[1040,128]{1,0:T(8,128)(2,1)S(1)}, u32[]{:S(2)}, u32[]{:S(2)}) collective-permute-start(bf16[1040,128]{1,0:T(8,128)(2,1)S(1)} %get-tuple-element.34.refs_0_), channel_id=1, source_target_pairs={{0,4},{4,8},{8,12},{12,14},{14,10},{10,6},{6,2},{2,0},{1,5},{5,9},... | collective-permute-start | bytes 798728 | tf_op jit(solution)/shard_map/ppermute | solution.py:416
  5.1 0.0 collective-permute-start.1
  5.1 2.0 %collective-permute-start.3 = (bf16[1056,128]{1,0:T(8,128)(2,1)S(1)}, bf16[1056,128]{1,0:T(8,128)(2,1)S(1)}, u32[]{:S(2)}, u32[]{:S(2)}) collective-permute-start(bf16[1056,128]{1,0:T(8,128)(2,1)S(1)} %get-tuple-element.37), channel_id=1, source_target_pairs={{0,4},{4,8},{8,12},{12,14},{14,10},{10,6},{6,2},{2,0},{1,5},{5,9},... | collective-permute-start | bytes 811016 | tf_op jit(solution)/shard_map/ppermute | solution.py:416
  7.1 0.0 collective-permute-start.5
  7.1 1.6 %fetch.1.decoder = bf16[512,2048]{1,0:T(8,128)(2,1)S(1)} custom-call(bf16[512,2048]{1,0:T(8,128)(2,1)} %source.1), custom_call_target="tpu_custom_call" | custom-call | tf_op jit(solution)/shard_map/fetch/pallas_call | solution.py:157
  8.7 5.6 %collective-permute-done.1.refs_5_ = bf16[1024,128]{1,0:T(8,128)(2,1)S(1)} collective-permute-done((bf16[1024,128]{1,0:T(8,128)(2,1)S(1)}, bf16[1024,128]{1,0:T(8,128)(2,1)S(1)}, u32[]{:S(2)}, u32[]{:S(2)}) %collective-permute-start.1) | collective-permute-done | bytes 262176 | tf_op jit(solution)/shard_map/ppermute | solution.py:416
  14.3 0.0 collective-permute-done.refs_2_
  14.3 1.6 %collective-permute-start.2 = (bf16[1040,128]{1,0:T(8,128)(2,1)S(1)}, bf16[1040,128]{1,0:T(8,128)(2,1)S(1)}, u32[]{:S(2)}, u32[]{:S(2)}) collective-permute-start(bf16[1040,128]{1,0:T(8,128)(2,1)S(1)} %collective-permute-done.refs_2_), channel_id=1, source_target_pairs={{0,4},{4,8},{8,12},{12,14},{14,10},{10,6},{6,2},{2,0},{1,5},{5,9},... | collective-permute-start | bytes 798728 | tf_op jit(solution)/shard_map/ppermute | solution.py:416
  15.9 0.4 collective-permute-start.7
  16.3 1.7 %collective-permute-done.3.refs_3_ = bf16[1056,128]{1,0:T(8,128)(2,1)S(1)} collective-permute-done((bf16[1056,128]{1,0:T(8,128)(2,1)S(1)}, bf16[1056,128]{1,0:T(8,128)(2,1)S(1)}, u32[]{:S(2)}, u32[]{:S(2)}) %collective-permute-start.3) | collective-permute-done | bytes 270368 | tf_op jit(solution)/shard_map/ppermute | solution.py:416
  18.0 2.1 %collective-permute-start.4 = (bf16[1056,128]{1,0:T(8,128)(2,1)S(1)}, bf16[1056,128]{1,0:T(8,128)(2,1)S(1)}, u32[]{:S(2)}, u32[]{:S(2)}) collective-permute-start(bf16[1056,128]{1,0:T(8,128)(2,1)S(1)} %collective-permute-done.3.refs_3_), channel_id=1, source_target_pairs={{0,4},{4,8},{8,12},{12,14},{14,10},{10,6},{6,2},{2,0},{1,5},{5,9},... | collective-permute-start | bytes 811016 | tf_op jit(solution)/shard_map/ppermute | solution.py:416
  20.1 0.0 collective-permute-done.5.refs_4_
  20.1 0.0 collective-permute-start.6
  20.1 3.6 %collective-permute-done.2.refs_0_ = bf16[1040,128]{1,0:T(8,128)(2,1)S(1)} collective-permute-done((bf16[1040,128]{1,0:T(8,128)(2,1)S(1)}, bf16[1040,128]{1,0:T(8,128)(2,1)S(1)}, u32[]{:S(2)}, u32[]{:S(2)}) %collective-permute-start.2) | collective-permute-done | bytes 266272 | tf_op jit(solution)/shard_map/ppermute | solution.py:416
  23.7 2.1 %collective-permute-start.8 = (bf16[1040,128]{1,0:T(8,128)(2,1)S(1)}, bf16[1040,128]{1,0:T(8,128)(2,1)S(1)}, u32[]{:S(2)}, u32[]{:S(2)}) collective-permute-start(bf16[1040,128]{1,0:T(8,128)(2,1)S(1)} %collective-permute-done.2.refs_0_), channel_id=1, source_target_pairs={{0,4},{4,8},{8,12},{12,14},{14,10},{10,6},{6,2},{2,0},{1,5},{5,9},... | collective-permute-start | bytes 798728 | tf_op jit(solution)/shard_map/ppermute | solution.py:416
  25.8 0.0 collective-permute-done.7.refs_3_
  25.8 0.0 collective-permute-start.9
  25.9 1.3 %scores.4 = (f32[8,128]{1,0:T(8,128)S(1)}, f32[8,128]{1,0:T(8,128)S(1)}, f32[8,128]{1,0:T(8,128)S(1)}) custom-call(bf16[512,2048]{1,0:T(8,128)(2,1)S(1)} %fetch.1.decoder, f32[8,128]{1,0:T(8,128)S(1)} %get-tuple-element.33.own_facts, bf16[1040,128]{1,0:T(8,128)(2,1)S(1)} %get-tuple-element.34.refs_0_, bf16[1024,128]{1,0:T(8,128)(2,1)S(1)} %get-tuple-element.35.refs_1_, ...), custom_call_target="tpu_custom_call" | custom-call | tf_op jit(solution)/shard_map/scores/pallas_call | solution.py:277
  27.2 2.3 %collective-permute-done.4.onward = bf16[1056,128]{1,0:T(8,128)(2,1)S(1)} collective-permute-done((bf16[1056,128]{1,0:T(8,128)(2,1)S(1)}, bf16[1056,128]{1,0:T(8,128)(2,1)S(1)}, u32[]{:S(2)}, u32[]{:S(2)}) %collective-permute-start.4) | collective-permute-done | bytes 270368 | tf_op jit(solution)/shard_map/ppermute | solution.py:416
  29.5 2.0 %collective-permute-done.6.back = bf16[1056,128]{1,0:T(8,128)(2,1)S(1)} collective-permute-done((bf16[1056,128]{1,0:T(8,128)(2,1)S(1)}, bf16[1056,128]{1,0:T(8,128)(2,1)S(1)}, u32[]{:S(2)}, u32[]{:S(2)}) %collective-permute-start.6) | collective-permute-done | bytes 270368 | tf_op jit(solution)/shard_map/ppermute | solution.py:416
  31.5 0.1 stamp.1
  31.6 1.6 %collective-permute-start.11 = (bf16[1056,128]{1,0:T(8,128)(2,1)S(1)}, bf16[1056,128]{1,0:T(8,128)(2,1)S(1)}, u32[]{:S(2)}, u32[]{:S(2)}) collective-permute-start(bf16[1056,128]{1,0:T(8,128)(2,1)S(1)} %get-tuple-element.43.refs_1_), channel_id=1, source_target_pairs={{0,4},{4,8},{8,12},{12,14},{14,10},{10,6},{6,2},{2,0},{1,5},{5,9},... | collective-permute-start | bytes 811016 | tf_op jit(solution)/shard_map/ppermute | solution.py:416
  33.2 0.4 collective-permute-start.12
  33.7 0.8 %scores.5 = (f32[8,128]{1,0:T(8,128)S(1)}, f32[8,128]{1,0:T(8,128)S(1)}) custom-call(bf16[512,2048]{1,0:T(8,128)(2,1)S(1)} %fetch.1.decoder, f32[8,128]{1,0:T(8,128)S(1)} %get-tuple-element.33.own_facts, bf16[1040,128]{1,0:T(8,128)(2,1)S(1)} %collective-permute-done.2.refs_0_, bf16[1056,128]{1,0:T(8,128)(2,1)S(1)} %get-tuple-element.43.refs_1_, ...), custom_call_target="tpu_custom_call" | custom-call | tf_op jit(solution)/shard_map/scores/pallas_call | solution.py:277
  34.5 0.1 collective-permute-start.10
  34.6 1.3 %gradients.3.refs_4_ = f32[512,2048]{1,0:T(8,128)S(1)} custom-call(f32[8,128]{1,0:T(8,128)S(1)} %get-tuple-element.33.own_facts, bf16[1040,128]{1,0:T(8,128)(2,1)S(1)} %get-tuple-element.34.refs_0_, bf16[1024,128]{1,0:T(8,128)(2,1)S(1)} %get-tuple-element.35.refs_1_, bf16[1040,128]{1,0:T(8,128)(2,1)S(1)} %collective-permute-done.refs_2_, ...), custom_call_target="tpu_custom_call" | custom-call | tf_op jit(solution)/shard_map/gradients/pallas_call | solution.py:298
  35.8 0.9 %gradients.4.refs_4_ = f32[512,2048]{1,0:T(8,128)S(1)} custom-call(f32[8,128]{1,0:T(8,128)S(1)} %get-tuple-element.33.own_facts, bf16[1040,128]{1,0:T(8,128)(2,1)S(1)} %collective-permute-done.2.refs_0_, bf16[1056,128]{1,0:T(8,128)(2,1)S(1)} %get-tuple-element.43.refs_1_, ...), custom_call_target="tpu_custom_call", output_to_operand_aliasing={{}: (5, {})} | custom-call | tf_op jit(solution)/shard_map/gradients/pallas_call | solution.py:298
  36.8 0.0 collective-permute-done.10
  36.8 0.3 collective-permute-done.9.refs_3_
  37.1 0.0 collective-permute-done.8.refs_0_
  37.1 1.6 %collective-permute-start.14 = (bf16[1040,128]{1,0:T(8,128)(2,1)S(1)}, bf16[1040,128]{1,0:T(8,128)(2,1)S(1)}, u32[]{:S(2)}, u32[]{:S(2)}) collective-permute-start(bf16[1040,128]{1,0:T(8,128)(2,1)S(1)} %collective-permute-done.8.refs_0_), channel_id=1, source_target_pairs={{0,4},{4,8},{8,12},{12,14},{14,10},{10,6},{6,2},{2,0},{1,5},{5,9},... | collective-permute-start | bytes 798728 | tf_op jit(solution)/shard_map/ppermute | solution.py:416
  38.7 0.4 collective-permute-start.15
  39.2 1.4 %collective-permute-start.18 = (f32[32,128]{1,0:T(8,128)S(1)}, f32[32,128]{1,0:T(8,128)S(1)}, u32[]{:S(2)}, u32[]{:S(2)}) collective-permute-start(f32[32,128]{1,0:T(8,128)S(1)} %concatenate.3), channel_id=1, source_target_pairs={{0,6},{1,9},{4,2},{5,13},{8,0},{9,15},{12,4},{13,11},{14,8},{15,7}... | collective-permute-start | bytes 49160 | tf_op jit(solution)/shard_map/ppermute | solution.py:434
  40.5 0.0 collective-permute-done.11.refs_1_.onward
  40.5 1.0 %collective-permute-done.12.refs_2_.back = bf16[1056,128]{1,0:T(8,128)(2,1)S(1)} collective-permute-done((bf16[1056,128]{1,0:T(8,128)(2,1)S(1)}, bf16[1056,128]{1,0:T(8,128)(2,1)S(1)}, u32[]{:S(2)}, u32[]{:S(2)}) %collective-permute-start.12) | collective-permute-done | bytes 270368 | tf_op jit(solution)/shard_map/ppermute | solution.py:416
  41.6 0.8 %scores.6 = (f32[8,128]{1,0:T(8,128)S(1)}, f32[8,128]{1,0:T(8,128)S(1)}) custom-call(bf16[512,2048]{1,0:T(8,128)(2,1)S(1)} %fetch.1.decoder, f32[8,128]{1,0:T(8,128)S(1)} %get-tuple-element.33.own_facts, bf16[1040,128]{1,0:T(8,128)(2,1)S(1)} %collective-permute-done.8.refs_0_, bf16[1056,128]{1,0:T(8,128)(2,1)S(1)} %collective-permute-done.11.refs_1_.onward, ...), custom_call_target="tpu_custom_call" | custom-call | tf_op jit(solution)/shard_map/scores/pallas_call | solution.py:277
  42.4 0.1 collective-permute-start.13
  42.5 0.9 %gradients.5.total = f32[512,2048]{1,0:T(8,128)S(1)} custom-call(f32[8,128]{1,0:T(8,128)S(1)} %get-tuple-element.33.own_facts, bf16[1040,128]{1,0:T(8,128)(2,1)S(1)} %collective-permute-done.8.refs_0_, bf16[1056,128]{1,0:T(8,128)(2,1)S(1)} %collective-permute-done.11.refs_1_.onward, ...), custom_call_target="tpu_custom_call", output_to_operand_aliasing={{}: (5, {})} | custom-call | tf_op jit(solution)/shard_map/gradients/pallas_call | solution.py:298
  43.4 0.2 collective-permute-done.13
  43.6 3.5 %collective-permute-start.16 = (f32[8,128]{1,0:T(8,128)S(1)}, f32[8,128]{1,0:T(8,128)S(1)}, u32[]{:S(2)}, u32[]{:S(2)}) collective-permute-start(f32[8,128]{1,0:T(8,128)S(1)} %add.12), channel_id=1, source_target_pairs={{0,10},{1,13},{4,6},{5,15},{8,2},{9,11},{12,0},{13,7},{14,4},{15,3... | collective-permute-start | bytes 12296 | tf_op jit(solution)/shard_map/ppermute | solution.py:434
  47.1 0.0 collective-permute-done.15.right.refs_1_
  47.2 0.0 collective-permute-done.14.left.refs_0_
  47.2 0.7 %scores.7 = f32[8,128]{1,0:T(8,128)S(1)} custom-call(bf16[512,2048]{1,0:T(8,128)(2,1)S(1)} %fetch.1.decoder, f32[8,128]{1,0:T(8,128)S(1)} %get-tuple-element.33.own_facts, bf16[1040,128]{1,0:T(8,128)(2,1)S(1)} %collective-permute-done.14.left.refs_0_, bf16[1024,128]{1,0:T(8,128)(2,1)S(1)} %collective-permute-done.15.right.refs_1_), custom_call_target="tpu_custom_call" | custom-call | tf_op jit(solution)/shard_map/scores/pallas_call | solution.py:277
  47.9 3.7 %collective-permute-start.17 = (f32[8,128]{1,0:T(8,128)S(1)}, f32[8,128]{1,0:T(8,128)S(1)}, u32[]{:S(2)}, u32[]{:S(2)}) collective-permute-start(f32[8,128]{1,0:T(8,128)S(1)} %scores.7), channel_id=1, source_target_pairs={{0,14},{4,10},{8,6},{12,2},{14,0},{10,4},{6,8},{2,12},{1,15},{5,11... | collective-permute-start | bytes 12296 | tf_op jit(solution)/shard_map/ppermute | solution.py:416
  51.6 0.0 collective-permute-done.18
  51.6 0.0 collective-permute-done.16.third
  51.6 1.7 %last_gradients.1 = bf16[512,2048]{1,0:T(8,128)(2,1)} custom-call(bf16[1040,128]{1,0:T(8,128)(2,1)S(1)} %collective-permute-done.14.left.refs_0_, bf16[1024,128]{1,0:T(8,128)(2,1)S(1)} %collective-permute-done.15.right.refs_1_, f32[512,2048]{1,0:T(8,128)S(1)} %gradients.5.total), custom_call_target="tpu_custom_call" | custom-call | tf_op jit(solution)/shard_map/last_gradients/pallas_call | solution.py:325
  53.4 0.9 %collective-permute-done.17.opposite = f32[8,128]{1,0:T(8,128)S(1)} collective-permute-done((f32[8,128]{1,0:T(8,128)S(1)}, f32[8,128]{1,0:T(8,128)S(1)}, u32[]{:S(2)}, u32[]{:S(2)}) %collective-permute-start.17) | collective-permute-done | bytes 4128 | tf_op jit(solution)/shard_map/ppermute | solution.py:416
  54.3 0.2 collective-permute-start.19
  54.5 1.1 %collective-permute-done.19 = f32[32,128]{1,0:T(8,128)S(1)} collective-permute-done((f32[32,128]{1,0:T(8,128)S(1)}, f32[32,128]{1,0:T(8,128)S(1)}, u32[]{:S(2)}, u32[]{:S(2)}) %collective-permute-start.19) | collective-permute-done | bytes 16416 | tf_op jit(solution)/shard_map/ppermute | solution.py:427
  55.5 0.6 %add_bitcast_fusion = f32[128,32]{0,1:T(8,128)} fusion(f32[32,128]{1,0:T(8,128)S(1)} %unpack.1, f32[32,128]{1,0:T(8,128)S(1)} %collective-permute-done.19), kind=kLoop, calls=%fused_computation | loop fusion | flops 4096 | bytes 49152 | tf_op jit(solution)/shard_map/transpose | solution.py:473
  (5 shorter events, 0.0 us)
Async XLA Ops:
  2.0 12.3 %collective-permute-start = (bf16[1040,128]{1,0:T(8,128)(2,1)S(1)}, bf16[1040,128]{1,0:T(8,128)(2,1)S(1)}, u32[]{:S(2)}, u32[]{:S(2)}) collective-permute-start(bf16[1040,128]{1,0:T(8,128)(2,1)S(1)} %get-tuple-element.34.refs_0_), channel_id=1, source_target_pairs={{0,4},{4,8},{8,12},{12,14},{14,10},{10,6},{6,2},{2,0},{1,5},{5,9},... | collective-permute-start | bytes 798728 | tf_op jit(solution)/shard_map/ppermute | solution.py:416
  5.1 9.2 %collective-permute-start.1 = (bf16[1024,128]{1,0:T(8,128)(2,1)S(1)}, bf16[1024,128]{1,0:T(8,128)(2,1)S(1)}, u32[]{:S(2)}, u32[]{:S(2)}) collective-permute-start(bf16[1024,128]{1,0:T(8,128)(2,1)S(1)} %get-tuple-element.35.refs_1_), channel_id=1, source_target_pairs={{0,2},{4,0},{8,4},{12,8},{14,12},{10,14},{6,10},{2,6},{1,3},{5,1},... | collective-permute-start | bytes 786440 | tf_op jit(solution)/shard_map/ppermute | solution.py:416
  5.1 12.9 %collective-permute-start.3 = (bf16[1056,128]{1,0:T(8,128)(2,1)S(1)}, bf16[1056,128]{1,0:T(8,128)(2,1)S(1)}, u32[]{:S(2)}, u32[]{:S(2)}) collective-permute-start(bf16[1056,128]{1,0:T(8,128)(2,1)S(1)} %get-tuple-element.37), channel_id=1, source_target_pairs={{0,4},{4,8},{8,12},{12,14},{14,10},{10,6},{6,2},{2,0},{1,5},{5,9},... | collective-permute-start | bytes 811016 | tf_op jit(solution)/shard_map/ppermute | solution.py:416
  7.1 13.1 %collective-permute-start.5 = (bf16[1056,128]{1,0:T(8,128)(2,1)S(1)}, bf16[1056,128]{1,0:T(8,128)(2,1)S(1)}, u32[]{:S(2)}, u32[]{:S(2)}) collective-permute-start(bf16[1056,128]{1,0:T(8,128)(2,1)S(1)} %get-tuple-element.38), channel_id=1, source_target_pairs={{0,2},{4,0},{8,4},{12,8},{14,12},{10,14},{6,10},{2,6},{1,3},{5,1},... | collective-permute-start | bytes 811016 | tf_op jit(solution)/shard_map/ppermute | solution.py:416
  14.3 9.4 %collective-permute-start.2 = (bf16[1040,128]{1,0:T(8,128)(2,1)S(1)}, bf16[1040,128]{1,0:T(8,128)(2,1)S(1)}, u32[]{:S(2)}, u32[]{:S(2)}) collective-permute-start(bf16[1040,128]{1,0:T(8,128)(2,1)S(1)} %collective-permute-done.refs_2_), channel_id=1, source_target_pairs={{0,4},{4,8},{8,12},{12,14},{14,10},{10,6},{6,2},{2,0},{1,5},{5,9},... | collective-permute-start | bytes 798728 | tf_op jit(solution)/shard_map/ppermute | solution.py:416
  15.9 10.0 %collective-permute-start.7 = (bf16[1024,128]{1,0:T(8,128)(2,1)S(1)}, bf16[1024,128]{1,0:T(8,128)(2,1)S(1)}, u32[]{:S(2)}, u32[]{:S(2)}) collective-permute-start(bf16[1024,128]{1,0:T(8,128)(2,1)S(1)} %collective-permute-done.1.refs_5_), channel_id=1, source_target_pairs={{0,2},{4,0},{8,4},{12,8},{14,12},{10,14},{6,10},{2,6},{1,3},{5,1},... | collective-permute-start | bytes 786440 | tf_op jit(solution)/shard_map/ppermute | solution.py:416
  18.0 11.5 %collective-permute-start.4 = (bf16[1056,128]{1,0:T(8,128)(2,1)S(1)}, bf16[1056,128]{1,0:T(8,128)(2,1)S(1)}, u32[]{:S(2)}, u32[]{:S(2)}) collective-permute-start(bf16[1056,128]{1,0:T(8,128)(2,1)S(1)} %collective-permute-done.3.refs_3_), channel_id=1, source_target_pairs={{0,4},{4,8},{8,12},{12,14},{14,10},{10,6},{6,2},{2,0},{1,5},{5,9},... | collective-permute-start | bytes 811016 | tf_op jit(solution)/shard_map/ppermute | solution.py:416
  20.1 11.4 %collective-permute-start.6 = (bf16[1056,128]{1,0:T(8,128)(2,1)S(1)}, bf16[1056,128]{1,0:T(8,128)(2,1)S(1)}, u32[]{:S(2)}, u32[]{:S(2)}) collective-permute-start(bf16[1056,128]{1,0:T(8,128)(2,1)S(1)} %collective-permute-done.5.refs_4_), channel_id=1, source_target_pairs={{0,2},{4,0},{8,4},{12,8},{14,12},{10,14},{6,10},{2,6},{1,3},{5,1},... | collective-permute-start | bytes 811016 | tf_op jit(solution)/shard_map/ppermute | solution.py:416
  23.7 13.4 %collective-permute-start.8 = (bf16[1040,128]{1,0:T(8,128)(2,1)S(1)}, bf16[1040,128]{1,0:T(8,128)(2,1)S(1)}, u32[]{:S(2)}, u32[]{:S(2)}) collective-permute-start(bf16[1040,128]{1,0:T(8,128)(2,1)S(1)} %collective-permute-done.2.refs_0_), channel_id=1, source_target_pairs={{0,4},{4,8},{8,12},{12,14},{14,10},{10,6},{6,2},{2,0},{1,5},{5,9},... | collective-permute-start | bytes 798728 | tf_op jit(solution)/shard_map/ppermute | solution.py:416
  25.8 11.3 %collective-permute-start.9 = (bf16[1024,128]{1,0:T(8,128)(2,1)S(1)}, bf16[1024,128]{1,0:T(8,128)(2,1)S(1)}, u32[]{:S(2)}, u32[]{:S(2)}) collective-permute-start(bf16[1024,128]{1,0:T(8,128)(2,1)S(1)} %collective-permute-done.7.refs_3_), channel_id=1, source_target_pairs={{0,2},{4,0},{8,4},{12,8},{14,12},{10,14},{6,10},{2,6},{1,3},{5,1},... | collective-permute-start | bytes 786440 | tf_op jit(solution)/shard_map/ppermute | solution.py:416
  31.6 9.0 %collective-permute-start.11 = (bf16[1056,128]{1,0:T(8,128)(2,1)S(1)}, bf16[1056,128]{1,0:T(8,128)(2,1)S(1)}, u32[]{:S(2)}, u32[]{:S(2)}) collective-permute-start(bf16[1056,128]{1,0:T(8,128)(2,1)S(1)} %get-tuple-element.43.refs_1_), channel_id=1, source_target_pairs={{0,4},{4,8},{8,12},{12,14},{14,10},{10,6},{6,2},{2,0},{1,5},{5,9},... | collective-permute-start | bytes 811016 | tf_op jit(solution)/shard_map/ppermute | solution.py:416
  33.2 8.3 %collective-permute-start.12 = (bf16[1056,128]{1,0:T(8,128)(2,1)S(1)}, bf16[1056,128]{1,0:T(8,128)(2,1)S(1)}, u32[]{:S(2)}, u32[]{:S(2)}) collective-permute-start(bf16[1056,128]{1,0:T(8,128)(2,1)S(1)} %get-tuple-element.44.refs_2_), channel_id=1, source_target_pairs={{0,2},{4,0},{8,4},{12,8},{14,12},{10,14},{6,10},{2,6},{1,3},{5,1},... | collective-permute-start | bytes 811016 | tf_op jit(solution)/shard_map/ppermute | solution.py:416
  34.5 2.3 %collective-permute-start.10 = (f32[8,128]{1,0:T(8,128)S(1)}, f32[8,128]{1,0:T(8,128)S(1)}, u32[]{:S(2)}, u32[]{:S(2)}) collective-permute-start(f32[8,128]{1,0:T(8,128)S(1)} %get-tuple-element.46), channel_id=1, source_target_pairs={{0,1},{1,0},{2,3},{3,2},{4,5},{5,4},{6,7},{7,6},{8,9},{9,8},{10,11... | collective-permute-start | bytes 12296 | tf_op jit(solution)/shard_map/ppermute | solution.py:427
  37.1 10.0 %collective-permute-start.14 = (bf16[1040,128]{1,0:T(8,128)(2,1)S(1)}, bf16[1040,128]{1,0:T(8,128)(2,1)S(1)}, u32[]{:S(2)}, u32[]{:S(2)}) collective-permute-start(bf16[1040,128]{1,0:T(8,128)(2,1)S(1)} %collective-permute-done.8.refs_0_), channel_id=1, source_target_pairs={{0,4},{4,8},{8,12},{12,14},{14,10},{10,6},{6,2},{2,0},{1,5},{5,9},... | collective-permute-start | bytes 798728 | tf_op jit(solution)/shard_map/ppermute | solution.py:416
  38.7 8.5 %collective-permute-start.15 = (bf16[1024,128]{1,0:T(8,128)(2,1)S(1)}, bf16[1024,128]{1,0:T(8,128)(2,1)S(1)}, u32[]{:S(2)}, u32[]{:S(2)}) collective-permute-start(bf16[1024,128]{1,0:T(8,128)(2,1)S(1)} %collective-permute-done.9.refs_3_), channel_id=1, source_target_pairs={{0,2},{4,0},{8,4},{12,8},{14,12},{10,14},{6,10},{2,6},{1,3},{5,1},... | collective-permute-start | bytes 786440 | tf_op jit(solution)/shard_map/ppermute | solution.py:416
  39.2 12.5 %collective-permute-start.18 = (f32[32,128]{1,0:T(8,128)S(1)}, f32[32,128]{1,0:T(8,128)S(1)}, u32[]{:S(2)}, u32[]{:S(2)}) collective-permute-start(f32[32,128]{1,0:T(8,128)S(1)} %concatenate.3), channel_id=1, source_target_pairs={{0,6},{1,9},{4,2},{5,13},{8,0},{9,15},{12,4},{13,11},{14,8},{15,7}... | collective-permute-start | bytes 49160 | tf_op jit(solution)/shard_map/ppermute | solution.py:434
  42.4 1.2 %collective-permute-start.13 = (f32[8,128]{1,0:T(8,128)S(1)}, f32[8,128]{1,0:T(8,128)S(1)}, u32[]{:S(2)}, u32[]{:S(2)}) collective-permute-start(f32[8,128]{1,0:T(8,128)S(1)} %get-tuple-element.51), channel_id=1, source_target_pairs={{0,1},{1,0},{2,3},{3,2},{4,5},{5,4},{6,7},{7,6},{8,9},{9,8},{10,11... | collective-permute-start | bytes 12296 | tf_op jit(solution)/shard_map/ppermute | solution.py:427
  43.6 8.0 %collective-permute-start.16 = (f32[8,128]{1,0:T(8,128)S(1)}, f32[8,128]{1,0:T(8,128)S(1)}, u32[]{:S(2)}, u32[]{:S(2)}) collective-permute-start(f32[8,128]{1,0:T(8,128)S(1)} %add.12), channel_id=1, source_target_pairs={{0,10},{1,13},{4,6},{5,15},{8,2},{9,11},{12,0},{13,7},{14,4},{15,3... | collective-permute-start | bytes 12296 | tf_op jit(solution)/shard_map/ppermute | solution.py:434
  47.9 6.4 %collective-permute-start.17 = (f32[8,128]{1,0:T(8,128)S(1)}, f32[8,128]{1,0:T(8,128)S(1)}, u32[]{:S(2)}, u32[]{:S(2)}) collective-permute-start(f32[8,128]{1,0:T(8,128)S(1)} %scores.7), channel_id=1, source_target_pairs={{0,14},{4,10},{8,6},{12,2},{14,0},{10,4},{6,8},{2,12},{1,15},{5,11... | collective-permute-start | bytes 12296 | tf_op jit(solution)/shard_map/ppermute | solution.py:416
  54.3 1.2 %collective-permute-start.19 = (f32[32,128]{1,0:T(8,128)S(1)}, f32[32,128]{1,0:T(8,128)S(1)}, u32[]{:S(2)}, u32[]{:S(2)}) collective-permute-start(f32[32,128]{1,0:T(8,128)S(1)} %unpack.1), channel_id=1, source_target_pairs={{0,1},{1,0},{2,3},{3,2},{4,5},{5,4},{6,7},{7,6},{8,9},{9,8},{10,11... | collective-permute-start | bytes 49160 | tf_op jit(solution)/shard_map/ppermute | solution.py:427

commit v17 on v12

--- a/solution.py
+++ b/solution.py
@@ -285,6 +285,45 @@
     )(kept(decoder), kept(own_facts), *pieces)
 
 
+def half_kernel(decoder, piece, partial):
+    cut = decoder.shape[1] // 2
+    rows = columns_of([piece], partial.shape[1], range(cut // 128))
+    partial[...] = lax.dot_general(
+        decoder[:, :cut], rows, (((1,), (1,)), ((), ())), preferred_element_type=jnp.float32
+    )
+
+
+def half_scores(decoder, piece, tok_rows):
+    return pl.pallas_call(
+        half_kernel,
+        out_shape=pltpu.VMEM((decoder.shape[0], tok_rows), jnp.float32),
+        in_specs=[VMEM] * 2,
+        out_specs=VMEM,
+        compiler_params=limit(8),
+        name="half_scores",
+    )(kept(decoder), kept(piece))
+
+
+def rest_kernel(decoder, partial, left, right, picked):
+    cut = decoder.shape[1] // 2
+    rows = columns_of([right], partial.shape[1], range(cut // 128))
+    scores = partial[...] + lax.dot_general(
+        decoder[:, cut:], rows, (((1,), (1,)), ((), ())), preferred_element_type=jnp.float32
+    )
+    picked[...] = jnp.concatenate(pick(scores, last_facts_in(left)) * 2, axis=0)
+
+
+def rest_scores(decoder, partial, left, right):
+    return pl.pallas_call(
+        rest_kernel,
+        out_shape=pltpu.VMEM((2 * KPB, partial.shape[1]), jnp.float32),
+        in_specs=[VMEM] * 4,
+        out_specs=VMEM,
+        compiler_params=limit(8),
+        name="rest_scores",
+    )(kept(decoder), kept(partial), kept(left), kept(right))
+
+
 def gradients_kernel(distances, own_facts, *refs):
     pieces, refs = refs[: 2 * len(distances)], refs[2 * len(distances) :]
     total = refs[-1]
@@ -463,8 +502,12 @@
     third = mine + other_core(others)
     total, third = lax.optimization_barrier((total, third))
     third = return_by(3, third)
-    total, first_4 = lax.optimization_barrier((total, first_4))
-    (opposite,) = scores_of((4,), [first_4], decoder, own_facts)
+    last_left, last_right = first_4
+    total, last_left = lax.optimization_barrier((total, last_left))
+    partial = half_scores(decoder, last_left, tok_rows)
+    partial, last_right = lax.optimization_barrier((partial, last_right))
+    opposite = rest_scores(decoder, partial, last_left, last_right)
+    first_4 = last_left, last_right
     opposite = shift(opposite, -owners // 2)
     total, third = lax.optimization_barrier((total, third))
     decoder_grad = last_gradients(first_4, total)

time: 56.2 us -> 56.3 us (level)
    pallas_call x0 -> x2, Pallas kernels: none -> 0.9 us  [the longest x1 0.46 us: rest_scores(): pl.pallas_call(rest_kernel, out_shape=pltpu.VMEM((2 * KPB, partial.shape[...]
    pallas_call x4 -> x3, Pallas kernels: 3.72 us -> 2.99 us  [scores_of(): pl.pallas_call(functools.partial(scores_kernel, distances, split), out_sh...]
  transfers between devices with their start and end apart: 20 -> 20, of which waited for: 10 -> 10; matrix products, arithmetic and copies ran while one was open for 0% -> 0% of each run, Pallas kernels for 18% -> 19%
where the time goes in v17:
time: 56.3 us; the launch traced here: 56.2 us
  starting transfers between devices  24.5 us (44%)
  waiting for transfers between devices  18.6 us (33%)
  Pallas kernels  11.7 us (21%)
  between operations  0.79 us (1%)
  other arithmetic  0.62 us (1%)
    ppermute x15, starting transfers between devices, shift(): return lax.ppermute(x, 'dp', pairs)  19.3 us
    ppermute x15, waiting for transfers between devices, shift(): return lax.ppermute(x, 'dp', pairs)  17.3 us
    ppermute x2, starting transfers between devices, return_by(): return lax.ppermute(x, ('dp', 'width'), pairs)  4.89 us
    pallas_call x3, Pallas kernels, gradients_of(): pl.pallas_call(functools.partial(gradients_kernel, distances), out_shape=...  3.13 us
    pallas_call x3, Pallas kernels, scores_of(): pl.pallas_call(functools.partial(scores_kernel, distances, split), out_sh...  2.99 us
    pallas_call x1, Pallas kernels, last_gradients(): pl.pallas_call(last_gradients_kernel, out_shape=jax.ShapeDtypeStruct(tota...  1.74 us
    pallas_call x1, Pallas kernels, fetch(): pl.pallas_call(fetch_kernel, out_shape=pltpu.VMEM(x.shape, x.dtype), in_s...  1.6 us
    ppermute x3, waiting for transfers between devices, other_core(): return lax.ppermute(x, 'width', ((0, 1), (1, 0)))  1.28 us
  transfers between devices with their start and end apart: 20, of which 10 were waited for; matrix products, arithmetic and copies ran while one was open for 0% of the time, Pallas kernels for 19%

profile of v17, /device:TPU:0, one launch (start us, length us, event | category | flops | bytes accessed | tf_op | source)
XLA Modules:
  0.0 56.2 jit_solution(4820721449392051604)
XLA Ops:
  0.6 1.2 %prepare.1 = (bf16[1040,128]{1,0:T(8,128)(2,1)S(1)}, bf16[1024,128]{1,0:T(8,128)(2,1)S(1)}, bf16[1056,128]{1,0:T(8,128)(2,1)S(1)}, bf16[1056,128]{1,0:T(8,128)(2...) custom-call(s32[32]{0:T(128)} %refs_0_.1, s32[8,128]{1,0:T(8,128)} %bitcast.7, s32[32,128]{1,0:T(8,128)} %bitcast.5, ...), custom_call_target="tpu_custom_call" | custom-call | tf_op jit(solution)/shard_map/prepare/pallas_call | solution.py:124
  1.8 3.1 %collective-permute-start = (bf16[1040,128]{1,0:T(8,128)(2,1)S(1)}, bf16[1040,128]{1,0:T(8,128)(2,1)S(1)}, u32[]{:S(2)}, u32[]{:S(2)}) collective-permute-start(bf16[1040,128]{1,0:T(8,128)(2,1)S(1)} %get-tuple-element.35.refs_0_), channel_id=1, source_target_pairs={{0,4},{4,8},{8,12},{12,14},{14,10},{10,6},{6,2},{2,0},{1,5},{5,9},... | collective-permute-start | bytes 798728 | tf_op jit(solution)/shard_map/ppermute | solution.py:456
  4.9 0.0 collective-permute-start.1
  4.9 2.0 %collective-permute-start.3 = (bf16[1056,128]{1,0:T(8,128)(2,1)S(1)}, bf16[1056,128]{1,0:T(8,128)(2,1)S(1)}, u32[]{:S(2)}, u32[]{:S(2)}) collective-permute-start(bf16[1056,128]{1,0:T(8,128)(2,1)S(1)} %get-tuple-element.38), channel_id=1, source_target_pairs={{0,4},{4,8},{8,12},{12,14},{14,10},{10,6},{6,2},{2,0},{1,5},{5,9},... | collective-permute-start | bytes 811016 | tf_op jit(solution)/shard_map/ppermute | solution.py:456
  6.9 0.0 collective-permute-start.5
  6.9 1.6 %fetch.1.decoder = bf16[512,2048]{1,0:T(8,128)(2,1)S(1)} custom-call(bf16[512,2048]{1,0:T(8,128)(2,1)} %source.1), custom_call_target="tpu_custom_call" | custom-call | tf_op jit(solution)/shard_map/fetch/pallas_call | solution.py:158
  8.6 5.6 %collective-permute-done.1.refs_5_ = bf16[1024,128]{1,0:T(8,128)(2,1)S(1)} collective-permute-done((bf16[1024,128]{1,0:T(8,128)(2,1)S(1)}, bf16[1024,128]{1,0:T(8,128)(2,1)S(1)}, u32[]{:S(2)}, u32[]{:S(2)}) %collective-permute-start.1) | collective-permute-done | bytes 262176 | tf_op jit(solution)/shard_map/ppermute | solution.py:456
  14.1 0.0 collective-permute-done.refs_2_
  14.2 1.6 %collective-permute-start.2 = (bf16[1040,128]{1,0:T(8,128)(2,1)S(1)}, bf16[1040,128]{1,0:T(8,128)(2,1)S(1)}, u32[]{:S(2)}, u32[]{:S(2)}) collective-permute-start(bf16[1040,128]{1,0:T(8,128)(2,1)S(1)} %collective-permute-done.refs_2_), channel_id=1, source_target_pairs={{0,4},{4,8},{8,12},{12,14},{14,10},{10,6},{6,2},{2,0},{1,5},{5,9},... | collective-permute-start | bytes 798728 | tf_op jit(solution)/shard_map/ppermute | solution.py:456
  15.7 0.4 collective-permute-start.7
  16.2 1.7 %collective-permute-done.3.refs_3_ = bf16[1056,128]{1,0:T(8,128)(2,1)S(1)} collective-permute-done((bf16[1056,128]{1,0:T(8,128)(2,1)S(1)}, bf16[1056,128]{1,0:T(8,128)(2,1)S(1)}, u32[]{:S(2)}, u32[]{:S(2)}) %collective-permute-start.3) | collective-permute-done | bytes 270368 | tf_op jit(solution)/shard_map/ppermute | solution.py:456
  17.8 2.1 %collective-permute-start.4 = (bf16[1056,128]{1,0:T(8,128)(2,1)S(1)}, bf16[1056,128]{1,0:T(8,128)(2,1)S(1)}, u32[]{:S(2)}, u32[]{:S(2)}) collective-permute-start(bf16[1056,128]{1,0:T(8,128)(2,1)S(1)} %collective-permute-done.3.refs_3_), channel_id=1, source_target_pairs={{0,4},{4,8},{8,12},{12,14},{14,10},{10,6},{6,2},{2,0},{1,5},{5,9},... | collective-permute-start | bytes 811016 | tf_op jit(solution)/shard_map/ppermute | solution.py:456
  20.0 0.0 collective-permute-done.5.refs_4_
  20.0 0.0 collective-permute-start.6
  20.0 3.6 %collective-permute-done.2.refs_0_ = bf16[1040,128]{1,0:T(8,128)(2,1)S(1)} collective-permute-done((bf16[1040,128]{1,0:T(8,128)(2,1)S(1)}, bf16[1040,128]{1,0:T(8,128)(2,1)S(1)}, u32[]{:S(2)}, u32[]{:S(2)}) %collective-permute-start.2) | collective-permute-done | bytes 266272 | tf_op jit(solution)/shard_map/ppermute | solution.py:456
  23.6 2.1 %collective-permute-start.8 = (bf16[1040,128]{1,0:T(8,128)(2,1)S(1)}, bf16[1040,128]{1,0:T(8,128)(2,1)S(1)}, u32[]{:S(2)}, u32[]{:S(2)}) collective-permute-start(bf16[1040,128]{1,0:T(8,128)(2,1)S(1)} %collective-permute-done.2.refs_0_), channel_id=1, source_target_pairs={{0,4},{4,8},{8,12},{12,14},{14,10},{10,6},{6,2},{2,0},{1,5},{5,9},... | collective-permute-start | bytes 798728 | tf_op jit(solution)/shard_map/ppermute | solution.py:456
  25.7 0.0 collective-permute-done.7.refs_3_
  25.7 0.0 collective-permute-start.9
  25.7 1.4 %scores.3 = (f32[8,128]{1,0:T(8,128)S(1)}, f32[8,128]{1,0:T(8,128)S(1)}, f32[8,128]{1,0:T(8,128)S(1)}) custom-call(bf16[512,2048]{1,0:T(8,128)(2,1)S(1)} %fetch.1.decoder, f32[8,128]{1,0:T(8,128)S(1)} %get-tuple-element.34.own_facts, bf16[1040,128]{1,0:T(8,128)(2,1)S(1)} %get-tuple-element.35.refs_0_, bf16[1024,128]{1,0:T(8,128)(2,1)S(1)} %get-tuple-element.36.refs_1_, ...), custom_call_target="tpu_custom_call" | custom-call | tf_op jit(solution)/shard_map/scores/pallas_call | solution.py:278
  27.1 2.3 %collective-permute-done.4.onward = bf16[1056,128]{1,0:T(8,128)(2,1)S(1)} collective-permute-done((bf16[1056,128]{1,0:T(8,128)(2,1)S(1)}, bf16[1056,128]{1,0:T(8,128)(2,1)S(1)}, u32[]{:S(2)}, u32[]{:S(2)}) %collective-permute-start.4) | collective-permute-done | bytes 270368 | tf_op jit(solution)/shard_map/ppermute | solution.py:456
  29.3 2.0 %collective-permute-done.6.back = bf16[1056,128]{1,0:T(8,128)(2,1)S(1)} collective-permute-done((bf16[1056,128]{1,0:T(8,128)(2,1)S(1)}, bf16[1056,128]{1,0:T(8,128)(2,1)S(1)}, u32[]{:S(2)}, u32[]{:S(2)}) %collective-permute-start.6) | collective-permute-done | bytes 270368 | tf_op jit(solution)/shard_map/ppermute | solution.py:456
  31.4 0.1 stamp.1
  31.4 1.6 %collective-permute-start.11 = (bf16[1056,128]{1,0:T(8,128)(2,1)S(1)}, bf16[1056,128]{1,0:T(8,128)(2,1)S(1)}, u32[]{:S(2)}, u32[]{:S(2)}) collective-permute-start(bf16[1056,128]{1,0:T(8,128)(2,1)S(1)} %get-tuple-element.44.refs_1_), channel_id=1, source_target_pairs={{0,4},{4,8},{8,12},{12,14},{14,10},{10,6},{6,2},{2,0},{1,5},{5,9},... | collective-permute-start | bytes 811016 | tf_op jit(solution)/shard_map/ppermute | solution.py:456
  33.1 0.4 collective-permute-start.12
  33.5 0.8 %scores.4 = (f32[8,128]{1,0:T(8,128)S(1)}, f32[8,128]{1,0:T(8,128)S(1)}) custom-call(bf16[512,2048]{1,0:T(8,128)(2,1)S(1)} %fetch.1.decoder, f32[8,128]{1,0:T(8,128)S(1)} %get-tuple-element.34.own_facts, bf16[1040,128]{1,0:T(8,128)(2,1)S(1)} %collective-permute-done.2.refs_0_, bf16[1056,128]{1,0:T(8,128)(2,1)S(1)} %get-tuple-element.44.refs_1_, ...), custom_call_target="tpu_custom_call" | custom-call | tf_op jit(solution)/shard_map/scores/pallas_call | solution.py:278
  34.3 0.1 collective-permute-start.10
  34.4 1.3 %gradients.3.refs_4_ = f32[512,2048]{1,0:T(8,128)S(1)} custom-call(f32[8,128]{1,0:T(8,128)S(1)} %get-tuple-element.34.own_facts, bf16[1040,128]{1,0:T(8,128)(2,1)S(1)} %get-tuple-element.35.refs_0_, bf16[1024,128]{1,0:T(8,128)(2,1)S(1)} %get-tuple-element.36.refs_1_, bf16[1040,128]{1,0:T(8,128)(2,1)S(1)} %collective-permute-done.refs_2_, ...), custom_call_target="tpu_custom_call" | custom-call | tf_op jit(solution)/shard_map/gradients/pallas_call | solution.py:338
  35.7 0.9 %gradients.4.refs_4_ = f32[512,2048]{1,0:T(8,128)S(1)} custom-call(f32[8,128]{1,0:T(8,128)S(1)} %get-tuple-element.34.own_facts, bf16[1040,128]{1,0:T(8,128)(2,1)S(1)} %collective-permute-done.2.refs_0_, bf16[1056,128]{1,0:T(8,128)(2,1)S(1)} %get-tuple-element.44.refs_1_, ...), custom_call_target="tpu_custom_call", output_to_operand_aliasing={{}: (5, {})} | custom-call | tf_op jit(solution)/shard_map/gradients/pallas_call | solution.py:338
  36.6 0.0 collective-permute-done.10
  36.6 0.3 collective-permute-done.9.refs_3_
  37.0 0.0 collective-permute-done.8.refs_0_
  37.0 1.6 %collective-permute-start.14 = (bf16[1040,128]{1,0:T(8,128)(2,1)S(1)}, bf16[1040,128]{1,0:T(8,128)(2,1)S(1)}, u32[]{:S(2)}, u32[]{:S(2)}) collective-permute-start(bf16[1040,128]{1,0:T(8,128)(2,1)S(1)} %collective-permute-done.8.refs_0_), channel_id=1, source_target_pairs={{0,4},{4,8},{8,12},{12,14},{14,10},{10,6},{6,2},{2,0},{1,5},{5,9},... | collective-permute-start | bytes 798728 | tf_op jit(solution)/shard_map/ppermute | solution.py:456
  38.6 0.4 collective-permute-start.15
  39.0 1.4 %collective-permute-start.18 = (f32[32,128]{1,0:T(8,128)S(1)}, f32[32,128]{1,0:T(8,128)S(1)}, u32[]{:S(2)}, u32[]{:S(2)}) collective-permute-start(f32[32,128]{1,0:T(8,128)S(1)} %concatenate.3), channel_id=1, source_target_pairs={{0,6},{1,9},{4,2},{5,13},{8,0},{9,15},{12,4},{13,11},{14,8},{15,7}... | collective-permute-start | bytes 49160 | tf_op jit(solution)/shard_map/ppermute | solution.py:474
  40.4 0.0 collective-permute-done.11.refs_1_.onward
  40.4 1.0 %collective-permute-done.12.refs_2_.back = bf16[1056,128]{1,0:T(8,128)(2,1)S(1)} collective-permute-done((bf16[1056,128]{1,0:T(8,128)(2,1)S(1)}, bf16[1056,128]{1,0:T(8,128)(2,1)S(1)}, u32[]{:S(2)}, u32[]{:S(2)}) %collective-permute-start.12) | collective-permute-done | bytes 270368 | tf_op jit(solution)/shard_map/ppermute | solution.py:456
  41.4 0.8 %scores.5 = (f32[8,128]{1,0:T(8,128)S(1)}, f32[8,128]{1,0:T(8,128)S(1)}) custom-call(bf16[512,2048]{1,0:T(8,128)(2,1)S(1)} %fetch.1.decoder, f32[8,128]{1,0:T(8,128)S(1)} %get-tuple-element.34.own_facts, bf16[1040,128]{1,0:T(8,128)(2,1)S(1)} %collective-permute-done.8.refs_0_, bf16[1056,128]{1,0:T(8,128)(2,1)S(1)} %collective-permute-done.11.refs_1_.onward, ...), custom_call_target="tpu_custom_call" | custom-call | tf_op jit(solution)/shard_map/scores/pallas_call | solution.py:278
  42.2 0.1 collective-permute-start.13
  42.3 0.9 %gradients.5.total = f32[512,2048]{1,0:T(8,128)S(1)} custom-call(f32[8,128]{1,0:T(8,128)S(1)} %get-tuple-element.34.own_facts, bf16[1040,128]{1,0:T(8,128)(2,1)S(1)} %collective-permute-done.8.refs_0_, bf16[1056,128]{1,0:T(8,128)(2,1)S(1)} %collective-permute-done.11.refs_1_.onward, ...), custom_call_target="tpu_custom_call", output_to_operand_aliasing={{}: (5, {})} | custom-call | tf_op jit(solution)/shard_map/gradients/pallas_call | solution.py:338
  43.3 0.2 collective-permute-done.13
  43.5 3.5 %collective-permute-start.16 = (f32[8,128]{1,0:T(8,128)S(1)}, f32[8,128]{1,0:T(8,128)S(1)}, u32[]{:S(2)}, u32[]{:S(2)}) collective-permute-start(f32[8,128]{1,0:T(8,128)S(1)} %add.12), channel_id=1, source_target_pairs={{0,10},{1,13},{4,6},{5,15},{8,2},{9,11},{12,0},{13,7},{14,4},{15,3... | collective-permute-start | bytes 12296 | tf_op jit(solution)/shard_map/ppermute | solution.py:474
  47.0 0.0 collective-permute-done.14.piece.left
  47.0 0.4 half_scores.1.partial
  47.4 0.0 collective-permute-done.15.right
  47.4 0.5 rest_scores.1
  47.9 3.7 %collective-permute-start.17 = (f32[8,128]{1,0:T(8,128)S(1)}, f32[8,128]{1,0:T(8,128)S(1)}, u32[]{:S(2)}, u32[]{:S(2)}) collective-permute-start(f32[8,128]{1,0:T(8,128)S(1)} %rest_scores.1), channel_id=1, source_target_pairs={{0,14},{4,10},{8,6},{12,2},{14,0},{10,4},{6,8},{2,12},{1,15},{5,11... | collective-permute-start | bytes 12296 | tf_op jit(solution)/shard_map/ppermute | solution.py:456
  51.7 0.0 collective-permute-done.18
  51.7 0.0 collective-permute-done.16.third
  51.7 1.7 %last_gradients.1 = bf16[512,2048]{1,0:T(8,128)(2,1)} custom-call(bf16[1040,128]{1,0:T(8,128)(2,1)S(1)} %collective-permute-done.14.piece.left, bf16[1024,128]{1,0:T(8,128)(2,1)S(1)} %collective-permute-done.15.right, f32[512,2048]{1,0:T(8,128)S(1)} %gradients.5.total), custom_call_target="tpu_custom_call" | custom-call | tf_op jit(solution)/shard_map/last_gradients/pallas_call | solution.py:365
  53.4 0.9 %collective-permute-done.17.opposite = f32[8,128]{1,0:T(8,128)S(1)} collective-permute-done((f32[8,128]{1,0:T(8,128)S(1)}, f32[8,128]{1,0:T(8,128)S(1)}, u32[]{:S(2)}, u32[]{:S(2)}) %collective-permute-start.17) | collective-permute-done | bytes 4128 | tf_op jit(solution)/shard_map/ppermute | solution.py:456
  54.3 0.2 collective-permute-start.19
  54.5 1.1 %collective-permute-done.19 = f32[32,128]{1,0:T(8,128)S(1)} collective-permute-done((f32[32,128]{1,0:T(8,128)S(1)}, f32[32,128]{1,0:T(8,128)S(1)}, u32[]{:S(2)}, u32[]{:S(2)}) %collective-permute-start.19) | collective-permute-done | bytes 16416 | tf_op jit(solution)/shard_map/ppermute | solution.py:467
  55.6 0.6 %add_bitcast_fusion = f32[128,32]{0,1:T(8,128)} fusion(f32[32,128]{1,0:T(8,128)S(1)} %unpack.1, f32[32,128]{1,0:T(8,128)S(1)} %collective-permute-done.19), kind=kLoop, calls=%fused_computation | loop fusion | flops 4096 | bytes 49152 | tf_op jit(solution)/shard_map/transpose | solution.py:517
  (5 shorter events, 0.0 us)
Async XLA Ops:
  1.8 12.3 %collective-permute-start = (bf16[1040,128]{1,0:T(8,128)(2,1)S(1)}, bf16[1040,128]{1,0:T(8,128)(2,1)S(1)}, u32[]{:S(2)}, u32[]{:S(2)}) collective-permute-start(bf16[1040,128]{1,0:T(8,128)(2,1)S(1)} %get-tuple-element.35.refs_0_), channel_id=1, source_target_pairs={{0,4},{4,8},{8,12},{12,14},{14,10},{10,6},{6,2},{2,0},{1,5},{5,9},... | collective-permute-start | bytes 798728 | tf_op jit(solution)/shard_map/ppermute | solution.py:456
  4.9 9.2 %collective-permute-start.1 = (bf16[1024,128]{1,0:T(8,128)(2,1)S(1)}, bf16[1024,128]{1,0:T(8,128)(2,1)S(1)}, u32[]{:S(2)}, u32[]{:S(2)}) collective-permute-start(bf16[1024,128]{1,0:T(8,128)(2,1)S(1)} %get-tuple-element.36.refs_1_), channel_id=1, source_target_pairs={{0,2},{4,0},{8,4},{12,8},{14,12},{10,14},{6,10},{2,6},{1,3},{5,1},... | collective-permute-start | bytes 786440 | tf_op jit(solution)/shard_map/ppermute | solution.py:456
  4.9 12.9 %collective-permute-start.3 = (bf16[1056,128]{1,0:T(8,128)(2,1)S(1)}, bf16[1056,128]{1,0:T(8,128)(2,1)S(1)}, u32[]{:S(2)}, u32[]{:S(2)}) collective-permute-start(bf16[1056,128]{1,0:T(8,128)(2,1)S(1)} %get-tuple-element.38), channel_id=1, source_target_pairs={{0,4},{4,8},{8,12},{12,14},{14,10},{10,6},{6,2},{2,0},{1,5},{5,9},... | collective-permute-start | bytes 811016 | tf_op jit(solution)/shard_map/ppermute | solution.py:456
  6.9 13.1 %collective-permute-start.5 = (bf16[1056,128]{1,0:T(8,128)(2,1)S(1)}, bf16[1056,128]{1,0:T(8,128)(2,1)S(1)}, u32[]{:S(2)}, u32[]{:S(2)}) collective-permute-start(bf16[1056,128]{1,0:T(8,128)(2,1)S(1)} %get-tuple-element.39), channel_id=1, source_target_pairs={{0,2},{4,0},{8,4},{12,8},{14,12},{10,14},{6,10},{2,6},{1,3},{5,1},... | collective-permute-start | bytes 811016 | tf_op jit(solution)/shard_map/ppermute | solution.py:456
  14.2 9.4 %collective-permute-start.2 = (bf16[1040,128]{1,0:T(8,128)(2,1)S(1)}, bf16[1040,128]{1,0:T(8,128)(2,1)S(1)}, u32[]{:S(2)}, u32[]{:S(2)}) collective-permute-start(bf16[1040,128]{1,0:T(8,128)(2,1)S(1)} %collective-permute-done.refs_2_), channel_id=1, source_target_pairs={{0,4},{4,8},{8,12},{12,14},{14,10},{10,6},{6,2},{2,0},{1,5},{5,9},... | collective-permute-start | bytes 798728 | tf_op jit(solution)/shard_map/ppermute | solution.py:456
  15.7 10.0 %collective-permute-start.7 = (bf16[1024,128]{1,0:T(8,128)(2,1)S(1)}, bf16[1024,128]{1,0:T(8,128)(2,1)S(1)}, u32[]{:S(2)}, u32[]{:S(2)}) collective-permute-start(bf16[1024,128]{1,0:T(8,128)(2,1)S(1)} %collective-permute-done.1.refs_5_), channel_id=1, source_target_pairs={{0,2},{4,0},{8,4},{12,8},{14,12},{10,14},{6,10},{2,6},{1,3},{5,1},... | collective-permute-start | bytes 786440 | tf_op jit(solution)/shard_map/ppermute | solution.py:456
  17.8 11.5 %collective-permute-start.4 = (bf16[1056,128]{1,0:T(8,128)(2,1)S(1)}, bf16[1056,128]{1,0:T(8,128)(2,1)S(1)}, u32[]{:S(2)}, u32[]{:S(2)}) collective-permute-start(bf16[1056,128]{1,0:T(8,128)(2,1)S(1)} %collective-permute-done.3.refs_3_), channel_id=1, source_target_pairs={{0,4},{4,8},{8,12},{12,14},{14,10},{10,6},{6,2},{2,0},{1,5},{5,9},... | collective-permute-start | bytes 811016 | tf_op jit(solution)/shard_map/ppermute | solution.py:456
  20.0 11.4 %collective-permute-start.6 = (bf16[1056,128]{1,0:T(8,128)(2,1)S(1)}, bf16[1056,128]{1,0:T(8,128)(2,1)S(1)}, u32[]{:S(2)}, u32[]{:S(2)}) collective-permute-start(bf16[1056,128]{1,0:T(8,128)(2,1)S(1)} %collective-permute-done.5.refs_4_), channel_id=1, source_target_pairs={{0,2},{4,0},{8,4},{12,8},{14,12},{10,14},{6,10},{2,6},{1,3},{5,1},... | collective-permute-start | bytes 811016 | tf_op jit(solution)/shard_map/ppermute | solution.py:456
  23.6 13.4 %collective-permute-start.8 = (bf16[1040,128]{1,0:T(8,128)(2,1)S(1)}, bf16[1040,128]{1,0:T(8,128)(2,1)S(1)}, u32[]{:S(2)}, u32[]{:S(2)}) collective-permute-start(bf16[1040,128]{1,0:T(8,128)(2,1)S(1)} %collective-permute-done.2.refs_0_), channel_id=1, source_target_pairs={{0,4},{4,8},{8,12},{12,14},{14,10},{10,6},{6,2},{2,0},{1,5},{5,9},... | collective-permute-start | bytes 798728 | tf_op jit(solution)/shard_map/ppermute | solution.py:456
  25.7 11.3 %collective-permute-start.9 = (bf16[1024,128]{1,0:T(8,128)(2,1)S(1)}, bf16[1024,128]{1,0:T(8,128)(2,1)S(1)}, u32[]{:S(2)}, u32[]{:S(2)}) collective-permute-start(bf16[1024,128]{1,0:T(8,128)(2,1)S(1)} %collective-permute-done.7.refs_3_), channel_id=1, source_target_pairs={{0,2},{4,0},{8,4},{12,8},{14,12},{10,14},{6,10},{2,6},{1,3},{5,1},... | collective-permute-start | bytes 786440 | tf_op jit(solution)/shard_map/ppermute | solution.py:456
  31.4 9.0 %collective-permute-start.11 = (bf16[1056,128]{1,0:T(8,128)(2,1)S(1)}, bf16[1056,128]{1,0:T(8,128)(2,1)S(1)}, u32[]{:S(2)}, u32[]{:S(2)}) collective-permute-start(bf16[1056,128]{1,0:T(8,128)(2,1)S(1)} %get-tuple-element.44.refs_1_), channel_id=1, source_target_pairs={{0,4},{4,8},{8,12},{12,14},{14,10},{10,6},{6,2},{2,0},{1,5},{5,9},... | collective-permute-start | bytes 811016 | tf_op jit(solution)/shard_map/ppermute | solution.py:456
  33.1 8.4 %collective-permute-start.12 = (bf16[1056,128]{1,0:T(8,128)(2,1)S(1)}, bf16[1056,128]{1,0:T(8,128)(2,1)S(1)}, u32[]{:S(2)}, u32[]{:S(2)}) collective-permute-start(bf16[1056,128]{1,0:T(8,128)(2,1)S(1)} %get-tuple-element.45.refs_2_), channel_id=1, source_target_pairs={{0,2},{4,0},{8,4},{12,8},{14,12},{10,14},{6,10},{2,6},{1,3},{5,1},... | collective-permute-start | bytes 811016 | tf_op jit(solution)/shard_map/ppermute | solution.py:456
  34.3 2.3 %collective-permute-start.10 = (f32[8,128]{1,0:T(8,128)S(1)}, f32[8,128]{1,0:T(8,128)S(1)}, u32[]{:S(2)}, u32[]{:S(2)}) collective-permute-start(f32[8,128]{1,0:T(8,128)S(1)} %get-tuple-element.47), channel_id=1, source_target_pairs={{0,1},{1,0},{2,3},{3,2},{4,5},{5,4},{6,7},{7,6},{8,9},{9,8},{10,11... | collective-permute-start | bytes 12296 | tf_op jit(solution)/shard_map/ppermute | solution.py:467
  37.0 10.0 %collective-permute-start.14 = (bf16[1040,128]{1,0:T(8,128)(2,1)S(1)}, bf16[1040,128]{1,0:T(8,128)(2,1)S(1)}, u32[]{:S(2)}, u32[]{:S(2)}) collective-permute-start(bf16[1040,128]{1,0:T(8,128)(2,1)S(1)} %collective-permute-done.8.refs_0_), channel_id=1, source_target_pairs={{0,4},{4,8},{8,12},{12,14},{14,10},{10,6},{6,2},{2,0},{1,5},{5,9},... | collective-permute-start | bytes 798728 | tf_op jit(solution)/shard_map/ppermute | solution.py:456
  38.6 8.9 %collective-permute-start.15 = (bf16[1024,128]{1,0:T(8,128)(2,1)S(1)}, bf16[1024,128]{1,0:T(8,128)(2,1)S(1)}, u32[]{:S(2)}, u32[]{:S(2)}) collective-permute-start(bf16[1024,128]{1,0:T(8,128)(2,1)S(1)} %collective-permute-done.9.refs_3_), channel_id=1, source_target_pairs={{0,2},{4,0},{8,4},{12,8},{14,12},{10,14},{6,10},{2,6},{1,3},{5,1},... | collective-permute-start | bytes 786440 | tf_op jit(solution)/shard_map/ppermute | solution.py:456
  39.0 12.7 %collective-permute-start.18 = (f32[32,128]{1,0:T(8,128)S(1)}, f32[32,128]{1,0:T(8,128)S(1)}, u32[]{:S(2)}, u32[]{:S(2)}) collective-permute-start(f32[32,128]{1,0:T(8,128)S(1)} %concatenate.3), channel_id=1, source_target_pairs={{0,6},{1,9},{4,2},{5,13},{8,0},{9,15},{12,4},{13,11},{14,8},{15,7}... | collective-permute-start | bytes 49160 | tf_op jit(solution)/shard_map/ppermute | solution.py:474
  42.2 1.2 %collective-permute-start.13 = (f32[8,128]{1,0:T(8,128)S(1)}, f32[8,128]{1,0:T(8,128)S(1)}, u32[]{:S(2)}, u32[]{:S(2)}) collective-permute-start(f32[8,128]{1,0:T(8,128)S(1)} %get-tuple-element.52), channel_id=1, source_target_pairs={{0,1},{1,0},{2,3},{3,2},{4,5},{5,4},{6,7},{7,6},{8,9},{9,8},{10,11... | collective-permute-start | bytes 12296 | tf_op jit(solution)/shard_map/ppermute | solution.py:467
  43.5 8.2 %collective-permute-start.16 = (f32[8,128]{1,0:T(8,128)S(1)}, f32[8,128]{1,0:T(8,128)S(1)}, u32[]{:S(2)}, u32[]{:S(2)}) collective-permute-start(f32[8,128]{1,0:T(8,128)S(1)} %add.12), channel_id=1, source_target_pairs={{0,10},{1,13},{4,6},{5,15},{8,2},{9,11},{12,0},{13,7},{14,4},{15,3... | collective-permute-start | bytes 12296 | tf_op jit(solution)/shard_map/ppermute | solution.py:474
  47.9 6.4 %collective-permute-start.17 = (f32[8,128]{1,0:T(8,128)S(1)}, f32[8,128]{1,0:T(8,128)S(1)}, u32[]{:S(2)}, u32[]{:S(2)}) collective-permute-start(f32[8,128]{1,0:T(8,128)S(1)} %rest_scores.1), channel_id=1, source_target_pairs={{0,14},{4,10},{8,6},{12,2},{14,0},{10,4},{6,8},{2,12},{1,15},{5,11... | collective-permute-start | bytes 12296 | tf_op jit(solution)/shard_map/ppermute | solution.py:456
  54.3 1.2 %collective-permute-start.19 = (f32[32,128]{1,0:T(8,128)S(1)}, f32[32,128]{1,0:T(8,128)S(1)}, u32[]{:S(2)}, u32[]{:S(2)}) collective-permute-start(f32[32,128]{1,0:T(8,128)S(1)} %unpack.1), channel_id=1, source_target_pairs={{0,1},{1,0},{2,3},{3,2},{4,5},{5,4},{6,7},{7,6},{8,9},{9,8},{10,11... | collective-permute-start | bytes 49160 | tf_op jit(solution)/shard_map/ppermute | solution.py:467

commit v18 on v12

--- a/solution.py
+++ b/solution.py
@@ -307,10 +307,11 @@
     )(*operands)
 
 
-def last_gradients_kernel(left, right, total, out, rounded, sems):
+def last_gradients_kernel(distances, own_facts, *refs):
+    pieces, (total, out, rounded, sems) = refs[:-4], refs[-4:]
     copies = []
-    facts = [last_facts_in(left)]
-    for columns, part in gradient_blocks(facts, (left, right), out.shape[1]):
+    facts = facts_of(distances, own_facts, pieces)
+    for columns, part in gradient_blocks(facts, pieces, out.shape[1]):
         rounded[:, columns] = (total[:, columns] + part).astype(out.dtype)
         copies.append(
             pltpu.make_async_copy(
@@ -322,11 +323,13 @@
         copy.wait()
 
 
-def last_gradients(pair, total):
-    return pl.pallas_call(
-        last_gradients_kernel,
+def last_gradients(distances, pairs, own_facts, total):
+    operands = [kept(own_facts)] + [kept(piece) for pair in pairs for piece in pair]
+    operands.append(kept(total))
+    return pl.pallas_call(
+        functools.partial(last_gradients_kernel, distances),
         out_shape=jax.ShapeDtypeStruct(total.shape, jnp.bfloat16),
-        in_specs=[VMEM] * 3,
+        in_specs=[VMEM] * len(operands),
         out_specs=ANY,
         scratch_shapes=[
             pltpu.VMEM(total.shape, jnp.bfloat16),
@@ -334,7 +337,7 @@
         ],
         compiler_params=limit(16),
         name="last_gradients",
-    )(kept(pair[0]), kept(pair[1]), kept(total))
+    )(*operands)
 
 
 def stamp_kernel(onward, back, for_onward, for_back, onward_out, back_out, rows, sems):
@@ -378,7 +381,7 @@
     )(*[kept(piece) for piece in pieces], *[kept(value) for value in values])
 
 
-def unpack_kernel(owners, slots, own, onward, back, second, third, opposite, out):
+def unpack_kernel(owners, slots, own, onward, back, second, ahead, behind, opposite, out):
     owner = slots[...] // BLK_DEV
     start = onward.shape[0] - FACTS
     way = 1 - 2 * lax.axis_index("width")
@@ -386,7 +389,8 @@
     for distance, piece in ((-1, onward), (1, back)):
         rows = piece[start : start + 16, :].astype(jnp.float32)
         returned.append((distance, rows[:KPB] + rows[KPB : 2 * KPB]))
-    returned += [(2 * way, second[...]), (3 * way, third[...]), (4, opposite[...])]
+    returned += [(2 * way, second[...]), (3, ahead[...]), (-3, behind[...])]
+    returned.append((4, opposite[...]))
     mine = [owner == peer_at(distance, owners) for distance, _ in returned]
     for k in range(KPB):
         total = jnp.zeros(owner.shape, jnp.float32)
@@ -458,18 +462,14 @@
     second = return_by(2, jnp.concatenate([second, jnp.zeros((24, 128), jnp.float32)]))[:8]
     first_4 = hop(first_3)
     pairs = [(first_3[0], second_3[0]), (second_3[1], first_3[1])]
-    mine, others = scores_of((-3, 3), pairs, decoder, own_facts, True)
-    total = gradients_of((-3, 3), pairs, own_facts, decoder.shape, total)
-    third = mine + other_core(others)
-    total, third = lax.optimization_barrier((total, third))
-    third = return_by(3, third)
-    total, first_4 = lax.optimization_barrier((total, first_4))
+    onward, back = scores_of((-3, 3), pairs, decoder, own_facts)
+    ahead, behind = shift(onward, -3), shift(back, 3)
     (opposite,) = scores_of((4,), [first_4], decoder, own_facts)
     opposite = shift(opposite, -owners // 2)
-    total, third = lax.optimization_barrier((total, third))
-    decoder_grad = last_gradients(first_4, total)
+    total, ahead, behind = lax.optimization_barrier((total, ahead, behind))
+    decoder_grad = last_gradients((-3, 3, 4), pairs + [first_4], own_facts, total)
     decoder_grad, opposite = lax.optimization_barrier((decoder_grad, opposite))
-    act_grad = unpack(slots, own, *second_3, second, third, opposite)
+    act_grad = unpack(slots, own, *second_3, second, ahead, behind, opposite)
     act_grad = act_grad + other_core(act_grad)
     return (decoder_grad, act_grad.T)
 

time: 56.2 us -> 56.2 us (level)
  starting transfers between devices: 24.5 us -> 25.5 us
  waiting for transfers between devices: 18.6 us -> 18 us
    ppermute x15 -> x17, starting transfers between devices: 19.3 us -> 24 us  [shift(): return lax.ppermute(x, 'dp', pairs)]
    ppermute x2 -> x1, starting transfers between devices: 4.9 us -> 1.38 us  [return_by(): return lax.ppermute(x, ('dp', 'width'), pairs)]
    pallas_call x3 -> x2, Pallas kernels: 3.14 us -> 2.21 us  [gradients_of(): pl.pallas_call(functools.partial(gradients_kernel, distances), out_shape=...]
    ppermute x15 -> x17, waiting for transfers between devices: 17.3 us -> 16.8 us  [shift(): return lax.ppermute(x, 'dp', pairs)]
    ppermute x3 -> x2, waiting for transfers between devices: 1.28 us -> 1.17 us  [other_core(): return lax.ppermute(x, 'width', ((0, 1), (1, 0)))]
  transfers between devices with their start and end apart: 20 -> 20, of which waited for: 10 -> 9; matrix products, arithmetic and copies ran while one was open for 0% -> 0% of each run, Pallas kernels for 18% -> 18%
where the time goes in v18:
time: 56.2 us; the launch traced here: 56 us
  starting transfers between devices  25.5 us (45%)
  waiting for transfers between devices  18 us (32%)
  Pallas kernels  11.1 us (20%)
  between operations  0.77 us (1%)
  other arithmetic  0.61 us (1%)
    ppermute x17, starting transfers between devices, shift(): return lax.ppermute(x, 'dp', pairs)  24 us
    ppermute x17, waiting for transfers between devices, shift(): return lax.ppermute(x, 'dp', pairs)  16.8 us
    pallas_call x4, Pallas kernels, scores_of(): pl.pallas_call(functools.partial(scores_kernel, distances, split), out_sh...  3.72 us
    pallas_call x1, Pallas kernels, last_gradients(): pl.pallas_call(functools.partial(last_gradients_kernel, distances), out_s...  2.28 us
    pallas_call x2, Pallas kernels, gradients_of(): pl.pallas_call(functools.partial(gradients_kernel, distances), out_shape=...  2.21 us
    pallas_call x1, Pallas kernels, fetch(): pl.pallas_call(fetch_kernel, out_shape=pltpu.VMEM(x.shape, x.dtype), in_s...  1.6 us
    ppermute x1, starting transfers between devices, return_by(): return lax.ppermute(x, ('dp', 'width'), pairs)  1.38 us
    pallas_call x1, Pallas kernels, prepare(): pl.pallas_call(functools.partial(prepare_kernel, owners), out_shape=(piec...  1.2 us
  transfers between devices with their start and end apart: 20, of which 9 were waited for; matrix products, arithmetic and copies ran while one was open for 0% of the time, Pallas kernels for 18%

profile of v18, /device:TPU:0, one launch (start us, length us, event | category | flops | bytes accessed | tf_op | source)
XLA Modules:
  0.0 56.0 jit_solution(16614402263561576387)
XLA Ops:
  0.6 1.2 %prepare.1 = (bf16[1040,128]{1,0:T(8,128)(2,1)S(1)}, bf16[1024,128]{1,0:T(8,128)(2,1)S(1)}, bf16[1056,128]{1,0:T(8,128)(2,1)S(1)}, bf16[1056,128]{1,0:T(8,128)(2...) custom-call(s32[32]{0:T(128)} %refs_0_.1, s32[8,128]{1,0:T(8,128)} %bitcast.7, s32[32,128]{1,0:T(8,128)} %bitcast.5, ...), custom_call_target="tpu_custom_call" | custom-call | tf_op jit(solution)/shard_map/prepare/pallas_call | solution.py:124
  1.8 3.1 %collective-permute-start = (bf16[1040,128]{1,0:T(8,128)(2,1)S(1)}, bf16[1040,128]{1,0:T(8,128)(2,1)S(1)}, u32[]{:S(2)}, u32[]{:S(2)}) collective-permute-start(bf16[1040,128]{1,0:T(8,128)(2,1)S(1)} %get-tuple-element.30.refs_0_), channel_id=1, source_target_pairs={{0,4},{4,8},{8,12},{12,14},{14,10},{10,6},{6,2},{2,0},{1,5},{5,9},... | collective-permute-start | bytes 798728 | tf_op jit(solution)/shard_map/ppermute | solution.py:421
  4.9 0.0 collective-permute-start.1
  4.9 2.0 %collective-permute-start.3 = (bf16[1056,128]{1,0:T(8,128)(2,1)S(1)}, bf16[1056,128]{1,0:T(8,128)(2,1)S(1)}, u32[]{:S(2)}, u32[]{:S(2)}) collective-permute-start(bf16[1056,128]{1,0:T(8,128)(2,1)S(1)} %get-tuple-element.33), channel_id=1, source_target_pairs={{0,4},{4,8},{8,12},{12,14},{14,10},{10,6},{6,2},{2,0},{1,5},{5,9},... | collective-permute-start | bytes 811016 | tf_op jit(solution)/shard_map/ppermute | solution.py:421
  6.9 0.0 collective-permute-start.5
  6.9 1.6 %fetch.1.decoder = bf16[512,2048]{1,0:T(8,128)(2,1)S(1)} custom-call(bf16[512,2048]{1,0:T(8,128)(2,1)} %source.1), custom_call_target="tpu_custom_call" | custom-call | tf_op jit(solution)/shard_map/fetch/pallas_call | solution.py:158
  8.6 5.6 %collective-permute-done.1.refs_5_ = bf16[1024,128]{1,0:T(8,128)(2,1)S(1)} collective-permute-done((bf16[1024,128]{1,0:T(8,128)(2,1)S(1)}, bf16[1024,128]{1,0:T(8,128)(2,1)S(1)}, u32[]{:S(2)}, u32[]{:S(2)}) %collective-permute-start.1) | collective-permute-done | bytes 262176 | tf_op jit(solution)/shard_map/ppermute | solution.py:421
  14.1 0.0 collective-permute-done.refs_2_
  14.2 1.6 %collective-permute-start.2 = (bf16[1040,128]{1,0:T(8,128)(2,1)S(1)}, bf16[1040,128]{1,0:T(8,128)(2,1)S(1)}, u32[]{:S(2)}, u32[]{:S(2)}) collective-permute-start(bf16[1040,128]{1,0:T(8,128)(2,1)S(1)} %collective-permute-done.refs_2_), channel_id=1, source_target_pairs={{0,4},{4,8},{8,12},{12,14},{14,10},{10,6},{6,2},{2,0},{1,5},{5,9},... | collective-permute-start | bytes 798728 | tf_op jit(solution)/shard_map/ppermute | solution.py:421
  15.7 0.4 collective-permute-start.7
  16.2 1.7 %collective-permute-done.3.refs_3_ = bf16[1056,128]{1,0:T(8,128)(2,1)S(1)} collective-permute-done((bf16[1056,128]{1,0:T(8,128)(2,1)S(1)}, bf16[1056,128]{1,0:T(8,128)(2,1)S(1)}, u32[]{:S(2)}, u32[]{:S(2)}) %collective-permute-start.3) | collective-permute-done | bytes 270368 | tf_op jit(solution)/shard_map/ppermute | solution.py:421
  17.8 2.1 %collective-permute-start.4 = (bf16[1056,128]{1,0:T(8,128)(2,1)S(1)}, bf16[1056,128]{1,0:T(8,128)(2,1)S(1)}, u32[]{:S(2)}, u32[]{:S(2)}) collective-permute-start(bf16[1056,128]{1,0:T(8,128)(2,1)S(1)} %collective-permute-done.3.refs_3_), channel_id=1, source_target_pairs={{0,4},{4,8},{8,12},{12,14},{14,10},{10,6},{6,2},{2,0},{1,5},{5,9},... | collective-permute-start | bytes 811016 | tf_op jit(solution)/shard_map/ppermute | solution.py:421
  20.0 0.0 collective-permute-done.5.refs_4_
  20.0 0.0 collective-permute-start.6
  20.0 3.6 %collective-permute-done.2.refs_0_ = bf16[1040,128]{1,0:T(8,128)(2,1)S(1)} collective-permute-done((bf16[1040,128]{1,0:T(8,128)(2,1)S(1)}, bf16[1040,128]{1,0:T(8,128)(2,1)S(1)}, u32[]{:S(2)}, u32[]{:S(2)}) %collective-permute-start.2) | collective-permute-done | bytes 266272 | tf_op jit(solution)/shard_map/ppermute | solution.py:421
  23.6 2.1 %collective-permute-start.8 = (bf16[1040,128]{1,0:T(8,128)(2,1)S(1)}, bf16[1040,128]{1,0:T(8,128)(2,1)S(1)}, u32[]{:S(2)}, u32[]{:S(2)}) collective-permute-start(bf16[1040,128]{1,0:T(8,128)(2,1)S(1)} %collective-permute-done.2.refs_0_), channel_id=1, source_target_pairs={{0,4},{4,8},{8,12},{12,14},{14,10},{10,6},{6,2},{2,0},{1,5},{5,9},... | collective-permute-start | bytes 798728 | tf_op jit(solution)/shard_map/ppermute | solution.py:421
  25.7 0.0 collective-permute-done.7.refs_3_
  25.7 0.0 collective-permute-start.9
  25.7 1.4 %scores.4 = (f32[8,128]{1,0:T(8,128)S(1)}, f32[8,128]{1,0:T(8,128)S(1)}, f32[8,128]{1,0:T(8,128)S(1)}) custom-call(bf16[512,2048]{1,0:T(8,128)(2,1)S(1)} %fetch.1.decoder, f32[8,128]{1,0:T(8,128)S(1)} %get-tuple-element.29.own_facts, bf16[1040,128]{1,0:T(8,128)(2,1)S(1)} %get-tuple-element.30.refs_0_, bf16[1024,128]{1,0:T(8,128)(2,1)S(1)} %get-tuple-element.31.refs_1_, ...), custom_call_target="tpu_custom_call" | custom-call | tf_op jit(solution)/shard_map/scores/pallas_call | solution.py:278
  27.1 2.3 %collective-permute-done.4.onward = bf16[1056,128]{1,0:T(8,128)(2,1)S(1)} collective-permute-done((bf16[1056,128]{1,0:T(8,128)(2,1)S(1)}, bf16[1056,128]{1,0:T(8,128)(2,1)S(1)}, u32[]{:S(2)}, u32[]{:S(2)}) %collective-permute-start.4) | collective-permute-done | bytes 270368 | tf_op jit(solution)/shard_map/ppermute | solution.py:421
  29.3 2.0 %collective-permute-done.6.back = bf16[1056,128]{1,0:T(8,128)(2,1)S(1)} collective-permute-done((bf16[1056,128]{1,0:T(8,128)(2,1)S(1)}, bf16[1056,128]{1,0:T(8,128)(2,1)S(1)}, u32[]{:S(2)}, u32[]{:S(2)}) %collective-permute-start.6) | collective-permute-done | bytes 270368 | tf_op jit(solution)/shard_map/ppermute | solution.py:421
  31.4 0.1 stamp.1
  31.4 1.6 %collective-permute-start.11 = (bf16[1056,128]{1,0:T(8,128)(2,1)S(1)}, bf16[1056,128]{1,0:T(8,128)(2,1)S(1)}, u32[]{:S(2)}, u32[]{:S(2)}) collective-permute-start(bf16[1056,128]{1,0:T(8,128)(2,1)S(1)} %get-tuple-element.39.refs_1_), channel_id=1, source_target_pairs={{0,4},{4,8},{8,12},{12,14},{14,10},{10,6},{6,2},{2,0},{1,5},{5,9},... | collective-permute-start | bytes 811016 | tf_op jit(solution)/shard_map/ppermute | solution.py:421
  33.1 0.4 collective-permute-start.12
  33.5 0.8 %scores.5 = (f32[8,128]{1,0:T(8,128)S(1)}, f32[8,128]{1,0:T(8,128)S(1)}) custom-call(bf16[512,2048]{1,0:T(8,128)(2,1)S(1)} %fetch.1.decoder, f32[8,128]{1,0:T(8,128)S(1)} %get-tuple-element.29.own_facts, bf16[1040,128]{1,0:T(8,128)(2,1)S(1)} %collective-permute-done.2.refs_0_, bf16[1056,128]{1,0:T(8,128)(2,1)S(1)} %get-tuple-element.39.refs_1_, ...), custom_call_target="tpu_custom_call" | custom-call | tf_op jit(solution)/shard_map/scores/pallas_call | solution.py:278
  34.3 0.1 collective-permute-start.10
  34.4 1.3 %gradients.2.refs_4_ = f32[512,2048]{1,0:T(8,128)S(1)} custom-call(f32[8,128]{1,0:T(8,128)S(1)} %get-tuple-element.29.own_facts, bf16[1040,128]{1,0:T(8,128)(2,1)S(1)} %get-tuple-element.30.refs_0_, bf16[1024,128]{1,0:T(8,128)(2,1)S(1)} %get-tuple-element.31.refs_1_, bf16[1040,128]{1,0:T(8,128)(2,1)S(1)} %collective-permute-done.refs_2_, ...), custom_call_target="tpu_custom_call" | custom-call | tf_op jit(solution)/shard_map/gradients/pallas_call | solution.py:299
  35.7 0.9 %gradients.3.refs_6_ = f32[512,2048]{1,0:T(8,128)S(1)} custom-call(f32[8,128]{1,0:T(8,128)S(1)} %get-tuple-element.29.own_facts, bf16[1040,128]{1,0:T(8,128)(2,1)S(1)} %collective-permute-done.2.refs_0_, bf16[1056,128]{1,0:T(8,128)(2,1)S(1)} %get-tuple-element.39.refs_1_, ...), custom_call_target="tpu_custom_call", output_to_operand_aliasing={{}: (5, {})} | custom-call | tf_op jit(solution)/shard_map/gradients/pallas_call | solution.py:299
  36.6 0.0 collective-permute-done.10
  36.7 0.3 collective-permute-done.9.refs_3_
  37.0 0.0 collective-permute-done.8.refs_0_
  37.0 1.6 %collective-permute-start.13 = (bf16[1040,128]{1,0:T(8,128)(2,1)S(1)}, bf16[1040,128]{1,0:T(8,128)(2,1)S(1)}, u32[]{:S(2)}, u32[]{:S(2)}) collective-permute-start(bf16[1040,128]{1,0:T(8,128)(2,1)S(1)} %collective-permute-done.8.refs_0_), channel_id=1, source_target_pairs={{0,4},{4,8},{8,12},{12,14},{14,10},{10,6},{6,2},{2,0},{1,5},{5,9},... | collective-permute-start | bytes 798728 | tf_op jit(solution)/shard_map/ppermute | solution.py:421
  38.6 0.4 collective-permute-start.14
  39.0 1.4 %collective-permute-start.18 = (f32[32,128]{1,0:T(8,128)S(1)}, f32[32,128]{1,0:T(8,128)S(1)}, u32[]{:S(2)}, u32[]{:S(2)}) collective-permute-start(f32[32,128]{1,0:T(8,128)S(1)} %concatenate.3), channel_id=1, source_target_pairs={{0,6},{1,9},{4,2},{5,13},{8,0},{9,15},{12,4},{13,11},{14,8},{15,7}... | collective-permute-start | bytes 49160 | tf_op jit(solution)/shard_map/ppermute | solution.py:439
  40.4 0.0 collective-permute-done.11.refs_1_.onward
  40.4 1.0 %collective-permute-done.12.refs_2_.back = bf16[1056,128]{1,0:T(8,128)(2,1)S(1)} collective-permute-done((bf16[1056,128]{1,0:T(8,128)(2,1)S(1)}, bf16[1056,128]{1,0:T(8,128)(2,1)S(1)}, u32[]{:S(2)}, u32[]{:S(2)}) %collective-permute-start.12) | collective-permute-done | bytes 270368 | tf_op jit(solution)/shard_map/ppermute | solution.py:421
  41.4 0.8 %scores.6 = (f32[8,128]{1,0:T(8,128)S(1)}, f32[8,128]{1,0:T(8,128)S(1)}) custom-call(bf16[512,2048]{1,0:T(8,128)(2,1)S(1)} %fetch.1.decoder, f32[8,128]{1,0:T(8,128)S(1)} %get-tuple-element.29.own_facts, bf16[1040,128]{1,0:T(8,128)(2,1)S(1)} %collective-permute-done.8.refs_0_, bf16[1056,128]{1,0:T(8,128)(2,1)S(1)} %collective-permute-done.11.refs_1_.onward, ...), custom_call_target="tpu_custom_call" | custom-call | tf_op jit(solution)/shard_map/scores/pallas_call | solution.py:278
  42.2 3.6 %collective-permute-start.15 = (f32[8,128]{1,0:T(8,128)S(1)}, f32[8,128]{1,0:T(8,128)S(1)}, u32[]{:S(2)}, u32[]{:S(2)}) collective-permute-start(f32[8,128]{1,0:T(8,128)S(1)} %get-tuple-element.46), channel_id=1, source_target_pairs={{0,10},{4,6},{8,2},{12,0},{14,4},{10,8},{6,12},{2,14},{1,11},{5,7}... | collective-permute-start | bytes 12296 | tf_op jit(solution)/shard_map/ppermute | solution.py:421
  45.8 1.2 %collective-permute-start.16 = (f32[8,128]{1,0:T(8,128)S(1)}, f32[8,128]{1,0:T(8,128)S(1)}, u32[]{:S(2)}, u32[]{:S(2)}) collective-permute-start(f32[8,128]{1,0:T(8,128)S(1)} %get-tuple-element.47), channel_id=1, source_target_pairs={{0,12},{4,14},{8,10},{12,6},{14,2},{10,0},{6,4},{2,8},{1,13},{5,15... | collective-permute-start | bytes 12296 | tf_op jit(solution)/shard_map/ppermute | solution.py:421
  47.0 0.0 collective-permute-done.14.refs_5_.refs_1_
  47.0 0.0 collective-permute-done.13.refs_4_.refs_0_
  47.0 0.7 %scores.7 = f32[8,128]{1,0:T(8,128)S(1)} custom-call(bf16[512,2048]{1,0:T(8,128)(2,1)S(1)} %fetch.1.decoder, f32[8,128]{1,0:T(8,128)S(1)} %get-tuple-element.29.own_facts, bf16[1040,128]{1,0:T(8,128)(2,1)S(1)} %collective-permute-done.13.refs_4_.refs_0_, bf16[1024,128]{1,0:T(8,128)(2,1)S(1)} %collective-permute-done.14.refs_5_.refs_1_), custom_call_target="tpu_custom_call" | custom-call | tf_op jit(solution)/shard_map/scores/pallas_call | solution.py:278
  47.7 3.7 %collective-permute-start.17 = (f32[8,128]{1,0:T(8,128)S(1)}, f32[8,128]{1,0:T(8,128)S(1)}, u32[]{:S(2)}, u32[]{:S(2)}) collective-permute-start(f32[8,128]{1,0:T(8,128)S(1)} %scores.7), channel_id=1, source_target_pairs={{0,14},{4,10},{8,6},{12,2},{14,0},{10,4},{6,8},{2,12},{1,15},{5,11... | collective-permute-start | bytes 12296 | tf_op jit(solution)/shard_map/ppermute | solution.py:421
  51.5 0.0 collective-permute-done.15.ahead
  51.5 0.0 collective-permute-done.16.behind
  51.5 0.0 collective-permute-done.18
  51.5 2.3 %last_gradients.1 = bf16[512,2048]{1,0:T(8,128)(2,1)} custom-call(f32[8,128]{1,0:T(8,128)S(1)} %get-tuple-element.29.own_facts, bf16[1040,128]{1,0:T(8,128)(2,1)S(1)} %collective-permute-done.8.refs_0_, bf16[1056,128]{1,0:T(8,128)(2,1)S(1)} %collective-permute-done.11.refs_1_.onward, bf16[1056,128]{1,0:T(8,128)(2,1)S(1)} %collective-permute-done.12.refs_2_.back, ...), custom_call_target="tpu_custom_call" | custom-call | tf_op jit(solution)/shard_map/last_gradients/pallas_call | solution.py:329
  53.8 0.3 collective-permute-done.17.opposite
  54.1 0.1 collective-permute-start.19
  54.2 1.2 %collective-permute-done.19 = f32[32,128]{1,0:T(8,128)S(1)} collective-permute-done((f32[32,128]{1,0:T(8,128)S(1)}, f32[32,128]{1,0:T(8,128)S(1)}, u32[]{:S(2)}, u32[]{:S(2)}) %collective-permute-start.19) | collective-permute-done | bytes 16416 | tf_op jit(solution)/shard_map/ppermute | solution.py:432
  55.4 0.6 %add_bitcast_fusion = f32[128,32]{0,1:T(8,128)} fusion(f32[32,128]{1,0:T(8,128)S(1)} %unpack.1, f32[32,128]{1,0:T(8,128)S(1)} %collective-permute-done.19), kind=kLoop, calls=%fused_computation | loop fusion | flops 4096 | bytes 49152 | tf_op jit(solution)/shard_map/transpose | solution.py:474
  (4 shorter events, 0.0 us)
Async XLA Ops:
  1.8 12.3 %collective-permute-start = (bf16[1040,128]{1,0:T(8,128)(2,1)S(1)}, bf16[1040,128]{1,0:T(8,128)(2,1)S(1)}, u32[]{:S(2)}, u32[]{:S(2)}) collective-permute-start(bf16[1040,128]{1,0:T(8,128)(2,1)S(1)} %get-tuple-element.30.refs_0_), channel_id=1, source_target_pairs={{0,4},{4,8},{8,12},{12,14},{14,10},{10,6},{6,2},{2,0},{1,5},{5,9},... | collective-permute-start | bytes 798728 | tf_op jit(solution)/shard_map/ppermute | solution.py:421
  4.9 9.2 %collective-permute-start.1 = (bf16[1024,128]{1,0:T(8,128)(2,1)S(1)}, bf16[1024,128]{1,0:T(8,128)(2,1)S(1)}, u32[]{:S(2)}, u32[]{:S(2)}) collective-permute-start(bf16[1024,128]{1,0:T(8,128)(2,1)S(1)} %get-tuple-element.31.refs_1_), channel_id=1, source_target_pairs={{0,2},{4,0},{8,4},{12,8},{14,12},{10,14},{6,10},{2,6},{1,3},{5,1},... | collective-permute-start | bytes 786440 | tf_op jit(solution)/shard_map/ppermute | solution.py:421
  4.9 12.9 %collective-permute-start.3 = (bf16[1056,128]{1,0:T(8,128)(2,1)S(1)}, bf16[1056,128]{1,0:T(8,128)(2,1)S(1)}, u32[]{:S(2)}, u32[]{:S(2)}) collective-permute-start(bf16[1056,128]{1,0:T(8,128)(2,1)S(1)} %get-tuple-element.33), channel_id=1, source_target_pairs={{0,4},{4,8},{8,12},{12,14},{14,10},{10,6},{6,2},{2,0},{1,5},{5,9},... | collective-permute-start | bytes 811016 | tf_op jit(solution)/shard_map/ppermute | solution.py:421
  6.9 13.1 %collective-permute-start.5 = (bf16[1056,128]{1,0:T(8,128)(2,1)S(1)}, bf16[1056,128]{1,0:T(8,128)(2,1)S(1)}, u32[]{:S(2)}, u32[]{:S(2)}) collective-permute-start(bf16[1056,128]{1,0:T(8,128)(2,1)S(1)} %get-tuple-element.34), channel_id=1, source_target_pairs={{0,2},{4,0},{8,4},{12,8},{14,12},{10,14},{6,10},{2,6},{1,3},{5,1},... | collective-permute-start | bytes 811016 | tf_op jit(solution)/shard_map/ppermute | solution.py:421
  14.2 9.4 %collective-permute-start.2 = (bf16[1040,128]{1,0:T(8,128)(2,1)S(1)}, bf16[1040,128]{1,0:T(8,128)(2,1)S(1)}, u32[]{:S(2)}, u32[]{:S(2)}) collective-permute-start(bf16[1040,128]{1,0:T(8,128)(2,1)S(1)} %collective-permute-done.refs_2_), channel_id=1, source_target_pairs={{0,4},{4,8},{8,12},{12,14},{14,10},{10,6},{6,2},{2,0},{1,5},{5,9},... | collective-permute-start | bytes 798728 | tf_op jit(solution)/shard_map/ppermute | solution.py:421
  15.7 10.0 %collective-permute-start.7 = (bf16[1024,128]{1,0:T(8,128)(2,1)S(1)}, bf16[1024,128]{1,0:T(8,128)(2,1)S(1)}, u32[]{:S(2)}, u32[]{:S(2)}) collective-permute-start(bf16[1024,128]{1,0:T(8,128)(2,1)S(1)} %collective-permute-done.1.refs_5_), channel_id=1, source_target_pairs={{0,2},{4,0},{8,4},{12,8},{14,12},{10,14},{6,10},{2,6},{1,3},{5,1},... | collective-permute-start | bytes 786440 | tf_op jit(solution)/shard_map/ppermute | solution.py:421
  17.8 11.5 %collective-permute-start.4 = (bf16[1056,128]{1,0:T(8,128)(2,1)S(1)}, bf16[1056,128]{1,0:T(8,128)(2,1)S(1)}, u32[]{:S(2)}, u32[]{:S(2)}) collective-permute-start(bf16[1056,128]{1,0:T(8,128)(2,1)S(1)} %collective-permute-done.3.refs_3_), channel_id=1, source_target_pairs={{0,4},{4,8},{8,12},{12,14},{14,10},{10,6},{6,2},{2,0},{1,5},{5,9},... | collective-permute-start | bytes 811016 | tf_op jit(solution)/shard_map/ppermute | solution.py:421
  20.0 11.4 %collective-permute-start.6 = (bf16[1056,128]{1,0:T(8,128)(2,1)S(1)}, bf16[1056,128]{1,0:T(8,128)(2,1)S(1)}, u32[]{:S(2)}, u32[]{:S(2)}) collective-permute-start(bf16[1056,128]{1,0:T(8,128)(2,1)S(1)} %collective-permute-done.5.refs_4_), channel_id=1, source_target_pairs={{0,2},{4,0},{8,4},{12,8},{14,12},{10,14},{6,10},{2,6},{1,3},{5,1},... | collective-permute-start | bytes 811016 | tf_op jit(solution)/shard_map/ppermute | solution.py:421
  23.6 13.4 %collective-permute-start.8 = (bf16[1040,128]{1,0:T(8,128)(2,1)S(1)}, bf16[1040,128]{1,0:T(8,128)(2,1)S(1)}, u32[]{:S(2)}, u32[]{:S(2)}) collective-permute-start(bf16[1040,128]{1,0:T(8,128)(2,1)S(1)} %collective-permute-done.2.refs_0_), channel_id=1, source_target_pairs={{0,4},{4,8},{8,12},{12,14},{14,10},{10,6},{6,2},{2,0},{1,5},{5,9},... | collective-permute-start | bytes 798728 | tf_op jit(solution)/shard_map/ppermute | solution.py:421
  25.7 11.3 %collective-permute-start.9 = (bf16[1024,128]{1,0:T(8,128)(2,1)S(1)}, bf16[1024,128]{1,0:T(8,128)(2,1)S(1)}, u32[]{:S(2)}, u32[]{:S(2)}) collective-permute-start(bf16[1024,128]{1,0:T(8,128)(2,1)S(1)} %collective-permute-done.7.refs_3_), channel_id=1, source_target_pairs={{0,2},{4,0},{8,4},{12,8},{14,12},{10,14},{6,10},{2,6},{1,3},{5,1},... | collective-permute-start | bytes 786440 | tf_op jit(solution)/shard_map/ppermute | solution.py:421
  31.4 9.0 %collective-permute-start.11 = (bf16[1056,128]{1,0:T(8,128)(2,1)S(1)}, bf16[1056,128]{1,0:T(8,128)(2,1)S(1)}, u32[]{:S(2)}, u32[]{:S(2)}) collective-permute-start(bf16[1056,128]{1,0:T(8,128)(2,1)S(1)} %get-tuple-element.39.refs_1_), channel_id=1, source_target_pairs={{0,4},{4,8},{8,12},{12,14},{14,10},{10,6},{6,2},{2,0},{1,5},{5,9},... | collective-permute-start | bytes 811016 | tf_op jit(solution)/shard_map/ppermute | solution.py:421
  33.1 8.4 %collective-permute-start.12 = (bf16[1056,128]{1,0:T(8,128)(2,1)S(1)}, bf16[1056,128]{1,0:T(8,128)(2,1)S(1)}, u32[]{:S(2)}, u32[]{:S(2)}) collective-permute-start(bf16[1056,128]{1,0:T(8,128)(2,1)S(1)} %get-tuple-element.40.refs_2_), channel_id=1, source_target_pairs={{0,2},{4,0},{8,4},{12,8},{14,12},{10,14},{6,10},{2,6},{1,3},{5,1},... | collective-permute-start | bytes 811016 | tf_op jit(solution)/shard_map/ppermute | solution.py:421
  34.3 2.3 %collective-permute-start.10 = (f32[8,128]{1,0:T(8,128)S(1)}, f32[8,128]{1,0:T(8,128)S(1)}, u32[]{:S(2)}, u32[]{:S(2)}) collective-permute-start(f32[8,128]{1,0:T(8,128)S(1)} %get-tuple-element.42), channel_id=1, source_target_pairs={{0,1},{1,0},{2,3},{3,2},{4,5},{5,4},{6,7},{7,6},{8,9},{9,8},{10,11... | collective-permute-start | bytes 12296 | tf_op jit(solution)/shard_map/ppermute | solution.py:432
  37.0 10.0 %collective-permute-start.13 = (bf16[1040,128]{1,0:T(8,128)(2,1)S(1)}, bf16[1040,128]{1,0:T(8,128)(2,1)S(1)}, u32[]{:S(2)}, u32[]{:S(2)}) collective-permute-start(bf16[1040,128]{1,0:T(8,128)(2,1)S(1)} %collective-permute-done.8.refs_0_), channel_id=1, source_target_pairs={{0,4},{4,8},{8,12},{12,14},{14,10},{10,6},{6,2},{2,0},{1,5},{5,9},... | collective-permute-start | bytes 798728 | tf_op jit(solution)/shard_map/ppermute | solution.py:421
  38.6 8.5 %collective-permute-start.14 = (bf16[1024,128]{1,0:T(8,128)(2,1)S(1)}, bf16[1024,128]{1,0:T(8,128)(2,1)S(1)}, u32[]{:S(2)}, u32[]{:S(2)}) collective-permute-start(bf16[1024,128]{1,0:T(8,128)(2,1)S(1)} %collective-permute-done.9.refs_3_), channel_id=1, source_target_pairs={{0,2},{4,0},{8,4},{12,8},{14,12},{10,14},{6,10},{2,6},{1,3},{5,1},... | collective-permute-start | bytes 786440 | tf_op jit(solution)/shard_map/ppermute | solution.py:421
  39.0 12.5 %collective-permute-start.18 = (f32[32,128]{1,0:T(8,128)S(1)}, f32[32,128]{1,0:T(8,128)S(1)}, u32[]{:S(2)}, u32[]{:S(2)}) collective-permute-start(f32[32,128]{1,0:T(8,128)S(1)} %concatenate.3), channel_id=1, source_target_pairs={{0,6},{1,9},{4,2},{5,13},{8,0},{9,15},{12,4},{13,11},{14,8},{15,7}... | collective-permute-start | bytes 49160 | tf_op jit(solution)/shard_map/ppermute | solution.py:439
  42.2 9.2 %collective-permute-start.15 = (f32[8,128]{1,0:T(8,128)S(1)}, f32[8,128]{1,0:T(8,128)S(1)}, u32[]{:S(2)}, u32[]{:S(2)}) collective-permute-start(f32[8,128]{1,0:T(8,128)S(1)} %get-tuple-element.46), channel_id=1, source_target_pairs={{0,10},{4,6},{8,2},{12,0},{14,4},{10,8},{6,12},{2,14},{1,11},{5,7}... | collective-permute-start | bytes 12296 | tf_op jit(solution)/shard_map/ppermute | solution.py:421
  45.8 5.7 %collective-permute-start.16 = (f32[8,128]{1,0:T(8,128)S(1)}, f32[8,128]{1,0:T(8,128)S(1)}, u32[]{:S(2)}, u32[]{:S(2)}) collective-permute-start(f32[8,128]{1,0:T(8,128)S(1)} %get-tuple-element.47), channel_id=1, source_target_pairs={{0,12},{4,14},{8,10},{12,6},{14,2},{10,0},{6,4},{2,8},{1,13},{5,15... | collective-permute-start | bytes 12296 | tf_op jit(solution)/shard_map/ppermute | solution.py:421
  47.7 6.4 %collective-permute-start.17 = (f32[8,128]{1,0:T(8,128)S(1)}, f32[8,128]{1,0:T(8,128)S(1)}, u32[]{:S(2)}, u32[]{:S(2)}) collective-permute-start(f32[8,128]{1,0:T(8,128)S(1)} %scores.7), channel_id=1, source_target_pairs={{0,14},{4,10},{8,6},{12,2},{14,0},{10,4},{6,8},{2,12},{1,15},{5,11... | collective-permute-start | bytes 12296 | tf_op jit(solution)/shard_map/ppermute | solution.py:421
  54.1 1.2 %collective-permute-start.19 = (f32[32,128]{1,0:T(8,128)S(1)}, f32[32,128]{1,0:T(8,128)S(1)}, u32[]{:S(2)}, u32[]{:S(2)}) collective-permute-start(f32[32,128]{1,0:T(8,128)S(1)} %unpack.1), channel_id=1, source_target_pairs={{0,1},{1,0},{2,3},{3,2},{4,5},{5,4},{6,7},{7,6},{8,9},{9,8},{10,11... | collective-permute-start | bytes 49160 | tf_op jit(solution)/shard_map/ppermute | solution.py:432

commit v19 on v18

--- a/solution.py
+++ b/solution.py
@@ -459,11 +459,13 @@
     total = gradients_of((-2, 2), pairs, own_facts, decoder.shape, total)
     second = mine + other_core(others)
     total, first_3, second = lax.optimization_barrier((total, first_3, second))
-    second = return_by(2, jnp.concatenate([second, jnp.zeros((24, 128), jnp.float32)]))[:8]
+    second = return_by(2, jnp.concatenate([second, jnp.zeros((8, 128), jnp.float32)]))[:8]
     first_4 = hop(first_3)
     pairs = [(first_3[0], second_3[0]), (second_3[1], first_3[1])]
-    onward, back = scores_of((-3, 3), pairs, decoder, own_facts)
-    ahead, behind = shift(onward, -3), shift(back, 3)
+    (onward,) = scores_of((-3,), pairs[:1], decoder, own_facts)
+    ahead = shift(onward, -3)
+    (back,) = scores_of((3,), pairs[1:], decoder, own_facts)
+    behind = shift(back, 3)
     (opposite,) = scores_of((4,), [first_4], decoder, own_facts)
     opposite = shift(opposite, -owners // 2)
     total, ahead, behind = lax.optimization_barrier((total, ahead, behind))

time: 56.2 us -> 57.6 us (1.025)
  waiting for transfers between devices: 18 us -> 19.6 us
  starting transfers between devices: 25.5 us -> 24.7 us
  Pallas kernels: 11.1 us -> 11.7 us
    ppermute x17, waiting for transfers between devices: 16.8 us -> 18.5 us  [shift(): return lax.ppermute(x, 'dp', pairs)]
    ppermute x17, starting transfers between devices: 24 us -> 23.2 us  [shift(): return lax.ppermute(x, 'dp', pairs)]
    pallas_call x4 -> x5, Pallas kernels: 3.72 us -> 4.33 us  [scores_of(): pl.pallas_call(functools.partial(scores_kernel, distances, split), out_sh...]
where the time goes in v19:
time: 57.6 us; the launch traced here: 57.5 us
  starting transfers between devices  24.7 us (43%)
  waiting for transfers between devices  19.6 us (34%)
  Pallas kernels  11.7 us (20%)
  between operations  0.79 us (1%)
  other arithmetic  0.61 us (1%)
    ppermute x17, starting transfers between devices, shift(): return lax.ppermute(x, 'dp', pairs)  23.2 us
    ppermute x17, waiting for transfers between devices, shift(): return lax.ppermute(x, 'dp', pairs)  18.5 us
    pallas_call x5, Pallas kernels, scores_of(): pl.pallas_call(functools.partial(scores_kernel, distances, split), out_sh...  4.33 us
    pallas_call x1, Pallas kernels, last_gradients(): pl.pallas_call(functools.partial(last_gradients_kernel, distances), out_s...  2.3 us
    pallas_call x2, Pallas kernels, gradients_of(): pl.pallas_call(functools.partial(gradients_kernel, distances), out_shape=...  2.2 us
    pallas_call x1, Pallas kernels, fetch(): pl.pallas_call(fetch_kernel, out_shape=pltpu.VMEM(x.shape, x.dtype), in_s...  1.6 us
    ppermute x1, starting transfers between devices, return_by(): return lax.ppermute(x, ('dp', 'width'), pairs)  1.37 us
    pallas_call x1, Pallas kernels, prepare(): pl.pallas_call(functools.partial(prepare_kernel, owners), out_shape=(piec...  1.2 us
  transfers between devices with their start and end apart: 20, of which 9 were waited for; matrix products, arithmetic and copies ran while one was open for 0% of the time, Pallas kernels for 18%

profile of v19, /device:TPU:0, one launch (start us, length us, event | category | flops | bytes accessed | tf_op | source)
XLA Modules:
  0.0 57.5 jit_solution(8211716988794519803)
XLA Ops:
  0.6 1.2 %prepare.1 = (bf16[1040,128]{1,0:T(8,128)(2,1)S(1)}, bf16[1024,128]{1,0:T(8,128)(2,1)S(1)}, bf16[1056,128]{1,0:T(8,128)(2,1)S(1)}, bf16[1056,128]{1,0:T(8,128)(2...) custom-call(s32[32]{0:T(128)} %refs_0_.1, s32[8,128]{1,0:T(8,128)} %bitcast.7, s32[32,128]{1,0:T(8,128)} %bitcast.5, ...), custom_call_target="tpu_custom_call" | custom-call | tf_op jit(solution)/shard_map/prepare/pallas_call | solution.py:124
  1.8 3.1 %collective-permute-start = (bf16[1040,128]{1,0:T(8,128)(2,1)S(1)}, bf16[1040,128]{1,0:T(8,128)(2,1)S(1)}, u32[]{:S(2)}, u32[]{:S(2)}) collective-permute-start(bf16[1040,128]{1,0:T(8,128)(2,1)S(1)} %get-tuple-element.28.refs_0_), channel_id=1, source_target_pairs={{0,4},{4,8},{8,12},{12,14},{14,10},{10,6},{6,2},{2,0},{1,5},{5,9},... | collective-permute-start | bytes 798728 | tf_op jit(solution)/shard_map/ppermute | solution.py:421
  4.9 0.0 collective-permute-start.1
  4.9 2.0 %collective-permute-start.3 = (bf16[1056,128]{1,0:T(8,128)(2,1)S(1)}, bf16[1056,128]{1,0:T(8,128)(2,1)S(1)}, u32[]{:S(2)}, u32[]{:S(2)}) collective-permute-start(bf16[1056,128]{1,0:T(8,128)(2,1)S(1)} %get-tuple-element.31), channel_id=1, source_target_pairs={{0,4},{4,8},{8,12},{12,14},{14,10},{10,6},{6,2},{2,0},{1,5},{5,9},... | collective-permute-start | bytes 811016 | tf_op jit(solution)/shard_map/ppermute | solution.py:421
  6.9 0.0 collective-permute-start.5
  6.9 1.6 %fetch.1.decoder = bf16[512,2048]{1,0:T(8,128)(2,1)S(1)} custom-call(bf16[512,2048]{1,0:T(8,128)(2,1)} %source.1), custom_call_target="tpu_custom_call" | custom-call | tf_op jit(solution)/shard_map/fetch/pallas_call | solution.py:158
  8.6 5.6 %collective-permute-done.1.refs_5_ = bf16[1024,128]{1,0:T(8,128)(2,1)S(1)} collective-permute-done((bf16[1024,128]{1,0:T(8,128)(2,1)S(1)}, bf16[1024,128]{1,0:T(8,128)(2,1)S(1)}, u32[]{:S(2)}, u32[]{:S(2)}) %collective-permute-start.1) | collective-permute-done | bytes 262176 | tf_op jit(solution)/shard_map/ppermute | solution.py:421
  14.1 0.0 collective-permute-done.refs_2_
  14.2 1.6 %collective-permute-start.2 = (bf16[1040,128]{1,0:T(8,128)(2,1)S(1)}, bf16[1040,128]{1,0:T(8,128)(2,1)S(1)}, u32[]{:S(2)}, u32[]{:S(2)}) collective-permute-start(bf16[1040,128]{1,0:T(8,128)(2,1)S(1)} %collective-permute-done.refs_2_), channel_id=1, source_target_pairs={{0,4},{4,8},{8,12},{12,14},{14,10},{10,6},{6,2},{2,0},{1,5},{5,9},... | collective-permute-start | bytes 798728 | tf_op jit(solution)/shard_map/ppermute | solution.py:421
  15.7 0.4 collective-permute-start.7
  16.2 1.7 %collective-permute-done.3.refs_3_ = bf16[1056,128]{1,0:T(8,128)(2,1)S(1)} collective-permute-done((bf16[1056,128]{1,0:T(8,128)(2,1)S(1)}, bf16[1056,128]{1,0:T(8,128)(2,1)S(1)}, u32[]{:S(2)}, u32[]{:S(2)}) %collective-permute-start.3) | collective-permute-done | bytes 270368 | tf_op jit(solution)/shard_map/ppermute | solution.py:421
  17.8 2.1 %collective-permute-start.4 = (bf16[1056,128]{1,0:T(8,128)(2,1)S(1)}, bf16[1056,128]{1,0:T(8,128)(2,1)S(1)}, u32[]{:S(2)}, u32[]{:S(2)}) collective-permute-start(bf16[1056,128]{1,0:T(8,128)(2,1)S(1)} %collective-permute-done.3.refs_3_), channel_id=1, source_target_pairs={{0,4},{4,8},{8,12},{12,14},{14,10},{10,6},{6,2},{2,0},{1,5},{5,9},... | collective-permute-start | bytes 811016 | tf_op jit(solution)/shard_map/ppermute | solution.py:421
  20.0 0.0 collective-permute-done.5.refs_4_
  20.0 0.0 collective-permute-start.6
  20.0 3.6 %collective-permute-done.2.refs_0_ = bf16[1040,128]{1,0:T(8,128)(2,1)S(1)} collective-permute-done((bf16[1040,128]{1,0:T(8,128)(2,1)S(1)}, bf16[1040,128]{1,0:T(8,128)(2,1)S(1)}, u32[]{:S(2)}, u32[]{:S(2)}) %collective-permute-start.2) | collective-permute-done | bytes 266272 | tf_op jit(solution)/shard_map/ppermute | solution.py:421
  23.6 2.1 %collective-permute-start.8 = (bf16[1040,128]{1,0:T(8,128)(2,1)S(1)}, bf16[1040,128]{1,0:T(8,128)(2,1)S(1)}, u32[]{:S(2)}, u32[]{:S(2)}) collective-permute-start(bf16[1040,128]{1,0:T(8,128)(2,1)S(1)} %collective-permute-done.2.refs_0_), channel_id=1, source_target_pairs={{0,4},{4,8},{8,12},{12,14},{14,10},{10,6},{6,2},{2,0},{1,5},{5,9},... | collective-permute-start | bytes 798728 | tf_op jit(solution)/shard_map/ppermute | solution.py:421
  25.7 0.0 collective-permute-done.7.refs_3_
  25.7 0.0 collective-permute-start.9
  25.7 1.4 %scores.5 = (f32[8,128]{1,0:T(8,128)S(1)}, f32[8,128]{1,0:T(8,128)S(1)}, f32[8,128]{1,0:T(8,128)S(1)}) custom-call(bf16[512,2048]{1,0:T(8,128)(2,1)S(1)} %fetch.1.decoder, f32[8,128]{1,0:T(8,128)S(1)} %get-tuple-element.27.own_facts, bf16[1040,128]{1,0:T(8,128)(2,1)S(1)} %get-tuple-element.28.refs_0_, bf16[1024,128]{1,0:T(8,128)(2,1)S(1)} %get-tuple-element.29.refs_1_, ...), custom_call_target="tpu_custom_call" | custom-call | tf_op jit(solution)/shard_map/scores/pallas_call | solution.py:278
  27.1 2.3 %collective-permute-done.4.onward = bf16[1056,128]{1,0:T(8,128)(2,1)S(1)} collective-permute-done((bf16[1056,128]{1,0:T(8,128)(2,1)S(1)}, bf16[1056,128]{1,0:T(8,128)(2,1)S(1)}, u32[]{:S(2)}, u32[]{:S(2)}) %collective-permute-start.4) | collective-permute-done | bytes 270368 | tf_op jit(solution)/shard_map/ppermute | solution.py:421
  29.3 2.0 %collective-permute-done.6.back = bf16[1056,128]{1,0:T(8,128)(2,1)S(1)} collective-permute-done((bf16[1056,128]{1,0:T(8,128)(2,1)S(1)}, bf16[1056,128]{1,0:T(8,128)(2,1)S(1)}, u32[]{:S(2)}, u32[]{:S(2)}) %collective-permute-start.6) | collective-permute-done | bytes 270368 | tf_op jit(solution)/shard_map/ppermute | solution.py:421
  31.4 0.1 stamp.1
  31.4 1.6 %collective-permute-start.11 = (bf16[1056,128]{1,0:T(8,128)(2,1)S(1)}, bf16[1056,128]{1,0:T(8,128)(2,1)S(1)}, u32[]{:S(2)}, u32[]{:S(2)}) collective-permute-start(bf16[1056,128]{1,0:T(8,128)(2,1)S(1)} %get-tuple-element.37.refs_1_), channel_id=1, source_target_pairs={{0,4},{4,8},{8,12},{12,14},{14,10},{10,6},{6,2},{2,0},{1,5},{5,9},... | collective-permute-start | bytes 811016 | tf_op jit(solution)/shard_map/ppermute | solution.py:421
  33.1 0.8 %scores.6 = (f32[8,128]{1,0:T(8,128)S(1)}, f32[8,128]{1,0:T(8,128)S(1)}) custom-call(bf16[512,2048]{1,0:T(8,128)(2,1)S(1)} %fetch.1.decoder, f32[8,128]{1,0:T(8,128)S(1)} %get-tuple-element.27.own_facts, bf16[1040,128]{1,0:T(8,128)(2,1)S(1)} %collective-permute-done.2.refs_0_, bf16[1056,128]{1,0:T(8,128)(2,1)S(1)} %get-tuple-element.37.refs_1_, ...), custom_call_target="tpu_custom_call" | custom-call | tf_op jit(solution)/shard_map/scores/pallas_call | solution.py:278
  33.9 0.1 collective-permute-start.10
  34.0 0.5 collective-permute-start.12
  34.5 1.3 %gradients.2.refs_4_ = f32[512,2048]{1,0:T(8,128)S(1)} custom-call(f32[8,128]{1,0:T(8,128)S(1)} %get-tuple-element.27.own_facts, bf16[1040,128]{1,0:T(8,128)(2,1)S(1)} %get-tuple-element.28.refs_0_, bf16[1024,128]{1,0:T(8,128)(2,1)S(1)} %get-tuple-element.29.refs_1_, bf16[1040,128]{1,0:T(8,128)(2,1)S(1)} %collective-permute-done.refs_2_, ...), custom_call_target="tpu_custom_call" | custom-call | tf_op jit(solution)/shard_map/gradients/pallas_call | solution.py:299
  35.7 0.9 %gradients.3.refs_6_ = f32[512,2048]{1,0:T(8,128)S(1)} custom-call(f32[8,128]{1,0:T(8,128)S(1)} %get-tuple-element.27.own_facts, bf16[1040,128]{1,0:T(8,128)(2,1)S(1)} %collective-permute-done.2.refs_0_, bf16[1056,128]{1,0:T(8,128)(2,1)S(1)} %get-tuple-element.37.refs_1_, ...), custom_call_target="tpu_custom_call", output_to_operand_aliasing={{}: (5, {})} | custom-call | tf_op jit(solution)/shard_map/gradients/pallas_call | solution.py:299
  36.7 0.0 collective-permute-done.10
  36.7 0.0 collective-permute-done.9.refs_1_.refs_3_
  36.7 0.0 collective-permute-done.8.refs_0_
  36.7 1.6 %collective-permute-start.13 = (bf16[1040,128]{1,0:T(8,128)(2,1)S(1)}, bf16[1040,128]{1,0:T(8,128)(2,1)S(1)}, u32[]{:S(2)}, u32[]{:S(2)}) collective-permute-start(bf16[1040,128]{1,0:T(8,128)(2,1)S(1)} %collective-permute-done.8.refs_0_), channel_id=1, source_target_pairs={{0,4},{4,8},{8,12},{12,14},{14,10},{10,6},{6,2},{2,0},{1,5},{5,9},... | collective-permute-start | bytes 798728 | tf_op jit(solution)/shard_map/ppermute | solution.py:421
  38.4 0.5 collective-permute-start.14
  38.8 1.4 %collective-permute-start.18 = (f32[16,128]{1,0:T(8,128)S(1)}, f32[16,128]{1,0:T(8,128)S(1)}, u32[]{:S(2)}, u32[]{:S(2)}) collective-permute-start(f32[16,128]{1,0:T(8,128)S(1)} %concatenate.3), channel_id=1, source_target_pairs={{0,6},{1,9},{4,2},{5,13},{8,0},{9,15},{12,4},{13,11},{14,8},{15,7}... | collective-permute-start | bytes 24584 | tf_op jit(solution)/shard_map/ppermute | solution.py:439
  40.2 0.2 collective-permute-done.11.refs_1_.onward
  40.4 0.7 %scores.7 = f32[8,128]{1,0:T(8,128)S(1)} custom-call(bf16[512,2048]{1,0:T(8,128)(2,1)S(1)} %fetch.1.decoder, f32[8,128]{1,0:T(8,128)S(1)} %get-tuple-element.27.own_facts, bf16[1040,128]{1,0:T(8,128)(2,1)S(1)} %collective-permute-done.8.refs_0_, bf16[1056,128]{1,0:T(8,128)(2,1)S(1)} %collective-permute-done.11.refs_1_.onward), custom_call_target="tpu_custom_call" | custom-call | tf_op jit(solution)/shard_map/scores/pallas_call | solution.py:278
  41.2 4.6 %collective-permute-start.15 = (f32[8,128]{1,0:T(8,128)S(1)}, f32[8,128]{1,0:T(8,128)S(1)}, u32[]{:S(2)}, u32[]{:S(2)}) collective-permute-start(f32[8,128]{1,0:T(8,128)S(1)} %scores.7), channel_id=1, source_target_pairs={{0,10},{4,6},{8,2},{12,0},{14,4},{10,8},{6,12},{2,14},{1,11},{5,7}... | collective-permute-start | bytes 12296 | tf_op jit(solution)/shard_map/ppermute | solution.py:421
  45.7 0.0 collective-permute-done.12.refs_0_.refs_2_.back
  45.7 0.7 %scores.8 = f32[8,128]{1,0:T(8,128)S(1)} custom-call(bf16[512,2048]{1,0:T(8,128)(2,1)S(1)} %fetch.1.decoder, f32[8,128]{1,0:T(8,128)S(1)} %get-tuple-element.27.own_facts, bf16[1056,128]{1,0:T(8,128)(2,1)S(1)} %collective-permute-done.12.refs_0_.refs_2_.back, bf16[1024,128]{1,0:T(8,128)(2,1)S(1)} %collective-permute-done.9.refs_1_.refs_3_), custom_call_target="tpu_custom_call" | custom-call | tf_op jit(solution)/shard_map/scores/pallas_call | solution.py:278
  46.4 0.1 collective-permute-start.16
  46.5 2.0 %collective-permute-done.14.refs_5_.refs_1_ = bf16[1024,128]{1,0:T(8,128)(2,1)S(1)} collective-permute-done((bf16[1024,128]{1,0:T(8,128)(2,1)S(1)}, bf16[1024,128]{1,0:T(8,128)(2,1)S(1)}, u32[]{:S(2)}, u32[]{:S(2)}) %collective-permute-start.14) | collective-permute-done | bytes 262176 | tf_op jit(solution)/shard_map/ppermute | solution.py:421
  48.5 0.0 collective-permute-done.13.refs_4_.refs_0_
  48.5 0.7 %scores.9 = f32[8,128]{1,0:T(8,128)S(1)} custom-call(bf16[512,2048]{1,0:T(8,128)(2,1)S(1)} %fetch.1.decoder, f32[8,128]{1,0:T(8,128)S(1)} %get-tuple-element.27.own_facts, bf16[1040,128]{1,0:T(8,128)(2,1)S(1)} %collective-permute-done.13.refs_4_.refs_0_, bf16[1024,128]{1,0:T(8,128)(2,1)S(1)} %collective-permute-done.14.refs_5_.refs_1_), custom_call_target="tpu_custom_call" | custom-call | tf_op jit(solution)/shard_map/scores/pallas_call | solution.py:278
  49.2 2.9 %collective-permute-start.17 = (f32[8,128]{1,0:T(8,128)S(1)}, f32[8,128]{1,0:T(8,128)S(1)}, u32[]{:S(2)}, u32[]{:S(2)}) collective-permute-start(f32[8,128]{1,0:T(8,128)S(1)} %scores.9), channel_id=1, source_target_pairs={{0,14},{4,10},{8,6},{12,2},{14,0},{10,4},{6,8},{2,12},{1,15},{5,11... | collective-permute-start | bytes 12296 | tf_op jit(solution)/shard_map/ppermute | solution.py:421
  52.1 0.0 collective-permute-done.18
  52.1 0.0 collective-permute-done.15.ahead
  52.1 0.0 collective-permute-done.16.behind
  52.1 2.3 %last_gradients.1 = bf16[512,2048]{1,0:T(8,128)(2,1)} custom-call(f32[8,128]{1,0:T(8,128)S(1)} %get-tuple-element.27.own_facts, bf16[1040,128]{1,0:T(8,128)(2,1)S(1)} %collective-permute-done.8.refs_0_, bf16[1056,128]{1,0:T(8,128)(2,1)S(1)} %collective-permute-done.11.refs_1_.onward, bf16[1056,128]{1,0:T(8,128)(2,1)S(1)} %collective-permute-done.12.refs_0_.refs_2_.back, ...), custom_call_target="tpu_custom_call" | custom-call | tf_op jit(solution)/shard_map/last_gradients/pallas_call | solution.py:329
  54.4 1.1 %collective-permute-done.17.opposite = f32[8,128]{1,0:T(8,128)S(1)} collective-permute-done((f32[8,128]{1,0:T(8,128)S(1)}, f32[8,128]{1,0:T(8,128)S(1)}, u32[]{:S(2)}, u32[]{:S(2)}) %collective-permute-start.17) | collective-permute-done | bytes 4128 | tf_op jit(solution)/shard_map/ppermute | solution.py:421
  55.6 0.1 collective-permute-start.19
  55.7 1.2 %collective-permute-done.19 = f32[32,128]{1,0:T(8,128)S(1)} collective-permute-done((f32[32,128]{1,0:T(8,128)S(1)}, f32[32,128]{1,0:T(8,128)S(1)}, u32[]{:S(2)}, u32[]{:S(2)}) %collective-permute-start.19) | collective-permute-done | bytes 16416 | tf_op jit(solution)/shard_map/ppermute | solution.py:432
  56.9 0.6 %add_bitcast_fusion = f32[128,32]{0,1:T(8,128)} fusion(f32[32,128]{1,0:T(8,128)S(1)} %unpack.1, f32[32,128]{1,0:T(8,128)S(1)} %collective-permute-done.19), kind=kLoop, calls=%fused_computation | loop fusion | flops 4096 | bytes 49152 | tf_op jit(solution)/shard_map/transpose | solution.py:476
  (4 shorter events, 0.0 us)
Async XLA Ops:
  1.8 12.3 %collective-permute-start = (bf16[1040,128]{1,0:T(8,128)(2,1)S(1)}, bf16[1040,128]{1,0:T(8,128)(2,1)S(1)}, u32[]{:S(2)}, u32[]{:S(2)}) collective-permute-start(bf16[1040,128]{1,0:T(8,128)(2,1)S(1)} %get-tuple-element.28.refs_0_), channel_id=1, source_target_pairs={{0,4},{4,8},{8,12},{12,14},{14,10},{10,6},{6,2},{2,0},{1,5},{5,9},... | collective-permute-start | bytes 798728 | tf_op jit(solution)/shard_map/ppermute | solution.py:421
  4.9 9.2 %collective-permute-start.1 = (bf16[1024,128]{1,0:T(8,128)(2,1)S(1)}, bf16[1024,128]{1,0:T(8,128)(2,1)S(1)}, u32[]{:S(2)}, u32[]{:S(2)}) collective-permute-start(bf16[1024,128]{1,0:T(8,128)(2,1)S(1)} %get-tuple-element.29.refs_1_), channel_id=1, source_target_pairs={{0,2},{4,0},{8,4},{12,8},{14,12},{10,14},{6,10},{2,6},{1,3},{5,1},... | collective-permute-start | bytes 786440 | tf_op jit(solution)/shard_map/ppermute | solution.py:421
  4.9 12.9 %collective-permute-start.3 = (bf16[1056,128]{1,0:T(8,128)(2,1)S(1)}, bf16[1056,128]{1,0:T(8,128)(2,1)S(1)}, u32[]{:S(2)}, u32[]{:S(2)}) collective-permute-start(bf16[1056,128]{1,0:T(8,128)(2,1)S(1)} %get-tuple-element.31), channel_id=1, source_target_pairs={{0,4},{4,8},{8,12},{12,14},{14,10},{10,6},{6,2},{2,0},{1,5},{5,9},... | collective-permute-start | bytes 811016 | tf_op jit(solution)/shard_map/ppermute | solution.py:421
  6.9 13.1 %collective-permute-start.5 = (bf16[1056,128]{1,0:T(8,128)(2,1)S(1)}, bf16[1056,128]{1,0:T(8,128)(2,1)S(1)}, u32[]{:S(2)}, u32[]{:S(2)}) collective-permute-start(bf16[1056,128]{1,0:T(8,128)(2,1)S(1)} %get-tuple-element.32), channel_id=1, source_target_pairs={{0,2},{4,0},{8,4},{12,8},{14,12},{10,14},{6,10},{2,6},{1,3},{5,1},... | collective-permute-start | bytes 811016 | tf_op jit(solution)/shard_map/ppermute | solution.py:421
  14.2 9.4 %collective-permute-start.2 = (bf16[1040,128]{1,0:T(8,128)(2,1)S(1)}, bf16[1040,128]{1,0:T(8,128)(2,1)S(1)}, u32[]{:S(2)}, u32[]{:S(2)}) collective-permute-start(bf16[1040,128]{1,0:T(8,128)(2,1)S(1)} %collective-permute-done.refs_2_), channel_id=1, source_target_pairs={{0,4},{4,8},{8,12},{12,14},{14,10},{10,6},{6,2},{2,0},{1,5},{5,9},... | collective-permute-start | bytes 798728 | tf_op jit(solution)/shard_map/ppermute | solution.py:421
  15.7 10.0 %collective-permute-start.7 = (bf16[1024,128]{1,0:T(8,128)(2,1)S(1)}, bf16[1024,128]{1,0:T(8,128)(2,1)S(1)}, u32[]{:S(2)}, u32[]{:S(2)}) collective-permute-start(bf16[1024,128]{1,0:T(8,128)(2,1)S(1)} %collective-permute-done.1.refs_5_), channel_id=1, source_target_pairs={{0,2},{4,0},{8,4},{12,8},{14,12},{10,14},{6,10},{2,6},{1,3},{5,1},... | collective-permute-start | bytes 786440 | tf_op jit(solution)/shard_map/ppermute | solution.py:421
  17.8 11.5 %collective-permute-start.4 = (bf16[1056,128]{1,0:T(8,128)(2,1)S(1)}, bf16[1056,128]{1,0:T(8,128)(2,1)S(1)}, u32[]{:S(2)}, u32[]{:S(2)}) collective-permute-start(bf16[1056,128]{1,0:T(8,128)(2,1)S(1)} %collective-permute-done.3.refs_3_), channel_id=1, source_target_pairs={{0,4},{4,8},{8,12},{12,14},{14,10},{10,6},{6,2},{2,0},{1,5},{5,9},... | collective-permute-start | bytes 811016 | tf_op jit(solution)/shard_map/ppermute | solution.py:421
  20.0 11.4 %collective-permute-start.6 = (bf16[1056,128]{1,0:T(8,128)(2,1)S(1)}, bf16[1056,128]{1,0:T(8,128)(2,1)S(1)}, u32[]{:S(2)}, u32[]{:S(2)}) collective-permute-start(bf16[1056,128]{1,0:T(8,128)(2,1)S(1)} %collective-permute-done.5.refs_4_), channel_id=1, source_target_pairs={{0,2},{4,0},{8,4},{12,8},{14,12},{10,14},{6,10},{2,6},{1,3},{5,1},... | collective-permute-start | bytes 811016 | tf_op jit(solution)/shard_map/ppermute | solution.py:421
  23.6 13.2 %collective-permute-start.8 = (bf16[1040,128]{1,0:T(8,128)(2,1)S(1)}, bf16[1040,128]{1,0:T(8,128)(2,1)S(1)}, u32[]{:S(2)}, u32[]{:S(2)}) collective-permute-start(bf16[1040,128]{1,0:T(8,128)(2,1)S(1)} %collective-permute-done.2.refs_0_), channel_id=1, source_target_pairs={{0,4},{4,8},{8,12},{12,14},{14,10},{10,6},{6,2},{2,0},{1,5},{5,9},... | collective-permute-start | bytes 798728 | tf_op jit(solution)/shard_map/ppermute | solution.py:421
  25.7 11.0 %collective-permute-start.9 = (bf16[1024,128]{1,0:T(8,128)(2,1)S(1)}, bf16[1024,128]{1,0:T(8,128)(2,1)S(1)}, u32[]{:S(2)}, u32[]{:S(2)}) collective-permute-start(bf16[1024,128]{1,0:T(8,128)(2,1)S(1)} %collective-permute-done.7.refs_3_), channel_id=1, source_target_pairs={{0,2},{4,0},{8,4},{12,8},{14,12},{10,14},{6,10},{2,6},{1,3},{5,1},... | collective-permute-start | bytes 786440 | tf_op jit(solution)/shard_map/ppermute | solution.py:421
  31.4 9.0 %collective-permute-start.11 = (bf16[1056,128]{1,0:T(8,128)(2,1)S(1)}, bf16[1056,128]{1,0:T(8,128)(2,1)S(1)}, u32[]{:S(2)}, u32[]{:S(2)}) collective-permute-start(bf16[1056,128]{1,0:T(8,128)(2,1)S(1)} %get-tuple-element.37.refs_1_), channel_id=1, source_target_pairs={{0,4},{4,8},{8,12},{12,14},{14,10},{10,6},{6,2},{2,0},{1,5},{5,9},... | collective-permute-start | bytes 811016 | tf_op jit(solution)/shard_map/ppermute | solution.py:421
  33.9 2.8 %collective-permute-start.10 = (f32[8,128]{1,0:T(8,128)S(1)}, f32[8,128]{1,0:T(8,128)S(1)}, u32[]{:S(2)}, u32[]{:S(2)}) collective-permute-start(f32[8,128]{1,0:T(8,128)S(1)} %get-tuple-element.40), channel_id=1, source_target_pairs={{0,1},{1,0},{2,3},{3,2},{4,5},{5,4},{6,7},{7,6},{8,9},{9,8},{10,11... | collective-permute-start | bytes 12296 | tf_op jit(solution)/shard_map/ppermute | solution.py:432
  34.0 11.7 %collective-permute-start.12 = (bf16[1056,128]{1,0:T(8,128)(2,1)S(1)}, bf16[1056,128]{1,0:T(8,128)(2,1)S(1)}, u32[]{:S(2)}, u32[]{:S(2)}) collective-permute-start(bf16[1056,128]{1,0:T(8,128)(2,1)S(1)} %get-tuple-element.38.refs_2_), channel_id=1, source_target_pairs={{0,2},{4,0},{8,4},{12,8},{14,12},{10,14},{6,10},{2,6},{1,3},{5,1},... | collective-permute-start | bytes 811016 | tf_op jit(solution)/shard_map/ppermute | solution.py:421
  36.7 11.7 %collective-permute-start.13 = (bf16[1040,128]{1,0:T(8,128)(2,1)S(1)}, bf16[1040,128]{1,0:T(8,128)(2,1)S(1)}, u32[]{:S(2)}, u32[]{:S(2)}) collective-permute-start(bf16[1040,128]{1,0:T(8,128)(2,1)S(1)} %collective-permute-done.8.refs_0_), channel_id=1, source_target_pairs={{0,4},{4,8},{8,12},{12,14},{14,10},{10,6},{6,2},{2,0},{1,5},{5,9},... | collective-permute-start | bytes 798728 | tf_op jit(solution)/shard_map/ppermute | solution.py:421
  38.4 10.1 %collective-permute-start.14 = (bf16[1024,128]{1,0:T(8,128)(2,1)S(1)}, bf16[1024,128]{1,0:T(8,128)(2,1)S(1)}, u32[]{:S(2)}, u32[]{:S(2)}) collective-permute-start(bf16[1024,128]{1,0:T(8,128)(2,1)S(1)} %collective-permute-done.9.refs_1_.refs_3_), channel_id=1, source_target_pairs={{0,2},{4,0},{8,4},{12,8},{14,12},{10,14},{6,10},{2,6},{1,3},{5,1},... | collective-permute-start | bytes 786440 | tf_op jit(solution)/shard_map/ppermute | solution.py:421
  38.8 13.3 %collective-permute-start.18 = (f32[16,128]{1,0:T(8,128)S(1)}, f32[16,128]{1,0:T(8,128)S(1)}, u32[]{:S(2)}, u32[]{:S(2)}) collective-permute-start(f32[16,128]{1,0:T(8,128)S(1)} %concatenate.3), channel_id=1, source_target_pairs={{0,6},{1,9},{4,2},{5,13},{8,0},{9,15},{12,4},{13,11},{14,8},{15,7}... | collective-permute-start | bytes 24584 | tf_op jit(solution)/shard_map/ppermute | solution.py:439
  41.2 11.0 %collective-permute-start.15 = (f32[8,128]{1,0:T(8,128)S(1)}, f32[8,128]{1,0:T(8,128)S(1)}, u32[]{:S(2)}, u32[]{:S(2)}) collective-permute-start(f32[8,128]{1,0:T(8,128)S(1)} %scores.7), channel_id=1, source_target_pairs={{0,10},{4,6},{8,2},{12,0},{14,4},{10,8},{6,12},{2,14},{1,11},{5,7}... | collective-permute-start | bytes 12296 | tf_op jit(solution)/shard_map/ppermute | solution.py:421
  46.4 5.7 %collective-permute-start.16 = (f32[8,128]{1,0:T(8,128)S(1)}, f32[8,128]{1,0:T(8,128)S(1)}, u32[]{:S(2)}, u32[]{:S(2)}) collective-permute-start(f32[8,128]{1,0:T(8,128)S(1)} %scores.8), channel_id=1, source_target_pairs={{0,12},{4,14},{8,10},{12,6},{14,2},{10,0},{6,4},{2,8},{1,13},{5,15... | collective-permute-start | bytes 12296 | tf_op jit(solution)/shard_map/ppermute | solution.py:421
  49.2 6.4 %collective-permute-start.17 = (f32[8,128]{1,0:T(8,128)S(1)}, f32[8,128]{1,0:T(8,128)S(1)}, u32[]{:S(2)}, u32[]{:S(2)}) collective-permute-start(f32[8,128]{1,0:T(8,128)S(1)} %scores.9), channel_id=1, source_target_pairs={{0,14},{4,10},{8,6},{12,2},{14,0},{10,4},{6,8},{2,12},{1,15},{5,11... | collective-permute-start | bytes 12296 | tf_op jit(solution)/shard_map/ppermute | solution.py:421
  55.6 1.2 %collective-permute-start.19 = (f32[32,128]{1,0:T(8,128)S(1)}, f32[32,128]{1,0:T(8,128)S(1)}, u32[]{:S(2)}, u32[]{:S(2)}) collective-permute-start(f32[32,128]{1,0:T(8,128)S(1)} %unpack.1), channel_id=1, source_target_pairs={{0,1},{1,0},{2,3},{3,2},{4,5},{5,4},{6,7},{7,6},{8,9},{9,8},{10,11... | collective-permute-start | bytes 49160 | tf_op jit(solution)/shard_map/ppermute | solution.py:432

commit v20 on v18

--- a/solution.py
+++ b/solution.py
@@ -340,45 +340,34 @@
     )(*operands)
 
 
-def stamp_kernel(onward, back, for_onward, for_back, onward_out, back_out, rows, sems):
-    start = onward.shape[0] - FACTS
-    targets = (onward_out, back_out)
-    for i, piece in enumerate((onward, back)):
-        pltpu.make_async_copy(
-            piece.at[start : start + 16, :], rows.at[i], sems.at[i]
-        ).start()
-    for i, values in enumerate((for_onward, for_back)):
-        pltpu.make_async_copy(
-            onward.at[start : start + 16, :], rows.at[i], sems.at[i]
-        ).wait()
-        value = values[:KPB]
-        high = value.astype(jnp.bfloat16).astype(jnp.float32)
-        low = value - high
-        facts = rows[i].astype(jnp.float32)[2 * KPB :]
-        rows[i] = jnp.concatenate([high, low, facts], axis=0).astype(jnp.bfloat16)
-        pltpu.make_async_copy(
-            rows.at[i], targets[i].at[start : start + 16, :], sems.at[2 + i]
-        ).start()
-    for i in range(2):
-        pltpu.make_async_copy(
-            rows.at[i], targets[i].at[start : start + 16, :], sems.at[2 + i]
-        ).wait()
-
-
-def stamp(pieces, values):
+def stamp_kernel(piece, values, out, rows, sems):
+    place = pl.ds(piece.shape[0] - FACTS, 16)
+    load = pltpu.make_async_copy(piece.at[place, :], rows, sems.at[0])
+    load.start()
+    load.wait()
+    value = values[:KPB]
+    high = value.astype(jnp.bfloat16).astype(jnp.float32)
+    facts = rows[...].astype(jnp.float32)[2 * KPB :]
+    rows[...] = jnp.concatenate([high, value - high, facts], axis=0).astype(jnp.bfloat16)
+    store = pltpu.make_async_copy(rows, out.at[place, :], sems.at[1])
+    store.start()
+    store.wait()
+
+
+def stamp(piece, values):
     return pl.pallas_call(
         stamp_kernel,
-        out_shape=tuple(pltpu.VMEM(piece.shape, piece.dtype) for piece in pieces),
-        in_specs=[ANY, ANY, VMEM, VMEM],
-        out_specs=(ANY, ANY),
+        out_shape=pltpu.VMEM(piece.shape, piece.dtype),
+        in_specs=[ANY, VMEM],
+        out_specs=ANY,
         scratch_shapes=[
-            pltpu.VMEM((2, 16, 128), jnp.bfloat16),
-            pltpu.SemaphoreType.DMA((4,)),
+            pltpu.VMEM((16, 128), jnp.bfloat16),
+            pltpu.SemaphoreType.DMA((2,)),
         ],
-        input_output_aliases={0: 0, 1: 1},
+        input_output_aliases={0: 0},
         compiler_params=limit(4),
         name="stamp",
-    )(*[kept(piece) for piece in pieces], *[kept(value) for value in values])
+    )(kept(piece), kept(values))
 
 
 def unpack_kernel(owners, slots, own, onward, back, second, ahead, behind, opposite, out):
@@ -452,7 +441,9 @@
     own, onward, back = scores_of(distances, pairs, decoder, own_facts)
     total = gradients_of(distances, pairs, own_facts, decoder.shape)
     first_3 = hop(first_2)
-    second_2 = stamp(second_2, (back, onward))
+    right_2, left_2 = second_2
+    total, right_2 = lax.optimization_barrier((total, right_2))
+    second_2 = stamp(right_2, back), stamp(left_2, onward)
     second_3 = crossed(second_2)
     pairs = [(first_2[0], second_2[0]), (second_2[1], first_2[1])]
     mine, others = scores_of((-2, 2), pairs, decoder, own_facts, True)

time: 56.2 us -> 56.6 us (level)
  waiting for transfers between devices: 18 us -> 19.4 us
  starting transfers between devices: 25.5 us -> 24.6 us
    ppermute x17, waiting for transfers between devices: 16.8 us -> 18 us  [shift(): return lax.ppermute(x, 'dp', pairs)]
    ppermute x17, starting transfers between devices: 24 us -> 23.1 us  [shift(): return lax.ppermute(x, 'dp', pairs)]
  transfers between devices with their start and end apart: 20 -> 20, of which waited for: 9 -> 10; matrix products, arithmetic and copies ran while one was open for 0% -> 0% of each run, Pallas kernels for 18% -> 18%
where the time goes in v20:
time: 56.6 us; the launch traced here: 56.5 us
  starting transfers between devices  24.6 us (43%)
  waiting for transfers between devices  19.4 us (34%)
  Pallas kernels  11.1 us (20%)
  between operations  0.77 us (1%)
  other arithmetic  0.61 us (1%)
    ppermute x17, starting transfers between devices, shift(): return lax.ppermute(x, 'dp', pairs)  23.1 us
    ppermute x17, waiting for transfers between devices, shift(): return lax.ppermute(x, 'dp', pairs)  18 us
    pallas_call x4, Pallas kernels, scores_of(): pl.pallas_call(functools.partial(scores_kernel, distances, split), out_sh...  3.73 us
    pallas_call x1, Pallas kernels, last_gradients(): pl.pallas_call(functools.partial(last_gradients_kernel, distances), out_s...  2.29 us
    pallas_call x2, Pallas kernels, gradients_of(): pl.pallas_call(functools.partial(gradients_kernel, distances), out_shape=...  2.2 us
    pallas_call x1, Pallas kernels, fetch(): pl.pallas_call(fetch_kernel, out_shape=pltpu.VMEM(x.shape, x.dtype), in_s...  1.6 us
    ppermute x2, waiting for transfers between devices, other_core(): return lax.ppermute(x, 'width', ((0, 1), (1, 0)))  1.38 us
    ppermute x1, starting transfers between devices, return_by(): return lax.ppermute(x, ('dp', 'width'), pairs)  1.38 us
  transfers between devices with their start and end apart: 20, of which 10 were waited for; matrix products, arithmetic and copies ran while one was open for 0% of the time, Pallas kernels for 18%

profile of v20, /device:TPU:0, one launch (start us, length us, event | category | flops | bytes accessed | tf_op | source)
XLA Modules:
  0.0 56.5 jit_solution(11315764500231006878)
XLA Ops:
  0.6 1.2 %prepare.1 = (bf16[1040,128]{1,0:T(8,128)(2,1)S(1)}, bf16[1024,128]{1,0:T(8,128)(2,1)S(1)}, bf16[1056,128]{1,0:T(8,128)(2,1)S(1)}, bf16[1056,128]{1,0:T(8,128)(2...) custom-call(s32[32]{0:T(128)} %refs_0_.1, s32[8,128]{1,0:T(8,128)} %bitcast.7, s32[32,128]{1,0:T(8,128)} %bitcast.5, ...), custom_call_target="tpu_custom_call" | custom-call | tf_op jit(solution)/shard_map/prepare/pallas_call | solution.py:124
  1.8 3.1 %collective-permute-start = (bf16[1040,128]{1,0:T(8,128)(2,1)S(1)}, bf16[1040,128]{1,0:T(8,128)(2,1)S(1)}, u32[]{:S(2)}, u32[]{:S(2)}) collective-permute-start(bf16[1040,128]{1,0:T(8,128)(2,1)S(1)} %get-tuple-element.30.refs_0_), channel_id=1, source_target_pairs={{0,4},{4,8},{8,12},{12,14},{14,10},{10,6},{6,2},{2,0},{1,5},{5,9},... | collective-permute-start | bytes 798728 | tf_op jit(solution)/shard_map/ppermute | solution.py:410
  4.9 0.0 collective-permute-start.1
  4.9 2.0 %collective-permute-start.3 = (bf16[1056,128]{1,0:T(8,128)(2,1)S(1)}, bf16[1056,128]{1,0:T(8,128)(2,1)S(1)}, u32[]{:S(2)}, u32[]{:S(2)}) collective-permute-start(bf16[1056,128]{1,0:T(8,128)(2,1)S(1)} %get-tuple-element.33), channel_id=1, source_target_pairs={{0,4},{4,8},{8,12},{12,14},{14,10},{10,6},{6,2},{2,0},{1,5},{5,9},... | collective-permute-start | bytes 811016 | tf_op jit(solution)/shard_map/ppermute | solution.py:410
  6.9 0.0 collective-permute-start.4
  6.9 1.6 %fetch.1.decoder = bf16[512,2048]{1,0:T(8,128)(2,1)S(1)} custom-call(bf16[512,2048]{1,0:T(8,128)(2,1)} %source.1), custom_call_target="tpu_custom_call" | custom-call | tf_op jit(solution)/shard_map/fetch/pallas_call | solution.py:158
  8.6 5.6 %collective-permute-done.1.refs_5_ = bf16[1024,128]{1,0:T(8,128)(2,1)S(1)} collective-permute-done((bf16[1024,128]{1,0:T(8,128)(2,1)S(1)}, bf16[1024,128]{1,0:T(8,128)(2,1)S(1)}, u32[]{:S(2)}, u32[]{:S(2)}) %collective-permute-start.1) | collective-permute-done | bytes 262176 | tf_op jit(solution)/shard_map/ppermute | solution.py:410
  14.1 0.0 collective-permute-done.refs_2_
  14.2 1.6 %collective-permute-start.2 = (bf16[1040,128]{1,0:T(8,128)(2,1)S(1)}, bf16[1040,128]{1,0:T(8,128)(2,1)S(1)}, u32[]{:S(2)}, u32[]{:S(2)}) collective-permute-start(bf16[1040,128]{1,0:T(8,128)(2,1)S(1)} %collective-permute-done.refs_2_), channel_id=1, source_target_pairs={{0,4},{4,8},{8,12},{12,14},{14,10},{10,6},{6,2},{2,0},{1,5},{5,9},... | collective-permute-start | bytes 798728 | tf_op jit(solution)/shard_map/ppermute | solution.py:410
  15.7 0.4 collective-permute-start.7
  16.2 1.7 %collective-permute-done.3.refs_3_ = bf16[1056,128]{1,0:T(8,128)(2,1)S(1)} collective-permute-done((bf16[1056,128]{1,0:T(8,128)(2,1)S(1)}, bf16[1056,128]{1,0:T(8,128)(2,1)S(1)}, u32[]{:S(2)}, u32[]{:S(2)}) %collective-permute-start.3) | collective-permute-done | bytes 270368 | tf_op jit(solution)/shard_map/ppermute | solution.py:410
  17.8 2.1 %collective-permute-start.5 = (bf16[1056,128]{1,0:T(8,128)(2,1)S(1)}, bf16[1056,128]{1,0:T(8,128)(2,1)S(1)}, u32[]{:S(2)}, u32[]{:S(2)}) collective-permute-start(bf16[1056,128]{1,0:T(8,128)(2,1)S(1)} %collective-permute-done.3.refs_3_), channel_id=1, source_target_pairs={{0,4},{4,8},{8,12},{12,14},{14,10},{10,6},{6,2},{2,0},{1,5},{5,9},... | collective-permute-start | bytes 811016 | tf_op jit(solution)/shard_map/ppermute | solution.py:410
  20.0 0.0 collective-permute-done.4.refs_4_
  20.0 0.0 collective-permute-start.6
  20.0 3.6 %collective-permute-done.2.refs_0_ = bf16[1040,128]{1,0:T(8,128)(2,1)S(1)} collective-permute-done((bf16[1040,128]{1,0:T(8,128)(2,1)S(1)}, bf16[1040,128]{1,0:T(8,128)(2,1)S(1)}, u32[]{:S(2)}, u32[]{:S(2)}) %collective-permute-start.2) | collective-permute-done | bytes 266272 | tf_op jit(solution)/shard_map/ppermute | solution.py:410
  23.6 2.1 %collective-permute-start.8 = (bf16[1040,128]{1,0:T(8,128)(2,1)S(1)}, bf16[1040,128]{1,0:T(8,128)(2,1)S(1)}, u32[]{:S(2)}, u32[]{:S(2)}) collective-permute-start(bf16[1040,128]{1,0:T(8,128)(2,1)S(1)} %collective-permute-done.2.refs_0_), channel_id=1, source_target_pairs={{0,4},{4,8},{8,12},{12,14},{14,10},{10,6},{6,2},{2,0},{1,5},{5,9},... | collective-permute-start | bytes 798728 | tf_op jit(solution)/shard_map/ppermute | solution.py:410
  25.7 0.0 collective-permute-done.7.refs_3_
  25.7 0.0 collective-permute-start.9
  25.7 1.3 %gradients.2.refs_4_ = f32[512,2048]{1,0:T(8,128)S(1)} custom-call(f32[8,128]{1,0:T(8,128)S(1)} %get-tuple-element.29.own_facts, bf16[1040,128]{1,0:T(8,128)(2,1)S(1)} %get-tuple-element.30.refs_0_, bf16[1024,128]{1,0:T(8,128)(2,1)S(1)} %get-tuple-element.31.refs_1_, bf16[1040,128]{1,0:T(8,128)(2,1)S(1)} %collective-permute-done.refs_2_, ...), custom_call_target="tpu_custom_call" | custom-call | tf_op jit(solution)/shard_map/gradients/pallas_call | solution.py:299
  27.0 1.4 %scores.4 = (f32[8,128]{1,0:T(8,128)S(1)}, f32[8,128]{1,0:T(8,128)S(1)}, f32[8,128]{1,0:T(8,128)S(1)}) custom-call(bf16[512,2048]{1,0:T(8,128)(2,1)S(1)} %fetch.1.decoder, f32[8,128]{1,0:T(8,128)S(1)} %get-tuple-element.29.own_facts, bf16[1040,128]{1,0:T(8,128)(2,1)S(1)} %get-tuple-element.30.refs_0_, bf16[1024,128]{1,0:T(8,128)(2,1)S(1)} %get-tuple-element.31.refs_1_, ...), custom_call_target="tpu_custom_call" | custom-call | tf_op jit(solution)/shard_map/scores/pallas_call | solution.py:278
  28.3 1.0 %collective-permute-done.5.piece = bf16[1056,128]{1,0:T(8,128)(2,1)S(1)} collective-permute-done((bf16[1056,128]{1,0:T(8,128)(2,1)S(1)}, bf16[1056,128]{1,0:T(8,128)(2,1)S(1)}, u32[]{:S(2)}, u32[]{:S(2)}) %collective-permute-start.5) | collective-permute-done | bytes 270368 | tf_op jit(solution)/shard_map/ppermute | solution.py:410
  29.4 2.2 %collective-permute-start.11 = (bf16[1056,128]{1,0:T(8,128)(2,1)S(1)}, bf16[1056,128]{1,0:T(8,128)(2,1)S(1)}, u32[]{:S(2)}, u32[]{:S(2)}) collective-permute-start(bf16[1056,128]{1,0:T(8,128)(2,1)S(1)} %stamp.2.refs_1_), channel_id=1, source_target_pairs={{0,4},{4,8},{8,12},{12,14},{14,10},{10,6},{6,2},{2,0},{1,5},{5,9},... | collective-permute-start | bytes 811016 | tf_op jit(solution)/shard_map/ppermute | solution.py:410
  31.6 0.0 collective-permute-done.6.piece
  31.6 0.1 collective-permute-start.12
  31.7 0.8 %scores.5 = (f32[8,128]{1,0:T(8,128)S(1)}, f32[8,128]{1,0:T(8,128)S(1)}) custom-call(bf16[512,2048]{1,0:T(8,128)(2,1)S(1)} %fetch.1.decoder, f32[8,128]{1,0:T(8,128)S(1)} %get-tuple-element.29.own_facts, bf16[1040,128]{1,0:T(8,128)(2,1)S(1)} %collective-permute-done.2.refs_0_, bf16[1056,128]{1,0:T(8,128)(2,1)S(1)} %stamp.2.refs_1_, ...), custom_call_target="tpu_custom_call" | custom-call | tf_op jit(solution)/shard_map/scores/pallas_call | solution.py:278
  32.5 0.1 collective-permute-start.10
  32.6 0.9 %gradients.3.refs_6_ = f32[512,2048]{1,0:T(8,128)S(1)} custom-call(f32[8,128]{1,0:T(8,128)S(1)} %get-tuple-element.29.own_facts, bf16[1040,128]{1,0:T(8,128)(2,1)S(1)} %collective-permute-done.2.refs_0_, bf16[1056,128]{1,0:T(8,128)(2,1)S(1)} %stamp.2.refs_1_, bf16[1056,128]{1,0:T(8,128)(2,1)S(1)} %stamp.3.refs_2_, ...), custom_call_target="tpu_custom_call", output_to_operand_aliasing={{}: (5, {})} | custom-call | tf_op jit(solution)/shard_map/gradients/pallas_call | solution.py:299
  33.6 0.2 collective-permute-done.10
  33.8 3.2 %collective-permute-done.9.refs_3_ = bf16[1024,128]{1,0:T(8,128)(2,1)S(1)} collective-permute-done((bf16[1024,128]{1,0:T(8,128)(2,1)S(1)}, bf16[1024,128]{1,0:T(8,128)(2,1)S(1)}, u32[]{:S(2)}, u32[]{:S(2)}) %collective-permute-start.9) | collective-permute-done | bytes 262176 | tf_op jit(solution)/shard_map/ppermute | solution.py:410
  37.0 0.0 collective-permute-done.8.refs_0_
  37.0 1.6 %collective-permute-start.13 = (bf16[1040,128]{1,0:T(8,128)(2,1)S(1)}, bf16[1040,128]{1,0:T(8,128)(2,1)S(1)}, u32[]{:S(2)}, u32[]{:S(2)}) collective-permute-start(bf16[1040,128]{1,0:T(8,128)(2,1)S(1)} %collective-permute-done.8.refs_0_), channel_id=1, source_target_pairs={{0,4},{4,8},{8,12},{12,14},{14,10},{10,6},{6,2},{2,0},{1,5},{5,9},... | collective-permute-start | bytes 798728 | tf_op jit(solution)/shard_map/ppermute | solution.py:410
  38.6 0.4 collective-permute-start.14
  39.0 1.4 %collective-permute-start.18 = (f32[32,128]{1,0:T(8,128)S(1)}, f32[32,128]{1,0:T(8,128)S(1)}, u32[]{:S(2)}, u32[]{:S(2)}) collective-permute-start(f32[32,128]{1,0:T(8,128)S(1)} %concatenate.3), channel_id=1, source_target_pairs={{0,6},{1,9},{4,2},{5,13},{8,0},{9,15},{12,4},{13,11},{14,8},{15,7}... | collective-permute-start | bytes 49160 | tf_op jit(solution)/shard_map/ppermute | solution.py:428
  40.4 0.5 collective-permute-done.11.refs_1_.onward
  40.8 1.9 %collective-permute-done.12.refs_2_.back = bf16[1056,128]{1,0:T(8,128)(2,1)S(1)} collective-permute-done((bf16[1056,128]{1,0:T(8,128)(2,1)S(1)}, bf16[1056,128]{1,0:T(8,128)(2,1)S(1)}, u32[]{:S(2)}, u32[]{:S(2)}) %collective-permute-start.12) | collective-permute-done | bytes 270368 | tf_op jit(solution)/shard_map/ppermute | solution.py:410
  42.8 0.8 %scores.6 = (f32[8,128]{1,0:T(8,128)S(1)}, f32[8,128]{1,0:T(8,128)S(1)}) custom-call(bf16[512,2048]{1,0:T(8,128)(2,1)S(1)} %fetch.1.decoder, f32[8,128]{1,0:T(8,128)S(1)} %get-tuple-element.29.own_facts, bf16[1040,128]{1,0:T(8,128)(2,1)S(1)} %collective-permute-done.8.refs_0_, bf16[1056,128]{1,0:T(8,128)(2,1)S(1)} %collective-permute-done.11.refs_1_.onward, ...), custom_call_target="tpu_custom_call" | custom-call | tf_op jit(solution)/shard_map/scores/pallas_call | solution.py:278
  43.6 2.4 %collective-permute-start.15 = (f32[8,128]{1,0:T(8,128)S(1)}, f32[8,128]{1,0:T(8,128)S(1)}, u32[]{:S(2)}, u32[]{:S(2)}) collective-permute-start(f32[8,128]{1,0:T(8,128)S(1)} %get-tuple-element.46), channel_id=1, source_target_pairs={{0,10},{4,6},{8,2},{12,0},{14,4},{10,8},{6,12},{2,14},{1,11},{5,7}... | collective-permute-start | bytes 12296 | tf_op jit(solution)/shard_map/ppermute | solution.py:410
  46.0 1.4 %collective-permute-start.16 = (f32[8,128]{1,0:T(8,128)S(1)}, f32[8,128]{1,0:T(8,128)S(1)}, u32[]{:S(2)}, u32[]{:S(2)}) collective-permute-start(f32[8,128]{1,0:T(8,128)S(1)} %get-tuple-element.47), channel_id=1, source_target_pairs={{0,12},{4,14},{8,10},{12,6},{14,2},{10,0},{6,4},{2,8},{1,13},{5,15... | collective-permute-start | bytes 12296 | tf_op jit(solution)/shard_map/ppermute | solution.py:410
  47.5 0.0 collective-permute-done.14.refs_5_.refs_1_
  47.5 0.0 collective-permute-done.13.refs_4_.refs_0_
  47.5 0.7 %scores.7 = f32[8,128]{1,0:T(8,128)S(1)} custom-call(bf16[512,2048]{1,0:T(8,128)(2,1)S(1)} %fetch.1.decoder, f32[8,128]{1,0:T(8,128)S(1)} %get-tuple-element.29.own_facts, bf16[1040,128]{1,0:T(8,128)(2,1)S(1)} %collective-permute-done.13.refs_4_.refs_0_, bf16[1024,128]{1,0:T(8,128)(2,1)S(1)} %collective-permute-done.14.refs_5_.refs_1_), custom_call_target="tpu_custom_call" | custom-call | tf_op jit(solution)/shard_map/scores/pallas_call | solution.py:278
  48.2 3.5 %collective-permute-start.17 = (f32[8,128]{1,0:T(8,128)S(1)}, f32[8,128]{1,0:T(8,128)S(1)}, u32[]{:S(2)}, u32[]{:S(2)}) collective-permute-start(f32[8,128]{1,0:T(8,128)S(1)} %scores.7), channel_id=1, source_target_pairs={{0,14},{4,10},{8,6},{12,2},{14,0},{10,4},{6,8},{2,12},{1,15},{5,11... | collective-permute-start | bytes 12296 | tf_op jit(solution)/shard_map/ppermute | solution.py:410
  51.7 0.0 collective-permute-done.15.ahead
  51.7 0.0 collective-permute-done.16.behind
  51.7 0.0 collective-permute-done.18
  51.7 2.3 %last_gradients.1 = bf16[512,2048]{1,0:T(8,128)(2,1)} custom-call(f32[8,128]{1,0:T(8,128)S(1)} %get-tuple-element.29.own_facts, bf16[1040,128]{1,0:T(8,128)(2,1)S(1)} %collective-permute-done.8.refs_0_, bf16[1056,128]{1,0:T(8,128)(2,1)S(1)} %collective-permute-done.11.refs_1_.onward, bf16[1056,128]{1,0:T(8,128)(2,1)S(1)} %collective-permute-done.12.refs_2_.back, ...), custom_call_target="tpu_custom_call" | custom-call | tf_op jit(solution)/shard_map/last_gradients/pallas_call | solution.py:329
  54.0 0.6 %collective-permute-done.17.opposite = f32[8,128]{1,0:T(8,128)S(1)} collective-permute-done((f32[8,128]{1,0:T(8,128)S(1)}, f32[8,128]{1,0:T(8,128)S(1)}, u32[]{:S(2)}, u32[]{:S(2)}) %collective-permute-start.17) | collective-permute-done | bytes 4128 | tf_op jit(solution)/shard_map/ppermute | solution.py:410
  54.6 0.1 collective-permute-start.19
  54.7 1.2 %collective-permute-done.19 = f32[32,128]{1,0:T(8,128)S(1)} collective-permute-done((f32[32,128]{1,0:T(8,128)S(1)}, f32[32,128]{1,0:T(8,128)S(1)}, u32[]{:S(2)}, u32[]{:S(2)}) %collective-permute-start.19) | collective-permute-done | bytes 16416 | tf_op jit(solution)/shard_map/ppermute | solution.py:421
  55.9 0.6 %add_bitcast_fusion = f32[128,32]{0,1:T(8,128)} fusion(f32[32,128]{1,0:T(8,128)S(1)} %unpack.1, f32[32,128]{1,0:T(8,128)S(1)} %collective-permute-done.19), kind=kLoop, calls=%fused_computation | loop fusion | flops 4096 | bytes 49152 | tf_op jit(solution)/shard_map/transpose | solution.py:465
  (6 shorter events, 0.1 us)
Async XLA Ops:
  1.8 12.3 %collective-permute-start = (bf16[1040,128]{1,0:T(8,128)(2,1)S(1)}, bf16[1040,128]{1,0:T(8,128)(2,1)S(1)}, u32[]{:S(2)}, u32[]{:S(2)}) collective-permute-start(bf16[1040,128]{1,0:T(8,128)(2,1)S(1)} %get-tuple-element.30.refs_0_), channel_id=1, source_target_pairs={{0,4},{4,8},{8,12},{12,14},{14,10},{10,6},{6,2},{2,0},{1,5},{5,9},... | collective-permute-start | bytes 798728 | tf_op jit(solution)/shard_map/ppermute | solution.py:410
  4.9 9.2 %collective-permute-start.1 = (bf16[1024,128]{1,0:T(8,128)(2,1)S(1)}, bf16[1024,128]{1,0:T(8,128)(2,1)S(1)}, u32[]{:S(2)}, u32[]{:S(2)}) collective-permute-start(bf16[1024,128]{1,0:T(8,128)(2,1)S(1)} %get-tuple-element.31.refs_1_), channel_id=1, source_target_pairs={{0,2},{4,0},{8,4},{12,8},{14,12},{10,14},{6,10},{2,6},{1,3},{5,1},... | collective-permute-start | bytes 786440 | tf_op jit(solution)/shard_map/ppermute | solution.py:410
  4.9 12.9 %collective-permute-start.3 = (bf16[1056,128]{1,0:T(8,128)(2,1)S(1)}, bf16[1056,128]{1,0:T(8,128)(2,1)S(1)}, u32[]{:S(2)}, u32[]{:S(2)}) collective-permute-start(bf16[1056,128]{1,0:T(8,128)(2,1)S(1)} %get-tuple-element.33), channel_id=1, source_target_pairs={{0,4},{4,8},{8,12},{12,14},{14,10},{10,6},{6,2},{2,0},{1,5},{5,9},... | collective-permute-start | bytes 811016 | tf_op jit(solution)/shard_map/ppermute | solution.py:410
  6.9 13.1 %collective-permute-start.4 = (bf16[1056,128]{1,0:T(8,128)(2,1)S(1)}, bf16[1056,128]{1,0:T(8,128)(2,1)S(1)}, u32[]{:S(2)}, u32[]{:S(2)}) collective-permute-start(bf16[1056,128]{1,0:T(8,128)(2,1)S(1)} %get-tuple-element.34), channel_id=1, source_target_pairs={{0,2},{4,0},{8,4},{12,8},{14,12},{10,14},{6,10},{2,6},{1,3},{5,1},... | collective-permute-start | bytes 811016 | tf_op jit(solution)/shard_map/ppermute | solution.py:410
  14.2 9.4 %collective-permute-start.2 = (bf16[1040,128]{1,0:T(8,128)(2,1)S(1)}, bf16[1040,128]{1,0:T(8,128)(2,1)S(1)}, u32[]{:S(2)}, u32[]{:S(2)}) collective-permute-start(bf16[1040,128]{1,0:T(8,128)(2,1)S(1)} %collective-permute-done.refs_2_), channel_id=1, source_target_pairs={{0,4},{4,8},{8,12},{12,14},{14,10},{10,6},{6,2},{2,0},{1,5},{5,9},... | collective-permute-start | bytes 798728 | tf_op jit(solution)/shard_map/ppermute | solution.py:410
  15.7 10.0 %collective-permute-start.7 = (bf16[1024,128]{1,0:T(8,128)(2,1)S(1)}, bf16[1024,128]{1,0:T(8,128)(2,1)S(1)}, u32[]{:S(2)}, u32[]{:S(2)}) collective-permute-start(bf16[1024,128]{1,0:T(8,128)(2,1)S(1)} %collective-permute-done.1.refs_5_), channel_id=1, source_target_pairs={{0,2},{4,0},{8,4},{12,8},{14,12},{10,14},{6,10},{2,6},{1,3},{5,1},... | collective-permute-start | bytes 786440 | tf_op jit(solution)/shard_map/ppermute | solution.py:410
  17.8 11.5 %collective-permute-start.5 = (bf16[1056,128]{1,0:T(8,128)(2,1)S(1)}, bf16[1056,128]{1,0:T(8,128)(2,1)S(1)}, u32[]{:S(2)}, u32[]{:S(2)}) collective-permute-start(bf16[1056,128]{1,0:T(8,128)(2,1)S(1)} %collective-permute-done.3.refs_3_), channel_id=1, source_target_pairs={{0,4},{4,8},{8,12},{12,14},{14,10},{10,6},{6,2},{2,0},{1,5},{5,9},... | collective-permute-start | bytes 811016 | tf_op jit(solution)/shard_map/ppermute | solution.py:410
  20.0 11.6 %collective-permute-start.6 = (bf16[1056,128]{1,0:T(8,128)(2,1)S(1)}, bf16[1056,128]{1,0:T(8,128)(2,1)S(1)}, u32[]{:S(2)}, u32[]{:S(2)}) collective-permute-start(bf16[1056,128]{1,0:T(8,128)(2,1)S(1)} %collective-permute-done.4.refs_4_), channel_id=1, source_target_pairs={{0,2},{4,0},{8,4},{12,8},{14,12},{10,14},{6,10},{2,6},{1,3},{5,1},... | collective-permute-start | bytes 811016 | tf_op jit(solution)/shard_map/ppermute | solution.py:410
  23.6 13.4 %collective-permute-start.8 = (bf16[1040,128]{1,0:T(8,128)(2,1)S(1)}, bf16[1040,128]{1,0:T(8,128)(2,1)S(1)}, u32[]{:S(2)}, u32[]{:S(2)}) collective-permute-start(bf16[1040,128]{1,0:T(8,128)(2,1)S(1)} %collective-permute-done.2.refs_0_), channel_id=1, source_target_pairs={{0,4},{4,8},{8,12},{12,14},{14,10},{10,6},{6,2},{2,0},{1,5},{5,9},... | collective-permute-start | bytes 798728 | tf_op jit(solution)/shard_map/ppermute | solution.py:410
  25.7 11.3 %collective-permute-start.9 = (bf16[1024,128]{1,0:T(8,128)(2,1)S(1)}, bf16[1024,128]{1,0:T(8,128)(2,1)S(1)}, u32[]{:S(2)}, u32[]{:S(2)}) collective-permute-start(bf16[1024,128]{1,0:T(8,128)(2,1)S(1)} %collective-permute-done.7.refs_3_), channel_id=1, source_target_pairs={{0,2},{4,0},{8,4},{12,8},{14,12},{10,14},{6,10},{2,6},{1,3},{5,1},... | collective-permute-start | bytes 786440 | tf_op jit(solution)/shard_map/ppermute | solution.py:410
  29.4 11.5 %collective-permute-start.11 = (bf16[1056,128]{1,0:T(8,128)(2,1)S(1)}, bf16[1056,128]{1,0:T(8,128)(2,1)S(1)}, u32[]{:S(2)}, u32[]{:S(2)}) collective-permute-start(bf16[1056,128]{1,0:T(8,128)(2,1)S(1)} %stamp.2.refs_1_), channel_id=1, source_target_pairs={{0,4},{4,8},{8,12},{12,14},{14,10},{10,6},{6,2},{2,0},{1,5},{5,9},... | collective-permute-start | bytes 811016 | tf_op jit(solution)/shard_map/ppermute | solution.py:410
  31.6 11.1 %collective-permute-start.12 = (bf16[1056,128]{1,0:T(8,128)(2,1)S(1)}, bf16[1056,128]{1,0:T(8,128)(2,1)S(1)}, u32[]{:S(2)}, u32[]{:S(2)}) collective-permute-start(bf16[1056,128]{1,0:T(8,128)(2,1)S(1)} %stamp.3.refs_2_), channel_id=1, source_target_pairs={{0,2},{4,0},{8,4},{12,8},{14,12},{10,14},{6,10},{2,6},{1,3},{5,1},... | collective-permute-start | bytes 811016 | tf_op jit(solution)/shard_map/ppermute | solution.py:410
  32.5 1.2 %collective-permute-start.10 = (f32[8,128]{1,0:T(8,128)S(1)}, f32[8,128]{1,0:T(8,128)S(1)}, u32[]{:S(2)}, u32[]{:S(2)}) collective-permute-start(f32[8,128]{1,0:T(8,128)S(1)} %get-tuple-element.42), channel_id=1, source_target_pairs={{0,1},{1,0},{2,3},{3,2},{4,5},{5,4},{6,7},{7,6},{8,9},{9,8},{10,11... | collective-permute-start | bytes 12296 | tf_op jit(solution)/shard_map/ppermute | solution.py:421
  37.0 10.5 %collective-permute-start.13 = (bf16[1040,128]{1,0:T(8,128)(2,1)S(1)}, bf16[1040,128]{1,0:T(8,128)(2,1)S(1)}, u32[]{:S(2)}, u32[]{:S(2)}) collective-permute-start(bf16[1040,128]{1,0:T(8,128)(2,1)S(1)} %collective-permute-done.8.refs_0_), channel_id=1, source_target_pairs={{0,4},{4,8},{8,12},{12,14},{14,10},{10,6},{6,2},{2,0},{1,5},{5,9},... | collective-permute-start | bytes 798728 | tf_op jit(solution)/shard_map/ppermute | solution.py:410
  38.6 8.9 %collective-permute-start.14 = (bf16[1024,128]{1,0:T(8,128)(2,1)S(1)}, bf16[1024,128]{1,0:T(8,128)(2,1)S(1)}, u32[]{:S(2)}, u32[]{:S(2)}) collective-permute-start(bf16[1024,128]{1,0:T(8,128)(2,1)S(1)} %collective-permute-done.9.refs_3_), channel_id=1, source_target_pairs={{0,2},{4,0},{8,4},{12,8},{14,12},{10,14},{6,10},{2,6},{1,3},{5,1},... | collective-permute-start | bytes 786440 | tf_op jit(solution)/shard_map/ppermute | solution.py:410
  39.0 12.7 %collective-permute-start.18 = (f32[32,128]{1,0:T(8,128)S(1)}, f32[32,128]{1,0:T(8,128)S(1)}, u32[]{:S(2)}, u32[]{:S(2)}) collective-permute-start(f32[32,128]{1,0:T(8,128)S(1)} %concatenate.3), channel_id=1, source_target_pairs={{0,6},{1,9},{4,2},{5,13},{8,0},{9,15},{12,4},{13,11},{14,8},{15,7}... | collective-permute-start | bytes 49160 | tf_op jit(solution)/shard_map/ppermute | solution.py:428
  43.6 8.1 %collective-permute-start.15 = (f32[8,128]{1,0:T(8,128)S(1)}, f32[8,128]{1,0:T(8,128)S(1)}, u32[]{:S(2)}, u32[]{:S(2)}) collective-permute-start(f32[8,128]{1,0:T(8,128)S(1)} %get-tuple-element.46), channel_id=1, source_target_pairs={{0,10},{4,6},{8,2},{12,0},{14,4},{10,8},{6,12},{2,14},{1,11},{5,7}... | collective-permute-start | bytes 12296 | tf_op jit(solution)/shard_map/ppermute | solution.py:410
  46.0 5.6 %collective-permute-start.16 = (f32[8,128]{1,0:T(8,128)S(1)}, f32[8,128]{1,0:T(8,128)S(1)}, u32[]{:S(2)}, u32[]{:S(2)}) collective-permute-start(f32[8,128]{1,0:T(8,128)S(1)} %get-tuple-element.47), channel_id=1, source_target_pairs={{0,12},{4,14},{8,10},{12,6},{14,2},{10,0},{6,4},{2,8},{1,13},{5,15... | collective-permute-start | bytes 12296 | tf_op jit(solution)/shard_map/ppermute | solution.py:410
  48.2 6.4 %collective-permute-start.17 = (f32[8,128]{1,0:T(8,128)S(1)}, f32[8,128]{1,0:T(8,128)S(1)}, u32[]{:S(2)}, u32[]{:S(2)}) collective-permute-start(f32[8,128]{1,0:T(8,128)S(1)} %scores.7), channel_id=1, source_target_pairs={{0,14},{4,10},{8,6},{12,2},{14,0},{10,4},{6,8},{2,12},{1,15},{5,11... | collective-permute-start | bytes 12296 | tf_op jit(solution)/shard_map/ppermute | solution.py:410
  54.6 1.2 %collective-permute-start.19 = (f32[32,128]{1,0:T(8,128)S(1)}, f32[32,128]{1,0:T(8,128)S(1)}, u32[]{:S(2)}, u32[]{:S(2)}) collective-permute-start(f32[32,128]{1,0:T(8,128)S(1)} %unpack.1), channel_id=1, source_target_pairs={{0,1},{1,0},{2,3},{3,2},{4,5},{5,4},{6,7},{7,6},{8,9},{9,8},{10,11... | collective-permute-start | bytes 49160 | tf_op jit(solution)/shard_map/ppermute | solution.py:421

commit v21 on v18

--- a/solution.py
+++ b/solution.py
@@ -459,7 +459,7 @@
     total = gradients_of((-2, 2), pairs, own_facts, decoder.shape, total)
     second = mine + other_core(others)
     total, first_3, second = lax.optimization_barrier((total, first_3, second))
-    second = return_by(2, jnp.concatenate([second, jnp.zeros((24, 128), jnp.float32)]))[:8]
+    second = return_by(2, jnp.concatenate([second, jnp.zeros((8, 128), jnp.float32)]))[:8]
     first_4 = hop(first_3)
     pairs = [(first_3[0], second_3[0]), (second_3[1], first_3[1])]
     onward, back = scores_of((-3, 3), pairs, decoder, own_facts)

time: 56.2 us -> 56.2 us (level)
  no operation moved by 1% of the time
where the time goes in v21:
time: 56.2 us; the launch traced here: 56 us
  starting transfers between devices  25.5 us (45%)
  waiting for transfers between devices  18 us (32%)
  Pallas kernels  11.1 us (20%)
  between operations  0.77 us (1%)
  other arithmetic  0.61 us (1%)
    ppermute x17, starting transfers between devices, shift(): return lax.ppermute(x, 'dp', pairs)  24 us
    ppermute x17, waiting for transfers between devices, shift(): return lax.ppermute(x, 'dp', pairs)  16.8 us
    pallas_call x4, Pallas kernels, scores_of(): pl.pallas_call(functools.partial(scores_kernel, distances, split), out_sh...  3.72 us
    pallas_call x1, Pallas kernels, last_gradients(): pl.pallas_call(functools.partial(last_gradients_kernel, distances), out_s...  2.28 us
    pallas_call x2, Pallas kernels, gradients_of(): pl.pallas_call(functools.partial(gradients_kernel, distances), out_shape=...  2.21 us
    pallas_call x1, Pallas kernels, fetch(): pl.pallas_call(fetch_kernel, out_shape=pltpu.VMEM(x.shape, x.dtype), in_s...  1.6 us
    ppermute x1, starting transfers between devices, return_by(): return lax.ppermute(x, ('dp', 'width'), pairs)  1.38 us
    pallas_call x1, Pallas kernels, prepare(): pl.pallas_call(functools.partial(prepare_kernel, owners), out_shape=(piec...  1.2 us
  transfers between devices with their start and end apart: 20, of which 9 were waited for; matrix products, arithmetic and copies ran while one was open for 0% of the time, Pallas kernels for 18%

profile of v21, /device:TPU:0, one launch (start us, length us, event | category | flops | bytes accessed | tf_op | source)
XLA Modules:
  0.0 56.0 jit_solution(6936775626302047092)
XLA Ops:
  0.6 1.2 %prepare.1 = (bf16[1040,128]{1,0:T(8,128)(2,1)S(1)}, bf16[1024,128]{1,0:T(8,128)(2,1)S(1)}, bf16[1056,128]{1,0:T(8,128)(2,1)S(1)}, bf16[1056,128]{1,0:T(8,128)(2...) custom-call(s32[32]{0:T(128)} %refs_0_.1, s32[8,128]{1,0:T(8,128)} %bitcast.7, s32[32,128]{1,0:T(8,128)} %bitcast.5, ...), custom_call_target="tpu_custom_call" | custom-call | tf_op jit(solution)/shard_map/prepare/pallas_call | solution.py:124
  1.8 3.1 %collective-permute-start = (bf16[1040,128]{1,0:T(8,128)(2,1)S(1)}, bf16[1040,128]{1,0:T(8,128)(2,1)S(1)}, u32[]{:S(2)}, u32[]{:S(2)}) collective-permute-start(bf16[1040,128]{1,0:T(8,128)(2,1)S(1)} %get-tuple-element.30.refs_0_), channel_id=1, source_target_pairs={{0,4},{4,8},{8,12},{12,14},{14,10},{10,6},{6,2},{2,0},{1,5},{5,9},... | collective-permute-start | bytes 798728 | tf_op jit(solution)/shard_map/ppermute | solution.py:421
  4.9 0.0 collective-permute-start.1
  4.9 2.0 %collective-permute-start.3 = (bf16[1056,128]{1,0:T(8,128)(2,1)S(1)}, bf16[1056,128]{1,0:T(8,128)(2,1)S(1)}, u32[]{:S(2)}, u32[]{:S(2)}) collective-permute-start(bf16[1056,128]{1,0:T(8,128)(2,1)S(1)} %get-tuple-element.33), channel_id=1, source_target_pairs={{0,4},{4,8},{8,12},{12,14},{14,10},{10,6},{6,2},{2,0},{1,5},{5,9},... | collective-permute-start | bytes 811016 | tf_op jit(solution)/shard_map/ppermute | solution.py:421
  6.9 0.0 collective-permute-start.5
  6.9 1.6 %fetch.1.decoder = bf16[512,2048]{1,0:T(8,128)(2,1)S(1)} custom-call(bf16[512,2048]{1,0:T(8,128)(2,1)} %source.1), custom_call_target="tpu_custom_call" | custom-call | tf_op jit(solution)/shard_map/fetch/pallas_call | solution.py:158
  8.6 5.6 %collective-permute-done.1.refs_5_ = bf16[1024,128]{1,0:T(8,128)(2,1)S(1)} collective-permute-done((bf16[1024,128]{1,0:T(8,128)(2,1)S(1)}, bf16[1024,128]{1,0:T(8,128)(2,1)S(1)}, u32[]{:S(2)}, u32[]{:S(2)}) %collective-permute-start.1) | collective-permute-done | bytes 262176 | tf_op jit(solution)/shard_map/ppermute | solution.py:421
  14.1 0.0 collective-permute-done.refs_2_
  14.2 1.6 %collective-permute-start.2 = (bf16[1040,128]{1,0:T(8,128)(2,1)S(1)}, bf16[1040,128]{1,0:T(8,128)(2,1)S(1)}, u32[]{:S(2)}, u32[]{:S(2)}) collective-permute-start(bf16[1040,128]{1,0:T(8,128)(2,1)S(1)} %collective-permute-done.refs_2_), channel_id=1, source_target_pairs={{0,4},{4,8},{8,12},{12,14},{14,10},{10,6},{6,2},{2,0},{1,5},{5,9},... | collective-permute-start | bytes 798728 | tf_op jit(solution)/shard_map/ppermute | solution.py:421
  15.7 0.4 collective-permute-start.7
  16.2 1.7 %collective-permute-done.3.refs_3_ = bf16[1056,128]{1,0:T(8,128)(2,1)S(1)} collective-permute-done((bf16[1056,128]{1,0:T(8,128)(2,1)S(1)}, bf16[1056,128]{1,0:T(8,128)(2,1)S(1)}, u32[]{:S(2)}, u32[]{:S(2)}) %collective-permute-start.3) | collective-permute-done | bytes 270368 | tf_op jit(solution)/shard_map/ppermute | solution.py:421
  17.8 2.1 %collective-permute-start.4 = (bf16[1056,128]{1,0:T(8,128)(2,1)S(1)}, bf16[1056,128]{1,0:T(8,128)(2,1)S(1)}, u32[]{:S(2)}, u32[]{:S(2)}) collective-permute-start(bf16[1056,128]{1,0:T(8,128)(2,1)S(1)} %collective-permute-done.3.refs_3_), channel_id=1, source_target_pairs={{0,4},{4,8},{8,12},{12,14},{14,10},{10,6},{6,2},{2,0},{1,5},{5,9},... | collective-permute-start | bytes 811016 | tf_op jit(solution)/shard_map/ppermute | solution.py:421
  20.0 0.0 collective-permute-done.5.refs_4_
  20.0 0.0 collective-permute-start.6
  20.0 3.6 %collective-permute-done.2.refs_0_ = bf16[1040,128]{1,0:T(8,128)(2,1)S(1)} collective-permute-done((bf16[1040,128]{1,0:T(8,128)(2,1)S(1)}, bf16[1040,128]{1,0:T(8,128)(2,1)S(1)}, u32[]{:S(2)}, u32[]{:S(2)}) %collective-permute-start.2) | collective-permute-done | bytes 266272 | tf_op jit(solution)/shard_map/ppermute | solution.py:421
  23.6 2.1 %collective-permute-start.8 = (bf16[1040,128]{1,0:T(8,128)(2,1)S(1)}, bf16[1040,128]{1,0:T(8,128)(2,1)S(1)}, u32[]{:S(2)}, u32[]{:S(2)}) collective-permute-start(bf16[1040,128]{1,0:T(8,128)(2,1)S(1)} %collective-permute-done.2.refs_0_), channel_id=1, source_target_pairs={{0,4},{4,8},{8,12},{12,14},{14,10},{10,6},{6,2},{2,0},{1,5},{5,9},... | collective-permute-start | bytes 798728 | tf_op jit(solution)/shard_map/ppermute | solution.py:421
  25.7 0.0 collective-permute-done.7.refs_3_
  25.7 0.0 collective-permute-start.9
  25.7 1.4 %scores.4 = (f32[8,128]{1,0:T(8,128)S(1)}, f32[8,128]{1,0:T(8,128)S(1)}, f32[8,128]{1,0:T(8,128)S(1)}) custom-call(bf16[512,2048]{1,0:T(8,128)(2,1)S(1)} %fetch.1.decoder, f32[8,128]{1,0:T(8,128)S(1)} %get-tuple-element.29.own_facts, bf16[1040,128]{1,0:T(8,128)(2,1)S(1)} %get-tuple-element.30.refs_0_, bf16[1024,128]{1,0:T(8,128)(2,1)S(1)} %get-tuple-element.31.refs_1_, ...), custom_call_target="tpu_custom_call" | custom-call | tf_op jit(solution)/shard_map/scores/pallas_call | solution.py:278
  27.1 2.3 %collective-permute-done.4.onward = bf16[1056,128]{1,0:T(8,128)(2,1)S(1)} collective-permute-done((bf16[1056,128]{1,0:T(8,128)(2,1)S(1)}, bf16[1056,128]{1,0:T(8,128)(2,1)S(1)}, u32[]{:S(2)}, u32[]{:S(2)}) %collective-permute-start.4) | collective-permute-done | bytes 270368 | tf_op jit(solution)/shard_map/ppermute | solution.py:421
  29.3 2.0 %collective-permute-done.6.back = bf16[1056,128]{1,0:T(8,128)(2,1)S(1)} collective-permute-done((bf16[1056,128]{1,0:T(8,128)(2,1)S(1)}, bf16[1056,128]{1,0:T(8,128)(2,1)S(1)}, u32[]{:S(2)}, u32[]{:S(2)}) %collective-permute-start.6) | collective-permute-done | bytes 270368 | tf_op jit(solution)/shard_map/ppermute | solution.py:421
  31.4 0.1 stamp.1
  31.4 1.6 %collective-permute-start.11 = (bf16[1056,128]{1,0:T(8,128)(2,1)S(1)}, bf16[1056,128]{1,0:T(8,128)(2,1)S(1)}, u32[]{:S(2)}, u32[]{:S(2)}) collective-permute-start(bf16[1056,128]{1,0:T(8,128)(2,1)S(1)} %get-tuple-element.39.refs_1_), channel_id=1, source_target_pairs={{0,4},{4,8},{8,12},{12,14},{14,10},{10,6},{6,2},{2,0},{1,5},{5,9},... | collective-permute-start | bytes 811016 | tf_op jit(solution)/shard_map/ppermute | solution.py:421
  33.1 0.4 collective-permute-start.12
  33.5 0.8 %scores.5 = (f32[8,128]{1,0:T(8,128)S(1)}, f32[8,128]{1,0:T(8,128)S(1)}) custom-call(bf16[512,2048]{1,0:T(8,128)(2,1)S(1)} %fetch.1.decoder, f32[8,128]{1,0:T(8,128)S(1)} %get-tuple-element.29.own_facts, bf16[1040,128]{1,0:T(8,128)(2,1)S(1)} %collective-permute-done.2.refs_0_, bf16[1056,128]{1,0:T(8,128)(2,1)S(1)} %get-tuple-element.39.refs_1_, ...), custom_call_target="tpu_custom_call" | custom-call | tf_op jit(solution)/shard_map/scores/pallas_call | solution.py:278
  34.3 0.1 collective-permute-start.10
  34.4 1.3 %gradients.2.refs_4_ = f32[512,2048]{1,0:T(8,128)S(1)} custom-call(f32[8,128]{1,0:T(8,128)S(1)} %get-tuple-element.29.own_facts, bf16[1040,128]{1,0:T(8,128)(2,1)S(1)} %get-tuple-element.30.refs_0_, bf16[1024,128]{1,0:T(8,128)(2,1)S(1)} %get-tuple-element.31.refs_1_, bf16[1040,128]{1,0:T(8,128)(2,1)S(1)} %collective-permute-done.refs_2_, ...), custom_call_target="tpu_custom_call" | custom-call | tf_op jit(solution)/shard_map/gradients/pallas_call | solution.py:299
  35.7 0.9 %gradients.3.refs_6_ = f32[512,2048]{1,0:T(8,128)S(1)} custom-call(f32[8,128]{1,0:T(8,128)S(1)} %get-tuple-element.29.own_facts, bf16[1040,128]{1,0:T(8,128)(2,1)S(1)} %collective-permute-done.2.refs_0_, bf16[1056,128]{1,0:T(8,128)(2,1)S(1)} %get-tuple-element.39.refs_1_, ...), custom_call_target="tpu_custom_call", output_to_operand_aliasing={{}: (5, {})} | custom-call | tf_op jit(solution)/shard_map/gradients/pallas_call | solution.py:299
  36.6 0.0 collective-permute-done.10
  36.7 0.3 collective-permute-done.9.refs_3_
  37.0 0.0 collective-permute-done.8.refs_0_
  37.0 1.6 %collective-permute-start.13 = (bf16[1040,128]{1,0:T(8,128)(2,1)S(1)}, bf16[1040,128]{1,0:T(8,128)(2,1)S(1)}, u32[]{:S(2)}, u32[]{:S(2)}) collective-permute-start(bf16[1040,128]{1,0:T(8,128)(2,1)S(1)} %collective-permute-done.8.refs_0_), channel_id=1, source_target_pairs={{0,4},{4,8},{8,12},{12,14},{14,10},{10,6},{6,2},{2,0},{1,5},{5,9},... | collective-permute-start | bytes 798728 | tf_op jit(solution)/shard_map/ppermute | solution.py:421
  38.6 0.4 collective-permute-start.14
  39.0 1.4 %collective-permute-start.18 = (f32[16,128]{1,0:T(8,128)S(1)}, f32[16,128]{1,0:T(8,128)S(1)}, u32[]{:S(2)}, u32[]{:S(2)}) collective-permute-start(f32[16,128]{1,0:T(8,128)S(1)} %concatenate.3), channel_id=1, source_target_pairs={{0,6},{1,9},{4,2},{5,13},{8,0},{9,15},{12,4},{13,11},{14,8},{15,7}... | collective-permute-start | bytes 24584 | tf_op jit(solution)/shard_map/ppermute | solution.py:439
  40.4 0.0 collective-permute-done.11.refs_1_.onward
  40.4 1.0 %collective-permute-done.12.refs_2_.back = bf16[1056,128]{1,0:T(8,128)(2,1)S(1)} collective-permute-done((bf16[1056,128]{1,0:T(8,128)(2,1)S(1)}, bf16[1056,128]{1,0:T(8,128)(2,1)S(1)}, u32[]{:S(2)}, u32[]{:S(2)}) %collective-permute-start.12) | collective-permute-done | bytes 270368 | tf_op jit(solution)/shard_map/ppermute | solution.py:421
  41.4 0.8 %scores.6 = (f32[8,128]{1,0:T(8,128)S(1)}, f32[8,128]{1,0:T(8,128)S(1)}) custom-call(bf16[512,2048]{1,0:T(8,128)(2,1)S(1)} %fetch.1.decoder, f32[8,128]{1,0:T(8,128)S(1)} %get-tuple-element.29.own_facts, bf16[1040,128]{1,0:T(8,128)(2,1)S(1)} %collective-permute-done.8.refs_0_, bf16[1056,128]{1,0:T(8,128)(2,1)S(1)} %collective-permute-done.11.refs_1_.onward, ...), custom_call_target="tpu_custom_call" | custom-call | tf_op jit(solution)/shard_map/scores/pallas_call | solution.py:278
  42.2 3.6 %collective-permute-start.15 = (f32[8,128]{1,0:T(8,128)S(1)}, f32[8,128]{1,0:T(8,128)S(1)}, u32[]{:S(2)}, u32[]{:S(2)}) collective-permute-start(f32[8,128]{1,0:T(8,128)S(1)} %get-tuple-element.46), channel_id=1, source_target_pairs={{0,10},{4,6},{8,2},{12,0},{14,4},{10,8},{6,12},{2,14},{1,11},{5,7}... | collective-permute-start | bytes 12296 | tf_op jit(solution)/shard_map/ppermute | solution.py:421
  45.8 1.2 %collective-permute-start.16 = (f32[8,128]{1,0:T(8,128)S(1)}, f32[8,128]{1,0:T(8,128)S(1)}, u32[]{:S(2)}, u32[]{:S(2)}) collective-permute-start(f32[8,128]{1,0:T(8,128)S(1)} %get-tuple-element.47), channel_id=1, source_target_pairs={{0,12},{4,14},{8,10},{12,6},{14,2},{10,0},{6,4},{2,8},{1,13},{5,15... | collective-permute-start | bytes 12296 | tf_op jit(solution)/shard_map/ppermute | solution.py:421
  47.0 0.0 collective-permute-done.14.refs_5_.refs_1_
  47.0 0.0 collective-permute-done.13.refs_4_.refs_0_
  47.0 0.7 %scores.7 = f32[8,128]{1,0:T(8,128)S(1)} custom-call(bf16[512,2048]{1,0:T(8,128)(2,1)S(1)} %fetch.1.decoder, f32[8,128]{1,0:T(8,128)S(1)} %get-tuple-element.29.own_facts, bf16[1040,128]{1,0:T(8,128)(2,1)S(1)} %collective-permute-done.13.refs_4_.refs_0_, bf16[1024,128]{1,0:T(8,128)(2,1)S(1)} %collective-permute-done.14.refs_5_.refs_1_), custom_call_target="tpu_custom_call" | custom-call | tf_op jit(solution)/shard_map/scores/pallas_call | solution.py:278
  47.7 3.7 %collective-permute-start.17 = (f32[8,128]{1,0:T(8,128)S(1)}, f32[8,128]{1,0:T(8,128)S(1)}, u32[]{:S(2)}, u32[]{:S(2)}) collective-permute-start(f32[8,128]{1,0:T(8,128)S(1)} %scores.7), channel_id=1, source_target_pairs={{0,14},{4,10},{8,6},{12,2},{14,0},{10,4},{6,8},{2,12},{1,15},{5,11... | collective-permute-start | bytes 12296 | tf_op jit(solution)/shard_map/ppermute | solution.py:421
  51.5 0.0 collective-permute-done.18
  51.5 0.0 collective-permute-done.15.ahead
  51.5 0.0 collective-permute-done.16.behind
  51.5 2.3 %last_gradients.1 = bf16[512,2048]{1,0:T(8,128)(2,1)} custom-call(f32[8,128]{1,0:T(8,128)S(1)} %get-tuple-element.29.own_facts, bf16[1040,128]{1,0:T(8,128)(2,1)S(1)} %collective-permute-done.8.refs_0_, bf16[1056,128]{1,0:T(8,128)(2,1)S(1)} %collective-permute-done.11.refs_1_.onward, bf16[1056,128]{1,0:T(8,128)(2,1)S(1)} %collective-permute-done.12.refs_2_.back, ...), custom_call_target="tpu_custom_call" | custom-call | tf_op jit(solution)/shard_map/last_gradients/pallas_call | solution.py:329
  53.8 0.3 collective-permute-done.17.opposite
  54.1 0.1 collective-permute-start.19
  54.2 1.2 %collective-permute-done.19 = f32[32,128]{1,0:T(8,128)S(1)} collective-permute-done((f32[32,128]{1,0:T(8,128)S(1)}, f32[32,128]{1,0:T(8,128)S(1)}, u32[]{:S(2)}, u32[]{:S(2)}) %collective-permute-start.19) | collective-permute-done | bytes 16416 | tf_op jit(solution)/shard_map/ppermute | solution.py:432
  55.4 0.6 %add_bitcast_fusion = f32[128,32]{0,1:T(8,128)} fusion(f32[32,128]{1,0:T(8,128)S(1)} %unpack.1, f32[32,128]{1,0:T(8,128)S(1)} %collective-permute-done.19), kind=kLoop, calls=%fused_computation | loop fusion | flops 4096 | bytes 49152 | tf_op jit(solution)/shard_map/transpose | solution.py:474
  (4 shorter events, 0.0 us)
Async XLA Ops:
  1.8 12.3 %collective-permute-start = (bf16[1040,128]{1,0:T(8,128)(2,1)S(1)}, bf16[1040,128]{1,0:T(8,128)(2,1)S(1)}, u32[]{:S(2)}, u32[]{:S(2)}) collective-permute-start(bf16[1040,128]{1,0:T(8,128)(2,1)S(1)} %get-tuple-element.30.refs_0_), channel_id=1, source_target_pairs={{0,4},{4,8},{8,12},{12,14},{14,10},{10,6},{6,2},{2,0},{1,5},{5,9},... | collective-permute-start | bytes 798728 | tf_op jit(solution)/shard_map/ppermute | solution.py:421
  4.9 9.2 %collective-permute-start.1 = (bf16[1024,128]{1,0:T(8,128)(2,1)S(1)}, bf16[1024,128]{1,0:T(8,128)(2,1)S(1)}, u32[]{:S(2)}, u32[]{:S(2)}) collective-permute-start(bf16[1024,128]{1,0:T(8,128)(2,1)S(1)} %get-tuple-element.31.refs_1_), channel_id=1, source_target_pairs={{0,2},{4,0},{8,4},{12,8},{14,12},{10,14},{6,10},{2,6},{1,3},{5,1},... | collective-permute-start | bytes 786440 | tf_op jit(solution)/shard_map/ppermute | solution.py:421
  4.9 12.9 %collective-permute-start.3 = (bf16[1056,128]{1,0:T(8,128)(2,1)S(1)}, bf16[1056,128]{1,0:T(8,128)(2,1)S(1)}, u32[]{:S(2)}, u32[]{:S(2)}) collective-permute-start(bf16[1056,128]{1,0:T(8,128)(2,1)S(1)} %get-tuple-element.33), channel_id=1, source_target_pairs={{0,4},{4,8},{8,12},{12,14},{14,10},{10,6},{6,2},{2,0},{1,5},{5,9},... | collective-permute-start | bytes 811016 | tf_op jit(solution)/shard_map/ppermute | solution.py:421
  6.9 13.1 %collective-permute-start.5 = (bf16[1056,128]{1,0:T(8,128)(2,1)S(1)}, bf16[1056,128]{1,0:T(8,128)(2,1)S(1)}, u32[]{:S(2)}, u32[]{:S(2)}) collective-permute-start(bf16[1056,128]{1,0:T(8,128)(2,1)S(1)} %get-tuple-element.34), channel_id=1, source_target_pairs={{0,2},{4,0},{8,4},{12,8},{14,12},{10,14},{6,10},{2,6},{1,3},{5,1},... | collective-permute-start | bytes 811016 | tf_op jit(solution)/shard_map/ppermute | solution.py:421
  14.2 9.4 %collective-permute-start.2 = (bf16[1040,128]{1,0:T(8,128)(2,1)S(1)}, bf16[1040,128]{1,0:T(8,128)(2,1)S(1)}, u32[]{:S(2)}, u32[]{:S(2)}) collective-permute-start(bf16[1040,128]{1,0:T(8,128)(2,1)S(1)} %collective-permute-done.refs_2_), channel_id=1, source_target_pairs={{0,4},{4,8},{8,12},{12,14},{14,10},{10,6},{6,2},{2,0},{1,5},{5,9},... | collective-permute-start | bytes 798728 | tf_op jit(solution)/shard_map/ppermute | solution.py:421
  15.7 10.0 %collective-permute-start.7 = (bf16[1024,128]{1,0:T(8,128)(2,1)S(1)}, bf16[1024,128]{1,0:T(8,128)(2,1)S(1)}, u32[]{:S(2)}, u32[]{:S(2)}) collective-permute-start(bf16[1024,128]{1,0:T(8,128)(2,1)S(1)} %collective-permute-done.1.refs_5_), channel_id=1, source_target_pairs={{0,2},{4,0},{8,4},{12,8},{14,12},{10,14},{6,10},{2,6},{1,3},{5,1},... | collective-permute-start | bytes 786440 | tf_op jit(solution)/shard_map/ppermute | solution.py:421
  17.8 11.5 %collective-permute-start.4 = (bf16[1056,128]{1,0:T(8,128)(2,1)S(1)}, bf16[1056,128]{1,0:T(8,128)(2,1)S(1)}, u32[]{:S(2)}, u32[]{:S(2)}) collective-permute-start(bf16[1056,128]{1,0:T(8,128)(2,1)S(1)} %collective-permute-done.3.refs_3_), channel_id=1, source_target_pairs={{0,4},{4,8},{8,12},{12,14},{14,10},{10,6},{6,2},{2,0},{1,5},{5,9},... | collective-permute-start | bytes 811016 | tf_op jit(solution)/shard_map/ppermute | solution.py:421
  20.0 11.4 %collective-permute-start.6 = (bf16[1056,128]{1,0:T(8,128)(2,1)S(1)}, bf16[1056,128]{1,0:T(8,128)(2,1)S(1)}, u32[]{:S(2)}, u32[]{:S(2)}) collective-permute-start(bf16[1056,128]{1,0:T(8,128)(2,1)S(1)} %collective-permute-done.5.refs_4_), channel_id=1, source_target_pairs={{0,2},{4,0},{8,4},{12,8},{14,12},{10,14},{6,10},{2,6},{1,3},{5,1},... | collective-permute-start | bytes 811016 | tf_op jit(solution)/shard_map/ppermute | solution.py:421
  23.6 13.4 %collective-permute-start.8 = (bf16[1040,128]{1,0:T(8,128)(2,1)S(1)}, bf16[1040,128]{1,0:T(8,128)(2,1)S(1)}, u32[]{:S(2)}, u32[]{:S(2)}) collective-permute-start(bf16[1040,128]{1,0:T(8,128)(2,1)S(1)} %collective-permute-done.2.refs_0_), channel_id=1, source_target_pairs={{0,4},{4,8},{8,12},{12,14},{14,10},{10,6},{6,2},{2,0},{1,5},{5,9},... | collective-permute-start | bytes 798728 | tf_op jit(solution)/shard_map/ppermute | solution.py:421
  25.7 11.3 %collective-permute-start.9 = (bf16[1024,128]{1,0:T(8,128)(2,1)S(1)}, bf16[1024,128]{1,0:T(8,128)(2,1)S(1)}, u32[]{:S(2)}, u32[]{:S(2)}) collective-permute-start(bf16[1024,128]{1,0:T(8,128)(2,1)S(1)} %collective-permute-done.7.refs_3_), channel_id=1, source_target_pairs={{0,2},{4,0},{8,4},{12,8},{14,12},{10,14},{6,10},{2,6},{1,3},{5,1},... | collective-permute-start | bytes 786440 | tf_op jit(solution)/shard_map/ppermute | solution.py:421
  31.4 9.0 %collective-permute-start.11 = (bf16[1056,128]{1,0:T(8,128)(2,1)S(1)}, bf16[1056,128]{1,0:T(8,128)(2,1)S(1)}, u32[]{:S(2)}, u32[]{:S(2)}) collective-permute-start(bf16[1056,128]{1,0:T(8,128)(2,1)S(1)} %get-tuple-element.39.refs_1_), channel_id=1, source_target_pairs={{0,4},{4,8},{8,12},{12,14},{14,10},{10,6},{6,2},{2,0},{1,5},{5,9},... | collective-permute-start | bytes 811016 | tf_op jit(solution)/shard_map/ppermute | solution.py:421
  33.1 8.4 %collective-permute-start.12 = (bf16[1056,128]{1,0:T(8,128)(2,1)S(1)}, bf16[1056,128]{1,0:T(8,128)(2,1)S(1)}, u32[]{:S(2)}, u32[]{:S(2)}) collective-permute-start(bf16[1056,128]{1,0:T(8,128)(2,1)S(1)} %get-tuple-element.40.refs_2_), channel_id=1, source_target_pairs={{0,2},{4,0},{8,4},{12,8},{14,12},{10,14},{6,10},{2,6},{1,3},{5,1},... | collective-permute-start | bytes 811016 | tf_op jit(solution)/shard_map/ppermute | solution.py:421
  34.3 2.3 %collective-permute-start.10 = (f32[8,128]{1,0:T(8,128)S(1)}, f32[8,128]{1,0:T(8,128)S(1)}, u32[]{:S(2)}, u32[]{:S(2)}) collective-permute-start(f32[8,128]{1,0:T(8,128)S(1)} %get-tuple-element.42), channel_id=1, source_target_pairs={{0,1},{1,0},{2,3},{3,2},{4,5},{5,4},{6,7},{7,6},{8,9},{9,8},{10,11... | collective-permute-start | bytes 12296 | tf_op jit(solution)/shard_map/ppermute | solution.py:432
  37.0 10.0 %collective-permute-start.13 = (bf16[1040,128]{1,0:T(8,128)(2,1)S(1)}, bf16[1040,128]{1,0:T(8,128)(2,1)S(1)}, u32[]{:S(2)}, u32[]{:S(2)}) collective-permute-start(bf16[1040,128]{1,0:T(8,128)(2,1)S(1)} %collective-permute-done.8.refs_0_), channel_id=1, source_target_pairs={{0,4},{4,8},{8,12},{12,14},{14,10},{10,6},{6,2},{2,0},{1,5},{5,9},... | collective-permute-start | bytes 798728 | tf_op jit(solution)/shard_map/ppermute | solution.py:421
  38.6 8.5 %collective-permute-start.14 = (bf16[1024,128]{1,0:T(8,128)(2,1)S(1)}, bf16[1024,128]{1,0:T(8,128)(2,1)S(1)}, u32[]{:S(2)}, u32[]{:S(2)}) collective-permute-start(bf16[1024,128]{1,0:T(8,128)(2,1)S(1)} %collective-permute-done.9.refs_3_), channel_id=1, source_target_pairs={{0,2},{4,0},{8,4},{12,8},{14,12},{10,14},{6,10},{2,6},{1,3},{5,1},... | collective-permute-start | bytes 786440 | tf_op jit(solution)/shard_map/ppermute | solution.py:421
  39.0 12.5 %collective-permute-start.18 = (f32[16,128]{1,0:T(8,128)S(1)}, f32[16,128]{1,0:T(8,128)S(1)}, u32[]{:S(2)}, u32[]{:S(2)}) collective-permute-start(f32[16,128]{1,0:T(8,128)S(1)} %concatenate.3), channel_id=1, source_target_pairs={{0,6},{1,9},{4,2},{5,13},{8,0},{9,15},{12,4},{13,11},{14,8},{15,7}... | collective-permute-start | bytes 24584 | tf_op jit(solution)/shard_map/ppermute | solution.py:439
  42.2 9.2 %collective-permute-start.15 = (f32[8,128]{1,0:T(8,128)S(1)}, f32[8,128]{1,0:T(8,128)S(1)}, u32[]{:S(2)}, u32[]{:S(2)}) collective-permute-start(f32[8,128]{1,0:T(8,128)S(1)} %get-tuple-element.46), channel_id=1, source_target_pairs={{0,10},{4,6},{8,2},{12,0},{14,4},{10,8},{6,12},{2,14},{1,11},{5,7}... | collective-permute-start | bytes 12296 | tf_op jit(solution)/shard_map/ppermute | solution.py:421
  45.8 5.6 %collective-permute-start.16 = (f32[8,128]{1,0:T(8,128)S(1)}, f32[8,128]{1,0:T(8,128)S(1)}, u32[]{:S(2)}, u32[]{:S(2)}) collective-permute-start(f32[8,128]{1,0:T(8,128)S(1)} %get-tuple-element.47), channel_id=1, source_target_pairs={{0,12},{4,14},{8,10},{12,6},{14,2},{10,0},{6,4},{2,8},{1,13},{5,15... | collective-permute-start | bytes 12296 | tf_op jit(solution)/shard_map/ppermute | solution.py:421
  47.7 6.4 %collective-permute-start.17 = (f32[8,128]{1,0:T(8,128)S(1)}, f32[8,128]{1,0:T(8,128)S(1)}, u32[]{:S(2)}, u32[]{:S(2)}) collective-permute-start(f32[8,128]{1,0:T(8,128)S(1)} %scores.7), channel_id=1, source_target_pairs={{0,14},{4,10},{8,6},{12,2},{14,0},{10,4},{6,8},{2,12},{1,15},{5,11... | collective-permute-start | bytes 12296 | tf_op jit(solution)/shard_map/ppermute | solution.py:421
  54.1 1.2 %collective-permute-start.19 = (f32[32,128]{1,0:T(8,128)S(1)}, f32[32,128]{1,0:T(8,128)S(1)}, u32[]{:S(2)}, u32[]{:S(2)}) collective-permute-start(f32[32,128]{1,0:T(8,128)S(1)} %unpack.1), channel_id=1, source_target_pairs={{0,1},{1,0},{2,3},{3,2},{4,5},{5,4},{6,7},{7,6},{8,9},{9,8},{10,11... | collective-permute-start | bytes 49160 | tf_op jit(solution)/shard_map/ppermute | solution.py:432

commit v22 on v12

--- a/solution.py
+++ b/solution.py
@@ -30,15 +30,17 @@
 
 
 def ring_of(owners):
-    return list(range(0, owners, 2)) + list(range(owners - 1, 0, -2))
+    return [0] + list(range(1, owners, 2)) + list(range(owners - 2, 0, -2))
 
 
 def peer_at(distance, owners):
     me = lax.axis_index("dp")
     half_ring = owners // 2
-    place = jnp.where(lax.rem(me, 2) == 0, lax.div(me, 2), owners - 1 - lax.div(me, 2))
+    up = lax.rem(me, 2) == 1
+    place = jnp.where(up, lax.div(me, 2) + 1, lax.rem(owners - lax.div(me, 2), owners))
     at = lax.rem(place + owners + distance, owners)
-    return jnp.where(at < half_ring, 2 * at, 2 * (owners - 1 - at) + 1)
+    other = lax.rem(2 * (owners - at), 2 * owners)
+    return jnp.where((at > 0) & (at <= half_ring), 2 * at - 1, other)
 
 
 ROW_SHIFT = BLK_DEV * BW // 2

time: 56.2 us -> 56.3 us (level)
  no operation moved by 1% of the time
where the time goes in v22:
time: 56.3 us; the launch traced here: 56.1 us
  starting transfers between devices  24.8 us (44%)
  waiting for transfers between devices  18.4 us (33%)
  Pallas kernels  11.5 us (20%)
  between operations  0.77 us (1%)
  other arithmetic  0.62 us (1%)
    ppermute x15, starting transfers between devices, shift(): return lax.ppermute(x, 'dp', pairs)  19.2 us
    ppermute x15, waiting for transfers between devices, shift(): return lax.ppermute(x, 'dp', pairs)  17.1 us
    ppermute x2, starting transfers between devices, return_by(): return lax.ppermute(x, ('dp', 'width'), pairs)  5.25 us
    pallas_call x4, Pallas kernels, scores_of(): pl.pallas_call(functools.partial(scores_kernel, distances, split), out_sh...  3.72 us
    pallas_call x3, Pallas kernels, gradients_of(): pl.pallas_call(functools.partial(gradients_kernel, distances), out_shape=...  3.14 us
    pallas_call x1, Pallas kernels, last_gradients(): pl.pallas_call(last_gradients_kernel, out_shape=jax.ShapeDtypeStruct(tota...  1.75 us
    pallas_call x1, Pallas kernels, fetch(): pl.pallas_call(fetch_kernel, out_shape=pltpu.VMEM(x.shape, x.dtype), in_s...  1.6 us
    ppermute x3, waiting for transfers between devices, other_core(): return lax.ppermute(x, 'width', ((0, 1), (1, 0)))  1.28 us
  transfers between devices with their start and end apart: 20, of which 10 were waited for; matrix products, arithmetic and copies ran while one was open for 0% of the time, Pallas kernels for 18%

profile of v22, /device:TPU:0, one launch (start us, length us, event | category | flops | bytes accessed | tf_op | source)
XLA Modules:
  0.0 56.1 jit_solution(14050991333138969134)
XLA Ops:
  0.6 1.2 %prepare.1 = (bf16[1040,128]{1,0:T(8,128)(2,1)S(1)}, bf16[1024,128]{1,0:T(8,128)(2,1)S(1)}, bf16[1056,128]{1,0:T(8,128)(2,1)S(1)}, bf16[1056,128]{1,0:T(8,128)(2...) custom-call(s32[32]{0:T(128)} %refs_0_.1, s32[8,128]{1,0:T(8,128)} %bitcast.7, s32[32,128]{1,0:T(8,128)} %bitcast.5, ...), custom_call_target="tpu_custom_call" | custom-call | tf_op jit(solution)/shard_map/prepare/pallas_call | solution.py:126
  1.8 3.0 %collective-permute-start = (bf16[1040,128]{1,0:T(8,128)(2,1)S(1)}, bf16[1040,128]{1,0:T(8,128)(2,1)S(1)}, u32[]{:S(2)}, u32[]{:S(2)}) collective-permute-start(bf16[1040,128]{1,0:T(8,128)(2,1)S(1)} %get-tuple-element.34.refs_0_), channel_id=1, source_target_pairs={{0,2},{2,6},{6,10},{10,14},{14,12},{12,8},{8,4},{4,0},{1,3},{3,7},... | collective-permute-start | bytes 798728 | tf_op jit(solution)/shard_map/ppermute | solution.py:419
  4.8 0.2 collective-permute-start.1
  5.0 1.9 %collective-permute-start.3 = (bf16[1056,128]{1,0:T(8,128)(2,1)S(1)}, bf16[1056,128]{1,0:T(8,128)(2,1)S(1)}, u32[]{:S(2)}, u32[]{:S(2)}) collective-permute-start(bf16[1056,128]{1,0:T(8,128)(2,1)S(1)} %get-tuple-element.37), channel_id=1, source_target_pairs={{0,2},{2,6},{6,10},{10,14},{14,12},{12,8},{8,4},{4,0},{1,3},{3,7},... | collective-permute-start | bytes 811016 | tf_op jit(solution)/shard_map/ppermute | solution.py:419
  6.9 0.2 collective-permute-start.5
  7.0 1.6 %fetch.1.decoder = bf16[512,2048]{1,0:T(8,128)(2,1)S(1)} custom-call(bf16[512,2048]{1,0:T(8,128)(2,1)} %source.1), custom_call_target="tpu_custom_call" | custom-call | tf_op jit(solution)/shard_map/fetch/pallas_call | solution.py:160
  8.6 5.4 %collective-permute-done.1.refs_5_ = bf16[1024,128]{1,0:T(8,128)(2,1)S(1)} collective-permute-done((bf16[1024,128]{1,0:T(8,128)(2,1)S(1)}, bf16[1024,128]{1,0:T(8,128)(2,1)S(1)}, u32[]{:S(2)}, u32[]{:S(2)}) %collective-permute-start.1) | collective-permute-done | bytes 262176 | tf_op jit(solution)/shard_map/ppermute | solution.py:419
  14.1 0.0 collective-permute-done.refs_2_
  14.1 1.6 %collective-permute-start.2 = (bf16[1040,128]{1,0:T(8,128)(2,1)S(1)}, bf16[1040,128]{1,0:T(8,128)(2,1)S(1)}, u32[]{:S(2)}, u32[]{:S(2)}) collective-permute-start(bf16[1040,128]{1,0:T(8,128)(2,1)S(1)} %collective-permute-done.refs_2_), channel_id=1, source_target_pairs={{0,2},{2,6},{6,10},{10,14},{14,12},{12,8},{8,4},{4,0},{1,3},{3,7},... | collective-permute-start | bytes 798728 | tf_op jit(solution)/shard_map/ppermute | solution.py:419
  15.6 0.4 collective-permute-start.7
  16.1 1.8 %collective-permute-done.3.refs_3_ = bf16[1056,128]{1,0:T(8,128)(2,1)S(1)} collective-permute-done((bf16[1056,128]{1,0:T(8,128)(2,1)S(1)}, bf16[1056,128]{1,0:T(8,128)(2,1)S(1)}, u32[]{:S(2)}, u32[]{:S(2)}) %collective-permute-start.3) | collective-permute-done | bytes 270368 | tf_op jit(solution)/shard_map/ppermute | solution.py:419
  17.9 2.0 %collective-permute-start.4 = (bf16[1056,128]{1,0:T(8,128)(2,1)S(1)}, bf16[1056,128]{1,0:T(8,128)(2,1)S(1)}, u32[]{:S(2)}, u32[]{:S(2)}) collective-permute-start(bf16[1056,128]{1,0:T(8,128)(2,1)S(1)} %collective-permute-done.3.refs_3_), channel_id=1, source_target_pairs={{0,2},{2,6},{6,10},{10,14},{14,12},{12,8},{8,4},{4,0},{1,3},{3,7},... | collective-permute-start | bytes 811016 | tf_op jit(solution)/shard_map/ppermute | solution.py:419
  19.9 0.0 collective-permute-done.5.refs_4_
  19.9 0.1 collective-permute-start.6
  20.0 3.6 %collective-permute-done.2.refs_0_ = bf16[1040,128]{1,0:T(8,128)(2,1)S(1)} collective-permute-done((bf16[1040,128]{1,0:T(8,128)(2,1)S(1)}, bf16[1040,128]{1,0:T(8,128)(2,1)S(1)}, u32[]{:S(2)}, u32[]{:S(2)}) %collective-permute-start.2) | collective-permute-done | bytes 266272 | tf_op jit(solution)/shard_map/ppermute | solution.py:419
  23.6 2.0 %collective-permute-start.8 = (bf16[1040,128]{1,0:T(8,128)(2,1)S(1)}, bf16[1040,128]{1,0:T(8,128)(2,1)S(1)}, u32[]{:S(2)}, u32[]{:S(2)}) collective-permute-start(bf16[1040,128]{1,0:T(8,128)(2,1)S(1)} %collective-permute-done.2.refs_0_), channel_id=1, source_target_pairs={{0,2},{2,6},{6,10},{10,14},{14,12},{12,8},{8,4},{4,0},{1,3},{3,7},... | collective-permute-start | bytes 798728 | tf_op jit(solution)/shard_map/ppermute | solution.py:419
  25.6 0.0 collective-permute-done.7.refs_3_
  25.6 0.1 collective-permute-start.9
  25.7 1.4 %scores.4 = (f32[8,128]{1,0:T(8,128)S(1)}, f32[8,128]{1,0:T(8,128)S(1)}, f32[8,128]{1,0:T(8,128)S(1)}) custom-call(bf16[512,2048]{1,0:T(8,128)(2,1)S(1)} %fetch.1.decoder, f32[8,128]{1,0:T(8,128)S(1)} %get-tuple-element.33.own_facts, bf16[1040,128]{1,0:T(8,128)(2,1)S(1)} %get-tuple-element.34.refs_0_, bf16[1024,128]{1,0:T(8,128)(2,1)S(1)} %get-tuple-element.35.refs_1_, ...), custom_call_target="tpu_custom_call" | custom-call | tf_op jit(solution)/shard_map/scores/pallas_call | solution.py:280
  27.1 2.4 %collective-permute-done.4.onward = bf16[1056,128]{1,0:T(8,128)(2,1)S(1)} collective-permute-done((bf16[1056,128]{1,0:T(8,128)(2,1)S(1)}, bf16[1056,128]{1,0:T(8,128)(2,1)S(1)}, u32[]{:S(2)}, u32[]{:S(2)}) %collective-permute-start.4) | collective-permute-done | bytes 270368 | tf_op jit(solution)/shard_map/ppermute | solution.py:419
  29.4 1.8 %collective-permute-done.6.back = bf16[1056,128]{1,0:T(8,128)(2,1)S(1)} collective-permute-done((bf16[1056,128]{1,0:T(8,128)(2,1)S(1)}, bf16[1056,128]{1,0:T(8,128)(2,1)S(1)}, u32[]{:S(2)}, u32[]{:S(2)}) %collective-permute-start.6) | collective-permute-done | bytes 270368 | tf_op jit(solution)/shard_map/ppermute | solution.py:419
  31.3 0.1 stamp.1
  31.3 1.6 %collective-permute-start.11 = (bf16[1056,128]{1,0:T(8,128)(2,1)S(1)}, bf16[1056,128]{1,0:T(8,128)(2,1)S(1)}, u32[]{:S(2)}, u32[]{:S(2)}) collective-permute-start(bf16[1056,128]{1,0:T(8,128)(2,1)S(1)} %get-tuple-element.43.refs_1_), channel_id=1, source_target_pairs={{0,2},{2,6},{6,10},{10,14},{14,12},{12,8},{8,4},{4,0},{1,3},{3,7},... | collective-permute-start | bytes 811016 | tf_op jit(solution)/shard_map/ppermute | solution.py:419
  33.0 0.4 collective-permute-start.12
  33.4 0.8 %scores.5 = (f32[8,128]{1,0:T(8,128)S(1)}, f32[8,128]{1,0:T(8,128)S(1)}) custom-call(bf16[512,2048]{1,0:T(8,128)(2,1)S(1)} %fetch.1.decoder, f32[8,128]{1,0:T(8,128)S(1)} %get-tuple-element.33.own_facts, bf16[1040,128]{1,0:T(8,128)(2,1)S(1)} %collective-permute-done.2.refs_0_, bf16[1056,128]{1,0:T(8,128)(2,1)S(1)} %get-tuple-element.43.refs_1_, ...), custom_call_target="tpu_custom_call" | custom-call | tf_op jit(solution)/shard_map/scores/pallas_call | solution.py:280
  34.3 0.1 collective-permute-start.10
  34.3 1.3 %gradients.3.refs_4_ = f32[512,2048]{1,0:T(8,128)S(1)} custom-call(f32[8,128]{1,0:T(8,128)S(1)} %get-tuple-element.33.own_facts, bf16[1040,128]{1,0:T(8,128)(2,1)S(1)} %get-tuple-element.34.refs_0_, bf16[1024,128]{1,0:T(8,128)(2,1)S(1)} %get-tuple-element.35.refs_1_, bf16[1040,128]{1,0:T(8,128)(2,1)S(1)} %collective-permute-done.refs_2_, ...), custom_call_target="tpu_custom_call" | custom-call | tf_op jit(solution)/shard_map/gradients/pallas_call | solution.py:301
  35.6 0.9 %gradients.4.refs_4_ = f32[512,2048]{1,0:T(8,128)S(1)} custom-call(f32[8,128]{1,0:T(8,128)S(1)} %get-tuple-element.33.own_facts, bf16[1040,128]{1,0:T(8,128)(2,1)S(1)} %collective-permute-done.2.refs_0_, bf16[1056,128]{1,0:T(8,128)(2,1)S(1)} %get-tuple-element.43.refs_1_, ...), custom_call_target="tpu_custom_call", output_to_operand_aliasing={{}: (5, {})} | custom-call | tf_op jit(solution)/shard_map/gradients/pallas_call | solution.py:301
  36.6 0.0 collective-permute-done.10
  36.6 0.3 collective-permute-done.9.refs_3_
  36.9 0.0 collective-permute-done.8.refs_0_
  36.9 1.6 %collective-permute-start.14 = (bf16[1040,128]{1,0:T(8,128)(2,1)S(1)}, bf16[1040,128]{1,0:T(8,128)(2,1)S(1)}, u32[]{:S(2)}, u32[]{:S(2)}) collective-permute-start(bf16[1040,128]{1,0:T(8,128)(2,1)S(1)} %collective-permute-done.8.refs_0_), channel_id=1, source_target_pairs={{0,2},{2,6},{6,10},{10,14},{14,12},{12,8},{8,4},{4,0},{1,3},{3,7},... | collective-permute-start | bytes 798728 | tf_op jit(solution)/shard_map/ppermute | solution.py:419
  38.5 0.4 collective-permute-start.15
  38.9 1.5 %collective-permute-start.18 = (f32[32,128]{1,0:T(8,128)S(1)}, f32[32,128]{1,0:T(8,128)S(1)}, u32[]{:S(2)}, u32[]{:S(2)}) collective-permute-start(f32[32,128]{1,0:T(8,128)S(1)} %concatenate.3), channel_id=1, source_target_pairs={{0,8},{1,7},{2,4},{3,11},{6,0},{7,15},{10,2},{11,13},{14,6},{15,9}... | collective-permute-start | bytes 49160 | tf_op jit(solution)/shard_map/ppermute | solution.py:437
  40.5 0.0 collective-permute-done.11.refs_1_.onward
  40.5 0.9 %collective-permute-done.12.refs_2_.back = bf16[1056,128]{1,0:T(8,128)(2,1)S(1)} collective-permute-done((bf16[1056,128]{1,0:T(8,128)(2,1)S(1)}, bf16[1056,128]{1,0:T(8,128)(2,1)S(1)}, u32[]{:S(2)}, u32[]{:S(2)}) %collective-permute-start.12) | collective-permute-done | bytes 270368 | tf_op jit(solution)/shard_map/ppermute | solution.py:419
  41.3 0.8 %scores.6 = (f32[8,128]{1,0:T(8,128)S(1)}, f32[8,128]{1,0:T(8,128)S(1)}) custom-call(bf16[512,2048]{1,0:T(8,128)(2,1)S(1)} %fetch.1.decoder, f32[8,128]{1,0:T(8,128)S(1)} %get-tuple-element.33.own_facts, bf16[1040,128]{1,0:T(8,128)(2,1)S(1)} %collective-permute-done.8.refs_0_, bf16[1056,128]{1,0:T(8,128)(2,1)S(1)} %collective-permute-done.11.refs_1_.onward, ...), custom_call_target="tpu_custom_call" | custom-call | tf_op jit(solution)/shard_map/scores/pallas_call | solution.py:280
  42.2 0.1 collective-permute-start.13
  42.2 0.9 %gradients.5.total = f32[512,2048]{1,0:T(8,128)S(1)} custom-call(f32[8,128]{1,0:T(8,128)S(1)} %get-tuple-element.33.own_facts, bf16[1040,128]{1,0:T(8,128)(2,1)S(1)} %collective-permute-done.8.refs_0_, bf16[1056,128]{1,0:T(8,128)(2,1)S(1)} %collective-permute-done.11.refs_1_.onward, ...), custom_call_target="tpu_custom_call", output_to_operand_aliasing={{}: (5, {})} | custom-call | tf_op jit(solution)/shard_map/gradients/pallas_call | solution.py:301
  43.2 0.2 collective-permute-done.13
  43.4 3.7 %collective-permute-start.16 = (f32[8,128]{1,0:T(8,128)S(1)}, f32[8,128]{1,0:T(8,128)S(1)}, u32[]{:S(2)}, u32[]{:S(2)}) collective-permute-start(f32[8,128]{1,0:T(8,128)S(1)} %add.12), channel_id=1, source_target_pairs={{0,12},{1,11},{2,8},{3,15},{6,4},{7,13},{10,0},{11,9},{14,2},{15,5... | collective-permute-start | bytes 12296 | tf_op jit(solution)/shard_map/ppermute | solution.py:437
  47.1 0.0 collective-permute-done.15.right.refs_1_
  47.1 0.0 collective-permute-done.14.left.refs_0_
  47.1 0.7 %scores.7 = f32[8,128]{1,0:T(8,128)S(1)} custom-call(bf16[512,2048]{1,0:T(8,128)(2,1)S(1)} %fetch.1.decoder, f32[8,128]{1,0:T(8,128)S(1)} %get-tuple-element.33.own_facts, bf16[1040,128]{1,0:T(8,128)(2,1)S(1)} %collective-permute-done.14.left.refs_0_, bf16[1024,128]{1,0:T(8,128)(2,1)S(1)} %collective-permute-done.15.right.refs_1_), custom_call_target="tpu_custom_call" | custom-call | tf_op jit(solution)/shard_map/scores/pallas_call | solution.py:280
  47.8 3.8 %collective-permute-start.17 = (f32[8,128]{1,0:T(8,128)S(1)}, f32[8,128]{1,0:T(8,128)S(1)}, u32[]{:S(2)}, u32[]{:S(2)}) collective-permute-start(f32[8,128]{1,0:T(8,128)S(1)} %scores.7), channel_id=1, source_target_pairs={{0,14},{2,12},{6,8},{10,4},{14,0},{12,2},{8,6},{4,10},{1,15},{3,13... | collective-permute-start | bytes 12296 | tf_op jit(solution)/shard_map/ppermute | solution.py:419
  51.6 0.0 collective-permute-done.18
  51.6 0.0 collective-permute-done.16.third
  51.7 1.8 %last_gradients.1 = bf16[512,2048]{1,0:T(8,128)(2,1)} custom-call(bf16[1040,128]{1,0:T(8,128)(2,1)S(1)} %collective-permute-done.14.left.refs_0_, bf16[1024,128]{1,0:T(8,128)(2,1)S(1)} %collective-permute-done.15.right.refs_1_, f32[512,2048]{1,0:T(8,128)S(1)} %gradients.5.total), custom_call_target="tpu_custom_call" | custom-call | tf_op jit(solution)/shard_map/last_gradients/pallas_call | solution.py:328
  53.4 0.8 %collective-permute-done.17.opposite = f32[8,128]{1,0:T(8,128)S(1)} collective-permute-done((f32[8,128]{1,0:T(8,128)S(1)}, f32[8,128]{1,0:T(8,128)S(1)}, u32[]{:S(2)}, u32[]{:S(2)}) %collective-permute-start.17) | collective-permute-done | bytes 4128 | tf_op jit(solution)/shard_map/ppermute | solution.py:419
  54.2 0.2 collective-permute-start.19
  54.4 1.1 %collective-permute-done.19 = f32[32,128]{1,0:T(8,128)S(1)} collective-permute-done((f32[32,128]{1,0:T(8,128)S(1)}, f32[32,128]{1,0:T(8,128)S(1)}, u32[]{:S(2)}, u32[]{:S(2)}) %collective-permute-start.19) | collective-permute-done | bytes 16416 | tf_op jit(solution)/shard_map/ppermute | solution.py:430
  55.5 0.6 %add_bitcast_fusion = f32[128,32]{0,1:T(8,128)} fusion(f32[32,128]{1,0:T(8,128)S(1)} %unpack.1, f32[32,128]{1,0:T(8,128)S(1)} %collective-permute-done.19), kind=kLoop, calls=%fused_computation | loop fusion | flops 4096 | bytes 49152 | tf_op jit(solution)/shard_map/transpose | solution.py:476
  (5 shorter events, 0.1 us)
Async XLA Ops:
  1.8 12.2 %collective-permute-start = (bf16[1040,128]{1,0:T(8,128)(2,1)S(1)}, bf16[1040,128]{1,0:T(8,128)(2,1)S(1)}, u32[]{:S(2)}, u32[]{:S(2)}) collective-permute-start(bf16[1040,128]{1,0:T(8,128)(2,1)S(1)} %get-tuple-element.34.refs_0_), channel_id=1, source_target_pairs={{0,2},{2,6},{6,10},{10,14},{14,12},{12,8},{8,4},{4,0},{1,3},{3,7},... | collective-permute-start | bytes 798728 | tf_op jit(solution)/shard_map/ppermute | solution.py:419
  4.8 9.2 %collective-permute-start.1 = (bf16[1024,128]{1,0:T(8,128)(2,1)S(1)}, bf16[1024,128]{1,0:T(8,128)(2,1)S(1)}, u32[]{:S(2)}, u32[]{:S(2)}) collective-permute-start(bf16[1024,128]{1,0:T(8,128)(2,1)S(1)} %get-tuple-element.35.refs_1_), channel_id=1, source_target_pairs={{0,4},{2,0},{6,2},{10,6},{14,10},{12,14},{8,12},{4,8},{1,5},{3,1},... | collective-permute-start | bytes 786440 | tf_op jit(solution)/shard_map/ppermute | solution.py:419
  5.0 12.9 %collective-permute-start.3 = (bf16[1056,128]{1,0:T(8,128)(2,1)S(1)}, bf16[1056,128]{1,0:T(8,128)(2,1)S(1)}, u32[]{:S(2)}, u32[]{:S(2)}) collective-permute-start(bf16[1056,128]{1,0:T(8,128)(2,1)S(1)} %get-tuple-element.37), channel_id=1, source_target_pairs={{0,2},{2,6},{6,10},{10,14},{14,12},{12,8},{8,4},{4,0},{1,3},{3,7},... | collective-permute-start | bytes 811016 | tf_op jit(solution)/shard_map/ppermute | solution.py:419
  6.9 13.1 %collective-permute-start.5 = (bf16[1056,128]{1,0:T(8,128)(2,1)S(1)}, bf16[1056,128]{1,0:T(8,128)(2,1)S(1)}, u32[]{:S(2)}, u32[]{:S(2)}) collective-permute-start(bf16[1056,128]{1,0:T(8,128)(2,1)S(1)} %get-tuple-element.38), channel_id=1, source_target_pairs={{0,4},{2,0},{6,2},{10,6},{14,10},{12,14},{8,12},{4,8},{1,5},{3,1},... | collective-permute-start | bytes 811016 | tf_op jit(solution)/shard_map/ppermute | solution.py:419
  14.1 9.6 %collective-permute-start.2 = (bf16[1040,128]{1,0:T(8,128)(2,1)S(1)}, bf16[1040,128]{1,0:T(8,128)(2,1)S(1)}, u32[]{:S(2)}, u32[]{:S(2)}) collective-permute-start(bf16[1040,128]{1,0:T(8,128)(2,1)S(1)} %collective-permute-done.refs_2_), channel_id=1, source_target_pairs={{0,2},{2,6},{6,10},{10,14},{14,12},{12,8},{8,4},{4,0},{1,3},{3,7},... | collective-permute-start | bytes 798728 | tf_op jit(solution)/shard_map/ppermute | solution.py:419
  15.6 10.0 %collective-permute-start.7 = (bf16[1024,128]{1,0:T(8,128)(2,1)S(1)}, bf16[1024,128]{1,0:T(8,128)(2,1)S(1)}, u32[]{:S(2)}, u32[]{:S(2)}) collective-permute-start(bf16[1024,128]{1,0:T(8,128)(2,1)S(1)} %collective-permute-done.1.refs_5_), channel_id=1, source_target_pairs={{0,4},{2,0},{6,2},{10,6},{14,10},{12,14},{8,12},{4,8},{1,5},{3,1},... | collective-permute-start | bytes 786440 | tf_op jit(solution)/shard_map/ppermute | solution.py:419
  17.9 11.5 %collective-permute-start.4 = (bf16[1056,128]{1,0:T(8,128)(2,1)S(1)}, bf16[1056,128]{1,0:T(8,128)(2,1)S(1)}, u32[]{:S(2)}, u32[]{:S(2)}) collective-permute-start(bf16[1056,128]{1,0:T(8,128)(2,1)S(1)} %collective-permute-done.3.refs_3_), channel_id=1, source_target_pairs={{0,2},{2,6},{6,10},{10,14},{14,12},{12,8},{8,4},{4,0},{1,3},{3,7},... | collective-permute-start | bytes 811016 | tf_op jit(solution)/shard_map/ppermute | solution.py:419
  19.9 11.4 %collective-permute-start.6 = (bf16[1056,128]{1,0:T(8,128)(2,1)S(1)}, bf16[1056,128]{1,0:T(8,128)(2,1)S(1)}, u32[]{:S(2)}, u32[]{:S(2)}) collective-permute-start(bf16[1056,128]{1,0:T(8,128)(2,1)S(1)} %collective-permute-done.5.refs_4_), channel_id=1, source_target_pairs={{0,4},{2,0},{6,2},{10,6},{14,10},{12,14},{8,12},{4,8},{1,5},{3,1},... | collective-permute-start | bytes 811016 | tf_op jit(solution)/shard_map/ppermute | solution.py:419
  23.6 13.2 %collective-permute-start.8 = (bf16[1040,128]{1,0:T(8,128)(2,1)S(1)}, bf16[1040,128]{1,0:T(8,128)(2,1)S(1)}, u32[]{:S(2)}, u32[]{:S(2)}) collective-permute-start(bf16[1040,128]{1,0:T(8,128)(2,1)S(1)} %collective-permute-done.2.refs_0_), channel_id=1, source_target_pairs={{0,2},{2,6},{6,10},{10,14},{14,12},{12,8},{8,4},{4,0},{1,3},{3,7},... | collective-permute-start | bytes 798728 | tf_op jit(solution)/shard_map/ppermute | solution.py:419
  25.6 11.3 %collective-permute-start.9 = (bf16[1024,128]{1,0:T(8,128)(2,1)S(1)}, bf16[1024,128]{1,0:T(8,128)(2,1)S(1)}, u32[]{:S(2)}, u32[]{:S(2)}) collective-permute-start(bf16[1024,128]{1,0:T(8,128)(2,1)S(1)} %collective-permute-done.7.refs_3_), channel_id=1, source_target_pairs={{0,4},{2,0},{6,2},{10,6},{14,10},{12,14},{8,12},{4,8},{1,5},{3,1},... | collective-permute-start | bytes 786440 | tf_op jit(solution)/shard_map/ppermute | solution.py:419
  31.3 9.1 %collective-permute-start.11 = (bf16[1056,128]{1,0:T(8,128)(2,1)S(1)}, bf16[1056,128]{1,0:T(8,128)(2,1)S(1)}, u32[]{:S(2)}, u32[]{:S(2)}) collective-permute-start(bf16[1056,128]{1,0:T(8,128)(2,1)S(1)} %get-tuple-element.43.refs_1_), channel_id=1, source_target_pairs={{0,2},{2,6},{6,10},{10,14},{14,12},{12,8},{8,4},{4,0},{1,3},{3,7},... | collective-permute-start | bytes 811016 | tf_op jit(solution)/shard_map/ppermute | solution.py:419
  33.0 8.3 %collective-permute-start.12 = (bf16[1056,128]{1,0:T(8,128)(2,1)S(1)}, bf16[1056,128]{1,0:T(8,128)(2,1)S(1)}, u32[]{:S(2)}, u32[]{:S(2)}) collective-permute-start(bf16[1056,128]{1,0:T(8,128)(2,1)S(1)} %get-tuple-element.44.refs_2_), channel_id=1, source_target_pairs={{0,4},{2,0},{6,2},{10,6},{14,10},{12,14},{8,12},{4,8},{1,5},{3,1},... | collective-permute-start | bytes 811016 | tf_op jit(solution)/shard_map/ppermute | solution.py:419
  34.3 2.3 %collective-permute-start.10 = (f32[8,128]{1,0:T(8,128)S(1)}, f32[8,128]{1,0:T(8,128)S(1)}, u32[]{:S(2)}, u32[]{:S(2)}) collective-permute-start(f32[8,128]{1,0:T(8,128)S(1)} %get-tuple-element.46), channel_id=1, source_target_pairs={{0,1},{1,0},{2,3},{3,2},{4,5},{5,4},{6,7},{7,6},{8,9},{9,8},{10,11... | collective-permute-start | bytes 12296 | tf_op jit(solution)/shard_map/ppermute | solution.py:430
  36.9 10.2 %collective-permute-start.14 = (bf16[1040,128]{1,0:T(8,128)(2,1)S(1)}, bf16[1040,128]{1,0:T(8,128)(2,1)S(1)}, u32[]{:S(2)}, u32[]{:S(2)}) collective-permute-start(bf16[1040,128]{1,0:T(8,128)(2,1)S(1)} %collective-permute-done.8.refs_0_), channel_id=1, source_target_pairs={{0,2},{2,6},{6,10},{10,14},{14,12},{12,8},{8,4},{4,0},{1,3},{3,7},... | collective-permute-start | bytes 798728 | tf_op jit(solution)/shard_map/ppermute | solution.py:419
  38.5 8.6 %collective-permute-start.15 = (bf16[1024,128]{1,0:T(8,128)(2,1)S(1)}, bf16[1024,128]{1,0:T(8,128)(2,1)S(1)}, u32[]{:S(2)}, u32[]{:S(2)}) collective-permute-start(bf16[1024,128]{1,0:T(8,128)(2,1)S(1)} %collective-permute-done.9.refs_3_), channel_id=1, source_target_pairs={{0,4},{2,0},{6,2},{10,6},{14,10},{12,14},{8,12},{4,8},{1,5},{3,1},... | collective-permute-start | bytes 786440 | tf_op jit(solution)/shard_map/ppermute | solution.py:419
  38.9 12.7 %collective-permute-start.18 = (f32[32,128]{1,0:T(8,128)S(1)}, f32[32,128]{1,0:T(8,128)S(1)}, u32[]{:S(2)}, u32[]{:S(2)}) collective-permute-start(f32[32,128]{1,0:T(8,128)S(1)} %concatenate.3), channel_id=1, source_target_pairs={{0,8},{1,7},{2,4},{3,11},{6,0},{7,15},{10,2},{11,13},{14,6},{15,9}... | collective-permute-start | bytes 49160 | tf_op jit(solution)/shard_map/ppermute | solution.py:437
  42.2 1.2 %collective-permute-start.13 = (f32[8,128]{1,0:T(8,128)S(1)}, f32[8,128]{1,0:T(8,128)S(1)}, u32[]{:S(2)}, u32[]{:S(2)}) collective-permute-start(f32[8,128]{1,0:T(8,128)S(1)} %get-tuple-element.51), channel_id=1, source_target_pairs={{0,1},{1,0},{2,3},{3,2},{4,5},{5,4},{6,7},{7,6},{8,9},{9,8},{10,11... | collective-permute-start | bytes 12296 | tf_op jit(solution)/shard_map/ppermute | solution.py:430
  43.4 8.3 %collective-permute-start.16 = (f32[8,128]{1,0:T(8,128)S(1)}, f32[8,128]{1,0:T(8,128)S(1)}, u32[]{:S(2)}, u32[]{:S(2)}) collective-permute-start(f32[8,128]{1,0:T(8,128)S(1)} %add.12), channel_id=1, source_target_pairs={{0,12},{1,11},{2,8},{3,15},{6,4},{7,13},{10,0},{11,9},{14,2},{15,5... | collective-permute-start | bytes 12296 | tf_op jit(solution)/shard_map/ppermute | solution.py:437
  47.8 6.4 %collective-permute-start.17 = (f32[8,128]{1,0:T(8,128)S(1)}, f32[8,128]{1,0:T(8,128)S(1)}, u32[]{:S(2)}, u32[]{:S(2)}) collective-permute-start(f32[8,128]{1,0:T(8,128)S(1)} %scores.7), channel_id=1, source_target_pairs={{0,14},{2,12},{6,8},{10,4},{14,0},{12,2},{8,6},{4,10},{1,15},{3,13... | collective-permute-start | bytes 12296 | tf_op jit(solution)/shard_map/ppermute | solution.py:419
  54.2 1.2 %collective-permute-start.19 = (f32[32,128]{1,0:T(8,128)S(1)}, f32[32,128]{1,0:T(8,128)S(1)}, u32[]{:S(2)}, u32[]{:S(2)}) collective-permute-start(f32[32,128]{1,0:T(8,128)S(1)} %unpack.1), channel_id=1, source_target_pairs={{0,1},{1,0},{2,3},{3,2},{4,5},{5,4},{6,7},{7,6},{8,9},{9,8},{10,11... | collective-permute-start | bytes 49160 | tf_op jit(solution)/shard_map/ppermute | solution.py:430

commit v23 on v18

--- a/solution.py
+++ b/solution.py
@@ -30,15 +30,17 @@
 
 
 def ring_of(owners):
-    return list(range(0, owners, 2)) + list(range(owners - 1, 0, -2))
+    return [0] + list(range(1, owners, 2)) + list(range(owners - 2, 0, -2))
 
 
 def peer_at(distance, owners):
     me = lax.axis_index("dp")
     half_ring = owners // 2
-    place = jnp.where(lax.rem(me, 2) == 0, lax.div(me, 2), owners - 1 - lax.div(me, 2))
+    up = lax.rem(me, 2) == 1
+    place = jnp.where(up, lax.div(me, 2) + 1, lax.rem(owners - lax.div(me, 2), owners))
     at = lax.rem(place + owners + distance, owners)
-    return jnp.where(at < half_ring, 2 * at, 2 * (owners - 1 - at) + 1)
+    other = lax.rem(2 * (owners - at), 2 * owners)
+    return jnp.where((at > 0) & (at <= half_ring), 2 * at - 1, other)
 
 
 ROW_SHIFT = BLK_DEV * BW // 2

time: 56.2 us -> 56.1 us (level)
  transfers between devices with their start and end apart: 20 -> 20, of which waited for: 9 -> 8; matrix products, arithmetic and copies ran while one was open for 0% -> 0% of each run, Pallas kernels for 18% -> 18%
where the time goes in v23:
time: 56.1 us; the launch traced here: 56 us
  starting transfers between devices  25.9 us (46%)
  waiting for transfers between devices  17.5 us (31%)
  Pallas kernels  11.1 us (20%)
  between operations  0.78 us (1%)
  other arithmetic  0.61 us (1%)
    ppermute x17, starting transfers between devices, shift(): return lax.ppermute(x, 'dp', pairs)  24.3 us
    ppermute x17, waiting for transfers between devices, shift(): return lax.ppermute(x, 'dp', pairs)  16.3 us
    pallas_call x4, Pallas kernels, scores_of(): pl.pallas_call(functools.partial(scores_kernel, distances, split), out_sh...  3.71 us
    pallas_call x1, Pallas kernels, last_gradients(): pl.pallas_call(functools.partial(last_gradients_kernel, distances), out_s...  2.3 us
    pallas_call x2, Pallas kernels, gradients_of(): pl.pallas_call(functools.partial(gradients_kernel, distances), out_shape=...  2.2 us
    pallas_call x1, Pallas kernels, fetch(): pl.pallas_call(fetch_kernel, out_shape=pltpu.VMEM(x.shape, x.dtype), in_s...  1.6 us
    ppermute x1, starting transfers between devices, return_by(): return lax.ppermute(x, ('dp', 'width'), pairs)  1.55 us
    pallas_call x1, Pallas kernels, prepare(): pl.pallas_call(functools.partial(prepare_kernel, owners), out_shape=(piec...  1.2 us
  transfers between devices with their start and end apart: 20, of which 8 were waited for; matrix products, arithmetic and copies ran while one was open for 0% of the time, Pallas kernels for 18%

profile of v23, /device:TPU:0, one launch (start us, length us, event | category | flops | bytes accessed | tf_op | source)
XLA Modules:
  0.0 56.0 jit_solution(1018894769603025358)
XLA Ops:
  0.6 1.2 %prepare.1 = (bf16[1040,128]{1,0:T(8,128)(2,1)S(1)}, bf16[1024,128]{1,0:T(8,128)(2,1)S(1)}, bf16[1056,128]{1,0:T(8,128)(2,1)S(1)}, bf16[1056,128]{1,0:T(8,128)(2...) custom-call(s32[32]{0:T(128)} %refs_0_.1, s32[8,128]{1,0:T(8,128)} %bitcast.7, s32[32,128]{1,0:T(8,128)} %bitcast.5, ...), custom_call_target="tpu_custom_call" | custom-call | tf_op jit(solution)/shard_map/prepare/pallas_call | solution.py:126
  1.8 3.0 %collective-permute-start = (bf16[1040,128]{1,0:T(8,128)(2,1)S(1)}, bf16[1040,128]{1,0:T(8,128)(2,1)S(1)}, u32[]{:S(2)}, u32[]{:S(2)}) collective-permute-start(bf16[1040,128]{1,0:T(8,128)(2,1)S(1)} %get-tuple-element.30.refs_0_), channel_id=1, source_target_pairs={{0,2},{2,6},{6,10},{10,14},{14,12},{12,8},{8,4},{4,0},{1,3},{3,7},... | collective-permute-start | bytes 798728 | tf_op jit(solution)/shard_map/ppermute | solution.py:423
  4.8 0.2 collective-permute-start.1
  5.0 1.9 %collective-permute-start.3 = (bf16[1056,128]{1,0:T(8,128)(2,1)S(1)}, bf16[1056,128]{1,0:T(8,128)(2,1)S(1)}, u32[]{:S(2)}, u32[]{:S(2)}) collective-permute-start(bf16[1056,128]{1,0:T(8,128)(2,1)S(1)} %get-tuple-element.33), channel_id=1, source_target_pairs={{0,2},{2,6},{6,10},{10,14},{14,12},{12,8},{8,4},{4,0},{1,3},{3,7},... | collective-permute-start | bytes 811016 | tf_op jit(solution)/shard_map/ppermute | solution.py:423
  6.9 0.2 collective-permute-start.5
  7.0 1.6 %fetch.1.decoder = bf16[512,2048]{1,0:T(8,128)(2,1)S(1)} custom-call(bf16[512,2048]{1,0:T(8,128)(2,1)} %source.1), custom_call_target="tpu_custom_call" | custom-call | tf_op jit(solution)/shard_map/fetch/pallas_call | solution.py:160
  8.6 5.4 %collective-permute-done.1.refs_5_ = bf16[1024,128]{1,0:T(8,128)(2,1)S(1)} collective-permute-done((bf16[1024,128]{1,0:T(8,128)(2,1)S(1)}, bf16[1024,128]{1,0:T(8,128)(2,1)S(1)}, u32[]{:S(2)}, u32[]{:S(2)}) %collective-permute-start.1) | collective-permute-done | bytes 262176 | tf_op jit(solution)/shard_map/ppermute | solution.py:423
  14.1 0.0 collective-permute-done.refs_2_
  14.1 1.6 %collective-permute-start.2 = (bf16[1040,128]{1,0:T(8,128)(2,1)S(1)}, bf16[1040,128]{1,0:T(8,128)(2,1)S(1)}, u32[]{:S(2)}, u32[]{:S(2)}) collective-permute-start(bf16[1040,128]{1,0:T(8,128)(2,1)S(1)} %collective-permute-done.refs_2_), channel_id=1, source_target_pairs={{0,2},{2,6},{6,10},{10,14},{14,12},{12,8},{8,4},{4,0},{1,3},{3,7},... | collective-permute-start | bytes 798728 | tf_op jit(solution)/shard_map/ppermute | solution.py:423
  15.6 0.4 collective-permute-start.7
  16.1 1.8 %collective-permute-done.3.refs_3_ = bf16[1056,128]{1,0:T(8,128)(2,1)S(1)} collective-permute-done((bf16[1056,128]{1,0:T(8,128)(2,1)S(1)}, bf16[1056,128]{1,0:T(8,128)(2,1)S(1)}, u32[]{:S(2)}, u32[]{:S(2)}) %collective-permute-start.3) | collective-permute-done | bytes 270368 | tf_op jit(solution)/shard_map/ppermute | solution.py:423
  17.9 2.0 %collective-permute-start.4 = (bf16[1056,128]{1,0:T(8,128)(2,1)S(1)}, bf16[1056,128]{1,0:T(8,128)(2,1)S(1)}, u32[]{:S(2)}, u32[]{:S(2)}) collective-permute-start(bf16[1056,128]{1,0:T(8,128)(2,1)S(1)} %collective-permute-done.3.refs_3_), channel_id=1, source_target_pairs={{0,2},{2,6},{6,10},{10,14},{14,12},{12,8},{8,4},{4,0},{1,3},{3,7},... | collective-permute-start | bytes 811016 | tf_op jit(solution)/shard_map/ppermute | solution.py:423
  19.9 0.0 collective-permute-done.5.refs_4_
  19.9 0.1 collective-permute-start.6
  20.0 3.6 %collective-permute-done.2.refs_0_ = bf16[1040,128]{1,0:T(8,128)(2,1)S(1)} collective-permute-done((bf16[1040,128]{1,0:T(8,128)(2,1)S(1)}, bf16[1040,128]{1,0:T(8,128)(2,1)S(1)}, u32[]{:S(2)}, u32[]{:S(2)}) %collective-permute-start.2) | collective-permute-done | bytes 266272 | tf_op jit(solution)/shard_map/ppermute | solution.py:423
  23.6 2.0 %collective-permute-start.8 = (bf16[1040,128]{1,0:T(8,128)(2,1)S(1)}, bf16[1040,128]{1,0:T(8,128)(2,1)S(1)}, u32[]{:S(2)}, u32[]{:S(2)}) collective-permute-start(bf16[1040,128]{1,0:T(8,128)(2,1)S(1)} %collective-permute-done.2.refs_0_), channel_id=1, source_target_pairs={{0,2},{2,6},{6,10},{10,14},{14,12},{12,8},{8,4},{4,0},{1,3},{3,7},... | collective-permute-start | bytes 798728 | tf_op jit(solution)/shard_map/ppermute | solution.py:423
  25.6 0.0 collective-permute-done.7.refs_3_
  25.6 0.1 collective-permute-start.9
  25.7 1.4 %scores.4 = (f32[8,128]{1,0:T(8,128)S(1)}, f32[8,128]{1,0:T(8,128)S(1)}, f32[8,128]{1,0:T(8,128)S(1)}) custom-call(bf16[512,2048]{1,0:T(8,128)(2,1)S(1)} %fetch.1.decoder, f32[8,128]{1,0:T(8,128)S(1)} %get-tuple-element.29.own_facts, bf16[1040,128]{1,0:T(8,128)(2,1)S(1)} %get-tuple-element.30.refs_0_, bf16[1024,128]{1,0:T(8,128)(2,1)S(1)} %get-tuple-element.31.refs_1_, ...), custom_call_target="tpu_custom_call" | custom-call | tf_op jit(solution)/shard_map/scores/pallas_call | solution.py:280
  27.1 2.4 %collective-permute-done.4.onward = bf16[1056,128]{1,0:T(8,128)(2,1)S(1)} collective-permute-done((bf16[1056,128]{1,0:T(8,128)(2,1)S(1)}, bf16[1056,128]{1,0:T(8,128)(2,1)S(1)}, u32[]{:S(2)}, u32[]{:S(2)}) %collective-permute-start.4) | collective-permute-done | bytes 270368 | tf_op jit(solution)/shard_map/ppermute | solution.py:423
  29.4 1.8 %collective-permute-done.6.back = bf16[1056,128]{1,0:T(8,128)(2,1)S(1)} collective-permute-done((bf16[1056,128]{1,0:T(8,128)(2,1)S(1)}, bf16[1056,128]{1,0:T(8,128)(2,1)S(1)}, u32[]{:S(2)}, u32[]{:S(2)}) %collective-permute-start.6) | collective-permute-done | bytes 270368 | tf_op jit(solution)/shard_map/ppermute | solution.py:423
  31.3 0.1 stamp.1
  31.3 1.6 %collective-permute-start.11 = (bf16[1056,128]{1,0:T(8,128)(2,1)S(1)}, bf16[1056,128]{1,0:T(8,128)(2,1)S(1)}, u32[]{:S(2)}, u32[]{:S(2)}) collective-permute-start(bf16[1056,128]{1,0:T(8,128)(2,1)S(1)} %get-tuple-element.39.refs_1_), channel_id=1, source_target_pairs={{0,2},{2,6},{6,10},{10,14},{14,12},{12,8},{8,4},{4,0},{1,3},{3,7},... | collective-permute-start | bytes 811016 | tf_op jit(solution)/shard_map/ppermute | solution.py:423
  33.0 0.4 collective-permute-start.12
  33.4 0.8 %scores.5 = (f32[8,128]{1,0:T(8,128)S(1)}, f32[8,128]{1,0:T(8,128)S(1)}) custom-call(bf16[512,2048]{1,0:T(8,128)(2,1)S(1)} %fetch.1.decoder, f32[8,128]{1,0:T(8,128)S(1)} %get-tuple-element.29.own_facts, bf16[1040,128]{1,0:T(8,128)(2,1)S(1)} %collective-permute-done.2.refs_0_, bf16[1056,128]{1,0:T(8,128)(2,1)S(1)} %get-tuple-element.39.refs_1_, ...), custom_call_target="tpu_custom_call" | custom-call | tf_op jit(solution)/shard_map/scores/pallas_call | solution.py:280
  34.2 0.1 collective-permute-start.10
  34.3 1.3 %gradients.2.refs_4_ = f32[512,2048]{1,0:T(8,128)S(1)} custom-call(f32[8,128]{1,0:T(8,128)S(1)} %get-tuple-element.29.own_facts, bf16[1040,128]{1,0:T(8,128)(2,1)S(1)} %get-tuple-element.30.refs_0_, bf16[1024,128]{1,0:T(8,128)(2,1)S(1)} %get-tuple-element.31.refs_1_, bf16[1040,128]{1,0:T(8,128)(2,1)S(1)} %collective-permute-done.refs_2_, ...), custom_call_target="tpu_custom_call" | custom-call | tf_op jit(solution)/shard_map/gradients/pallas_call | solution.py:301
  35.6 0.9 %gradients.3.refs_6_ = f32[512,2048]{1,0:T(8,128)S(1)} custom-call(f32[8,128]{1,0:T(8,128)S(1)} %get-tuple-element.29.own_facts, bf16[1040,128]{1,0:T(8,128)(2,1)S(1)} %collective-permute-done.2.refs_0_, bf16[1056,128]{1,0:T(8,128)(2,1)S(1)} %get-tuple-element.39.refs_1_, ...), custom_call_target="tpu_custom_call", output_to_operand_aliasing={{}: (5, {})} | custom-call | tf_op jit(solution)/shard_map/gradients/pallas_call | solution.py:301
  36.5 0.0 collective-permute-done.10
  36.6 0.3 collective-permute-done.9.refs_3_
  36.9 0.0 collective-permute-done.8.refs_0_
  36.9 1.6 %collective-permute-start.13 = (bf16[1040,128]{1,0:T(8,128)(2,1)S(1)}, bf16[1040,128]{1,0:T(8,128)(2,1)S(1)}, u32[]{:S(2)}, u32[]{:S(2)}) collective-permute-start(bf16[1040,128]{1,0:T(8,128)(2,1)S(1)} %collective-permute-done.8.refs_0_), channel_id=1, source_target_pairs={{0,2},{2,6},{6,10},{10,14},{14,12},{12,8},{8,4},{4,0},{1,3},{3,7},... | collective-permute-start | bytes 798728 | tf_op jit(solution)/shard_map/ppermute | solution.py:423
  38.5 0.4 collective-permute-start.14
  38.9 1.5 %collective-permute-start.18 = (f32[32,128]{1,0:T(8,128)S(1)}, f32[32,128]{1,0:T(8,128)S(1)}, u32[]{:S(2)}, u32[]{:S(2)}) collective-permute-start(f32[32,128]{1,0:T(8,128)S(1)} %concatenate.3), channel_id=1, source_target_pairs={{0,8},{1,7},{2,4},{3,11},{6,0},{7,15},{10,2},{11,13},{14,6},{15,9}... | collective-permute-start | bytes 49160 | tf_op jit(solution)/shard_map/ppermute | solution.py:441
  40.5 0.0 collective-permute-done.11.refs_1_.onward
  40.5 0.9 %collective-permute-done.12.refs_2_.back = bf16[1056,128]{1,0:T(8,128)(2,1)S(1)} collective-permute-done((bf16[1056,128]{1,0:T(8,128)(2,1)S(1)}, bf16[1056,128]{1,0:T(8,128)(2,1)S(1)}, u32[]{:S(2)}, u32[]{:S(2)}) %collective-permute-start.12) | collective-permute-done | bytes 270368 | tf_op jit(solution)/shard_map/ppermute | solution.py:423
  41.3 0.8 %scores.6 = (f32[8,128]{1,0:T(8,128)S(1)}, f32[8,128]{1,0:T(8,128)S(1)}) custom-call(bf16[512,2048]{1,0:T(8,128)(2,1)S(1)} %fetch.1.decoder, f32[8,128]{1,0:T(8,128)S(1)} %get-tuple-element.29.own_facts, bf16[1040,128]{1,0:T(8,128)(2,1)S(1)} %collective-permute-done.8.refs_0_, bf16[1056,128]{1,0:T(8,128)(2,1)S(1)} %collective-permute-done.11.refs_1_.onward, ...), custom_call_target="tpu_custom_call" | custom-call | tf_op jit(solution)/shard_map/scores/pallas_call | solution.py:280
  42.2 3.7 %collective-permute-start.15 = (f32[8,128]{1,0:T(8,128)S(1)}, f32[8,128]{1,0:T(8,128)S(1)}, u32[]{:S(2)}, u32[]{:S(2)}) collective-permute-start(f32[8,128]{1,0:T(8,128)S(1)} %get-tuple-element.46), channel_id=1, source_target_pairs={{0,12},{2,8},{6,4},{10,0},{14,2},{12,6},{8,10},{4,14},{1,13},{3,9}... | collective-permute-start | bytes 12296 | tf_op jit(solution)/shard_map/ppermute | solution.py:423
  45.9 1.0 %collective-permute-start.16 = (f32[8,128]{1,0:T(8,128)S(1)}, f32[8,128]{1,0:T(8,128)S(1)}, u32[]{:S(2)}, u32[]{:S(2)}) collective-permute-start(f32[8,128]{1,0:T(8,128)S(1)} %get-tuple-element.47), channel_id=1, source_target_pairs={{0,10},{2,14},{6,12},{10,8},{14,4},{12,0},{8,2},{4,6},{1,11},{3,15... | collective-permute-start | bytes 12296 | tf_op jit(solution)/shard_map/ppermute | solution.py:423
  46.9 0.0 collective-permute-done.14.refs_5_.refs_1_
  46.9 0.0 collective-permute-done.13.refs_4_.refs_0_
  46.9 0.7 %scores.7 = f32[8,128]{1,0:T(8,128)S(1)} custom-call(bf16[512,2048]{1,0:T(8,128)(2,1)S(1)} %fetch.1.decoder, f32[8,128]{1,0:T(8,128)S(1)} %get-tuple-element.29.own_facts, bf16[1040,128]{1,0:T(8,128)(2,1)S(1)} %collective-permute-done.13.refs_4_.refs_0_, bf16[1024,128]{1,0:T(8,128)(2,1)S(1)} %collective-permute-done.14.refs_5_.refs_1_), custom_call_target="tpu_custom_call" | custom-call | tf_op jit(solution)/shard_map/scores/pallas_call | solution.py:280
  47.7 4.1 %collective-permute-start.17 = (f32[8,128]{1,0:T(8,128)S(1)}, f32[8,128]{1,0:T(8,128)S(1)}, u32[]{:S(2)}, u32[]{:S(2)}) collective-permute-start(f32[8,128]{1,0:T(8,128)S(1)} %scores.7), channel_id=1, source_target_pairs={{0,14},{2,12},{6,8},{10,4},{14,0},{12,2},{8,6},{4,10},{1,15},{3,13... | collective-permute-start | bytes 12296 | tf_op jit(solution)/shard_map/ppermute | solution.py:423
  51.7 0.0 collective-permute-done.15.ahead
  51.7 0.0 collective-permute-done.16.behind
  51.7 0.0 collective-permute-done.18
  51.7 2.3 %last_gradients.1 = bf16[512,2048]{1,0:T(8,128)(2,1)} custom-call(f32[8,128]{1,0:T(8,128)S(1)} %get-tuple-element.29.own_facts, bf16[1040,128]{1,0:T(8,128)(2,1)S(1)} %collective-permute-done.8.refs_0_, bf16[1056,128]{1,0:T(8,128)(2,1)S(1)} %collective-permute-done.11.refs_1_.onward, bf16[1056,128]{1,0:T(8,128)(2,1)S(1)} %collective-permute-done.12.refs_2_.back, ...), custom_call_target="tpu_custom_call" | custom-call | tf_op jit(solution)/shard_map/last_gradients/pallas_call | solution.py:331
  54.1 0.0 collective-permute-done.17.opposite
  54.1 0.1 unpack.1
  54.1 0.1 collective-permute-start.19
  54.2 1.2 %collective-permute-done.19 = f32[32,128]{1,0:T(8,128)S(1)} collective-permute-done((f32[32,128]{1,0:T(8,128)S(1)}, f32[32,128]{1,0:T(8,128)S(1)}, u32[]{:S(2)}, u32[]{:S(2)}) %collective-permute-start.19) | collective-permute-done | bytes 16416 | tf_op jit(solution)/shard_map/ppermute | solution.py:434
  55.4 0.6 %add_bitcast_fusion = f32[128,32]{0,1:T(8,128)} fusion(f32[32,128]{1,0:T(8,128)S(1)} %unpack.1, f32[32,128]{1,0:T(8,128)S(1)} %collective-permute-done.19), kind=kLoop, calls=%fused_computation | loop fusion | flops 4096 | bytes 49152 | tf_op jit(solution)/shard_map/transpose | solution.py:476
  (3 shorter events, 0.0 us)
Async XLA Ops:
  1.8 12.2 %collective-permute-start = (bf16[1040,128]{1,0:T(8,128)(2,1)S(1)}, bf16[1040,128]{1,0:T(8,128)(2,1)S(1)}, u32[]{:S(2)}, u32[]{:S(2)}) collective-permute-start(bf16[1040,128]{1,0:T(8,128)(2,1)S(1)} %get-tuple-element.30.refs_0_), channel_id=1, source_target_pairs={{0,2},{2,6},{6,10},{10,14},{14,12},{12,8},{8,4},{4,0},{1,3},{3,7},... | collective-permute-start | bytes 798728 | tf_op jit(solution)/shard_map/ppermute | solution.py:423
  4.8 9.2 %collective-permute-start.1 = (bf16[1024,128]{1,0:T(8,128)(2,1)S(1)}, bf16[1024,128]{1,0:T(8,128)(2,1)S(1)}, u32[]{:S(2)}, u32[]{:S(2)}) collective-permute-start(bf16[1024,128]{1,0:T(8,128)(2,1)S(1)} %get-tuple-element.31.refs_1_), channel_id=1, source_target_pairs={{0,4},{2,0},{6,2},{10,6},{14,10},{12,14},{8,12},{4,8},{1,5},{3,1},... | collective-permute-start | bytes 786440 | tf_op jit(solution)/shard_map/ppermute | solution.py:423
  5.0 12.9 %collective-permute-start.3 = (bf16[1056,128]{1,0:T(8,128)(2,1)S(1)}, bf16[1056,128]{1,0:T(8,128)(2,1)S(1)}, u32[]{:S(2)}, u32[]{:S(2)}) collective-permute-start(bf16[1056,128]{1,0:T(8,128)(2,1)S(1)} %get-tuple-element.33), channel_id=1, source_target_pairs={{0,2},{2,6},{6,10},{10,14},{14,12},{12,8},{8,4},{4,0},{1,3},{3,7},... | collective-permute-start | bytes 811016 | tf_op jit(solution)/shard_map/ppermute | solution.py:423
  6.9 13.1 %collective-permute-start.5 = (bf16[1056,128]{1,0:T(8,128)(2,1)S(1)}, bf16[1056,128]{1,0:T(8,128)(2,1)S(1)}, u32[]{:S(2)}, u32[]{:S(2)}) collective-permute-start(bf16[1056,128]{1,0:T(8,128)(2,1)S(1)} %get-tuple-element.34), channel_id=1, source_target_pairs={{0,4},{2,0},{6,2},{10,6},{14,10},{12,14},{8,12},{4,8},{1,5},{3,1},... | collective-permute-start | bytes 811016 | tf_op jit(solution)/shard_map/ppermute | solution.py:423
  14.1 9.6 %collective-permute-start.2 = (bf16[1040,128]{1,0:T(8,128)(2,1)S(1)}, bf16[1040,128]{1,0:T(8,128)(2,1)S(1)}, u32[]{:S(2)}, u32[]{:S(2)}) collective-permute-start(bf16[1040,128]{1,0:T(8,128)(2,1)S(1)} %collective-permute-done.refs_2_), channel_id=1, source_target_pairs={{0,2},{2,6},{6,10},{10,14},{14,12},{12,8},{8,4},{4,0},{1,3},{3,7},... | collective-permute-start | bytes 798728 | tf_op jit(solution)/shard_map/ppermute | solution.py:423
  15.6 10.0 %collective-permute-start.7 = (bf16[1024,128]{1,0:T(8,128)(2,1)S(1)}, bf16[1024,128]{1,0:T(8,128)(2,1)S(1)}, u32[]{:S(2)}, u32[]{:S(2)}) collective-permute-start(bf16[1024,128]{1,0:T(8,128)(2,1)S(1)} %collective-permute-done.1.refs_5_), channel_id=1, source_target_pairs={{0,4},{2,0},{6,2},{10,6},{14,10},{12,14},{8,12},{4,8},{1,5},{3,1},... | collective-permute-start | bytes 786440 | tf_op jit(solution)/shard_map/ppermute | solution.py:423
  17.9 11.5 %collective-permute-start.4 = (bf16[1056,128]{1,0:T(8,128)(2,1)S(1)}, bf16[1056,128]{1,0:T(8,128)(2,1)S(1)}, u32[]{:S(2)}, u32[]{:S(2)}) collective-permute-start(bf16[1056,128]{1,0:T(8,128)(2,1)S(1)} %collective-permute-done.3.refs_3_), channel_id=1, source_target_pairs={{0,2},{2,6},{6,10},{10,14},{14,12},{12,8},{8,4},{4,0},{1,3},{3,7},... | collective-permute-start | bytes 811016 | tf_op jit(solution)/shard_map/ppermute | solution.py:423
  19.9 11.4 %collective-permute-start.6 = (bf16[1056,128]{1,0:T(8,128)(2,1)S(1)}, bf16[1056,128]{1,0:T(8,128)(2,1)S(1)}, u32[]{:S(2)}, u32[]{:S(2)}) collective-permute-start(bf16[1056,128]{1,0:T(8,128)(2,1)S(1)} %collective-permute-done.5.refs_4_), channel_id=1, source_target_pairs={{0,4},{2,0},{6,2},{10,6},{14,10},{12,14},{8,12},{4,8},{1,5},{3,1},... | collective-permute-start | bytes 811016 | tf_op jit(solution)/shard_map/ppermute | solution.py:423
  23.6 13.2 %collective-permute-start.8 = (bf16[1040,128]{1,0:T(8,128)(2,1)S(1)}, bf16[1040,128]{1,0:T(8,128)(2,1)S(1)}, u32[]{:S(2)}, u32[]{:S(2)}) collective-permute-start(bf16[1040,128]{1,0:T(8,128)(2,1)S(1)} %collective-permute-done.2.refs_0_), channel_id=1, source_target_pairs={{0,2},{2,6},{6,10},{10,14},{14,12},{12,8},{8,4},{4,0},{1,3},{3,7},... | collective-permute-start | bytes 798728 | tf_op jit(solution)/shard_map/ppermute | solution.py:423
  25.6 11.3 %collective-permute-start.9 = (bf16[1024,128]{1,0:T(8,128)(2,1)S(1)}, bf16[1024,128]{1,0:T(8,128)(2,1)S(1)}, u32[]{:S(2)}, u32[]{:S(2)}) collective-permute-start(bf16[1024,128]{1,0:T(8,128)(2,1)S(1)} %collective-permute-done.7.refs_3_), channel_id=1, source_target_pairs={{0,4},{2,0},{6,2},{10,6},{14,10},{12,14},{8,12},{4,8},{1,5},{3,1},... | collective-permute-start | bytes 786440 | tf_op jit(solution)/shard_map/ppermute | solution.py:423
  31.3 9.1 %collective-permute-start.11 = (bf16[1056,128]{1,0:T(8,128)(2,1)S(1)}, bf16[1056,128]{1,0:T(8,128)(2,1)S(1)}, u32[]{:S(2)}, u32[]{:S(2)}) collective-permute-start(bf16[1056,128]{1,0:T(8,128)(2,1)S(1)} %get-tuple-element.39.refs_1_), channel_id=1, source_target_pairs={{0,2},{2,6},{6,10},{10,14},{14,12},{12,8},{8,4},{4,0},{1,3},{3,7},... | collective-permute-start | bytes 811016 | tf_op jit(solution)/shard_map/ppermute | solution.py:423
  33.0 8.4 %collective-permute-start.12 = (bf16[1056,128]{1,0:T(8,128)(2,1)S(1)}, bf16[1056,128]{1,0:T(8,128)(2,1)S(1)}, u32[]{:S(2)}, u32[]{:S(2)}) collective-permute-start(bf16[1056,128]{1,0:T(8,128)(2,1)S(1)} %get-tuple-element.40.refs_2_), channel_id=1, source_target_pairs={{0,4},{2,0},{6,2},{10,6},{14,10},{12,14},{8,12},{4,8},{1,5},{3,1},... | collective-permute-start | bytes 811016 | tf_op jit(solution)/shard_map/ppermute | solution.py:423
  34.2 2.3 %collective-permute-start.10 = (f32[8,128]{1,0:T(8,128)S(1)}, f32[8,128]{1,0:T(8,128)S(1)}, u32[]{:S(2)}, u32[]{:S(2)}) collective-permute-start(f32[8,128]{1,0:T(8,128)S(1)} %get-tuple-element.42), channel_id=1, source_target_pairs={{0,1},{1,0},{2,3},{3,2},{4,5},{5,4},{6,7},{7,6},{8,9},{9,8},{10,11... | collective-permute-start | bytes 12296 | tf_op jit(solution)/shard_map/ppermute | solution.py:434
  36.9 10.0 %collective-permute-start.13 = (bf16[1040,128]{1,0:T(8,128)(2,1)S(1)}, bf16[1040,128]{1,0:T(8,128)(2,1)S(1)}, u32[]{:S(2)}, u32[]{:S(2)}) collective-permute-start(bf16[1040,128]{1,0:T(8,128)(2,1)S(1)} %collective-permute-done.8.refs_0_), channel_id=1, source_target_pairs={{0,2},{2,6},{6,10},{10,14},{14,12},{12,8},{8,4},{4,0},{1,3},{3,7},... | collective-permute-start | bytes 798728 | tf_op jit(solution)/shard_map/ppermute | solution.py:423
  38.5 8.5 %collective-permute-start.14 = (bf16[1024,128]{1,0:T(8,128)(2,1)S(1)}, bf16[1024,128]{1,0:T(8,128)(2,1)S(1)}, u32[]{:S(2)}, u32[]{:S(2)}) collective-permute-start(bf16[1024,128]{1,0:T(8,128)(2,1)S(1)} %collective-permute-done.9.refs_3_), channel_id=1, source_target_pairs={{0,4},{2,0},{6,2},{10,6},{14,10},{12,14},{8,12},{4,8},{1,5},{3,1},... | collective-permute-start | bytes 786440 | tf_op jit(solution)/shard_map/ppermute | solution.py:423
  38.9 12.8 %collective-permute-start.18 = (f32[32,128]{1,0:T(8,128)S(1)}, f32[32,128]{1,0:T(8,128)S(1)}, u32[]{:S(2)}, u32[]{:S(2)}) collective-permute-start(f32[32,128]{1,0:T(8,128)S(1)} %concatenate.3), channel_id=1, source_target_pairs={{0,8},{1,7},{2,4},{3,11},{6,0},{7,15},{10,2},{11,13},{14,6},{15,9}... | collective-permute-start | bytes 49160 | tf_op jit(solution)/shard_map/ppermute | solution.py:441
  42.2 9.6 %collective-permute-start.15 = (f32[8,128]{1,0:T(8,128)S(1)}, f32[8,128]{1,0:T(8,128)S(1)}, u32[]{:S(2)}, u32[]{:S(2)}) collective-permute-start(f32[8,128]{1,0:T(8,128)S(1)} %get-tuple-element.46), channel_id=1, source_target_pairs={{0,12},{2,8},{6,4},{10,0},{14,2},{12,6},{8,10},{4,14},{1,13},{3,9}... | collective-permute-start | bytes 12296 | tf_op jit(solution)/shard_map/ppermute | solution.py:423
  45.9 5.8 %collective-permute-start.16 = (f32[8,128]{1,0:T(8,128)S(1)}, f32[8,128]{1,0:T(8,128)S(1)}, u32[]{:S(2)}, u32[]{:S(2)}) collective-permute-start(f32[8,128]{1,0:T(8,128)S(1)} %get-tuple-element.47), channel_id=1, source_target_pairs={{0,10},{2,14},{6,12},{10,8},{14,4},{12,0},{8,2},{4,6},{1,11},{3,15... | collective-permute-start | bytes 12296 | tf_op jit(solution)/shard_map/ppermute | solution.py:423
  47.7 6.4 %collective-permute-start.17 = (f32[8,128]{1,0:T(8,128)S(1)}, f32[8,128]{1,0:T(8,128)S(1)}, u32[]{:S(2)}, u32[]{:S(2)}) collective-permute-start(f32[8,128]{1,0:T(8,128)S(1)} %scores.7), channel_id=1, source_target_pairs={{0,14},{2,12},{6,8},{10,4},{14,0},{12,2},{8,6},{4,10},{1,15},{3,13... | collective-permute-start | bytes 12296 | tf_op jit(solution)/shard_map/ppermute | solution.py:423
  54.1 1.2 %collective-permute-start.19 = (f32[32,128]{1,0:T(8,128)S(1)}, f32[32,128]{1,0:T(8,128)S(1)}, u32[]{:S(2)}, u32[]{:S(2)}) collective-permute-start(f32[32,128]{1,0:T(8,128)S(1)} %unpack.1), channel_id=1, source_target_pairs={{0,1},{1,0},{2,3},{3,2},{4,5},{5,4},{6,7},{7,6},{8,9},{9,8},{10,11... | collective-permute-start | bytes 49160 | tf_op jit(solution)/shard_map/ppermute | solution.py:434

commit v24 on v14

--- a/solution.py
+++ b/solution.py
@@ -287,10 +287,11 @@
     )(*operands)
 
 
-def last_gradients_kernel(left, right, total, out, rounded, sems):
+def last_gradients_kernel(distances, own_facts, *refs):
+    pieces, (total, out, rounded, sems) = refs[:-4], refs[-4:]
     copies = []
-    facts = [facts_in(left, right, 4)]
-    for columns, part in gradient_blocks(facts, (left, right), out.shape[1]):
+    facts = facts_of(distances, own_facts, pieces)
+    for columns, part in gradient_blocks(facts, pieces, out.shape[1]):
         rounded[:, columns] = (total[:, columns] + part).astype(out.dtype)
         copies.append(
             pltpu.make_async_copy(
@@ -302,11 +303,13 @@
         copy.wait()
 
 
-def last_gradients(pair, total):
-    return pl.pallas_call(
-        last_gradients_kernel,
+def last_gradients(distances, pairs, own_facts, total):
+    operands = [kept(own_facts)] + [kept(piece) for pair in pairs for piece in pair]
+    operands.append(kept(total))
+    return pl.pallas_call(
+        functools.partial(last_gradients_kernel, distances),
         out_shape=jax.ShapeDtypeStruct(total.shape, jnp.bfloat16),
-        in_specs=[VMEM] * 3,
+        in_specs=[VMEM] * len(operands),
         out_specs=ANY,
         scratch_shapes=[
             pltpu.VMEM(total.shape, jnp.bfloat16),
@@ -314,7 +317,7 @@
         ],
         compiler_params=limit(16),
         name="last_gradients",
-    )(kept(pair[0]), kept(pair[1]), kept(total))
+    )(*operands)
 
 
 def stamp_kernel(onward, back, for_onward, for_back, onward_out, back_out, rows, sems):
@@ -358,7 +361,7 @@
     )(*[kept(piece) for piece in pieces], *[kept(value) for value in values])
 
 
-def unpack_kernel(owners, slots, own, onward, back, second, third, opposite, out):
+def unpack_kernel(owners, slots, own, onward, back, second, ahead, behind, opposite, out):
     owner = slots[...] // BLK_DEV
     start = onward.shape[0] - FACTS
     way = 1 - 2 * lax.axis_index("width")
@@ -366,7 +369,8 @@
     for distance, piece in ((-1, onward), (1, back)):
         rows = piece[start : start + 16, :].astype(jnp.float32)
         returned.append((distance, rows[:KPB] + rows[KPB : 2 * KPB]))
-    returned += [(2 * way, second[...]), (3 * way, third[...]), (4, opposite[...])]
+    returned += [(2 * way, second[...]), (3, ahead[...]), (-3, behind[...])]
+    returned.append((4, opposite[...]))
     mine = [owner == peer_at(distance, owners) for distance, _ in returned]
     for k in range(KPB):
         total = jnp.zeros(owner.shape, jnp.float32)
@@ -438,18 +442,14 @@
     second = return_by(2, jnp.concatenate([second, jnp.zeros((16, 128), jnp.float32)]))[:8]
     first_4 = hop(first_3)
     pairs = [(first_3[0], second_3[0]), (second_3[1], first_3[1])]
-    mine, others = scores_of((-3, 3), pairs, decoder, own_facts, True)
-    total = gradients_of((-3, 3), pairs, own_facts, decoder.shape, total)
-    third = mine + other_core(others)
-    total, third = lax.optimization_barrier((total, third))
-    third = return_by(3, third)
-    total, first_4 = lax.optimization_barrier((total, first_4))
+    onward, back = scores_of((-3, 3), pairs, decoder, own_facts)
+    ahead, behind = shift(onward, -3), shift(back, 3)
     (opposite,) = scores_of((4,), [first_4], decoder, own_facts)
     opposite = shift(opposite, -owners // 2)
-    total, third = lax.optimization_barrier((total, third))
-    decoder_grad = last_gradients(first_4, total)
+    total, ahead, behind = lax.optimization_barrier((total, ahead, behind))
+    decoder_grad = last_gradients((-3, 3, 4), pairs + [first_4], own_facts, total)
     decoder_grad, opposite = lax.optimization_barrier((decoder_grad, opposite))
-    act_grad = unpack(slots, own, *second_3, second, third, opposite)
+    act_grad = unpack(slots, own, *second_3, second, ahead, behind, opposite)
     act_grad = act_grad + other_core(act_grad)
     return (decoder_grad, act_grad.T)
 

time: 56.2 us -> 58.6 us (1.043)
  waiting for transfers between devices: 18.9 us -> 22.7 us
  starting transfers between devices: 24.2 us -> 23.3 us
    ppermute x15 -> x17, waiting for transfers between devices: 17.6 us -> 21.5 us  [shift(): return lax.ppermute(x, 'dp', pairs)]
    ppermute x2 -> x1, starting transfers between devices: 4.89 us -> 1.37 us  [return_by(): return lax.ppermute(x, ('dp', 'width'), pairs)]
    ppermute x15 -> x17, starting transfers between devices: 19 us -> 21.8 us  [shift(): return lax.ppermute(x, 'dp', pairs)]
    pallas_call x3 -> x2, Pallas kernels: 3.09 us -> 2.2 us  [gradients_of(): pl.pallas_call(functools.partial(gradients_kernel, distances), out_shape=...]
    ppermute x3 -> x2, waiting for transfers between devices: 1.33 us -> 1.17 us  [other_core(): return lax.ppermute(x, 'width', ((0, 1), (1, 0)))]
  transfers between devices with their start and end apart: 20 -> 20, of which waited for: 11 -> 11; matrix products, arithmetic and copies ran while one was open for 0% -> 0% of each run, Pallas kernels for 18% -> 17%
where the time goes in v24:
time: 58.6 us; the launch traced here: 58.5 us
  starting transfers between devices  23.3 us (40%)
  waiting for transfers between devices  22.7 us (39%)
  Pallas kernels  11.1 us (19%)
  between operations  0.79 us (1%)
  other arithmetic  0.61 us (1%)
    ppermute x17, starting transfers between devices, shift(): return lax.ppermute(x, 'dp', pairs)  21.8 us
    ppermute x17, waiting for transfers between devices, shift(): return lax.ppermute(x, 'dp', pairs)  21.5 us
    pallas_call x4, Pallas kernels, scores_of(): pl.pallas_call(functools.partial(scores_kernel, distances, split), out_sh...  3.71 us
    pallas_call x1, Pallas kernels, last_gradients(): pl.pallas_call(functools.partial(last_gradients_kernel, distances), out_s...  2.28 us
    pallas_call x2, Pallas kernels, gradients_of(): pl.pallas_call(functools.partial(gradients_kernel, distances), out_shape=...  2.2 us
    pallas_call x1, Pallas kernels, fetch(): pl.pallas_call(fetch_kernel, out_shape=pltpu.VMEM(x.shape, x.dtype), in_s...  1.6 us
    ppermute x1, starting transfers between devices, return_by(): return lax.ppermute(x, ('dp', 'width'), pairs)  1.37 us
    pallas_call x1, Pallas kernels, prepare(): pl.pallas_call(functools.partial(prepare_kernel, owners), out_shape=out_s...  1.2 us
  transfers between devices with their start and end apart: 20, of which 11 were waited for; matrix products, arithmetic and copies ran while one was open for 0% of the time, Pallas kernels for 17%

profile of v24, /device:TPU:0, one launch (start us, length us, event | category | flops | bytes accessed | tf_op | source)
XLA Modules:
  0.0 58.5 jit_solution(3311920744250774388)
XLA Ops:
  0.6 1.2 %prepare.1 = (bf16[1040,128]{1,0:T(8,128)(2,1)S(1)}, bf16[1040,128]{1,0:T(8,128)(2,1)S(1)}, bf16[1040,128]{1,0:T(8,128)(2,1)S(1)}, bf16[1040,128]{1,0:T(8,128)(2...) custom-call(s32[32]{0:T(128)} %refs_0_.1, s32[8,128]{1,0:T(8,128)} %bitcast.7, s32[32,128]{1,0:T(8,128)} %bitcast.5, ...), custom_call_target="tpu_custom_call" | custom-call | tf_op jit(solution)/shard_map/prepare/pallas_call | solution.py:117
  1.8 3.1 %collective-permute-start = (bf16[1040,128]{1,0:T(8,128)(2,1)S(1)}, bf16[1040,128]{1,0:T(8,128)(2,1)S(1)}, u32[]{:S(2)}, u32[]{:S(2)}) collective-permute-start(bf16[1040,128]{1,0:T(8,128)(2,1)S(1)} %get-tuple-element.30.refs_0_), channel_id=1, source_target_pairs={{0,4},{4,8},{8,12},{12,14},{14,10},{10,6},{6,2},{2,0},{1,5},{5,9},... | collective-permute-start | bytes 798728 | tf_op jit(solution)/shard_map/ppermute | solution.py:401
  4.9 0.0 collective-permute-start.1
  4.9 2.0 %collective-permute-start.3 = (bf16[1040,128]{1,0:T(8,128)(2,1)S(1)}, bf16[1040,128]{1,0:T(8,128)(2,1)S(1)}, u32[]{:S(2)}, u32[]{:S(2)}) collective-permute-start(bf16[1040,128]{1,0:T(8,128)(2,1)S(1)} %get-tuple-element.33), channel_id=1, source_target_pairs={{0,4},{4,8},{8,12},{12,14},{14,10},{10,6},{6,2},{2,0},{1,5},{5,9},... | collective-permute-start | bytes 798728 | tf_op jit(solution)/shard_map/ppermute | solution.py:401
  6.9 0.0 collective-permute-start.5
  6.9 1.6 %fetch.1.decoder = bf16[512,2048]{1,0:T(8,128)(2,1)S(1)} custom-call(bf16[512,2048]{1,0:T(8,128)(2,1)} %source.1), custom_call_target="tpu_custom_call" | custom-call | tf_op jit(solution)/shard_map/fetch/pallas_call | solution.py:144
  8.6 3.5 %collective-permute-done.refs_2_ = bf16[1040,128]{1,0:T(8,128)(2,1)S(1)} collective-permute-done((bf16[1040,128]{1,0:T(8,128)(2,1)S(1)}, bf16[1040,128]{1,0:T(8,128)(2,1)S(1)}, u32[]{:S(2)}, u32[]{:S(2)}) %collective-permute-start) | collective-permute-done | bytes 266272 | tf_op jit(solution)/shard_map/ppermute | solution.py:401
  12.1 2.2 %collective-permute-done.1.refs_5_ = bf16[1040,128]{1,0:T(8,128)(2,1)S(1)} collective-permute-done((bf16[1040,128]{1,0:T(8,128)(2,1)S(1)}, bf16[1040,128]{1,0:T(8,128)(2,1)S(1)}, u32[]{:S(2)}, u32[]{:S(2)}) %collective-permute-start.1) | collective-permute-done | bytes 266272 | tf_op jit(solution)/shard_map/ppermute | solution.py:401
  14.2 1.6 %collective-permute-start.2 = (bf16[1040,128]{1,0:T(8,128)(2,1)S(1)}, bf16[1040,128]{1,0:T(8,128)(2,1)S(1)}, u32[]{:S(2)}, u32[]{:S(2)}) collective-permute-start(bf16[1040,128]{1,0:T(8,128)(2,1)S(1)} %collective-permute-done.refs_2_), channel_id=1, source_target_pairs={{0,4},{4,8},{8,12},{12,14},{14,10},{10,6},{6,2},{2,0},{1,5},{5,9},... | collective-permute-start | bytes 798728 | tf_op jit(solution)/shard_map/ppermute | solution.py:401
  15.8 0.4 collective-permute-start.7
  16.3 1.5 %collective-permute-done.3.refs_3_ = bf16[1040,128]{1,0:T(8,128)(2,1)S(1)} collective-permute-done((bf16[1040,128]{1,0:T(8,128)(2,1)S(1)}, bf16[1040,128]{1,0:T(8,128)(2,1)S(1)}, u32[]{:S(2)}, u32[]{:S(2)}) %collective-permute-start.3) | collective-permute-done | bytes 266272 | tf_op jit(solution)/shard_map/ppermute | solution.py:401
  17.8 2.1 %collective-permute-start.4 = (bf16[1040,128]{1,0:T(8,128)(2,1)S(1)}, bf16[1040,128]{1,0:T(8,128)(2,1)S(1)}, u32[]{:S(2)}, u32[]{:S(2)}) collective-permute-start(bf16[1040,128]{1,0:T(8,128)(2,1)S(1)} %collective-permute-done.3.refs_3_), channel_id=1, source_target_pairs={{0,4},{4,8},{8,12},{12,14},{14,10},{10,6},{6,2},{2,0},{1,5},{5,9},... | collective-permute-start | bytes 798728 | tf_op jit(solution)/shard_map/ppermute | solution.py:401
  19.9 0.0 collective-permute-done.5.refs_4_
  19.9 0.0 collective-permute-start.6
  19.9 3.6 %collective-permute-done.2.refs_0_ = bf16[1040,128]{1,0:T(8,128)(2,1)S(1)} collective-permute-done((bf16[1040,128]{1,0:T(8,128)(2,1)S(1)}, bf16[1040,128]{1,0:T(8,128)(2,1)S(1)}, u32[]{:S(2)}, u32[]{:S(2)}) %collective-permute-start.2) | collective-permute-done | bytes 266272 | tf_op jit(solution)/shard_map/ppermute | solution.py:401
  23.6 2.0 %collective-permute-start.8 = (bf16[1040,128]{1,0:T(8,128)(2,1)S(1)}, bf16[1040,128]{1,0:T(8,128)(2,1)S(1)}, u32[]{:S(2)}, u32[]{:S(2)}) collective-permute-start(bf16[1040,128]{1,0:T(8,128)(2,1)S(1)} %collective-permute-done.2.refs_0_), channel_id=1, source_target_pairs={{0,4},{4,8},{8,12},{12,14},{14,10},{10,6},{6,2},{2,0},{1,5},{5,9},... | collective-permute-start | bytes 798728 | tf_op jit(solution)/shard_map/ppermute | solution.py:401
  25.6 0.0 collective-permute-done.7.refs_3_
  25.6 0.0 collective-permute-start.9
  25.6 1.3 %scores.4 = (f32[8,128]{1,0:T(8,128)S(1)}, f32[8,128]{1,0:T(8,128)S(1)}, f32[8,128]{1,0:T(8,128)S(1)}) custom-call(bf16[512,2048]{1,0:T(8,128)(2,1)S(1)} %fetch.1.decoder, f32[8,128]{1,0:T(8,128)S(1)} %get-tuple-element.29.own_facts, bf16[1040,128]{1,0:T(8,128)(2,1)S(1)} %get-tuple-element.30.refs_0_, bf16[1040,128]{1,0:T(8,128)(2,1)S(1)} %get-tuple-element.31.refs_1_, ...), custom_call_target="tpu_custom_call" | custom-call | tf_op jit(solution)/shard_map/scores/pallas_call | solution.py:258
  27.0 2.3 %collective-permute-done.4.onward = bf16[1040,128]{1,0:T(8,128)(2,1)S(1)} collective-permute-done((bf16[1040,128]{1,0:T(8,128)(2,1)S(1)}, bf16[1040,128]{1,0:T(8,128)(2,1)S(1)}, u32[]{:S(2)}, u32[]{:S(2)}) %collective-permute-start.4) | collective-permute-done | bytes 266272 | tf_op jit(solution)/shard_map/ppermute | solution.py:401
  29.3 2.1 %collective-permute-done.6.back = bf16[1040,128]{1,0:T(8,128)(2,1)S(1)} collective-permute-done((bf16[1040,128]{1,0:T(8,128)(2,1)S(1)}, bf16[1040,128]{1,0:T(8,128)(2,1)S(1)}, u32[]{:S(2)}, u32[]{:S(2)}) %collective-permute-start.6) | collective-permute-done | bytes 266272 | tf_op jit(solution)/shard_map/ppermute | solution.py:401
  31.4 0.1 stamp.1
  31.4 0.8 %scores.5 = (f32[8,128]{1,0:T(8,128)S(1)}, f32[8,128]{1,0:T(8,128)S(1)}) custom-call(bf16[512,2048]{1,0:T(8,128)(2,1)S(1)} %fetch.1.decoder, f32[8,128]{1,0:T(8,128)S(1)} %get-tuple-element.29.own_facts, bf16[1040,128]{1,0:T(8,128)(2,1)S(1)} %collective-permute-done.2.refs_0_, bf16[1040,128]{1,0:T(8,128)(2,1)S(1)} %get-tuple-element.39.refs_1_, ...), custom_call_target="tpu_custom_call" | custom-call | tf_op jit(solution)/shard_map/scores/pallas_call | solution.py:258
  32.3 0.1 collective-permute-start.10
  32.3 1.3 %gradients.2.refs_4_ = f32[512,2048]{1,0:T(8,128)S(1)} custom-call(f32[8,128]{1,0:T(8,128)S(1)} %get-tuple-element.29.own_facts, bf16[1040,128]{1,0:T(8,128)(2,1)S(1)} %get-tuple-element.30.refs_0_, bf16[1040,128]{1,0:T(8,128)(2,1)S(1)} %get-tuple-element.31.refs_1_, bf16[1040,128]{1,0:T(8,128)(2,1)S(1)} %collective-permute-done.refs_2_, ...), custom_call_target="tpu_custom_call" | custom-call | tf_op jit(solution)/shard_map/gradients/pallas_call | solution.py:279
  33.6 1.6 %collective-permute-start.11 = (bf16[1040,128]{1,0:T(8,128)(2,1)S(1)}, bf16[1040,128]{1,0:T(8,128)(2,1)S(1)}, u32[]{:S(2)}, u32[]{:S(2)}) collective-permute-start(bf16[1040,128]{1,0:T(8,128)(2,1)S(1)} %get-tuple-element.39.refs_1_), channel_id=1, source_target_pairs={{0,4},{4,8},{8,12},{12,14},{14,10},{10,6},{6,2},{2,0},{1,5},{5,9},... | collective-permute-start | bytes 798728 | tf_op jit(solution)/shard_map/ppermute | solution.py:401
  35.2 0.4 collective-permute-start.12
  35.7 0.9 %gradients.3.refs_6_ = f32[512,2048]{1,0:T(8,128)S(1)} custom-call(f32[8,128]{1,0:T(8,128)S(1)} %get-tuple-element.29.own_facts, bf16[1040,128]{1,0:T(8,128)(2,1)S(1)} %collective-permute-done.2.refs_0_, bf16[1040,128]{1,0:T(8,128)(2,1)S(1)} %get-tuple-element.39.refs_1_, ...), custom_call_target="tpu_custom_call", output_to_operand_aliasing={{}: (5, {})} | custom-call | tf_op jit(solution)/shard_map/gradients/pallas_call | solution.py:279
  36.6 0.0 collective-permute-done.10
  36.7 0.0 collective-permute-done.8.refs_0_
  36.7 0.0 collective-permute-done.9.refs_3_
  36.7 1.6 %collective-permute-start.13 = (bf16[1040,128]{1,0:T(8,128)(2,1)S(1)}, bf16[1040,128]{1,0:T(8,128)(2,1)S(1)}, u32[]{:S(2)}, u32[]{:S(2)}) collective-permute-start(bf16[1040,128]{1,0:T(8,128)(2,1)S(1)} %collective-permute-done.8.refs_0_), channel_id=1, source_target_pairs={{0,4},{4,8},{8,12},{12,14},{14,10},{10,6},{6,2},{2,0},{1,5},{5,9},... | collective-permute-start | bytes 798728 | tf_op jit(solution)/shard_map/ppermute | solution.py:401
  38.3 0.5 collective-permute-start.14
  38.8 1.4 %collective-permute-start.18 = (f32[24,128]{1,0:T(8,128)S(1)}, f32[24,128]{1,0:T(8,128)S(1)}, u32[]{:S(2)}, u32[]{:S(2)}) collective-permute-start(f32[24,128]{1,0:T(8,128)S(1)} %concatenate.3), channel_id=1, source_target_pairs={{0,6},{1,9},{4,2},{5,13},{8,0},{9,15},{12,4},{13,11},{14,8},{15,7}... | collective-permute-start | bytes 36872 | tf_op jit(solution)/shard_map/ppermute | solution.py:419
  40.1 2.7 %collective-permute-done.11.refs_1_.onward = bf16[1040,128]{1,0:T(8,128)(2,1)S(1)} collective-permute-done((bf16[1040,128]{1,0:T(8,128)(2,1)S(1)}, bf16[1040,128]{1,0:T(8,128)(2,1)S(1)}, u32[]{:S(2)}, u32[]{:S(2)}) %collective-permute-start.11) | collective-permute-done | bytes 266272 | tf_op jit(solution)/shard_map/ppermute | solution.py:401
  42.8 1.6 %collective-permute-done.12.refs_2_.back = bf16[1040,128]{1,0:T(8,128)(2,1)S(1)} collective-permute-done((bf16[1040,128]{1,0:T(8,128)(2,1)S(1)}, bf16[1040,128]{1,0:T(8,128)(2,1)S(1)}, u32[]{:S(2)}, u32[]{:S(2)}) %collective-permute-start.12) | collective-permute-done | bytes 266272 | tf_op jit(solution)/shard_map/ppermute | solution.py:401
  44.5 0.8 %scores.6 = (f32[8,128]{1,0:T(8,128)S(1)}, f32[8,128]{1,0:T(8,128)S(1)}) custom-call(bf16[512,2048]{1,0:T(8,128)(2,1)S(1)} %fetch.1.decoder, f32[8,128]{1,0:T(8,128)S(1)} %get-tuple-element.29.own_facts, bf16[1040,128]{1,0:T(8,128)(2,1)S(1)} %collective-permute-done.8.refs_0_, bf16[1040,128]{1,0:T(8,128)(2,1)S(1)} %collective-permute-done.11.refs_1_.onward, ...), custom_call_target="tpu_custom_call" | custom-call | tf_op jit(solution)/shard_map/scores/pallas_call | solution.py:258
  45.3 1.3 %collective-permute-start.15 = (f32[8,128]{1,0:T(8,128)S(1)}, f32[8,128]{1,0:T(8,128)S(1)}, u32[]{:S(2)}, u32[]{:S(2)}) collective-permute-start(f32[8,128]{1,0:T(8,128)S(1)} %get-tuple-element.46), channel_id=1, source_target_pairs={{0,10},{4,6},{8,2},{12,0},{14,4},{10,8},{6,12},{2,14},{1,11},{5,7}... | collective-permute-start | bytes 12296 | tf_op jit(solution)/shard_map/ppermute | solution.py:401
  46.6 2.6 %collective-permute-start.16 = (f32[8,128]{1,0:T(8,128)S(1)}, f32[8,128]{1,0:T(8,128)S(1)}, u32[]{:S(2)}, u32[]{:S(2)}) collective-permute-start(f32[8,128]{1,0:T(8,128)S(1)} %get-tuple-element.47), channel_id=1, source_target_pairs={{0,12},{4,14},{8,10},{12,6},{14,2},{10,0},{6,4},{2,8},{1,13},{5,15... | collective-permute-start | bytes 12296 | tf_op jit(solution)/shard_map/ppermute | solution.py:401
  49.2 0.0 collective-permute-done.13.refs_4_.refs_0_
  49.2 0.3 collective-permute-done.14.refs_5_.refs_1_
  49.5 0.7 %scores.7 = f32[8,128]{1,0:T(8,128)S(1)} custom-call(bf16[512,2048]{1,0:T(8,128)(2,1)S(1)} %fetch.1.decoder, f32[8,128]{1,0:T(8,128)S(1)} %get-tuple-element.29.own_facts, bf16[1040,128]{1,0:T(8,128)(2,1)S(1)} %collective-permute-done.13.refs_4_.refs_0_, bf16[1040,128]{1,0:T(8,128)(2,1)S(1)} %collective-permute-done.14.refs_5_.refs_1_), custom_call_target="tpu_custom_call" | custom-call | tf_op jit(solution)/shard_map/scores/pallas_call | solution.py:258
  50.2 2.4 %collective-permute-start.17 = (f32[8,128]{1,0:T(8,128)S(1)}, f32[8,128]{1,0:T(8,128)S(1)}, u32[]{:S(2)}, u32[]{:S(2)}) collective-permute-start(f32[8,128]{1,0:T(8,128)S(1)} %scores.7), channel_id=1, source_target_pairs={{0,14},{4,10},{8,6},{12,2},{14,0},{10,4},{6,8},{2,12},{1,15},{5,11... | collective-permute-start | bytes 12296 | tf_op jit(solution)/shard_map/ppermute | solution.py:401
  52.6 0.0 collective-permute-done.15.ahead
  52.6 0.0 collective-permute-done.16.behind
  52.6 0.0 collective-permute-done.18
  52.6 2.3 %last_gradients.1 = bf16[512,2048]{1,0:T(8,128)(2,1)} custom-call(f32[8,128]{1,0:T(8,128)S(1)} %get-tuple-element.29.own_facts, bf16[1040,128]{1,0:T(8,128)(2,1)S(1)} %collective-permute-done.8.refs_0_, bf16[1040,128]{1,0:T(8,128)(2,1)S(1)} %collective-permute-done.11.refs_1_.onward, bf16[1040,128]{1,0:T(8,128)(2,1)S(1)} %collective-permute-done.12.refs_2_.back, ...), custom_call_target="tpu_custom_call" | custom-call | tf_op jit(solution)/shard_map/last_gradients/pallas_call | solution.py:309
  54.9 1.6 %collective-permute-done.17.opposite = f32[8,128]{1,0:T(8,128)S(1)} collective-permute-done((f32[8,128]{1,0:T(8,128)S(1)}, f32[8,128]{1,0:T(8,128)S(1)}, u32[]{:S(2)}, u32[]{:S(2)}) %collective-permute-start.17) | collective-permute-done | bytes 4128 | tf_op jit(solution)/shard_map/ppermute | solution.py:401
  56.6 0.1 collective-permute-start.19
  56.7 1.2 %collective-permute-done.19 = f32[32,128]{1,0:T(8,128)S(1)} collective-permute-done((f32[32,128]{1,0:T(8,128)S(1)}, f32[32,128]{1,0:T(8,128)S(1)}, u32[]{:S(2)}, u32[]{:S(2)}) %collective-permute-start.19) | collective-permute-done | bytes 16416 | tf_op jit(solution)/shard_map/ppermute | solution.py:412
  57.8 0.6 %add_bitcast_fusion = f32[128,32]{0,1:T(8,128)} fusion(f32[32,128]{1,0:T(8,128)S(1)} %unpack.1, f32[32,128]{1,0:T(8,128)S(1)} %collective-permute-done.19), kind=kLoop, calls=%fused_computation | loop fusion | flops 4096 | bytes 49152 | tf_op jit(solution)/shard_map/transpose | solution.py:454
  (4 shorter events, 0.0 us)
Async XLA Ops:
  1.8 10.2 %collective-permute-start = (bf16[1040,128]{1,0:T(8,128)(2,1)S(1)}, bf16[1040,128]{1,0:T(8,128)(2,1)S(1)}, u32[]{:S(2)}, u32[]{:S(2)}) collective-permute-start(bf16[1040,128]{1,0:T(8,128)(2,1)S(1)} %get-tuple-element.30.refs_0_), channel_id=1, source_target_pairs={{0,4},{4,8},{8,12},{12,14},{14,10},{10,6},{6,2},{2,0},{1,5},{5,9},... | collective-permute-start | bytes 798728 | tf_op jit(solution)/shard_map/ppermute | solution.py:401
  4.9 9.3 %collective-permute-start.1 = (bf16[1040,128]{1,0:T(8,128)(2,1)S(1)}, bf16[1040,128]{1,0:T(8,128)(2,1)S(1)}, u32[]{:S(2)}, u32[]{:S(2)}) collective-permute-start(bf16[1040,128]{1,0:T(8,128)(2,1)S(1)} %get-tuple-element.31.refs_1_), channel_id=1, source_target_pairs={{0,2},{4,0},{8,4},{12,8},{14,12},{10,14},{6,10},{2,6},{1,3},{5,1},... | collective-permute-start | bytes 798728 | tf_op jit(solution)/shard_map/ppermute | solution.py:401
  4.9 12.8 %collective-permute-start.3 = (bf16[1040,128]{1,0:T(8,128)(2,1)S(1)}, bf16[1040,128]{1,0:T(8,128)(2,1)S(1)}, u32[]{:S(2)}, u32[]{:S(2)}) collective-permute-start(bf16[1040,128]{1,0:T(8,128)(2,1)S(1)} %get-tuple-element.33), channel_id=1, source_target_pairs={{0,4},{4,8},{8,12},{12,14},{14,10},{10,6},{6,2},{2,0},{1,5},{5,9},... | collective-permute-start | bytes 798728 | tf_op jit(solution)/shard_map/ppermute | solution.py:401
  6.9 13.0 %collective-permute-start.5 = (bf16[1040,128]{1,0:T(8,128)(2,1)S(1)}, bf16[1040,128]{1,0:T(8,128)(2,1)S(1)}, u32[]{:S(2)}, u32[]{:S(2)}) collective-permute-start(bf16[1040,128]{1,0:T(8,128)(2,1)S(1)} %get-tuple-element.34), channel_id=1, source_target_pairs={{0,2},{4,0},{8,4},{12,8},{14,12},{10,14},{6,10},{2,6},{1,3},{5,1},... | collective-permute-start | bytes 798728 | tf_op jit(solution)/shard_map/ppermute | solution.py:401
  14.2 9.3 %collective-permute-start.2 = (bf16[1040,128]{1,0:T(8,128)(2,1)S(1)}, bf16[1040,128]{1,0:T(8,128)(2,1)S(1)}, u32[]{:S(2)}, u32[]{:S(2)}) collective-permute-start(bf16[1040,128]{1,0:T(8,128)(2,1)S(1)} %collective-permute-done.refs_2_), channel_id=1, source_target_pairs={{0,4},{4,8},{8,12},{12,14},{14,10},{10,6},{6,2},{2,0},{1,5},{5,9},... | collective-permute-start | bytes 798728 | tf_op jit(solution)/shard_map/ppermute | solution.py:401
  15.8 9.8 %collective-permute-start.7 = (bf16[1040,128]{1,0:T(8,128)(2,1)S(1)}, bf16[1040,128]{1,0:T(8,128)(2,1)S(1)}, u32[]{:S(2)}, u32[]{:S(2)}) collective-permute-start(bf16[1040,128]{1,0:T(8,128)(2,1)S(1)} %collective-permute-done.1.refs_5_), channel_id=1, source_target_pairs={{0,2},{4,0},{8,4},{12,8},{14,12},{10,14},{6,10},{2,6},{1,3},{5,1},... | collective-permute-start | bytes 798728 | tf_op jit(solution)/shard_map/ppermute | solution.py:401
  17.8 11.5 %collective-permute-start.4 = (bf16[1040,128]{1,0:T(8,128)(2,1)S(1)}, bf16[1040,128]{1,0:T(8,128)(2,1)S(1)}, u32[]{:S(2)}, u32[]{:S(2)}) collective-permute-start(bf16[1040,128]{1,0:T(8,128)(2,1)S(1)} %collective-permute-done.3.refs_3_), channel_id=1, source_target_pairs={{0,4},{4,8},{8,12},{12,14},{14,10},{10,6},{6,2},{2,0},{1,5},{5,9},... | collective-permute-start | bytes 798728 | tf_op jit(solution)/shard_map/ppermute | solution.py:401
  19.9 11.4 %collective-permute-start.6 = (bf16[1040,128]{1,0:T(8,128)(2,1)S(1)}, bf16[1040,128]{1,0:T(8,128)(2,1)S(1)}, u32[]{:S(2)}, u32[]{:S(2)}) collective-permute-start(bf16[1040,128]{1,0:T(8,128)(2,1)S(1)} %collective-permute-done.5.refs_4_), channel_id=1, source_target_pairs={{0,2},{4,0},{8,4},{12,8},{14,12},{10,14},{6,10},{2,6},{1,3},{5,1},... | collective-permute-start | bytes 798728 | tf_op jit(solution)/shard_map/ppermute | solution.py:401
  23.6 13.1 %collective-permute-start.8 = (bf16[1040,128]{1,0:T(8,128)(2,1)S(1)}, bf16[1040,128]{1,0:T(8,128)(2,1)S(1)}, u32[]{:S(2)}, u32[]{:S(2)}) collective-permute-start(bf16[1040,128]{1,0:T(8,128)(2,1)S(1)} %collective-permute-done.2.refs_0_), channel_id=1, source_target_pairs={{0,4},{4,8},{8,12},{12,14},{14,10},{10,6},{6,2},{2,0},{1,5},{5,9},... | collective-permute-start | bytes 798728 | tf_op jit(solution)/shard_map/ppermute | solution.py:401
  25.6 11.0 %collective-permute-start.9 = (bf16[1040,128]{1,0:T(8,128)(2,1)S(1)}, bf16[1040,128]{1,0:T(8,128)(2,1)S(1)}, u32[]{:S(2)}, u32[]{:S(2)}) collective-permute-start(bf16[1040,128]{1,0:T(8,128)(2,1)S(1)} %collective-permute-done.7.refs_3_), channel_id=1, source_target_pairs={{0,2},{4,0},{8,4},{12,8},{14,12},{10,14},{6,10},{2,6},{1,3},{5,1},... | collective-permute-start | bytes 798728 | tf_op jit(solution)/shard_map/ppermute | solution.py:401
  32.3 4.4 %collective-permute-start.10 = (f32[8,128]{1,0:T(8,128)S(1)}, f32[8,128]{1,0:T(8,128)S(1)}, u32[]{:S(2)}, u32[]{:S(2)}) collective-permute-start(f32[8,128]{1,0:T(8,128)S(1)} %get-tuple-element.42), channel_id=1, source_target_pairs={{0,1},{1,0},{2,3},{3,2},{4,5},{5,4},{6,7},{7,6},{8,9},{9,8},{10,11... | collective-permute-start | bytes 12296 | tf_op jit(solution)/shard_map/ppermute | solution.py:412
  33.6 9.2 %collective-permute-start.11 = (bf16[1040,128]{1,0:T(8,128)(2,1)S(1)}, bf16[1040,128]{1,0:T(8,128)(2,1)S(1)}, u32[]{:S(2)}, u32[]{:S(2)}) collective-permute-start(bf16[1040,128]{1,0:T(8,128)(2,1)S(1)} %get-tuple-element.39.refs_1_), channel_id=1, source_target_pairs={{0,4},{4,8},{8,12},{12,14},{14,10},{10,6},{6,2},{2,0},{1,5},{5,9},... | collective-permute-start | bytes 798728 | tf_op jit(solution)/shard_map/ppermute | solution.py:401
  35.2 9.2 %collective-permute-start.12 = (bf16[1040,128]{1,0:T(8,128)(2,1)S(1)}, bf16[1040,128]{1,0:T(8,128)(2,1)S(1)}, u32[]{:S(2)}, u32[]{:S(2)}) collective-permute-start(bf16[1040,128]{1,0:T(8,128)(2,1)S(1)} %get-tuple-element.40.refs_2_), channel_id=1, source_target_pairs={{0,2},{4,0},{8,4},{12,8},{14,12},{10,14},{6,10},{2,6},{1,3},{5,1},... | collective-permute-start | bytes 798728 | tf_op jit(solution)/shard_map/ppermute | solution.py:401
  36.7 12.5 %collective-permute-start.13 = (bf16[1040,128]{1,0:T(8,128)(2,1)S(1)}, bf16[1040,128]{1,0:T(8,128)(2,1)S(1)}, u32[]{:S(2)}, u32[]{:S(2)}) collective-permute-start(bf16[1040,128]{1,0:T(8,128)(2,1)S(1)} %collective-permute-done.8.refs_0_), channel_id=1, source_target_pairs={{0,4},{4,8},{8,12},{12,14},{14,10},{10,6},{6,2},{2,0},{1,5},{5,9},... | collective-permute-start | bytes 798728 | tf_op jit(solution)/shard_map/ppermute | solution.py:401
  38.3 11.2 %collective-permute-start.14 = (bf16[1040,128]{1,0:T(8,128)(2,1)S(1)}, bf16[1040,128]{1,0:T(8,128)(2,1)S(1)}, u32[]{:S(2)}, u32[]{:S(2)}) collective-permute-start(bf16[1040,128]{1,0:T(8,128)(2,1)S(1)} %collective-permute-done.9.refs_3_), channel_id=1, source_target_pairs={{0,2},{4,0},{8,4},{12,8},{14,12},{10,14},{6,10},{2,6},{1,3},{5,1},... | collective-permute-start | bytes 798728 | tf_op jit(solution)/shard_map/ppermute | solution.py:401
  38.8 13.9 %collective-permute-start.18 = (f32[24,128]{1,0:T(8,128)S(1)}, f32[24,128]{1,0:T(8,128)S(1)}, u32[]{:S(2)}, u32[]{:S(2)}) collective-permute-start(f32[24,128]{1,0:T(8,128)S(1)} %concatenate.3), channel_id=1, source_target_pairs={{0,6},{1,9},{4,2},{5,13},{8,0},{9,15},{12,4},{13,11},{14,8},{15,7}... | collective-permute-start | bytes 36872 | tf_op jit(solution)/shard_map/ppermute | solution.py:419
  45.3 7.3 %collective-permute-start.15 = (f32[8,128]{1,0:T(8,128)S(1)}, f32[8,128]{1,0:T(8,128)S(1)}, u32[]{:S(2)}, u32[]{:S(2)}) collective-permute-start(f32[8,128]{1,0:T(8,128)S(1)} %get-tuple-element.46), channel_id=1, source_target_pairs={{0,10},{4,6},{8,2},{12,0},{14,4},{10,8},{6,12},{2,14},{1,11},{5,7}... | collective-permute-start | bytes 12296 | tf_op jit(solution)/shard_map/ppermute | solution.py:401
  46.6 6.0 %collective-permute-start.16 = (f32[8,128]{1,0:T(8,128)S(1)}, f32[8,128]{1,0:T(8,128)S(1)}, u32[]{:S(2)}, u32[]{:S(2)}) collective-permute-start(f32[8,128]{1,0:T(8,128)S(1)} %get-tuple-element.47), channel_id=1, source_target_pairs={{0,12},{4,14},{8,10},{12,6},{14,2},{10,0},{6,4},{2,8},{1,13},{5,15... | collective-permute-start | bytes 12296 | tf_op jit(solution)/shard_map/ppermute | solution.py:401
  50.2 6.4 %collective-permute-start.17 = (f32[8,128]{1,0:T(8,128)S(1)}, f32[8,128]{1,0:T(8,128)S(1)}, u32[]{:S(2)}, u32[]{:S(2)}) collective-permute-start(f32[8,128]{1,0:T(8,128)S(1)} %scores.7), channel_id=1, source_target_pairs={{0,14},{4,10},{8,6},{12,2},{14,0},{10,4},{6,8},{2,12},{1,15},{5,11... | collective-permute-start | bytes 12296 | tf_op jit(solution)/shard_map/ppermute | solution.py:401
  56.6 1.2 %collective-permute-start.19 = (f32[32,128]{1,0:T(8,128)S(1)}, f32[32,128]{1,0:T(8,128)S(1)}, u32[]{:S(2)}, u32[]{:S(2)}) collective-permute-start(f32[32,128]{1,0:T(8,128)S(1)} %unpack.1), channel_id=1, source_target_pairs={{0,1},{1,0},{2,3},{3,2},{4,5},{5,4},{6,7},{7,6},{8,9},{9,8},{10,11... | collective-permute-start | bytes 49160 | tf_op jit(solution)/shard_map/ppermute | solution.py:412

commit v25 on v18

--- a/solution.py
+++ b/solution.py
@@ -452,6 +452,7 @@
     own, onward, back = scores_of(distances, pairs, decoder, own_facts)
     total = gradients_of(distances, pairs, own_facts, decoder.shape)
     first_3 = hop(first_2)
+    total, second_2 = lax.optimization_barrier((total, second_2))
     second_2 = stamp(second_2, (back, onward))
     second_3 = crossed(second_2)
     pairs = [(first_2[0], second_2[0]), (second_2[1], first_2[1])]

time: 56.2 us -> 56.6 us (level)
  waiting for transfers between devices: 18 us -> 19.4 us
  starting transfers between devices: 25.5 us -> 24.5 us
    ppermute x17, waiting for transfers between devices: 16.8 us -> 18.1 us  [shift(): return lax.ppermute(x, 'dp', pairs)]
    ppermute x17, starting transfers between devices: 24 us -> 22.9 us  [shift(): return lax.ppermute(x, 'dp', pairs)]
  transfers between devices with their start and end apart: 20 -> 20, of which waited for: 9 -> 11; matrix products, arithmetic and copies ran while one was open for 0% -> 0% of each run, Pallas kernels for 18% -> 18%
where the time goes in v25:
time: 56.6 us; the launch traced here: 56.4 us
  starting transfers between devices  24.5 us (43%)
  waiting for transfers between devices  19.4 us (34%)
  Pallas kernels  11.1 us (20%)
  between operations  0.76 us (1%)
  other arithmetic  0.61 us (1%)
    ppermute x17, starting transfers between devices, shift(): return lax.ppermute(x, 'dp', pairs)  22.9 us
    ppermute x17, waiting for transfers between devices, shift(): return lax.ppermute(x, 'dp', pairs)  18.1 us
    pallas_call x4, Pallas kernels, scores_of(): pl.pallas_call(functools.partial(scores_kernel, distances, split), out_sh...  3.71 us
    pallas_call x1, Pallas kernels, last_gradients(): pl.pallas_call(functools.partial(last_gradients_kernel, distances), out_s...  2.29 us
    pallas_call x2, Pallas kernels, gradients_of(): pl.pallas_call(functools.partial(gradients_kernel, distances), out_shape=...  2.21 us
    pallas_call x1, Pallas kernels, fetch(): pl.pallas_call(fetch_kernel, out_shape=pltpu.VMEM(x.shape, x.dtype), in_s...  1.6 us
    ppermute x1, starting transfers between devices, return_by(): return lax.ppermute(x, ('dp', 'width'), pairs)  1.38 us
    ppermute x2, waiting for transfers between devices, other_core(): return lax.ppermute(x, 'width', ((0, 1), (1, 0)))  1.37 us
  transfers between devices with their start and end apart: 20, of which 11 were waited for; matrix products, arithmetic and copies ran while one was open for 0% of the time, Pallas kernels for 18%

profile of v25, /device:TPU:0, one launch (start us, length us, event | category | flops | bytes accessed | tf_op | source)
XLA Modules:
  0.0 56.4 jit_solution(10395753103662356183)
XLA Ops:
  0.6 1.2 %prepare.1 = (bf16[1040,128]{1,0:T(8,128)(2,1)S(1)}, bf16[1024,128]{1,0:T(8,128)(2,1)S(1)}, bf16[1056,128]{1,0:T(8,128)(2,1)S(1)}, bf16[1056,128]{1,0:T(8,128)(2...) custom-call(s32[32]{0:T(128)} %refs_0_.1, s32[8,128]{1,0:T(8,128)} %bitcast.7, s32[32,128]{1,0:T(8,128)} %bitcast.5, ...), custom_call_target="tpu_custom_call" | custom-call | tf_op jit(solution)/shard_map/prepare/pallas_call | solution.py:124
  1.8 3.1 %collective-permute-start = (bf16[1040,128]{1,0:T(8,128)(2,1)S(1)}, bf16[1040,128]{1,0:T(8,128)(2,1)S(1)}, u32[]{:S(2)}, u32[]{:S(2)}) collective-permute-start(bf16[1040,128]{1,0:T(8,128)(2,1)S(1)} %get-tuple-element.33.refs_0_), channel_id=1, source_target_pairs={{0,4},{4,8},{8,12},{12,14},{14,10},{10,6},{6,2},{2,0},{1,5},{5,9},... | collective-permute-start | bytes 798728 | tf_op jit(solution)/shard_map/ppermute | solution.py:421
  4.9 0.0 collective-permute-start.1
  4.9 2.0 %collective-permute-start.3 = (bf16[1056,128]{1,0:T(8,128)(2,1)S(1)}, bf16[1056,128]{1,0:T(8,128)(2,1)S(1)}, u32[]{:S(2)}, u32[]{:S(2)}) collective-permute-start(bf16[1056,128]{1,0:T(8,128)(2,1)S(1)} %get-tuple-element.36), channel_id=1, source_target_pairs={{0,4},{4,8},{8,12},{12,14},{14,10},{10,6},{6,2},{2,0},{1,5},{5,9},... | collective-permute-start | bytes 811016 | tf_op jit(solution)/shard_map/ppermute | solution.py:421
  6.9 0.0 collective-permute-start.4
  6.9 1.6 %fetch.1.decoder = bf16[512,2048]{1,0:T(8,128)(2,1)S(1)} custom-call(bf16[512,2048]{1,0:T(8,128)(2,1)} %source.1), custom_call_target="tpu_custom_call" | custom-call | tf_op jit(solution)/shard_map/fetch/pallas_call | solution.py:158
  8.6 5.6 %collective-permute-done.1.refs_5_ = bf16[1024,128]{1,0:T(8,128)(2,1)S(1)} collective-permute-done((bf16[1024,128]{1,0:T(8,128)(2,1)S(1)}, bf16[1024,128]{1,0:T(8,128)(2,1)S(1)}, u32[]{:S(2)}, u32[]{:S(2)}) %collective-permute-start.1) | collective-permute-done | bytes 262176 | tf_op jit(solution)/shard_map/ppermute | solution.py:421
  14.1 0.0 collective-permute-done.refs_2_
  14.2 1.6 %collective-permute-start.2 = (bf16[1040,128]{1,0:T(8,128)(2,1)S(1)}, bf16[1040,128]{1,0:T(8,128)(2,1)S(1)}, u32[]{:S(2)}, u32[]{:S(2)}) collective-permute-start(bf16[1040,128]{1,0:T(8,128)(2,1)S(1)} %collective-permute-done.refs_2_), channel_id=1, source_target_pairs={{0,4},{4,8},{8,12},{12,14},{14,10},{10,6},{6,2},{2,0},{1,5},{5,9},... | collective-permute-start | bytes 798728 | tf_op jit(solution)/shard_map/ppermute | solution.py:421
  15.7 0.4 collective-permute-start.7
  16.2 1.7 %collective-permute-done.3.refs_3_ = bf16[1056,128]{1,0:T(8,128)(2,1)S(1)} collective-permute-done((bf16[1056,128]{1,0:T(8,128)(2,1)S(1)}, bf16[1056,128]{1,0:T(8,128)(2,1)S(1)}, u32[]{:S(2)}, u32[]{:S(2)}) %collective-permute-start.3) | collective-permute-done | bytes 270368 | tf_op jit(solution)/shard_map/ppermute | solution.py:421
  17.8 2.1 %collective-permute-start.5 = (bf16[1056,128]{1,0:T(8,128)(2,1)S(1)}, bf16[1056,128]{1,0:T(8,128)(2,1)S(1)}, u32[]{:S(2)}, u32[]{:S(2)}) collective-permute-start(bf16[1056,128]{1,0:T(8,128)(2,1)S(1)} %collective-permute-done.3.refs_3_), channel_id=1, source_target_pairs={{0,4},{4,8},{8,12},{12,14},{14,10},{10,6},{6,2},{2,0},{1,5},{5,9},... | collective-permute-start | bytes 811016 | tf_op jit(solution)/shard_map/ppermute | solution.py:421
  20.0 0.0 collective-permute-done.4.refs_4_
  20.0 0.0 collective-permute-start.6
  20.0 3.6 %collective-permute-done.2.refs_0_ = bf16[1040,128]{1,0:T(8,128)(2,1)S(1)} collective-permute-done((bf16[1040,128]{1,0:T(8,128)(2,1)S(1)}, bf16[1040,128]{1,0:T(8,128)(2,1)S(1)}, u32[]{:S(2)}, u32[]{:S(2)}) %collective-permute-start.2) | collective-permute-done | bytes 266272 | tf_op jit(solution)/shard_map/ppermute | solution.py:421
  23.6 2.1 %collective-permute-start.8 = (bf16[1040,128]{1,0:T(8,128)(2,1)S(1)}, bf16[1040,128]{1,0:T(8,128)(2,1)S(1)}, u32[]{:S(2)}, u32[]{:S(2)}) collective-permute-start(bf16[1040,128]{1,0:T(8,128)(2,1)S(1)} %collective-permute-done.2.refs_0_), channel_id=1, source_target_pairs={{0,4},{4,8},{8,12},{12,14},{14,10},{10,6},{6,2},{2,0},{1,5},{5,9},... | collective-permute-start | bytes 798728 | tf_op jit(solution)/shard_map/ppermute | solution.py:421
  25.7 0.0 collective-permute-done.7.refs_3_
  25.7 0.0 collective-permute-start.9
  25.7 1.3 %gradients.2.refs_4_ = f32[512,2048]{1,0:T(8,128)S(1)} custom-call(f32[8,128]{1,0:T(8,128)S(1)} %get-tuple-element.32.own_facts, bf16[1040,128]{1,0:T(8,128)(2,1)S(1)} %get-tuple-element.33.refs_0_, bf16[1024,128]{1,0:T(8,128)(2,1)S(1)} %get-tuple-element.34.refs_1_, bf16[1040,128]{1,0:T(8,128)(2,1)S(1)} %collective-permute-done.refs_2_, ...), custom_call_target="tpu_custom_call" | custom-call | tf_op jit(solution)/shard_map/gradients/pallas_call | solution.py:299
  27.0 1.4 %scores.4 = (f32[8,128]{1,0:T(8,128)S(1)}, f32[8,128]{1,0:T(8,128)S(1)}, f32[8,128]{1,0:T(8,128)S(1)}) custom-call(bf16[512,2048]{1,0:T(8,128)(2,1)S(1)} %fetch.1.decoder, f32[8,128]{1,0:T(8,128)S(1)} %get-tuple-element.32.own_facts, bf16[1040,128]{1,0:T(8,128)(2,1)S(1)} %get-tuple-element.33.refs_0_, bf16[1024,128]{1,0:T(8,128)(2,1)S(1)} %get-tuple-element.34.refs_1_, ...), custom_call_target="tpu_custom_call" | custom-call | tf_op jit(solution)/shard_map/scores/pallas_call | solution.py:278
  28.3 1.0 %collective-permute-done.5.onward = bf16[1056,128]{1,0:T(8,128)(2,1)S(1)} collective-permute-done((bf16[1056,128]{1,0:T(8,128)(2,1)S(1)}, bf16[1056,128]{1,0:T(8,128)(2,1)S(1)}, u32[]{:S(2)}, u32[]{:S(2)}) %collective-permute-start.5) | collective-permute-done | bytes 270368 | tf_op jit(solution)/shard_map/ppermute | solution.py:421
  29.3 2.0 %collective-permute-done.6.back = bf16[1056,128]{1,0:T(8,128)(2,1)S(1)} collective-permute-done((bf16[1056,128]{1,0:T(8,128)(2,1)S(1)}, bf16[1056,128]{1,0:T(8,128)(2,1)S(1)}, u32[]{:S(2)}, u32[]{:S(2)}) %collective-permute-start.6) | collective-permute-done | bytes 270368 | tf_op jit(solution)/shard_map/ppermute | solution.py:421
  31.4 0.1 stamp.1
  31.4 1.6 %collective-permute-start.11 = (bf16[1056,128]{1,0:T(8,128)(2,1)S(1)}, bf16[1056,128]{1,0:T(8,128)(2,1)S(1)}, u32[]{:S(2)}, u32[]{:S(2)}) collective-permute-start(bf16[1056,128]{1,0:T(8,128)(2,1)S(1)} %get-tuple-element.44.refs_1_), channel_id=1, source_target_pairs={{0,4},{4,8},{8,12},{12,14},{14,10},{10,6},{6,2},{2,0},{1,5},{5,9},... | collective-permute-start | bytes 811016 | tf_op jit(solution)/shard_map/ppermute | solution.py:421
  33.1 0.4 collective-permute-start.12
  33.5 0.8 %scores.5 = (f32[8,128]{1,0:T(8,128)S(1)}, f32[8,128]{1,0:T(8,128)S(1)}) custom-call(bf16[512,2048]{1,0:T(8,128)(2,1)S(1)} %fetch.1.decoder, f32[8,128]{1,0:T(8,128)S(1)} %get-tuple-element.32.own_facts, bf16[1040,128]{1,0:T(8,128)(2,1)S(1)} %collective-permute-done.2.refs_0_, bf16[1056,128]{1,0:T(8,128)(2,1)S(1)} %get-tuple-element.44.refs_1_, ...), custom_call_target="tpu_custom_call" | custom-call | tf_op jit(solution)/shard_map/scores/pallas_call | solution.py:278
  34.3 0.1 collective-permute-start.10
  34.4 0.9 %gradients.3.refs_6_ = f32[512,2048]{1,0:T(8,128)S(1)} custom-call(f32[8,128]{1,0:T(8,128)S(1)} %get-tuple-element.32.own_facts, bf16[1040,128]{1,0:T(8,128)(2,1)S(1)} %collective-permute-done.2.refs_0_, bf16[1056,128]{1,0:T(8,128)(2,1)S(1)} %get-tuple-element.44.refs_1_, ...), custom_call_target="tpu_custom_call", output_to_operand_aliasing={{}: (5, {})} | custom-call | tf_op jit(solution)/shard_map/gradients/pallas_call | solution.py:299
  35.4 0.2 collective-permute-done.10
  35.6 1.4 %collective-permute-done.9.refs_3_ = bf16[1024,128]{1,0:T(8,128)(2,1)S(1)} collective-permute-done((bf16[1024,128]{1,0:T(8,128)(2,1)S(1)}, bf16[1024,128]{1,0:T(8,128)(2,1)S(1)}, u32[]{:S(2)}, u32[]{:S(2)}) %collective-permute-start.9) | collective-permute-done | bytes 262176 | tf_op jit(solution)/shard_map/ppermute | solution.py:421
  37.0 0.0 collective-permute-done.8.refs_0_
  37.0 1.6 %collective-permute-start.13 = (bf16[1040,128]{1,0:T(8,128)(2,1)S(1)}, bf16[1040,128]{1,0:T(8,128)(2,1)S(1)}, u32[]{:S(2)}, u32[]{:S(2)}) collective-permute-start(bf16[1040,128]{1,0:T(8,128)(2,1)S(1)} %collective-permute-done.8.refs_0_), channel_id=1, source_target_pairs={{0,4},{4,8},{8,12},{12,14},{14,10},{10,6},{6,2},{2,0},{1,5},{5,9},... | collective-permute-start | bytes 798728 | tf_op jit(solution)/shard_map/ppermute | solution.py:421
  38.6 0.4 collective-permute-start.14
  39.0 1.4 %collective-permute-start.18 = (f32[32,128]{1,0:T(8,128)S(1)}, f32[32,128]{1,0:T(8,128)S(1)}, u32[]{:S(2)}, u32[]{:S(2)}) collective-permute-start(f32[32,128]{1,0:T(8,128)S(1)} %concatenate.3), channel_id=1, source_target_pairs={{0,6},{1,9},{4,2},{5,13},{8,0},{9,15},{12,4},{13,11},{14,8},{15,7}... | collective-permute-start | bytes 49160 | tf_op jit(solution)/shard_map/ppermute | solution.py:439
  40.4 0.5 collective-permute-done.11.refs_1_.onward
  40.8 1.8 %collective-permute-done.12.refs_2_.back = bf16[1056,128]{1,0:T(8,128)(2,1)S(1)} collective-permute-done((bf16[1056,128]{1,0:T(8,128)(2,1)S(1)}, bf16[1056,128]{1,0:T(8,128)(2,1)S(1)}, u32[]{:S(2)}, u32[]{:S(2)}) %collective-permute-start.12) | collective-permute-done | bytes 270368 | tf_op jit(solution)/shard_map/ppermute | solution.py:421
  42.7 0.8 %scores.6 = (f32[8,128]{1,0:T(8,128)S(1)}, f32[8,128]{1,0:T(8,128)S(1)}) custom-call(bf16[512,2048]{1,0:T(8,128)(2,1)S(1)} %fetch.1.decoder, f32[8,128]{1,0:T(8,128)S(1)} %get-tuple-element.32.own_facts, bf16[1040,128]{1,0:T(8,128)(2,1)S(1)} %collective-permute-done.8.refs_0_, bf16[1056,128]{1,0:T(8,128)(2,1)S(1)} %collective-permute-done.11.refs_1_.onward, ...), custom_call_target="tpu_custom_call" | custom-call | tf_op jit(solution)/shard_map/scores/pallas_call | solution.py:278
  43.5 2.5 %collective-permute-start.15 = (f32[8,128]{1,0:T(8,128)S(1)}, f32[8,128]{1,0:T(8,128)S(1)}, u32[]{:S(2)}, u32[]{:S(2)}) collective-permute-start(f32[8,128]{1,0:T(8,128)S(1)} %get-tuple-element.52), channel_id=1, source_target_pairs={{0,10},{4,6},{8,2},{12,0},{14,4},{10,8},{6,12},{2,14},{1,11},{5,7}... | collective-permute-start | bytes 12296 | tf_op jit(solution)/shard_map/ppermute | solution.py:421
  46.0 1.4 %collective-permute-start.16 = (f32[8,128]{1,0:T(8,128)S(1)}, f32[8,128]{1,0:T(8,128)S(1)}, u32[]{:S(2)}, u32[]{:S(2)}) collective-permute-start(f32[8,128]{1,0:T(8,128)S(1)} %get-tuple-element.53), channel_id=1, source_target_pairs={{0,12},{4,14},{8,10},{12,6},{14,2},{10,0},{6,4},{2,8},{1,13},{5,15... | collective-permute-start | bytes 12296 | tf_op jit(solution)/shard_map/ppermute | solution.py:421
  47.4 0.0 collective-permute-done.14.refs_5_.refs_1_
  47.4 0.0 collective-permute-done.13.refs_4_.refs_0_
  47.4 0.7 %scores.7 = f32[8,128]{1,0:T(8,128)S(1)} custom-call(bf16[512,2048]{1,0:T(8,128)(2,1)S(1)} %fetch.1.decoder, f32[8,128]{1,0:T(8,128)S(1)} %get-tuple-element.32.own_facts, bf16[1040,128]{1,0:T(8,128)(2,1)S(1)} %collective-permute-done.13.refs_4_.refs_0_, bf16[1024,128]{1,0:T(8,128)(2,1)S(1)} %collective-permute-done.14.refs_5_.refs_1_), custom_call_target="tpu_custom_call" | custom-call | tf_op jit(solution)/shard_map/scores/pallas_call | solution.py:278
  48.1 3.5 %collective-permute-start.17 = (f32[8,128]{1,0:T(8,128)S(1)}, f32[8,128]{1,0:T(8,128)S(1)}, u32[]{:S(2)}, u32[]{:S(2)}) collective-permute-start(f32[8,128]{1,0:T(8,128)S(1)} %scores.7), channel_id=1, source_target_pairs={{0,14},{4,10},{8,6},{12,2},{14,0},{10,4},{6,8},{2,12},{1,15},{5,11... | collective-permute-start | bytes 12296 | tf_op jit(solution)/shard_map/ppermute | solution.py:421
  51.7 0.0 collective-permute-done.15.ahead
  51.7 0.0 collective-permute-done.16.behind
  51.7 0.0 collective-permute-done.18
  51.7 2.3 %last_gradients.1 = bf16[512,2048]{1,0:T(8,128)(2,1)} custom-call(f32[8,128]{1,0:T(8,128)S(1)} %get-tuple-element.32.own_facts, bf16[1040,128]{1,0:T(8,128)(2,1)S(1)} %collective-permute-done.8.refs_0_, bf16[1056,128]{1,0:T(8,128)(2,1)S(1)} %collective-permute-done.11.refs_1_.onward, bf16[1056,128]{1,0:T(8,128)(2,1)S(1)} %collective-permute-done.12.refs_2_.back, ...), custom_call_target="tpu_custom_call" | custom-call | tf_op jit(solution)/shard_map/last_gradients/pallas_call | solution.py:329
  54.0 0.5 collective-permute-done.17.opposite
  54.5 0.1 collective-permute-start.19
  54.6 1.2 %collective-permute-done.19 = f32[32,128]{1,0:T(8,128)S(1)} collective-permute-done((f32[32,128]{1,0:T(8,128)S(1)}, f32[32,128]{1,0:T(8,128)S(1)}, u32[]{:S(2)}, u32[]{:S(2)}) %collective-permute-start.19) | collective-permute-done | bytes 16416 | tf_op jit(solution)/shard_map/ppermute | solution.py:432
  55.8 0.6 %add_bitcast_fusion = f32[128,32]{0,1:T(8,128)} fusion(f32[32,128]{1,0:T(8,128)S(1)} %unpack.1, f32[32,128]{1,0:T(8,128)S(1)} %collective-permute-done.19), kind=kLoop, calls=%fused_computation | loop fusion | flops 4096 | bytes 49152 | tf_op jit(solution)/shard_map/transpose | solution.py:475
  (4 shorter events, 0.0 us)
Async XLA Ops:
  1.8 12.3 %collective-permute-start = (bf16[1040,128]{1,0:T(8,128)(2,1)S(1)}, bf16[1040,128]{1,0:T(8,128)(2,1)S(1)}, u32[]{:S(2)}, u32[]{:S(2)}) collective-permute-start(bf16[1040,128]{1,0:T(8,128)(2,1)S(1)} %get-tuple-element.33.refs_0_), channel_id=1, source_target_pairs={{0,4},{4,8},{8,12},{12,14},{14,10},{10,6},{6,2},{2,0},{1,5},{5,9},... | collective-permute-start | bytes 798728 | tf_op jit(solution)/shard_map/ppermute | solution.py:421
  4.9 9.2 %collective-permute-start.1 = (bf16[1024,128]{1,0:T(8,128)(2,1)S(1)}, bf16[1024,128]{1,0:T(8,128)(2,1)S(1)}, u32[]{:S(2)}, u32[]{:S(2)}) collective-permute-start(bf16[1024,128]{1,0:T(8,128)(2,1)S(1)} %get-tuple-element.34.refs_1_), channel_id=1, source_target_pairs={{0,2},{4,0},{8,4},{12,8},{14,12},{10,14},{6,10},{2,6},{1,3},{5,1},... | collective-permute-start | bytes 786440 | tf_op jit(solution)/shard_map/ppermute | solution.py:421
  4.9 12.9 %collective-permute-start.3 = (bf16[1056,128]{1,0:T(8,128)(2,1)S(1)}, bf16[1056,128]{1,0:T(8,128)(2,1)S(1)}, u32[]{:S(2)}, u32[]{:S(2)}) collective-permute-start(bf16[1056,128]{1,0:T(8,128)(2,1)S(1)} %get-tuple-element.36), channel_id=1, source_target_pairs={{0,4},{4,8},{8,12},{12,14},{14,10},{10,6},{6,2},{2,0},{1,5},{5,9},... | collective-permute-start | bytes 811016 | tf_op jit(solution)/shard_map/ppermute | solution.py:421
  6.9 13.1 %collective-permute-start.4 = (bf16[1056,128]{1,0:T(8,128)(2,1)S(1)}, bf16[1056,128]{1,0:T(8,128)(2,1)S(1)}, u32[]{:S(2)}, u32[]{:S(2)}) collective-permute-start(bf16[1056,128]{1,0:T(8,128)(2,1)S(1)} %get-tuple-element.37), channel_id=1, source_target_pairs={{0,2},{4,0},{8,4},{12,8},{14,12},{10,14},{6,10},{2,6},{1,3},{5,1},... | collective-permute-start | bytes 811016 | tf_op jit(solution)/shard_map/ppermute | solution.py:421
  14.2 9.4 %collective-permute-start.2 = (bf16[1040,128]{1,0:T(8,128)(2,1)S(1)}, bf16[1040,128]{1,0:T(8,128)(2,1)S(1)}, u32[]{:S(2)}, u32[]{:S(2)}) collective-permute-start(bf16[1040,128]{1,0:T(8,128)(2,1)S(1)} %collective-permute-done.refs_2_), channel_id=1, source_target_pairs={{0,4},{4,8},{8,12},{12,14},{14,10},{10,6},{6,2},{2,0},{1,5},{5,9},... | collective-permute-start | bytes 798728 | tf_op jit(solution)/shard_map/ppermute | solution.py:421
  15.7 10.0 %collective-permute-start.7 = (bf16[1024,128]{1,0:T(8,128)(2,1)S(1)}, bf16[1024,128]{1,0:T(8,128)(2,1)S(1)}, u32[]{:S(2)}, u32[]{:S(2)}) collective-permute-start(bf16[1024,128]{1,0:T(8,128)(2,1)S(1)} %collective-permute-done.1.refs_5_), channel_id=1, source_target_pairs={{0,2},{4,0},{8,4},{12,8},{14,12},{10,14},{6,10},{2,6},{1,3},{5,1},... | collective-permute-start | bytes 786440 | tf_op jit(solution)/shard_map/ppermute | solution.py:421
  17.8 11.5 %collective-permute-start.5 = (bf16[1056,128]{1,0:T(8,128)(2,1)S(1)}, bf16[1056,128]{1,0:T(8,128)(2,1)S(1)}, u32[]{:S(2)}, u32[]{:S(2)}) collective-permute-start(bf16[1056,128]{1,0:T(8,128)(2,1)S(1)} %collective-permute-done.3.refs_3_), channel_id=1, source_target_pairs={{0,4},{4,8},{8,12},{12,14},{14,10},{10,6},{6,2},{2,0},{1,5},{5,9},... | collective-permute-start | bytes 811016 | tf_op jit(solution)/shard_map/ppermute | solution.py:421
  20.0 11.4 %collective-permute-start.6 = (bf16[1056,128]{1,0:T(8,128)(2,1)S(1)}, bf16[1056,128]{1,0:T(8,128)(2,1)S(1)}, u32[]{:S(2)}, u32[]{:S(2)}) collective-permute-start(bf16[1056,128]{1,0:T(8,128)(2,1)S(1)} %collective-permute-done.4.refs_4_), channel_id=1, source_target_pairs={{0,2},{4,0},{8,4},{12,8},{14,12},{10,14},{6,10},{2,6},{1,3},{5,1},... | collective-permute-start | bytes 811016 | tf_op jit(solution)/shard_map/ppermute | solution.py:421
  23.6 13.4 %collective-permute-start.8 = (bf16[1040,128]{1,0:T(8,128)(2,1)S(1)}, bf16[1040,128]{1,0:T(8,128)(2,1)S(1)}, u32[]{:S(2)}, u32[]{:S(2)}) collective-permute-start(bf16[1040,128]{1,0:T(8,128)(2,1)S(1)} %collective-permute-done.2.refs_0_), channel_id=1, source_target_pairs={{0,4},{4,8},{8,12},{12,14},{14,10},{10,6},{6,2},{2,0},{1,5},{5,9},... | collective-permute-start | bytes 798728 | tf_op jit(solution)/shard_map/ppermute | solution.py:421
  25.7 11.3 %collective-permute-start.9 = (bf16[1024,128]{1,0:T(8,128)(2,1)S(1)}, bf16[1024,128]{1,0:T(8,128)(2,1)S(1)}, u32[]{:S(2)}, u32[]{:S(2)}) collective-permute-start(bf16[1024,128]{1,0:T(8,128)(2,1)S(1)} %collective-permute-done.7.refs_3_), channel_id=1, source_target_pairs={{0,2},{4,0},{8,4},{12,8},{14,12},{10,14},{6,10},{2,6},{1,3},{5,1},... | collective-permute-start | bytes 786440 | tf_op jit(solution)/shard_map/ppermute | solution.py:421
  31.4 9.4 %collective-permute-start.11 = (bf16[1056,128]{1,0:T(8,128)(2,1)S(1)}, bf16[1056,128]{1,0:T(8,128)(2,1)S(1)}, u32[]{:S(2)}, u32[]{:S(2)}) collective-permute-start(bf16[1056,128]{1,0:T(8,128)(2,1)S(1)} %get-tuple-element.44.refs_1_), channel_id=1, source_target_pairs={{0,4},{4,8},{8,12},{12,14},{14,10},{10,6},{6,2},{2,0},{1,5},{5,9},... | collective-permute-start | bytes 811016 | tf_op jit(solution)/shard_map/ppermute | solution.py:421
  33.1 9.6 %collective-permute-start.12 = (bf16[1056,128]{1,0:T(8,128)(2,1)S(1)}, bf16[1056,128]{1,0:T(8,128)(2,1)S(1)}, u32[]{:S(2)}, u32[]{:S(2)}) collective-permute-start(bf16[1056,128]{1,0:T(8,128)(2,1)S(1)} %get-tuple-element.45.refs_2_), channel_id=1, source_target_pairs={{0,2},{4,0},{8,4},{12,8},{14,12},{10,14},{6,10},{2,6},{1,3},{5,1},... | collective-permute-start | bytes 811016 | tf_op jit(solution)/shard_map/ppermute | solution.py:421
  34.3 1.2 %collective-permute-start.10 = (f32[8,128]{1,0:T(8,128)S(1)}, f32[8,128]{1,0:T(8,128)S(1)}, u32[]{:S(2)}, u32[]{:S(2)}) collective-permute-start(f32[8,128]{1,0:T(8,128)S(1)} %get-tuple-element.48), channel_id=1, source_target_pairs={{0,1},{1,0},{2,3},{3,2},{4,5},{5,4},{6,7},{7,6},{8,9},{9,8},{10,11... | collective-permute-start | bytes 12296 | tf_op jit(solution)/shard_map/ppermute | solution.py:432
  37.0 10.4 %collective-permute-start.13 = (bf16[1040,128]{1,0:T(8,128)(2,1)S(1)}, bf16[1040,128]{1,0:T(8,128)(2,1)S(1)}, u32[]{:S(2)}, u32[]{:S(2)}) collective-permute-start(bf16[1040,128]{1,0:T(8,128)(2,1)S(1)} %collective-permute-done.8.refs_0_), channel_id=1, source_target_pairs={{0,4},{4,8},{8,12},{12,14},{14,10},{10,6},{6,2},{2,0},{1,5},{5,9},... | collective-permute-start | bytes 798728 | tf_op jit(solution)/shard_map/ppermute | solution.py:421
  38.6 8.8 %collective-permute-start.14 = (bf16[1024,128]{1,0:T(8,128)(2,1)S(1)}, bf16[1024,128]{1,0:T(8,128)(2,1)S(1)}, u32[]{:S(2)}, u32[]{:S(2)}) collective-permute-start(bf16[1024,128]{1,0:T(8,128)(2,1)S(1)} %collective-permute-done.9.refs_3_), channel_id=1, source_target_pairs={{0,2},{4,0},{8,4},{12,8},{14,12},{10,14},{6,10},{2,6},{1,3},{5,1},... | collective-permute-start | bytes 786440 | tf_op jit(solution)/shard_map/ppermute | solution.py:421
  39.0 12.7 %collective-permute-start.18 = (f32[32,128]{1,0:T(8,128)S(1)}, f32[32,128]{1,0:T(8,128)S(1)}, u32[]{:S(2)}, u32[]{:S(2)}) collective-permute-start(f32[32,128]{1,0:T(8,128)S(1)} %concatenate.3), channel_id=1, source_target_pairs={{0,6},{1,9},{4,2},{5,13},{8,0},{9,15},{12,4},{13,11},{14,8},{15,7}... | collective-permute-start | bytes 49160 | tf_op jit(solution)/shard_map/ppermute | solution.py:439
  43.5 8.2 %collective-permute-start.15 = (f32[8,128]{1,0:T(8,128)S(1)}, f32[8,128]{1,0:T(8,128)S(1)}, u32[]{:S(2)}, u32[]{:S(2)}) collective-permute-start(f32[8,128]{1,0:T(8,128)S(1)} %get-tuple-element.52), channel_id=1, source_target_pairs={{0,10},{4,6},{8,2},{12,0},{14,4},{10,8},{6,12},{2,14},{1,11},{5,7}... | collective-permute-start | bytes 12296 | tf_op jit(solution)/shard_map/ppermute | solution.py:421
  46.0 5.6 %collective-permute-start.16 = (f32[8,128]{1,0:T(8,128)S(1)}, f32[8,128]{1,0:T(8,128)S(1)}, u32[]{:S(2)}, u32[]{:S(2)}) collective-permute-start(f32[8,128]{1,0:T(8,128)S(1)} %get-tuple-element.53), channel_id=1, source_target_pairs={{0,12},{4,14},{8,10},{12,6},{14,2},{10,0},{6,4},{2,8},{1,13},{5,15... | collective-permute-start | bytes 12296 | tf_op jit(solution)/shard_map/ppermute | solution.py:421
  48.1 6.4 %collective-permute-start.17 = (f32[8,128]{1,0:T(8,128)S(1)}, f32[8,128]{1,0:T(8,128)S(1)}, u32[]{:S(2)}, u32[]{:S(2)}) collective-permute-start(f32[8,128]{1,0:T(8,128)S(1)} %scores.7), channel_id=1, source_target_pairs={{0,14},{4,10},{8,6},{12,2},{14,0},{10,4},{6,8},{2,12},{1,15},{5,11... | collective-permute-start | bytes 12296 | tf_op jit(solution)/shard_map/ppermute | solution.py:421
  54.5 1.2 %collective-permute-start.19 = (f32[32,128]{1,0:T(8,128)S(1)}, f32[32,128]{1,0:T(8,128)S(1)}, u32[]{:S(2)}, u32[]{:S(2)}) collective-permute-start(f32[32,128]{1,0:T(8,128)S(1)} %unpack.1), channel_id=1, source_target_pairs={{0,1},{1,0},{2,3},{3,2},{4,5},{5,4},{6,7},{7,6},{8,9},{9,8},{10,11... | collective-permute-start | bytes 49160 | tf_op jit(solution)/shard_map/ppermute | solution.py:432

commit v26 on v18

--- a/solution.py
+++ b/solution.py
@@ -381,7 +381,7 @@
     )(*[kept(piece) for piece in pieces], *[kept(value) for value in values])
 
 
-def unpack_kernel(owners, slots, own, onward, back, second, ahead, behind, opposite, out):
+def unpack_kernel(owners, slots, own, onward, back, second, third, opposite, out):
     owner = slots[...] // BLK_DEV
     start = onward.shape[0] - FACTS
     way = 1 - 2 * lax.axis_index("width")
@@ -389,8 +389,7 @@
     for distance, piece in ((-1, onward), (1, back)):
         rows = piece[start : start + 16, :].astype(jnp.float32)
         returned.append((distance, rows[:KPB] + rows[KPB : 2 * KPB]))
-    returned += [(2 * way, second[...]), (3, ahead[...]), (-3, behind[...])]
-    returned.append((4, opposite[...]))
+    returned += [(2 * way, second[...]), (3 * way, third[...]), (4, opposite[...])]
     mine = [owner == peer_at(distance, owners) for distance, _ in returned]
     for k in range(KPB):
         total = jnp.zeros(owner.shape, jnp.float32)
@@ -462,14 +461,16 @@
     second = return_by(2, jnp.concatenate([second, jnp.zeros((24, 128), jnp.float32)]))[:8]
     first_4 = hop(first_3)
     pairs = [(first_3[0], second_3[0]), (second_3[1], first_3[1])]
-    onward, back = scores_of((-3, 3), pairs, decoder, own_facts)
-    ahead, behind = shift(onward, -3), shift(back, 3)
+    mine, others = scores_of((-3, 3), pairs, decoder, own_facts, True)
+    third = mine + other_core(others)
+    third = return_by(3, third)
+    total, first_4 = lax.optimization_barrier((total, first_4))
     (opposite,) = scores_of((4,), [first_4], decoder, own_facts)
     opposite = shift(opposite, -owners // 2)
-    total, ahead, behind = lax.optimization_barrier((total, ahead, behind))
+    total, third = lax.optimization_barrier((total, third))
     decoder_grad = last_gradients((-3, 3, 4), pairs + [first_4], own_facts, total)
     decoder_grad, opposite = lax.optimization_barrier((decoder_grad, opposite))
-    act_grad = unpack(slots, own, *second_3, second, ahead, behind, opposite)
+    act_grad = unpack(slots, own, *second_3, second, third, opposite)
     act_grad = act_grad + other_core(act_grad)
     return (decoder_grad, act_grad.T)
 

time: 56.2 us -> 56.2 us (level)
  starting transfers between devices: 25.5 us -> 24.5 us
  waiting for transfers between devices: 18 us -> 19 us
    ppermute x17 -> x15, starting transfers between devices: 24 us -> 19.3 us  [shift(): return lax.ppermute(x, 'dp', pairs)]
    ppermute x1 -> x2, starting transfers between devices: 1.38 us -> 4.9 us  [return_by(): return lax.ppermute(x, ('dp', 'width'), pairs)]
    ppermute x2 -> x3, waiting for transfers between devices: 1.17 us -> 2.22 us  [other_core(): return lax.ppermute(x, 'width', ((0, 1), (1, 0)))]
    ppermute x17 -> x15, waiting for transfers between devices: 16.8 us -> 16.8 us  [shift(): return lax.ppermute(x, 'dp', pairs)]
  transfers between devices with their start and end apart: 20 -> 20, of which waited for: 9 -> 10; matrix products, arithmetic and copies ran while one was open for 0% -> 0% of each run, Pallas kernels for 18% -> 18%
where the time goes in v26:
time: 56.2 us; the launch traced here: 56 us
  starting transfers between devices  24.5 us (44%)
  waiting for transfers between devices  19 us (34%)
  Pallas kernels  11.1 us (20%)
  between operations  0.76 us (1%)
  other arithmetic  0.62 us (1%)
    ppermute x15, starting transfers between devices, shift(): return lax.ppermute(x, 'dp', pairs)  19.3 us
    ppermute x15, waiting for transfers between devices, shift(): return lax.ppermute(x, 'dp', pairs)  16.8 us
    ppermute x2, starting transfers between devices, return_by(): return lax.ppermute(x, ('dp', 'width'), pairs)  4.9 us
    pallas_call x4, Pallas kernels, scores_of(): pl.pallas_call(functools.partial(scores_kernel, distances, split), out_sh...  3.72 us
    pallas_call x1, Pallas kernels, last_gradients(): pl.pallas_call(functools.partial(last_gradients_kernel, distances), out_s...  2.28 us
    ppermute x3, waiting for transfers between devices, other_core(): return lax.ppermute(x, 'width', ((0, 1), (1, 0)))  2.22 us
    pallas_call x2, Pallas kernels, gradients_of(): pl.pallas_call(functools.partial(gradients_kernel, distances), out_shape=...  2.21 us
    pallas_call x1, Pallas kernels, fetch(): pl.pallas_call(fetch_kernel, out_shape=pltpu.VMEM(x.shape, x.dtype), in_s...  1.6 us
  transfers between devices with their start and end apart: 20, of which 10 were waited for; matrix products, arithmetic and copies ran while one was open for 0% of the time, Pallas kernels for 18%

profile of v26, /device:TPU:0, one launch (start us, length us, event | category | flops | bytes accessed | tf_op | source)
XLA Modules:
  0.0 56.0 jit_solution(15597981250694788275)
XLA Ops:
  0.6 1.2 %prepare.1 = (bf16[1040,128]{1,0:T(8,128)(2,1)S(1)}, bf16[1024,128]{1,0:T(8,128)(2,1)S(1)}, bf16[1056,128]{1,0:T(8,128)(2,1)S(1)}, bf16[1056,128]{1,0:T(8,128)(2...) custom-call(s32[32]{0:T(128)} %refs_0_.1, s32[8,128]{1,0:T(8,128)} %bitcast.7, s32[32,128]{1,0:T(8,128)} %bitcast.5, ...), custom_call_target="tpu_custom_call" | custom-call | tf_op jit(solution)/shard_map/prepare/pallas_call | solution.py:124
  1.8 3.1 %collective-permute-start = (bf16[1040,128]{1,0:T(8,128)(2,1)S(1)}, bf16[1040,128]{1,0:T(8,128)(2,1)S(1)}, u32[]{:S(2)}, u32[]{:S(2)}) collective-permute-start(bf16[1040,128]{1,0:T(8,128)(2,1)S(1)} %get-tuple-element.32.refs_0_), channel_id=1, source_target_pairs={{0,4},{4,8},{8,12},{12,14},{14,10},{10,6},{6,2},{2,0},{1,5},{5,9},... | collective-permute-start | bytes 798728 | tf_op jit(solution)/shard_map/ppermute | solution.py:420
  4.9 0.0 collective-permute-start.1
  4.9 2.0 %collective-permute-start.3 = (bf16[1056,128]{1,0:T(8,128)(2,1)S(1)}, bf16[1056,128]{1,0:T(8,128)(2,1)S(1)}, u32[]{:S(2)}, u32[]{:S(2)}) collective-permute-start(bf16[1056,128]{1,0:T(8,128)(2,1)S(1)} %get-tuple-element.35), channel_id=1, source_target_pairs={{0,4},{4,8},{8,12},{12,14},{14,10},{10,6},{6,2},{2,0},{1,5},{5,9},... | collective-permute-start | bytes 811016 | tf_op jit(solution)/shard_map/ppermute | solution.py:420
  6.9 0.0 collective-permute-start.5
  6.9 1.6 %fetch.1.decoder = bf16[512,2048]{1,0:T(8,128)(2,1)S(1)} custom-call(bf16[512,2048]{1,0:T(8,128)(2,1)} %source.1), custom_call_target="tpu_custom_call" | custom-call | tf_op jit(solution)/shard_map/fetch/pallas_call | solution.py:158
  8.6 5.6 %collective-permute-done.1.refs_5_ = bf16[1024,128]{1,0:T(8,128)(2,1)S(1)} collective-permute-done((bf16[1024,128]{1,0:T(8,128)(2,1)S(1)}, bf16[1024,128]{1,0:T(8,128)(2,1)S(1)}, u32[]{:S(2)}, u32[]{:S(2)}) %collective-permute-start.1) | collective-permute-done | bytes 262176 | tf_op jit(solution)/shard_map/ppermute | solution.py:420
  14.1 0.0 collective-permute-done.refs_2_
  14.2 1.6 %collective-permute-start.2 = (bf16[1040,128]{1,0:T(8,128)(2,1)S(1)}, bf16[1040,128]{1,0:T(8,128)(2,1)S(1)}, u32[]{:S(2)}, u32[]{:S(2)}) collective-permute-start(bf16[1040,128]{1,0:T(8,128)(2,1)S(1)} %collective-permute-done.refs_2_), channel_id=1, source_target_pairs={{0,4},{4,8},{8,12},{12,14},{14,10},{10,6},{6,2},{2,0},{1,5},{5,9},... | collective-permute-start | bytes 798728 | tf_op jit(solution)/shard_map/ppermute | solution.py:420
  15.7 0.4 collective-permute-start.7
  16.2 1.7 %collective-permute-done.3.refs_3_ = bf16[1056,128]{1,0:T(8,128)(2,1)S(1)} collective-permute-done((bf16[1056,128]{1,0:T(8,128)(2,1)S(1)}, bf16[1056,128]{1,0:T(8,128)(2,1)S(1)}, u32[]{:S(2)}, u32[]{:S(2)}) %collective-permute-start.3) | collective-permute-done | bytes 270368 | tf_op jit(solution)/shard_map/ppermute | solution.py:420
  17.8 2.1 %collective-permute-start.4 = (bf16[1056,128]{1,0:T(8,128)(2,1)S(1)}, bf16[1056,128]{1,0:T(8,128)(2,1)S(1)}, u32[]{:S(2)}, u32[]{:S(2)}) collective-permute-start(bf16[1056,128]{1,0:T(8,128)(2,1)S(1)} %collective-permute-done.3.refs_3_), channel_id=1, source_target_pairs={{0,4},{4,8},{8,12},{12,14},{14,10},{10,6},{6,2},{2,0},{1,5},{5,9},... | collective-permute-start | bytes 811016 | tf_op jit(solution)/shard_map/ppermute | solution.py:420
  20.0 0.0 collective-permute-done.5.refs_4_
  20.0 0.0 collective-permute-start.6
  20.0 3.6 %collective-permute-done.2.refs_0_ = bf16[1040,128]{1,0:T(8,128)(2,1)S(1)} collective-permute-done((bf16[1040,128]{1,0:T(8,128)(2,1)S(1)}, bf16[1040,128]{1,0:T(8,128)(2,1)S(1)}, u32[]{:S(2)}, u32[]{:S(2)}) %collective-permute-start.2) | collective-permute-done | bytes 266272 | tf_op jit(solution)/shard_map/ppermute | solution.py:420
  23.6 2.1 %collective-permute-start.8 = (bf16[1040,128]{1,0:T(8,128)(2,1)S(1)}, bf16[1040,128]{1,0:T(8,128)(2,1)S(1)}, u32[]{:S(2)}, u32[]{:S(2)}) collective-permute-start(bf16[1040,128]{1,0:T(8,128)(2,1)S(1)} %collective-permute-done.2.refs_0_), channel_id=1, source_target_pairs={{0,4},{4,8},{8,12},{12,14},{14,10},{10,6},{6,2},{2,0},{1,5},{5,9},... | collective-permute-start | bytes 798728 | tf_op jit(solution)/shard_map/ppermute | solution.py:420
  25.7 0.0 collective-permute-done.7.refs_3_
  25.7 0.0 collective-permute-start.9
  25.7 1.4 %scores.4 = (f32[8,128]{1,0:T(8,128)S(1)}, f32[8,128]{1,0:T(8,128)S(1)}, f32[8,128]{1,0:T(8,128)S(1)}) custom-call(bf16[512,2048]{1,0:T(8,128)(2,1)S(1)} %fetch.1.decoder, f32[8,128]{1,0:T(8,128)S(1)} %get-tuple-element.31.own_facts, bf16[1040,128]{1,0:T(8,128)(2,1)S(1)} %get-tuple-element.32.refs_0_, bf16[1024,128]{1,0:T(8,128)(2,1)S(1)} %get-tuple-element.33.refs_1_, ...), custom_call_target="tpu_custom_call" | custom-call | tf_op jit(solution)/shard_map/scores/pallas_call | solution.py:278
  27.1 2.3 %collective-permute-done.4.onward = bf16[1056,128]{1,0:T(8,128)(2,1)S(1)} collective-permute-done((bf16[1056,128]{1,0:T(8,128)(2,1)S(1)}, bf16[1056,128]{1,0:T(8,128)(2,1)S(1)}, u32[]{:S(2)}, u32[]{:S(2)}) %collective-permute-start.4) | collective-permute-done | bytes 270368 | tf_op jit(solution)/shard_map/ppermute | solution.py:420
  29.3 2.0 %collective-permute-done.6.back = bf16[1056,128]{1,0:T(8,128)(2,1)S(1)} collective-permute-done((bf16[1056,128]{1,0:T(8,128)(2,1)S(1)}, bf16[1056,128]{1,0:T(8,128)(2,1)S(1)}, u32[]{:S(2)}, u32[]{:S(2)}) %collective-permute-start.6) | collective-permute-done | bytes 270368 | tf_op jit(solution)/shard_map/ppermute | solution.py:420
  31.4 0.1 stamp.1
  31.4 1.6 %collective-permute-start.11 = (bf16[1056,128]{1,0:T(8,128)(2,1)S(1)}, bf16[1056,128]{1,0:T(8,128)(2,1)S(1)}, u32[]{:S(2)}, u32[]{:S(2)}) collective-permute-start(bf16[1056,128]{1,0:T(8,128)(2,1)S(1)} %get-tuple-element.41.refs_1_), channel_id=1, source_target_pairs={{0,4},{4,8},{8,12},{12,14},{14,10},{10,6},{6,2},{2,0},{1,5},{5,9},... | collective-permute-start | bytes 811016 | tf_op jit(solution)/shard_map/ppermute | solution.py:420
  33.1 0.4 collective-permute-start.12
  33.5 0.8 %scores.5 = (f32[8,128]{1,0:T(8,128)S(1)}, f32[8,128]{1,0:T(8,128)S(1)}) custom-call(bf16[512,2048]{1,0:T(8,128)(2,1)S(1)} %fetch.1.decoder, f32[8,128]{1,0:T(8,128)S(1)} %get-tuple-element.31.own_facts, bf16[1040,128]{1,0:T(8,128)(2,1)S(1)} %collective-permute-done.2.refs_0_, bf16[1056,128]{1,0:T(8,128)(2,1)S(1)} %get-tuple-element.41.refs_1_, ...), custom_call_target="tpu_custom_call" | custom-call | tf_op jit(solution)/shard_map/scores/pallas_call | solution.py:278
  34.3 0.1 collective-permute-start.10
  34.4 1.3 %gradients.2.refs_4_ = f32[512,2048]{1,0:T(8,128)S(1)} custom-call(f32[8,128]{1,0:T(8,128)S(1)} %get-tuple-element.31.own_facts, bf16[1040,128]{1,0:T(8,128)(2,1)S(1)} %get-tuple-element.32.refs_0_, bf16[1024,128]{1,0:T(8,128)(2,1)S(1)} %get-tuple-element.33.refs_1_, bf16[1040,128]{1,0:T(8,128)(2,1)S(1)} %collective-permute-done.refs_2_, ...), custom_call_target="tpu_custom_call" | custom-call | tf_op jit(solution)/shard_map/gradients/pallas_call | solution.py:299
  35.7 0.9 %gradients.3.refs_6_ = f32[512,2048]{1,0:T(8,128)S(1)} custom-call(f32[8,128]{1,0:T(8,128)S(1)} %get-tuple-element.31.own_facts, bf16[1040,128]{1,0:T(8,128)(2,1)S(1)} %collective-permute-done.2.refs_0_, bf16[1056,128]{1,0:T(8,128)(2,1)S(1)} %get-tuple-element.41.refs_1_, ...), custom_call_target="tpu_custom_call", output_to_operand_aliasing={{}: (5, {})} | custom-call | tf_op jit(solution)/shard_map/gradients/pallas_call | solution.py:299
  36.6 0.0 collective-permute-done.10
  36.7 0.3 collective-permute-done.9.refs_3_
  37.0 0.0 collective-permute-done.8.refs_0_
  37.0 1.6 %collective-permute-start.13 = (bf16[1040,128]{1,0:T(8,128)(2,1)S(1)}, bf16[1040,128]{1,0:T(8,128)(2,1)S(1)}, u32[]{:S(2)}, u32[]{:S(2)}) collective-permute-start(bf16[1040,128]{1,0:T(8,128)(2,1)S(1)} %collective-permute-done.8.refs_0_), channel_id=1, source_target_pairs={{0,4},{4,8},{8,12},{12,14},{14,10},{10,6},{6,2},{2,0},{1,5},{5,9},... | collective-permute-start | bytes 798728 | tf_op jit(solution)/shard_map/ppermute | solution.py:420
  38.6 0.4 collective-permute-start.14
  39.0 1.4 %collective-permute-start.18 = (f32[32,128]{1,0:T(8,128)S(1)}, f32[32,128]{1,0:T(8,128)S(1)}, u32[]{:S(2)}, u32[]{:S(2)}) collective-permute-start(f32[32,128]{1,0:T(8,128)S(1)} %concatenate.3), channel_id=1, source_target_pairs={{0,6},{1,9},{4,2},{5,13},{8,0},{9,15},{12,4},{13,11},{14,8},{15,7}... | collective-permute-start | bytes 49160 | tf_op jit(solution)/shard_map/ppermute | solution.py:438
  40.4 0.0 collective-permute-done.11.refs_1_.onward
  40.4 1.0 %collective-permute-done.12.refs_2_.back = bf16[1056,128]{1,0:T(8,128)(2,1)S(1)} collective-permute-done((bf16[1056,128]{1,0:T(8,128)(2,1)S(1)}, bf16[1056,128]{1,0:T(8,128)(2,1)S(1)}, u32[]{:S(2)}, u32[]{:S(2)}) %collective-permute-start.12) | collective-permute-done | bytes 270368 | tf_op jit(solution)/shard_map/ppermute | solution.py:420
  41.4 0.8 %scores.6 = (f32[8,128]{1,0:T(8,128)S(1)}, f32[8,128]{1,0:T(8,128)S(1)}) custom-call(bf16[512,2048]{1,0:T(8,128)(2,1)S(1)} %fetch.1.decoder, f32[8,128]{1,0:T(8,128)S(1)} %get-tuple-element.31.own_facts, bf16[1040,128]{1,0:T(8,128)(2,1)S(1)} %collective-permute-done.8.refs_0_, bf16[1056,128]{1,0:T(8,128)(2,1)S(1)} %collective-permute-done.11.refs_1_.onward, ...), custom_call_target="tpu_custom_call" | custom-call | tf_op jit(solution)/shard_map/scores/pallas_call | solution.py:278
  42.2 0.1 collective-permute-start.15
  42.3 1.2 %collective-permute-done.15 = f32[8,128]{1,0:T(8,128)S(1)} collective-permute-done((f32[8,128]{1,0:T(8,128)S(1)}, f32[8,128]{1,0:T(8,128)S(1)}, u32[]{:S(2)}, u32[]{:S(2)}) %collective-permute-start.15) | collective-permute-done | bytes 4128 | tf_op jit(solution)/shard_map/ppermute | solution.py:431
  43.5 3.5 %collective-permute-start.16 = (f32[8,128]{1,0:T(8,128)S(1)}, f32[8,128]{1,0:T(8,128)S(1)}, u32[]{:S(2)}, u32[]{:S(2)}) collective-permute-start(f32[8,128]{1,0:T(8,128)S(1)} %add.12), channel_id=1, source_target_pairs={{0,10},{1,13},{4,6},{5,15},{8,2},{9,11},{12,0},{13,7},{14,4},{15,3... | collective-permute-start | bytes 12296 | tf_op jit(solution)/shard_map/ppermute | solution.py:438
  47.0 0.0 collective-permute-done.14.refs_5_.refs_1_
  47.0 0.0 collective-permute-done.13.refs_4_.refs_0_
  47.0 0.7 %scores.7 = f32[8,128]{1,0:T(8,128)S(1)} custom-call(bf16[512,2048]{1,0:T(8,128)(2,1)S(1)} %fetch.1.decoder, f32[8,128]{1,0:T(8,128)S(1)} %get-tuple-element.31.own_facts, bf16[1040,128]{1,0:T(8,128)(2,1)S(1)} %collective-permute-done.13.refs_4_.refs_0_, bf16[1024,128]{1,0:T(8,128)(2,1)S(1)} %collective-permute-done.14.refs_5_.refs_1_), custom_call_target="tpu_custom_call" | custom-call | tf_op jit(solution)/shard_map/scores/pallas_call | solution.py:278
  47.7 3.7 %collective-permute-start.17 = (f32[8,128]{1,0:T(8,128)S(1)}, f32[8,128]{1,0:T(8,128)S(1)}, u32[]{:S(2)}, u32[]{:S(2)}) collective-permute-start(f32[8,128]{1,0:T(8,128)S(1)} %scores.7), channel_id=1, source_target_pairs={{0,14},{4,10},{8,6},{12,2},{14,0},{10,4},{6,8},{2,12},{1,15},{5,11... | collective-permute-start | bytes 12296 | tf_op jit(solution)/shard_map/ppermute | solution.py:420
  51.5 0.0 collective-permute-done.18
  51.5 0.0 collective-permute-done.16.third
  51.5 2.3 %last_gradients.1 = bf16[512,2048]{1,0:T(8,128)(2,1)} custom-call(f32[8,128]{1,0:T(8,128)S(1)} %get-tuple-element.31.own_facts, bf16[1040,128]{1,0:T(8,128)(2,1)S(1)} %collective-permute-done.8.refs_0_, bf16[1056,128]{1,0:T(8,128)(2,1)S(1)} %collective-permute-done.11.refs_1_.onward, bf16[1056,128]{1,0:T(8,128)(2,1)S(1)} %collective-permute-done.12.refs_2_.back, ...), custom_call_target="tpu_custom_call" | custom-call | tf_op jit(solution)/shard_map/last_gradients/pallas_call | solution.py:329
  53.8 0.3 collective-permute-done.17.opposite
  54.1 0.2 collective-permute-start.19
  54.3 1.1 %collective-permute-done.19 = f32[32,128]{1,0:T(8,128)S(1)} collective-permute-done((f32[32,128]{1,0:T(8,128)S(1)}, f32[32,128]{1,0:T(8,128)S(1)}, u32[]{:S(2)}, u32[]{:S(2)}) %collective-permute-start.19) | collective-permute-done | bytes 16416 | tf_op jit(solution)/shard_map/ppermute | solution.py:431
  55.4 0.6 %add_bitcast_fusion = f32[128,32]{0,1:T(8,128)} fusion(f32[32,128]{1,0:T(8,128)S(1)} %unpack.1, f32[32,128]{1,0:T(8,128)S(1)} %collective-permute-done.19), kind=kLoop, calls=%fused_computation | loop fusion | flops 4096 | bytes 49152 | tf_op jit(solution)/shard_map/transpose | solution.py:475
  (5 shorter events, 0.0 us)
Async XLA Ops:
  1.8 12.3 %collective-permute-start = (bf16[1040,128]{1,0:T(8,128)(2,1)S(1)}, bf16[1040,128]{1,0:T(8,128)(2,1)S(1)}, u32[]{:S(2)}, u32[]{:S(2)}) collective-permute-start(bf16[1040,128]{1,0:T(8,128)(2,1)S(1)} %get-tuple-element.32.refs_0_), channel_id=1, source_target_pairs={{0,4},{4,8},{8,12},{12,14},{14,10},{10,6},{6,2},{2,0},{1,5},{5,9},... | collective-permute-start | bytes 798728 | tf_op jit(solution)/shard_map/ppermute | solution.py:420
  4.9 9.2 %collective-permute-start.1 = (bf16[1024,128]{1,0:T(8,128)(2,1)S(1)}, bf16[1024,128]{1,0:T(8,128)(2,1)S(1)}, u32[]{:S(2)}, u32[]{:S(2)}) collective-permute-start(bf16[1024,128]{1,0:T(8,128)(2,1)S(1)} %get-tuple-element.33.refs_1_), channel_id=1, source_target_pairs={{0,2},{4,0},{8,4},{12,8},{14,12},{10,14},{6,10},{2,6},{1,3},{5,1},... | collective-permute-start | bytes 786440 | tf_op jit(solution)/shard_map/ppermute | solution.py:420
  4.9 12.9 %collective-permute-start.3 = (bf16[1056,128]{1,0:T(8,128)(2,1)S(1)}, bf16[1056,128]{1,0:T(8,128)(2,1)S(1)}, u32[]{:S(2)}, u32[]{:S(2)}) collective-permute-start(bf16[1056,128]{1,0:T(8,128)(2,1)S(1)} %get-tuple-element.35), channel_id=1, source_target_pairs={{0,4},{4,8},{8,12},{12,14},{14,10},{10,6},{6,2},{2,0},{1,5},{5,9},... | collective-permute-start | bytes 811016 | tf_op jit(solution)/shard_map/ppermute | solution.py:420
  6.9 13.1 %collective-permute-start.5 = (bf16[1056,128]{1,0:T(8,128)(2,1)S(1)}, bf16[1056,128]{1,0:T(8,128)(2,1)S(1)}, u32[]{:S(2)}, u32[]{:S(2)}) collective-permute-start(bf16[1056,128]{1,0:T(8,128)(2,1)S(1)} %get-tuple-element.36), channel_id=1, source_target_pairs={{0,2},{4,0},{8,4},{12,8},{14,12},{10,14},{6,10},{2,6},{1,3},{5,1},... | collective-permute-start | bytes 811016 | tf_op jit(solution)/shard_map/ppermute | solution.py:420
  14.2 9.4 %collective-permute-start.2 = (bf16[1040,128]{1,0:T(8,128)(2,1)S(1)}, bf16[1040,128]{1,0:T(8,128)(2,1)S(1)}, u32[]{:S(2)}, u32[]{:S(2)}) collective-permute-start(bf16[1040,128]{1,0:T(8,128)(2,1)S(1)} %collective-permute-done.refs_2_), channel_id=1, source_target_pairs={{0,4},{4,8},{8,12},{12,14},{14,10},{10,6},{6,2},{2,0},{1,5},{5,9},... | collective-permute-start | bytes 798728 | tf_op jit(solution)/shard_map/ppermute | solution.py:420
  15.7 10.0 %collective-permute-start.7 = (bf16[1024,128]{1,0:T(8,128)(2,1)S(1)}, bf16[1024,128]{1,0:T(8,128)(2,1)S(1)}, u32[]{:S(2)}, u32[]{:S(2)}) collective-permute-start(bf16[1024,128]{1,0:T(8,128)(2,1)S(1)} %collective-permute-done.1.refs_5_), channel_id=1, source_target_pairs={{0,2},{4,0},{8,4},{12,8},{14,12},{10,14},{6,10},{2,6},{1,3},{5,1},... | collective-permute-start | bytes 786440 | tf_op jit(solution)/shard_map/ppermute | solution.py:420
  17.8 11.5 %collective-permute-start.4 = (bf16[1056,128]{1,0:T(8,128)(2,1)S(1)}, bf16[1056,128]{1,0:T(8,128)(2,1)S(1)}, u32[]{:S(2)}, u32[]{:S(2)}) collective-permute-start(bf16[1056,128]{1,0:T(8,128)(2,1)S(1)} %collective-permute-done.3.refs_3_), channel_id=1, source_target_pairs={{0,4},{4,8},{8,12},{12,14},{14,10},{10,6},{6,2},{2,0},{1,5},{5,9},... | collective-permute-start | bytes 811016 | tf_op jit(solution)/shard_map/ppermute | solution.py:420
  20.0 11.4 %collective-permute-start.6 = (bf16[1056,128]{1,0:T(8,128)(2,1)S(1)}, bf16[1056,128]{1,0:T(8,128)(2,1)S(1)}, u32[]{:S(2)}, u32[]{:S(2)}) collective-permute-start(bf16[1056,128]{1,0:T(8,128)(2,1)S(1)} %collective-permute-done.5.refs_4_), channel_id=1, source_target_pairs={{0,2},{4,0},{8,4},{12,8},{14,12},{10,14},{6,10},{2,6},{1,3},{5,1},... | collective-permute-start | bytes 811016 | tf_op jit(solution)/shard_map/ppermute | solution.py:420
  23.6 13.4 %collective-permute-start.8 = (bf16[1040,128]{1,0:T(8,128)(2,1)S(1)}, bf16[1040,128]{1,0:T(8,128)(2,1)S(1)}, u32[]{:S(2)}, u32[]{:S(2)}) collective-permute-start(bf16[1040,128]{1,0:T(8,128)(2,1)S(1)} %collective-permute-done.2.refs_0_), channel_id=1, source_target_pairs={{0,4},{4,8},{8,12},{12,14},{14,10},{10,6},{6,2},{2,0},{1,5},{5,9},... | collective-permute-start | bytes 798728 | tf_op jit(solution)/shard_map/ppermute | solution.py:420
  25.7 11.3 %collective-permute-start.9 = (bf16[1024,128]{1,0:T(8,128)(2,1)S(1)}, bf16[1024,128]{1,0:T(8,128)(2,1)S(1)}, u32[]{:S(2)}, u32[]{:S(2)}) collective-permute-start(bf16[1024,128]{1,0:T(8,128)(2,1)S(1)} %collective-permute-done.7.refs_3_), channel_id=1, source_target_pairs={{0,2},{4,0},{8,4},{12,8},{14,12},{10,14},{6,10},{2,6},{1,3},{5,1},... | collective-permute-start | bytes 786440 | tf_op jit(solution)/shard_map/ppermute | solution.py:420
  31.4 9.0 %collective-permute-start.11 = (bf16[1056,128]{1,0:T(8,128)(2,1)S(1)}, bf16[1056,128]{1,0:T(8,128)(2,1)S(1)}, u32[]{:S(2)}, u32[]{:S(2)}) collective-permute-start(bf16[1056,128]{1,0:T(8,128)(2,1)S(1)} %get-tuple-element.41.refs_1_), channel_id=1, source_target_pairs={{0,4},{4,8},{8,12},{12,14},{14,10},{10,6},{6,2},{2,0},{1,5},{5,9},... | collective-permute-start | bytes 811016 | tf_op jit(solution)/shard_map/ppermute | solution.py:420
  33.1 8.4 %collective-permute-start.12 = (bf16[1056,128]{1,0:T(8,128)(2,1)S(1)}, bf16[1056,128]{1,0:T(8,128)(2,1)S(1)}, u32[]{:S(2)}, u32[]{:S(2)}) collective-permute-start(bf16[1056,128]{1,0:T(8,128)(2,1)S(1)} %get-tuple-element.42.refs_2_), channel_id=1, source_target_pairs={{0,2},{4,0},{8,4},{12,8},{14,12},{10,14},{6,10},{2,6},{1,3},{5,1},... | collective-permute-start | bytes 811016 | tf_op jit(solution)/shard_map/ppermute | solution.py:420
  34.3 2.3 %collective-permute-start.10 = (f32[8,128]{1,0:T(8,128)S(1)}, f32[8,128]{1,0:T(8,128)S(1)}, u32[]{:S(2)}, u32[]{:S(2)}) collective-permute-start(f32[8,128]{1,0:T(8,128)S(1)} %get-tuple-element.44), channel_id=1, source_target_pairs={{0,1},{1,0},{2,3},{3,2},{4,5},{5,4},{6,7},{7,6},{8,9},{9,8},{10,11... | collective-permute-start | bytes 12296 | tf_op jit(solution)/shard_map/ppermute | solution.py:431
  37.0 10.0 %collective-permute-start.13 = (bf16[1040,128]{1,0:T(8,128)(2,1)S(1)}, bf16[1040,128]{1,0:T(8,128)(2,1)S(1)}, u32[]{:S(2)}, u32[]{:S(2)}) collective-permute-start(bf16[1040,128]{1,0:T(8,128)(2,1)S(1)} %collective-permute-done.8.refs_0_), channel_id=1, source_target_pairs={{0,4},{4,8},{8,12},{12,14},{14,10},{10,6},{6,2},{2,0},{1,5},{5,9},... | collective-permute-start | bytes 798728 | tf_op jit(solution)/shard_map/ppermute | solution.py:420
  38.6 8.5 %collective-permute-start.14 = (bf16[1024,128]{1,0:T(8,128)(2,1)S(1)}, bf16[1024,128]{1,0:T(8,128)(2,1)S(1)}, u32[]{:S(2)}, u32[]{:S(2)}) collective-permute-start(bf16[1024,128]{1,0:T(8,128)(2,1)S(1)} %collective-permute-done.9.refs_3_), channel_id=1, source_target_pairs={{0,2},{4,0},{8,4},{12,8},{14,12},{10,14},{6,10},{2,6},{1,3},{5,1},... | collective-permute-start | bytes 786440 | tf_op jit(solution)/shard_map/ppermute | solution.py:420
  39.0 12.5 %collective-permute-start.18 = (f32[32,128]{1,0:T(8,128)S(1)}, f32[32,128]{1,0:T(8,128)S(1)}, u32[]{:S(2)}, u32[]{:S(2)}) collective-permute-start(f32[32,128]{1,0:T(8,128)S(1)} %concatenate.3), channel_id=1, source_target_pairs={{0,6},{1,9},{4,2},{5,13},{8,0},{9,15},{12,4},{13,11},{14,8},{15,7}... | collective-permute-start | bytes 49160 | tf_op jit(solution)/shard_map/ppermute | solution.py:438
  42.2 1.2 %collective-permute-start.15 = (f32[8,128]{1,0:T(8,128)S(1)}, f32[8,128]{1,0:T(8,128)S(1)}, u32[]{:S(2)}, u32[]{:S(2)}) collective-permute-start(f32[8,128]{1,0:T(8,128)S(1)} %get-tuple-element.52), channel_id=1, source_target_pairs={{0,1},{1,0},{2,3},{3,2},{4,5},{5,4},{6,7},{7,6},{8,9},{9,8},{10,11... | collective-permute-start | bytes 12296 | tf_op jit(solution)/shard_map/ppermute | solution.py:431
  43.5 8.0 %collective-permute-start.16 = (f32[8,128]{1,0:T(8,128)S(1)}, f32[8,128]{1,0:T(8,128)S(1)}, u32[]{:S(2)}, u32[]{:S(2)}) collective-permute-start(f32[8,128]{1,0:T(8,128)S(1)} %add.12), channel_id=1, source_target_pairs={{0,10},{1,13},{4,6},{5,15},{8,2},{9,11},{12,0},{13,7},{14,4},{15,3... | collective-permute-start | bytes 12296 | tf_op jit(solution)/shard_map/ppermute | solution.py:438
  47.7 6.4 %collective-permute-start.17 = (f32[8,128]{1,0:T(8,128)S(1)}, f32[8,128]{1,0:T(8,128)S(1)}, u32[]{:S(2)}, u32[]{:S(2)}) collective-permute-start(f32[8,128]{1,0:T(8,128)S(1)} %scores.7), channel_id=1, source_target_pairs={{0,14},{4,10},{8,6},{12,2},{14,0},{10,4},{6,8},{2,12},{1,15},{5,11... | collective-permute-start | bytes 12296 | tf_op jit(solution)/shard_map/ppermute | solution.py:420
  54.1 1.2 %collective-permute-start.19 = (f32[32,128]{1,0:T(8,128)S(1)}, f32[32,128]{1,0:T(8,128)S(1)}, u32[]{:S(2)}, u32[]{:S(2)}) collective-permute-start(f32[32,128]{1,0:T(8,128)S(1)} %unpack.1), channel_id=1, source_target_pairs={{0,1},{1,0},{2,3},{3,2},{4,5},{5,4},{6,7},{7,6},{8,9},{9,8},{10,11... | collective-permute-start | bytes 49160 | tf_op jit(solution)/shard_map/ppermute | solution.py:431

commit v27 on v12

--- a/solution.py
+++ b/solution.py
@@ -455,7 +455,7 @@
     total = gradients_of((-2, 2), pairs, own_facts, decoder.shape, total)
     second = mine + other_core(others)
     total, first_3, second = lax.optimization_barrier((total, first_3, second))
-    second = return_by(2, jnp.concatenate([second, jnp.zeros((24, 128), jnp.float32)]))[:8]
+    second = return_by(2, jnp.concatenate([second, jnp.zeros((16, 128), jnp.float32)]))[:8]
     first_4 = hop(first_3)
     pairs = [(first_3[0], second_3[0]), (second_3[1], first_3[1])]
     mine, others = scores_of((-3, 3), pairs, decoder, own_facts, True)

time: 56.2 us -> 56.2 us (level)
  no operation moved by 1% of the time
where the time goes in v27:
time: 56.2 us; the launch traced here: 56 us
  starting transfers between devices  24.4 us (43%)
  waiting for transfers between devices  18.7 us (33%)
  Pallas kernels  11.5 us (20%)
  between operations  0.77 us (1%)
  other arithmetic  0.62 us (1%)
    ppermute x15, starting transfers between devices, shift(): return lax.ppermute(x, 'dp', pairs)  19.2 us
    ppermute x15, waiting for transfers between devices, shift(): return lax.ppermute(x, 'dp', pairs)  17.4 us
    ppermute x2, starting transfers between devices, return_by(): return lax.ppermute(x, ('dp', 'width'), pairs)  4.9 us
    pallas_call x4, Pallas kernels, scores_of(): pl.pallas_call(functools.partial(scores_kernel, distances, split), out_sh...  3.72 us
    pallas_call x3, Pallas kernels, gradients_of(): pl.pallas_call(functools.partial(gradients_kernel, distances), out_shape=...  3.14 us
    pallas_call x1, Pallas kernels, last_gradients(): pl.pallas_call(last_gradients_kernel, out_shape=jax.ShapeDtypeStruct(tota...  1.74 us
    pallas_call x1, Pallas kernels, fetch(): pl.pallas_call(fetch_kernel, out_shape=pltpu.VMEM(x.shape, x.dtype), in_s...  1.6 us
    ppermute x3, waiting for transfers between devices, other_core(): return lax.ppermute(x, 'width', ((0, 1), (1, 0)))  1.28 us
  transfers between devices with their start and end apart: 20, of which 10 were waited for; matrix products, arithmetic and copies ran while one was open for 0% of the time, Pallas kernels for 18%

profile of v27, /device:TPU:0, one launch (start us, length us, event | category | flops | bytes accessed | tf_op | source)
XLA Modules:
  0.0 56.0 jit_solution(8714330838651382236)
XLA Ops:
  0.6 1.2 %prepare.1 = (bf16[1040,128]{1,0:T(8,128)(2,1)S(1)}, bf16[1024,128]{1,0:T(8,128)(2,1)S(1)}, bf16[1056,128]{1,0:T(8,128)(2,1)S(1)}, bf16[1056,128]{1,0:T(8,128)(2...) custom-call(s32[32]{0:T(128)} %refs_0_.1, s32[8,128]{1,0:T(8,128)} %bitcast.7, s32[32,128]{1,0:T(8,128)} %bitcast.5, ...), custom_call_target="tpu_custom_call" | custom-call | tf_op jit(solution)/shard_map/prepare/pallas_call | solution.py:124
  1.8 3.1 %collective-permute-start = (bf16[1040,128]{1,0:T(8,128)(2,1)S(1)}, bf16[1040,128]{1,0:T(8,128)(2,1)S(1)}, u32[]{:S(2)}, u32[]{:S(2)}) collective-permute-start(bf16[1040,128]{1,0:T(8,128)(2,1)S(1)} %get-tuple-element.34.refs_0_), channel_id=1, source_target_pairs={{0,4},{4,8},{8,12},{12,14},{14,10},{10,6},{6,2},{2,0},{1,5},{5,9},... | collective-permute-start | bytes 798728 | tf_op jit(solution)/shard_map/ppermute | solution.py:417
  4.9 0.0 collective-permute-start.1
  4.9 2.0 %collective-permute-start.3 = (bf16[1056,128]{1,0:T(8,128)(2,1)S(1)}, bf16[1056,128]{1,0:T(8,128)(2,1)S(1)}, u32[]{:S(2)}, u32[]{:S(2)}) collective-permute-start(bf16[1056,128]{1,0:T(8,128)(2,1)S(1)} %get-tuple-element.37), channel_id=1, source_target_pairs={{0,4},{4,8},{8,12},{12,14},{14,10},{10,6},{6,2},{2,0},{1,5},{5,9},... | collective-permute-start | bytes 811016 | tf_op jit(solution)/shard_map/ppermute | solution.py:417
  6.9 0.0 collective-permute-start.5
  6.9 1.6 %fetch.1.decoder = bf16[512,2048]{1,0:T(8,128)(2,1)S(1)} custom-call(bf16[512,2048]{1,0:T(8,128)(2,1)} %source.1), custom_call_target="tpu_custom_call" | custom-call | tf_op jit(solution)/shard_map/fetch/pallas_call | solution.py:158
  8.6 5.6 %collective-permute-done.1.refs_5_ = bf16[1024,128]{1,0:T(8,128)(2,1)S(1)} collective-permute-done((bf16[1024,128]{1,0:T(8,128)(2,1)S(1)}, bf16[1024,128]{1,0:T(8,128)(2,1)S(1)}, u32[]{:S(2)}, u32[]{:S(2)}) %collective-permute-start.1) | collective-permute-done | bytes 262176 | tf_op jit(solution)/shard_map/ppermute | solution.py:417
  14.1 0.0 collective-permute-done.refs_2_
  14.2 1.6 %collective-permute-start.2 = (bf16[1040,128]{1,0:T(8,128)(2,1)S(1)}, bf16[1040,128]{1,0:T(8,128)(2,1)S(1)}, u32[]{:S(2)}, u32[]{:S(2)}) collective-permute-start(bf16[1040,128]{1,0:T(8,128)(2,1)S(1)} %collective-permute-done.refs_2_), channel_id=1, source_target_pairs={{0,4},{4,8},{8,12},{12,14},{14,10},{10,6},{6,2},{2,0},{1,5},{5,9},... | collective-permute-start | bytes 798728 | tf_op jit(solution)/shard_map/ppermute | solution.py:417
  15.7 0.4 collective-permute-start.7
  16.2 1.7 %collective-permute-done.3.refs_3_ = bf16[1056,128]{1,0:T(8,128)(2,1)S(1)} collective-permute-done((bf16[1056,128]{1,0:T(8,128)(2,1)S(1)}, bf16[1056,128]{1,0:T(8,128)(2,1)S(1)}, u32[]{:S(2)}, u32[]{:S(2)}) %collective-permute-start.3) | collective-permute-done | bytes 270368 | tf_op jit(solution)/shard_map/ppermute | solution.py:417
  17.8 2.1 %collective-permute-start.4 = (bf16[1056,128]{1,0:T(8,128)(2,1)S(1)}, bf16[1056,128]{1,0:T(8,128)(2,1)S(1)}, u32[]{:S(2)}, u32[]{:S(2)}) collective-permute-start(bf16[1056,128]{1,0:T(8,128)(2,1)S(1)} %collective-permute-done.3.refs_3_), channel_id=1, source_target_pairs={{0,4},{4,8},{8,12},{12,14},{14,10},{10,6},{6,2},{2,0},{1,5},{5,9},... | collective-permute-start | bytes 811016 | tf_op jit(solution)/shard_map/ppermute | solution.py:417
  20.0 0.0 collective-permute-done.5.refs_4_
  20.0 0.0 collective-permute-start.6
  20.0 3.6 %collective-permute-done.2.refs_0_ = bf16[1040,128]{1,0:T(8,128)(2,1)S(1)} collective-permute-done((bf16[1040,128]{1,0:T(8,128)(2,1)S(1)}, bf16[1040,128]{1,0:T(8,128)(2,1)S(1)}, u32[]{:S(2)}, u32[]{:S(2)}) %collective-permute-start.2) | collective-permute-done | bytes 266272 | tf_op jit(solution)/shard_map/ppermute | solution.py:417
  23.6 2.1 %collective-permute-start.8 = (bf16[1040,128]{1,0:T(8,128)(2,1)S(1)}, bf16[1040,128]{1,0:T(8,128)(2,1)S(1)}, u32[]{:S(2)}, u32[]{:S(2)}) collective-permute-start(bf16[1040,128]{1,0:T(8,128)(2,1)S(1)} %collective-permute-done.2.refs_0_), channel_id=1, source_target_pairs={{0,4},{4,8},{8,12},{12,14},{14,10},{10,6},{6,2},{2,0},{1,5},{5,9},... | collective-permute-start | bytes 798728 | tf_op jit(solution)/shard_map/ppermute | solution.py:417
  25.7 0.0 collective-permute-done.7.refs_3_
  25.7 0.0 collective-permute-start.9
  25.7 1.4 %scores.4 = (f32[8,128]{1,0:T(8,128)S(1)}, f32[8,128]{1,0:T(8,128)S(1)}, f32[8,128]{1,0:T(8,128)S(1)}) custom-call(bf16[512,2048]{1,0:T(8,128)(2,1)S(1)} %fetch.1.decoder, f32[8,128]{1,0:T(8,128)S(1)} %get-tuple-element.33.own_facts, bf16[1040,128]{1,0:T(8,128)(2,1)S(1)} %get-tuple-element.34.refs_0_, bf16[1024,128]{1,0:T(8,128)(2,1)S(1)} %get-tuple-element.35.refs_1_, ...), custom_call_target="tpu_custom_call" | custom-call | tf_op jit(solution)/shard_map/scores/pallas_call | solution.py:278
  27.1 2.3 %collective-permute-done.4.onward = bf16[1056,128]{1,0:T(8,128)(2,1)S(1)} collective-permute-done((bf16[1056,128]{1,0:T(8,128)(2,1)S(1)}, bf16[1056,128]{1,0:T(8,128)(2,1)S(1)}, u32[]{:S(2)}, u32[]{:S(2)}) %collective-permute-start.4) | collective-permute-done | bytes 270368 | tf_op jit(solution)/shard_map/ppermute | solution.py:417
  29.3 2.0 %collective-permute-done.6.back = bf16[1056,128]{1,0:T(8,128)(2,1)S(1)} collective-permute-done((bf16[1056,128]{1,0:T(8,128)(2,1)S(1)}, bf16[1056,128]{1,0:T(8,128)(2,1)S(1)}, u32[]{:S(2)}, u32[]{:S(2)}) %collective-permute-start.6) | collective-permute-done | bytes 270368 | tf_op jit(solution)/shard_map/ppermute | solution.py:417
  31.4 0.1 stamp.1
  31.4 1.6 %collective-permute-start.11 = (bf16[1056,128]{1,0:T(8,128)(2,1)S(1)}, bf16[1056,128]{1,0:T(8,128)(2,1)S(1)}, u32[]{:S(2)}, u32[]{:S(2)}) collective-permute-start(bf16[1056,128]{1,0:T(8,128)(2,1)S(1)} %get-tuple-element.43.refs_1_), channel_id=1, source_target_pairs={{0,4},{4,8},{8,12},{12,14},{14,10},{10,6},{6,2},{2,0},{1,5},{5,9},... | collective-permute-start | bytes 811016 | tf_op jit(solution)/shard_map/ppermute | solution.py:417
  33.1 0.4 collective-permute-start.12
  33.5 0.8 %scores.5 = (f32[8,128]{1,0:T(8,128)S(1)}, f32[8,128]{1,0:T(8,128)S(1)}) custom-call(bf16[512,2048]{1,0:T(8,128)(2,1)S(1)} %fetch.1.decoder, f32[8,128]{1,0:T(8,128)S(1)} %get-tuple-element.33.own_facts, bf16[1040,128]{1,0:T(8,128)(2,1)S(1)} %collective-permute-done.2.refs_0_, bf16[1056,128]{1,0:T(8,128)(2,1)S(1)} %get-tuple-element.43.refs_1_, ...), custom_call_target="tpu_custom_call" | custom-call | tf_op jit(solution)/shard_map/scores/pallas_call | solution.py:278
  34.3 0.1 collective-permute-start.10
  34.4 1.3 %gradients.3.refs_4_ = f32[512,2048]{1,0:T(8,128)S(1)} custom-call(f32[8,128]{1,0:T(8,128)S(1)} %get-tuple-element.33.own_facts, bf16[1040,128]{1,0:T(8,128)(2,1)S(1)} %get-tuple-element.34.refs_0_, bf16[1024,128]{1,0:T(8,128)(2,1)S(1)} %get-tuple-element.35.refs_1_, bf16[1040,128]{1,0:T(8,128)(2,1)S(1)} %collective-permute-done.refs_2_, ...), custom_call_target="tpu_custom_call" | custom-call | tf_op jit(solution)/shard_map/gradients/pallas_call | solution.py:299
  35.7 0.9 %gradients.4.refs_4_ = f32[512,2048]{1,0:T(8,128)S(1)} custom-call(f32[8,128]{1,0:T(8,128)S(1)} %get-tuple-element.33.own_facts, bf16[1040,128]{1,0:T(8,128)(2,1)S(1)} %collective-permute-done.2.refs_0_, bf16[1056,128]{1,0:T(8,128)(2,1)S(1)} %get-tuple-element.43.refs_1_, ...), custom_call_target="tpu_custom_call", output_to_operand_aliasing={{}: (5, {})} | custom-call | tf_op jit(solution)/shard_map/gradients/pallas_call | solution.py:299
  36.6 0.0 collective-permute-done.10
  36.7 0.3 collective-permute-done.9.refs_3_
  37.0 0.0 collective-permute-done.8.refs_0_
  37.0 1.6 %collective-permute-start.14 = (bf16[1040,128]{1,0:T(8,128)(2,1)S(1)}, bf16[1040,128]{1,0:T(8,128)(2,1)S(1)}, u32[]{:S(2)}, u32[]{:S(2)}) collective-permute-start(bf16[1040,128]{1,0:T(8,128)(2,1)S(1)} %collective-permute-done.8.refs_0_), channel_id=1, source_target_pairs={{0,4},{4,8},{8,12},{12,14},{14,10},{10,6},{6,2},{2,0},{1,5},{5,9},... | collective-permute-start | bytes 798728 | tf_op jit(solution)/shard_map/ppermute | solution.py:417
  38.6 0.4 collective-permute-start.15
  39.0 1.4 %collective-permute-start.18 = (f32[24,128]{1,0:T(8,128)S(1)}, f32[24,128]{1,0:T(8,128)S(1)}, u32[]{:S(2)}, u32[]{:S(2)}) collective-permute-start(f32[24,128]{1,0:T(8,128)S(1)} %concatenate.3), channel_id=1, source_target_pairs={{0,6},{1,9},{4,2},{5,13},{8,0},{9,15},{12,4},{13,11},{14,8},{15,7}... | collective-permute-start | bytes 36872 | tf_op jit(solution)/shard_map/ppermute | solution.py:435
  40.4 0.0 collective-permute-done.11.refs_1_.onward
  40.4 1.0 %collective-permute-done.12.refs_2_.back = bf16[1056,128]{1,0:T(8,128)(2,1)S(1)} collective-permute-done((bf16[1056,128]{1,0:T(8,128)(2,1)S(1)}, bf16[1056,128]{1,0:T(8,128)(2,1)S(1)}, u32[]{:S(2)}, u32[]{:S(2)}) %collective-permute-start.12) | collective-permute-done | bytes 270368 | tf_op jit(solution)/shard_map/ppermute | solution.py:417
  41.4 0.8 %scores.6 = (f32[8,128]{1,0:T(8,128)S(1)}, f32[8,128]{1,0:T(8,128)S(1)}) custom-call(bf16[512,2048]{1,0:T(8,128)(2,1)S(1)} %fetch.1.decoder, f32[8,128]{1,0:T(8,128)S(1)} %get-tuple-element.33.own_facts, bf16[1040,128]{1,0:T(8,128)(2,1)S(1)} %collective-permute-done.8.refs_0_, bf16[1056,128]{1,0:T(8,128)(2,1)S(1)} %collective-permute-done.11.refs_1_.onward, ...), custom_call_target="tpu_custom_call" | custom-call | tf_op jit(solution)/shard_map/scores/pallas_call | solution.py:278
  42.2 0.1 collective-permute-start.13
  42.3 0.9 %gradients.5.total = f32[512,2048]{1,0:T(8,128)S(1)} custom-call(f32[8,128]{1,0:T(8,128)S(1)} %get-tuple-element.33.own_facts, bf16[1040,128]{1,0:T(8,128)(2,1)S(1)} %collective-permute-done.8.refs_0_, bf16[1056,128]{1,0:T(8,128)(2,1)S(1)} %collective-permute-done.11.refs_1_.onward, ...), custom_call_target="tpu_custom_call", output_to_operand_aliasing={{}: (5, {})} | custom-call | tf_op jit(solution)/shard_map/gradients/pallas_call | solution.py:299
  43.3 0.2 collective-permute-done.13
  43.5 3.5 %collective-permute-start.16 = (f32[8,128]{1,0:T(8,128)S(1)}, f32[8,128]{1,0:T(8,128)S(1)}, u32[]{:S(2)}, u32[]{:S(2)}) collective-permute-start(f32[8,128]{1,0:T(8,128)S(1)} %add.12), channel_id=1, source_target_pairs={{0,10},{1,13},{4,6},{5,15},{8,2},{9,11},{12,0},{13,7},{14,4},{15,3... | collective-permute-start | bytes 12296 | tf_op jit(solution)/shard_map/ppermute | solution.py:435
  47.0 0.0 collective-permute-done.15.right.refs_1_
  47.0 0.0 collective-permute-done.14.left.refs_0_
  47.0 0.7 %scores.7 = f32[8,128]{1,0:T(8,128)S(1)} custom-call(bf16[512,2048]{1,0:T(8,128)(2,1)S(1)} %fetch.1.decoder, f32[8,128]{1,0:T(8,128)S(1)} %get-tuple-element.33.own_facts, bf16[1040,128]{1,0:T(8,128)(2,1)S(1)} %collective-permute-done.14.left.refs_0_, bf16[1024,128]{1,0:T(8,128)(2,1)S(1)} %collective-permute-done.15.right.refs_1_), custom_call_target="tpu_custom_call" | custom-call | tf_op jit(solution)/shard_map/scores/pallas_call | solution.py:278
  47.7 3.7 %collective-permute-start.17 = (f32[8,128]{1,0:T(8,128)S(1)}, f32[8,128]{1,0:T(8,128)S(1)}, u32[]{:S(2)}, u32[]{:S(2)}) collective-permute-start(f32[8,128]{1,0:T(8,128)S(1)} %scores.7), channel_id=1, source_target_pairs={{0,14},{4,10},{8,6},{12,2},{14,0},{10,4},{6,8},{2,12},{1,15},{5,11... | collective-permute-start | bytes 12296 | tf_op jit(solution)/shard_map/ppermute | solution.py:417
  51.4 0.0 collective-permute-done.18
  51.4 0.0 collective-permute-done.16.third
  51.4 1.7 %last_gradients.1 = bf16[512,2048]{1,0:T(8,128)(2,1)} custom-call(bf16[1040,128]{1,0:T(8,128)(2,1)S(1)} %collective-permute-done.14.left.refs_0_, bf16[1024,128]{1,0:T(8,128)(2,1)S(1)} %collective-permute-done.15.right.refs_1_, f32[512,2048]{1,0:T(8,128)S(1)} %gradients.5.total), custom_call_target="tpu_custom_call" | custom-call | tf_op jit(solution)/shard_map/last_gradients/pallas_call | solution.py:326
  53.2 0.9 %collective-permute-done.17.opposite = f32[8,128]{1,0:T(8,128)S(1)} collective-permute-done((f32[8,128]{1,0:T(8,128)S(1)}, f32[8,128]{1,0:T(8,128)S(1)}, u32[]{:S(2)}, u32[]{:S(2)}) %collective-permute-start.17) | collective-permute-done | bytes 4128 | tf_op jit(solution)/shard_map/ppermute | solution.py:417
  54.1 0.2 collective-permute-start.19
  54.3 1.1 %collective-permute-done.19 = f32[32,128]{1,0:T(8,128)S(1)} collective-permute-done((f32[32,128]{1,0:T(8,128)S(1)}, f32[32,128]{1,0:T(8,128)S(1)}, u32[]{:S(2)}, u32[]{:S(2)}) %collective-permute-start.19) | collective-permute-done | bytes 16416 | tf_op jit(solution)/shard_map/ppermute | solution.py:428
  55.4 0.6 %add_bitcast_fusion = f32[128,32]{0,1:T(8,128)} fusion(f32[32,128]{1,0:T(8,128)S(1)} %unpack.1, f32[32,128]{1,0:T(8,128)S(1)} %collective-permute-done.19), kind=kLoop, calls=%fused_computation | loop fusion | flops 4096 | bytes 49152 | tf_op jit(solution)/shard_map/transpose | solution.py:474
  (5 shorter events, 0.0 us)
Async XLA Ops:
  1.8 12.3 %collective-permute-start = (bf16[1040,128]{1,0:T(8,128)(2,1)S(1)}, bf16[1040,128]{1,0:T(8,128)(2,1)S(1)}, u32[]{:S(2)}, u32[]{:S(2)}) collective-permute-start(bf16[1040,128]{1,0:T(8,128)(2,1)S(1)} %get-tuple-element.34.refs_0_), channel_id=1, source_target_pairs={{0,4},{4,8},{8,12},{12,14},{14,10},{10,6},{6,2},{2,0},{1,5},{5,9},... | collective-permute-start | bytes 798728 | tf_op jit(solution)/shard_map/ppermute | solution.py:417
  4.9 9.2 %collective-permute-start.1 = (bf16[1024,128]{1,0:T(8,128)(2,1)S(1)}, bf16[1024,128]{1,0:T(8,128)(2,1)S(1)}, u32[]{:S(2)}, u32[]{:S(2)}) collective-permute-start(bf16[1024,128]{1,0:T(8,128)(2,1)S(1)} %get-tuple-element.35.refs_1_), channel_id=1, source_target_pairs={{0,2},{4,0},{8,4},{12,8},{14,12},{10,14},{6,10},{2,6},{1,3},{5,1},... | collective-permute-start | bytes 786440 | tf_op jit(solution)/shard_map/ppermute | solution.py:417
  4.9 12.9 %collective-permute-start.3 = (bf16[1056,128]{1,0:T(8,128)(2,1)S(1)}, bf16[1056,128]{1,0:T(8,128)(2,1)S(1)}, u32[]{:S(2)}, u32[]{:S(2)}) collective-permute-start(bf16[1056,128]{1,0:T(8,128)(2,1)S(1)} %get-tuple-element.37), channel_id=1, source_target_pairs={{0,4},{4,8},{8,12},{12,14},{14,10},{10,6},{6,2},{2,0},{1,5},{5,9},... | collective-permute-start | bytes 811016 | tf_op jit(solution)/shard_map/ppermute | solution.py:417
  6.9 13.1 %collective-permute-start.5 = (bf16[1056,128]{1,0:T(8,128)(2,1)S(1)}, bf16[1056,128]{1,0:T(8,128)(2,1)S(1)}, u32[]{:S(2)}, u32[]{:S(2)}) collective-permute-start(bf16[1056,128]{1,0:T(8,128)(2,1)S(1)} %get-tuple-element.38), channel_id=1, source_target_pairs={{0,2},{4,0},{8,4},{12,8},{14,12},{10,14},{6,10},{2,6},{1,3},{5,1},... | collective-permute-start | bytes 811016 | tf_op jit(solution)/shard_map/ppermute | solution.py:417
  14.2 9.4 %collective-permute-start.2 = (bf16[1040,128]{1,0:T(8,128)(2,1)S(1)}, bf16[1040,128]{1,0:T(8,128)(2,1)S(1)}, u32[]{:S(2)}, u32[]{:S(2)}) collective-permute-start(bf16[1040,128]{1,0:T(8,128)(2,1)S(1)} %collective-permute-done.refs_2_), channel_id=1, source_target_pairs={{0,4},{4,8},{8,12},{12,14},{14,10},{10,6},{6,2},{2,0},{1,5},{5,9},... | collective-permute-start | bytes 798728 | tf_op jit(solution)/shard_map/ppermute | solution.py:417
  15.7 10.0 %collective-permute-start.7 = (bf16[1024,128]{1,0:T(8,128)(2,1)S(1)}, bf16[1024,128]{1,0:T(8,128)(2,1)S(1)}, u32[]{:S(2)}, u32[]{:S(2)}) collective-permute-start(bf16[1024,128]{1,0:T(8,128)(2,1)S(1)} %collective-permute-done.1.refs_5_), channel_id=1, source_target_pairs={{0,2},{4,0},{8,4},{12,8},{14,12},{10,14},{6,10},{2,6},{1,3},{5,1},... | collective-permute-start | bytes 786440 | tf_op jit(solution)/shard_map/ppermute | solution.py:417
  17.8 11.5 %collective-permute-start.4 = (bf16[1056,128]{1,0:T(8,128)(2,1)S(1)}, bf16[1056,128]{1,0:T(8,128)(2,1)S(1)}, u32[]{:S(2)}, u32[]{:S(2)}) collective-permute-start(bf16[1056,128]{1,0:T(8,128)(2,1)S(1)} %collective-permute-done.3.refs_3_), channel_id=1, source_target_pairs={{0,4},{4,8},{8,12},{12,14},{14,10},{10,6},{6,2},{2,0},{1,5},{5,9},... | collective-permute-start | bytes 811016 | tf_op jit(solution)/shard_map/ppermute | solution.py:417
  20.0 11.4 %collective-permute-start.6 = (bf16[1056,128]{1,0:T(8,128)(2,1)S(1)}, bf16[1056,128]{1,0:T(8,128)(2,1)S(1)}, u32[]{:S(2)}, u32[]{:S(2)}) collective-permute-start(bf16[1056,128]{1,0:T(8,128)(2,1)S(1)} %collective-permute-done.5.refs_4_), channel_id=1, source_target_pairs={{0,2},{4,0},{8,4},{12,8},{14,12},{10,14},{6,10},{2,6},{1,3},{5,1},... | collective-permute-start | bytes 811016 | tf_op jit(solution)/shard_map/ppermute | solution.py:417
  23.6 13.4 %collective-permute-start.8 = (bf16[1040,128]{1,0:T(8,128)(2,1)S(1)}, bf16[1040,128]{1,0:T(8,128)(2,1)S(1)}, u32[]{:S(2)}, u32[]{:S(2)}) collective-permute-start(bf16[1040,128]{1,0:T(8,128)(2,1)S(1)} %collective-permute-done.2.refs_0_), channel_id=1, source_target_pairs={{0,4},{4,8},{8,12},{12,14},{14,10},{10,6},{6,2},{2,0},{1,5},{5,9},... | collective-permute-start | bytes 798728 | tf_op jit(solution)/shard_map/ppermute | solution.py:417
  25.7 11.3 %collective-permute-start.9 = (bf16[1024,128]{1,0:T(8,128)(2,1)S(1)}, bf16[1024,128]{1,0:T(8,128)(2,1)S(1)}, u32[]{:S(2)}, u32[]{:S(2)}) collective-permute-start(bf16[1024,128]{1,0:T(8,128)(2,1)S(1)} %collective-permute-done.7.refs_3_), channel_id=1, source_target_pairs={{0,2},{4,0},{8,4},{12,8},{14,12},{10,14},{6,10},{2,6},{1,3},{5,1},... | collective-permute-start | bytes 786440 | tf_op jit(solution)/shard_map/ppermute | solution.py:417
  31.4 9.0 %collective-permute-start.11 = (bf16[1056,128]{1,0:T(8,128)(2,1)S(1)}, bf16[1056,128]{1,0:T(8,128)(2,1)S(1)}, u32[]{:S(2)}, u32[]{:S(2)}) collective-permute-start(bf16[1056,128]{1,0:T(8,128)(2,1)S(1)} %get-tuple-element.43.refs_1_), channel_id=1, source_target_pairs={{0,4},{4,8},{8,12},{12,14},{14,10},{10,6},{6,2},{2,0},{1,5},{5,9},... | collective-permute-start | bytes 811016 | tf_op jit(solution)/shard_map/ppermute | solution.py:417
  33.1 8.3 %collective-permute-start.12 = (bf16[1056,128]{1,0:T(8,128)(2,1)S(1)}, bf16[1056,128]{1,0:T(8,128)(2,1)S(1)}, u32[]{:S(2)}, u32[]{:S(2)}) collective-permute-start(bf16[1056,128]{1,0:T(8,128)(2,1)S(1)} %get-tuple-element.44.refs_2_), channel_id=1, source_target_pairs={{0,2},{4,0},{8,4},{12,8},{14,12},{10,14},{6,10},{2,6},{1,3},{5,1},... | collective-permute-start | bytes 811016 | tf_op jit(solution)/shard_map/ppermute | solution.py:417
  34.3 2.3 %collective-permute-start.10 = (f32[8,128]{1,0:T(8,128)S(1)}, f32[8,128]{1,0:T(8,128)S(1)}, u32[]{:S(2)}, u32[]{:S(2)}) collective-permute-start(f32[8,128]{1,0:T(8,128)S(1)} %get-tuple-element.46), channel_id=1, source_target_pairs={{0,1},{1,0},{2,3},{3,2},{4,5},{5,4},{6,7},{7,6},{8,9},{9,8},{10,11... | collective-permute-start | bytes 12296 | tf_op jit(solution)/shard_map/ppermute | solution.py:428
  37.0 10.0 %collective-permute-start.14 = (bf16[1040,128]{1,0:T(8,128)(2,1)S(1)}, bf16[1040,128]{1,0:T(8,128)(2,1)S(1)}, u32[]{:S(2)}, u32[]{:S(2)}) collective-permute-start(bf16[1040,128]{1,0:T(8,128)(2,1)S(1)} %collective-permute-done.8.refs_0_), channel_id=1, source_target_pairs={{0,4},{4,8},{8,12},{12,14},{14,10},{10,6},{6,2},{2,0},{1,5},{5,9},... | collective-permute-start | bytes 798728 | tf_op jit(solution)/shard_map/ppermute | solution.py:417
  38.6 8.5 %collective-permute-start.15 = (bf16[1024,128]{1,0:T(8,128)(2,1)S(1)}, bf16[1024,128]{1,0:T(8,128)(2,1)S(1)}, u32[]{:S(2)}, u32[]{:S(2)}) collective-permute-start(bf16[1024,128]{1,0:T(8,128)(2,1)S(1)} %collective-permute-done.9.refs_3_), channel_id=1, source_target_pairs={{0,2},{4,0},{8,4},{12,8},{14,12},{10,14},{6,10},{2,6},{1,3},{5,1},... | collective-permute-start | bytes 786440 | tf_op jit(solution)/shard_map/ppermute | solution.py:417
  39.0 12.4 %collective-permute-start.18 = (f32[24,128]{1,0:T(8,128)S(1)}, f32[24,128]{1,0:T(8,128)S(1)}, u32[]{:S(2)}, u32[]{:S(2)}) collective-permute-start(f32[24,128]{1,0:T(8,128)S(1)} %concatenate.3), channel_id=1, source_target_pairs={{0,6},{1,9},{4,2},{5,13},{8,0},{9,15},{12,4},{13,11},{14,8},{15,7}... | collective-permute-start | bytes 36872 | tf_op jit(solution)/shard_map/ppermute | solution.py:435
  42.2 1.2 %collective-permute-start.13 = (f32[8,128]{1,0:T(8,128)S(1)}, f32[8,128]{1,0:T(8,128)S(1)}, u32[]{:S(2)}, u32[]{:S(2)}) collective-permute-start(f32[8,128]{1,0:T(8,128)S(1)} %get-tuple-element.51), channel_id=1, source_target_pairs={{0,1},{1,0},{2,3},{3,2},{4,5},{5,4},{6,7},{7,6},{8,9},{9,8},{10,11... | collective-permute-start | bytes 12296 | tf_op jit(solution)/shard_map/ppermute | solution.py:428
  43.5 8.0 %collective-permute-start.16 = (f32[8,128]{1,0:T(8,128)S(1)}, f32[8,128]{1,0:T(8,128)S(1)}, u32[]{:S(2)}, u32[]{:S(2)}) collective-permute-start(f32[8,128]{1,0:T(8,128)S(1)} %add.12), channel_id=1, source_target_pairs={{0,10},{1,13},{4,6},{5,15},{8,2},{9,11},{12,0},{13,7},{14,4},{15,3... | collective-permute-start | bytes 12296 | tf_op jit(solution)/shard_map/ppermute | solution.py:435
  47.7 6.4 %collective-permute-start.17 = (f32[8,128]{1,0:T(8,128)S(1)}, f32[8,128]{1,0:T(8,128)S(1)}, u32[]{:S(2)}, u32[]{:S(2)}) collective-permute-start(f32[8,128]{1,0:T(8,128)S(1)} %scores.7), channel_id=1, source_target_pairs={{0,14},{4,10},{8,6},{12,2},{14,0},{10,4},{6,8},{2,12},{1,15},{5,11... | collective-permute-start | bytes 12296 | tf_op jit(solution)/shard_map/ppermute | solution.py:417
  54.1 1.2 %collective-permute-start.19 = (f32[32,128]{1,0:T(8,128)S(1)}, f32[32,128]{1,0:T(8,128)S(1)}, u32[]{:S(2)}, u32[]{:S(2)}) collective-permute-start(f32[32,128]{1,0:T(8,128)S(1)} %unpack.1), channel_id=1, source_target_pairs={{0,1},{1,0},{2,3},{3,2},{4,5},{5,4},{6,7},{7,6},{8,9},{9,8},{10,11... | collective-permute-start | bytes 49160 | tf_op jit(solution)/shard_map/ppermute | solution.py:428

commit v28 on v22

--- a/solution.py
+++ b/solution.py
@@ -457,7 +457,7 @@
     total = gradients_of((-2, 2), pairs, own_facts, decoder.shape, total)
     second = mine + other_core(others)
     total, first_3, second = lax.optimization_barrier((total, first_3, second))
-    second = return_by(2, jnp.concatenate([second, jnp.zeros((24, 128), jnp.float32)]))[:8]
+    second = return_by(2, jnp.concatenate([second, jnp.zeros((16, 128), jnp.float32)]))[:8]
     first_4 = hop(first_3)
     pairs = [(first_3[0], second_3[0]), (second_3[1], first_3[1])]
     mine, others = scores_of((-3, 3), pairs, decoder, own_facts, True)

time: 56.3 us -> 56.3 us (level)
  no operation moved by 1% of the time
where the time goes in v28:
time: 56.3 us; the launch traced here: 56.1 us
  starting transfers between devices  24.7 us (44%)
  waiting for transfers between devices  18.5 us (33%)
  Pallas kernels  11.5 us (20%)
  between operations  0.77 us (1%)
  other arithmetic  0.62 us (1%)
    ppermute x15, starting transfers between devices, shift(): return lax.ppermute(x, 'dp', pairs)  19.2 us
    ppermute x15, waiting for transfers between devices, shift(): return lax.ppermute(x, 'dp', pairs)  17.2 us
    ppermute x2, starting transfers between devices, return_by(): return lax.ppermute(x, ('dp', 'width'), pairs)  5.25 us
    pallas_call x4, Pallas kernels, scores_of(): pl.pallas_call(functools.partial(scores_kernel, distances, split), out_sh...  3.72 us
    pallas_call x3, Pallas kernels, gradients_of(): pl.pallas_call(functools.partial(gradients_kernel, distances), out_shape=...  3.14 us
    pallas_call x1, Pallas kernels, last_gradients(): pl.pallas_call(last_gradients_kernel, out_shape=jax.ShapeDtypeStruct(tota...  1.76 us
    pallas_call x1, Pallas kernels, fetch(): pl.pallas_call(fetch_kernel, out_shape=pltpu.VMEM(x.shape, x.dtype), in_s...  1.6 us
    ppermute x3, waiting for transfers between devices, other_core(): return lax.ppermute(x, 'width', ((0, 1), (1, 0)))  1.28 us
  transfers between devices with their start and end apart: 20, of which 10 were waited for; matrix products, arithmetic and copies ran while one was open for 0% of the time, Pallas kernels for 18%

profile of v28, /device:TPU:0, one launch (start us, length us, event | category | flops | bytes accessed | tf_op | source)
XLA Modules:
  0.0 56.1 jit_solution(1758212056071291111)
XLA Ops:
  0.6 1.2 %prepare.1 = (bf16[1040,128]{1,0:T(8,128)(2,1)S(1)}, bf16[1024,128]{1,0:T(8,128)(2,1)S(1)}, bf16[1056,128]{1,0:T(8,128)(2,1)S(1)}, bf16[1056,128]{1,0:T(8,128)(2...) custom-call(s32[32]{0:T(128)} %refs_0_.1, s32[8,128]{1,0:T(8,128)} %bitcast.7, s32[32,128]{1,0:T(8,128)} %bitcast.5, ...), custom_call_target="tpu_custom_call" | custom-call | tf_op jit(solution)/shard_map/prepare/pallas_call | solution.py:126
  1.8 3.0 %collective-permute-start = (bf16[1040,128]{1,0:T(8,128)(2,1)S(1)}, bf16[1040,128]{1,0:T(8,128)(2,1)S(1)}, u32[]{:S(2)}, u32[]{:S(2)}) collective-permute-start(bf16[1040,128]{1,0:T(8,128)(2,1)S(1)} %get-tuple-element.34.refs_0_), channel_id=1, source_target_pairs={{0,2},{2,6},{6,10},{10,14},{14,12},{12,8},{8,4},{4,0},{1,3},{3,7},... | collective-permute-start | bytes 798728 | tf_op jit(solution)/shard_map/ppermute | solution.py:419
  4.8 0.2 collective-permute-start.1
  5.0 1.9 %collective-permute-start.3 = (bf16[1056,128]{1,0:T(8,128)(2,1)S(1)}, bf16[1056,128]{1,0:T(8,128)(2,1)S(1)}, u32[]{:S(2)}, u32[]{:S(2)}) collective-permute-start(bf16[1056,128]{1,0:T(8,128)(2,1)S(1)} %get-tuple-element.37), channel_id=1, source_target_pairs={{0,2},{2,6},{6,10},{10,14},{14,12},{12,8},{8,4},{4,0},{1,3},{3,7},... | collective-permute-start | bytes 811016 | tf_op jit(solution)/shard_map/ppermute | solution.py:419
  6.9 0.2 collective-permute-start.5
  7.0 1.6 %fetch.1.decoder = bf16[512,2048]{1,0:T(8,128)(2,1)S(1)} custom-call(bf16[512,2048]{1,0:T(8,128)(2,1)} %source.1), custom_call_target="tpu_custom_call" | custom-call | tf_op jit(solution)/shard_map/fetch/pallas_call | solution.py:160
  8.6 5.4 %collective-permute-done.1.refs_5_ = bf16[1024,128]{1,0:T(8,128)(2,1)S(1)} collective-permute-done((bf16[1024,128]{1,0:T(8,128)(2,1)S(1)}, bf16[1024,128]{1,0:T(8,128)(2,1)S(1)}, u32[]{:S(2)}, u32[]{:S(2)}) %collective-permute-start.1) | collective-permute-done | bytes 262176 | tf_op jit(solution)/shard_map/ppermute | solution.py:419
  14.1 0.0 collective-permute-done.refs_2_
  14.1 1.6 %collective-permute-start.2 = (bf16[1040,128]{1,0:T(8,128)(2,1)S(1)}, bf16[1040,128]{1,0:T(8,128)(2,1)S(1)}, u32[]{:S(2)}, u32[]{:S(2)}) collective-permute-start(bf16[1040,128]{1,0:T(8,128)(2,1)S(1)} %collective-permute-done.refs_2_), channel_id=1, source_target_pairs={{0,2},{2,6},{6,10},{10,14},{14,12},{12,8},{8,4},{4,0},{1,3},{3,7},... | collective-permute-start | bytes 798728 | tf_op jit(solution)/shard_map/ppermute | solution.py:419
  15.6 0.4 collective-permute-start.7
  16.1 1.8 %collective-permute-done.3.refs_3_ = bf16[1056,128]{1,0:T(8,128)(2,1)S(1)} collective-permute-done((bf16[1056,128]{1,0:T(8,128)(2,1)S(1)}, bf16[1056,128]{1,0:T(8,128)(2,1)S(1)}, u32[]{:S(2)}, u32[]{:S(2)}) %collective-permute-start.3) | collective-permute-done | bytes 270368 | tf_op jit(solution)/shard_map/ppermute | solution.py:419
  17.9 2.0 %collective-permute-start.4 = (bf16[1056,128]{1,0:T(8,128)(2,1)S(1)}, bf16[1056,128]{1,0:T(8,128)(2,1)S(1)}, u32[]{:S(2)}, u32[]{:S(2)}) collective-permute-start(bf16[1056,128]{1,0:T(8,128)(2,1)S(1)} %collective-permute-done.3.refs_3_), channel_id=1, source_target_pairs={{0,2},{2,6},{6,10},{10,14},{14,12},{12,8},{8,4},{4,0},{1,3},{3,7},... | collective-permute-start | bytes 811016 | tf_op jit(solution)/shard_map/ppermute | solution.py:419
  19.9 0.0 collective-permute-done.5.refs_4_
  19.9 0.1 collective-permute-start.6
  20.0 3.6 %collective-permute-done.2.refs_0_ = bf16[1040,128]{1,0:T(8,128)(2,1)S(1)} collective-permute-done((bf16[1040,128]{1,0:T(8,128)(2,1)S(1)}, bf16[1040,128]{1,0:T(8,128)(2,1)S(1)}, u32[]{:S(2)}, u32[]{:S(2)}) %collective-permute-start.2) | collective-permute-done | bytes 266272 | tf_op jit(solution)/shard_map/ppermute | solution.py:419
  23.6 2.0 %collective-permute-start.8 = (bf16[1040,128]{1,0:T(8,128)(2,1)S(1)}, bf16[1040,128]{1,0:T(8,128)(2,1)S(1)}, u32[]{:S(2)}, u32[]{:S(2)}) collective-permute-start(bf16[1040,128]{1,0:T(8,128)(2,1)S(1)} %collective-permute-done.2.refs_0_), channel_id=1, source_target_pairs={{0,2},{2,6},{6,10},{10,14},{14,12},{12,8},{8,4},{4,0},{1,3},{3,7},... | collective-permute-start | bytes 798728 | tf_op jit(solution)/shard_map/ppermute | solution.py:419
  25.6 0.0 collective-permute-done.7.refs_3_
  25.6 0.1 collective-permute-start.9
  25.7 1.4 %scores.4 = (f32[8,128]{1,0:T(8,128)S(1)}, f32[8,128]{1,0:T(8,128)S(1)}, f32[8,128]{1,0:T(8,128)S(1)}) custom-call(bf16[512,2048]{1,0:T(8,128)(2,1)S(1)} %fetch.1.decoder, f32[8,128]{1,0:T(8,128)S(1)} %get-tuple-element.33.own_facts, bf16[1040,128]{1,0:T(8,128)(2,1)S(1)} %get-tuple-element.34.refs_0_, bf16[1024,128]{1,0:T(8,128)(2,1)S(1)} %get-tuple-element.35.refs_1_, ...), custom_call_target="tpu_custom_call" | custom-call | tf_op jit(solution)/shard_map/scores/pallas_call | solution.py:280
  27.1 2.4 %collective-permute-done.4.onward = bf16[1056,128]{1,0:T(8,128)(2,1)S(1)} collective-permute-done((bf16[1056,128]{1,0:T(8,128)(2,1)S(1)}, bf16[1056,128]{1,0:T(8,128)(2,1)S(1)}, u32[]{:S(2)}, u32[]{:S(2)}) %collective-permute-start.4) | collective-permute-done | bytes 270368 | tf_op jit(solution)/shard_map/ppermute | solution.py:419
  29.4 1.8 %collective-permute-done.6.back = bf16[1056,128]{1,0:T(8,128)(2,1)S(1)} collective-permute-done((bf16[1056,128]{1,0:T(8,128)(2,1)S(1)}, bf16[1056,128]{1,0:T(8,128)(2,1)S(1)}, u32[]{:S(2)}, u32[]{:S(2)}) %collective-permute-start.6) | collective-permute-done | bytes 270368 | tf_op jit(solution)/shard_map/ppermute | solution.py:419
  31.3 0.1 stamp.1
  31.3 1.6 %collective-permute-start.11 = (bf16[1056,128]{1,0:T(8,128)(2,1)S(1)}, bf16[1056,128]{1,0:T(8,128)(2,1)S(1)}, u32[]{:S(2)}, u32[]{:S(2)}) collective-permute-start(bf16[1056,128]{1,0:T(8,128)(2,1)S(1)} %get-tuple-element.43.refs_1_), channel_id=1, source_target_pairs={{0,2},{2,6},{6,10},{10,14},{14,12},{12,8},{8,4},{4,0},{1,3},{3,7},... | collective-permute-start | bytes 811016 | tf_op jit(solution)/shard_map/ppermute | solution.py:419
  33.0 0.4 collective-permute-start.12
  33.4 0.8 %scores.5 = (f32[8,128]{1,0:T(8,128)S(1)}, f32[8,128]{1,0:T(8,128)S(1)}) custom-call(bf16[512,2048]{1,0:T(8,128)(2,1)S(1)} %fetch.1.decoder, f32[8,128]{1,0:T(8,128)S(1)} %get-tuple-element.33.own_facts, bf16[1040,128]{1,0:T(8,128)(2,1)S(1)} %collective-permute-done.2.refs_0_, bf16[1056,128]{1,0:T(8,128)(2,1)S(1)} %get-tuple-element.43.refs_1_, ...), custom_call_target="tpu_custom_call" | custom-call | tf_op jit(solution)/shard_map/scores/pallas_call | solution.py:280
  34.3 0.1 collective-permute-start.10
  34.3 1.3 %gradients.3.refs_4_ = f32[512,2048]{1,0:T(8,128)S(1)} custom-call(f32[8,128]{1,0:T(8,128)S(1)} %get-tuple-element.33.own_facts, bf16[1040,128]{1,0:T(8,128)(2,1)S(1)} %get-tuple-element.34.refs_0_, bf16[1024,128]{1,0:T(8,128)(2,1)S(1)} %get-tuple-element.35.refs_1_, bf16[1040,128]{1,0:T(8,128)(2,1)S(1)} %collective-permute-done.refs_2_, ...), custom_call_target="tpu_custom_call" | custom-call | tf_op jit(solution)/shard_map/gradients/pallas_call | solution.py:301
  35.6 0.9 %gradients.4.refs_4_ = f32[512,2048]{1,0:T(8,128)S(1)} custom-call(f32[8,128]{1,0:T(8,128)S(1)} %get-tuple-element.33.own_facts, bf16[1040,128]{1,0:T(8,128)(2,1)S(1)} %collective-permute-done.2.refs_0_, bf16[1056,128]{1,0:T(8,128)(2,1)S(1)} %get-tuple-element.43.refs_1_, ...), custom_call_target="tpu_custom_call", output_to_operand_aliasing={{}: (5, {})} | custom-call | tf_op jit(solution)/shard_map/gradients/pallas_call | solution.py:301
  36.6 0.0 collective-permute-done.10
  36.6 0.3 collective-permute-done.9.refs_3_
  36.9 0.0 collective-permute-done.8.refs_0_
  36.9 1.6 %collective-permute-start.14 = (bf16[1040,128]{1,0:T(8,128)(2,1)S(1)}, bf16[1040,128]{1,0:T(8,128)(2,1)S(1)}, u32[]{:S(2)}, u32[]{:S(2)}) collective-permute-start(bf16[1040,128]{1,0:T(8,128)(2,1)S(1)} %collective-permute-done.8.refs_0_), channel_id=1, source_target_pairs={{0,2},{2,6},{6,10},{10,14},{14,12},{12,8},{8,4},{4,0},{1,3},{3,7},... | collective-permute-start | bytes 798728 | tf_op jit(solution)/shard_map/ppermute | solution.py:419
  38.5 0.4 collective-permute-start.15
  38.9 1.5 %collective-permute-start.18 = (f32[24,128]{1,0:T(8,128)S(1)}, f32[24,128]{1,0:T(8,128)S(1)}, u32[]{:S(2)}, u32[]{:S(2)}) collective-permute-start(f32[24,128]{1,0:T(8,128)S(1)} %concatenate.3), channel_id=1, source_target_pairs={{0,8},{1,7},{2,4},{3,11},{6,0},{7,15},{10,2},{11,13},{14,6},{15,9}... | collective-permute-start | bytes 36872 | tf_op jit(solution)/shard_map/ppermute | solution.py:437
  40.5 0.0 collective-permute-done.11.refs_1_.onward
  40.5 0.9 %collective-permute-done.12.refs_2_.back = bf16[1056,128]{1,0:T(8,128)(2,1)S(1)} collective-permute-done((bf16[1056,128]{1,0:T(8,128)(2,1)S(1)}, bf16[1056,128]{1,0:T(8,128)(2,1)S(1)}, u32[]{:S(2)}, u32[]{:S(2)}) %collective-permute-start.12) | collective-permute-done | bytes 270368 | tf_op jit(solution)/shard_map/ppermute | solution.py:419
  41.3 0.8 %scores.6 = (f32[8,128]{1,0:T(8,128)S(1)}, f32[8,128]{1,0:T(8,128)S(1)}) custom-call(bf16[512,2048]{1,0:T(8,128)(2,1)S(1)} %fetch.1.decoder, f32[8,128]{1,0:T(8,128)S(1)} %get-tuple-element.33.own_facts, bf16[1040,128]{1,0:T(8,128)(2,1)S(1)} %collective-permute-done.8.refs_0_, bf16[1056,128]{1,0:T(8,128)(2,1)S(1)} %collective-permute-done.11.refs_1_.onward, ...), custom_call_target="tpu_custom_call" | custom-call | tf_op jit(solution)/shard_map/scores/pallas_call | solution.py:280
  42.2 0.1 collective-permute-start.13
  42.2 0.9 %gradients.5.total = f32[512,2048]{1,0:T(8,128)S(1)} custom-call(f32[8,128]{1,0:T(8,128)S(1)} %get-tuple-element.33.own_facts, bf16[1040,128]{1,0:T(8,128)(2,1)S(1)} %collective-permute-done.8.refs_0_, bf16[1056,128]{1,0:T(8,128)(2,1)S(1)} %collective-permute-done.11.refs_1_.onward, ...), custom_call_target="tpu_custom_call", output_to_operand_aliasing={{}: (5, {})} | custom-call | tf_op jit(solution)/shard_map/gradients/pallas_call | solution.py:301
  43.2 0.2 collective-permute-done.13
  43.4 3.7 %collective-permute-start.16 = (f32[8,128]{1,0:T(8,128)S(1)}, f32[8,128]{1,0:T(8,128)S(1)}, u32[]{:S(2)}, u32[]{:S(2)}) collective-permute-start(f32[8,128]{1,0:T(8,128)S(1)} %add.12), channel_id=1, source_target_pairs={{0,12},{1,11},{2,8},{3,15},{6,4},{7,13},{10,0},{11,9},{14,2},{15,5... | collective-permute-start | bytes 12296 | tf_op jit(solution)/shard_map/ppermute | solution.py:437
  47.1 0.0 collective-permute-done.15.right.refs_1_
  47.1 0.0 collective-permute-done.14.left.refs_0_
  47.1 0.7 %scores.7 = f32[8,128]{1,0:T(8,128)S(1)} custom-call(bf16[512,2048]{1,0:T(8,128)(2,1)S(1)} %fetch.1.decoder, f32[8,128]{1,0:T(8,128)S(1)} %get-tuple-element.33.own_facts, bf16[1040,128]{1,0:T(8,128)(2,1)S(1)} %collective-permute-done.14.left.refs_0_, bf16[1024,128]{1,0:T(8,128)(2,1)S(1)} %collective-permute-done.15.right.refs_1_), custom_call_target="tpu_custom_call" | custom-call | tf_op jit(solution)/shard_map/scores/pallas_call | solution.py:280
  47.8 3.7 %collective-permute-start.17 = (f32[8,128]{1,0:T(8,128)S(1)}, f32[8,128]{1,0:T(8,128)S(1)}, u32[]{:S(2)}, u32[]{:S(2)}) collective-permute-start(f32[8,128]{1,0:T(8,128)S(1)} %scores.7), channel_id=1, source_target_pairs={{0,14},{2,12},{6,8},{10,4},{14,0},{12,2},{8,6},{4,10},{1,15},{3,13... | collective-permute-start | bytes 12296 | tf_op jit(solution)/shard_map/ppermute | solution.py:419
  51.6 0.0 collective-permute-done.18
  51.6 0.0 collective-permute-done.16.third
  51.6 1.8 %last_gradients.1 = bf16[512,2048]{1,0:T(8,128)(2,1)} custom-call(bf16[1040,128]{1,0:T(8,128)(2,1)S(1)} %collective-permute-done.14.left.refs_0_, bf16[1024,128]{1,0:T(8,128)(2,1)S(1)} %collective-permute-done.15.right.refs_1_, f32[512,2048]{1,0:T(8,128)S(1)} %gradients.5.total), custom_call_target="tpu_custom_call" | custom-call | tf_op jit(solution)/shard_map/last_gradients/pallas_call | solution.py:328
  53.3 0.9 %collective-permute-done.17.opposite = f32[8,128]{1,0:T(8,128)S(1)} collective-permute-done((f32[8,128]{1,0:T(8,128)S(1)}, f32[8,128]{1,0:T(8,128)S(1)}, u32[]{:S(2)}, u32[]{:S(2)}) %collective-permute-start.17) | collective-permute-done | bytes 4128 | tf_op jit(solution)/shard_map/ppermute | solution.py:419
  54.2 0.2 collective-permute-start.19
  54.4 1.1 %collective-permute-done.19 = f32[32,128]{1,0:T(8,128)S(1)} collective-permute-done((f32[32,128]{1,0:T(8,128)S(1)}, f32[32,128]{1,0:T(8,128)S(1)}, u32[]{:S(2)}, u32[]{:S(2)}) %collective-permute-start.19) | collective-permute-done | bytes 16416 | tf_op jit(solution)/shard_map/ppermute | solution.py:430
  55.5 0.6 %add_bitcast_fusion = f32[128,32]{0,1:T(8,128)} fusion(f32[32,128]{1,0:T(8,128)S(1)} %unpack.1, f32[32,128]{1,0:T(8,128)S(1)} %collective-permute-done.19), kind=kLoop, calls=%fused_computation | loop fusion | flops 4096 | bytes 49152 | tf_op jit(solution)/shard_map/transpose | solution.py:476
  (5 shorter events, 0.1 us)
Async XLA Ops:
  1.8 12.2 %collective-permute-start = (bf16[1040,128]{1,0:T(8,128)(2,1)S(1)}, bf16[1040,128]{1,0:T(8,128)(2,1)S(1)}, u32[]{:S(2)}, u32[]{:S(2)}) collective-permute-start(bf16[1040,128]{1,0:T(8,128)(2,1)S(1)} %get-tuple-element.34.refs_0_), channel_id=1, source_target_pairs={{0,2},{2,6},{6,10},{10,14},{14,12},{12,8},{8,4},{4,0},{1,3},{3,7},... | collective-permute-start | bytes 798728 | tf_op jit(solution)/shard_map/ppermute | solution.py:419
  4.8 9.2 %collective-permute-start.1 = (bf16[1024,128]{1,0:T(8,128)(2,1)S(1)}, bf16[1024,128]{1,0:T(8,128)(2,1)S(1)}, u32[]{:S(2)}, u32[]{:S(2)}) collective-permute-start(bf16[1024,128]{1,0:T(8,128)(2,1)S(1)} %get-tuple-element.35.refs_1_), channel_id=1, source_target_pairs={{0,4},{2,0},{6,2},{10,6},{14,10},{12,14},{8,12},{4,8},{1,5},{3,1},... | collective-permute-start | bytes 786440 | tf_op jit(solution)/shard_map/ppermute | solution.py:419
  5.0 12.9 %collective-permute-start.3 = (bf16[1056,128]{1,0:T(8,128)(2,1)S(1)}, bf16[1056,128]{1,0:T(8,128)(2,1)S(1)}, u32[]{:S(2)}, u32[]{:S(2)}) collective-permute-start(bf16[1056,128]{1,0:T(8,128)(2,1)S(1)} %get-tuple-element.37), channel_id=1, source_target_pairs={{0,2},{2,6},{6,10},{10,14},{14,12},{12,8},{8,4},{4,0},{1,3},{3,7},... | collective-permute-start | bytes 811016 | tf_op jit(solution)/shard_map/ppermute | solution.py:419
  6.9 13.1 %collective-permute-start.5 = (bf16[1056,128]{1,0:T(8,128)(2,1)S(1)}, bf16[1056,128]{1,0:T(8,128)(2,1)S(1)}, u32[]{:S(2)}, u32[]{:S(2)}) collective-permute-start(bf16[1056,128]{1,0:T(8,128)(2,1)S(1)} %get-tuple-element.38), channel_id=1, source_target_pairs={{0,4},{2,0},{6,2},{10,6},{14,10},{12,14},{8,12},{4,8},{1,5},{3,1},... | collective-permute-start | bytes 811016 | tf_op jit(solution)/shard_map/ppermute | solution.py:419
  14.1 9.6 %collective-permute-start.2 = (bf16[1040,128]{1,0:T(8,128)(2,1)S(1)}, bf16[1040,128]{1,0:T(8,128)(2,1)S(1)}, u32[]{:S(2)}, u32[]{:S(2)}) collective-permute-start(bf16[1040,128]{1,0:T(8,128)(2,1)S(1)} %collective-permute-done.refs_2_), channel_id=1, source_target_pairs={{0,2},{2,6},{6,10},{10,14},{14,12},{12,8},{8,4},{4,0},{1,3},{3,7},... | collective-permute-start | bytes 798728 | tf_op jit(solution)/shard_map/ppermute | solution.py:419
  15.6 10.0 %collective-permute-start.7 = (bf16[1024,128]{1,0:T(8,128)(2,1)S(1)}, bf16[1024,128]{1,0:T(8,128)(2,1)S(1)}, u32[]{:S(2)}, u32[]{:S(2)}) collective-permute-start(bf16[1024,128]{1,0:T(8,128)(2,1)S(1)} %collective-permute-done.1.refs_5_), channel_id=1, source_target_pairs={{0,4},{2,0},{6,2},{10,6},{14,10},{12,14},{8,12},{4,8},{1,5},{3,1},... | collective-permute-start | bytes 786440 | tf_op jit(solution)/shard_map/ppermute | solution.py:419
  17.9 11.5 %collective-permute-start.4 = (bf16[1056,128]{1,0:T(8,128)(2,1)S(1)}, bf16[1056,128]{1,0:T(8,128)(2,1)S(1)}, u32[]{:S(2)}, u32[]{:S(2)}) collective-permute-start(bf16[1056,128]{1,0:T(8,128)(2,1)S(1)} %collective-permute-done.3.refs_3_), channel_id=1, source_target_pairs={{0,2},{2,6},{6,10},{10,14},{14,12},{12,8},{8,4},{4,0},{1,3},{3,7},... | collective-permute-start | bytes 811016 | tf_op jit(solution)/shard_map/ppermute | solution.py:419
  19.9 11.4 %collective-permute-start.6 = (bf16[1056,128]{1,0:T(8,128)(2,1)S(1)}, bf16[1056,128]{1,0:T(8,128)(2,1)S(1)}, u32[]{:S(2)}, u32[]{:S(2)}) collective-permute-start(bf16[1056,128]{1,0:T(8,128)(2,1)S(1)} %collective-permute-done.5.refs_4_), channel_id=1, source_target_pairs={{0,4},{2,0},{6,2},{10,6},{14,10},{12,14},{8,12},{4,8},{1,5},{3,1},... | collective-permute-start | bytes 811016 | tf_op jit(solution)/shard_map/ppermute | solution.py:419
  23.6 13.2 %collective-permute-start.8 = (bf16[1040,128]{1,0:T(8,128)(2,1)S(1)}, bf16[1040,128]{1,0:T(8,128)(2,1)S(1)}, u32[]{:S(2)}, u32[]{:S(2)}) collective-permute-start(bf16[1040,128]{1,0:T(8,128)(2,1)S(1)} %collective-permute-done.2.refs_0_), channel_id=1, source_target_pairs={{0,2},{2,6},{6,10},{10,14},{14,12},{12,8},{8,4},{4,0},{1,3},{3,7},... | collective-permute-start | bytes 798728 | tf_op jit(solution)/shard_map/ppermute | solution.py:419
  25.6 11.3 %collective-permute-start.9 = (bf16[1024,128]{1,0:T(8,128)(2,1)S(1)}, bf16[1024,128]{1,0:T(8,128)(2,1)S(1)}, u32[]{:S(2)}, u32[]{:S(2)}) collective-permute-start(bf16[1024,128]{1,0:T(8,128)(2,1)S(1)} %collective-permute-done.7.refs_3_), channel_id=1, source_target_pairs={{0,4},{2,0},{6,2},{10,6},{14,10},{12,14},{8,12},{4,8},{1,5},{3,1},... | collective-permute-start | bytes 786440 | tf_op jit(solution)/shard_map/ppermute | solution.py:419
  31.3 9.1 %collective-permute-start.11 = (bf16[1056,128]{1,0:T(8,128)(2,1)S(1)}, bf16[1056,128]{1,0:T(8,128)(2,1)S(1)}, u32[]{:S(2)}, u32[]{:S(2)}) collective-permute-start(bf16[1056,128]{1,0:T(8,128)(2,1)S(1)} %get-tuple-element.43.refs_1_), channel_id=1, source_target_pairs={{0,2},{2,6},{6,10},{10,14},{14,12},{12,8},{8,4},{4,0},{1,3},{3,7},... | collective-permute-start | bytes 811016 | tf_op jit(solution)/shard_map/ppermute | solution.py:419
  33.0 8.3 %collective-permute-start.12 = (bf16[1056,128]{1,0:T(8,128)(2,1)S(1)}, bf16[1056,128]{1,0:T(8,128)(2,1)S(1)}, u32[]{:S(2)}, u32[]{:S(2)}) collective-permute-start(bf16[1056,128]{1,0:T(8,128)(2,1)S(1)} %get-tuple-element.44.refs_2_), channel_id=1, source_target_pairs={{0,4},{2,0},{6,2},{10,6},{14,10},{12,14},{8,12},{4,8},{1,5},{3,1},... | collective-permute-start | bytes 811016 | tf_op jit(solution)/shard_map/ppermute | solution.py:419
  34.3 2.3 %collective-permute-start.10 = (f32[8,128]{1,0:T(8,128)S(1)}, f32[8,128]{1,0:T(8,128)S(1)}, u32[]{:S(2)}, u32[]{:S(2)}) collective-permute-start(f32[8,128]{1,0:T(8,128)S(1)} %get-tuple-element.46), channel_id=1, source_target_pairs={{0,1},{1,0},{2,3},{3,2},{4,5},{5,4},{6,7},{7,6},{8,9},{9,8},{10,11... | collective-permute-start | bytes 12296 | tf_op jit(solution)/shard_map/ppermute | solution.py:430
  36.9 10.2 %collective-permute-start.14 = (bf16[1040,128]{1,0:T(8,128)(2,1)S(1)}, bf16[1040,128]{1,0:T(8,128)(2,1)S(1)}, u32[]{:S(2)}, u32[]{:S(2)}) collective-permute-start(bf16[1040,128]{1,0:T(8,128)(2,1)S(1)} %collective-permute-done.8.refs_0_), channel_id=1, source_target_pairs={{0,2},{2,6},{6,10},{10,14},{14,12},{12,8},{8,4},{4,0},{1,3},{3,7},... | collective-permute-start | bytes 798728 | tf_op jit(solution)/shard_map/ppermute | solution.py:419
  38.5 8.6 %collective-permute-start.15 = (bf16[1024,128]{1,0:T(8,128)(2,1)S(1)}, bf16[1024,128]{1,0:T(8,128)(2,1)S(1)}, u32[]{:S(2)}, u32[]{:S(2)}) collective-permute-start(bf16[1024,128]{1,0:T(8,128)(2,1)S(1)} %collective-permute-done.9.refs_3_), channel_id=1, source_target_pairs={{0,4},{2,0},{6,2},{10,6},{14,10},{12,14},{8,12},{4,8},{1,5},{3,1},... | collective-permute-start | bytes 786440 | tf_op jit(solution)/shard_map/ppermute | solution.py:419
  38.9 12.6 %collective-permute-start.18 = (f32[24,128]{1,0:T(8,128)S(1)}, f32[24,128]{1,0:T(8,128)S(1)}, u32[]{:S(2)}, u32[]{:S(2)}) collective-permute-start(f32[24,128]{1,0:T(8,128)S(1)} %concatenate.3), channel_id=1, source_target_pairs={{0,8},{1,7},{2,4},{3,11},{6,0},{7,15},{10,2},{11,13},{14,6},{15,9}... | collective-permute-start | bytes 36872 | tf_op jit(solution)/shard_map/ppermute | solution.py:437
  42.2 1.2 %collective-permute-start.13 = (f32[8,128]{1,0:T(8,128)S(1)}, f32[8,128]{1,0:T(8,128)S(1)}, u32[]{:S(2)}, u32[]{:S(2)}) collective-permute-start(f32[8,128]{1,0:T(8,128)S(1)} %get-tuple-element.51), channel_id=1, source_target_pairs={{0,1},{1,0},{2,3},{3,2},{4,5},{5,4},{6,7},{7,6},{8,9},{9,8},{10,11... | collective-permute-start | bytes 12296 | tf_op jit(solution)/shard_map/ppermute | solution.py:430
  43.4 8.2 %collective-permute-start.16 = (f32[8,128]{1,0:T(8,128)S(1)}, f32[8,128]{1,0:T(8,128)S(1)}, u32[]{:S(2)}, u32[]{:S(2)}) collective-permute-start(f32[8,128]{1,0:T(8,128)S(1)} %add.12), channel_id=1, source_target_pairs={{0,12},{1,11},{2,8},{3,15},{6,4},{7,13},{10,0},{11,9},{14,2},{15,5... | collective-permute-start | bytes 12296 | tf_op jit(solution)/shard_map/ppermute | solution.py:437
  47.8 6.4 %collective-permute-start.17 = (f32[8,128]{1,0:T(8,128)S(1)}, f32[8,128]{1,0:T(8,128)S(1)}, u32[]{:S(2)}, u32[]{:S(2)}) collective-permute-start(f32[8,128]{1,0:T(8,128)S(1)} %scores.7), channel_id=1, source_target_pairs={{0,14},{2,12},{6,8},{10,4},{14,0},{12,2},{8,6},{4,10},{1,15},{3,13... | collective-permute-start | bytes 12296 | tf_op jit(solution)/shard_map/ppermute | solution.py:419
  54.2 1.2 %collective-permute-start.19 = (f32[32,128]{1,0:T(8,128)S(1)}, f32[32,128]{1,0:T(8,128)S(1)}, u32[]{:S(2)}, u32[]{:S(2)}) collective-permute-start(f32[32,128]{1,0:T(8,128)S(1)} %unpack.1), channel_id=1, source_target_pairs={{0,1},{1,0},{2,3},{3,2},{4,5},{5,4},{6,7},{7,6},{8,9},{9,8},{10,11... | collective-permute-start | bytes 49160 | tf_op jit(solution)/shard_map/ppermute | solution.py:430
